TPU v7x, 128 devices: a whole 4x4x4 slice. The times are simulated.
128 devices in a mesh: graph: 8 (over z, core), feat: 16 (over y, x).
Axes of the slice: x: 4, y: 4, z: 4, core: 2. Of those that a mesh axis runs over, the one named last changes fastest.
Arguments:
- node_features: bfloat16 [131072, 1024], P('graph', 'feat'), may hold values from -6 to 6
- proj_weight: bfloat16 [1024, 512], P('feat'), may hold values from -0.1875 to 0.1875
- relation_weight: bfloat16 [2, 512, 512], replicated, may hold values from -0.25 to 0.25
- att_source: float32 [2, 512], replicated, may hold values from -8 to 8
- att_target: float32 [2, 512], replicated, may hold values from -8 to 8
- edge_mask: int32 [1024, 12, 128, 128], P(('graph', 'feat')), may hold values from 0 to 1, as said below
- relation_ids: int32 [1024, 12], P(('graph', 'feat')), may hold values from 0 to 1
- send_blocks: int32 [128, 8, 4], P(('graph', 'feat')), may hold values from 0 to 7, as said below
- source_slots: int32 [1024, 12], P(('graph', 'feat')), may hold values from 0 to 31
Outputs:
- layer_out: bfloat16 [131072, 512], P(('graph', 'feat'))
Inputs may be any that keep to these rules, and one draw needn't show every extreme that they name: `edge_mask`: every target row i has an edge at list position 0 to row i of that source block. `send_blocks`: the 4 entries of one device's list to one graph index are distinct block numbers of that device.
All inputs are finite; a program needn't handle non-finite values.
Results may differ from a plain program's by a relative error of at most 0.034.
Values may be sent and summed in bfloat16 or wider, within the bound.
No kernel may reach another device: no remote copies, remote signals or barrier semaphores. Data moves between devices by JAX's collectives and lax.ppermute only.
A program may use at most 128 MiB of HBM per device.

v0:
```python
import jax
import jax.numpy as jnp
from jax import lax
from jax.sharding import PartitionSpec as P

HEADS = 4


def attend(target_scores, source_scores, live, values, own):
    heads_count = target_scores.shape[1]
    width = values.shape[2]
    lists = target_scores.shape[0]
    rows = target_scores.shape[2]
    lhs = jnp.transpose(target_scores, (1, 2, 0))
    rhs = jnp.transpose(source_scores, (1, 0, 2))
    raw = lhs[:, :, :, None] + rhs[:, None, :, :]
    leaky = jnp.where(raw > 0, raw, 0.2 * raw)
    usable = (jnp.transpose(live, (1, 0, 2)) > 0)[None]
    masked = jnp.where(usable, leaky, -jnp.inf)
    highest = jnp.max(masked, axis=(2, 3), keepdims=True)
    prob = jnp.exp(masked - highest)
    total = jnp.sum(prob, axis=(2, 3))
    weights = prob.astype(jnp.bfloat16).reshape(heads_count, rows, lists * values.shape[1])
    stacked = values.reshape(lists * values.shape[1], heads_count, width // heads_count)
    summed = jnp.einsum("hix,xhd->hid", weights, stacked, preferred_element_type=jnp.float32)
    summed = summed / total[:, :, None]
    mixed = jnp.transpose(summed, (1, 0, 2)).reshape(rows, width) + own.astype(jnp.float32)
    return jax.nn.elu(mixed).astype(jnp.bfloat16)


def shards(
    node_features,
    proj_weight,
    relation_weight,
    att_source,
    att_target,
    edge_mask,
    relation_ids,
    send_blocks,
    source_slots,
):
    block_rows = edge_mask.shape[-1]
    local_blocks = edge_mask.shape[0]
    rows_local = local_blocks * block_rows
    width = proj_weight.shape[1]
    head_width = width // HEADS
    relations = relation_weight.shape[0]
    hidden = lax.psum_scatter(
        jnp.dot(node_features, proj_weight, preferred_element_type=jnp.float32),
        "feat",
        scatter_dimension=0,
        tiled=True,
    ).astype(jnp.bfloat16)
    blocks = hidden.reshape(local_blocks, block_rows, width)
    outgoing = blocks[send_blocks[0]]
    src_att = att_source.reshape(relations, 1, HEADS, head_width)
    transform_values = jnp.einsum(
        "gnrc,scd->gnsrd",
        lax.all_to_all(outgoing, "graph", split_axis=0, concat_axis=0, tiled=True),
        relation_weight,
        preferred_element_type=jnp.float32,
    ).astype(jnp.bfloat16)
    split_heads = transform_values.astype(jnp.float32).reshape(
        transform_values.shape[:4] + (HEADS, head_width)
    )
    scores = jnp.sum(split_heads * src_att[None, None], axis=-1)
    values = transform_values
    source_all = jnp.transpose(scores, (0, 1, 2, 4, 3))
    slots_total = values.shape[0] * values.shape[1]
    values = values.reshape((slots_total,) + values.shape[2:])
    source_all = source_all.reshape((slots_total,) + source_all.shape[2:])
    own_heads = blocks.astype(jnp.float32).reshape(local_blocks, block_rows, HEADS, head_width)
    tgt_att = att_target.reshape(relations, HEADS, head_width)
    target_all = jnp.sum(own_heads[:, None] * tgt_att[None, :, None], axis=-1)

    def one_block(inputs):
        target_block, live, rels, slots, own = inputs
        chosen = values[slots, rels]
        source_scores = source_all[slots, rels]
        target_scores = jnp.transpose(target_block[rels], (0, 2, 1))
        return attend(target_scores, source_scores, live, chosen, own)

    result = lax.map(one_block, (target_all, edge_mask, relation_ids, source_slots, blocks))
    return result.reshape(rows_local, width)


def solution(mesh):
    placed = (
        P("graph", "feat"),
        P("feat", None),
        P(),
        P(),
        P(),
        P(("graph", "feat"), None, None, None),
        P(("graph", "feat"), None),
        P(("graph", "feat"), None, None),
        P(("graph", "feat"), None),
    )
    return jax.shard_map(
        shards, mesh=mesh, in_specs=placed, out_specs=P(("graph", "feat"), None), check_vma=False
    )
```

profile of v0, /device:TPU:1, one launch (start us, length us, event | category | flops | bytes accessed | tf_op | source)
XLA Modules:
  0.0 479.9 jit_solution(13800237439874070092)
XLA Ops:
  6.5 1.6 copy-done
  8.1 13.9 %fusion.21 = f32[16384,512]{1,0:T(8,128)} fusion(bf16[16384,64]{0,1:T(8,128)(2,1)S(1)} %copy-done, bf16[64,512]{1,0:T(8,128)(2,1)} %param.12), kind=kOutput, calls=%fused_computation.45 | convolution fusion | flops 1073741824 | bytes 35717120 | tf_op jit(solution)/shard_map/dot_general | solution.py:49
  22.9 197.2 %reduce-scatter.2.cloned.1.call-done = f32[1024,512]{1,0:T(8,128)} async-done(((f32[16384,512]{1,0:T(8,128)}), f32[1024,512]{1,0:T(8,128)}) %reduce-scatter.2.cloned.1.call-update) | async-done | bytes 2097168 | tf_op jit(solution)/shard_map/reduce_scatter | solution.py:48
  220.2 1.7 convert_element_type.32
  221.9 2.7 gather_fusion.3
  224.6 5.5 %all-to-all-start = ((bf16[8,4,128,512]{3,2,1,0:T(8,128)(2,1)}), bf16[8,4,128,512]{3,2,1,0:T(8,128)(2,1)}, u32[]{:S(2)}, u32[]{:S(2)}) async-start(bf16[8,4,128,512]{3,2,1,0:T(8,128)(2,1)} %bitcast.107), calls=%async_computation.1 | async-start | bytes 8388608 | tf_op jit(solution)/shard_map/all_to_all | solution.py:59
  230.1 1.7 reshape.137
  231.9 1.9 copy.37
  233.7 1.2 multiply_reduce_fusion.1
  234.9 44.1 %all-to-all-done = bf16[8,4,128,512]{3,2,1,0:T(8,128)(2,1)} async-done(((bf16[8,4,128,512]{3,2,1,0:T(8,128)(2,1)}), bf16[8,4,128,512]{3,2,1,0:T(8,128)(2,1)}, u32[]{:S(2)}, u32[]{:S(2)}) %all-to-all-start) | async-done | bytes 4194336 | tf_op jit(solution)/shard_map/all_to_all | solution.py:59
  279.0 15.2 %bitcast_convert_fusion = (f32[8,4,2,128,512]{4,3,2,1,0:T(8,128)}, bf16[8,4,128,2,512]{4,2,3,1,0:T(8,128)(2,1)}) fusion(bf16[2,512,512]{2,1,0:T(8,128)(2,1)} %param.13, bf16[8,4,128,512]{3,2,1,0:T(8,128)(2,1)} %all-to-all-done), kind=kOutput, calls=%fused_computation.38 | convolution fusion | flops 4303355904 | bytes 30408704 | tf_op jit(solution)/shard_map/gnrc,scd->gnsrd/dot_general | solution.py:57
  294.3 19.2 %reshape.139 = f32[8,4,2,128,4,128]{5,4,3,2,1,0:T(4,128)} reshape(f32[8,4,2,128,512]{4,3,2,1,0:T(8,128)} %get-tuple-element.109) | data formatting | bytes 33554432 | tf_op jit(solution)/shard_map/reshape | solution.py:63
  313.5 14.7 %multiply_reduce_fusion = f32[8,4,2,128,4]{4,3,2,1,0:T(8,128)} fusion(f32[8,4,2,128,4,128]{5,4,3,2,1,0:T(4,128)} %reshape.139, f32[2,4,128]{2,1,0:T(4,128)S(1)} %mul.35), kind=kLoop, calls=%fused_computation.37 | loop fusion | flops 8355840 | bytes 16912384 | tf_op jit(solution)/shard_map/reduce_sum | solution.py:66
  328.2 2.8 copy.40
  331.0 140.5 %while.10 = (s32[]{:T(128)}, bf16[8,128,512]{2,1,0:T(8,128)(2,1)}, s32[8,12,128,128]{3,2,1,0:T(8,128)}, f32[8,2,128,4]{2,3,1,0:T(4,128)S(1)}, s32[8,12]{1,0:T(8,...) while((s32[]{:T(128)}, bf16[8,128,512]{2,1,0:T(8,128)(2,1)}, ...), condition=%wide.region_6.7_spmd, body=%wide.region_3.6_spmd.sunk | while | flops 217907328 | bytes 18914388 | solution.py:83
  333.0 1.2 constant_dynamic-slice_fusion.6
  335.6 1.2 exponential_reduce_fusion.2
  337.0 2.1 fusion.39
  339.1 4.0 gather_fusion.2
  343.1 1.9 reshape.185
  345.0 2.5 fusion.40
  350.6 1.2 constant_dynamic-slice_fusion.6
  353.1 1.2 exponential_reduce_fusion.2
  354.5 2.1 fusion.39
  356.6 4.0 gather_fusion.2
  360.7 1.9 reshape.185
  362.6 2.5 fusion.40
  368.1 1.2 constant_dynamic-slice_fusion.6
  370.7 1.2 exponential_reduce_fusion.2
  372.1 2.1 fusion.39
  374.2 4.0 gather_fusion.2
  378.2 1.9 reshape.185
  380.1 2.5 fusion.40
  385.7 1.2 constant_dynamic-slice_fusion.6
  388.3 1.2 exponential_reduce_fusion.2
  389.6 2.1 fusion.39
  391.7 4.0 gather_fusion.2
  395.8 1.9 reshape.185
  397.7 2.5 fusion.40
  403.2 1.2 constant_dynamic-slice_fusion.6
  405.8 1.2 exponential_reduce_fusion.2
  407.2 2.1 fusion.39
  409.3 4.0 gather_fusion.2
  413.3 1.9 reshape.185
  415.2 2.5 fusion.40
  420.8 1.2 constant_dynamic-slice_fusion.6
  423.4 1.2 exponential_reduce_fusion.2
  424.7 2.1 fusion.39
  426.9 4.0 gather_fusion.2
  430.9 1.9 reshape.185
  432.8 2.5 fusion.40
  438.3 1.2 constant_dynamic-slice_fusion.6
  440.9 1.2 exponential_reduce_fusion.2
  442.3 2.1 fusion.39
  444.4 4.0 gather_fusion.2
  448.4 1.9 reshape.185
  450.3 2.5 fusion.40
  455.9 1.2 constant_dynamic-slice_fusion.6
  458.5 1.2 exponential_reduce_fusion.2
  459.9 2.1 fusion.39
  462.0 4.0 gather_fusion.2
  466.0 1.9 reshape.185
  467.9 2.5 fusion.40
  471.5 1.6 copy-done.1
  (145 shorter events, 36.8 us)
Async XLA Ops:
  6.5 1.6 copy-start
  6.5 213.6 %reduce-scatter.2.cloned.1.call-start = ((), (), s32[]{:S(2)}) async-start(), calls=%async_computation.2 | async-start | bytes 35651584 | tf_op jit(solution)/shard_map/reduce_scatter | solution.py:48
  22.1 0.7 copy-start.4
  224.6 5.5 %copy-start.2 = (f32[2,512]{1,0:T(2,128)S(1)}, f32[2,512]{1,0:T(2,128)}, u32[]{:S(2)}) copy-start(f32[2,512]{1,0:T(2,128)} %param.14) | copy-start | bytes 12292
  224.6 5.5 %copy-start.3 = (f32[2,512]{1,0:T(2,128)S(1)}, f32[2,512]{1,0:T(2,128)}, u32[]{:S(2)}) copy-start(f32[2,512]{1,0:T(2,128)} %param.15) | copy-start | bytes 12292
  224.6 54.4 %all-to-all-start = ((bf16[8,4,128,512]{3,2,1,0:T(8,128)(2,1)}), bf16[8,4,128,512]{3,2,1,0:T(8,128)(2,1)}, u32[]{:S(2)}, u32[]{:S(2)}) async-start(bf16[8,4,128,512]{3,2,1,0:T(8,128)(2,1)} %bitcast.107), calls=%async_computation.1 | async-start | bytes 8388608 | tf_op jit(solution)/shard_map/all_to_all | solution.py:59
  471.5 1.6 copy-start.1
Sparse Core Ops, SparseCore 0:
  22.2 197.9 reduce-scatter.1
where the time goes:
time: 482 us; the launch traced here: 480 us
  waiting for transfers between devices  241 us (50%)
  local copies, waits for them, and re-layouts  109 us (23%)
  other arithmetic  60.9 us (13%)
  matrix products  49.1 us (10%)
  between operations  13.4 us (3%)
  starting transfers between devices  5.48 us (1%)
    reduce_scatter x1, waiting for transfers between devices, shards(): lax.psum_scatter(jnp.dot(node_features, proj_weight, preferred_element_ty...  197 us
    all_to_all x1, waiting for transfers between devices, shards(): lax.all_to_all(outgoing, 'graph', split_axis=0, concat_axis=0, tiled=True)  44.1 us
    gather x8, local copies, waits for them, and re-layouts, one_block(): chosen = values[slots, rels]  32.3 us
    dot_general x8, matrix products, attend(): jnp.einsum('hix,xhd->hid', weights, stacked, preferred_element_type=jnp.f...  20 us
    reshape x1, local copies, waits for them, and re-layouts, shards(): transform_values.astype(jnp.float32)  19.2 us
    convert_element_type x8, other arithmetic, attend(): prob.astype(jnp.bfloat16)  16.9 us
    dot_general x1, matrix products, shards(): jnp.einsum('gnrc,scd->gnsrd', lax.all_to_all(outgoing, 'graph', split_axi...  15.2 us
    reshape x8, local copies, waits for them, and re-layouts, attend(): values.reshape(lists * values.shape[1], heads_count, width // heads_count)  15.1 us
  transfers between devices with their start and end apart: 2, of which 2 were waited for; matrix products, arithmetic and copies ran while one was open for 1% of the time, Pallas kernels for 0%

commit v1 on v0

v1 whole, which is shorter than its diff:
```python
import functools

import jax
import jax.numpy as jnp
from jax import lax
from jax.experimental import pallas as pl
from jax.experimental.pallas import tpu as pltpu
from jax.sharding import PartitionSpec as P

HEADS = 4
LOG2E = 1.4426950408889634
F32 = jnp.float32
BF16 = jnp.bfloat16


def three_parts(x):
    hi = lax.reduce_precision(x, 8, 7)
    rest = x - hi
    mid = lax.reduce_precision(rest, 8, 7)
    return hi.astype(BF16), mid.astype(BF16), (rest - mid).astype(BF16)


def transform_kernel(hid_ref, rw_ref, src_ref, val_ref, score_ref):
    hid = hid_ref[0]
    rows, width = hid.shape
    blocks = val_ref.shape[1]
    relations = rw_ref.shape[0]
    for r in range(relations):
        moved = jnp.dot(hid, rw_ref[r], preferred_element_type=F32).astype(BF16)
        val_ref[0, :, r] = moved.reshape(blocks, rows // blocks, width)
    raw = lax.dot_general(src_ref[...], hid, (((1,), (1,)), ((), ())), preferred_element_type=F32)
    score = raw[0:8] + raw[8:16] + raw[16:24]
    block = rows // blocks
    for c in range(blocks):
        score_ref[0, c] = score[:, c * block : (c + 1) * block]


def transform(frontier, relation_weight, src_vectors):
    peers, cap, block, width = frontier.shape
    relations = relation_weight.shape[0]
    return pl.pallas_call(
        transform_kernel,
        grid=(peers,),
        in_specs=[
            pl.BlockSpec((1, cap * block, width), lambda p: (p, 0, 0)),
            pl.BlockSpec((relations, width, width), lambda p: (0, 0, 0)),
            pl.BlockSpec(src_vectors.shape, lambda p: (0, 0)),
        ],
        out_specs=[
            pl.BlockSpec((1, cap, relations, block, width), lambda p: (p, 0, 0, 0, 0)),
            pl.BlockSpec((1, cap, 8, block), lambda p: (p, 0, 0, 0)),
        ],
        out_shape=[
            jax.ShapeDtypeStruct((peers, cap, relations, block, width), BF16),
            jax.ShapeDtypeStruct((peers, cap, 8, block), F32),
        ],
        compiler_params=pltpu.CompilerParams(vmem_limit_bytes=48 * 1024 * 1024),
        name="transform",
    )(frontier.reshape(peers, cap * block, width), relation_weight, src_vectors)


def attend_kernel(
    rel_ref, slot_ref, own_ref, mask_ref, val_ref, score_ref, tgt_ref, out_ref, tb_ref, log_ref, prob_ref, cat_ref, den_ref
):
    b = pl.program_id(0)
    lists, rows, cols = mask_ref.shape[1:]
    chunk = 32
    own = own_ref[...]
    target = jnp.dot(own, tgt_ref[0], preferred_element_type=F32)
    target += jnp.dot(own, tgt_ref[1], preferred_element_type=F32)
    target += jnp.dot(own, tgt_ref[2], preferred_element_type=F32)
    for r in range(tb_ref.shape[0]):
        for h in range(HEADS):
            c = r * HEADS + h
            tb_ref[r, h] = jnp.broadcast_to(target[:, c : c + 1], (rows, cols))
    rels = [rel_ref[b, k] for k in range(lists)]
    slots = [slot_ref[b, k] for k in range(lists)]
    for k in range(lists):
        cat_ref[k * cols : (k + 1) * cols, :] = val_ref[slots[k], rels[k]]
    for i in range(0, rows, chunk):
        here = slice(i, i + chunk)
        top = [jnp.full((chunk, cols), -jnp.inf, F32) for _ in range(HEADS)]
        for k in range(lists):
            used = mask_ref[0, k, here, :] > 0
            for h in range(HEADS):
                source = score_ref[slots[k], pl.ds(rels[k] * HEADS + h, 1), :]
                raw = tb_ref[rels[k], h, here, :] + source
                logit = jnp.where(used, jnp.maximum(raw, 0.2 * raw), -jnp.inf)
                log_ref[h, k, here, :] = logit
                top[h] = jnp.maximum(top[h], logit)
        for h in range(HEADS):
            highest = jnp.broadcast_to(jnp.max(top[h], axis=1, keepdims=True), (chunk, cols))
            total = jnp.zeros((chunk, cols), F32)
            for k in range(lists):
                prob = jnp.exp2(log_ref[h, k, here, :] - highest)
                total += prob
                prob_ref[h, here, k * cols : (k + 1) * cols] = prob.astype(BF16)
            den_ref[h, here, :] = jnp.broadcast_to(jnp.sum(total, axis=1, keepdims=True), (chunk, cols))
    for h in range(HEADS):
        lanes = slice(h * cols, (h + 1) * cols)
        summed = jnp.dot(prob_ref[h], cat_ref[:, lanes], preferred_element_type=F32)
        mixed = summed / den_ref[h] + own[:, lanes].astype(F32)
        out_ref[:, lanes] = jnp.where(mixed > 0, mixed, jnp.exp(jnp.minimum(mixed, 0.0)) - 1.0).astype(BF16)


def attend(hidden, edge_mask, relation_ids, source_slots, values, scores, tgt_vectors):
    blocks, lists, rows, cols = edge_mask.shape
    width = hidden.shape[1]
    slots, relations = values.shape[:2]
    return pl.pallas_call(
        attend_kernel,
        grid_spec=pltpu.PrefetchScalarGridSpec(
            num_scalar_prefetch=2,
            grid=(blocks,),
            in_specs=[
                pl.BlockSpec((rows, width), lambda b, *_: (b, 0)),
                pl.BlockSpec((1, lists, rows, cols), lambda b, *_: (b, 0, 0, 0)),
                pl.BlockSpec(values.shape, lambda b, *_: (0, 0, 0, 0)),
                pl.BlockSpec(scores.shape, lambda b, *_: (0, 0, 0)),
                pl.BlockSpec(tgt_vectors.shape, lambda b, *_: (0, 0, 0)),
            ],
            out_specs=pl.BlockSpec((rows, width), lambda b, *_: (b, 0)),
            scratch_shapes=[
                pltpu.VMEM((relations, HEADS, rows, cols), F32),
                pltpu.VMEM((HEADS, lists, rows, cols), F32),
                pltpu.VMEM((HEADS, rows, lists * cols), BF16),
                pltpu.VMEM((lists * cols, width), BF16),
                pltpu.VMEM((HEADS, rows, cols), F32),
            ],
        ),
        out_shape=jax.ShapeDtypeStruct(hidden.shape, BF16),
        compiler_params=pltpu.CompilerParams(vmem_limit_bytes=56 * 1024 * 1024),
        name="attend",
    )(relation_ids, source_slots, hidden, edge_mask, values, scores, tgt_vectors)


def score_vectors(relation_weight, att_source, att_target):
    relations, width = att_source.shape
    head_width = width // HEADS
    split = att_source.reshape(relations, HEADS, head_width)
    moved = jnp.einsum(
        "rche,rhe->rhc",
        relation_weight.astype(F32).reshape(relations, width, HEADS, head_width),
        split,
        precision=lax.Precision.HIGHEST,
        preferred_element_type=F32,
    ).reshape(relations * HEADS, width)
    src = jnp.concatenate(three_parts(moved * LOG2E) + (jnp.zeros((8, width), BF16),), axis=0)
    own_head = (jnp.arange(width)[:, None] // head_width) == (jnp.arange(relations * HEADS)[None, :] % HEADS)
    spread = jnp.repeat(att_target.T, HEADS, axis=1)
    tgt = jnp.where(own_head, spread, 0.0) * LOG2E
    tgt = jnp.pad(tgt, ((0, 0), (0, 128 - relations * HEADS)))
    return src, jnp.stack(three_parts(tgt))


def shards(
    node_features,
    proj_weight,
    relation_weight,
    att_source,
    att_target,
    edge_mask,
    relation_ids,
    send_blocks,
    source_slots,
):
    block_rows = edge_mask.shape[-1]
    local_blocks = edge_mask.shape[0]
    rows_local = local_blocks * block_rows
    depth, width = proj_weight.shape
    n_feat = lax.axis_size("feat")
    src_vectors, tgt_vectors = score_vectors(relation_weight, att_source, att_target)
    slices = node_features.T.reshape(depth, n_feat, rows_local).transpose(1, 0, 2)
    weights = jnp.broadcast_to(proj_weight[None], (n_feat, depth, width))
    got = lax.all_to_all(jnp.concatenate([slices, weights], axis=2), "feat", 0, 0, tiled=True)
    got = got.reshape(n_feat * depth, rows_local + width)
    hidden = lax.dot_general(
        got[:, :rows_local], got[:, rows_local:], (((0,), (0,)), ((), ())), preferred_element_type=F32
    ).astype(BF16)
    blocks = hidden.reshape(local_blocks, block_rows, width)
    frontier = lax.all_to_all(blocks[send_blocks[0]], "graph", split_axis=0, concat_axis=0, tiled=True)
    values, scores = transform(frontier, relation_weight, src_vectors)
    slots = values.shape[0] * values.shape[1]
    values = values.reshape((slots,) + values.shape[2:])
    scores = scores.reshape((slots,) + scores.shape[2:])
    return attend(hidden, edge_mask, relation_ids, source_slots, values, scores, tgt_vectors)


def solution(mesh):
    placed = (
        P("graph", "feat"),
        P("feat", None),
        P(),
        P(),
        P(),
        P(("graph", "feat"), None, None, None),
        P(("graph", "feat"), None),
        P(("graph", "feat"), None, None),
        P(("graph", "feat"), None),
    )
    return jax.shard_map(
        shards, mesh=mesh, in_specs=placed, out_specs=P(("graph", "feat"), None), check_vma=False
    )
```

time: 482 us -> 159 us (0.33)
  waiting for transfers between devices: 241 us -> 93 us
  local copies, waits for them, and re-layouts: 109 us -> 11.7 us
  other arithmetic: 60.9 us -> 1.43 us
  matrix products: 49.1 us -> 4.04 us
  Pallas kernels: 0 us -> 32.6 us
  between operations: 13.4 us -> 0.15 us
  starting transfers between devices: 5.48 us -> 15 us
    reduce_scatter x1 -> x0, waiting for transfers between devices: 197 us -> none  [shards(): lax.psum_scatter(jnp.dot(node_features, proj_weight, preferred_element_ty...]
    all_to_all x1 -> x2, waiting for transfers between devices: 44.1 us -> 93 us  [the longest x1 46.6 us: shards(): lax.all_to_all(blocks[send_blocks[0]], 'graph', split_axis=0, concat_axis...]
    dot_general x10 -> x2, matrix products: 49.1 us -> 4.04 us  [the longest x1 3.13 us: shards(): lax.dot_general(got[:, :rows_local], got[:, rows_local:], (((0,), (0,)),...]
    gather x25 -> x1, local copies, waits for them, and re-layouts: 44.8 us -> 2.76 us  [shards(): blocks[send_blocks[0]]]
    reshape x9 -> x3, local copies, waits for them, and re-layouts: 34.4 us -> 0.15 us  [the longest x2 0.13 us: score_vectors(): spread = jnp.repeat(att_target.T, HEADS, axis=1)]
    pallas_call x0 -> x2, Pallas kernels: none -> 32.6 us  [the longest x1 22.5 us: attend(): pl.pallas_call(attend_kernel, grid_spec=pltpu.PrefetchScalarGridSpec(num_...]
    reduce_sum x10 -> x0, other arithmetic: 25.8 us -> none  [the longest x1 14.7 us: shards(): scores = jnp.sum(split_heads * src_att[None, None], axis=-1)]
    convert_element_type x17 -> x1, other arithmetic: 19.6 us -> 0.01 us  [three_parts(): return (hi.astype(BF16), mid.astype(BF16), (rest - mid).astype(BF16))]
  transfers between devices with their start and end apart: 2 -> 2, of which waited for: 2 -> 2; matrix products, arithmetic and copies ran while one was open for 1% -> 2% of each run, Pallas kernels for 0% -> 0%
where the time goes in v1:
time: 159 us; the launch traced here: 158 us
  waiting for transfers between devices  93 us (58%)
  Pallas kernels  32.6 us (21%)
  starting transfers between devices  15 us (9%)
  local copies, waits for them, and re-layouts  11.7 us (7%)
  matrix products  4.04 us (3%)
    all_to_all x1, waiting for transfers between devices, shards(): lax.all_to_all(blocks[send_blocks[0]], 'graph', split_axis=0, concat_axis...  46.6 us
    all_to_all x1, waiting for transfers between devices, shards(): lax.all_to_all(jnp.concatenate([slices, weights], axis=2), 'feat', 0, 0,...  46.4 us
    pallas_call x1, Pallas kernels, attend(): pl.pallas_call(attend_kernel, grid_spec=pltpu.PrefetchScalarGridSpec(num_...  22.5 us
    pallas_call x1, Pallas kernels, transform(): pl.pallas_call(transform_kernel, grid=(peers,), in_specs=[pl.BlockSpec((1...  10.1 us
    all_to_all x1, starting transfers between devices, shards(): lax.all_to_all(jnp.concatenate([slices, weights], axis=2), 'feat', 0, 0,...  7.72 us
    all_to_all x1, starting transfers between devices, shards(): lax.all_to_all(blocks[send_blocks[0]], 'graph', split_axis=0, concat_axis...  7.28 us
    unnamed x17, local copies, waits for them, and re-layouts  5.13 us
    concatenate x1, local copies, waits for them, and re-layouts, shards(): jnp.concatenate([slices, weights], axis=2)  3.36 us
  transfers between devices with their start and end apart: 2, of which 2 were waited for; matrix products, arithmetic and copies ran while one was open for 2% of the time, Pallas kernels for 0%

profile of v1, /device:TPU:1, one launch (start us, length us, event | category | flops | bytes accessed | tf_op | source)
XLA Modules:
  0.0 158.0 jit_solution(17073764153588957948)
XLA Ops:
  0.0 0.0 copy-start.4
  0.0 2.8 %copy.24 = bf16[8,8,16,1024]{3,2,1,0:T(8,128)(2,1)S(1)} copy(bf16[8,8,16,1024]{3,1,2,0:T(8,128)(2,1)} %bitcast.41) | data formatting | bytes 4194304
  2.8 0.0 copy-done.4
  2.8 0.1 broadcast_in_dim.10
  2.9 0.3 pad_maximum_fusion
  3.2 3.4 %copy.17 = bf16[16,64,1536]{2,1,0:T(8,128)(2,1)} copy(bf16[16,64,1536]{2,0,1:T(8,128)(2,1)S(1)} %pad_maximum_fusion) | data formatting | bytes 6291456 | tf_op jit(solution)/shard_map/concatenate | solution.py:175
  6.6 0.0 copy-start.7
  6.6 7.7 %all-to-all-start = ((bf16[16,64,1536]{2,1,0:T(8,128)(2,1)}), bf16[16,64,1536]{2,1,0:T(8,128)(2,1)S(1)}, u32[]{:S(2)}, u32[]{:S(2)}) async-start(bf16[16,64,1536]{2,1,0:T(8,128)(2,1)} %copy.17), calls=%async_computation | async-start | bytes 6291456 | tf_op jit(solution)/shard_map/all_to_all | solution.py:175
  14.3 0.0 copy-done.7
  14.3 0.1 copy.18
  14.4 0.1 reshape.122
  14.5 46.4 %all-to-all-done = bf16[16,64,1536]{2,1,0:T(8,128)(2,1)S(1)} async-done(((bf16[16,64,1536]{2,1,0:T(8,128)(2,1)}), bf16[16,64,1536]{2,1,0:T(8,128)(2,1)S(1)}, u32[]{:S(2)}, u32[]{:S(2)}) %all-to-all-start) | async-done | bytes 3145760 | tf_op jit(solution)/shard_map/all_to_all | solution.py:175
  60.9 0.0 copy-start.3
  60.9 1.6 %copy-done.3 = bf16[16,64,1536]{2,1,0:T(8,128)(2,1)} copy-done((bf16[16,64,1536]{2,1,0:T(8,128)(2,1)}, bf16[16,64,1536]{2,1,0:T(8,128)(2,1)S(1)}, u32[]{:S(2)}) %copy-start.3) | copy-done | bytes 3145752
  62.6 3.1 %fusion.2.own_ref = bf16[1024,512]{1,0:T(8,128)(2,1)S(1)} fusion(bf16[1024,1536]{1,0:T(8,128)(2,1)} %bitcast.40), kind=kOutput, calls=%fused_computation.4 | convolution fusion | flops 1074266112 | bytes 4194304 | tf_op jit(solution)/shard_map/dot_general | solution.py:177
  65.7 0.0 copy-start.2
  65.7 2.8 %gather_fusion = bf16[32,128,512]{2,1,0:T(8,128)(2,1)} fusion(bf16[8,128,512]{2,1,0:T(8,128)(2,1)S(1)} %bitcast.36, s32[1024]{0:T(1024)S(1)} %pad_clamp_fusion), kind=kCustom, calls=%fused_computation | custom fusion | bytes 8388736 | tf_op jit(solution)/shard_map/gather | solution.py:181
  68.5 0.0 copy-done.2
  68.5 0.0 copy-start.6
  68.5 0.0 copy-start
  68.5 0.0 copy-start.5
  68.5 7.3 %all-to-all-start.1 = ((bf16[8,4,128,512]{3,2,1,0:T(8,128)(2,1)}), bf16[8,4,128,512]{3,2,1,0:T(8,128)(2,1)}, u32[]{:S(2)}, u32[]{:S(2)}) async-start(bf16[8,4,128,512]{3,2,1,0:T(8,128)(2,1)} %bitcast.37), calls=%async_computation.1 | async-start | bytes 8388608 | tf_op jit(solution)/shard_map/all_to_all | solution.py:181
  75.8 0.0 copy-done.6
  75.8 0.0 copy-done
  75.8 0.9 fusion.5
  76.8 0.0 copy-done.5
  76.8 0.1 copy.19
  76.9 0.1 pad.11.clone
  77.0 0.1 select_multiply_fusion
  77.2 0.1 fusion.11
  77.2 0.8 pad_maximum_fusion.1.tgt_ref
  78.1 0.1 maximum_maximum_fusion.src_ref
  78.1 46.6 %all-to-all-done.1 = bf16[8,4,128,512]{3,2,1,0:T(8,128)(2,1)} async-done(((bf16[8,4,128,512]{3,2,1,0:T(8,128)(2,1)}), bf16[8,4,128,512]{3,2,1,0:T(8,128)(2,1)}, u32[]{:S(2)}, u32[]{:S(2)}) %all-to-all-start.1) | async-done | bytes 4194336 | tf_op jit(solution)/shard_map/all_to_all | solution.py:181
  124.7 10.1 %transform.1 = (bf16[8,4,2,128,512]{4,3,2,1,0:T(8,128)(2,1)}, f32[8,4,8,128]{3,2,1,0:T(8,128)S(1)}) custom-call(bf16[8,512,512]{2,1,0:T(8,128)(2,1)} %bitcast.6.hid_ref, bf16[2,512,512]{2,1,0:T(8,128)(2,1)S(1)} %copy-done, bf16[32,512]{1,0:T(8,128)(2,1)S(1)} %maximum_maximum_fusion.src_ref), custom_call_target="tpu_custom_call" | custom-call | tf_op jit(solution)/shard_map/transform/pallas_call | solution.py:41
  134.8 0.0 copy-start.1
  134.8 0.6 copy-done.1
  135.5 22.5 %attend.1 = bf16[1024,512]{1,0:T(8,128)(2,1)} custom-call(s32[8,12]{1,0:T(8,128)} %rel_ref.1, s32[8,12]{1,0:T(8,128)} %slot_ref.1, bf16[1024,512]{1,0:T(8,128)(2,1)} %copy-done.2, s32[8,12,128,128]{3,2,1,0:T(8,128)} %mask_ref.1, bf16[32,2,128,512]{3,2,1,0:T(8,128)(2,1)} %bitcast.39, f32[32,8,128]{2,1,0:T(8,128)} %bitcast.35, ...), custom_call_target="tpu_custom_call" | custom-call | tf_op jit(solution)/shard_map/attend/pallas_call | solution.py:110
  (11 shorter events, 0.1 us)
Async XLA Ops:
  0.0 2.8 %copy-start.4 = (bf16[64,512]{1,0:T(8,128)(2,1)S(1)}, bf16[64,512]{1,0:T(8,128)(2,1)}, u32[]{:S(2)}) copy-start(bf16[64,512]{1,0:T(8,128)(2,1)} %param.10) | copy-start | bytes 196612
  6.6 7.7 %copy-start.7 = (s32[1,8,4]{1,2,0:T(4,128)S(1)}, s32[1,8,4]{1,2,0:T(4,128)}, u32[]{:S(2)}) copy-start(s32[1,8,4]{1,2,0:T(4,128)} %param.16) | copy-start | bytes 388
  6.6 54.3 %all-to-all-start = ((bf16[16,64,1536]{2,1,0:T(8,128)(2,1)}), bf16[16,64,1536]{2,1,0:T(8,128)(2,1)S(1)}, u32[]{:S(2)}, u32[]{:S(2)}) async-start(bf16[16,64,1536]{2,1,0:T(8,128)(2,1)} %copy.17), calls=%async_computation | async-start | bytes 6291456 | tf_op jit(solution)/shard_map/all_to_all | solution.py:175
  60.9 1.6 %copy-start.3 = (bf16[16,64,1536]{2,1,0:T(8,128)(2,1)}, bf16[16,64,1536]{2,1,0:T(8,128)(2,1)S(1)}, u32[]{:S(2)}) copy-start(bf16[16,64,1536]{2,1,0:T(8,128)(2,1)S(1)} %all-to-all-done) | copy-start | bytes 9437188
  65.7 2.8 %copy-start.2 = (bf16[1024,512]{1,0:T(8,128)(2,1)}, bf16[1024,512]{1,0:T(8,128)(2,1)S(1)}, u32[]{:S(2)}) copy-start(bf16[1024,512]{1,0:T(8,128)(2,1)S(1)} %fusion.2.own_ref) | copy-start | bytes 3145732
  68.5 7.3 %copy-start.6 = (f32[2,512]{1,0:T(2,128)S(1)}, f32[2,512]{1,0:T(2,128)}, u32[]{:S(2)}) copy-start(f32[2,512]{1,0:T(2,128)} %param.12) | copy-start | bytes 12292
  68.5 7.3 %copy-start = (bf16[2,512,512]{2,1,0:T(8,128)(2,1)S(1)}, bf16[2,512,512]{2,1,0:T(8,128)(2,1)}, u32[]{:S(2)}) copy-start(bf16[2,512,512]{2,1,0:T(8,128)(2,1)} %rw_ref.1) | copy-start | bytes 3145732
  68.5 8.3 %copy-start.5 = (f32[2,512]{1,0:T(2,128)S(1)}, f32[2,512]{1,0:T(2,128)}, u32[]{:S(2)}) copy-start(f32[2,512]{1,0:T(2,128)} %param.13) | copy-start | bytes 12292
  68.5 56.2 %all-to-all-start.1 = ((bf16[8,4,128,512]{3,2,1,0:T(8,128)(2,1)}), bf16[8,4,128,512]{3,2,1,0:T(8,128)(2,1)}, u32[]{:S(2)}, u32[]{:S(2)}) async-start(bf16[8,4,128,512]{3,2,1,0:T(8,128)(2,1)} %bitcast.37), calls=%async_computation.1 | async-start | bytes 8388608 | tf_op jit(solution)/shard_map/all_to_all | solution.py:181
  134.8 0.7 copy-start.1

commit v2 on v1

--- a/solution.py
+++ b/solution.py
@@ -8,6 +8,7 @@
 from jax.sharding import PartitionSpec as P
 
 HEADS = 4
+CAP = 4
 LOG2E = 1.4426950408889634
 F32 = jnp.float32
 BF16 = jnp.bfloat16
@@ -20,51 +21,112 @@
     return hi.astype(BF16), mid.astype(BF16), (rest - mid).astype(BF16)
 
 
-def transform_kernel(hid_ref, rw_ref, src_ref, val_ref, score_ref):
-    hid = hid_ref[0]
-    rows, width = hid.shape
-    blocks = val_ref.shape[1]
-    relations = rw_ref.shape[0]
+def transform_kernel(bounds, first, idx_ref, *refs):
+    n_pieces = sum(len(pieces) for pieces in bounds)
+    pieces = refs[:n_pieces]
+    rw_ref, src_ref = refs[n_pieces : n_pieces + 2]
+    val_ref, score_ref, hid_ref, sem = refs[-4:]
+    sources = len(bounds)
+    blocks, relations, block = val_ref.shape[1:4]
+    now = pl.program_id(0)
+
+    def copy(piece, row, slot, c):
+        return pltpu.make_async_copy(
+            piece.at[pl.ds(row, block)], hid_ref.at[slot, pl.ds(c * block, block)], sem.at[slot, c]
+        )
+
+    def fetch(source):
+        begin = sum(len(p) for p in bounds[:source])
+        for c in range(blocks):
+            wanted = idx_ref[first + source, c]
+            for n, (low, high) in enumerate(bounds[source]):
+
+                @pl.when((wanted >= low) & (wanted < high))
+                def _():
+                    row = pl.multiple_of((wanted - low) * block, block)
+                    copy(pieces[begin + n], row, source % 2, c).start()
+
+    @pl.when(now == 0)
+    def _():
+        fetch(0)
+
+    for source in range(1, sources):
+
+        @pl.when(now == source - 1)
+        def _():
+            fetch(source)
+
+    slot = lax.rem(now, 2)
+    for c in range(blocks):
+        copy(pieces[0], 0, slot, c).wait()
+    hid = hid_ref[slot]
     for r in range(relations):
         moved = jnp.dot(hid, rw_ref[r], preferred_element_type=F32).astype(BF16)
-        val_ref[0, :, r] = moved.reshape(blocks, rows // blocks, width)
+        val_ref[0, :, r] = moved.reshape(blocks, block, moved.shape[1])
     raw = lax.dot_general(src_ref[...], hid, (((1,), (1,)), ((), ())), preferred_element_type=F32)
     score = raw[0:8] + raw[8:16] + raw[16:24]
-    block = rows // blocks
     for c in range(blocks):
         score_ref[0, c] = score[:, c * block : (c + 1) * block]
 
 
-def transform(frontier, relation_weight, src_vectors):
-    peers, cap, block, width = frontier.shape
-    relations = relation_weight.shape[0]
+def transform(sources, first, index, relation_weight, src_vectors, block, values, scores):
+    bounds = tuple(tuple((low, high) for _, low, high in pieces) for pieces in sources)
+    arrays = [array for pieces in sources for array, _, _ in pieces]
+    peers, cap = index.shape
+    relations, width = relation_weight.shape[:2]
+    anywhere = pl.BlockSpec(memory_space=pl.ANY)
+    at = len(arrays) + 1 + 2
+    kept = () if values is None else (values, scores)
     return pl.pallas_call(
-        transform_kernel,
-        grid=(peers,),
-        in_specs=[
-            pl.BlockSpec((1, cap * block, width), lambda p: (p, 0, 0)),
-            pl.BlockSpec((relations, width, width), lambda p: (0, 0, 0)),
-            pl.BlockSpec(src_vectors.shape, lambda p: (0, 0)),
-        ],
-        out_specs=[
-            pl.BlockSpec((1, cap, relations, block, width), lambda p: (p, 0, 0, 0, 0)),
-            pl.BlockSpec((1, cap, 8, block), lambda p: (p, 0, 0, 0)),
-        ],
+        functools.partial(transform_kernel, bounds, first),
+        grid_spec=pltpu.PrefetchScalarGridSpec(
+            num_scalar_prefetch=1,
+            grid=(len(sources),),
+            in_specs=[anywhere] * len(arrays)
+            + [
+                pl.BlockSpec((relations, width, width), lambda p, *_: (0, 0, 0)),
+                pl.BlockSpec(src_vectors.shape, lambda p, *_: (0, 0)),
+            ]
+            + [anywhere] * len(kept),
+            out_specs=[
+                pl.BlockSpec((1, cap, relations, block, width), lambda p, *_: (p + first, 0, 0, 0, 0)),
+                pl.BlockSpec((1, cap, 8, block), lambda p, *_: (p + first, 0, 0, 0)),
+            ],
+            scratch_shapes=[pltpu.VMEM((2, cap * block, width), BF16), pltpu.SemaphoreType.DMA((2, cap))],
+        ),
         out_shape=[
             jax.ShapeDtypeStruct((peers, cap, relations, block, width), BF16),
             jax.ShapeDtypeStruct((peers, cap, 8, block), F32),
         ],
+        input_output_aliases={at + n: n for n in range(len(kept))},
         compiler_params=pltpu.CompilerParams(vmem_limit_bytes=48 * 1024 * 1024),
         name="transform",
-    )(frontier.reshape(peers, cap * block, width), relation_weight, src_vectors)
+    )(index, *arrays, relation_weight, src_vectors, *kept)
 
 
 def attend_kernel(
-    rel_ref, slot_ref, own_ref, mask_ref, val_ref, score_ref, tgt_ref, out_ref, tb_ref, log_ref, prob_ref, cat_ref, den_ref
+    rel_ref, slot_ref, own_ref, mask_ref, val_ref, score_ref, tgt_ref, out_ref, tb_ref, log_ref, prob_ref, cats_ref, den_ref, sem
 ):
     b = pl.program_id(0)
     lists, rows, cols = mask_ref.shape[1:]
     chunk = 32
+
+    def copy(block, slot, k):
+        return pltpu.make_async_copy(
+            val_ref.at[slot_ref[block, k], rel_ref[block, k]], cats_ref.at[slot, pl.ds(k * cols, cols)], sem.at[slot, k]
+        )
+
+    @pl.when(b == 0)
+    def _():
+        for k in range(lists):
+            copy(0, 0, k).start()
+
+    @pl.when(b + 1 < pl.num_programs(0))
+    def _():
+        for k in range(lists):
+            copy(b + 1, lax.rem(b + 1, 2), k).start()
+
+    half = lax.rem(b, 2)
     own = own_ref[...]
     target = jnp.dot(own, tgt_ref[0], preferred_element_type=F32)
     target += jnp.dot(own, tgt_ref[1], preferred_element_type=F32)
@@ -75,8 +137,6 @@
             tb_ref[r, h] = jnp.broadcast_to(target[:, c : c + 1], (rows, cols))
     rels = [rel_ref[b, k] for k in range(lists)]
     slots = [slot_ref[b, k] for k in range(lists)]
-    for k in range(lists):
-        cat_ref[k * cols : (k + 1) * cols, :] = val_ref[slots[k], rels[k]]
     for i in range(0, rows, chunk):
         here = slice(i, i + chunk)
         top = [jnp.full((chunk, cols), -jnp.inf, F32) for _ in range(HEADS)]
@@ -96,9 +156,11 @@
                 total += prob
                 prob_ref[h, here, k * cols : (k + 1) * cols] = prob.astype(BF16)
             den_ref[h, here, :] = jnp.broadcast_to(jnp.sum(total, axis=1, keepdims=True), (chunk, cols))
+    for k in range(lists):
+        copy(b, half, k).wait()
     for h in range(HEADS):
         lanes = slice(h * cols, (h + 1) * cols)
-        summed = jnp.dot(prob_ref[h], cat_ref[:, lanes], preferred_element_type=F32)
+        summed = jnp.dot(prob_ref[h], cats_ref[half, :, lanes], preferred_element_type=F32)
         mixed = summed / den_ref[h] + own[:, lanes].astype(F32)
         out_ref[:, lanes] = jnp.where(mixed > 0, mixed, jnp.exp(jnp.minimum(mixed, 0.0)) - 1.0).astype(BF16)
 
@@ -115,7 +177,7 @@
             in_specs=[
                 pl.BlockSpec((rows, width), lambda b, *_: (b, 0)),
                 pl.BlockSpec((1, lists, rows, cols), lambda b, *_: (b, 0, 0, 0)),
-                pl.BlockSpec(values.shape, lambda b, *_: (0, 0, 0, 0)),
+                pl.BlockSpec(memory_space=pl.ANY),
                 pl.BlockSpec(scores.shape, lambda b, *_: (0, 0, 0)),
                 pl.BlockSpec(tgt_vectors.shape, lambda b, *_: (0, 0, 0)),
             ],
@@ -124,8 +186,9 @@
                 pltpu.VMEM((relations, HEADS, rows, cols), F32),
                 pltpu.VMEM((HEADS, lists, rows, cols), F32),
                 pltpu.VMEM((HEADS, rows, lists * cols), BF16),
-                pltpu.VMEM((lists * cols, width), BF16),
+                pltpu.VMEM((2, lists * cols, width), BF16),
                 pltpu.VMEM((HEADS, rows, cols), F32),
+                pltpu.SemaphoreType.DMA((2, lists)),
             ],
         ),
         out_shape=jax.ShapeDtypeStruct(hidden.shape, BF16),
@@ -169,21 +232,71 @@
     rows_local = local_blocks * block_rows
     depth, width = proj_weight.shape
     n_feat = lax.axis_size("feat")
+    n_graph = lax.axis_size("graph")
+    depth_z = n_graph // 2
+    place = lax.axis_index("graph")
+    core, level = lax.rem(place, 2), place // 2
+
+    def send(x, levels, cores=0):
+        pairs = [(p, (p + 2 * levels) % n_graph ^ cores) for p in range(n_graph)]
+        return lax.ppermute(x, "graph", pairs)
+
+    cut = 3
+    parts = ((0, cut), (cut, local_blocks))
+    features = node_features.T.reshape(depth, n_feat, local_blocks, block_rows)
+
+    def slices(low, high):
+        return features[:, :, low:high].reshape(depth, n_feat, (high - low) * block_rows).transpose(1, 0, 2)
+
+    half = width // 2
+    share = lax.dynamic_slice(proj_weight, (0, core * half), (depth, half))
+    share = jnp.broadcast_to(share[None], (n_feat, depth, half))
+    got = lax.all_to_all(jnp.concatenate([slices(*parts[0]), share], axis=2), "feat", 0, 0, tiled=True)
+    got = got.reshape(n_feat * depth, cut * block_rows + half)
+    later = lax.all_to_all(slices(*parts[1]), "feat", 0, 0, tiled=True)
+    later = later.reshape(n_feat * depth, (local_blocks - cut) * block_rows)
+    mine = got[:, cut * block_rows :]
+    other = send(mine, 0, 1)
+    whole = jnp.where(core == 0, jnp.concatenate([mine, other], axis=1), jnp.concatenate([other, mine], axis=1))
+
     src_vectors, tgt_vectors = score_vectors(relation_weight, att_source, att_target)
-    slices = node_features.T.reshape(depth, n_feat, rows_local).transpose(1, 0, 2)
-    weights = jnp.broadcast_to(proj_weight[None], (n_feat, depth, width))
-    got = lax.all_to_all(jnp.concatenate([slices, weights], axis=2), "feat", 0, 0, tiled=True)
-    got = got.reshape(n_feat * depth, rows_local + width)
-    hidden = lax.dot_general(
-        got[:, :rows_local], got[:, rows_local:], (((0,), (0,)), ((), ())), preferred_element_type=F32
-    ).astype(BF16)
-    blocks = hidden.reshape(local_blocks, block_rows, width)
-    frontier = lax.all_to_all(blocks[send_blocks[0]], "graph", split_axis=0, concat_axis=0, tiled=True)
-    values, scores = transform(frontier, relation_weight, src_vectors)
-    slots = values.shape[0] * values.shape[1]
-    values = values.reshape((slots,) + values.shape[2:])
-    scores = scores.reshape((slots,) + scores.shape[2:])
-    return attend(hidden, edge_mask, relation_ids, source_slots, values, scores, tgt_vectors)
+    tables = lax.all_gather(send_blocks[0], "graph")[:, place]
+    relative = jnp.arange(n_graph)
+    index = tables[2 * lax.rem(level - relative // 2 + depth_z, depth_z) + (relative % 2 ^ core)]
+    peer = source_slots // CAP
+    distance = lax.rem(level - peer // 2 + depth_z, depth_z)
+    slots = (2 * distance + (peer % 2 ^ core)) * CAP + source_slots % CAP
+
+    hidden = []
+    sources = [[] for _ in range(n_graph)]
+    for (low, high), x in zip(parts, (got[:, : cut * block_rows], later)):
+        part = lax.dot_general(x, whole, (((0,), (0,)), ((), ())), preferred_element_type=F32).astype(BF16)
+        hidden.append(part)
+        middle = (high - low + (low == 0)) // 2
+        split = middle * block_rows
+        up, down = send(part, 1), send(part, -1)
+        arrived = (
+            (0, part, low, high),
+            (1, up, low, high),
+            (3, down, low, high),
+            (2, send(up[:split], 1), low, low + middle),
+            (2, send(down[split:], -1), low + middle, high),
+        )
+        for steps, array, first, end in arrived:
+            sources[2 * steps].append((array, first, end))
+            sources[2 * steps + 1].append((send(array, 0, 1), first, end))
+
+    values = scores = None
+    index = index.astype(jnp.int32)
+    for group in ((0, 1), (2, 3), (6, 7), (4, 5)):
+        values, scores = transform(
+            [sources[s] for s in group], group[0], index, relation_weight, src_vectors, block_rows, values, scores
+        )
+    total = n_graph * CAP
+    values = values.reshape((total,) + values.shape[2:])
+    scores = scores.reshape((total,) + scores.shape[2:])
+    hidden = jnp.concatenate(hidden, axis=0)
+    return attend(hidden, edge_mask, relation_ids, slots, values, scores, tgt_vectors)
 
 
 def solution(mesh):

time: 159 us -> 164 us (1.031)
  waiting for transfers between devices: 93 us -> 35.7 us
  starting transfers between devices: 15 us -> 38.4 us
  blocking collectives: 0 us -> 15.9 us
  local copies, waits for them, and re-layouts: 11.7 us -> 20.2 us
  other arithmetic: 1.43 us -> 8.46 us
  Pallas kernels: 32.6 us -> 38.7 us
    all_to_all x2, waiting for transfers between devices: 93 us -> 20.7 us  [the longest x1 12.2 us: shards(): lax.all_to_all(jnp.concatenate([slices(*parts[0]), share], axis=2), 'feat...]
    ppermute x0 -> x19, starting transfers between devices: none -> 25.3 us  [send(): return lax.ppermute(x, 'graph', pairs)]
    all_gather x0 -> x1, blocking collectives: none -> 15.9 us  [shards(): tables = lax.all_gather(send_blocks[0], 'graph')[:, place]]
    ppermute x0 -> x19, waiting for transfers between devices: none -> 15 us  [send(): return lax.ppermute(x, 'graph', pairs)]
    pallas_call x1 -> x4, Pallas kernels: 10.1 us -> 17.7 us  [transform(): pl.pallas_call(functools.partial(transform_kernel, bounds, first), grid_s...]
    slice x0 -> x7, local copies, waits for them, and re-layouts: none -> 7.01 us  [the longest x2 2.55 us: slices(): features[:, :, low:high].reshape(depth, n_feat, (high - low) * block_rows)]
    reshape x0 -> x2, local copies, waits for them, and re-layouts: none -> 4.76 us  [slices(): features[:, :, low:high].reshape(depth, n_feat, (high - low) * block_rows)]
    another operation x2, other arithmetic: 0.88 us -> 3.58 us  [score_vectors(): return (src, jnp.stack(three_parts(tgt)))]
  transfers between devices with their start and end apart: 2 -> 21, of which waited for: 2 -> 5; matrix products, arithmetic and copies ran while one was open for 2% -> 16% of each run, Pallas kernels for 0% -> 8%
where the time goes in v2:
time: 164 us; the launch traced here: 163 us
  Pallas kernels  38.7 us (24%)
  starting transfers between devices  38.4 us (23%)
  waiting for transfers between devices  35.7 us (22%)
  local copies, waits for them, and re-layouts  20.2 us (12%)
  blocking collectives  15.9 us (10%)
  other arithmetic  8.46 us (5%)
  matrix products  5.48 us (3%)
    ppermute x19, starting transfers between devices, send(): return lax.ppermute(x, 'graph', pairs)  25.3 us
    pallas_call x1, Pallas kernels, attend(): pl.pallas_call(attend_kernel, grid_spec=pltpu.PrefetchScalarGridSpec(num_...  21 us
    pallas_call x4, Pallas kernels, transform(): pl.pallas_call(functools.partial(transform_kernel, bounds, first), grid_s...  17.7 us
    all_gather x1, blocking collectives, shards(): tables = lax.all_gather(send_blocks[0], 'graph')[:, place]  15.9 us
    ppermute x19, waiting for transfers between devices, send(): return lax.ppermute(x, 'graph', pairs)  15 us
    all_to_all x1, waiting for transfers between devices, shards(): lax.all_to_all(jnp.concatenate([slices(*parts[0]), share], axis=2), 'feat...  12.2 us
    all_to_all x1, waiting for transfers between devices, shards(): later = lax.all_to_all(slices(*parts[1]), 'feat', 0, 0, tiled=True)  8.52 us
    all_to_all x1, starting transfers between devices, shards(): lax.all_to_all(jnp.concatenate([slices(*parts[0]), share], axis=2), 'feat...  7.63 us
  transfers between devices with their start and end apart: 21, of which 5 were waited for; matrix products, arithmetic and copies ran while one was open for 16% of the time, Pallas kernels for 8%

profile of v2, /device:TPU:1, one launch (start us, length us, event | category | flops | bytes accessed | tf_op | source)
XLA Modules:
  0.0 163.3 jit_solution(7490203652718273487)
XLA Ops:
  0.0 2.2 %copy.37 = bf16[8,8,128,128]{3,2,1,0:T(8,128)(2,1)S(1)} copy(bf16[8,8,128,128]{3,1,2,0:T(8,128)(2,1)} %bitcast.42) | data formatting | bytes 4194304
  2.2 0.5 slice.34
  2.8 1.4 reshape.178
  4.2 1.3 pad_maximum_fusion
  5.5 1.3 copy.26
  6.9 7.6 %all-to-all-start = ((bf16[16,64,640]{2,1,0:T(8,128)(2,1)}), bf16[16,64,640]{2,1,0:T(8,128)(2,1)}, u32[]{:S(2)}, u32[]{:S(2)}) async-start(bf16[16,64,640]{2,1,0:T(8,128)(2,1)} %copy.26), calls=%async_computation | async-start | bytes 2621440 | tf_op jit(solution)/shard_map/all_to_all | solution.py:254
  14.5 2.0 %slice.37 = bf16[64,16,5,128]{3,2,1,0:T(8,128)(2,1)} slice(bf16[64,16,8,128]{3,2,1,0:T(8,128)(2,1)S(1)} %bitcast.39), slice={[0:64], [0:16], [3:8], [0:128]} | slice | bytes 2621440 | tf_op jit(solution)/shard_map/slice | solution.py:249
  16.5 3.3 %reshape.180 = bf16[64,16,640]{2,1,0:T(8,128)(2,1)S(1)} reshape(bf16[64,16,5,128]{3,2,1,0:T(8,128)(2,1)} %slice.37) | data formatting | bytes 2621440 | tf_op jit(solution)/shard_map/reshape | solution.py:249
  19.8 1.4 copy.27
  21.2 12.2 %all-to-all-done = bf16[16,64,640]{2,1,0:T(8,128)(2,1)} async-done(((bf16[16,64,640]{2,1,0:T(8,128)(2,1)}), bf16[16,64,640]{2,1,0:T(8,128)(2,1)}, u32[]{:S(2)}, u32[]{:S(2)}) %all-to-all-start) | async-done | bytes 1310752 | tf_op jit(solution)/shard_map/all_to_all | solution.py:254
  33.4 5.4 %all-to-all-start.1 = ((bf16[16,64,640]{2,1,0:T(8,128)(2,1)}), bf16[16,64,640]{2,1,0:T(8,128)(2,1)S(1)}, u32[]{:S(2)}, u32[]{:S(2)}) async-start(bf16[16,64,640]{2,1,0:T(8,128)(2,1)} %copy.27), calls=%async_computation.1 | async-start | bytes 2621440 | tf_op jit(solution)/shard_map/all_to_all | solution.py:256
  38.8 1.1 slice.36
  39.9 1.3 collective-permute-start
  41.2 0.9 fusion.1
  42.2 0.7 collective-permute-done
  42.9 2.0 %convolution_convert_fusion.1.refs_0_ = bf16[384,512]{1,0:T(8,128)(2,1)S(1)} fusion(bf16[1024,640]{1,0:T(8,128)(2,1)} %bitcast.2, bf16[1024,256]{1,0:T(8,128)(2,1)} %collective-permute-done, bf16[1024,256]{1,0:T(8,128)(2,1)S(1)} %slice.36, pred[]{:T(512)S(6)} %eq.23), kind=kOutput, calls=%fused_computation.4 | convolution fusion | flops 407568384 | bytes 2228225 | tf_op jit(solution)/shard_map/dot_general | solution.py:273
  44.9 1.7 %collective-permute-start.1 = (bf16[384,512]{1,0:T(8,128)(2,1)S(1)}, bf16[384,512]{1,0:T(8,128)(2,1)}, u32[]{:S(2)}, u32[]{:S(2)}) collective-permute-start(bf16[384,512]{1,0:T(8,128)(2,1)S(1)} %convolution_convert_fusion.1.refs_0_), channel_id=1, source_target_pairs={{0,32},{16,48},{32,64},{48,80},{64,96},{80,112},{96,0},{112,16},{1... | collective-permute-start | bytes 1179656 | tf_op jit(solution)/shard_map/ppermute | solution.py:242
  46.6 2.2 %collective-permute-start.3 = (bf16[384,512]{1,0:T(8,128)(2,1)S(1)}, bf16[384,512]{1,0:T(8,128)(2,1)}, u32[]{:S(2)}, u32[]{:S(2)}) collective-permute-start(bf16[384,512]{1,0:T(8,128)(2,1)S(1)} %convolution_convert_fusion.1.refs_0_), channel_id=1, source_target_pairs={{0,96},{16,112},{32,0},{48,16},{64,32},{80,48},{96,64},{112,80},{1... | collective-permute-start | bytes 1179656 | tf_op jit(solution)/shard_map/ppermute | solution.py:242
  48.8 8.5 %all-to-all-done.1 = bf16[16,64,640]{2,1,0:T(8,128)(2,1)S(1)} async-done(((bf16[16,64,640]{2,1,0:T(8,128)(2,1)}), bf16[16,64,640]{2,1,0:T(8,128)(2,1)S(1)}, u32[]{:S(2)}, u32[]{:S(2)}) %all-to-all-start.1) | async-done | bytes 1310752 | tf_op jit(solution)/shard_map/all_to_all | solution.py:256
  57.4 1.1 copy-done.5
  58.4 2.5 %fusion.refs_1_ = bf16[640,512]{1,0:T(8,128)(2,1)S(1)} fusion(bf16[1024,640]{1,0:T(8,128)(2,1)} %bitcast.43, bf16[1024,256]{1,0:T(8,128)(2,1)} %collective-permute-done, bf16[1024,256]{1,0:T(8,128)(2,1)S(1)} %slice.36, pred[]{:T(512)S(6)} %eq.23), kind=kOutput, calls=%fused_computation.3 | convolution fusion | flops 676134912 | bytes 3014657 | tf_op jit(solution)/shard_map/dot_general | solution.py:273
  61.0 0.0 copy-start.8
  61.0 0.0 copy-start.9
  61.0 3.8 %collective-permute-start.7 = (bf16[640,512]{1,0:T(8,128)(2,1)S(1)}, bf16[640,512]{1,0:T(8,128)(2,1)S(1)}, u32[]{:S(2)}, u32[]{:S(2)}) collective-permute-start(bf16[640,512]{1,0:T(8,128)(2,1)S(1)} %fusion.refs_1_), channel_id=1, source_target_pairs={{0,96},{16,112},{32,0},{48,16},{64,32},{80,48},{96,64},{112,80},{1... | collective-permute-start | bytes 1966088 | tf_op jit(solution)/shard_map/ppermute | solution.py:242
  64.9 0.8 copy.31
  65.7 3.5 %collective-permute-start.17 = (bf16[384,512]{1,0:T(8,128)(2,1)S(1)}, bf16[384,512]{1,0:T(8,128)(2,1)}, u32[]{:S(2)}, u32[]{:S(2)}) collective-permute-start(bf16[384,512]{1,0:T(8,128)(2,1)S(1)} %convolution_convert_fusion.1.refs_0_), channel_id=1, source_target_pairs={{0,16},{16,0},{32,48},{48,32},{64,80},{80,64},{96,112},{112,96},{1... | collective-permute-start | bytes 1179656 | tf_op jit(solution)/shard_map/ppermute | solution.py:242
  69.2 1.8 %select_multiply_fusion = f32[512,8]{1,0:T(8,128)} fusion(f32[512,8]{1,0:T(8,128)} %copy.31, s32[8]{0:T(128)S(1)} %and_select_fusion, s32[512]{0:T(512)S(1)} %add_select_fusion.4), kind=kLoop, calls=%fused_computation.17 | loop fusion | flops 12288 | bytes 34848 | tf_op jit(solution)/shard_map/mul | solution.py:214
  71.0 0.0 collective-permute-start.18
  71.0 1.7 %slice.38 = bf16[256,512]{1,0:T(8,128)(2,1)} slice(bf16[384,512]{1,0:T(8,128)(2,1)} %collective-permute-done.1.refs_0_), slice={[0:256], [0:512]} | slice | bytes 524288 | tf_op jit(solution)/shard_map/slice | solution.py:282
  72.7 0.1 pad.11.clone
  72.8 0.9 slice.39
  73.7 0.0 collective-permute-done.17.refs_2_
  73.7 3.0 %collective-permute-start.4 = (bf16[128,512]{1,0:T(8,128)(2,1)S(1)}, bf16[128,512]{1,0:T(8,128)(2,1)S(1)}, u32[]{:S(2)}, u32[]{:S(2)}) collective-permute-start(bf16[128,512]{1,0:T(8,128)(2,1)S(1)} %slice.39), channel_id=1, source_target_pairs={{0,96},{16,112},{32,0},{48,16},{64,32},{80,48},{96,64},{112,80},{1... | collective-permute-start | bytes 393224 | tf_op jit(solution)/shard_map/ppermute | solution.py:242
  76.7 0.0 collective-permute-done.7.refs_1_
  76.7 4.4 %collective-permute-start.15 = (bf16[384,512]{1,0:T(8,128)(2,1)}, bf16[384,512]{1,0:T(8,128)(2,1)}, u32[]{:S(2)}, u32[]{:S(2)}) collective-permute-start(bf16[384,512]{1,0:T(8,128)(2,1)} %collective-permute-done.1.refs_0_), channel_id=1, source_target_pairs={{0,16},{16,0},{32,48},{48,32},{64,80},{80,64},{96,112},{112,96},{1... | collective-permute-start | bytes 1179656 | tf_op jit(solution)/shard_map/ppermute | solution.py:242
  81.2 0.1 maximum_maximum_fusion.refs_5_.refs_9_
  81.3 0.8 slice.41
  82.0 0.6 collective-permute-start.13
  82.6 9.9 %collective-permute-done.2.refs_0_ = bf16[256,512]{1,0:T(8,128)(2,1)} collective-permute-done((bf16[256,512]{1,0:T(8,128)(2,1)}, bf16[256,512]{1,0:T(8,128)(2,1)}, u32[]{:S(2)}, u32[]{:S(2)}) %collective-permute-start.2) | collective-permute-done | bytes 262176 | tf_op jit(solution)/shard_map/ppermute | solution.py:242
  92.5 0.0 collective-permute-start.8
  92.5 0.9 collective-permute-start.16
  93.4 0.6 fusion.16.slot_ref
  94.0 15.9 %all_gather.3 = s32[8,8,4]{1,2,0:T(4,128)S(1)} all-gather(s32[1,8,4]{1,2,0:T(4,128)S(1)} %copy-done.9), channel_id=1, replica_groups=mesh['graph'=8,'feat'=16] {'graph'}, dimensions={0}, use_global_device_ids=true | all-gather | bytes 1152 | tf_op jit(solution)/shard_map/all_gather | solution.py:263
  109.9 1.6 collective-permute-start.6
  111.5 0.0 collective-permute-done.15.refs_2_
  111.5 0.5 collective-permute-start.14
  112.0 0.1 constant_dynamic-slice_fusion
  112.1 1.8 %fusion.7 = (bf16[1,512,128]{2,1,0:T(8,128)(2,1)}, bf16[1,512,128]{2,1,0:T(8,128)(2,1)}, bf16[1,512,128]{2,1,0:T(8,128)(2,1)}) fusion(f32[512,8]{1,0:T(8,128)} %select_multiply_fusion), kind=kLoop, calls=%fused_computation.19 | loop fusion | flops 458752 | bytes 409600 | tf_op jit(solution)/shard_map/stack | solution.py:216
  113.9 0.0 collective-permute-start.12
  113.9 0.7 collective-permute-start.9
  114.7 4.3 %collective-permute-done.6.refs_2_ = bf16[256,512]{1,0:T(8,128)(2,1)} collective-permute-done((bf16[256,512]{1,0:T(8,128)(2,1)S(1)}, bf16[256,512]{1,0:T(8,128)(2,1)}, u32[]{:S(2)}, u32[]{:S(2)}) %collective-permute-start.6) | collective-permute-done | bytes 262176 | tf_op jit(solution)/shard_map/ppermute | solution.py:242
  119.0 1.0 collective-permute-start.11
  120.0 0.1 copy.29
  120.1 0.1 copy.30
  120.2 0.6 gather_fusion
  120.8 1.8 %pad_maximum_fusion.2.tgt_ref = bf16[3,512,128]{2,1,0:T(8,128)(2,1)} fusion(bf16[1,512,128]{2,1,0:T(8,128)(2,1)} %get-tuple-element.22, bf16[1,512,128]{2,1,0:T(8,128)(2,1)} %get-tuple-element.23, bf16[1,512,128]{2,1,0:T(8,128)(2,1)} %get-tuple-element.21), kind=kLoop, calls=%fused_computation.11 | loop fusion | flops 393216 | bytes 786432 | tf_op jit(solution)/shard_map/stack | solution.py:216
  122.6 0.0 collective-permute-start.10
  122.6 1.1 pad_maximum_fusion.1.own_ref
  123.7 4.2 %transform.4 = (bf16[8,4,2,128,512]{4,3,2,1,0:T(8,128)(2,1)}, f32[8,4,8,128]{3,2,1,0:T(8,128)S(1)}) custom-call(s32[8,4]{1,0:T(8,128)S(1)} %gather_fusion, bf16[384,512]{1,0:T(8,128)(2,1)S(1)} %convolution_convert_fusion.1.refs_0_, bf16[640,512]{1,0:T(8,128)(2,1)S(1)} %fusion.refs_1_, bf16[384,512]{1,0:T(8,128)(2,1)} %collective-permute-done.17.refs_2_, ...), custom_call_target="tpu_custom_call" | custom-call | tf_op jit(solution)/shard_map/transform/pallas_call | solution.py:80
  127.9 4.5 %transform.5 = (bf16[8,4,2,128,512]{4,3,2,1,0:T(8,128)(2,1)}, f32[8,4,8,128]{3,2,1,0:T(8,128)S(1)}) custom-call(s32[8,4]{1,0:T(8,128)S(1)} %gather_fusion, bf16[384,512]{1,0:T(8,128)(2,1)} %collective-permute-done.1.refs_0_, bf16[640,512]{1,0:T(8,128)(2,1)S(1)} %collective-permute-done.5.refs_1_, ...), custom_call_target="tpu_custom_call", output_to_operand_aliasing={{0}: (7, {}), {1}: (8, {})} | custom-call | tf_op jit(solution)/shard_map/transform/pallas_call | solution.py:80
  132.5 4.6 %transform.6 = (bf16[8,4,2,128,512]{4,3,2,1,0:T(8,128)(2,1)}, f32[8,4,8,128]{3,2,1,0:T(8,128)S(1)}) custom-call(s32[8,4]{1,0:T(8,128)S(1)} %gather_fusion, bf16[384,512]{1,0:T(8,128)(2,1)} %collective-permute-done.3.refs_0_, bf16[640,512]{1,0:T(8,128)(2,1)S(1)} %collective-permute-done.7.refs_1_, ...), custom_call_target="tpu_custom_call", output_to_operand_aliasing={{0}: (7, {}), {1}: (8, {})} | custom-call | tf_op jit(solution)/shard_map/transform/pallas_call | solution.py:80
  137.1 4.3 %transform.7 = (bf16[8,4,2,128,512]{4,3,2,1,0:T(8,128)(2,1)}, f32[8,4,8,128]{3,2,1,0:T(8,128)S(1)}) custom-call(s32[8,4]{1,0:T(8,128)S(1)} %gather_fusion, bf16[256,512]{1,0:T(8,128)(2,1)} %collective-permute-done.2.refs_0_, bf16[128,512]{1,0:T(8,128)(2,1)S(1)} %copy-done.4, ...), custom_call_target="tpu_custom_call", output_to_operand_aliasing={{0}: (11, {}), {1}: (12, {})} | custom-call | tf_op jit(solution)/shard_map/transform/pallas_call | solution.py:80
  141.5 0.6 copy-done.2
  142.1 21.0 %attend.1 = bf16[1024,512]{1,0:T(8,128)(2,1)} custom-call(s32[8,12]{1,0:T(8,128)} %rel_ref.1, s32[8,12]{1,0:T(8,128)} %fusion.16.slot_ref, bf16[1024,512]{1,0:T(8,128)(2,1)} %pad_maximum_fusion.1.own_ref, s32[8,12,128,128]{3,2,1,0:T(8,128)} %mask_ref.1, bf16[32,2,128,512]{3,2,1,0:T(8,128)(2,1)} %bitcast.37, f32[32,8,128]{2,1,0:T(8,128)} %bitcast.36, ...), custom_call_target="tpu_custom_call" | custom-call | tf_op jit(solution)/shard_map/attend/pallas_call | solution.py:172
  (45 shorter events, 0.2 us)
Async XLA Ops:
  0.0 4.2 %copy-start = (bf16[64,512]{1,0:T(8,128)(2,1)S(1)}, bf16[64,512]{1,0:T(8,128)(2,1)}, u32[]{:S(2)}) copy-start(bf16[64,512]{1,0:T(8,128)(2,1)} %param.10) | copy-start | bytes 196612
  6.9 26.5 %all-to-all-start = ((bf16[16,64,640]{2,1,0:T(8,128)(2,1)}), bf16[16,64,640]{2,1,0:T(8,128)(2,1)}, u32[]{:S(2)}, u32[]{:S(2)}) async-start(bf16[16,64,640]{2,1,0:T(8,128)(2,1)} %copy.26), calls=%async_computation | async-start | bytes 2621440 | tf_op jit(solution)/shard_map/all_to_all | solution.py:254
  21.2 20.0 %copy-start.7 = (f32[2,512]{1,0:T(2,128)S(1)}, f32[2,512]{1,0:T(2,128)}, u32[]{:S(2)}) copy-start(f32[2,512]{1,0:T(2,128)} %param.12) | copy-start | bytes 12292
  21.2 20.0 %copy-start.1 = (bf16[2,512,512]{2,1,0:T(8,128)(2,1)S(1)}, bf16[2,512,512]{2,1,0:T(8,128)(2,1)}, u32[]{:S(2)}) copy-start(bf16[2,512,512]{2,1,0:T(8,128)(2,1)} %refs_8_.1) | copy-start | bytes 3145732
  33.4 24.0 %all-to-all-start.1 = ((bf16[16,64,640]{2,1,0:T(8,128)(2,1)}), bf16[16,64,640]{2,1,0:T(8,128)(2,1)S(1)}, u32[]{:S(2)}, u32[]{:S(2)}) async-start(bf16[16,64,640]{2,1,0:T(8,128)(2,1)} %copy.27), calls=%async_computation.1 | async-start | bytes 2621440 | tf_op jit(solution)/shard_map/all_to_all | solution.py:256
  39.9 3.0 %collective-permute-start = (bf16[1024,256]{1,0:T(8,128)(2,1)S(1)}, bf16[1024,256]{1,0:T(8,128)(2,1)}, u32[]{:S(2)}, u32[]{:S(2)}) collective-permute-start(bf16[1024,256]{1,0:T(8,128)(2,1)S(1)} %slice.36), channel_id=1, source_target_pairs={{0,16},{16,0},{32,48},{48,32},{64,80},{80,64},{96,112},{112,96},{1... | collective-permute-start | bytes 1572872 | tf_op jit(solution)/shard_map/ppermute | solution.py:242
  44.9 26.1 %collective-permute-start.1 = (bf16[384,512]{1,0:T(8,128)(2,1)S(1)}, bf16[384,512]{1,0:T(8,128)(2,1)}, u32[]{:S(2)}, u32[]{:S(2)}) collective-permute-start(bf16[384,512]{1,0:T(8,128)(2,1)S(1)} %convolution_convert_fusion.1.refs_0_), channel_id=1, source_target_pairs={{0,32},{16,48},{32,64},{48,80},{64,96},{80,112},{96,0},{112,16},{1... | collective-permute-start | bytes 1179656 | tf_op jit(solution)/shard_map/ppermute | solution.py:242
  46.6 26.0 %collective-permute-start.3 = (bf16[384,512]{1,0:T(8,128)(2,1)S(1)}, bf16[384,512]{1,0:T(8,128)(2,1)}, u32[]{:S(2)}, u32[]{:S(2)}) collective-permute-start(bf16[384,512]{1,0:T(8,128)(2,1)S(1)} %convolution_convert_fusion.1.refs_0_), channel_id=1, source_target_pairs={{0,96},{16,112},{32,0},{48,16},{64,32},{80,48},{96,64},{112,80},{1... | collective-permute-start | bytes 1179656 | tf_op jit(solution)/shard_map/ppermute | solution.py:242
  57.4 1.1 copy-start.5
  58.4 6.4 %copy-start.6 = (f32[2,512]{1,0:T(2,128)S(1)}, f32[2,512]{1,0:T(2,128)}, u32[]{:S(2)}) copy-start(f32[2,512]{1,0:T(2,128)} %param.13) | copy-start | bytes 12292
  61.0 32.4 %copy-start.8 = (s32[8,12]{1,0:T(8,128)S(1)}, s32[8,12]{1,0:T(8,128)}, u32[]{:S(2)}) copy-start(s32[8,12]{1,0:T(8,128)} %param.17) | copy-start | bytes 1156
  61.0 33.0 %copy-start.9 = (s32[1,8,4]{1,2,0:T(4,128)S(1)}, s32[1,8,4]{1,2,0:T(4,128)}, u32[]{:S(2)}) copy-start(s32[1,8,4]{1,2,0:T(4,128)} %param.16) | copy-start | bytes 388
  61.0 15.7 %collective-permute-start.7 = (bf16[640,512]{1,0:T(8,128)(2,1)S(1)}, bf16[640,512]{1,0:T(8,128)(2,1)S(1)}, u32[]{:S(2)}, u32[]{:S(2)}) collective-permute-start(bf16[640,512]{1,0:T(8,128)(2,1)S(1)} %fusion.refs_1_), channel_id=1, source_target_pairs={{0,96},{16,112},{32,0},{48,16},{64,32},{80,48},{96,64},{112,80},{1... | collective-permute-start | bytes 1966088 | tf_op jit(solution)/shard_map/ppermute | solution.py:242
  65.7 8.0 %collective-permute-start.17 = (bf16[384,512]{1,0:T(8,128)(2,1)S(1)}, bf16[384,512]{1,0:T(8,128)(2,1)}, u32[]{:S(2)}, u32[]{:S(2)}) collective-permute-start(bf16[384,512]{1,0:T(8,128)(2,1)S(1)} %convolution_convert_fusion.1.refs_0_), channel_id=1, source_target_pairs={{0,16},{16,0},{32,48},{48,32},{64,80},{80,64},{96,112},{112,96},{1... | collective-permute-start | bytes 1179656 | tf_op jit(solution)/shard_map/ppermute | solution.py:242
  69.2 23.3 %collective-permute-start.5 = (bf16[640,512]{1,0:T(8,128)(2,1)S(1)}, bf16[640,512]{1,0:T(8,128)(2,1)S(1)}, u32[]{:S(2)}, u32[]{:S(2)}) collective-permute-start(bf16[640,512]{1,0:T(8,128)(2,1)S(1)} %fusion.refs_1_), channel_id=1, source_target_pairs={{0,32},{16,48},{32,64},{48,80},{64,96},{80,112},{96,0},{112,16},{1... | collective-permute-start | bytes 1966088 | tf_op jit(solution)/shard_map/ppermute | solution.py:242
  71.0 38.9 %collective-permute-start.18 = (bf16[640,512]{1,0:T(8,128)(2,1)S(1)}, bf16[640,512]{1,0:T(8,128)(2,1)}, u32[]{:S(2)}, u32[]{:S(2)}) collective-permute-start(bf16[640,512]{1,0:T(8,128)(2,1)S(1)} %fusion.refs_1_), channel_id=1, source_target_pairs={{0,16},{16,0},{32,48},{48,32},{64,80},{80,64},{96,112},{112,96},{1... | collective-permute-start | bytes 1966088 | tf_op jit(solution)/shard_map/ppermute | solution.py:242
  72.7 19.8 %collective-permute-start.2 = (bf16[256,512]{1,0:T(8,128)(2,1)}, bf16[256,512]{1,0:T(8,128)(2,1)}, u32[]{:S(2)}, u32[]{:S(2)}) collective-permute-start(bf16[256,512]{1,0:T(8,128)(2,1)} %slice.38), channel_id=1, source_target_pairs={{0,32},{16,48},{32,64},{48,80},{64,96},{80,112},{96,0},{112,16},{1... | collective-permute-start | bytes 786440 | tf_op jit(solution)/shard_map/ppermute | solution.py:242
  73.7 8.3 %collective-permute-start.4 = (bf16[128,512]{1,0:T(8,128)(2,1)S(1)}, bf16[128,512]{1,0:T(8,128)(2,1)S(1)}, u32[]{:S(2)}, u32[]{:S(2)}) collective-permute-start(bf16[128,512]{1,0:T(8,128)(2,1)S(1)} %slice.39), channel_id=1, source_target_pairs={{0,96},{16,112},{32,0},{48,16},{64,32},{80,48},{96,64},{112,80},{1... | collective-permute-start | bytes 393224 | tf_op jit(solution)/shard_map/ppermute | solution.py:242
  76.7 34.8 %collective-permute-start.15 = (bf16[384,512]{1,0:T(8,128)(2,1)}, bf16[384,512]{1,0:T(8,128)(2,1)}, u32[]{:S(2)}, u32[]{:S(2)}) collective-permute-start(bf16[384,512]{1,0:T(8,128)(2,1)} %collective-permute-done.1.refs_0_), channel_id=1, source_target_pairs={{0,16},{16,0},{32,48},{48,32},{64,80},{80,64},{96,112},{112,96},{1... | collective-permute-start | bytes 1179656 | tf_op jit(solution)/shard_map/ppermute | solution.py:242
  82.0 10.5 %copy-start.3 = (bf16[128,512]{1,0:T(8,128)(2,1)}, bf16[128,512]{1,0:T(8,128)(2,1)S(1)}, u32[]{:S(2)}) copy-start(bf16[128,512]{1,0:T(8,128)(2,1)S(1)} %collective-permute-done.4.refs_1_) | copy-start | bytes 393220
  82.0 31.9 %collective-permute-start.13 = (bf16[384,512]{1,0:T(8,128)(2,1)}, bf16[384,512]{1,0:T(8,128)(2,1)}, u32[]{:S(2)}, u32[]{:S(2)}) collective-permute-start(bf16[384,512]{1,0:T(8,128)(2,1)} %collective-permute-done.3.refs_0_), channel_id=1, source_target_pairs={{0,16},{16,0},{32,48},{48,32},{64,80},{80,64},{96,112},{112,96},{1... | collective-permute-start | bytes 1179656 | tf_op jit(solution)/shard_map/ppermute | solution.py:242
  92.5 21.4 %collective-permute-start.8 = (bf16[384,512]{1,0:T(8,128)(2,1)}, bf16[384,512]{1,0:T(8,128)(2,1)}, u32[]{:S(2)}, u32[]{:S(2)}) collective-permute-start(bf16[384,512]{1,0:T(8,128)(2,1)} %slice.41), channel_id=1, source_target_pairs={{0,96},{16,112},{32,0},{48,16},{64,32},{80,48},{96,64},{112,80},{1... | collective-permute-start | bytes 1179656 | tf_op jit(solution)/shard_map/ppermute | solution.py:242
  92.5 30.1 %collective-permute-start.16 = (bf16[640,512]{1,0:T(8,128)(2,1)S(1)}, bf16[640,512]{1,0:T(8,128)(2,1)}, u32[]{:S(2)}, u32[]{:S(2)}) collective-permute-start(bf16[640,512]{1,0:T(8,128)(2,1)S(1)} %collective-permute-done.5.refs_1_), channel_id=1, source_target_pairs={{0,16},{16,0},{32,48},{48,32},{64,80},{80,64},{96,112},{112,96},{1... | collective-permute-start | bytes 1966088 | tf_op jit(solution)/shard_map/ppermute | solution.py:242
  109.9 9.1 %collective-permute-start.6 = (bf16[256,512]{1,0:T(8,128)(2,1)S(1)}, bf16[256,512]{1,0:T(8,128)(2,1)}, u32[]{:S(2)}, u32[]{:S(2)}) collective-permute-start(bf16[256,512]{1,0:T(8,128)(2,1)S(1)} %slice.40), channel_id=1, source_target_pairs={{0,32},{16,48},{32,64},{48,80},{64,96},{80,112},{96,0},{112,16},{1... | collective-permute-start | bytes 786440 | tf_op jit(solution)/shard_map/ppermute | solution.py:242
  111.5 20.9 %collective-permute-start.14 = (bf16[640,512]{1,0:T(8,128)(2,1)S(1)}, bf16[640,512]{1,0:T(8,128)(2,1)}, u32[]{:S(2)}, u32[]{:S(2)}) collective-permute-start(bf16[640,512]{1,0:T(8,128)(2,1)S(1)} %collective-permute-done.7.refs_1_), channel_id=1, source_target_pairs={{0,16},{16,0},{32,48},{48,32},{64,80},{80,64},{96,112},{112,96},{1... | collective-permute-start | bytes 1966088 | tf_op jit(solution)/shard_map/ppermute | solution.py:242
  113.9 23.3 %collective-permute-start.12 = (bf16[384,512]{1,0:T(8,128)(2,1)}, bf16[384,512]{1,0:T(8,128)(2,1)}, u32[]{:S(2)}, u32[]{:S(2)}) collective-permute-start(bf16[384,512]{1,0:T(8,128)(2,1)} %collective-permute-done.8.refs_3_), channel_id=1, source_target_pairs={{0,16},{16,0},{32,48},{48,32},{64,80},{80,64},{96,112},{112,96},{1... | collective-permute-start | bytes 1179656 | tf_op jit(solution)/shard_map/ppermute | solution.py:242
  113.9 23.2 %collective-permute-start.9 = (bf16[256,512]{1,0:T(8,128)(2,1)}, bf16[256,512]{1,0:T(8,128)(2,1)}, u32[]{:S(2)}, u32[]{:S(2)}) collective-permute-start(bf16[256,512]{1,0:T(8,128)(2,1)} %collective-permute-done.2.refs_0_), channel_id=1, source_target_pairs={{0,16},{16,0},{32,48},{48,32},{64,80},{80,64},{96,112},{112,96},{1... | collective-permute-start | bytes 786440 | tf_op jit(solution)/shard_map/ppermute | solution.py:242
  119.0 18.1 %collective-permute-start.11 = (bf16[256,512]{1,0:T(8,128)(2,1)}, bf16[256,512]{1,0:T(8,128)(2,1)}, u32[]{:S(2)}, u32[]{:S(2)}) collective-permute-start(bf16[256,512]{1,0:T(8,128)(2,1)} %collective-permute-done.6.refs_2_), channel_id=1, source_target_pairs={{0,16},{16,0},{32,48},{48,32},{64,80},{80,64},{96,112},{112,96},{1... | collective-permute-start | bytes 786440 | tf_op jit(solution)/shard_map/ppermute | solution.py:242
  122.6 14.5 %collective-permute-start.10 = (bf16[128,512]{1,0:T(8,128)(2,1)}, bf16[128,512]{1,0:T(8,128)(2,1)S(1)}, u32[]{:S(2)}, u32[]{:S(2)}) collective-permute-start(bf16[128,512]{1,0:T(8,128)(2,1)} %copy-done.3), channel_id=1, source_target_pairs={{0,16},{16,0},{32,48},{48,32},{64,80},{80,64},{96,112},{112,96},{1... | collective-permute-start | bytes 393224 | tf_op jit(solution)/shard_map/ppermute | solution.py:242
  132.5 4.7 %copy-start.4 = (bf16[128,512]{1,0:T(8,128)(2,1)S(1)}, bf16[128,512]{1,0:T(8,128)(2,1)}, u32[]{:S(2)}) copy-start(bf16[128,512]{1,0:T(8,128)(2,1)} %copy-done.3) | copy-start | bytes 393220
  141.5 0.6 copy-start.2

commit v3 on v2

--- a/solution.py
+++ b/solution.py
@@ -12,6 +12,72 @@
 LOG2E = 1.4426950408889634
 F32 = jnp.float32
 BF16 = jnp.bfloat16
+
+
+def arrange_kernel(x_ref, out_ref, sem):
+    peers, _, rows = out_ref.shape
+    copies = [
+        pltpu.make_async_copy(x_ref.at[:, pl.ds(q * rows, rows)], out_ref.at[q], sem.at[q]) for q in range(peers)
+    ]
+    for c in copies:
+        c.start()
+    for c in copies:
+        c.wait()
+
+
+def arrange(features, peers):
+    depth, columns = features.shape
+    return pl.pallas_call(
+        arrange_kernel,
+        in_specs=[pl.BlockSpec(memory_space=pltpu.HBM)],
+        out_specs=pl.BlockSpec(memory_space=pltpu.HBM),
+        out_shape=jax.ShapeDtypeStruct((peers, depth, columns // peers), BF16),
+        scratch_shapes=[pltpu.SemaphoreType.DMA((peers,))],
+        name="arrange",
+    )(features)
+
+
+def project_kernel(row_ref, x_ref, mine_ref, other_ref, out_ref, w_ref, sem):
+    pieces, part = mine_ref.shape[:2]
+
+    @pl.when(pl.program_id(0) == 0)
+    def _():
+        copies = []
+        for n in range(pieces):
+            for which, ref in enumerate((mine_ref, other_ref)):
+                row = pl.multiple_of(row_ref[which, n], part)
+                copies.append(pltpu.make_async_copy(ref.at[n], w_ref.at[pl.ds(row, part)], sem.at[which, n]))
+        for c in copies:
+            c.start()
+        for c in copies:
+            c.wait()
+
+    out_ref[...] = lax.dot_general(
+        x_ref[...], w_ref[...], (((0,), (0,)), ((), ())), preferred_element_type=F32
+    ).astype(BF16)
+
+
+def project(x, mine, other, place):
+    depth, rows = x.shape
+    pieces, part, width = mine.shape
+    step = rows // 4
+    return pl.pallas_call(
+        project_kernel,
+        grid_spec=pltpu.PrefetchScalarGridSpec(
+            num_scalar_prefetch=1,
+            grid=(rows // step,),
+            in_specs=[
+                pl.BlockSpec((depth, step), lambda i, *_: (0, i)),
+                pl.BlockSpec(memory_space=pl.ANY),
+                pl.BlockSpec(memory_space=pl.ANY),
+            ],
+            out_specs=pl.BlockSpec((step, width), lambda i, *_: (i, 0)),
+            scratch_shapes=[pltpu.VMEM((depth, width), BF16), pltpu.SemaphoreType.DMA((2, pieces))],
+        ),
+        out_shape=jax.ShapeDtypeStruct((rows, width), BF16),
+        compiler_params=pltpu.CompilerParams(vmem_limit_bytes=32 * 1024 * 1024),
+        name="project",
+    )(place, x, mine, other)
 
 
 def three_parts(x):
@@ -233,69 +299,65 @@
     depth, width = proj_weight.shape
     n_feat = lax.axis_size("feat")
     n_graph = lax.axis_size("graph")
-    depth_z = n_graph // 2
+    levels = n_graph // 2
+    side = 4
     place = lax.axis_index("graph")
     core, level = lax.rem(place, 2), place // 2
 
-    def send(x, levels, cores=0):
-        pairs = [(p, (p + 2 * levels) % n_graph ^ cores) for p in range(n_graph)]
+    def send(x, up, cores=0):
+        pairs = [(p, (p + 2 * up) % n_graph ^ cores) for p in range(n_graph)]
         return lax.ppermute(x, "graph", pairs)
 
-    cut = 3
-    parts = ((0, cut), (cut, local_blocks))
-    features = node_features.T.reshape(depth, n_feat, local_blocks, block_rows)
-
-    def slices(low, high):
-        return features[:, :, low:high].reshape(depth, n_feat, (high - low) * block_rows).transpose(1, 0, 2)
-
-    half = width // 2
-    share = lax.dynamic_slice(proj_weight, (0, core * half), (depth, half))
-    share = jnp.broadcast_to(share[None], (n_feat, depth, half))
-    got = lax.all_to_all(jnp.concatenate([slices(*parts[0]), share], axis=2), "feat", 0, 0, tiled=True)
-    got = got.reshape(n_feat * depth, cut * block_rows + half)
-    later = lax.all_to_all(slices(*parts[1]), "feat", 0, 0, tiled=True)
-    later = later.reshape(n_feat * depth, (local_blocks - cut) * block_rows)
-    mine = got[:, cut * block_rows :]
+    def shift(x, right, ahead):
+        pairs = [(q, (q // side + ahead) % side * side + (q + right) % side) for q in range(n_feat)]
+        return lax.ppermute(x, "feat", pairs)
+
+    outgoing = arrange(node_features.T, n_feat)
+    got = lax.all_to_all(outgoing, "feat", 0, 0, tiled=True).reshape(n_feat * depth, rows_local)
+
+    half = depth // 2
+    share = lax.dynamic_slice(proj_weight, (core * half, 0), (half, width))
+    row = jnp.stack([share] + [shift(share, d, 0) for d in range(1, side)])
+    mine = jnp.concatenate([row] + [shift(row, 0, d) for d in range(1, side)])
     other = send(mine, 0, 1)
-    whole = jnp.where(core == 0, jnp.concatenate([mine, other], axis=1), jnp.concatenate([other, mine], axis=1))
-
+    here = lax.axis_index("feat")
+    piece = jnp.arange(n_feat)
+    owner = (here // side - piece // side + side) % side * side + (here - piece + n_feat) % side
+    begins = (owner * depth + jnp.stack([core, 1 - core])[:, None] * half).astype(jnp.int32)
+
+    tables = jnp.stack([send_blocks[0]] + [send(send_blocks[0], d) for d in range(1, levels)])
+    tables = jnp.stack([tables, send(tables, 0, 1)], axis=1)
+    order = jnp.array([0, 1, 3, 2])
+    index = tables[order, :, place].reshape(n_graph, CAP)
+    peer = source_slots // CAP
+    distance = (level - peer // 2 + levels) % levels
+    slots = (2 * (distance ^ (distance >> 1)) + (peer % 2 ^ core)) * CAP + source_slots % CAP
     src_vectors, tgt_vectors = score_vectors(relation_weight, att_source, att_target)
-    tables = lax.all_gather(send_blocks[0], "graph")[:, place]
-    relative = jnp.arange(n_graph)
-    index = tables[2 * lax.rem(level - relative // 2 + depth_z, depth_z) + (relative % 2 ^ core)]
-    peer = source_slots // CAP
-    distance = lax.rem(level - peer // 2 + depth_z, depth_z)
-    slots = (2 * distance + (peer % 2 ^ core)) * CAP + source_slots % CAP
-
-    hidden = []
-    sources = [[] for _ in range(n_graph)]
-    for (low, high), x in zip(parts, (got[:, : cut * block_rows], later)):
-        part = lax.dot_general(x, whole, (((0,), (0,)), ((), ())), preferred_element_type=F32).astype(BF16)
-        hidden.append(part)
-        middle = (high - low + (low == 0)) // 2
-        split = middle * block_rows
-        up, down = send(part, 1), send(part, -1)
-        arrived = (
-            (0, part, low, high),
-            (1, up, low, high),
-            (3, down, low, high),
-            (2, send(up[:split], 1), low, low + middle),
-            (2, send(down[split:], -1), low + middle, high),
-        )
-        for steps, array, first, end in arrived:
-            sources[2 * steps].append((array, first, end))
-            sources[2 * steps + 1].append((send(array, 0, 1), first, end))
-
+
+    hidden = project(got, mine, other, begins)
+    middle = local_blocks // 2
+    split = middle * block_rows
+    up, down = send(hidden, 1), send(hidden, -1)
+    far = (send(up[:split], 1), send(down[split:], -1))
+    groups = []
+    for arrived in (
+        (((hidden, 0, local_blocks),),),
+        (((up, 0, local_blocks),), ((down, 0, local_blocks),)),
+        (((far[0], 0, middle), (far[1], middle, local_blocks)),),
+    ):
+        group = []
+        for pieces in arrived:
+            group.append(pieces)
+            group.append([(send(x, 0, 1), low, high) for x, low, high in pieces])
+        groups.append(group)
     values = scores = None
-    index = index.astype(jnp.int32)
-    for group in ((0, 1), (2, 3), (6, 7), (4, 5)):
-        values, scores = transform(
-            [sources[s] for s in group], group[0], index, relation_weight, src_vectors, block_rows, values, scores
-        )
+    first = 0
+    for group in groups:
+        values, scores = transform(group, first, index, relation_weight, src_vectors, block_rows, values, scores)
+        first += len(group)
     total = n_graph * CAP
     values = values.reshape((total,) + values.shape[2:])
     scores = scores.reshape((total,) + scores.shape[2:])
-    hidden = jnp.concatenate(hidden, axis=0)
     return attend(hidden, edge_mask, relation_ids, slots, values, scores, tgt_vectors)
 
 

time: 164 us -> 215 us (1.31)
  Pallas kernels: 38.7 us -> 105 us
  waiting for transfers between devices: 35.7 us -> 52.2 us
  blocking collectives: 15.9 us -> 0 us
  other arithmetic: 8.46 us -> 2.66 us
  local copies, waits for them, and re-layouts: 20.2 us -> 15.3 us
  matrix products: 5.48 us -> 1.59 us
    pallas_call x0 -> x2, Pallas kernels: none -> 69.4 us  [the longest x1 64.8 us: arrange(): pl.pallas_call(arrange_kernel, in_specs=[pl.BlockSpec(memory_space=pltpu....]
    ppermute x0 -> x6, waiting for transfers between devices: none -> 24.2 us  [shift(): return lax.ppermute(x, 'feat', pairs)]
    all_to_all x2 -> x1, waiting for transfers between devices: 20.7 us -> 0.01 us  [shards(): lax.all_to_all(outgoing, 'feat', 0, 0, tiled=True)]
    all_gather x1 -> x0, blocking collectives: 15.9 us -> none  [shards(): tables = lax.all_gather(send_blocks[0], 'graph')[:, place]]
    ppermute x19 -> x14, waiting for transfers between devices: 15 us -> 28 us  [send(): return lax.ppermute(x, 'graph', pairs)]
    ppermute x0 -> x6, starting transfers between devices: none -> 7.38 us  [shift(): return lax.ppermute(x, 'feat', pairs)]
    unnamed x21 -> x32, local copies, waits for them, and re-layouts: 3.93 us -> 10.3 us
    all_to_all x2 -> x1, starting transfers between devices: 13.1 us -> 7.73 us  [shards(): lax.all_to_all(outgoing, 'feat', 0, 0, tiled=True)]
  transfers between devices with their start and end apart: 21 -> 21, of which waited for: 5 -> 7; matrix products, arithmetic and copies ran while one was open for 16% -> 6% of each run, Pallas kernels for 8% -> 7%
where the time goes in v3:
time: 215 us; the launch traced here: 214 us
  Pallas kernels  105 us (49%)
  waiting for transfers between devices  52.2 us (24%)
  starting transfers between devices  36.8 us (17%)
  local copies, waits for them, and re-layouts  15.3 us (7%)
  other arithmetic  2.66 us (1%)
    pallas_call x1, Pallas kernels, arrange(): pl.pallas_call(arrange_kernel, in_specs=[pl.BlockSpec(memory_space=pltpu....  64.8 us
    ppermute x14, waiting for transfers between devices, send(): return lax.ppermute(x, 'graph', pairs)  28 us
    ppermute x6, waiting for transfers between devices, shift(): return lax.ppermute(x, 'feat', pairs)  24.2 us
    ppermute x14, starting transfers between devices, send(): return lax.ppermute(x, 'graph', pairs)  21.7 us
    pallas_call x1, Pallas kernels, attend(): pl.pallas_call(attend_kernel, grid_spec=pltpu.PrefetchScalarGridSpec(num_...  21 us
    pallas_call x3, Pallas kernels, transform(): pl.pallas_call(functools.partial(transform_kernel, bounds, first), grid_s...  15 us
    unnamed x32, local copies, waits for them, and re-layouts  10.3 us
    all_to_all x1, starting transfers between devices, shards(): lax.all_to_all(outgoing, 'feat', 0, 0, tiled=True)  7.73 us
  transfers between devices with their start and end apart: 21, of which 7 were waited for; matrix products, arithmetic and copies ran while one was open for 6% of the time, Pallas kernels for 7%

profile of v3, /device:TPU:1, one launch (start us, length us, event | category | flops | bytes accessed | tf_op | source)
XLA Modules:
  0.0 214.4 jit_solution(5222863573542111305)
XLA Ops:
  0.0 64.8 %arrange.1 = bf16[16,64,1024]{2,1,0:T(8,128)(2,1)} custom-call(bf16[64,16384]{1,0:T(8,128)(2,1)} %bitcast.50), custom_call_target="tpu_custom_call" | custom-call | tf_op jit(solution)/shard_map/arrange/pallas_call | solution.py:30
  64.8 0.0 copy-start
  64.8 7.7 %all-to-all-start = ((bf16[16,64,1024]{2,1,0:T(8,128)(2,1)}), bf16[16,64,1024]{2,1,0:T(8,128)(2,1)S(1)}, u32[]{:S(2)}, u32[]{:S(2)}) async-start(bf16[16,64,1024]{2,1,0:T(8,128)(2,1)} %arrange.1), calls=%async_computation | async-start | bytes 4194304 | tf_op jit(solution)/shard_map/all_to_all | solution.py:316
  72.6 0.6 constant_dynamic-update-slice_fusion.6
  73.2 1.3 collective-permute-start
  74.5 2.4 %collective-permute-start.1 = (bf16[32,512]{1,0:T(8,128)(2,1)S(1)}, bf16[32,512]{1,0:T(8,128)(2,1)S(1)}, u32[]{:S(2)}, u32[]{:S(2)}) collective-permute-start(bf16[32,512]{1,0:T(8,128)(2,1)S(1)} %get-tuple-element.18), channel_id=1, source_target_pairs={{0,2},{1,3},{2,0},{3,1},{4,6},{5,7},{6,4},{7,5},{8,10},{9,11},{10,... | collective-permute-start | bytes 98312 | tf_op jit(solution)/shard_map/ppermute | solution.py:313
  76.9 1.2 collective-permute-start.2
  78.1 3.6 %collective-permute-start.8 = (s32[8,4]{0,1:T(4,128)}, s32[8,4]{0,1:T(4,128)}, u32[]{:S(2)}, u32[]{:S(2)}) collective-permute-start(s32[8,4]{0,1:T(4,128)} %bitcast.8), channel_id=1, source_target_pairs={{0,64},{16,80},{32,96},{48,112},{64,0},{80,16},{96,32},{112,48},{1... | collective-permute-start | bytes 392 | tf_op jit(solution)/shard_map/ppermute | solution.py:309
  81.7 0.4 collective-permute-start.9
  82.1 0.6 reshape.150
  82.8 0.1 copy.19
  82.9 0.0 copy-start.11
  82.9 0.0 copy-start.12
  82.9 16.0 %collective-permute-done = bf16[32,512]{1,0:T(8,128)(2,1)S(1)} collective-permute-done((bf16[32,512]{1,0:T(8,128)(2,1)S(1)}, bf16[32,512]{1,0:T(8,128)(2,1)S(1)}, u32[]{:S(2)}, u32[]{:S(2)}) %collective-permute-start) | collective-permute-done | bytes 32800 | tf_op jit(solution)/shard_map/ppermute | solution.py:313
  98.9 1.6 collective-permute-start.7
  100.6 3.2 %collective-permute-done.1 = bf16[32,512]{1,0:T(8,128)(2,1)S(1)} collective-permute-done((bf16[32,512]{1,0:T(8,128)(2,1)S(1)}, bf16[32,512]{1,0:T(8,128)(2,1)S(1)}, u32[]{:S(2)}, u32[]{:S(2)}) %collective-permute-start.1) | collective-permute-done | bytes 32800 | tf_op jit(solution)/shard_map/ppermute | solution.py:313
  103.8 0.1 collective-permute-start.3
  103.9 2.4 %collective-permute-start.4 = (bf16[4,32,512]{2,1,0:T(8,128)(2,1)S(1)}, bf16[4,32,512]{2,1,0:T(8,128)(2,1)S(1)}, u32[]{:S(2)}, u32[]{:S(2)}) collective-permute-start(bf16[4,32,512]{2,1,0:T(8,128)(2,1)S(1)} %pad_maximum_fusion.1), channel_id=1, source_target_pairs={{0,8},{1,9},{2,10},{3,11},{4,12},{5,13},{6,14},{7,15},{8,0},{9,1},... | collective-permute-start | bytes 393224 | tf_op jit(solution)/shard_map/ppermute | solution.py:313
  106.3 0.6 constant_dynamic-update-slice_fusion.5
  106.9 0.6 constant_dynamic-update-slice_fusion.4
  107.5 0.6 constant_dynamic-update-slice_fusion.3
  108.1 2.5 %collective-permute-done.3 = bf16[4,32,512]{2,1,0:T(8,128)(2,1)S(1)} collective-permute-done((bf16[4,32,512]{2,1,0:T(8,128)(2,1)S(1)}, bf16[4,32,512]{2,1,0:T(8,128)(2,1)S(1)}, u32[]{:S(2)}, u32[]{:S(2)}) %collective-permute-start.3) | collective-permute-done | bytes 131104 | tf_op jit(solution)/shard_map/ppermute | solution.py:313
  110.6 0.7 constant_dynamic-update-slice_fusion.2
  111.3 0.7 constant_dynamic-update-slice_fusion.1
  111.9 2.5 %collective-permute-done.5 = bf16[4,32,512]{2,1,0:T(8,128)(2,1)S(1)} collective-permute-done((bf16[4,32,512]{2,1,0:T(8,128)(2,1)S(1)}, bf16[4,32,512]{2,1,0:T(8,128)(2,1)S(1)}, u32[]{:S(2)}, u32[]{:S(2)}) %collective-permute-start.5) | collective-permute-done | bytes 131104 | tf_op jit(solution)/shard_map/ppermute | solution.py:313
  114.4 0.7 constant_dynamic-update-slice_fusion.mine_ref
  115.1 4.4 %collective-permute-start.6 = (bf16[16,32,512]{2,1,0:T(8,128)(2,1)}, bf16[16,32,512]{2,1,0:T(8,128)(2,1)S(1)}, u32[]{:S(2)}, u32[]{:S(2)}) collective-permute-start(bf16[16,32,512]{2,1,0:T(8,128)(2,1)} %constant_dynamic-update-slice_fusion.mine_ref), channel_id=1, source_target_pairs={{0,16},{16,0},{32,48},{48,32},{64,80},{80,64},{96,112},{112,96},{1... | collective-permute-start | bytes 1572872 | tf_op jit(solution)/shard_map/ppermute | solution.py:309
  119.5 0.1 add_multiply_fusion
  119.6 0.1 broadcast_add_fusion.row_ref
  119.6 1.6 collective-permute-done.6.other_ref
  121.2 0.8 copy-done.6
  122.0 1.4 copy-done.2
  123.4 1.6 copy-done.3
  125.0 1.0 copy-done.5
  126.0 1.0 copy-done.7
  127.0 4.6 %project.1.refs_0_.own_ref = bf16[1024,512]{1,0:T(8,128)(2,1)S(1)} custom-call(s32[2,16]{1,0:T(2,128)S(1)} %broadcast_add_fusion.row_ref, bf16[1024,1024]{1,0:T(8,128)(2,1)S(1)} %bitcast.44, bf16[16,32,512]{2,1,0:T(8,128)(2,1)S(1)} %copy-done.5, bf16[16,32,512]{2,1,0:T(8,128)(2,1)S(1)} %copy-done.7), custom_call_target="tpu_custom_call" | custom-call | tf_op jit(solution)/shard_map/project/pallas_call | solution.py:64
  131.7 1.7 collective-permute-start.11
  133.4 2.2 %collective-permute-start.13 = (bf16[1024,512]{1,0:T(8,128)(2,1)S(1)}, bf16[1024,512]{1,0:T(8,128)(2,1)}, u32[]{:S(2)}, u32[]{:S(2)}) collective-permute-start(bf16[1024,512]{1,0:T(8,128)(2,1)S(1)} %project.1.refs_0_.own_ref), channel_id=1, source_target_pairs={{0,96},{16,112},{32,0},{48,16},{64,32},{80,48},{96,64},{112,80},{1... | collective-permute-start | bytes 3145736 | tf_op jit(solution)/shard_map/ppermute | solution.py:309
  135.6 0.1 select_multiply_fusion
  135.7 1.6 fusion
  137.4 0.7 fusion.28
  138.1 0.7 collective-permute-start.10
  138.7 0.1 fusion.5
  138.8 0.1 collective-permute-start.19
  138.9 19.8 %collective-permute-done.11.refs_0_ = bf16[1024,512]{1,0:T(8,128)(2,1)S(1)} collective-permute-done((bf16[1024,512]{1,0:T(8,128)(2,1)S(1)}, bf16[1024,512]{1,0:T(8,128)(2,1)S(1)}, u32[]{:S(2)}, u32[]{:S(2)}) %collective-permute-start.11) | collective-permute-done | bytes 1048608 | tf_op jit(solution)/shard_map/ppermute | solution.py:309
  158.7 0.8 slice.10
  159.5 1.9 slice.11
  161.4 2.7 %collective-permute-start.14 = (bf16[512,512]{1,0:T(8,128)(2,1)}, bf16[512,512]{1,0:T(8,128)(2,1)}, u32[]{:S(2)}, u32[]{:S(2)}) collective-permute-start(bf16[512,512]{1,0:T(8,128)(2,1)} %slice.11), channel_id=1, source_target_pairs={{0,96},{16,112},{32,0},{48,16},{64,32},{80,48},{96,64},{112,80},{1... | collective-permute-start | bytes 1572872 | tf_op jit(solution)/shard_map/ppermute | solution.py:309
  164.1 1.4 collective-permute-start.17
  165.5 0.8 pad_maximum_fusion.tgt_ref
  166.3 0.1 pad.12.clone
  166.4 0.6 fusion.14.slot_ref
  167.1 6.6 %collective-permute-done.12.refs_0_ = bf16[512,512]{1,0:T(8,128)(2,1)} collective-permute-done((bf16[512,512]{1,0:T(8,128)(2,1)}, bf16[512,512]{1,0:T(8,128)(2,1)}, u32[]{:S(2)}, u32[]{:S(2)}) %collective-permute-start.12) | collective-permute-done | bytes 524320 | tf_op jit(solution)/shard_map/ppermute | solution.py:309
  173.6 1.8 collective-permute-start.15
  175.4 1.1 collective-permute-start.16
  176.5 0.1 maximum_maximum_fusion.refs_3_.refs_5_
  176.6 0.1 copy.17
  176.7 0.1 copy.18
  176.8 0.6 gather_fusion
  177.4 4.2 %transform.3 = (bf16[8,4,2,128,512]{4,3,2,1,0:T(8,128)(2,1)}, f32[8,4,8,128]{3,2,1,0:T(8,128)S(1)}) custom-call(s32[8,4]{1,0:T(8,128)S(1)} %bitcast.46, bf16[1024,512]{1,0:T(8,128)(2,1)S(1)} %project.1.refs_0_.own_ref, bf16[1024,512]{1,0:T(8,128)(2,1)} %collective-permute-done.19.refs_1_, bf16[2,512,512]{2,1,0:T(8,128)(2,1)S(1)} %copy-done, ...), custom_call_target="tpu_custom_call" | custom-call | tf_op jit(solution)/shard_map/transform/pallas_call | solution.py:146
  181.6 6.4 %transform.4 = (bf16[8,4,2,128,512]{4,3,2,1,0:T(8,128)(2,1)}, f32[8,4,8,128]{3,2,1,0:T(8,128)S(1)}) custom-call(s32[8,4]{1,0:T(8,128)S(1)} %bitcast.47, bf16[1024,512]{1,0:T(8,128)(2,1)S(1)} %collective-permute-done.11.refs_0_, bf16[1024,512]{1,0:T(8,128)(2,1)} %collective-permute-done.17.refs_1_, ...), custom_call_target="tpu_custom_call", output_to_operand_aliasing={{0}: (7, {}), {1}: (8, {})} | custom-call | tf_op jit(solution)/shard_map/transform/pallas_call | solution.py:146
  188.1 4.4 %transform.5 = (bf16[8,4,2,128,512]{4,3,2,1,0:T(8,128)(2,1)}, f32[8,4,8,128]{3,2,1,0:T(8,128)S(1)}) custom-call(s32[8,4]{1,0:T(8,128)S(1)} %bitcast.48, bf16[512,512]{1,0:T(8,128)(2,1)} %collective-permute-done.12.refs_0_, bf16[512,512]{1,0:T(8,128)(2,1)} %collective-permute-done.14.refs_1_, ...), custom_call_target="tpu_custom_call", output_to_operand_aliasing={{0}: (7, {}), {1}: (8, {})} | custom-call | tf_op jit(solution)/shard_map/transform/pallas_call | solution.py:146
  192.5 0.6 copy-done.4
  193.1 21.0 %attend.1 = bf16[1024,512]{1,0:T(8,128)(2,1)} custom-call(s32[8,12]{1,0:T(8,128)} %rel_ref.1, s32[8,12]{1,0:T(8,128)} %fusion.14.slot_ref, bf16[1024,512]{1,0:T(8,128)(2,1)} %copy-done.1, s32[8,12,128,128]{3,2,1,0:T(8,128)} %mask_ref.1, bf16[32,2,128,512]{3,2,1,0:T(8,128)(2,1)} %bitcast.49, f32[32,8,128]{2,1,0:T(8,128)} %bitcast.45, ...), custom_call_target="tpu_custom_call" | custom-call | tf_op jit(solution)/shard_map/attend/pallas_call | solution.py:238
  (46 shorter events, 0.2 us)
Async XLA Ops:
  0.0 72.6 %copy-start.8 = (bf16[64,512]{1,0:T(8,128)(2,1)S(1)}, bf16[64,512]{1,0:T(8,128)(2,1)}, u32[]{:S(2)}) copy-start(bf16[64,512]{1,0:T(8,128)(2,1)} %param.11) | copy-start | bytes 196612
  0.0 82.1 %copy-start.10 = (f32[2,512]{1,0:T(2,128)S(1)}, f32[2,512]{1,0:T(2,128)}, u32[]{:S(2)}) copy-start(f32[2,512]{1,0:T(2,128)} %param.13) | copy-start | bytes 12292
  0.0 82.7 %copy-start.9 = (f32[2,512]{1,0:T(2,128)S(1)}, f32[2,512]{1,0:T(2,128)}, u32[]{:S(2)}) copy-start(f32[2,512]{1,0:T(2,128)} %param.14) | copy-start | bytes 12292
  64.8 70.9 %copy-start = (bf16[2,512,512]{2,1,0:T(8,128)(2,1)S(1)}, bf16[2,512,512]{2,1,0:T(8,128)(2,1)}, u32[]{:S(2)}) copy-start(bf16[2,512,512]{2,1,0:T(8,128)(2,1)} %refs_4_.3) | copy-start | bytes 3145732
  64.8 57.2 %all-to-all-start = ((bf16[16,64,1024]{2,1,0:T(8,128)(2,1)}), bf16[16,64,1024]{2,1,0:T(8,128)(2,1)S(1)}, u32[]{:S(2)}, u32[]{:S(2)}) async-start(bf16[16,64,1024]{2,1,0:T(8,128)(2,1)} %arrange.1), calls=%async_computation | async-start | bytes 4194304 | tf_op jit(solution)/shard_map/all_to_all | solution.py:316
  73.2 25.8 %collective-permute-start = (bf16[32,512]{1,0:T(8,128)(2,1)S(1)}, bf16[32,512]{1,0:T(8,128)(2,1)S(1)}, u32[]{:S(2)}, u32[]{:S(2)}) collective-permute-start(bf16[32,512]{1,0:T(8,128)(2,1)S(1)} %get-tuple-element.18), channel_id=1, source_target_pairs={{0,1},{1,2},{2,3},{3,0},{4,5},{5,6},{6,7},{7,4},{8,9},{9,10},{10,1... | collective-permute-start | bytes 98312 | tf_op jit(solution)/shard_map/ppermute | solution.py:313
  74.5 29.3 %collective-permute-start.1 = (bf16[32,512]{1,0:T(8,128)(2,1)S(1)}, bf16[32,512]{1,0:T(8,128)(2,1)S(1)}, u32[]{:S(2)}, u32[]{:S(2)}) collective-permute-start(bf16[32,512]{1,0:T(8,128)(2,1)S(1)} %get-tuple-element.18), channel_id=1, source_target_pairs={{0,2},{1,3},{2,0},{3,1},{4,6},{5,7},{6,4},{7,5},{8,10},{9,11},{10,... | collective-permute-start | bytes 98312 | tf_op jit(solution)/shard_map/ppermute | solution.py:313
  76.9 26.9 %collective-permute-start.2 = (bf16[32,512]{1,0:T(8,128)(2,1)S(1)}, bf16[32,512]{1,0:T(8,128)(2,1)S(1)}, u32[]{:S(2)}, u32[]{:S(2)}) collective-permute-start(bf16[32,512]{1,0:T(8,128)(2,1)S(1)} %get-tuple-element.18), channel_id=1, source_target_pairs={{0,3},{1,0},{2,1},{3,2},{4,7},{5,4},{6,5},{7,6},{8,11},{9,8},{10,9... | collective-permute-start | bytes 98312 | tf_op jit(solution)/shard_map/ppermute | solution.py:313
  78.1 59.2 %collective-permute-start.8 = (s32[8,4]{0,1:T(4,128)}, s32[8,4]{0,1:T(4,128)}, u32[]{:S(2)}, u32[]{:S(2)}) collective-permute-start(s32[8,4]{0,1:T(4,128)} %bitcast.8), channel_id=1, source_target_pairs={{0,64},{16,80},{32,96},{48,112},{64,0},{80,16},{96,32},{112,48},{1... | collective-permute-start | bytes 392 | tf_op jit(solution)/shard_map/ppermute | solution.py:309
  81.7 55.6 %collective-permute-start.9 = (s32[8,4]{0,1:T(4,128)}, s32[8,4]{0,1:T(4,128)}, u32[]{:S(2)}, u32[]{:S(2)}) collective-permute-start(s32[8,4]{0,1:T(4,128)} %bitcast.8), channel_id=1, source_target_pairs={{0,96},{16,112},{32,0},{48,16},{64,32},{80,48},{96,64},{112,80},{1... | collective-permute-start | bytes 392 | tf_op jit(solution)/shard_map/ppermute | solution.py:309
  82.9 83.5 %copy-start.11 = (s32[8,12]{1,0:T(8,128)S(1)}, s32[8,12]{1,0:T(8,128)}, u32[]{:S(2)}) copy-start(s32[8,12]{1,0:T(8,128)} %param.18) | copy-start | bytes 1156
  82.9 93.6 %copy-start.12 = (s32[4,1]{0,1:T(1,128)S(1)}, s32[4,1]{0,1:T(1,128)}, u32[]{:S(2)}) copy-start(s32[4,1]{0,1:T(1,128)} %constant.178) | copy-start | bytes 52
  98.9 38.4 %collective-permute-start.7 = (s32[8,4]{0,1:T(4,128)}, s32[8,4]{0,1:T(4,128)S(1)}, u32[]{:S(2)}, u32[]{:S(2)}) collective-permute-start(s32[8,4]{0,1:T(4,128)} %bitcast.8), channel_id=1, source_target_pairs={{0,32},{16,48},{32,64},{48,80},{64,96},{80,112},{96,0},{112,16},{1... | collective-permute-start | bytes 392 | tf_op jit(solution)/shard_map/ppermute | solution.py:309
  103.8 6.8 %collective-permute-start.3 = (bf16[4,32,512]{2,1,0:T(8,128)(2,1)S(1)}, bf16[4,32,512]{2,1,0:T(8,128)(2,1)S(1)}, u32[]{:S(2)}, u32[]{:S(2)}) collective-permute-start(bf16[4,32,512]{2,1,0:T(8,128)(2,1)S(1)} %pad_maximum_fusion.1), channel_id=1, source_target_pairs={{0,4},{1,5},{2,6},{3,7},{4,8},{5,9},{6,10},{7,11},{8,12},{9,13},{1... | collective-permute-start | bytes 393224 | tf_op jit(solution)/shard_map/ppermute | solution.py:313
  103.9 7.4 %collective-permute-start.4 = (bf16[4,32,512]{2,1,0:T(8,128)(2,1)S(1)}, bf16[4,32,512]{2,1,0:T(8,128)(2,1)S(1)}, u32[]{:S(2)}, u32[]{:S(2)}) collective-permute-start(bf16[4,32,512]{2,1,0:T(8,128)(2,1)S(1)} %pad_maximum_fusion.1), channel_id=1, source_target_pairs={{0,8},{1,9},{2,10},{3,11},{4,12},{5,13},{6,14},{7,15},{8,0},{9,1},... | collective-permute-start | bytes 393224 | tf_op jit(solution)/shard_map/ppermute | solution.py:313
  110.6 3.8 %collective-permute-start.5 = (bf16[4,32,512]{2,1,0:T(8,128)(2,1)S(1)}, bf16[4,32,512]{2,1,0:T(8,128)(2,1)S(1)}, u32[]{:S(2)}, u32[]{:S(2)}) collective-permute-start(bf16[4,32,512]{2,1,0:T(8,128)(2,1)S(1)} %pad_maximum_fusion.1), channel_id=1, source_target_pairs={{0,12},{1,13},{2,14},{3,15},{4,0},{5,1},{6,2},{7,3},{8,4},{9,5},{1... | collective-permute-start | bytes 393224 | tf_op jit(solution)/shard_map/ppermute | solution.py:313
  115.1 6.1 %collective-permute-start.6 = (bf16[16,32,512]{2,1,0:T(8,128)(2,1)}, bf16[16,32,512]{2,1,0:T(8,128)(2,1)S(1)}, u32[]{:S(2)}, u32[]{:S(2)}) collective-permute-start(bf16[16,32,512]{2,1,0:T(8,128)(2,1)} %constant_dynamic-update-slice_fusion.mine_ref), channel_id=1, source_target_pairs={{0,16},{16,0},{32,48},{48,32},{64,80},{80,64},{96,112},{112,96},{1... | collective-permute-start | bytes 1572872 | tf_op jit(solution)/shard_map/ppermute | solution.py:309
  121.2 0.8 copy-start.6
  122.0 1.4 copy-start.2
  123.4 1.6 copy-start.3
  125.0 1.0 copy-start.5
  126.0 1.0 copy-start.7
  131.6 56.4 %copy-start.1 = (bf16[1024,512]{1,0:T(8,128)(2,1)}, bf16[1024,512]{1,0:T(8,128)(2,1)S(1)}, u32[]{:S(2)}) copy-start(bf16[1024,512]{1,0:T(8,128)(2,1)S(1)} %project.1.refs_0_.own_ref) | copy-start | bytes 3145732
  131.7 27.1 %collective-permute-start.11 = (bf16[1024,512]{1,0:T(8,128)(2,1)S(1)}, bf16[1024,512]{1,0:T(8,128)(2,1)S(1)}, u32[]{:S(2)}, u32[]{:S(2)}) collective-permute-start(bf16[1024,512]{1,0:T(8,128)(2,1)S(1)} %project.1.refs_0_.own_ref), channel_id=1, source_target_pairs={{0,32},{16,48},{32,64},{48,80},{64,96},{80,112},{96,0},{112,16},{1... | collective-permute-start | bytes 3145736 | tf_op jit(solution)/shard_map/ppermute | solution.py:309
  133.4 26.2 %collective-permute-start.13 = (bf16[1024,512]{1,0:T(8,128)(2,1)S(1)}, bf16[1024,512]{1,0:T(8,128)(2,1)}, u32[]{:S(2)}, u32[]{:S(2)}) collective-permute-start(bf16[1024,512]{1,0:T(8,128)(2,1)S(1)} %project.1.refs_0_.own_ref), channel_id=1, source_target_pairs={{0,96},{16,112},{32,0},{48,16},{64,32},{80,48},{96,64},{112,80},{1... | collective-permute-start | bytes 3145736 | tf_op jit(solution)/shard_map/ppermute | solution.py:309
  138.1 27.5 %collective-permute-start.10 = (s32[4,8,4]{1,2,0:T(4,128)S(1)}, s32[4,8,4]{1,2,0:T(4,128)S(1)}, u32[]{:S(2)}, u32[]{:S(2)}) collective-permute-start(s32[4,8,4]{1,2,0:T(4,128)S(1)} %get-tuple-element.26), channel_id=1, source_target_pairs={{0,16},{16,0},{32,48},{48,32},{64,80},{80,64},{96,112},{112,96},{1... | collective-permute-start | bytes 1544 | tf_op jit(solution)/shard_map/ppermute | solution.py:309
  138.8 38.6 %collective-permute-start.19 = (bf16[1024,512]{1,0:T(8,128)(2,1)S(1)}, bf16[1024,512]{1,0:T(8,128)(2,1)}, u32[]{:S(2)}, u32[]{:S(2)}) collective-permute-start(bf16[1024,512]{1,0:T(8,128)(2,1)S(1)} %project.1.refs_0_.own_ref), channel_id=1, source_target_pairs={{0,16},{16,0},{32,48},{48,32},{64,80},{80,64},{96,112},{112,96},{1... | collective-permute-start | bytes 3145736 | tf_op jit(solution)/shard_map/ppermute | solution.py:309
  159.5 14.1 %collective-permute-start.12 = (bf16[512,512]{1,0:T(8,128)(2,1)}, bf16[512,512]{1,0:T(8,128)(2,1)}, u32[]{:S(2)}, u32[]{:S(2)}) collective-permute-start(bf16[512,512]{1,0:T(8,128)(2,1)} %slice.10), channel_id=1, source_target_pairs={{0,32},{16,48},{32,64},{48,80},{64,96},{80,112},{96,0},{112,16},{1... | collective-permute-start | bytes 1572872 | tf_op jit(solution)/shard_map/ppermute | solution.py:309
  161.4 14.0 %collective-permute-start.14 = (bf16[512,512]{1,0:T(8,128)(2,1)}, bf16[512,512]{1,0:T(8,128)(2,1)}, u32[]{:S(2)}, u32[]{:S(2)}) collective-permute-start(bf16[512,512]{1,0:T(8,128)(2,1)} %slice.11), channel_id=1, source_target_pairs={{0,96},{16,112},{32,0},{48,16},{64,32},{80,48},{96,64},{112,80},{1... | collective-permute-start | bytes 1572872 | tf_op jit(solution)/shard_map/ppermute | solution.py:309
  164.1 17.6 %collective-permute-start.17 = (bf16[1024,512]{1,0:T(8,128)(2,1)S(1)}, bf16[1024,512]{1,0:T(8,128)(2,1)}, u32[]{:S(2)}, u32[]{:S(2)}) collective-permute-start(bf16[1024,512]{1,0:T(8,128)(2,1)S(1)} %collective-permute-done.11.refs_0_), channel_id=1, source_target_pairs={{0,16},{16,0},{32,48},{48,32},{64,80},{80,64},{96,112},{112,96},{1... | collective-permute-start | bytes 3145736 | tf_op jit(solution)/shard_map/ppermute | solution.py:309
  165.5 16.1 %collective-permute-start.18 = (bf16[1024,512]{1,0:T(8,128)(2,1)}, bf16[1024,512]{1,0:T(8,128)(2,1)}, u32[]{:S(2)}, u32[]{:S(2)}) collective-permute-start(bf16[1024,512]{1,0:T(8,128)(2,1)} %collective-permute-done.13.refs_2_), channel_id=1, source_target_pairs={{0,16},{16,0},{32,48},{48,32},{64,80},{80,64},{96,112},{112,96},{1... | collective-permute-start | bytes 3145736 | tf_op jit(solution)/shard_map/ppermute | solution.py:309
  173.6 14.4 %collective-permute-start.15 = (bf16[512,512]{1,0:T(8,128)(2,1)}, bf16[512,512]{1,0:T(8,128)(2,1)}, u32[]{:S(2)}, u32[]{:S(2)}) collective-permute-start(bf16[512,512]{1,0:T(8,128)(2,1)} %collective-permute-done.12.refs_0_), channel_id=1, source_target_pairs={{0,16},{16,0},{32,48},{48,32},{64,80},{80,64},{96,112},{112,96},{1... | collective-permute-start | bytes 1572872 | tf_op jit(solution)/shard_map/ppermute | solution.py:309
  175.4 12.7 %collective-permute-start.16 = (bf16[512,512]{1,0:T(8,128)(2,1)}, bf16[512,512]{1,0:T(8,128)(2,1)}, u32[]{:S(2)}, u32[]{:S(2)}) collective-permute-start(bf16[512,512]{1,0:T(8,128)(2,1)} %collective-permute-done.14.refs_1_), channel_id=1, source_target_pairs={{0,16},{16,0},{32,48},{48,32},{64,80},{80,64},{96,112},{112,96},{1... | collective-permute-start | bytes 1572872 | tf_op jit(solution)/shard_map/ppermute | solution.py:309
  192.5 0.7 copy-start.4

commit v4 on v2

--- a/solution.py
+++ b/solution.py
@@ -12,6 +12,36 @@
 LOG2E = 1.4426950408889634
 F32 = jnp.float32
 BF16 = jnp.bfloat16
+
+
+def arrange_kernel(core_ref, x_ref, w_ref, out_ref):
+    peers, _, columns = out_ref.shape
+    half = w_ref.shape[1]
+    rows = columns - half
+    for q in range(peers):
+        out_ref[q, :, :rows] = x_ref[:, q * rows : (q + 1) * rows]
+        out_ref[q, :, rows:] = w_ref[...]
+
+
+def arrange(features, weight, core, peers):
+    depth, columns = features.shape
+    half = weight.shape[1] // 2
+    rows = columns // peers
+    step = 4
+    return pl.pallas_call(
+        arrange_kernel,
+        grid_spec=pltpu.PrefetchScalarGridSpec(
+            num_scalar_prefetch=1,
+            grid=(peers // step,),
+            in_specs=[
+                pl.BlockSpec((depth, step * rows), lambda i, core_ref: (0, i)),
+                pl.BlockSpec((depth, half), lambda i, core_ref: (0, core_ref[0])),
+            ],
+            out_specs=pl.BlockSpec((step, depth, rows + half), lambda i, core_ref: (i, 0, 0)),
+        ),
+        out_shape=jax.ShapeDtypeStruct((peers, depth, rows + half), BF16),
+        name="arrange",
+    )(core.reshape(1), features, weight)
 
 
 def three_parts(x):
@@ -233,69 +263,54 @@
     depth, width = proj_weight.shape
     n_feat = lax.axis_size("feat")
     n_graph = lax.axis_size("graph")
-    depth_z = n_graph // 2
+    levels = n_graph // 2
     place = lax.axis_index("graph")
     core, level = lax.rem(place, 2), place // 2
 
-    def send(x, levels, cores=0):
-        pairs = [(p, (p + 2 * levels) % n_graph ^ cores) for p in range(n_graph)]
+    def send(x, up, cores=0):
+        pairs = [(p, (p + 2 * up) % n_graph ^ cores) for p in range(n_graph)]
         return lax.ppermute(x, "graph", pairs)
 
-    cut = 3
-    parts = ((0, cut), (cut, local_blocks))
-    features = node_features.T.reshape(depth, n_feat, local_blocks, block_rows)
-
-    def slices(low, high):
-        return features[:, :, low:high].reshape(depth, n_feat, (high - low) * block_rows).transpose(1, 0, 2)
-
-    half = width // 2
-    share = lax.dynamic_slice(proj_weight, (0, core * half), (depth, half))
-    share = jnp.broadcast_to(share[None], (n_feat, depth, half))
-    got = lax.all_to_all(jnp.concatenate([slices(*parts[0]), share], axis=2), "feat", 0, 0, tiled=True)
-    got = got.reshape(n_feat * depth, cut * block_rows + half)
-    later = lax.all_to_all(slices(*parts[1]), "feat", 0, 0, tiled=True)
-    later = later.reshape(n_feat * depth, (local_blocks - cut) * block_rows)
-    mine = got[:, cut * block_rows :]
+    outgoing = arrange(node_features.T, proj_weight, core, n_feat)
+    got = lax.all_to_all(outgoing, "feat", 0, 0, tiled=True).reshape(n_feat * depth, rows_local + width // 2)
+
+    tables = jnp.stack([send_blocks[0]] + [send(send_blocks[0], d) for d in range(1, levels)])
+    tables = jnp.stack([tables, send(tables, 0, 1)], axis=1)
+    order = jnp.array([0, 1, 3, 2])
+    index = tables[order, :, place].reshape(n_graph, CAP)
+    peer = source_slots // CAP
+    distance = (level - peer // 2 + levels) % levels
+    slots = (2 * (distance ^ (distance >> 1)) + (peer % 2 ^ core)) * CAP + source_slots % CAP
+    src_vectors, tgt_vectors = score_vectors(relation_weight, att_source, att_target)
+
+    got, src_vectors, tgt_vectors, index, slots = lax.optimization_barrier(
+        (got, src_vectors, tgt_vectors, index, slots)
+    )
+    mine = got[:, rows_local:]
     other = send(mine, 0, 1)
     whole = jnp.where(core == 0, jnp.concatenate([mine, other], axis=1), jnp.concatenate([other, mine], axis=1))
-
-    src_vectors, tgt_vectors = score_vectors(relation_weight, att_source, att_target)
-    tables = lax.all_gather(send_blocks[0], "graph")[:, place]
-    relative = jnp.arange(n_graph)
-    index = tables[2 * lax.rem(level - relative // 2 + depth_z, depth_z) + (relative % 2 ^ core)]
-    peer = source_slots // CAP
-    distance = lax.rem(level - peer // 2 + depth_z, depth_z)
-    slots = (2 * distance + (peer % 2 ^ core)) * CAP + source_slots % CAP
-
-    hidden = []
-    sources = [[] for _ in range(n_graph)]
-    for (low, high), x in zip(parts, (got[:, : cut * block_rows], later)):
-        part = lax.dot_general(x, whole, (((0,), (0,)), ((), ())), preferred_element_type=F32).astype(BF16)
-        hidden.append(part)
-        middle = (high - low + (low == 0)) // 2
-        split = middle * block_rows
-        up, down = send(part, 1), send(part, -1)
-        arrived = (
-            (0, part, low, high),
-            (1, up, low, high),
-            (3, down, low, high),
-            (2, send(up[:split], 1), low, low + middle),
-            (2, send(down[split:], -1), low + middle, high),
-        )
-        for steps, array, first, end in arrived:
-            sources[2 * steps].append((array, first, end))
-            sources[2 * steps + 1].append((send(array, 0, 1), first, end))
-
-    values = scores = None
-    index = index.astype(jnp.int32)
-    for group in ((0, 1), (2, 3), (6, 7), (4, 5)):
-        values, scores = transform(
-            [sources[s] for s in group], group[0], index, relation_weight, src_vectors, block_rows, values, scores
-        )
+    hidden = lax.dot_general(
+        got[:, :rows_local], whole, (((0,), (0,)), ((), ())), preferred_element_type=F32
+    ).astype(BF16)
+
+    def both(pieces):
+        return [pieces, [(send(x, 0, 1), low, high) for x, low, high in pieces]]
+
+    def spread(group, first, kept):
+        return transform(group, first, index, relation_weight, src_vectors, block_rows, *kept)
+
+    middle = local_blocks // 2
+    split = middle * block_rows
+    up, down = send(hidden, 1), send(hidden, -1)
+    done = spread(both([(hidden, 0, local_blocks)]), 0, (None, None))
+    up, down, done = lax.optimization_barrier((up, down, done))
+    far_up, far_down = send(up[:split], 1), send(down[split:], -1)
+    done = spread(both([(up, 0, local_blocks)]) + both([(down, 0, local_blocks)]), 2, done)
+    far_up, far_down, done = lax.optimization_barrier((far_up, far_down, done))
+    values, scores = spread(both([(far_up, 0, middle), (far_down, middle, local_blocks)]), 6, done)
     total = n_graph * CAP
     values = values.reshape((total,) + values.shape[2:])
     scores = scores.reshape((total,) + scores.shape[2:])
-    hidden = jnp.concatenate(hidden, axis=0)
     return attend(hidden, edge_mask, relation_ids, slots, values, scores, tgt_vectors)
 
 

time: 164 us -> 131 us (0.80)
  waiting for transfers between devices: 35.7 us -> 53.7 us
  local copies, waits for them, and re-layouts: 20.2 us -> 2.85 us
  blocking collectives: 15.9 us -> 0 us
  starting transfers between devices: 38.4 us -> 26.7 us
  other arithmetic: 8.46 us -> 1.78 us
  Pallas kernels: 38.7 us -> 41.8 us
  matrix products: 5.48 us -> 3.8 us
    all_gather x1 -> x0, blocking collectives: 15.9 us -> none  [shards(): tables = lax.all_gather(send_blocks[0], 'graph')[:, place]]
    ppermute x19 -> x14, waiting for transfers between devices: 15 us -> 26.5 us  [send(): return lax.ppermute(x, 'graph', pairs)]
    all_to_all x2 -> x1, waiting for transfers between devices: 20.7 us -> 27.2 us  [shards(): lax.all_to_all(outgoing, 'feat', 0, 0, tiled=True)]
    ppermute x19 -> x14, starting transfers between devices: 25.3 us -> 18.9 us  [send(): return lax.ppermute(x, 'graph', pairs)]
    slice x7 -> x3, local copies, waits for them, and re-layouts: 7.01 us -> 1.15 us  [the longest x1 1.08 us: shards(): mine = got[:, rows_local:]]
    all_to_all x2 -> x1, starting transfers between devices: 13.1 us -> 7.77 us  [shards(): lax.all_to_all(outgoing, 'feat', 0, 0, tiled=True)]
    reshape x2 -> x0, local copies, waits for them, and re-layouts: 4.76 us -> none  [slices(): features[:, :, low:high].reshape(depth, n_feat, (high - low) * block_rows)]
    pallas_call x0 -> x1, Pallas kernels: none -> 3.89 us  [arrange(): pl.pallas_call(arrange_kernel, grid_spec=pltpu.PrefetchScalarGridSpec(num...]
  transfers between devices with their start and end apart: 21 -> 15, of which waited for: 5 -> 7; matrix products, arithmetic and copies ran while one was open for 16% -> 3% of each run, Pallas kernels for 8% -> 9%
where the time goes in v4:
time: 131 us
  waiting for transfers between devices  53.7 us (41%)
  Pallas kernels  41.8 us (32%)
  starting transfers between devices  26.7 us (20%)
  matrix products  3.8 us (3%)
  local copies, waits for them, and re-layouts  2.85 us (2%)
  other arithmetic  1.78 us (1%)
    all_to_all x1, waiting for transfers between devices, shards(): lax.all_to_all(outgoing, 'feat', 0, 0, tiled=True)  27.2 us
    ppermute x14, waiting for transfers between devices, send(): return lax.ppermute(x, 'graph', pairs)  26.5 us
    pallas_call x1, Pallas kernels, attend(): pl.pallas_call(attend_kernel, grid_spec=pltpu.PrefetchScalarGridSpec(num_...  21 us
    ppermute x14, starting transfers between devices, send(): return lax.ppermute(x, 'graph', pairs)  18.9 us
    pallas_call x3, Pallas kernels, transform(): pl.pallas_call(functools.partial(transform_kernel, bounds, first), grid_s...  16.9 us
    all_to_all x1, starting transfers between devices, shards(): lax.all_to_all(outgoing, 'feat', 0, 0, tiled=True)  7.77 us
    pallas_call x1, Pallas kernels, arrange(): pl.pallas_call(arrange_kernel, grid_spec=pltpu.PrefetchScalarGridSpec(num...  3.89 us
    dot_general x1, matrix products, shards(): lax.dot_general(got[:, :rows_local], whole, (((0,), (0,)), ((), ())), pre...  2.89 us
  transfers between devices with their start and end apart: 15, of which 7 were waited for; matrix products, arithmetic and copies ran while one was open for 3% of the time, Pallas kernels for 9%

profile of v4, /device:TPU:1, one launch (start us, length us, event | category | flops | bytes accessed | tf_op | source)
XLA Modules:
  0.0 130.9 jit_solution(3663300754687014080)
XLA Ops:
  0.0 3.9 %arrange.1 = bf16[16,64,1280]{2,1,0:T(8,128)(2,1)} custom-call(s32[1]{0:T(128)} %bitcast.core_ref, bf16[64,16384]{1,0:T(8,128)(2,1)} %bitcast.40, bf16[64,512]{1,0:T(8,128)(2,1)} %w_ref.1), custom_call_target="tpu_custom_call" | custom-call | tf_op jit(solution)/shard_map/arrange/pallas_call | solution.py:31
  3.9 0.0 copy-start.6
  3.9 0.0 copy-start.3
  3.9 0.0 copy-start.4
  3.9 0.0 copy-start
  3.9 0.0 copy-start.7
  3.9 0.0 copy-start.5
  3.9 7.8 %all-to-all-start = ((bf16[16,64,1280]{2,1,0:T(8,128)(2,1)}), bf16[16,64,1280]{2,1,0:T(8,128)(2,1)}, u32[]{:S(2)}, u32[]{:S(2)}) async-start(bf16[16,64,1280]{2,1,0:T(8,128)(2,1)} %arrange.1), calls=%async_computation | async-start | bytes 5242880 | tf_op jit(solution)/shard_map/all_to_all | solution.py:275
  11.7 0.0 copy-done.6
  11.7 1.7 %collective-permute-start = (s32[8,4]{0,1:T(4,128)S(1)}, s32[8,4]{0,1:T(4,128)S(1)}, u32[]{:S(2)}, u32[]{:S(2)}) collective-permute-start(s32[8,4]{0,1:T(4,128)S(1)} %bitcast.44), channel_id=1, source_target_pairs={{0,32},{16,48},{32,64},{48,80},{64,96},{80,112},{96,0},{112,16},{1... | collective-permute-start | bytes 392 | tf_op jit(solution)/shard_map/ppermute | solution.py:272
  13.4 3.3 %collective-permute-start.1 = (s32[8,4]{0,1:T(4,128)S(1)}, s32[8,4]{0,1:T(4,128)S(1)}, u32[]{:S(2)}, u32[]{:S(2)}) collective-permute-start(s32[8,4]{0,1:T(4,128)S(1)} %bitcast.45), channel_id=1, source_target_pairs={{0,64},{16,80},{32,96},{48,112},{64,0},{80,16},{96,32},{112,48},{1... | collective-permute-start | bytes 392 | tf_op jit(solution)/shard_map/ppermute | solution.py:272
  16.7 0.7 collective-permute-start.2
  17.5 0.0 copy-done.3
  17.5 0.1 copy.17
  17.6 0.0 copy-done.4
  17.6 0.0 copy-done
  17.7 0.9 fusion.5
  18.6 0.1 pad.22.clone
  18.7 0.0 copy-done.7
  18.7 0.0 copy-done.5
  18.7 0.6 fusion.25.slot_ref
  19.4 0.1 maximum_maximum_fusion.refs_3_.refs_5_
  19.4 0.1 select_multiply_fusion
  19.6 0.1 fusion.16
  19.7 0.0 collective-permute-done
  19.7 0.0 collective-permute-done.1
  19.7 0.0 collective-permute-done.2
  19.7 2.1 %collective-permute-start.3 = (s32[4,8,4]{1,2,0:T(4,128)S(1)}, s32[4,8,4]{1,2,0:T(4,128)S(1)}, u32[]{:S(2)}, u32[]{:S(2)}) collective-permute-start(s32[4,8,4]{1,2,0:T(4,128)S(1)} %get-tuple-element.50), channel_id=1, source_target_pairs={{0,16},{16,0},{32,48},{48,32},{64,80},{80,64},{96,112},{112,96},{1... | collective-permute-start | bytes 1544 | tf_op jit(solution)/shard_map/ppermute | solution.py:272
  21.8 0.8 pad_maximum_fusion.tgt_ref
  22.6 0.1 copy.18
  22.7 0.0 collective-permute-done.3
  22.7 0.1 copy.19
  22.9 0.6 gather_fusion
  23.5 27.2 %all-to-all-done = bf16[16,64,1280]{2,1,0:T(8,128)(2,1)} async-done(((bf16[16,64,1280]{2,1,0:T(8,128)(2,1)}), bf16[16,64,1280]{2,1,0:T(8,128)(2,1)}, u32[]{:S(2)}, u32[]{:S(2)}) %all-to-all-start) | async-done | bytes 2621472 | tf_op jit(solution)/shard_map/all_to_all | solution.py:275
  50.7 1.1 slice.13
  51.8 1.9 %collective-permute-start.4 = (bf16[1024,256]{1,0:T(8,128)(2,1)S(1)}, bf16[1024,256]{1,0:T(8,128)(2,1)S(1)}, u32[]{:S(2)}, u32[]{:S(2)}) collective-permute-start(bf16[1024,256]{1,0:T(8,128)(2,1)S(1)} %slice.13), channel_id=1, source_target_pairs={{0,16},{16,0},{32,48},{48,32},{64,80},{80,64},{96,112},{112,96},{1... | collective-permute-start | bytes 1572872 | tf_op jit(solution)/shard_map/ppermute | solution.py:272
  53.7 1.5 %collective-permute-done.4 = bf16[1024,256]{1,0:T(8,128)(2,1)S(1)} collective-permute-done((bf16[1024,256]{1,0:T(8,128)(2,1)S(1)}, bf16[1024,256]{1,0:T(8,128)(2,1)S(1)}, u32[]{:S(2)}, u32[]{:S(2)}) %collective-permute-start.4) | collective-permute-done | bytes 524320 | tf_op jit(solution)/shard_map/ppermute | solution.py:272
  55.2 2.9 %fusion.2.refs_0_.own_ref = bf16[1024,512]{1,0:T(8,128)(2,1)S(1)} fusion(bf16[1024,1280]{1,0:T(8,128)(2,1)} %bitcast.2, bf16[1024,256]{1,0:T(8,128)(2,1)S(1)} %collective-permute-done.4, bf16[1024,256]{1,0:T(8,128)(2,1)S(1)} %slice.13, pred[]{:T(512)S(6)} %eq.25), kind=kOutput, calls=%fused_computation.3 | convolution fusion | flops 1078984704 | bytes 4194305 | tf_op jit(solution)/shard_map/dot_general | solution.py:292
  58.1 0.0 copy-start.1
  58.1 0.4 collective-permute-start.7
  58.6 1.6 %collective-permute-start.5 = (bf16[1024,512]{1,0:T(8,128)(2,1)S(1)}, bf16[1024,512]{1,0:T(8,128)(2,1)S(1)}, u32[]{:S(2)}, u32[]{:S(2)}) collective-permute-start(bf16[1024,512]{1,0:T(8,128)(2,1)S(1)} %fusion.2.refs_0_.own_ref), channel_id=1, source_target_pairs={{0,32},{16,48},{32,64},{48,80},{64,96},{80,112},{96,0},{112,16},{1... | collective-permute-start | bytes 3145736 | tf_op jit(solution)/shard_map/ppermute | solution.py:272
  60.2 2.1 %collective-permute-start.6 = (bf16[1024,512]{1,0:T(8,128)(2,1)S(1)}, bf16[1024,512]{1,0:T(8,128)(2,1)S(1)}, u32[]{:S(2)}, u32[]{:S(2)}) collective-permute-start(bf16[1024,512]{1,0:T(8,128)(2,1)S(1)} %fusion.2.refs_0_.own_ref), channel_id=1, source_target_pairs={{0,96},{16,112},{32,0},{48,16},{64,32},{80,48},{96,64},{112,80},{1... | collective-permute-start | bytes 3145736 | tf_op jit(solution)/shard_map/ppermute | solution.py:272
  62.3 0.0 collective-permute-done.7.refs_1_
  62.3 4.6 %transform.3 = (bf16[8,4,2,128,512]{4,3,2,1,0:T(8,128)(2,1)}, f32[8,4,8,128]{3,2,1,0:T(8,128)S(1)}) custom-call(s32[8,4]{1,0:T(8,128)S(1)} %bitcast.36, bf16[1024,512]{1,0:T(8,128)(2,1)S(1)} %fusion.2.refs_0_.own_ref, bf16[1024,512]{1,0:T(8,128)(2,1)S(1)} %collective-permute-done.7.refs_1_, bf16[2,512,512]{2,1,0:T(8,128)(2,1)S(1)} %copy-done, ...), custom_call_target="tpu_custom_call" | custom-call | tf_op jit(solution)/shard_map/transform/pallas_call | solution.py:110
  66.9 18.8 %collective-permute-done.5.refs_0_ = bf16[1024,512]{1,0:T(8,128)(2,1)S(1)} collective-permute-done((bf16[1024,512]{1,0:T(8,128)(2,1)S(1)}, bf16[1024,512]{1,0:T(8,128)(2,1)S(1)}, u32[]{:S(2)}, u32[]{:S(2)}) %collective-permute-start.5) | collective-permute-done | bytes 1048608 | tf_op jit(solution)/shard_map/ppermute | solution.py:272
  85.7 0.0 collective-permute-done.6.refs_2_
  85.7 0.7 collective-permute-start.10
  86.4 0.0 collective-permute-start.11
  86.5 0.0 copy-done.1
  86.5 1.0 collective-permute-start.8
  87.6 1.8 %collective-permute-start.9 = (bf16[512,512]{1,0:T(8,128)(2,1)S(1)}, bf16[512,512]{1,0:T(8,128)(2,1)S(1)}, u32[]{:S(2)}, u32[]{:S(2)}) collective-permute-start(bf16[512,512]{1,0:T(8,128)(2,1)S(1)} %slice.15), channel_id=1, source_target_pairs={{0,96},{16,112},{32,0},{48,16},{64,32},{80,48},{96,64},{112,80},{1... | collective-permute-start | bytes 1572872 | tf_op jit(solution)/shard_map/ppermute | solution.py:272
  89.4 0.0 collective-permute-done.10.refs_1_
  89.4 0.9 collective-permute-done.11.refs_3_
  90.2 7.6 %transform.4 = (bf16[8,4,2,128,512]{4,3,2,1,0:T(8,128)(2,1)}, f32[8,4,8,128]{3,2,1,0:T(8,128)S(1)}) custom-call(s32[8,4]{1,0:T(8,128)S(1)} %bitcast.37, bf16[1024,512]{1,0:T(8,128)(2,1)S(1)} %collective-permute-done.5.refs_0_, bf16[1024,512]{1,0:T(8,128)(2,1)S(1)} %collective-permute-done.10.refs_1_, ...), custom_call_target="tpu_custom_call", output_to_operand_aliasing={{0}: (7, {}), {1}: (8, {})} | custom-call | tf_op jit(solution)/shard_map/transform/pallas_call | solution.py:110
  97.8 3.0 %collective-permute-done.8.refs_0_ = bf16[512,512]{1,0:T(8,128)(2,1)S(1)} collective-permute-done((bf16[512,512]{1,0:T(8,128)(2,1)S(1)}, bf16[512,512]{1,0:T(8,128)(2,1)S(1)}, u32[]{:S(2)}, u32[]{:S(2)}) %collective-permute-start.8) | collective-permute-done | bytes 524320 | tf_op jit(solution)/shard_map/ppermute | solution.py:272
  100.8 0.0 collective-permute-done.9.refs_1_
  100.8 1.4 %collective-permute-start.12 = (bf16[512,512]{1,0:T(8,128)(2,1)S(1)}, bf16[512,512]{1,0:T(8,128)(2,1)S(1)}, u32[]{:S(2)}, u32[]{:S(2)}) collective-permute-start(bf16[512,512]{1,0:T(8,128)(2,1)S(1)} %collective-permute-done.8.refs_0_), channel_id=1, source_target_pairs={{0,16},{16,0},{32,48},{48,32},{64,80},{80,64},{96,112},{112,96},{1... | collective-permute-start | bytes 1572872 | tf_op jit(solution)/shard_map/ppermute | solution.py:272
  102.2 0.0 collective-permute-start.13
  102.2 1.5 %collective-permute-done.12.refs_2_ = bf16[512,512]{1,0:T(8,128)(2,1)S(1)} collective-permute-done((bf16[512,512]{1,0:T(8,128)(2,1)S(1)}, bf16[512,512]{1,0:T(8,128)(2,1)S(1)}, u32[]{:S(2)}, u32[]{:S(2)}) %collective-permute-start.12) | collective-permute-done | bytes 524320 | tf_op jit(solution)/shard_map/ppermute | solution.py:272
  103.7 0.7 collective-permute-done.13.refs_3_
  104.4 4.8 %transform.5 = (bf16[8,4,2,128,512]{4,3,2,1,0:T(8,128)(2,1)}, f32[8,4,8,128]{3,2,1,0:T(8,128)S(1)}) custom-call(s32[8,4]{1,0:T(8,128)S(1)} %bitcast.38, bf16[512,512]{1,0:T(8,128)(2,1)S(1)} %collective-permute-done.8.refs_0_, bf16[512,512]{1,0:T(8,128)(2,1)S(1)} %collective-permute-done.9.refs_1_, ...), custom_call_target="tpu_custom_call", output_to_operand_aliasing={{0}: (7, {}), {1}: (8, {})} | custom-call | tf_op jit(solution)/shard_map/transform/pallas_call | solution.py:110
  109.2 0.0 copy-start.2
  109.2 0.6 copy-done.2
  109.9 21.0 %attend.1 = bf16[1024,512]{1,0:T(8,128)(2,1)} custom-call(s32[8,12]{1,0:T(8,128)} %rel_ref.1, s32[8,12]{1,0:T(8,128)} %fusion.25.slot_ref, bf16[1024,512]{1,0:T(8,128)(2,1)} %copy-done.1, s32[8,12,128,128]{3,2,1,0:T(8,128)} %mask_ref.1, bf16[32,2,128,512]{3,2,1,0:T(8,128)(2,1)} %bitcast.39, f32[32,8,128]{2,1,0:T(8,128)} %bitcast.35, ...), custom_call_target="tpu_custom_call" | custom-call | tf_op jit(solution)/shard_map/attend/pallas_call | solution.py:202
  (14 shorter events, 0.2 us)
Async XLA Ops:
  3.9 7.8 %copy-start.6 = (s32[1,8,4]{1,2,0:T(4,128)S(1)}, s32[1,8,4]{1,2,0:T(4,128)}, u32[]{:S(2)}) copy-start(s32[1,8,4]{1,2,0:T(4,128)} %param.17) | copy-start | bytes 388
  3.9 13.6 %copy-start.3 = (f32[2,512]{1,0:T(2,128)S(1)}, f32[2,512]{1,0:T(2,128)}, u32[]{:S(2)}) copy-start(f32[2,512]{1,0:T(2,128)} %param.14) | copy-start | bytes 12292
  3.9 13.7 %copy-start.4 = (f32[2,512]{1,0:T(2,128)S(1)}, f32[2,512]{1,0:T(2,128)}, u32[]{:S(2)}) copy-start(f32[2,512]{1,0:T(2,128)} %param.13) | copy-start | bytes 12292
  3.9 13.7 %copy-start = (bf16[2,512,512]{2,1,0:T(8,128)(2,1)S(1)}, bf16[2,512,512]{2,1,0:T(8,128)(2,1)}, u32[]{:S(2)}) copy-start(bf16[2,512,512]{2,1,0:T(8,128)(2,1)} %refs_4_.3) | copy-start | bytes 3145732
  3.9 14.8 %copy-start.7 = (s32[4,1]{0,1:T(1,128)S(1)}, s32[4,1]{0,1:T(1,128)}, u32[]{:S(2)}) copy-start(s32[4,1]{0,1:T(1,128)} %constant.134) | copy-start | bytes 52
  3.9 14.8 %copy-start.5 = (s32[8,12]{1,0:T(8,128)S(1)}, s32[8,12]{1,0:T(8,128)}, u32[]{:S(2)}) copy-start(s32[8,12]{1,0:T(8,128)} %param.18) | copy-start | bytes 1156
  3.9 46.7 %all-to-all-start = ((bf16[16,64,1280]{2,1,0:T(8,128)(2,1)}), bf16[16,64,1280]{2,1,0:T(8,128)(2,1)}, u32[]{:S(2)}, u32[]{:S(2)}) async-start(bf16[16,64,1280]{2,1,0:T(8,128)(2,1)} %arrange.1), calls=%async_computation | async-start | bytes 5242880 | tf_op jit(solution)/shard_map/all_to_all | solution.py:275
  11.7 7.9 %collective-permute-start = (s32[8,4]{0,1:T(4,128)S(1)}, s32[8,4]{0,1:T(4,128)S(1)}, u32[]{:S(2)}, u32[]{:S(2)}) collective-permute-start(s32[8,4]{0,1:T(4,128)S(1)} %bitcast.44), channel_id=1, source_target_pairs={{0,32},{16,48},{32,64},{48,80},{64,96},{80,112},{96,0},{112,16},{1... | collective-permute-start | bytes 392 | tf_op jit(solution)/shard_map/ppermute | solution.py:272
  13.4 6.3 %collective-permute-start.1 = (s32[8,4]{0,1:T(4,128)S(1)}, s32[8,4]{0,1:T(4,128)S(1)}, u32[]{:S(2)}, u32[]{:S(2)}) collective-permute-start(s32[8,4]{0,1:T(4,128)S(1)} %bitcast.45), channel_id=1, source_target_pairs={{0,64},{16,80},{32,96},{48,112},{64,0},{80,16},{96,32},{112,48},{1... | collective-permute-start | bytes 392 | tf_op jit(solution)/shard_map/ppermute | solution.py:272
  16.7 3.0 %collective-permute-start.2 = (s32[8,4]{0,1:T(4,128)S(1)}, s32[8,4]{0,1:T(4,128)S(1)}, u32[]{:S(2)}, u32[]{:S(2)}) collective-permute-start(s32[8,4]{0,1:T(4,128)S(1)} %bitcast.46), channel_id=1, source_target_pairs={{0,96},{16,112},{32,0},{48,16},{64,32},{80,48},{96,64},{112,80},{1... | collective-permute-start | bytes 392 | tf_op jit(solution)/shard_map/ppermute | solution.py:272
  19.7 3.0 %collective-permute-start.3 = (s32[4,8,4]{1,2,0:T(4,128)S(1)}, s32[4,8,4]{1,2,0:T(4,128)S(1)}, u32[]{:S(2)}, u32[]{:S(2)}) collective-permute-start(s32[4,8,4]{1,2,0:T(4,128)S(1)} %get-tuple-element.50), channel_id=1, source_target_pairs={{0,16},{16,0},{32,48},{48,32},{64,80},{80,64},{96,112},{112,96},{1... | collective-permute-start | bytes 1544 | tf_op jit(solution)/shard_map/ppermute | solution.py:272
  51.8 3.4 %collective-permute-start.4 = (bf16[1024,256]{1,0:T(8,128)(2,1)S(1)}, bf16[1024,256]{1,0:T(8,128)(2,1)S(1)}, u32[]{:S(2)}, u32[]{:S(2)}) collective-permute-start(bf16[1024,256]{1,0:T(8,128)(2,1)S(1)} %slice.13), channel_id=1, source_target_pairs={{0,16},{16,0},{32,48},{48,32},{64,80},{80,64},{96,112},{112,96},{1... | collective-permute-start | bytes 1572872 | tf_op jit(solution)/shard_map/ppermute | solution.py:272
  58.1 28.4 %copy-start.1 = (bf16[1024,512]{1,0:T(8,128)(2,1)}, bf16[1024,512]{1,0:T(8,128)(2,1)S(1)}, u32[]{:S(2)}) copy-start(bf16[1024,512]{1,0:T(8,128)(2,1)S(1)} %fusion.2.refs_0_.own_ref) | copy-start | bytes 3145732
  58.1 4.2 %collective-permute-start.7 = (bf16[1024,512]{1,0:T(8,128)(2,1)S(1)}, bf16[1024,512]{1,0:T(8,128)(2,1)S(1)}, u32[]{:S(2)}, u32[]{:S(2)}) collective-permute-start(bf16[1024,512]{1,0:T(8,128)(2,1)S(1)} %fusion.2.refs_0_.own_ref), channel_id=1, source_target_pairs={{0,16},{16,0},{32,48},{48,32},{64,80},{80,64},{96,112},{112,96},{1... | collective-permute-start | bytes 3145736 | tf_op jit(solution)/shard_map/ppermute | solution.py:272
  58.6 27.2 %collective-permute-start.5 = (bf16[1024,512]{1,0:T(8,128)(2,1)S(1)}, bf16[1024,512]{1,0:T(8,128)(2,1)S(1)}, u32[]{:S(2)}, u32[]{:S(2)}) collective-permute-start(bf16[1024,512]{1,0:T(8,128)(2,1)S(1)} %fusion.2.refs_0_.own_ref), channel_id=1, source_target_pairs={{0,32},{16,48},{32,64},{48,80},{64,96},{80,112},{96,0},{112,16},{1... | collective-permute-start | bytes 3145736 | tf_op jit(solution)/shard_map/ppermute | solution.py:272
  60.2 25.5 %collective-permute-start.6 = (bf16[1024,512]{1,0:T(8,128)(2,1)S(1)}, bf16[1024,512]{1,0:T(8,128)(2,1)S(1)}, u32[]{:S(2)}, u32[]{:S(2)}) collective-permute-start(bf16[1024,512]{1,0:T(8,128)(2,1)S(1)} %fusion.2.refs_0_.own_ref), channel_id=1, source_target_pairs={{0,96},{16,112},{32,0},{48,16},{64,32},{80,48},{96,64},{112,80},{1... | collective-permute-start | bytes 3145736 | tf_op jit(solution)/shard_map/ppermute | solution.py:272
  85.7 3.6 %collective-permute-start.10 = (bf16[1024,512]{1,0:T(8,128)(2,1)S(1)}, bf16[1024,512]{1,0:T(8,128)(2,1)S(1)}, u32[]{:S(2)}, u32[]{:S(2)}) collective-permute-start(bf16[1024,512]{1,0:T(8,128)(2,1)S(1)} %collective-permute-done.5.refs_0_), channel_id=1, source_target_pairs={{0,16},{16,0},{32,48},{48,32},{64,80},{80,64},{96,112},{112,96},{1... | collective-permute-start | bytes 3145736 | tf_op jit(solution)/shard_map/ppermute | solution.py:272
  86.4 3.8 %collective-permute-start.11 = (bf16[1024,512]{1,0:T(8,128)(2,1)S(1)}, bf16[1024,512]{1,0:T(8,128)(2,1)S(1)}, u32[]{:S(2)}, u32[]{:S(2)}) collective-permute-start(bf16[1024,512]{1,0:T(8,128)(2,1)S(1)} %collective-permute-done.6.refs_2_), channel_id=1, source_target_pairs={{0,16},{16,0},{32,48},{48,32},{64,80},{80,64},{96,112},{112,96},{1... | collective-permute-start | bytes 3145736 | tf_op jit(solution)/shard_map/ppermute | solution.py:272
  86.5 14.3 %collective-permute-start.8 = (bf16[512,512]{1,0:T(8,128)(2,1)S(1)}, bf16[512,512]{1,0:T(8,128)(2,1)S(1)}, u32[]{:S(2)}, u32[]{:S(2)}) collective-permute-start(bf16[512,512]{1,0:T(8,128)(2,1)S(1)} %slice.14), channel_id=1, source_target_pairs={{0,32},{16,48},{32,64},{48,80},{64,96},{80,112},{96,0},{112,16},{1... | collective-permute-start | bytes 1572872 | tf_op jit(solution)/shard_map/ppermute | solution.py:272
  87.6 13.2 %collective-permute-start.9 = (bf16[512,512]{1,0:T(8,128)(2,1)S(1)}, bf16[512,512]{1,0:T(8,128)(2,1)S(1)}, u32[]{:S(2)}, u32[]{:S(2)}) collective-permute-start(bf16[512,512]{1,0:T(8,128)(2,1)S(1)} %slice.15), channel_id=1, source_target_pairs={{0,96},{16,112},{32,0},{48,16},{64,32},{80,48},{96,64},{112,80},{1... | collective-permute-start | bytes 1572872 | tf_op jit(solution)/shard_map/ppermute | solution.py:272
  100.8 2.9 %collective-permute-start.12 = (bf16[512,512]{1,0:T(8,128)(2,1)S(1)}, bf16[512,512]{1,0:T(8,128)(2,1)S(1)}, u32[]{:S(2)}, u32[]{:S(2)}) collective-permute-start(bf16[512,512]{1,0:T(8,128)(2,1)S(1)} %collective-permute-done.8.refs_0_), channel_id=1, source_target_pairs={{0,16},{16,0},{32,48},{48,32},{64,80},{80,64},{96,112},{112,96},{1... | collective-permute-start | bytes 1572872 | tf_op jit(solution)/shard_map/ppermute | solution.py:272
  102.2 2.3 %collective-permute-start.13 = (bf16[512,512]{1,0:T(8,128)(2,1)S(1)}, bf16[512,512]{1,0:T(8,128)(2,1)S(1)}, u32[]{:S(2)}, u32[]{:S(2)}) collective-permute-start(bf16[512,512]{1,0:T(8,128)(2,1)S(1)} %collective-permute-done.9.refs_1_), channel_id=1, source_target_pairs={{0,16},{16,0},{32,48},{48,32},{64,80},{80,64},{96,112},{112,96},{1... | collective-permute-start | bytes 1572872 | tf_op jit(solution)/shard_map/ppermute | solution.py:272
  109.2 0.7 copy-start.2

commit v5 on v4

--- a/solution.py
+++ b/solution.py
@@ -14,32 +14,32 @@
 BF16 = jnp.bfloat16
 
 
-def arrange_kernel(core_ref, x_ref, w_ref, out_ref):
+def arrange_kernel(low, high, core_ref, x_ref, w_ref, out_ref):
     peers, _, columns = out_ref.shape
-    half = w_ref.shape[1]
-    rows = columns - half
+    total = x_ref.shape[1] // peers
+    rows = high - low
     for q in range(peers):
-        out_ref[q, :, :rows] = x_ref[:, q * rows : (q + 1) * rows]
-        out_ref[q, :, rows:] = w_ref[...]
-
-
-def arrange(features, weight, core, peers):
+        out_ref[q, :, :rows] = x_ref[:, q * total + low : q * total + high]
+        if columns > rows:
+            out_ref[q, :, rows:] = w_ref[...]
+
+
+def arrange(features, weight, core, peers, low, high, half):
     depth, columns = features.shape
-    half = weight.shape[1] // 2
     rows = columns // peers
     step = 4
     return pl.pallas_call(
-        arrange_kernel,
+        functools.partial(arrange_kernel, low, high),
         grid_spec=pltpu.PrefetchScalarGridSpec(
             num_scalar_prefetch=1,
             grid=(peers // step,),
             in_specs=[
                 pl.BlockSpec((depth, step * rows), lambda i, core_ref: (0, i)),
-                pl.BlockSpec((depth, half), lambda i, core_ref: (0, core_ref[0])),
+                pl.BlockSpec((depth, weight.shape[1] // 2), lambda i, core_ref: (0, core_ref[0])),
             ],
-            out_specs=pl.BlockSpec((step, depth, rows + half), lambda i, core_ref: (i, 0, 0)),
+            out_specs=pl.BlockSpec((step, depth, high - low + half), lambda i, core_ref: (i, 0, 0)),
         ),
-        out_shape=jax.ShapeDtypeStruct((peers, depth, rows + half), BF16),
+        out_shape=jax.ShapeDtypeStruct((peers, depth, high - low + half), BF16),
         name="arrange",
     )(core.reshape(1), features, weight)
 
@@ -271,8 +271,15 @@
         pairs = [(p, (p + 2 * up) % n_graph ^ cores) for p in range(n_graph)]
         return lax.ppermute(x, "graph", pairs)
 
-    outgoing = arrange(node_features.T, proj_weight, core, n_feat)
-    got = lax.all_to_all(outgoing, "feat", 0, 0, tiled=True).reshape(n_feat * depth, rows_local + width // 2)
+    cut = local_blocks // 2
+    rows_a, half = cut * block_rows, width // 2
+    features = node_features.T
+    got = lax.all_to_all(
+        arrange(features, proj_weight, core, n_feat, 0, rows_a, half), "feat", 0, 0, tiled=True
+    ).reshape(n_feat * depth, rows_a + half)
+    outgoing = arrange(features, proj_weight, core, n_feat, rows_a, rows_local, 0)
+    got, outgoing = lax.optimization_barrier((got, outgoing))
+    later = lax.all_to_all(outgoing, "feat", 0, 0, tiled=True).reshape(n_feat * depth, rows_local - rows_a)
 
     tables = jnp.stack([send_blocks[0]] + [send(send_blocks[0], d) for d in range(1, levels)])
     tables = jnp.stack([tables, send(tables, 0, 1)], axis=1)
@@ -286,12 +293,12 @@
     got, src_vectors, tgt_vectors, index, slots = lax.optimization_barrier(
         (got, src_vectors, tgt_vectors, index, slots)
     )
-    mine = got[:, rows_local:]
+    mine = got[:, rows_a:]
     other = send(mine, 0, 1)
     whole = jnp.where(core == 0, jnp.concatenate([mine, other], axis=1), jnp.concatenate([other, mine], axis=1))
-    hidden = lax.dot_general(
-        got[:, :rows_local], whole, (((0,), (0,)), ((), ())), preferred_element_type=F32
-    ).astype(BF16)
+
+    def project(x):
+        return lax.dot_general(x, whole, (((0,), (0,)), ((), ())), preferred_element_type=F32).astype(BF16)
 
     def both(pieces):
         return [pieces, [(send(x, 0, 1), low, high) for x, low, high in pieces]]
@@ -299,15 +306,30 @@
     def spread(group, first, kept):
         return transform(group, first, index, relation_weight, src_vectors, block_rows, *kept)
 
-    middle = local_blocks // 2
-    split = middle * block_rows
-    up, down = send(hidden, 1), send(hidden, -1)
-    done = spread(both([(hidden, 0, local_blocks)]), 0, (None, None))
-    up, down, done = lax.optimization_barrier((up, down, done))
-    far_up, far_down = send(up[:split], 1), send(down[split:], -1)
-    done = spread(both([(up, 0, local_blocks)]) + both([(down, 0, local_blocks)]), 2, done)
-    far_up, far_down, done = lax.optimization_barrier((far_up, far_down, done))
-    values, scores = spread(both([(far_up, 0, middle), (far_down, middle, local_blocks)]), 6, done)
+    def ring(part):
+        return send(part, 1), send(part, -1)
+
+    def forward(up, down):
+        middle = up.shape[0] // 2
+        return send(up[:middle], 1), send(down[middle:], -1)
+
+    a = project(got[:, :rows_a])
+    up_a, down_a = ring(a)
+    later, up_a, down_a = lax.optimization_barrier((later, up_a, down_a))
+    far_a = forward(up_a, down_a)
+    b = project(later)
+    up_b, down_b = ring(b)
+    done = spread(both([(a, 0, cut), (b, cut, local_blocks)]), 0, (None, None))
+    up_b, down_b, done = lax.optimization_barrier((up_b, down_b, done))
+    far_b = forward(up_b, down_b)
+    done = spread(
+        both([(up_a, 0, cut), (up_b, cut, local_blocks)]) + both([(down_a, 0, cut), (down_b, cut, local_blocks)]), 2, done
+    )
+    far_b, done = lax.optimization_barrier((far_b, done))
+    quarter = cut // 2
+    far = [(x, n * quarter, (n + 1) * quarter) for n, x in enumerate(far_a + far_b)]
+    values, scores = spread(both(far), 6, done)
+    hidden = jnp.concatenate([a, b])
     total = n_graph * CAP
     values = values.reshape((total,) + values.shape[2:])
     scores = scores.reshape((total,) + scores.shape[2:])

time: 131 us -> 139 us (1.061)
  starting transfers between devices: 26.7 us -> 39.2 us
  waiting for transfers between devices: 53.7 us -> 42.4 us
  Pallas kernels: 41.8 us -> 45.5 us
  matrix products: 3.8 us -> 5.78 us
    all_to_all x1, waiting for transfers between devices: 27.2 us -> 13.5 us  [shards(): lax.all_to_all(outgoing, 'feat', 0, 0, tiled=True)]
    all_to_all x0 -> x1, waiting for transfers between devices: none -> 11.4 us  [shards(): lax.all_to_all(arrange(features, proj_weight, core, n_feat, 0, rows_a, ha...]
    ppermute x14 -> x23, starting transfers between devices: 18.9 us -> 27.9 us  [send(): return lax.ppermute(x, 'graph', pairs)]
    ppermute x14 -> x23, waiting for transfers between devices: 26.5 us -> 17.5 us  [send(): return lax.ppermute(x, 'graph', pairs)]
    all_to_all x0 -> x1, starting transfers between devices: none -> 6.9 us  [shards(): lax.all_to_all(arrange(features, proj_weight, core, n_feat, 0, rows_a, ha...]
    all_to_all x1, starting transfers between devices: 7.77 us -> 4.34 us  [shards(): lax.all_to_all(outgoing, 'feat', 0, 0, tiled=True)]
    pallas_call x1 -> x2, Pallas kernels: 3.89 us -> 7.24 us  [arrange(): pl.pallas_call(functools.partial(arrange_kernel, low, high), grid_spec=pl...]
    dot_general x1 -> x2, matrix products: 2.89 us -> 4.87 us  [project(): lax.dot_general(x, whole, (((0,), (0,)), ((), ())), preferred_element_typ...]
  transfers between devices with their start and end apart: 15 -> 25, of which waited for: 7 -> 7; matrix products, arithmetic and copies ran while one was open for 3% -> 7% of each run, Pallas kernels for 9% -> 14%
where the time goes in v5:
time: 139 us; the launch traced here: 138 us
  Pallas kernels  45.5 us (33%)
  waiting for transfers between devices  42.4 us (31%)
  starting transfers between devices  39.2 us (28%)
  matrix products  5.78 us (4%)
  other arithmetic  2.84 us (2%)
  local copies, waits for them, and re-layouts  1.81 us (1%)
    ppermute x23, starting transfers between devices, send(): return lax.ppermute(x, 'graph', pairs)  27.9 us
    pallas_call x1, Pallas kernels, attend(): pl.pallas_call(attend_kernel, grid_spec=pltpu.PrefetchScalarGridSpec(num_...  21.1 us
    ppermute x23, waiting for transfers between devices, send(): return lax.ppermute(x, 'graph', pairs)  17.5 us
    pallas_call x3, Pallas kernels, transform(): pl.pallas_call(functools.partial(transform_kernel, bounds, first), grid_s...  17.2 us
    all_to_all x1, waiting for transfers between devices, shards(): lax.all_to_all(outgoing, 'feat', 0, 0, tiled=True)  13.5 us
    all_to_all x1, waiting for transfers between devices, shards(): lax.all_to_all(arrange(features, proj_weight, core, n_feat, 0, rows_a, ha...  11.4 us
    pallas_call x2, Pallas kernels, arrange(): pl.pallas_call(functools.partial(arrange_kernel, low, high), grid_spec=pl...  7.24 us
    all_to_all x1, starting transfers between devices, shards(): lax.all_to_all(arrange(features, proj_weight, core, n_feat, 0, rows_a, ha...  6.9 us
  transfers between devices with their start and end apart: 25, of which 7 were waited for; matrix products, arithmetic and copies ran while one was open for 7% of the time, Pallas kernels for 14%

profile of v5, /device:TPU:1, one launch (start us, length us, event | category | flops | bytes accessed | tf_op | source)
XLA Modules:
  0.0 138.0 jit_solution(9294678510810647391)
XLA Ops:
  0.0 2.5 %collective-permute-start = (s32[8,4]{0,1:T(4,128)}, s32[8,4]{0,1:T(4,128)S(1)}, u32[]{:S(2)}, u32[]{:S(2)}) collective-permute-start(s32[8,4]{0,1:T(4,128)} %bitcast.49), channel_id=1, source_target_pairs={{0,32},{16,48},{32,64},{48,80},{64,96},{80,112},{96,0},{112,16},{1... | collective-permute-start | bytes 392 | tf_op jit(solution)/shard_map/ppermute | solution.py:272
  2.5 3.3 %collective-permute-start.1 = (s32[8,4]{0,1:T(4,128)}, s32[8,4]{0,1:T(4,128)S(1)}, u32[]{:S(2)}, u32[]{:S(2)}) collective-permute-start(s32[8,4]{0,1:T(4,128)} %bitcast.50), channel_id=1, source_target_pairs={{0,64},{16,80},{32,96},{48,112},{64,0},{80,16},{96,32},{112,48},{1... | collective-permute-start | bytes 392 | tf_op jit(solution)/shard_map/ppermute | solution.py:272
  5.8 0.7 collective-permute-start.2
  6.5 3.7 %arrange.2 = bf16[16,64,768]{2,1,0:T(8,128)(2,1)} custom-call(s32[1]{0:T(128)} %bitcast.core_ref, bf16[64,16384]{1,0:T(8,128)(2,1)} %bitcast.42, bf16[64,512]{1,0:T(8,128)(2,1)} %w_ref.3), custom_call_target="tpu_custom_call" | custom-call | tf_op jit(solution)/shard_map/arrange/pallas_call | solution.py:31
  10.2 0.0 copy-start.7
  10.2 0.0 copy-start.5
  10.2 6.9 %all-to-all-start = ((bf16[16,64,768]{2,1,0:T(8,128)(2,1)}), bf16[16,64,768]{2,1,0:T(8,128)(2,1)S(1)}, u32[]{:S(2)}, u32[]{:S(2)}) async-start(bf16[16,64,768]{2,1,0:T(8,128)(2,1)} %arrange.2), calls=%async_computation | async-start | bytes 3145728 | tf_op jit(solution)/shard_map/all_to_all | solution.py:277
  17.1 0.0 copy-start.6
  17.2 0.1 copy.17
  17.4 0.9 fusion
  18.4 0.1 pad.24.clone
  18.4 0.6 fusion.15.slot_ref
  19.1 0.1 maximum_maximum_fusion.refs_5_.refs_9_
  19.1 0.1 select_multiply_fusion
  19.3 0.1 fusion.6
  19.4 0.0 collective-permute-done
  19.4 0.0 collective-permute-done.1
  19.4 1.9 %collective-permute-start.3 = (s32[4,8,4]{1,2,0:T(4,128)S(1)}, s32[4,8,4]{1,2,0:T(4,128)S(1)}, u32[]{:S(2)}, u32[]{:S(2)}) collective-permute-start(s32[4,8,4]{1,2,0:T(4,128)S(1)} %get-tuple-element.60), channel_id=1, source_target_pairs={{0,16},{16,0},{32,48},{48,32},{64,80},{80,64},{96,112},{112,96},{1... | collective-permute-start | bytes 1544 | tf_op jit(solution)/shard_map/ppermute | solution.py:272
  21.3 0.8 pad_maximum_fusion.1.tgt_ref
  22.1 3.6 %arrange.3 = bf16[16,64,512]{2,1,0:T(8,128)(2,1)} custom-call(s32[1]{0:T(128)} %bitcast.core_ref, bf16[64,16384]{1,0:T(8,128)(2,1)} %bitcast.43, bf16[64,512]{1,0:T(8,128)(2,1)} %w_ref.3), custom_call_target="tpu_custom_call" | custom-call | tf_op jit(solution)/shard_map/arrange/pallas_call | solution.py:31
  25.7 0.1 copy.18
  25.8 0.0 collective-permute-done.3
  25.8 0.1 copy.19
  25.9 0.6 gather_fusion
  26.5 11.4 %all-to-all-done = bf16[16,64,768]{2,1,0:T(8,128)(2,1)S(1)} async-done(((bf16[16,64,768]{2,1,0:T(8,128)(2,1)}), bf16[16,64,768]{2,1,0:T(8,128)(2,1)S(1)}, u32[]{:S(2)}, u32[]{:S(2)}) %all-to-all-start) | async-done | bytes 1572896 | tf_op jit(solution)/shard_map/all_to_all | solution.py:277
  37.9 3.9 %collective-permute-start.4 = (bf16[1024,256]{1,0:T(8,128)(2,1)S(1)}, bf16[1024,256]{1,0:T(8,128)(2,1)}, u32[]{:S(2)}, u32[]{:S(2)}) collective-permute-start(bf16[1024,256]{1,0:T(8,128)(2,1)S(1)} %slice.19), channel_id=1, source_target_pairs={{0,16},{16,0},{32,48},{48,32},{64,80},{80,64},{96,112},{112,96},{1... | collective-permute-start | bytes 1572872 | tf_op jit(solution)/shard_map/ppermute | solution.py:272
  41.8 4.3 %all-to-all-start.1 = ((bf16[16,64,512]{2,1,0:T(8,128)(2,1)}), bf16[16,64,512]{2,1,0:T(8,128)(2,1)}, u32[]{:S(2)}, u32[]{:S(2)}) async-start(bf16[16,64,512]{2,1,0:T(8,128)(2,1)} %arrange.3), calls=%async_computation.1 | async-start | bytes 2097152 | tf_op jit(solution)/shard_map/all_to_all | solution.py:282
  46.2 0.0 collective-permute-done.4
  46.2 2.3 %convolution_convert_fusion.1.refs_0_ = bf16[512,512]{1,0:T(8,128)(2,1)S(1)} fusion(bf16[1024,768]{1,0:T(8,128)(2,1)S(1)} %bitcast.45, bf16[1024,256]{1,0:T(8,128)(2,1)} %collective-permute-done.4, bf16[1024,256]{1,0:T(8,128)(2,1)} %copy-done.2, pred[]{:T(512)S(6)} %eq.25), kind=kOutput, calls=%fused_computation.2 | convolution fusion | flops 541851648 | bytes 2621441 | tf_op jit(solution)/shard_map/dot_general | solution.py:301
  48.5 0.8 collective-permute-start.5
  49.3 1.9 %collective-permute-start.6 = (bf16[512,512]{1,0:T(8,128)(2,1)S(1)}, bf16[512,512]{1,0:T(8,128)(2,1)S(1)}, u32[]{:S(2)}, u32[]{:S(2)}) collective-permute-start(bf16[512,512]{1,0:T(8,128)(2,1)S(1)} %convolution_convert_fusion.1.refs_0_), channel_id=1, source_target_pairs={{0,96},{16,112},{32,0},{48,16},{64,32},{80,48},{96,64},{112,80},{1... | collective-permute-start | bytes 1572872 | tf_op jit(solution)/shard_map/ppermute | solution.py:272
  51.3 0.6 collective-permute-start.11
  51.8 13.5 %all-to-all-done.1 = bf16[16,64,512]{2,1,0:T(8,128)(2,1)} async-done(((bf16[16,64,512]{2,1,0:T(8,128)(2,1)}), bf16[16,64,512]{2,1,0:T(8,128)(2,1)}, u32[]{:S(2)}, u32[]{:S(2)}) %all-to-all-start.1) | async-done | bytes 1048608 | tf_op jit(solution)/shard_map/all_to_all | solution.py:282
  65.3 2.6 %convolution_convert_fusion.refs_1_ = bf16[512,512]{1,0:T(8,128)(2,1)S(1)} fusion(bf16[1024,512]{1,0:T(8,128)(2,1)} %bitcast.17, bf16[1024,256]{1,0:T(8,128)(2,1)} %collective-permute-done.4, bf16[1024,256]{1,0:T(8,128)(2,1)} %copy-done.2, pred[]{:T(512)S(6)} %eq.25), kind=kOutput, calls=%fused_computation.1 | convolution fusion | flops 541851648 | bytes 2621441 | tf_op jit(solution)/shard_map/dot_general | solution.py:301
  67.9 0.9 collective-permute-start.12
  68.8 0.7 collective-permute-start.10
  69.5 0.8 collective-permute-start.9
  70.3 0.8 collective-permute-start.7
  71.1 0.0 collective-permute-done.11.refs_2_
  71.1 0.9 collective-permute-start.15
  72.0 0.1 collective-permute-start.17
  72.1 4.6 %transform.3 = (bf16[8,4,2,128,512]{4,3,2,1,0:T(8,128)(2,1)}, f32[8,4,8,128]{3,2,1,0:T(8,128)S(1)}) custom-call(s32[8,4]{1,0:T(8,128)S(1)} %bitcast.38, bf16[512,512]{1,0:T(8,128)(2,1)S(1)} %convolution_convert_fusion.1.refs_0_, bf16[512,512]{1,0:T(8,128)(2,1)S(1)} %convolution_convert_fusion.refs_1_, bf16[512,512]{1,0:T(8,128)(2,1)S(1)} %collective-permute-done.11.refs_2_, ...), custom_call_target="tpu_custom_call" | custom-call | tf_op jit(solution)/shard_map/transform/pallas_call | solution.py:110
  76.8 5.5 %collective-permute-done.10.refs_5_ = bf16[512,512]{1,0:T(8,128)(2,1)S(1)} collective-permute-done((bf16[512,512]{1,0:T(8,128)(2,1)S(1)}, bf16[512,512]{1,0:T(8,128)(2,1)S(1)}, u32[]{:S(2)}, u32[]{:S(2)}) %collective-permute-start.10) | collective-permute-done | bytes 524320 | tf_op jit(solution)/shard_map/ppermute | solution.py:272
  82.3 1.6 %collective-permute-done.9.refs_1_ = bf16[512,512]{1,0:T(8,128)(2,1)S(1)} collective-permute-done((bf16[512,512]{1,0:T(8,128)(2,1)S(1)}, bf16[512,512]{1,0:T(8,128)(2,1)S(1)}, u32[]{:S(2)}, u32[]{:S(2)}) %collective-permute-start.9) | collective-permute-done | bytes 524320 | tf_op jit(solution)/shard_map/ppermute | solution.py:272
  83.8 2.0 %collective-permute-start.16 = (bf16[512,512]{1,0:T(8,128)(2,1)S(1)}, bf16[512,512]{1,0:T(8,128)(2,1)S(1)}, u32[]{:S(2)}, u32[]{:S(2)}) collective-permute-start(bf16[512,512]{1,0:T(8,128)(2,1)S(1)} %collective-permute-done.9.refs_1_), channel_id=1, source_target_pairs={{0,16},{16,0},{32,48},{48,32},{64,80},{80,64},{96,112},{112,96},{1... | collective-permute-start | bytes 1572872 | tf_op jit(solution)/shard_map/ppermute | solution.py:272
  85.8 0.0 collective-permute-start.18
  85.8 3.7 %collective-permute-done.7.refs_0_ = bf16[256,512]{1,0:T(8,128)(2,1)S(1)} collective-permute-done((bf16[256,512]{1,0:T(8,128)(2,1)S(1)}, bf16[256,512]{1,0:T(8,128)(2,1)S(1)}, u32[]{:S(2)}, u32[]{:S(2)}) %collective-permute-start.7) | collective-permute-done | bytes 262176 | tf_op jit(solution)/shard_map/ppermute | solution.py:272
  89.5 0.0 collective-permute-start.8
  89.5 6.6 %collective-permute-done.8.refs_1_ = bf16[256,512]{1,0:T(8,128)(2,1)S(1)} collective-permute-done((bf16[256,512]{1,0:T(8,128)(2,1)S(1)}, bf16[256,512]{1,0:T(8,128)(2,1)S(1)}, u32[]{:S(2)}, u32[]{:S(2)}) %collective-permute-start.8) | collective-permute-done | bytes 262176 | tf_op jit(solution)/shard_map/ppermute | solution.py:272
  96.1 0.0 collective-permute-start.13
  96.1 0.0 collective-permute-done.15.refs_2_
  96.1 2.7 %collective-permute-start.14 = (bf16[256,512]{1,0:T(8,128)(2,1)S(1)}, bf16[256,512]{1,0:T(8,128)(2,1)S(1)}, u32[]{:S(2)}, u32[]{:S(2)}) collective-permute-start(bf16[256,512]{1,0:T(8,128)(2,1)S(1)} %slice.23), channel_id=1, source_target_pairs={{0,96},{16,112},{32,0},{48,16},{64,32},{80,48},{96,64},{112,80},{1... | collective-permute-start | bytes 786440 | tf_op jit(solution)/shard_map/ppermute | solution.py:272
  98.8 2.7 %collective-permute-start.19 = (bf16[256,512]{1,0:T(8,128)(2,1)S(1)}, bf16[256,512]{1,0:T(8,128)(2,1)S(1)}, u32[]{:S(2)}, u32[]{:S(2)}) collective-permute-start(bf16[256,512]{1,0:T(8,128)(2,1)S(1)} %collective-permute-done.7.refs_0_), channel_id=1, source_target_pairs={{0,16},{16,0},{32,48},{48,32},{64,80},{80,64},{96,112},{112,96},{1... | collective-permute-start | bytes 786440 | tf_op jit(solution)/shard_map/ppermute | solution.py:272
  101.4 0.0 collective-permute-done.16.refs_3_
  101.4 0.1 collective-permute-start.20
  101.5 7.7 %transform.4 = (bf16[8,4,2,128,512]{4,3,2,1,0:T(8,128)(2,1)}, f32[8,4,8,128]{3,2,1,0:T(8,128)S(1)}) custom-call(s32[8,4]{1,0:T(8,128)S(1)} %bitcast.39, bf16[512,512]{1,0:T(8,128)(2,1)S(1)} %collective-permute-done.5.refs_0_, bf16[512,512]{1,0:T(8,128)(2,1)S(1)} %collective-permute-done.9.refs_1_, ...), custom_call_target="tpu_custom_call", output_to_operand_aliasing={{0}: (11, {}), {1}: (12, {})} | custom-call | tf_op jit(solution)/shard_map/transform/pallas_call | solution.py:110
  109.2 0.0 collective-permute-done.13.refs_2_
  109.2 0.5 collective-permute-start.21
  109.7 0.3 collective-permute-start.22
  110.0 1.1 pad_maximum_fusion.own_ref
  111.1 0.2 collective-permute-done.22.refs_7_
  111.3 4.8 %transform.5 = (bf16[8,4,2,128,512]{4,3,2,1,0:T(8,128)(2,1)}, f32[8,4,8,128]{3,2,1,0:T(8,128)S(1)}) custom-call(s32[8,4]{1,0:T(8,128)S(1)} %bitcast.40, bf16[256,512]{1,0:T(8,128)(2,1)S(1)} %collective-permute-done.7.refs_0_, bf16[256,512]{1,0:T(8,128)(2,1)S(1)} %collective-permute-done.8.refs_1_, ...), custom_call_target="tpu_custom_call", output_to_operand_aliasing={{0}: (11, {}), {1}: (12, {})} | custom-call | tf_op jit(solution)/shard_map/transform/pallas_call | solution.py:110
  116.1 0.7 copy-done.1
  116.8 21.1 %attend.1 = bf16[1024,512]{1,0:T(8,128)(2,1)} custom-call(s32[8,12]{1,0:T(8,128)} %rel_ref.1, s32[8,12]{1,0:T(8,128)} %fusion.15.slot_ref, bf16[1024,512]{1,0:T(8,128)(2,1)} %pad_maximum_fusion.own_ref, s32[8,12,128,128]{3,2,1,0:T(8,128)} %mask_ref.1, bf16[32,2,128,512]{3,2,1,0:T(8,128)(2,1)} %bitcast.41, f32[32,8,128]{2,1,0:T(8,128)} %bitcast.37, ...), custom_call_target="tpu_custom_call" | custom-call | tf_op jit(solution)/shard_map/attend/pallas_call | solution.py:202
  (39 shorter events, 0.3 us)
Async XLA Ops:
  0.0 19.4 %collective-permute-start = (s32[8,4]{0,1:T(4,128)}, s32[8,4]{0,1:T(4,128)S(1)}, u32[]{:S(2)}, u32[]{:S(2)}) collective-permute-start(s32[8,4]{0,1:T(4,128)} %bitcast.49), channel_id=1, source_target_pairs={{0,32},{16,48},{32,64},{48,80},{64,96},{80,112},{96,0},{112,16},{1... | collective-permute-start | bytes 392 | tf_op jit(solution)/shard_map/ppermute | solution.py:272
  2.5 16.9 %collective-permute-start.1 = (s32[8,4]{0,1:T(4,128)}, s32[8,4]{0,1:T(4,128)S(1)}, u32[]{:S(2)}, u32[]{:S(2)}) collective-permute-start(s32[8,4]{0,1:T(4,128)} %bitcast.50), channel_id=1, source_target_pairs={{0,64},{16,80},{32,96},{48,112},{64,0},{80,16},{96,32},{112,48},{1... | collective-permute-start | bytes 392 | tf_op jit(solution)/shard_map/ppermute | solution.py:272
  5.8 13.6 %collective-permute-start.2 = (s32[8,4]{0,1:T(4,128)}, s32[8,4]{0,1:T(4,128)S(1)}, u32[]{:S(2)}, u32[]{:S(2)}) collective-permute-start(s32[8,4]{0,1:T(4,128)} %bitcast.51), channel_id=1, source_target_pairs={{0,96},{16,112},{32,0},{48,16},{64,32},{80,48},{96,64},{112,80},{1... | collective-permute-start | bytes 392 | tf_op jit(solution)/shard_map/ppermute | solution.py:272
  10.2 7.0 %copy-start.3 = (f32[2,512]{1,0:T(2,128)S(1)}, f32[2,512]{1,0:T(2,128)}, u32[]{:S(2)}) copy-start(f32[2,512]{1,0:T(2,128)} %param.14) | copy-start | bytes 12292
  10.2 7.1 %copy-start.4 = (f32[2,512]{1,0:T(2,128)S(1)}, f32[2,512]{1,0:T(2,128)}, u32[]{:S(2)}) copy-start(f32[2,512]{1,0:T(2,128)} %param.13) | copy-start | bytes 12292
  10.2 7.2 %copy-start = (bf16[2,512,512]{2,1,0:T(8,128)(2,1)S(1)}, bf16[2,512,512]{2,1,0:T(8,128)(2,1)}, u32[]{:S(2)}) copy-start(bf16[2,512,512]{2,1,0:T(8,128)(2,1)} %refs_8_.3) | copy-start | bytes 3145732
  10.2 8.1 %copy-start.7 = (s32[4,1]{0,1:T(1,128)S(1)}, s32[4,1]{0,1:T(1,128)}, u32[]{:S(2)}) copy-start(s32[4,1]{0,1:T(1,128)} %constant.134) | copy-start | bytes 52
  10.2 8.2 %copy-start.5 = (s32[8,12]{1,0:T(8,128)S(1)}, s32[8,12]{1,0:T(8,128)}, u32[]{:S(2)}) copy-start(s32[8,12]{1,0:T(8,128)} %param.18) | copy-start | bytes 1156
  10.2 27.7 %all-to-all-start = ((bf16[16,64,768]{2,1,0:T(8,128)(2,1)}), bf16[16,64,768]{2,1,0:T(8,128)(2,1)S(1)}, u32[]{:S(2)}, u32[]{:S(2)}) async-start(bf16[16,64,768]{2,1,0:T(8,128)(2,1)} %arrange.2), calls=%async_computation | async-start | bytes 3145728 | tf_op jit(solution)/shard_map/all_to_all | solution.py:277
  17.1 2.3 %copy-start.6 = (s32[1,8,4]{1,2,0:T(4,128)S(1)}, s32[1,8,4]{1,2,0:T(4,128)}, u32[]{:S(2)}) copy-start(s32[1,8,4]{1,2,0:T(4,128)} %param.17) | copy-start | bytes 388
  19.4 6.3 %collective-permute-start.3 = (s32[4,8,4]{1,2,0:T(4,128)S(1)}, s32[4,8,4]{1,2,0:T(4,128)S(1)}, u32[]{:S(2)}, u32[]{:S(2)}) collective-permute-start(s32[4,8,4]{1,2,0:T(4,128)S(1)} %get-tuple-element.60), channel_id=1, source_target_pairs={{0,16},{16,0},{32,48},{48,32},{64,80},{80,64},{96,112},{112,96},{1... | collective-permute-start | bytes 1544 | tf_op jit(solution)/shard_map/ppermute | solution.py:272
  37.9 8.3 %copy-start.2 = (bf16[1024,256]{1,0:T(8,128)(2,1)}, bf16[1024,256]{1,0:T(8,128)(2,1)S(1)}, u32[]{:S(2)}) copy-start(bf16[1024,256]{1,0:T(8,128)(2,1)S(1)} %slice.19) | copy-start | bytes 1572868
  37.9 8.3 %collective-permute-start.4 = (bf16[1024,256]{1,0:T(8,128)(2,1)S(1)}, bf16[1024,256]{1,0:T(8,128)(2,1)}, u32[]{:S(2)}, u32[]{:S(2)}) collective-permute-start(bf16[1024,256]{1,0:T(8,128)(2,1)S(1)} %slice.19), channel_id=1, source_target_pairs={{0,16},{16,0},{32,48},{48,32},{64,80},{80,64},{96,112},{112,96},{1... | collective-permute-start | bytes 1572872 | tf_op jit(solution)/shard_map/ppermute | solution.py:272
  41.8 23.5 %all-to-all-start.1 = ((bf16[16,64,512]{2,1,0:T(8,128)(2,1)}), bf16[16,64,512]{2,1,0:T(8,128)(2,1)}, u32[]{:S(2)}, u32[]{:S(2)}) async-start(bf16[16,64,512]{2,1,0:T(8,128)(2,1)} %arrange.3), calls=%async_computation.1 | async-start | bytes 2097152 | tf_op jit(solution)/shard_map/all_to_all | solution.py:282
  48.5 16.8 %collective-permute-start.5 = (bf16[512,512]{1,0:T(8,128)(2,1)S(1)}, bf16[512,512]{1,0:T(8,128)(2,1)S(1)}, u32[]{:S(2)}, u32[]{:S(2)}) collective-permute-start(bf16[512,512]{1,0:T(8,128)(2,1)S(1)} %convolution_convert_fusion.1.refs_0_), channel_id=1, source_target_pairs={{0,32},{16,48},{32,64},{48,80},{64,96},{80,112},{96,0},{112,16},{1... | collective-permute-start | bytes 1572872 | tf_op jit(solution)/shard_map/ppermute | solution.py:272
  49.3 16.0 %collective-permute-start.6 = (bf16[512,512]{1,0:T(8,128)(2,1)S(1)}, bf16[512,512]{1,0:T(8,128)(2,1)S(1)}, u32[]{:S(2)}, u32[]{:S(2)}) collective-permute-start(bf16[512,512]{1,0:T(8,128)(2,1)S(1)} %convolution_convert_fusion.1.refs_0_), channel_id=1, source_target_pairs={{0,96},{16,112},{32,0},{48,16},{64,32},{80,48},{96,64},{112,80},{1... | collective-permute-start | bytes 1572872 | tf_op jit(solution)/shard_map/ppermute | solution.py:272
  51.3 19.8 %collective-permute-start.11 = (bf16[512,512]{1,0:T(8,128)(2,1)S(1)}, bf16[512,512]{1,0:T(8,128)(2,1)S(1)}, u32[]{:S(2)}, u32[]{:S(2)}) collective-permute-start(bf16[512,512]{1,0:T(8,128)(2,1)S(1)} %convolution_convert_fusion.1.refs_0_), channel_id=1, source_target_pairs={{0,16},{16,0},{32,48},{48,32},{64,80},{80,64},{96,112},{112,96},{1... | collective-permute-start | bytes 1572872 | tf_op jit(solution)/shard_map/ppermute | solution.py:272
  67.9 4.1 %collective-permute-start.12 = (bf16[512,512]{1,0:T(8,128)(2,1)S(1)}, bf16[512,512]{1,0:T(8,128)(2,1)S(1)}, u32[]{:S(2)}, u32[]{:S(2)}) collective-permute-start(bf16[512,512]{1,0:T(8,128)(2,1)S(1)} %convolution_convert_fusion.refs_1_), channel_id=1, source_target_pairs={{0,16},{16,0},{32,48},{48,32},{64,80},{80,64},{96,112},{112,96},{1... | collective-permute-start | bytes 1572872 | tf_op jit(solution)/shard_map/ppermute | solution.py:272
  68.8 13.5 %collective-permute-start.10 = (bf16[512,512]{1,0:T(8,128)(2,1)S(1)}, bf16[512,512]{1,0:T(8,128)(2,1)S(1)}, u32[]{:S(2)}, u32[]{:S(2)}) collective-permute-start(bf16[512,512]{1,0:T(8,128)(2,1)S(1)} %convolution_convert_fusion.refs_1_), channel_id=1, source_target_pairs={{0,96},{16,112},{32,0},{48,16},{64,32},{80,48},{96,64},{112,80},{1... | collective-permute-start | bytes 1572872 | tf_op jit(solution)/shard_map/ppermute | solution.py:272
  69.5 14.4 %collective-permute-start.9 = (bf16[512,512]{1,0:T(8,128)(2,1)S(1)}, bf16[512,512]{1,0:T(8,128)(2,1)S(1)}, u32[]{:S(2)}, u32[]{:S(2)}) collective-permute-start(bf16[512,512]{1,0:T(8,128)(2,1)S(1)} %convolution_convert_fusion.refs_1_), channel_id=1, source_target_pairs={{0,32},{16,48},{32,64},{48,80},{64,96},{80,112},{96,0},{112,16},{1... | collective-permute-start | bytes 1572872 | tf_op jit(solution)/shard_map/ppermute | solution.py:272
  70.3 19.2 %collective-permute-start.7 = (bf16[256,512]{1,0:T(8,128)(2,1)S(1)}, bf16[256,512]{1,0:T(8,128)(2,1)S(1)}, u32[]{:S(2)}, u32[]{:S(2)}) collective-permute-start(bf16[256,512]{1,0:T(8,128)(2,1)S(1)} %slice.20), channel_id=1, source_target_pairs={{0,32},{16,48},{32,64},{48,80},{64,96},{80,112},{96,0},{112,16},{1... | collective-permute-start | bytes 786440 | tf_op jit(solution)/shard_map/ppermute | solution.py:272
  71.1 25.0 %collective-permute-start.15 = (bf16[512,512]{1,0:T(8,128)(2,1)S(1)}, bf16[512,512]{1,0:T(8,128)(2,1)S(1)}, u32[]{:S(2)}, u32[]{:S(2)}) collective-permute-start(bf16[512,512]{1,0:T(8,128)(2,1)S(1)} %collective-permute-done.5.refs_0_), channel_id=1, source_target_pairs={{0,16},{16,0},{32,48},{48,32},{64,80},{80,64},{96,112},{112,96},{1... | collective-permute-start | bytes 1572872 | tf_op jit(solution)/shard_map/ppermute | solution.py:272
  72.0 26.7 %collective-permute-start.17 = (bf16[512,512]{1,0:T(8,128)(2,1)S(1)}, bf16[512,512]{1,0:T(8,128)(2,1)S(1)}, u32[]{:S(2)}, u32[]{:S(2)}) collective-permute-start(bf16[512,512]{1,0:T(8,128)(2,1)S(1)} %collective-permute-done.6.refs_4_), channel_id=1, source_target_pairs={{0,16},{16,0},{32,48},{48,32},{64,80},{80,64},{96,112},{112,96},{1... | collective-permute-start | bytes 1572872 | tf_op jit(solution)/shard_map/ppermute | solution.py:272
  83.8 17.6 %collective-permute-start.16 = (bf16[512,512]{1,0:T(8,128)(2,1)S(1)}, bf16[512,512]{1,0:T(8,128)(2,1)S(1)}, u32[]{:S(2)}, u32[]{:S(2)}) collective-permute-start(bf16[512,512]{1,0:T(8,128)(2,1)S(1)} %collective-permute-done.9.refs_1_), channel_id=1, source_target_pairs={{0,16},{16,0},{32,48},{48,32},{64,80},{80,64},{96,112},{112,96},{1... | collective-permute-start | bytes 1572872 | tf_op jit(solution)/shard_map/ppermute | solution.py:272
  85.8 15.7 %collective-permute-start.18 = (bf16[512,512]{1,0:T(8,128)(2,1)S(1)}, bf16[512,512]{1,0:T(8,128)(2,1)S(1)}, u32[]{:S(2)}, u32[]{:S(2)}) collective-permute-start(bf16[512,512]{1,0:T(8,128)(2,1)S(1)} %collective-permute-done.10.refs_5_), channel_id=1, source_target_pairs={{0,16},{16,0},{32,48},{48,32},{64,80},{80,64},{96,112},{112,96},{1... | collective-permute-start | bytes 1572872 | tf_op jit(solution)/shard_map/ppermute | solution.py:272
  89.5 6.6 %collective-permute-start.8 = (bf16[256,512]{1,0:T(8,128)(2,1)S(1)}, bf16[256,512]{1,0:T(8,128)(2,1)S(1)}, u32[]{:S(2)}, u32[]{:S(2)}) collective-permute-start(bf16[256,512]{1,0:T(8,128)(2,1)S(1)} %slice.21), channel_id=1, source_target_pairs={{0,96},{16,112},{32,0},{48,16},{64,32},{80,48},{96,64},{112,80},{1... | collective-permute-start | bytes 786440 | tf_op jit(solution)/shard_map/ppermute | solution.py:272
  96.1 13.1 %collective-permute-start.13 = (bf16[256,512]{1,0:T(8,128)(2,1)S(1)}, bf16[256,512]{1,0:T(8,128)(2,1)S(1)}, u32[]{:S(2)}, u32[]{:S(2)}) collective-permute-start(bf16[256,512]{1,0:T(8,128)(2,1)S(1)} %slice.22), channel_id=1, source_target_pairs={{0,32},{16,48},{32,64},{48,80},{64,96},{80,112},{96,0},{112,16},{1... | collective-permute-start | bytes 786440 | tf_op jit(solution)/shard_map/ppermute | solution.py:272
  96.1 13.1 %collective-permute-start.14 = (bf16[256,512]{1,0:T(8,128)(2,1)S(1)}, bf16[256,512]{1,0:T(8,128)(2,1)S(1)}, u32[]{:S(2)}, u32[]{:S(2)}) collective-permute-start(bf16[256,512]{1,0:T(8,128)(2,1)S(1)} %slice.23), channel_id=1, source_target_pairs={{0,96},{16,112},{32,0},{48,16},{64,32},{80,48},{96,64},{112,80},{1... | collective-permute-start | bytes 786440 | tf_op jit(solution)/shard_map/ppermute | solution.py:272
  98.8 12.3 %collective-permute-start.19 = (bf16[256,512]{1,0:T(8,128)(2,1)S(1)}, bf16[256,512]{1,0:T(8,128)(2,1)S(1)}, u32[]{:S(2)}, u32[]{:S(2)}) collective-permute-start(bf16[256,512]{1,0:T(8,128)(2,1)S(1)} %collective-permute-done.7.refs_0_), channel_id=1, source_target_pairs={{0,16},{16,0},{32,48},{48,32},{64,80},{80,64},{96,112},{112,96},{1... | collective-permute-start | bytes 786440 | tf_op jit(solution)/shard_map/ppermute | solution.py:272
  101.4 9.6 %collective-permute-start.20 = (bf16[256,512]{1,0:T(8,128)(2,1)S(1)}, bf16[256,512]{1,0:T(8,128)(2,1)S(1)}, u32[]{:S(2)}, u32[]{:S(2)}) collective-permute-start(bf16[256,512]{1,0:T(8,128)(2,1)S(1)} %collective-permute-done.8.refs_1_), channel_id=1, source_target_pairs={{0,16},{16,0},{32,48},{48,32},{64,80},{80,64},{96,112},{112,96},{1... | collective-permute-start | bytes 786440 | tf_op jit(solution)/shard_map/ppermute | solution.py:272
  109.2 1.9 %collective-permute-start.21 = (bf16[256,512]{1,0:T(8,128)(2,1)S(1)}, bf16[256,512]{1,0:T(8,128)(2,1)S(1)}, u32[]{:S(2)}, u32[]{:S(2)}) collective-permute-start(bf16[256,512]{1,0:T(8,128)(2,1)S(1)} %collective-permute-done.13.refs_2_), channel_id=1, source_target_pairs={{0,16},{16,0},{32,48},{48,32},{64,80},{80,64},{96,112},{112,96},{1... | collective-permute-start | bytes 786440 | tf_op jit(solution)/shard_map/ppermute | solution.py:272
  109.7 1.5 %collective-permute-start.22 = (bf16[256,512]{1,0:T(8,128)(2,1)S(1)}, bf16[256,512]{1,0:T(8,128)(2,1)S(1)}, u32[]{:S(2)}, u32[]{:S(2)}) collective-permute-start(bf16[256,512]{1,0:T(8,128)(2,1)S(1)} %collective-permute-done.14.refs_3_), channel_id=1, source_target_pairs={{0,16},{16,0},{32,48},{48,32},{64,80},{80,64},{96,112},{112,96},{1... | collective-permute-start | bytes 786440 | tf_op jit(solution)/shard_map/ppermute | solution.py:272
  116.1 0.7 copy-start.1

commit v6 on v5

v6 whole, which is shorter than its diff:
```python
import functools

import jax
import jax.numpy as jnp
from jax import lax
from jax.experimental import pallas as pl
from jax.experimental.pallas import tpu as pltpu
from jax.sharding import PartitionSpec as P

HEADS = 4
CAP = 4
LOG2E = 1.4426950408889634
F32 = jnp.float32
BF16 = jnp.bfloat16


def arrange_kernel(low, high, core_ref, x_ref, w_ref, out_ref):
    peers, _, columns = out_ref.shape
    total = x_ref.shape[1] // peers
    rows = high - low
    for q in range(peers):
        out_ref[q, :, :rows] = x_ref[:, q * total + low : q * total + high]
        if columns > rows:
            out_ref[q, :, rows:] = w_ref[...]


def arrange(features, weight, core, peers, low, high, half):
    depth, columns = features.shape
    rows = columns // peers
    step = 4
    return pl.pallas_call(
        functools.partial(arrange_kernel, low, high),
        grid_spec=pltpu.PrefetchScalarGridSpec(
            num_scalar_prefetch=1,
            grid=(peers // step,),
            in_specs=[
                pl.BlockSpec((depth, step * rows), lambda i, core_ref: (0, i)),
                pl.BlockSpec((depth, weight.shape[1] // 2), lambda i, core_ref: (0, core_ref[0])),
            ],
            out_specs=pl.BlockSpec((step, depth, high - low + half), lambda i, core_ref: (i, 0, 0)),
        ),
        out_shape=jax.ShapeDtypeStruct((peers, depth, high - low + half), BF16),
        name="arrange",
    )(core.reshape(1), features, weight)


def three_parts(x):
    hi = lax.reduce_precision(x, 8, 7)
    rest = x - hi
    mid = lax.reduce_precision(rest, 8, 7)
    return hi.astype(BF16), mid.astype(BF16), (rest - mid).astype(BF16)


def transform_kernel(bounds, first, idx_ref, *refs):
    n_pieces = sum(len(p) for p in bounds)
    pieces = refs[:n_pieces]
    rw_ref, src_ref = refs[n_pieces : n_pieces + 2]
    val_ref, score_ref, hid_ref, sem = refs[-4:]
    relations, block = val_ref.shape[1:3]
    cap = sem.shape[1]

    def copy(piece, row, source, c):
        return pltpu.make_async_copy(
            piece.at[pl.ds(row, block)], hid_ref.at[source, pl.ds(c * block, block)], sem.at[source, c]
        )

    begin = 0
    for source in range(len(bounds)):
        for c in range(cap):
            wanted = idx_ref[first + source, c]
            for n, (low, high) in enumerate(bounds[source]):

                @pl.when((wanted >= low) & (wanted < high))
                def _():
                    copy(pieces[begin + n], pl.multiple_of((wanted - low) * block, block), source, c).start()

        begin += len(bounds[source])
    for source in range(len(bounds)):
        for c in range(cap):
            copy(pieces[0], 0, source, c).wait()
        hid = hid_ref[source]
        at = (first + source) * cap
        for r in range(relations):
            moved = jnp.dot(hid, rw_ref[r], preferred_element_type=F32).astype(BF16)
            for c in range(cap):
                val_ref[at + c, r] = moved[c * block : (c + 1) * block]
        raw = lax.dot_general(src_ref[...], hid, (((1,), (1,)), ((), ())), preferred_element_type=F32)
        score = raw[0:8] + raw[8:16] + raw[16:24]
        for c in range(cap):
            score_ref[at + c] = score[:, c * block : (c + 1) * block]

def transform(sources, first, index, relation_weight, src_vectors, block, values, scores):
    bounds = tuple(tuple((low, high) for _, low, high in pieces) for pieces in sources)
    arrays = [array for pieces in sources for array, _, _ in pieces]
    peers, cap = index.shape
    relations, width = relation_weight.shape[:2]
    anywhere, inside = pl.BlockSpec(memory_space=pl.ANY), pl.BlockSpec(memory_space=pltpu.VMEM)
    kept = () if values is None else (values, scores)
    at = 1 + len(arrays) + 2
    return pl.pallas_call(
        functools.partial(transform_kernel, bounds, first),
        in_specs=[pl.BlockSpec(memory_space=pltpu.SMEM)] + [anywhere] * len(arrays) + [inside] * (2 + len(kept)),
        out_specs=[inside, inside],
        scratch_shapes=[
            pltpu.VMEM((len(bounds), cap * block, width), BF16),
            pltpu.SemaphoreType.DMA((len(bounds), cap)),
        ],
        out_shape=[
            jax.ShapeDtypeStruct((peers * cap, relations, block, width), BF16),
            jax.ShapeDtypeStruct((peers * cap, 8, block), F32),
        ],
        input_output_aliases={at + n: n for n in range(len(kept))},
        compiler_params=pltpu.CompilerParams(vmem_limit_bytes=24 * 1024 * 1024),
        name="transform",
    )(index, *arrays, relation_weight, src_vectors, *kept)


def cap_kernel(mask_ref, cap_ref):
    cap_ref[...] = jnp.where(mask_ref[...] > 0, jnp.inf, 0.0).astype(BF16)


def caps(edge_mask):
    shape = edge_mask.shape
    spec = pl.BlockSpec((1,) + shape[1:], lambda b: (b, 0, 0, 0))
    return pl.pallas_call(
        cap_kernel,
        grid=shape[:1],
        in_specs=[spec],
        out_specs=spec,
        out_shape=jax.ShapeDtypeStruct(shape, BF16),
        name="caps",
    )(edge_mask)


def attend_kernel(
    rel_ref, slot_ref, own_ref, cap_ref, tgt_ref, val_ref, score_ref, out_ref, u_ref, w_ref, prob_ref
):
    blocks, lists, rows, cols = cap_ref.shape
    relations = u_ref.shape[1]
    ones = jnp.ones((lists * cols, cols), BF16)

    def body(b, carry):
        own = own_ref[b]
        target = jnp.dot(own, tgt_ref[0], preferred_element_type=F32)
        target += jnp.dot(own, tgt_ref[1], preferred_element_type=F32)
        target += jnp.dot(own, tgt_ref[2], preferred_element_type=F32)
        rels = [rel_ref[b, k] for k in range(lists)]
        slots = [slot_ref[b, k] for k in range(lists)]

        def spread(r, h):
            return jnp.broadcast_to(target[:, r * HEADS + h : r * HEADS + h + 1], (rows, cols))

        def finish(h):
            lanes = slice(h * cols, (h + 1) * cols)
            value = jnp.concatenate([val_ref[slots[k], rels[k], :, lanes] for k in range(lists)], axis=0)
            summed = jnp.dot(prob_ref[h], jnp.concatenate([value, ones], axis=1), preferred_element_type=F32)
            total = summed[:, cols:]
            mixed = summed[:, :cols] / total + own[:, lanes].astype(F32)
            out_ref[b, :, lanes] = jnp.where(mixed > 0, mixed, jnp.exp(jnp.minimum(mixed, 0.0)) - 1.0).astype(BF16)
            return total

        reach = [jnp.full((8, cols), -jnp.inf, F32) for _ in range(relations)]
        for k in range(lists):
            source = score_ref[slots[k]]
            for r in range(relations):
                reach[r] = jnp.maximum(reach[r], jnp.where(rels[k] == r, source, -jnp.inf))
        for h in range(HEADS):
            bound = jnp.full((rows, cols), -jnp.inf, F32)
            for r in range(relations):
                c = r * HEADS + h
                most = spread(r, h) + jnp.max(reach[r][c : c + 1, :], axis=1, keepdims=True)
                bound = jnp.maximum(bound, jnp.maximum(most, 0.2 * most))
            for r in range(relations):
                u_ref[h, r] = spread(r, h) - bound
                w_ref[h, r] = 0.2 * spread(r, h) - bound
        least = jnp.full((rows, cols), jnp.inf, F32)
        for h in range(HEADS):
            for k in range(lists):
                source = score_ref[slots[k], pl.ds(rels[k] * HEADS + h, 1), :]
                logit = jnp.maximum(u_ref[h, rels[k]] + source, w_ref[h, rels[k]] + 0.2 * source)
                prob = jnp.exp2(logit).astype(BF16)
                prob_ref[h, :, k * cols : (k + 1) * cols] = jnp.minimum(prob, cap_ref[b, k])
        for h in range(HEADS):
            least = jnp.minimum(least, finish(h))

        @pl.when(jnp.logical_not(jnp.min(least) > 2.0**-90))
        def _():
            for h in range(HEADS):
                for r in range(relations):
                    u_ref[h, r] = spread(r, h)

                def raw(k):
                    r, slot = rel_ref[b, k], slot_ref[b, k]
                    x = u_ref[h, r] + score_ref[slot, pl.ds(r * HEADS + h, 1), :]
                    return jnp.where(cap_ref[b, k].astype(F32) > 0, jnp.maximum(x, 0.2 * x), -jnp.inf)

                w_ref[h, 0] = jnp.full((rows, cols), -jnp.inf, F32)

                def climb(k, carry):
                    w_ref[h, 0] = jnp.maximum(w_ref[h, 0], raw(k))
                    return carry

                lax.fori_loop(0, lists, climb, 0)
                w_ref[h, 0] = jnp.broadcast_to(jnp.max(w_ref[h, 0], axis=1, keepdims=True), (rows, cols))

                def weigh(k, carry):
                    at = pl.ds(pl.multiple_of(k * cols, cols), cols)
                    prob_ref[h, :, at] = jnp.exp2(raw(k) - w_ref[h, 0]).astype(BF16)
                    return carry

                lax.fori_loop(0, lists, weigh, 0)
                finish(h)

        return carry

    lax.fori_loop(0, blocks, body, 0)


def attend(hidden, cap, relation_ids, source_slots, values, scores, tgt_vectors):
    blocks, lists, rows, cols = cap.shape
    width = hidden.shape[1]
    relations = values.shape[1]
    scalars, inside = pl.BlockSpec(memory_space=pltpu.SMEM), pl.BlockSpec(memory_space=pltpu.VMEM)
    return pl.pallas_call(
        attend_kernel,
        in_specs=[scalars] * 2 + [inside] * 5,
        out_specs=inside,
        scratch_shapes=[
            pltpu.VMEM((HEADS, relations, rows, cols), F32),
            pltpu.VMEM((HEADS, relations, rows, cols), F32),
            pltpu.VMEM((HEADS, rows, lists * cols), BF16),
        ],
        out_shape=jax.ShapeDtypeStruct((blocks, rows, width), BF16),
        compiler_params=pltpu.CompilerParams(vmem_limit_bytes=24 * 1024 * 1024),
        name="attend",
    )(relation_ids, source_slots, hidden.reshape(blocks, rows, width), cap, tgt_vectors, values, scores).reshape(
        blocks * rows, width
    )


def score_vectors(relation_weight, att_source, att_target):
    relations, width = att_source.shape
    head_width = width // HEADS
    split = att_source.reshape(relations, HEADS, head_width)
    moved = jnp.einsum(
        "rche,rhe->rhc",
        relation_weight.astype(F32).reshape(relations, width, HEADS, head_width),
        split,
        precision=lax.Precision.HIGHEST,
        preferred_element_type=F32,
    ).reshape(relations * HEADS, width)
    src = jnp.concatenate(three_parts(moved * LOG2E) + (jnp.zeros((8, width), BF16),), axis=0)
    own_head = (jnp.arange(width)[:, None] // head_width) == (jnp.arange(relations * HEADS)[None, :] % HEADS)
    spread = jnp.repeat(att_target.T, HEADS, axis=1)
    tgt = jnp.where(own_head, spread, 0.0) * LOG2E
    tgt = jnp.pad(tgt, ((0, 0), (0, 128 - relations * HEADS)))
    return src, jnp.stack(three_parts(tgt))


def shards(
    node_features,
    proj_weight,
    relation_weight,
    att_source,
    att_target,
    edge_mask,
    relation_ids,
    send_blocks,
    source_slots,
):
    block_rows = edge_mask.shape[-1]
    local_blocks = edge_mask.shape[0]
    rows_local = local_blocks * block_rows
    depth, width = proj_weight.shape
    n_feat = lax.axis_size("feat")
    n_graph = lax.axis_size("graph")
    levels = n_graph // 2
    place = lax.axis_index("graph")
    core, level = lax.rem(place, 2), place // 2

    def send(x, up, cores=0):
        pairs = [(p, (p + 2 * up) % n_graph ^ cores) for p in range(n_graph)]
        return lax.ppermute(x, "graph", pairs)

    cut = local_blocks // 2
    rows_a, half = cut * block_rows, width // 2
    features = node_features.T
    got = lax.all_to_all(
        arrange(features, proj_weight, core, n_feat, 0, rows_a, half), "feat", 0, 0, tiled=True
    ).reshape(n_feat * depth, rows_a + half)
    outgoing = arrange(features, proj_weight, core, n_feat, rows_a, rows_local, 0)
    got, outgoing, send_blocks, cap = lax.optimization_barrier((got, outgoing, send_blocks, caps(edge_mask)))
    later = lax.all_to_all(outgoing, "feat", 0, 0, tiled=True).reshape(n_feat * depth, rows_local - rows_a)

    tables = jnp.stack([send_blocks[0]] + [send(send_blocks[0], d) for d in range(1, levels)])
    tables = jnp.stack([tables, send(tables, 0, 1)], axis=1)
    order = jnp.array([0, 1, 3, 2])
    index = tables[order, :, place].reshape(n_graph, CAP)
    peer = source_slots // CAP
    distance = (level - peer // 2 + levels) % levels
    slots = (2 * (distance ^ (distance >> 1)) + (peer % 2 ^ core)) * CAP + source_slots % CAP
    src_vectors, tgt_vectors = score_vectors(relation_weight, att_source, att_target)

    later, src_vectors, tgt_vectors, slots = lax.optimization_barrier((later, src_vectors, tgt_vectors, slots))
    mine = got[:, rows_a:]
    other = send(mine, 0, 1)
    whole = jnp.where(core == 0, jnp.concatenate([mine, other], axis=1), jnp.concatenate([other, mine], axis=1))

    def project(x):
        return lax.dot_general(x, whole, (((0,), (0,)), ((), ())), preferred_element_type=F32).astype(BF16)

    def both(pieces):
        return [pieces, [(send(x, 0, 1), low, high) for x, low, high in pieces]]

    def spread(group, first, kept):
        return transform(group, first, index, relation_weight, src_vectors, block_rows, *kept)

    def ring(part):
        return send(part, 1), send(part, -1)

    def forward(up, down):
        middle = up.shape[0] // 2
        return send(up[:middle], 1), send(down[middle:], -1)

    a = project(got[:, :rows_a])
    up_a, down_a = ring(a)
    far_a = forward(up_a, down_a)
    later, far_a = lax.optimization_barrier((later, far_a))
    b = project(later)
    up_b, down_b = ring(b)
    done = spread(both([(a, 0, cut), (b, cut, local_blocks)]), 0, (None, None))
    up_b, down_b, done = lax.optimization_barrier((up_b, down_b, done))
    far_b = forward(up_b, down_b)
    done = spread(
        both([(up_a, 0, cut), (up_b, cut, local_blocks)]) + both([(down_a, 0, cut), (down_b, cut, local_blocks)]), 2, done
    )
    far_b, done = lax.optimization_barrier((far_b, done))
    quarter = cut // 2
    far = [(x, n * quarter, (n + 1) * quarter) for n, x in enumerate(far_a + far_b)]
    values, scores = spread(both(far), 6, done)
    return attend(jnp.concatenate([a, b]), cap, relation_ids, slots, values, scores, tgt_vectors)


def solution(mesh):
    placed = (
        P("graph", "feat"),
        P("feat", None),
        P(),
        P(),
        P(),
        P(("graph", "feat"), None, None, None),
        P(("graph", "feat"), None),
        P(("graph", "feat"), None, None),
        P(("graph", "feat"), None),
    )
    return jax.shard_map(
        shards, mesh=mesh, in_specs=placed, out_specs=P(("graph", "feat"), None), check_vma=False
    )
```

time: 139 us -> 185 us (1.33)
  Pallas kernels: 45.5 us -> 79.4 us
  waiting for transfers between devices: 42.4 us -> 50.2 us
  local copies, waits for them, and re-layouts: 1.81 us -> 8.69 us
  starting transfers between devices: 39.2 us -> 35.6 us
    pallas_call x4 -> x5, Pallas kernels: 38.2 us -> 72.2 us  [the longest x1 52.3 us: attend(): pl.pallas_call(attend_kernel, in_specs=[scalars] * 2 + [inside] * 5, out_...]
    ppermute x23, waiting for transfers between devices: 17.5 us -> 38.9 us  [send(): return lax.ppermute(x, 'graph', pairs)]
    all_to_all x1, waiting for transfers between devices: 13.5 us -> 0.01 us  [shards(): lax.all_to_all(outgoing, 'feat', 0, 0, tiled=True)]
    ppermute x23, starting transfers between devices: 27.9 us -> 23.7 us  [send(): return lax.ppermute(x, 'graph', pairs)]
    slice x4, local copies, waits for them, and re-layouts: 0.07 us -> 2.67 us  [forward(): return (send(up[:middle], 1), send(down[middle:], -1))]
    another operation x2, other arithmetic: 0.05 us -> 1.97 us  [shards(): tables = jnp.stack([tables, send(tables, 0, 1)], axis=1)]
    another operation x2, local copies, waits for them, and re-layouts: 0.2 us -> 2.08 us  [shards(): tables = jnp.stack([tables, send(tables, 0, 1)], axis=1)]
  transfers between devices with their start and end apart: 25 -> 25, of which waited for: 7 -> 9; matrix products, arithmetic and copies ran while one was open for 7% -> 9% of each run, Pallas kernels for 14% -> 11%
where the time goes in v6:
time: 185 us; the launch traced here: 184 us
  Pallas kernels  79.4 us (43%)
  waiting for transfers between devices  50.2 us (27%)
  starting transfers between devices  35.6 us (19%)
  local copies, waits for them, and re-layouts  8.69 us (5%)
  matrix products  5.8 us (3%)
  other arithmetic  3.68 us (2%)
    pallas_call x1, Pallas kernels, attend(): pl.pallas_call(attend_kernel, in_specs=[scalars] * 2 + [inside] * 5, out_...  52.3 us
    ppermute x23, waiting for transfers between devices, send(): return lax.ppermute(x, 'graph', pairs)  38.9 us
    ppermute x23, starting transfers between devices, send(): return lax.ppermute(x, 'graph', pairs)  23.7 us
    pallas_call x3, Pallas kernels, transform(): pl.pallas_call(functools.partial(transform_kernel, bounds, first), in_spe...  12.9 us
    all_to_all x1, waiting for transfers between devices, shards(): lax.all_to_all(arrange(features, proj_weight, core, n_feat, 0, rows_a, ha...  11.3 us
    all_to_all x1, starting transfers between devices, shards(): lax.all_to_all(arrange(features, proj_weight, core, n_feat, 0, rows_a, ha...  7.58 us
    pallas_call x2, Pallas kernels, arrange(): pl.pallas_call(functools.partial(arrange_kernel, low, high), grid_spec=pl...  7.25 us
    pallas_call x1, Pallas kernels, caps(): pl.pallas_call(cap_kernel, grid=shape[:1], in_specs=[spec], out_specs=spe...  7.01 us
  transfers between devices with their start and end apart: 25, of which 9 were waited for; matrix products, arithmetic and copies ran while one was open for 9% of the time, Pallas kernels for 11%

profile of v6, /device:TPU:1, one launch (start us, length us, event | category | flops | bytes accessed | tf_op | source)
XLA Modules:
  0.0 183.7 jit_solution(14672431334956380467)
XLA Ops:
  0.0 3.7 %arrange.2 = bf16[16,64,768]{2,1,0:T(8,128)(2,1)} custom-call(s32[1]{0:T(128)} %bitcast.core_ref, bf16[64,16384]{1,0:T(8,128)(2,1)} %bitcast.41, bf16[64,512]{1,0:T(8,128)(2,1)} %w_ref.3), custom_call_target="tpu_custom_call" | custom-call | tf_op jit(solution)/shard_map/arrange/pallas_call | solution.py:31
  3.7 7.6 %all-to-all-start = ((bf16[16,64,768]{2,1,0:T(8,128)(2,1)}), bf16[16,64,768]{2,1,0:T(8,128)(2,1)S(1)}, u32[]{:S(2)}, u32[]{:S(2)}) async-start(bf16[16,64,768]{2,1,0:T(8,128)(2,1)} %arrange.2), calls=%async_computation | async-start | bytes 3145728 | tf_op jit(solution)/shard_map/all_to_all | solution.py:288
  11.3 3.6 %arrange.3 = bf16[16,64,512]{2,1,0:T(8,128)(2,1)} custom-call(s32[1]{0:T(128)} %bitcast.core_ref, bf16[64,16384]{1,0:T(8,128)(2,1)} %bitcast.42, bf16[64,512]{1,0:T(8,128)(2,1)} %w_ref.3), custom_call_target="tpu_custom_call" | custom-call | tf_op jit(solution)/shard_map/arrange/pallas_call | solution.py:31
  14.8 7.0 %caps.1.cap_ref = bf16[8,12,128,128]{3,2,1,0:T(8,128)(2,1)} custom-call(s32[8,12,128,128]{3,2,1,0:T(8,128)} %mask_ref.1), custom_call_target="tpu_custom_call" | custom-call | tf_op jit(solution)/shard_map/caps/pallas_call | solution.py:125
  21.9 0.9 fusion
  22.8 11.3 %all-to-all-done = bf16[16,64,768]{2,1,0:T(8,128)(2,1)S(1)} async-done(((bf16[16,64,768]{2,1,0:T(8,128)(2,1)}), bf16[16,64,768]{2,1,0:T(8,128)(2,1)S(1)}, u32[]{:S(2)}, u32[]{:S(2)}) %all-to-all-start) | async-done | bytes 1572896 | tf_op jit(solution)/shard_map/all_to_all | solution.py:288
  34.1 0.9 slice.19
  35.0 2.5 %collective-permute-start = (bf16[1024,256]{1,0:T(8,128)(2,1)}, bf16[1024,256]{1,0:T(8,128)(2,1)}, u32[]{:S(2)}, u32[]{:S(2)}) collective-permute-start(bf16[1024,256]{1,0:T(8,128)(2,1)} %slice.19), channel_id=1, source_target_pairs={{0,16},{16,0},{32,48},{48,32},{64,80},{80,64},{96,112},{112,96},{1... | collective-permute-start | bytes 1572872 | tf_op jit(solution)/shard_map/ppermute | solution.py:283
  37.6 0.1 copy.17
  37.8 0.1 select_multiply_fusion
  37.9 4.3 %all-to-all-start.1 = ((bf16[16,64,512]{2,1,0:T(8,128)(2,1)}), bf16[16,64,512]{2,1,0:T(8,128)(2,1)}, u32[]{:S(2)}, u32[]{:S(2)}) async-start(bf16[16,64,512]{2,1,0:T(8,128)(2,1)} %arrange.3), calls=%async_computation.1 | async-start | bytes 2097152 | tf_op jit(solution)/shard_map/all_to_all | solution.py:293
  42.3 0.0 copy-start.9
  42.3 2.3 %convolution_convert_fusion.1.refs_0_ = bf16[512,512]{1,0:T(8,128)(2,1)S(1)} fusion(bf16[1024,768]{1,0:T(8,128)(2,1)S(1)} %bitcast.44, bf16[1024,256]{1,0:T(8,128)(2,1)} %collective-permute-done, bf16[1024,256]{1,0:T(8,128)(2,1)} %slice.19, pred[]{:T(512)S(6)} %eq.25), kind=kOutput, calls=%fused_computation.2 | convolution fusion | flops 541851648 | bytes 2621441 | tf_op jit(solution)/shard_map/dot_general | solution.py:310
  44.6 1.7 collective-permute-start.1
  46.3 2.2 %collective-permute-start.3 = (bf16[512,512]{1,0:T(8,128)(2,1)S(1)}, bf16[512,512]{1,0:T(8,128)(2,1)S(1)}, u32[]{:S(2)}, u32[]{:S(2)}) collective-permute-start(bf16[512,512]{1,0:T(8,128)(2,1)S(1)} %convolution_convert_fusion.1.refs_0_), channel_id=1, source_target_pairs={{0,96},{16,112},{32,0},{48,16},{64,32},{80,48},{96,64},{112,80},{1... | collective-permute-start | bytes 1572872 | tf_op jit(solution)/shard_map/ppermute | solution.py:283
  48.5 0.1 fusion.6
  48.7 12.2 %collective-permute-done.1.refs_0_ = bf16[512,512]{1,0:T(8,128)(2,1)S(1)} collective-permute-done((bf16[512,512]{1,0:T(8,128)(2,1)S(1)}, bf16[512,512]{1,0:T(8,128)(2,1)S(1)}, u32[]{:S(2)}, u32[]{:S(2)}) %collective-permute-start.1) | collective-permute-done | bytes 524320 | tf_op jit(solution)/shard_map/ppermute | solution.py:283
  60.8 0.1 collective-permute-start.2
  60.9 0.7 slice.27
  61.7 2.7 %collective-permute-start.4 = (bf16[256,512]{1,0:T(8,128)(2,1)}, bf16[256,512]{1,0:T(8,128)(2,1)}, u32[]{:S(2)}, u32[]{:S(2)}) collective-permute-start(bf16[256,512]{1,0:T(8,128)(2,1)} %slice.27), channel_id=1, source_target_pairs={{0,96},{16,112},{32,0},{48,16},{64,32},{80,48},{96,64},{112,80},{1... | collective-permute-start | bytes 786440 | tf_op jit(solution)/shard_map/ppermute | solution.py:283
  64.4 0.1 pad.24.clone
  64.4 0.7 maximum_maximum_fusion.refs_5_.refs_9_
  65.1 1.1 collective-permute-start.11
  66.2 3.3 %collective-permute-done.2.refs_0_ = bf16[256,512]{1,0:T(8,128)(2,1)S(1)} collective-permute-done((bf16[256,512]{1,0:T(8,128)(2,1)S(1)}, bf16[256,512]{1,0:T(8,128)(2,1)S(1)}, u32[]{:S(2)}, u32[]{:S(2)}) %collective-permute-start.2) | collective-permute-done | bytes 262176 | tf_op jit(solution)/shard_map/ppermute | solution.py:283
  69.5 0.7 copy-done.4
  70.2 2.6 %convolution_convert_fusion.refs_1_ = bf16[512,512]{1,0:T(8,128)(2,1)S(1)} fusion(bf16[1024,512]{1,0:T(8,128)(2,1)} %bitcast.3, bf16[1024,256]{1,0:T(8,128)(2,1)} %collective-permute-done, bf16[1024,256]{1,0:T(8,128)(2,1)} %slice.19, pred[]{:T(512)S(6)} %eq.25), kind=kOutput, calls=%fused_computation.1 | convolution fusion | flops 541851648 | bytes 2621441 | tf_op jit(solution)/shard_map/dot_general | solution.py:310
  72.8 1.4 collective-permute-start.12
  74.2 3.0 %collective-permute-start.10 = (bf16[512,512]{1,0:T(8,128)(2,1)S(1)}, bf16[512,512]{1,0:T(8,128)(2,1)}, u32[]{:S(2)}, u32[]{:S(2)}) collective-permute-start(bf16[512,512]{1,0:T(8,128)(2,1)S(1)} %convolution_convert_fusion.refs_1_), channel_id=1, source_target_pairs={{0,96},{16,112},{32,0},{48,16},{64,32},{80,48},{96,64},{112,80},{1... | collective-permute-start | bytes 1572872 | tf_op jit(solution)/shard_map/ppermute | solution.py:283
  77.2 0.0 collective-permute-start.5
  77.2 14.5 %collective-permute-done.5 = s32[8,4]{0,1:T(4,128)S(1)} collective-permute-done((s32[8,4]{0,1:T(4,128)S(1)}, s32[8,4]{0,1:T(4,128)S(1)}, u32[]{:S(2)}, u32[]{:S(2)}) %collective-permute-start.5) | collective-permute-done | bytes 160 | tf_op jit(solution)/shard_map/ppermute | solution.py:283
  91.8 3.9 %collective-permute-done.6 = s32[8,4]{0,1:T(4,128)S(1)} collective-permute-done((s32[8,4]{0,1:T(4,128)S(1)}, s32[8,4]{0,1:T(4,128)S(1)}, u32[]{:S(2)}, u32[]{:S(2)}) %collective-permute-start.6) | collective-permute-done | bytes 160 | tf_op jit(solution)/shard_map/ppermute | solution.py:283
  95.7 0.0 collective-permute-start.7
  95.7 2.4 %collective-permute-done.7 = s32[8,4]{0,1:T(4,128)S(1)} collective-permute-done((s32[8,4]{0,1:T(4,128)S(1)}, s32[8,4]{0,1:T(4,128)S(1)}, u32[]{:S(2)}, u32[]{:S(2)}) %collective-permute-start.7) | collective-permute-done | bytes 160 | tf_op jit(solution)/shard_map/ppermute | solution.py:283
  98.1 0.6 fusion.24
  98.7 3.5 %collective-permute-start.8 = (s32[4,8,4]{1,2,0:T(4,128)}, s32[4,8,4]{1,2,0:T(4,128)}, u32[]{:S(2)}, u32[]{:S(2)}) collective-permute-start(s32[4,8,4]{1,2,0:T(4,128)} %get-tuple-element.62), channel_id=1, source_target_pairs={{0,16},{16,0},{32,48},{48,32},{64,80},{80,64},{96,112},{112,96},{1... | collective-permute-start | bytes 1544 | tf_op jit(solution)/shard_map/ppermute | solution.py:283
  102.2 1.2 collective-permute-done.8
  103.4 0.3 collective-permute-start.15
  103.7 0.7 or_bitcast_fusion
  104.4 0.7 copy.18
  105.1 1.4 copy.19
  106.4 1.4 pad_add_fusion
  107.8 1.3 gather_fusion
  109.1 0.0 collective-permute-done.11.refs_2_
  109.2 0.2 collective-permute-start.17
  109.4 0.8 copy-done.2
  110.2 3.3 %transform.3 = (bf16[32,2,128,512]{3,2,1,0:T(8,128)(2,1)S(1)}, f32[32,8,128]{2,1,0:T(8,128)S(1)}) custom-call(s32[8,4]{1,0:T(8,128)S(1)} %bitcast.38, bf16[512,512]{1,0:T(8,128)(2,1)S(1)} %convolution_convert_fusion.1.refs_0_, bf16[512,512]{1,0:T(8,128)(2,1)S(1)} %convolution_convert_fusion.refs_1_, bf16[512,512]{1,0:T(8,128)(2,1)} %collective-permute-done.11.refs_2_, ...), custom_call_target="tpu_custom_call" | custom-call | tf_op jit(solution)/shard_map/transform/pallas_call | solution.py:100
  113.5 0.0 collective-permute-done.10.refs_5_
  113.5 0.4 collective-permute-start.16
  113.9 0.2 collective-permute-start.18
  114.1 1.0 slice.22
  115.0 1.0 slice.23
  116.0 0.1 collective-permute-start.13
  116.1 2.7 %collective-permute-start.14 = (bf16[256,512]{1,0:T(8,128)(2,1)S(1)}, bf16[256,512]{1,0:T(8,128)(2,1)S(1)}, u32[]{:S(2)}, u32[]{:S(2)}) collective-permute-start(bf16[256,512]{1,0:T(8,128)(2,1)S(1)} %slice.23), channel_id=1, source_target_pairs={{0,96},{16,112},{32,0},{48,16},{64,32},{80,48},{96,64},{112,80},{1... | collective-permute-start | bytes 786440 | tf_op jit(solution)/shard_map/ppermute | solution.py:283
  118.8 0.9 collective-permute-start.19
  119.7 0.1 collective-permute-start.20
  119.8 6.0 %transform.4 = (bf16[32,2,128,512]{3,2,1,0:T(8,128)(2,1)S(1)}, f32[32,8,128]{2,1,0:T(8,128)S(1)}) custom-call(s32[8,4]{1,0:T(8,128)S(1)} %bitcast.39, bf16[512,512]{1,0:T(8,128)(2,1)S(1)} %collective-permute-done.1.refs_0_, bf16[512,512]{1,0:T(8,128)(2,1)} %collective-permute-done.9.refs_1_, ...), custom_call_target="tpu_custom_call", output_to_operand_aliasing={{0}: (11, {}), {1}: (12, {})} | custom-call | tf_op jit(solution)/shard_map/transform/pallas_call | solution.py:100
  125.8 0.5 collective-permute-start.21
  126.3 0.1 collective-permute-start.22
  126.4 0.1 pad_maximum_fusion
  126.4 0.0 copy-start.6
  126.5 1.0 collective-permute-done.21.refs_6_
  127.4 0.4 collective-permute-done.22.refs_7_
  127.8 3.6 %transform.5 = (bf16[32,2,128,512]{3,2,1,0:T(8,128)(2,1)S(1)}, f32[32,8,128]{2,1,0:T(8,128)S(1)}) custom-call(s32[8,4]{1,0:T(8,128)S(1)} %bitcast.40, bf16[256,512]{1,0:T(8,128)(2,1)S(1)} %copy-done.5, bf16[256,512]{1,0:T(8,128)(2,1)} %collective-permute-done.4.refs_1_, ...), custom_call_target="tpu_custom_call", output_to_operand_aliasing={{0}: (11, {}), {1}: (12, {})} | custom-call | tf_op jit(solution)/shard_map/transform/pallas_call | solution.py:100
  131.5 52.3 %attend.1 = bf16[8,128,512]{2,1,0:T(8,128)(2,1)} custom-call(s32[8,12]{1,0:T(8,128)S(1)} %copy-done.6, s32[8,12]{1,0:T(8,128)S(1)} %fusion.15.slot_ref, bf16[8,128,512]{2,1,0:T(8,128)(2,1)S(1)} %bitcast.37, bf16[8,12,128,128]{3,2,1,0:T(8,128)(2,1)S(1)} %copy-done, bf16[3,512,128]{2,1,0:T(8,128)(2,1)S(1)} %pad_maximum_fusion.1.tgt_ref, ...), custom_call_target="tpu_custom_call" | custom-call | tf_op jit(solution)/shard_map/attend/pallas_call | solution.py:224
  (46 shorter events, 0.2 us)
Async XLA Ops:
  3.7 30.5 %all-to-all-start = ((bf16[16,64,768]{2,1,0:T(8,128)(2,1)}), bf16[16,64,768]{2,1,0:T(8,128)(2,1)S(1)}, u32[]{:S(2)}, u32[]{:S(2)}) async-start(bf16[16,64,768]{2,1,0:T(8,128)(2,1)} %arrange.2), calls=%async_computation | async-start | bytes 3145728 | tf_op jit(solution)/shard_map/all_to_all | solution.py:288
  14.8 7.0 %copy-start.8 = (f32[2,512]{1,0:T(2,128)S(1)}, f32[2,512]{1,0:T(2,128)}, u32[]{:S(2)}) copy-start(f32[2,512]{1,0:T(2,128)} %param.13) | copy-start | bytes 12292
  14.8 7.0 %copy-start.1 = (bf16[2,512,512]{2,1,0:T(8,128)(2,1)S(1)}, bf16[2,512,512]{2,1,0:T(8,128)(2,1)}, u32[]{:S(2)}) copy-start(bf16[2,512,512]{2,1,0:T(8,128)(2,1)} %refs_8_.3) | copy-start | bytes 3145732
  21.9 15.7 %copy-start.7 = (f32[2,512]{1,0:T(2,128)S(1)}, f32[2,512]{1,0:T(2,128)}, u32[]{:S(2)}) copy-start(f32[2,512]{1,0:T(2,128)} %param.14) | copy-start | bytes 12292
  35.0 7.3 %collective-permute-start = (bf16[1024,256]{1,0:T(8,128)(2,1)}, bf16[1024,256]{1,0:T(8,128)(2,1)}, u32[]{:S(2)}, u32[]{:S(2)}) collective-permute-start(bf16[1024,256]{1,0:T(8,128)(2,1)} %slice.19), channel_id=1, source_target_pairs={{0,16},{16,0},{32,48},{48,32},{64,80},{80,64},{96,112},{112,96},{1... | collective-permute-start | bytes 1572872 | tf_op jit(solution)/shard_map/ppermute | solution.py:283
  37.9 28.3 %all-to-all-start.1 = ((bf16[16,64,512]{2,1,0:T(8,128)(2,1)}), bf16[16,64,512]{2,1,0:T(8,128)(2,1)}, u32[]{:S(2)}, u32[]{:S(2)}) async-start(bf16[16,64,512]{2,1,0:T(8,128)(2,1)} %arrange.3), calls=%async_computation.1 | async-start | bytes 2097152 | tf_op jit(solution)/shard_map/all_to_all | solution.py:293
  42.3 6.3 %copy-start.9 = (s32[8,12]{1,0:T(8,128)S(1)}, s32[8,12]{1,0:T(8,128)}, u32[]{:S(2)}) copy-start(s32[8,12]{1,0:T(8,128)} %param.18) | copy-start | bytes 1156
  44.6 16.2 %collective-permute-start.1 = (bf16[512,512]{1,0:T(8,128)(2,1)S(1)}, bf16[512,512]{1,0:T(8,128)(2,1)S(1)}, u32[]{:S(2)}, u32[]{:S(2)}) collective-permute-start(bf16[512,512]{1,0:T(8,128)(2,1)S(1)} %convolution_convert_fusion.1.refs_0_), channel_id=1, source_target_pairs={{0,32},{16,48},{32,64},{48,80},{64,96},{80,112},{96,0},{112,16},{1... | collective-permute-start | bytes 1572872 | tf_op jit(solution)/shard_map/ppermute | solution.py:283
  46.3 14.6 %collective-permute-start.3 = (bf16[512,512]{1,0:T(8,128)(2,1)S(1)}, bf16[512,512]{1,0:T(8,128)(2,1)S(1)}, u32[]{:S(2)}, u32[]{:S(2)}) collective-permute-start(bf16[512,512]{1,0:T(8,128)(2,1)S(1)} %convolution_convert_fusion.1.refs_0_), channel_id=1, source_target_pairs={{0,96},{16,112},{32,0},{48,16},{64,32},{80,48},{96,64},{112,80},{1... | collective-permute-start | bytes 1572872 | tf_op jit(solution)/shard_map/ppermute | solution.py:283
  60.8 8.7 %collective-permute-start.2 = (bf16[256,512]{1,0:T(8,128)(2,1)S(1)}, bf16[256,512]{1,0:T(8,128)(2,1)S(1)}, u32[]{:S(2)}, u32[]{:S(2)}) collective-permute-start(bf16[256,512]{1,0:T(8,128)(2,1)S(1)} %slice.26), channel_id=1, source_target_pairs={{0,32},{16,48},{32,64},{48,80},{64,96},{80,112},{96,0},{112,16},{1... | collective-permute-start | bytes 786440 | tf_op jit(solution)/shard_map/ppermute | solution.py:283
  61.7 8.5 %collective-permute-start.4 = (bf16[256,512]{1,0:T(8,128)(2,1)}, bf16[256,512]{1,0:T(8,128)(2,1)}, u32[]{:S(2)}, u32[]{:S(2)}) collective-permute-start(bf16[256,512]{1,0:T(8,128)(2,1)} %slice.27), channel_id=1, source_target_pairs={{0,96},{16,112},{32,0},{48,16},{64,32},{80,48},{96,64},{112,80},{1... | collective-permute-start | bytes 786440 | tf_op jit(solution)/shard_map/ppermute | solution.py:283
  65.1 44.0 %collective-permute-start.11 = (bf16[512,512]{1,0:T(8,128)(2,1)S(1)}, bf16[512,512]{1,0:T(8,128)(2,1)}, u32[]{:S(2)}, u32[]{:S(2)}) collective-permute-start(bf16[512,512]{1,0:T(8,128)(2,1)S(1)} %convolution_convert_fusion.1.refs_0_), channel_id=1, source_target_pairs={{0,16},{16,0},{32,48},{48,32},{64,80},{80,64},{96,112},{112,96},{1... | collective-permute-start | bytes 1572872 | tf_op jit(solution)/shard_map/ppermute | solution.py:283
  66.2 11.1 %copy-start.10 = (s32[1,8,4]{1,2,0:T(4,128)S(1)}, s32[1,8,4]{1,2,0:T(4,128)}, u32[]{:S(2)}) copy-start(s32[1,8,4]{1,2,0:T(4,128)} %param.17) | copy-start | bytes 388
  69.5 0.7 copy-start.4
  72.8 36.6 %collective-permute-start.12 = (bf16[512,512]{1,0:T(8,128)(2,1)S(1)}, bf16[512,512]{1,0:T(8,128)(2,1)}, u32[]{:S(2)}, u32[]{:S(2)}) collective-permute-start(bf16[512,512]{1,0:T(8,128)(2,1)S(1)} %convolution_convert_fusion.refs_1_), channel_id=1, source_target_pairs={{0,16},{16,0},{32,48},{48,32},{64,80},{80,64},{96,112},{112,96},{1... | collective-permute-start | bytes 1572872 | tf_op jit(solution)/shard_map/ppermute | solution.py:283
  74.2 39.2 %collective-permute-start.10 = (bf16[512,512]{1,0:T(8,128)(2,1)S(1)}, bf16[512,512]{1,0:T(8,128)(2,1)}, u32[]{:S(2)}, u32[]{:S(2)}) collective-permute-start(bf16[512,512]{1,0:T(8,128)(2,1)S(1)} %convolution_convert_fusion.refs_1_), channel_id=1, source_target_pairs={{0,96},{16,112},{32,0},{48,16},{64,32},{80,48},{96,64},{112,80},{1... | collective-permute-start | bytes 1572872 | tf_op jit(solution)/shard_map/ppermute | solution.py:283
  77.2 36.2 %collective-permute-start.9 = (bf16[512,512]{1,0:T(8,128)(2,1)S(1)}, bf16[512,512]{1,0:T(8,128)(2,1)}, u32[]{:S(2)}, u32[]{:S(2)}) collective-permute-start(bf16[512,512]{1,0:T(8,128)(2,1)S(1)} %convolution_convert_fusion.refs_1_), channel_id=1, source_target_pairs={{0,32},{16,48},{32,64},{48,80},{64,96},{80,112},{96,0},{112,16},{1... | collective-permute-start | bytes 1572872 | tf_op jit(solution)/shard_map/ppermute | solution.py:283
  77.2 14.5 %collective-permute-start.5 = (s32[8,4]{0,1:T(4,128)S(1)}, s32[8,4]{0,1:T(4,128)S(1)}, u32[]{:S(2)}, u32[]{:S(2)}) collective-permute-start(s32[8,4]{0,1:T(4,128)S(1)} %bitcast.47), channel_id=1, source_target_pairs={{0,32},{16,48},{32,64},{48,80},{64,96},{80,112},{96,0},{112,16},{1... | collective-permute-start | bytes 392 | tf_op jit(solution)/shard_map/ppermute | solution.py:283
  91.8 3.9 %collective-permute-start.6 = (s32[8,4]{0,1:T(4,128)S(1)}, s32[8,4]{0,1:T(4,128)S(1)}, u32[]{:S(2)}, u32[]{:S(2)}) collective-permute-start(s32[8,4]{0,1:T(4,128)S(1)} %bitcast.48), channel_id=1, source_target_pairs={{0,64},{16,80},{32,96},{48,112},{64,0},{80,16},{96,32},{112,48},{1... | collective-permute-start | bytes 392 | tf_op jit(solution)/shard_map/ppermute | solution.py:283
  95.7 2.4 %collective-permute-start.7 = (s32[8,4]{0,1:T(4,128)S(1)}, s32[8,4]{0,1:T(4,128)S(1)}, u32[]{:S(2)}, u32[]{:S(2)}) collective-permute-start(s32[8,4]{0,1:T(4,128)S(1)} %bitcast.49), channel_id=1, source_target_pairs={{0,96},{16,112},{32,0},{48,16},{64,32},{80,48},{96,64},{112,80},{1... | collective-permute-start | bytes 392 | tf_op jit(solution)/shard_map/ppermute | solution.py:283
  98.7 4.6 %collective-permute-start.8 = (s32[4,8,4]{1,2,0:T(4,128)}, s32[4,8,4]{1,2,0:T(4,128)}, u32[]{:S(2)}, u32[]{:S(2)}) collective-permute-start(s32[4,8,4]{1,2,0:T(4,128)} %get-tuple-element.62), channel_id=1, source_target_pairs={{0,16},{16,0},{32,48},{48,32},{64,80},{80,64},{96,112},{112,96},{1... | collective-permute-start | bytes 1544 | tf_op jit(solution)/shard_map/ppermute | solution.py:283
  103.4 12.7 %collective-permute-start.15 = (bf16[512,512]{1,0:T(8,128)(2,1)S(1)}, bf16[512,512]{1,0:T(8,128)(2,1)}, u32[]{:S(2)}, u32[]{:S(2)}) collective-permute-start(bf16[512,512]{1,0:T(8,128)(2,1)S(1)} %collective-permute-done.1.refs_0_), channel_id=1, source_target_pairs={{0,16},{16,0},{32,48},{48,32},{64,80},{80,64},{96,112},{112,96},{1... | collective-permute-start | bytes 1572872 | tf_op jit(solution)/shard_map/ppermute | solution.py:283
  109.2 9.6 %collective-permute-start.17 = (bf16[512,512]{1,0:T(8,128)(2,1)S(1)}, bf16[512,512]{1,0:T(8,128)(2,1)S(1)}, u32[]{:S(2)}, u32[]{:S(2)}) collective-permute-start(bf16[512,512]{1,0:T(8,128)(2,1)S(1)} %collective-permute-done.3.refs_4_), channel_id=1, source_target_pairs={{0,16},{16,0},{32,48},{48,32},{64,80},{80,64},{96,112},{112,96},{1... | collective-permute-start | bytes 1572872 | tf_op jit(solution)/shard_map/ppermute | solution.py:283
  109.4 0.8 copy-start.2
  110.2 8.6 %copy-start.5 = (bf16[256,512]{1,0:T(8,128)(2,1)S(1)}, bf16[256,512]{1,0:T(8,128)(2,1)}, u32[]{:S(2)}) copy-start(bf16[256,512]{1,0:T(8,128)(2,1)} %copy-done.4) | copy-start | bytes 786436
  113.5 6.2 %collective-permute-start.16 = (bf16[512,512]{1,0:T(8,128)(2,1)}, bf16[512,512]{1,0:T(8,128)(2,1)S(1)}, u32[]{:S(2)}, u32[]{:S(2)}) collective-permute-start(bf16[512,512]{1,0:T(8,128)(2,1)} %collective-permute-done.9.refs_1_), channel_id=1, source_target_pairs={{0,16},{16,0},{32,48},{48,32},{64,80},{80,64},{96,112},{112,96},{1... | collective-permute-start | bytes 1572872 | tf_op jit(solution)/shard_map/ppermute | solution.py:283
  113.9 5.9 %collective-permute-start.18 = (bf16[512,512]{1,0:T(8,128)(2,1)}, bf16[512,512]{1,0:T(8,128)(2,1)S(1)}, u32[]{:S(2)}, u32[]{:S(2)}) collective-permute-start(bf16[512,512]{1,0:T(8,128)(2,1)} %collective-permute-done.10.refs_5_), channel_id=1, source_target_pairs={{0,16},{16,0},{32,48},{48,32},{64,80},{80,64},{96,112},{112,96},{1... | collective-permute-start | bytes 1572872 | tf_op jit(solution)/shard_map/ppermute | solution.py:283
  116.0 9.7 %collective-permute-start.13 = (bf16[256,512]{1,0:T(8,128)(2,1)S(1)}, bf16[256,512]{1,0:T(8,128)(2,1)S(1)}, u32[]{:S(2)}, u32[]{:S(2)}) collective-permute-start(bf16[256,512]{1,0:T(8,128)(2,1)S(1)} %slice.22), channel_id=1, source_target_pairs={{0,32},{16,48},{32,64},{48,80},{64,96},{80,112},{96,0},{112,16},{1... | collective-permute-start | bytes 786440 | tf_op jit(solution)/shard_map/ppermute | solution.py:283
  116.1 9.7 %collective-permute-start.14 = (bf16[256,512]{1,0:T(8,128)(2,1)S(1)}, bf16[256,512]{1,0:T(8,128)(2,1)S(1)}, u32[]{:S(2)}, u32[]{:S(2)}) collective-permute-start(bf16[256,512]{1,0:T(8,128)(2,1)S(1)} %slice.23), channel_id=1, source_target_pairs={{0,96},{16,112},{32,0},{48,16},{64,32},{80,48},{96,64},{112,80},{1... | collective-permute-start | bytes 786440 | tf_op jit(solution)/shard_map/ppermute | solution.py:283
  118.8 7.7 %collective-permute-start.19 = (bf16[256,512]{1,0:T(8,128)(2,1)S(1)}, bf16[256,512]{1,0:T(8,128)(2,1)S(1)}, u32[]{:S(2)}, u32[]{:S(2)}) collective-permute-start(bf16[256,512]{1,0:T(8,128)(2,1)S(1)} %copy-done.5), channel_id=1, source_target_pairs={{0,16},{16,0},{32,48},{48,32},{64,80},{80,64},{96,112},{112,96},{1... | collective-permute-start | bytes 786440 | tf_op jit(solution)/shard_map/ppermute | solution.py:283
  119.7 6.8 %collective-permute-start.20 = (bf16[256,512]{1,0:T(8,128)(2,1)}, bf16[256,512]{1,0:T(8,128)(2,1)S(1)}, u32[]{:S(2)}, u32[]{:S(2)}) collective-permute-start(bf16[256,512]{1,0:T(8,128)(2,1)} %collective-permute-done.4.refs_1_), channel_id=1, source_target_pairs={{0,16},{16,0},{32,48},{48,32},{64,80},{80,64},{96,112},{112,96},{1... | collective-permute-start | bytes 786440 | tf_op jit(solution)/shard_map/ppermute | solution.py:283
  125.7 2.1 %copy-start.3 = (bf16[32,512]{1,0:T(8,128)(2,1)S(1)}, bf16[32,512]{1,0:T(8,128)(2,1)}, u32[]{:S(2)}) copy-start(bf16[32,512]{1,0:T(8,128)(2,1)} %maximum_maximum_fusion.refs_5_.refs_9_) | copy-start | bytes 98308
  125.8 1.7 collective-permute-start.21
  126.3 1.5 collective-permute-start.22
  126.4 5.0 %copy-start.6 = (s32[8,12]{1,0:T(8,128)S(1)}, s32[8,12]{1,0:T(8,128)}, u32[]{:S(2)}) copy-start(s32[8,12]{1,0:T(8,128)} %rel_ref.1) | copy-start | bytes 1156
  127.8 3.6 %copy-start = (bf16[8,12,128,128]{3,2,1,0:T(8,128)(2,1)S(1)}, bf16[8,12,128,128]{3,2,1,0:T(8,128)(2,1)}, u32[]{:S(2)}) copy-start(bf16[8,12,128,128]{3,2,1,0:T(8,128)(2,1)} %caps.1.cap_ref) | copy-start | bytes 9437188

commit v7 on v6

--- a/solution.py
+++ b/solution.py
@@ -282,15 +282,11 @@
         pairs = [(p, (p + 2 * up) % n_graph ^ cores) for p in range(n_graph)]
         return lax.ppermute(x, "graph", pairs)
 
-    cut = local_blocks // 2
-    rows_a, half = cut * block_rows, width // 2
+    half = width // 2
     features = node_features.T
-    got = lax.all_to_all(
-        arrange(features, proj_weight, core, n_feat, 0, rows_a, half), "feat", 0, 0, tiled=True
-    ).reshape(n_feat * depth, rows_a + half)
-    outgoing = arrange(features, proj_weight, core, n_feat, rows_a, rows_local, 0)
-    got, outgoing, send_blocks, cap = lax.optimization_barrier((got, outgoing, send_blocks, caps(edge_mask)))
-    later = lax.all_to_all(outgoing, "feat", 0, 0, tiled=True).reshape(n_feat * depth, rows_local - rows_a)
+    outgoing = arrange(features, proj_weight, core, n_feat, 0, rows_local, half)
+    outgoing, send_blocks = lax.optimization_barrier((outgoing, send_blocks))
+    got = lax.all_to_all(outgoing, "feat", 0, 0, tiled=True).reshape(n_feat * depth, rows_local + half)
 
     tables = jnp.stack([send_blocks[0]] + [send(send_blocks[0], d) for d in range(1, levels)])
     tables = jnp.stack([tables, send(tables, 0, 1)], axis=1)
@@ -301,13 +297,17 @@
     slots = (2 * (distance ^ (distance >> 1)) + (peer % 2 ^ core)) * CAP + source_slots % CAP
     src_vectors, tgt_vectors = score_vectors(relation_weight, att_source, att_target)
 
-    later, src_vectors, tgt_vectors, slots = lax.optimization_barrier((later, src_vectors, tgt_vectors, slots))
-    mine = got[:, rows_a:]
+    cap = caps(edge_mask)
+    got, cap, src_vectors, tgt_vectors, slots, index = lax.optimization_barrier(
+        (got, cap, src_vectors, tgt_vectors, slots, index)
+    )
+
+    mine = got[:, rows_local:]
     other = send(mine, 0, 1)
     whole = jnp.where(core == 0, jnp.concatenate([mine, other], axis=1), jnp.concatenate([other, mine], axis=1))
-
-    def project(x):
-        return lax.dot_general(x, whole, (((0,), (0,)), ((), ())), preferred_element_type=F32).astype(BF16)
+    hidden = lax.dot_general(
+        got[:, :rows_local], whole, (((0,), (0,)), ((), ())), preferred_element_type=F32
+    ).astype(BF16)
 
     def both(pieces):
         return [pieces, [(send(x, 0, 1), low, high) for x, low, high in pieces]]
@@ -315,30 +315,16 @@
     def spread(group, first, kept):
         return transform(group, first, index, relation_weight, src_vectors, block_rows, *kept)
 
-    def ring(part):
-        return send(part, 1), send(part, -1)
-
-    def forward(up, down):
-        middle = up.shape[0] // 2
-        return send(up[:middle], 1), send(down[middle:], -1)
-
-    a = project(got[:, :rows_a])
-    up_a, down_a = ring(a)
-    far_a = forward(up_a, down_a)
-    later, far_a = lax.optimization_barrier((later, far_a))
-    b = project(later)
-    up_b, down_b = ring(b)
-    done = spread(both([(a, 0, cut), (b, cut, local_blocks)]), 0, (None, None))
-    up_b, down_b, done = lax.optimization_barrier((up_b, down_b, done))
-    far_b = forward(up_b, down_b)
-    done = spread(
-        both([(up_a, 0, cut), (up_b, cut, local_blocks)]) + both([(down_a, 0, cut), (down_b, cut, local_blocks)]), 2, done
-    )
-    far_b, done = lax.optimization_barrier((far_b, done))
-    quarter = cut // 2
-    far = [(x, n * quarter, (n + 1) * quarter) for n, x in enumerate(far_a + far_b)]
-    values, scores = spread(both(far), 6, done)
-    return attend(jnp.concatenate([a, b]), cap, relation_ids, slots, values, scores, tgt_vectors)
+    middle = local_blocks // 2
+    split = middle * block_rows
+    up, down = send(hidden, 1), send(hidden, -1)
+    done = spread(both([(hidden, 0, local_blocks)]), 0, (None, None))
+    up, down, done = lax.optimization_barrier((up, down, done))
+    far_up, far_down = send(up[:split], 1), send(down[split:], -1)
+    done = spread(both([(up, 0, local_blocks)]) + both([(down, 0, local_blocks)]), 2, done)
+    far_up, far_down, done = lax.optimization_barrier((far_up, far_down, done))
+    values, scores = spread(both([(far_up, 0, middle), (far_down, middle, local_blocks)]), 6, done)
+    return attend(hidden, cap, relation_ids, slots, values, scores, tgt_vectors)
 
 
 def solution(mesh):

time: 185 us -> 162 us (0.88)
  starting transfers between devices: 35.6 us -> 26.9 us
  local copies, waits for them, and re-layouts: 8.69 us -> 2.21 us
  other arithmetic: 3.68 us -> 0.45 us
  matrix products: 5.8 us -> 3.8 us
    all_to_all x1, waiting for transfers between devices: 0.01 us -> 21 us  [shards(): lax.all_to_all(outgoing, 'feat', 0, 0, tiled=True)]
    all_to_all x1 -> x0, waiting for transfers between devices: 11.3 us -> none  [shards(): lax.all_to_all(arrange(features, proj_weight, core, n_feat, 0, rows_a, ha...]
    ppermute x23 -> x14, waiting for transfers between devices: 38.9 us -> 28.6 us  [send(): return lax.ppermute(x, 'graph', pairs)]
    all_to_all x1 -> x0, starting transfers between devices: 7.58 us -> none  [shards(): lax.all_to_all(arrange(features, proj_weight, core, n_feat, 0, rows_a, ha...]
    ppermute x23 -> x14, starting transfers between devices: 23.7 us -> 19.1 us  [send(): return lax.ppermute(x, 'graph', pairs)]
    all_to_all x1, starting transfers between devices: 4.35 us -> 7.77 us  [shards(): lax.all_to_all(outgoing, 'feat', 0, 0, tiled=True)]
    pallas_call x2 -> x1, Pallas kernels: 7.25 us -> 3.97 us  [arrange(): pl.pallas_call(functools.partial(arrange_kernel, low, high), grid_spec=pl...]
    slice x5 -> x3, local copies, waits for them, and re-layouts: 3.54 us -> 1.15 us  [the longest x1 1.08 us: shards(): mine = got[:, rows_local:]]
  transfers between devices with their start and end apart: 25 -> 15, of which waited for: 9 -> 8; matrix products, arithmetic and copies ran while one was open for 9% -> 2% of each run, Pallas kernels for 11% -> 11%
where the time goes in v7:
time: 162 us; the launch traced here: 161 us
  Pallas kernels  78 us (48%)
  waiting for transfers between devices  49.7 us (31%)
  starting transfers between devices  26.9 us (17%)
  matrix products  3.8 us (2%)
  local copies, waits for them, and re-layouts  2.21 us (1%)
    pallas_call x1, Pallas kernels, attend(): pl.pallas_call(attend_kernel, in_specs=[scalars] * 2 + [inside] * 5, out_...  52.8 us
    ppermute x14, waiting for transfers between devices, send(): return lax.ppermute(x, 'graph', pairs)  28.6 us
    all_to_all x1, waiting for transfers between devices, shards(): lax.all_to_all(outgoing, 'feat', 0, 0, tiled=True)  21 us
    ppermute x14, starting transfers between devices, send(): return lax.ppermute(x, 'graph', pairs)  19.1 us
    pallas_call x3, Pallas kernels, transform(): pl.pallas_call(functools.partial(transform_kernel, bounds, first), in_spe...  14.3 us
    all_to_all x1, starting transfers between devices, shards(): lax.all_to_all(outgoing, 'feat', 0, 0, tiled=True)  7.77 us
    pallas_call x1, Pallas kernels, caps(): pl.pallas_call(cap_kernel, grid=shape[:1], in_specs=[spec], out_specs=spe...  6.92 us
    pallas_call x1, Pallas kernels, arrange(): pl.pallas_call(functools.partial(arrange_kernel, low, high), grid_spec=pl...  3.97 us
  transfers between devices with their start and end apart: 15, of which 8 were waited for; matrix products, arithmetic and copies ran while one was open for 2% of the time, Pallas kernels for 11%

profile of v7, /device:TPU:1, one launch (start us, length us, event | category | flops | bytes accessed | tf_op | source)
XLA Modules:
  0.0 161.2 jit_solution(9038179778112609969)
XLA Ops:
  0.0 4.0 %arrange.1 = bf16[16,64,1280]{2,1,0:T(8,128)(2,1)} custom-call(s32[1]{0:T(128)} %bitcast.core_ref, bf16[64,16384]{1,0:T(8,128)(2,1)} %bitcast.39, bf16[64,512]{1,0:T(8,128)(2,1)} %w_ref.1), custom_call_target="tpu_custom_call" | custom-call | tf_op jit(solution)/shard_map/arrange/pallas_call | solution.py:31
  4.0 0.0 copy-start.6
  4.0 0.0 copy-start.3
  4.0 0.0 copy-start.4
  4.0 0.0 copy-start.1
  4.0 0.0 copy-start.7
  4.0 0.0 copy-start.5
  4.0 7.8 %all-to-all-start = ((bf16[16,64,1280]{2,1,0:T(8,128)(2,1)}), bf16[16,64,1280]{2,1,0:T(8,128)(2,1)}, u32[]{:S(2)}, u32[]{:S(2)}) async-start(bf16[16,64,1280]{2,1,0:T(8,128)(2,1)} %arrange.1), calls=%async_computation | async-start | bytes 5242880 | tf_op jit(solution)/shard_map/all_to_all | solution.py:289
  11.8 0.0 copy-done.6
  11.8 1.7 %collective-permute-start = (s32[8,4]{0,1:T(4,128)S(1)}, s32[8,4]{0,1:T(4,128)S(1)}, u32[]{:S(2)}, u32[]{:S(2)}) collective-permute-start(s32[8,4]{0,1:T(4,128)S(1)} %bitcast.43), channel_id=1, source_target_pairs={{0,32},{16,48},{32,64},{48,80},{64,96},{80,112},{96,0},{112,16},{1... | collective-permute-start | bytes 392 | tf_op jit(solution)/shard_map/ppermute | solution.py:283
  13.5 3.3 %collective-permute-start.1 = (s32[8,4]{0,1:T(4,128)S(1)}, s32[8,4]{0,1:T(4,128)S(1)}, u32[]{:S(2)}, u32[]{:S(2)}) collective-permute-start(s32[8,4]{0,1:T(4,128)S(1)} %bitcast.44), channel_id=1, source_target_pairs={{0,64},{16,80},{32,96},{48,112},{64,0},{80,16},{96,32},{112,48},{1... | collective-permute-start | bytes 392 | tf_op jit(solution)/shard_map/ppermute | solution.py:283
  16.8 0.7 collective-permute-start.2
  17.5 0.0 copy-done.3
  17.6 0.1 copy.17
  17.7 0.0 copy-done.4
  17.7 0.0 copy-done.1
  17.7 0.9 fusion.5
  18.7 0.1 pad.22.clone
  18.8 0.0 copy-done.7
  18.8 0.0 copy-done.5
  18.9 0.1 maximum_maximum_fusion.refs_3_.refs_5_
  18.9 0.1 select_multiply_fusion
  19.1 0.1 fusion.16
  19.2 0.0 collective-permute-done
  19.2 0.0 collective-permute-done.1
  19.2 0.5 collective-permute-done.2
  19.7 2.3 %collective-permute-start.3 = (s32[4,8,4]{1,2,0:T(4,128)S(1)}, s32[4,8,4]{1,2,0:T(4,128)S(1)}, u32[]{:S(2)}, u32[]{:S(2)}) collective-permute-start(s32[4,8,4]{1,2,0:T(4,128)S(1)} %get-tuple-element.56), channel_id=1, source_target_pairs={{0,16},{16,0},{32,48},{48,32},{64,80},{80,64},{96,112},{112,96},{1... | collective-permute-start | bytes 1544 | tf_op jit(solution)/shard_map/ppermute | solution.py:283
  22.0 6.9 %caps.1.cap_ref = bf16[8,12,128,128]{3,2,1,0:T(8,128)(2,1)} custom-call(s32[8,12,128,128]{3,2,1,0:T(8,128)} %mask_ref.1), custom_call_target="tpu_custom_call" | custom-call | tf_op jit(solution)/shard_map/caps/pallas_call | solution.py:125
  28.9 0.1 copy.18
  29.0 0.0 collective-permute-done.3
  29.0 0.1 copy.19
  29.1 0.6 gather_fusion
  29.7 21.0 %all-to-all-done = bf16[16,64,1280]{2,1,0:T(8,128)(2,1)} async-done(((bf16[16,64,1280]{2,1,0:T(8,128)(2,1)}), bf16[16,64,1280]{2,1,0:T(8,128)(2,1)}, u32[]{:S(2)}, u32[]{:S(2)}) %all-to-all-start) | async-done | bytes 2621472 | tf_op jit(solution)/shard_map/all_to_all | solution.py:289
  50.8 1.1 slice.13
  51.8 1.9 %collective-permute-start.4 = (bf16[1024,256]{1,0:T(8,128)(2,1)S(1)}, bf16[1024,256]{1,0:T(8,128)(2,1)S(1)}, u32[]{:S(2)}, u32[]{:S(2)}) collective-permute-start(bf16[1024,256]{1,0:T(8,128)(2,1)S(1)} %slice.13), channel_id=1, source_target_pairs={{0,16},{16,0},{32,48},{48,32},{64,80},{80,64},{96,112},{112,96},{1... | collective-permute-start | bytes 1572872 | tf_op jit(solution)/shard_map/ppermute | solution.py:283
  53.7 1.5 collective-permute-done.4
  55.3 2.9 %fusion.2.refs_0_ = bf16[1024,512]{1,0:T(8,128)(2,1)S(1)} fusion(bf16[1024,1280]{1,0:T(8,128)(2,1)} %bitcast.2, bf16[1024,256]{1,0:T(8,128)(2,1)S(1)} %collective-permute-done.4, bf16[1024,256]{1,0:T(8,128)(2,1)S(1)} %slice.13, pred[]{:T(512)S(6)} %eq.25), kind=kOutput, calls=%fused_computation.3 | convolution fusion | flops 1078984704 | bytes 4194305 | tf_op jit(solution)/shard_map/dot_general | solution.py:308
  58.2 0.4 collective-permute-start.7
  58.6 1.6 %collective-permute-start.5 = (bf16[1024,512]{1,0:T(8,128)(2,1)S(1)}, bf16[1024,512]{1,0:T(8,128)(2,1)S(1)}, u32[]{:S(2)}, u32[]{:S(2)}) collective-permute-start(bf16[1024,512]{1,0:T(8,128)(2,1)S(1)} %fusion.2.refs_0_), channel_id=1, source_target_pairs={{0,32},{16,48},{32,64},{48,80},{64,96},{80,112},{96,0},{112,16},{1... | collective-permute-start | bytes 3145736 | tf_op jit(solution)/shard_map/ppermute | solution.py:283
  60.3 2.1 %collective-permute-start.6 = (bf16[1024,512]{1,0:T(8,128)(2,1)S(1)}, bf16[1024,512]{1,0:T(8,128)(2,1)S(1)}, u32[]{:S(2)}, u32[]{:S(2)}) collective-permute-start(bf16[1024,512]{1,0:T(8,128)(2,1)S(1)} %fusion.2.refs_0_), channel_id=1, source_target_pairs={{0,96},{16,112},{32,0},{48,16},{64,32},{80,48},{96,64},{112,80},{1... | collective-permute-start | bytes 3145736 | tf_op jit(solution)/shard_map/ppermute | solution.py:283
  62.4 0.0 collective-permute-done.7.refs_1_
  62.4 3.7 %transform.3 = (bf16[32,2,128,512]{3,2,1,0:T(8,128)(2,1)S(1)}, f32[32,8,128]{2,1,0:T(8,128)S(1)}) custom-call(s32[8,4]{1,0:T(8,128)S(1)} %bitcast.36, bf16[1024,512]{1,0:T(8,128)(2,1)S(1)} %fusion.2.refs_0_, bf16[1024,512]{1,0:T(8,128)(2,1)S(1)} %collective-permute-done.7.refs_1_, bf16[2,512,512]{2,1,0:T(8,128)(2,1)S(1)} %copy-done.1, ...), custom_call_target="tpu_custom_call" | custom-call | tf_op jit(solution)/shard_map/transform/pallas_call | solution.py:100
  66.1 19.7 %collective-permute-done.5.refs_0_ = bf16[1024,512]{1,0:T(8,128)(2,1)S(1)} collective-permute-done((bf16[1024,512]{1,0:T(8,128)(2,1)S(1)}, bf16[1024,512]{1,0:T(8,128)(2,1)S(1)}, u32[]{:S(2)}, u32[]{:S(2)}) %collective-permute-start.5) | collective-permute-done | bytes 1048608 | tf_op jit(solution)/shard_map/ppermute | solution.py:283
  85.8 0.0 collective-permute-done.6.refs_2_
  85.8 0.7 collective-permute-start.10
  86.5 0.0 collective-permute-start.11
  86.6 1.1 collective-permute-start.8
  87.6 1.8 %collective-permute-start.9 = (bf16[512,512]{1,0:T(8,128)(2,1)S(1)}, bf16[512,512]{1,0:T(8,128)(2,1)S(1)}, u32[]{:S(2)}, u32[]{:S(2)}) collective-permute-start(bf16[512,512]{1,0:T(8,128)(2,1)S(1)} %slice.15), channel_id=1, source_target_pairs={{0,96},{16,112},{32,0},{48,16},{64,32},{80,48},{96,64},{112,80},{1... | collective-permute-start | bytes 1572872 | tf_op jit(solution)/shard_map/ppermute | solution.py:283
  89.4 0.0 collective-permute-done.10.refs_1_
  89.4 0.9 collective-permute-done.11.refs_3_
  90.3 6.7 %transform.4 = (bf16[32,2,128,512]{3,2,1,0:T(8,128)(2,1)S(1)}, f32[32,8,128]{2,1,0:T(8,128)S(1)}) custom-call(s32[8,4]{1,0:T(8,128)S(1)} %bitcast.37, bf16[1024,512]{1,0:T(8,128)(2,1)S(1)} %collective-permute-done.5.refs_0_, bf16[1024,512]{1,0:T(8,128)(2,1)S(1)} %collective-permute-done.10.refs_1_, ...), custom_call_target="tpu_custom_call", output_to_operand_aliasing={{0}: (7, {}), {1}: (8, {})} | custom-call | tf_op jit(solution)/shard_map/transform/pallas_call | solution.py:100
  97.0 3.8 %collective-permute-done.8.refs_0_ = bf16[512,512]{1,0:T(8,128)(2,1)S(1)} collective-permute-done((bf16[512,512]{1,0:T(8,128)(2,1)S(1)}, bf16[512,512]{1,0:T(8,128)(2,1)S(1)}, u32[]{:S(2)}, u32[]{:S(2)}) %collective-permute-start.8) | collective-permute-done | bytes 524320 | tf_op jit(solution)/shard_map/ppermute | solution.py:283
  100.8 0.0 collective-permute-done.9.refs_1_
  100.8 0.0 copy-start.2
  100.8 1.4 collective-permute-start.12
  102.2 0.1 collective-permute-start.13
  102.3 1.5 collective-permute-done.12.refs_2_
  103.7 0.7 collective-permute-done.13.refs_3_
  104.5 0.0 copy-start
  104.5 3.9 %transform.5 = (bf16[32,2,128,512]{3,2,1,0:T(8,128)(2,1)S(1)}, f32[32,8,128]{2,1,0:T(8,128)S(1)}) custom-call(s32[8,4]{1,0:T(8,128)S(1)} %bitcast.38, bf16[512,512]{1,0:T(8,128)(2,1)S(1)} %collective-permute-done.8.refs_0_, bf16[512,512]{1,0:T(8,128)(2,1)S(1)} %collective-permute-done.9.refs_1_, ...), custom_call_target="tpu_custom_call", output_to_operand_aliasing={{0}: (7, {}), {1}: (8, {})} | custom-call | tf_op jit(solution)/shard_map/transform/pallas_call | solution.py:100
  108.4 0.0 copy-done.2
  108.4 0.0 copy-done
  108.4 52.8 %attend.1 = bf16[8,128,512]{2,1,0:T(8,128)(2,1)} custom-call(s32[8,12]{1,0:T(8,128)S(1)} %copy-done.2, s32[8,12]{1,0:T(8,128)S(1)} %fusion.25.slot_ref, bf16[8,128,512]{2,1,0:T(8,128)(2,1)S(1)} %bitcast.35, bf16[8,12,128,128]{3,2,1,0:T(8,128)(2,1)S(1)} %copy-done, bf16[3,512,128]{2,1,0:T(8,128)(2,1)S(1)} %pad_maximum_fusion.tgt_ref, ...), custom_call_target="tpu_custom_call" | custom-call | tf_op jit(solution)/shard_map/attend/pallas_call | solution.py:224
  (16 shorter events, 0.3 us)
Async XLA Ops:
  4.0 7.8 %copy-start.6 = (s32[1,8,4]{1,2,0:T(4,128)S(1)}, s32[1,8,4]{1,2,0:T(4,128)}, u32[]{:S(2)}) copy-start(s32[1,8,4]{1,2,0:T(4,128)} %param.17) | copy-start | bytes 388
  4.0 13.6 %copy-start.3 = (f32[2,512]{1,0:T(2,128)S(1)}, f32[2,512]{1,0:T(2,128)}, u32[]{:S(2)}) copy-start(f32[2,512]{1,0:T(2,128)} %param.14) | copy-start | bytes 12292
  4.0 13.7 %copy-start.4 = (f32[2,512]{1,0:T(2,128)S(1)}, f32[2,512]{1,0:T(2,128)}, u32[]{:S(2)}) copy-start(f32[2,512]{1,0:T(2,128)} %param.13) | copy-start | bytes 12292
  4.0 13.7 %copy-start.1 = (bf16[2,512,512]{2,1,0:T(8,128)(2,1)S(1)}, bf16[2,512,512]{2,1,0:T(8,128)(2,1)}, u32[]{:S(2)}) copy-start(bf16[2,512,512]{2,1,0:T(8,128)(2,1)} %refs_4_.3) | copy-start | bytes 3145732
  4.0 14.8 %copy-start.7 = (s32[4,1]{0,1:T(1,128)S(1)}, s32[4,1]{0,1:T(1,128)}, u32[]{:S(2)}) copy-start(s32[4,1]{0,1:T(1,128)} %constant.134) | copy-start | bytes 52
  4.0 14.8 %copy-start.5 = (s32[8,12]{1,0:T(8,128)S(1)}, s32[8,12]{1,0:T(8,128)}, u32[]{:S(2)}) copy-start(s32[8,12]{1,0:T(8,128)} %param.18) | copy-start | bytes 1156
  4.0 46.7 %all-to-all-start = ((bf16[16,64,1280]{2,1,0:T(8,128)(2,1)}), bf16[16,64,1280]{2,1,0:T(8,128)(2,1)}, u32[]{:S(2)}, u32[]{:S(2)}) async-start(bf16[16,64,1280]{2,1,0:T(8,128)(2,1)} %arrange.1), calls=%async_computation | async-start | bytes 5242880 | tf_op jit(solution)/shard_map/all_to_all | solution.py:289
  11.8 7.4 %collective-permute-start = (s32[8,4]{0,1:T(4,128)S(1)}, s32[8,4]{0,1:T(4,128)S(1)}, u32[]{:S(2)}, u32[]{:S(2)}) collective-permute-start(s32[8,4]{0,1:T(4,128)S(1)} %bitcast.43), channel_id=1, source_target_pairs={{0,32},{16,48},{32,64},{48,80},{64,96},{80,112},{96,0},{112,16},{1... | collective-permute-start | bytes 392 | tf_op jit(solution)/shard_map/ppermute | solution.py:283
  13.5 5.7 %collective-permute-start.1 = (s32[8,4]{0,1:T(4,128)S(1)}, s32[8,4]{0,1:T(4,128)S(1)}, u32[]{:S(2)}, u32[]{:S(2)}) collective-permute-start(s32[8,4]{0,1:T(4,128)S(1)} %bitcast.44), channel_id=1, source_target_pairs={{0,64},{16,80},{32,96},{48,112},{64,0},{80,16},{96,32},{112,48},{1... | collective-permute-start | bytes 392 | tf_op jit(solution)/shard_map/ppermute | solution.py:283
  16.8 2.8 %collective-permute-start.2 = (s32[8,4]{0,1:T(4,128)S(1)}, s32[8,4]{0,1:T(4,128)S(1)}, u32[]{:S(2)}, u32[]{:S(2)}) collective-permute-start(s32[8,4]{0,1:T(4,128)S(1)} %bitcast.45), channel_id=1, source_target_pairs={{0,96},{16,112},{32,0},{48,16},{64,32},{80,48},{96,64},{112,80},{1... | collective-permute-start | bytes 392 | tf_op jit(solution)/shard_map/ppermute | solution.py:283
  19.7 9.3 %collective-permute-start.3 = (s32[4,8,4]{1,2,0:T(4,128)S(1)}, s32[4,8,4]{1,2,0:T(4,128)S(1)}, u32[]{:S(2)}, u32[]{:S(2)}) collective-permute-start(s32[4,8,4]{1,2,0:T(4,128)S(1)} %get-tuple-element.56), channel_id=1, source_target_pairs={{0,16},{16,0},{32,48},{48,32},{64,80},{80,64},{96,112},{112,96},{1... | collective-permute-start | bytes 1544 | tf_op jit(solution)/shard_map/ppermute | solution.py:283
  51.8 3.4 %collective-permute-start.4 = (bf16[1024,256]{1,0:T(8,128)(2,1)S(1)}, bf16[1024,256]{1,0:T(8,128)(2,1)S(1)}, u32[]{:S(2)}, u32[]{:S(2)}) collective-permute-start(bf16[1024,256]{1,0:T(8,128)(2,1)S(1)} %slice.13), channel_id=1, source_target_pairs={{0,16},{16,0},{32,48},{48,32},{64,80},{80,64},{96,112},{112,96},{1... | collective-permute-start | bytes 1572872 | tf_op jit(solution)/shard_map/ppermute | solution.py:283
  58.2 4.2 %collective-permute-start.7 = (bf16[1024,512]{1,0:T(8,128)(2,1)S(1)}, bf16[1024,512]{1,0:T(8,128)(2,1)S(1)}, u32[]{:S(2)}, u32[]{:S(2)}) collective-permute-start(bf16[1024,512]{1,0:T(8,128)(2,1)S(1)} %fusion.2.refs_0_), channel_id=1, source_target_pairs={{0,16},{16,0},{32,48},{48,32},{64,80},{80,64},{96,112},{112,96},{1... | collective-permute-start | bytes 3145736 | tf_op jit(solution)/shard_map/ppermute | solution.py:283
  58.6 27.1 %collective-permute-start.5 = (bf16[1024,512]{1,0:T(8,128)(2,1)S(1)}, bf16[1024,512]{1,0:T(8,128)(2,1)S(1)}, u32[]{:S(2)}, u32[]{:S(2)}) collective-permute-start(bf16[1024,512]{1,0:T(8,128)(2,1)S(1)} %fusion.2.refs_0_), channel_id=1, source_target_pairs={{0,32},{16,48},{32,64},{48,80},{64,96},{80,112},{96,0},{112,16},{1... | collective-permute-start | bytes 3145736 | tf_op jit(solution)/shard_map/ppermute | solution.py:283
  60.3 25.5 %collective-permute-start.6 = (bf16[1024,512]{1,0:T(8,128)(2,1)S(1)}, bf16[1024,512]{1,0:T(8,128)(2,1)S(1)}, u32[]{:S(2)}, u32[]{:S(2)}) collective-permute-start(bf16[1024,512]{1,0:T(8,128)(2,1)S(1)} %fusion.2.refs_0_), channel_id=1, source_target_pairs={{0,96},{16,112},{32,0},{48,16},{64,32},{80,48},{96,64},{112,80},{1... | collective-permute-start | bytes 3145736 | tf_op jit(solution)/shard_map/ppermute | solution.py:283
  85.8 3.6 %collective-permute-start.10 = (bf16[1024,512]{1,0:T(8,128)(2,1)S(1)}, bf16[1024,512]{1,0:T(8,128)(2,1)S(1)}, u32[]{:S(2)}, u32[]{:S(2)}) collective-permute-start(bf16[1024,512]{1,0:T(8,128)(2,1)S(1)} %collective-permute-done.5.refs_0_), channel_id=1, source_target_pairs={{0,16},{16,0},{32,48},{48,32},{64,80},{80,64},{96,112},{112,96},{1... | collective-permute-start | bytes 3145736 | tf_op jit(solution)/shard_map/ppermute | solution.py:283
  86.5 3.8 %collective-permute-start.11 = (bf16[1024,512]{1,0:T(8,128)(2,1)S(1)}, bf16[1024,512]{1,0:T(8,128)(2,1)S(1)}, u32[]{:S(2)}, u32[]{:S(2)}) collective-permute-start(bf16[1024,512]{1,0:T(8,128)(2,1)S(1)} %collective-permute-done.6.refs_2_), channel_id=1, source_target_pairs={{0,16},{16,0},{32,48},{48,32},{64,80},{80,64},{96,112},{112,96},{1... | collective-permute-start | bytes 3145736 | tf_op jit(solution)/shard_map/ppermute | solution.py:283
  86.6 14.3 %collective-permute-start.8 = (bf16[512,512]{1,0:T(8,128)(2,1)S(1)}, bf16[512,512]{1,0:T(8,128)(2,1)S(1)}, u32[]{:S(2)}, u32[]{:S(2)}) collective-permute-start(bf16[512,512]{1,0:T(8,128)(2,1)S(1)} %slice.14), channel_id=1, source_target_pairs={{0,32},{16,48},{32,64},{48,80},{64,96},{80,112},{96,0},{112,16},{1... | collective-permute-start | bytes 1572872 | tf_op jit(solution)/shard_map/ppermute | solution.py:283
  87.6 13.2 %collective-permute-start.9 = (bf16[512,512]{1,0:T(8,128)(2,1)S(1)}, bf16[512,512]{1,0:T(8,128)(2,1)S(1)}, u32[]{:S(2)}, u32[]{:S(2)}) collective-permute-start(bf16[512,512]{1,0:T(8,128)(2,1)S(1)} %slice.15), channel_id=1, source_target_pairs={{0,96},{16,112},{32,0},{48,16},{64,32},{80,48},{96,64},{112,80},{1... | collective-permute-start | bytes 1572872 | tf_op jit(solution)/shard_map/ppermute | solution.py:283
  100.8 7.6 %copy-start.2 = (s32[8,12]{1,0:T(8,128)S(1)}, s32[8,12]{1,0:T(8,128)}, u32[]{:S(2)}) copy-start(s32[8,12]{1,0:T(8,128)} %rel_ref.1) | copy-start | bytes 1156
  100.8 2.9 %collective-permute-start.12 = (bf16[512,512]{1,0:T(8,128)(2,1)S(1)}, bf16[512,512]{1,0:T(8,128)(2,1)S(1)}, u32[]{:S(2)}, u32[]{:S(2)}) collective-permute-start(bf16[512,512]{1,0:T(8,128)(2,1)S(1)} %collective-permute-done.8.refs_0_), channel_id=1, source_target_pairs={{0,16},{16,0},{32,48},{48,32},{64,80},{80,64},{96,112},{112,96},{1... | collective-permute-start | bytes 1572872 | tf_op jit(solution)/shard_map/ppermute | solution.py:283
  102.2 2.3 %collective-permute-start.13 = (bf16[512,512]{1,0:T(8,128)(2,1)S(1)}, bf16[512,512]{1,0:T(8,128)(2,1)S(1)}, u32[]{:S(2)}, u32[]{:S(2)}) collective-permute-start(bf16[512,512]{1,0:T(8,128)(2,1)S(1)} %collective-permute-done.9.refs_1_), channel_id=1, source_target_pairs={{0,16},{16,0},{32,48},{48,32},{64,80},{80,64},{96,112},{112,96},{1... | collective-permute-start | bytes 1572872 | tf_op jit(solution)/shard_map/ppermute | solution.py:283
  104.5 3.9 %copy-start = (bf16[8,12,128,128]{3,2,1,0:T(8,128)(2,1)S(1)}, bf16[8,12,128,128]{3,2,1,0:T(8,128)(2,1)}, u32[]{:S(2)}) copy-start(bf16[8,12,128,128]{3,2,1,0:T(8,128)(2,1)} %caps.1.cap_ref) | copy-start | bytes 9437188

commit v8 on v7

--- a/solution.py
+++ b/solution.py
@@ -317,13 +317,17 @@
 
     middle = local_blocks // 2
     split = middle * block_rows
-    up, down = send(hidden, 1), send(hidden, -1)
+    front, back = hidden[:split], hidden[split:]
+    up_front, down_back = send(front, 1), send(back, -1)
+    up_back, down_front = send(back, 1), send(front, -1)
     done = spread(both([(hidden, 0, local_blocks)]), 0, (None, None))
-    up, down, done = lax.optimization_barrier((up, down, done))
-    far_up, far_down = send(up[:split], 1), send(down[split:], -1)
-    done = spread(both([(up, 0, local_blocks)]) + both([(down, 0, local_blocks)]), 2, done)
-    far_up, far_down, done = lax.optimization_barrier((far_up, far_down, done))
-    values, scores = spread(both([(far_up, 0, middle), (far_down, middle, local_blocks)]), 6, done)
+    up_front, down_back, done = lax.optimization_barrier((up_front, down_back, done))
+    far_front, far_back = send(up_front, 1), send(down_back, -1)
+    near = both([(up_front, 0, middle), (up_back, middle, local_blocks)])
+    near += both([(down_front, 0, middle), (down_back, middle, local_blocks)])
+    done = spread(near, 2, done)
+    far_front, far_back, done = lax.optimization_barrier((far_front, far_back, done))
+    values, scores = spread(both([(far_front, 0, middle), (far_back, middle, local_blocks)]), 6, done)
     return attend(hidden, cap, relation_ids, slots, values, scores, tgt_vectors)
 
 

time: 162 us -> 162 us (level)
  waiting for transfers between devices: 49.7 us -> 45.8 us
  starting transfers between devices: 26.9 us -> 30.7 us
    ppermute x14 -> x18, waiting for transfers between devices: 28.6 us -> 24.8 us  [send(): return lax.ppermute(x, 'graph', pairs)]
    ppermute x14 -> x18, starting transfers between devices: 19.1 us -> 22.9 us  [send(): return lax.ppermute(x, 'graph', pairs)]
  transfers between devices with their start and end apart: 15 -> 19, of which waited for: 8 -> 8; matrix products, arithmetic and copies ran while one was open for 2% -> 2% of each run, Pallas kernels for 11% -> 11%
where the time goes in v8:
time: 162 us; the launch traced here: 161 us
  Pallas kernels  78.1 us (48%)
  waiting for transfers between devices  45.8 us (28%)
  starting transfers between devices  30.7 us (19%)
  matrix products  3.8 us (2%)
  local copies, waits for them, and re-layouts  2.2 us (1%)
    pallas_call x1, Pallas kernels, attend(): pl.pallas_call(attend_kernel, in_specs=[scalars] * 2 + [inside] * 5, out_...  52.8 us
    ppermute x18, waiting for transfers between devices, send(): return lax.ppermute(x, 'graph', pairs)  24.8 us
    ppermute x18, starting transfers between devices, send(): return lax.ppermute(x, 'graph', pairs)  22.9 us
    all_to_all x1, waiting for transfers between devices, shards(): lax.all_to_all(outgoing, 'feat', 0, 0, tiled=True)  21 us
    pallas_call x3, Pallas kernels, transform(): pl.pallas_call(functools.partial(transform_kernel, bounds, first), in_spe...  14.4 us
    all_to_all x1, starting transfers between devices, shards(): lax.all_to_all(outgoing, 'feat', 0, 0, tiled=True)  7.77 us
    pallas_call x1, Pallas kernels, caps(): pl.pallas_call(cap_kernel, grid=shape[:1], in_specs=[spec], out_specs=spe...  6.94 us
    pallas_call x1, Pallas kernels, arrange(): pl.pallas_call(functools.partial(arrange_kernel, low, high), grid_spec=pl...  3.97 us
  transfers between devices with their start and end apart: 19, of which 8 were waited for; matrix products, arithmetic and copies ran while one was open for 2% of the time, Pallas kernels for 11%

profile of v8, /device:TPU:1, one launch (start us, length us, event | category | flops | bytes accessed | tf_op | source)
XLA Modules:
  0.0 161.3 jit_solution(12616112340531666177)
XLA Ops:
  0.0 4.0 %arrange.1 = bf16[16,64,1280]{2,1,0:T(8,128)(2,1)} custom-call(s32[1]{0:T(128)} %bitcast.core_ref, bf16[64,16384]{1,0:T(8,128)(2,1)} %bitcast.39, bf16[64,512]{1,0:T(8,128)(2,1)} %w_ref.1), custom_call_target="tpu_custom_call" | custom-call | tf_op jit(solution)/shard_map/arrange/pallas_call | solution.py:31
  4.0 0.0 copy-start.1
  4.0 0.0 copy-start.7
  4.0 0.0 copy-start.5
  4.0 7.8 %all-to-all-start = ((bf16[16,64,1280]{2,1,0:T(8,128)(2,1)}), bf16[16,64,1280]{2,1,0:T(8,128)(2,1)}, u32[]{:S(2)}, u32[]{:S(2)}) async-start(bf16[16,64,1280]{2,1,0:T(8,128)(2,1)} %arrange.1), calls=%async_computation | async-start | bytes 5242880 | tf_op jit(solution)/shard_map/all_to_all | solution.py:289
  11.8 0.0 copy-done.6
  11.8 1.7 %collective-permute-start = (s32[8,4]{0,1:T(4,128)S(1)}, s32[8,4]{0,1:T(4,128)S(1)}, u32[]{:S(2)}, u32[]{:S(2)}) collective-permute-start(s32[8,4]{0,1:T(4,128)S(1)} %bitcast.43), channel_id=1, source_target_pairs={{0,32},{16,48},{32,64},{48,80},{64,96},{80,112},{96,0},{112,16},{1... | collective-permute-start | bytes 392 | tf_op jit(solution)/shard_map/ppermute | solution.py:283
  13.5 3.3 %collective-permute-start.1 = (s32[8,4]{0,1:T(4,128)S(1)}, s32[8,4]{0,1:T(4,128)S(1)}, u32[]{:S(2)}, u32[]{:S(2)}) collective-permute-start(s32[8,4]{0,1:T(4,128)S(1)} %bitcast.44), channel_id=1, source_target_pairs={{0,64},{16,80},{32,96},{48,112},{64,0},{80,16},{96,32},{112,48},{1... | collective-permute-start | bytes 392 | tf_op jit(solution)/shard_map/ppermute | solution.py:283
  16.8 0.7 collective-permute-start.2
  17.5 0.0 copy-done.3
  17.6 0.1 copy.17
  17.7 0.0 copy-done.4
  17.7 0.0 copy-done.1
  17.7 0.9 fusion.5
  18.7 0.1 pad.22.clone
  18.8 0.0 copy-done.7
  18.9 0.1 maximum_maximum_fusion.refs_3_.refs_9_.refs_5_
  18.9 0.1 select_multiply_fusion
  19.1 0.1 fusion.16
  19.2 0.0 collective-permute-done
  19.2 0.0 collective-permute-done.1
  19.2 0.5 collective-permute-done.2
  19.7 2.3 %collective-permute-start.3 = (s32[4,8,4]{1,2,0:T(4,128)S(1)}, s32[4,8,4]{1,2,0:T(4,128)S(1)}, u32[]{:S(2)}, u32[]{:S(2)}) collective-permute-start(s32[4,8,4]{1,2,0:T(4,128)S(1)} %get-tuple-element.58), channel_id=1, source_target_pairs={{0,16},{16,0},{32,48},{48,32},{64,80},{80,64},{96,112},{112,96},{1... | collective-permute-start | bytes 1544 | tf_op jit(solution)/shard_map/ppermute | solution.py:283
  22.0 6.9 %caps.1.cap_ref = bf16[8,12,128,128]{3,2,1,0:T(8,128)(2,1)} custom-call(s32[8,12,128,128]{3,2,1,0:T(8,128)} %mask_ref.1), custom_call_target="tpu_custom_call" | custom-call | tf_op jit(solution)/shard_map/caps/pallas_call | solution.py:125
  28.9 0.1 copy.18
  29.0 0.0 collective-permute-done.3
  29.0 0.1 copy.19
  29.2 0.6 gather_fusion
  29.7 21.0 %all-to-all-done = bf16[16,64,1280]{2,1,0:T(8,128)(2,1)} async-done(((bf16[16,64,1280]{2,1,0:T(8,128)(2,1)}), bf16[16,64,1280]{2,1,0:T(8,128)(2,1)}, u32[]{:S(2)}, u32[]{:S(2)}) %all-to-all-start) | async-done | bytes 2621472 | tf_op jit(solution)/shard_map/all_to_all | solution.py:289
  50.8 1.1 slice.13
  51.8 1.9 %collective-permute-start.4 = (bf16[1024,256]{1,0:T(8,128)(2,1)S(1)}, bf16[1024,256]{1,0:T(8,128)(2,1)S(1)}, u32[]{:S(2)}, u32[]{:S(2)}) collective-permute-start(bf16[1024,256]{1,0:T(8,128)(2,1)S(1)} %slice.13), channel_id=1, source_target_pairs={{0,16},{16,0},{32,48},{48,32},{64,80},{80,64},{96,112},{112,96},{1... | collective-permute-start | bytes 1572872 | tf_op jit(solution)/shard_map/ppermute | solution.py:283
  53.7 1.5 collective-permute-done.4
  55.3 2.9 %fusion.2.refs_0_ = bf16[1024,512]{1,0:T(8,128)(2,1)S(1)} fusion(bf16[1024,1280]{1,0:T(8,128)(2,1)} %bitcast.2, bf16[1024,256]{1,0:T(8,128)(2,1)S(1)} %collective-permute-done.4, bf16[1024,256]{1,0:T(8,128)(2,1)S(1)} %slice.13, pred[]{:T(512)S(6)} %eq.25), kind=kOutput, calls=%fused_computation.3 | convolution fusion | flops 1078984704 | bytes 4194305 | tf_op jit(solution)/shard_map/dot_general | solution.py:308
  58.2 0.4 collective-permute-start.7
  58.6 0.1 fusion.34
  58.7 1.7 %collective-permute-start.10 = (bf16[512,512]{1,0:T(8,128)(2,1)S(1)}, bf16[512,512]{1,0:T(8,128)(2,1)S(1)}, u32[]{:S(2)}, u32[]{:S(2)}) collective-permute-start(bf16[512,512]{1,0:T(8,128)(2,1)S(1)} %get-tuple-element.49), channel_id=1, source_target_pairs={{0,32},{16,48},{32,64},{48,80},{64,96},{80,112},{96,0},{112,16},{1... | collective-permute-start | bytes 1572872 | tf_op jit(solution)/shard_map/ppermute | solution.py:283
  60.4 2.2 %collective-permute-start.13 = (bf16[512,512]{1,0:T(8,128)(2,1)S(1)}, bf16[512,512]{1,0:T(8,128)(2,1)S(1)}, u32[]{:S(2)}, u32[]{:S(2)}) collective-permute-start(bf16[512,512]{1,0:T(8,128)(2,1)S(1)} %get-tuple-element.50), channel_id=1, source_target_pairs={{0,96},{16,112},{32,0},{48,16},{64,32},{80,48},{96,64},{112,80},{1... | collective-permute-start | bytes 1572872 | tf_op jit(solution)/shard_map/ppermute | solution.py:283
  62.6 0.0 collective-permute-start.5
  62.6 2.7 %collective-permute-start.6 = (bf16[512,512]{1,0:T(8,128)(2,1)S(1)}, bf16[512,512]{1,0:T(8,128)(2,1)S(1)}, u32[]{:S(2)}, u32[]{:S(2)}) collective-permute-start(bf16[512,512]{1,0:T(8,128)(2,1)S(1)} %get-tuple-element.49), channel_id=1, source_target_pairs={{0,96},{16,112},{32,0},{48,16},{64,32},{80,48},{96,64},{112,80},{1... | collective-permute-start | bytes 1572872 | tf_op jit(solution)/shard_map/ppermute | solution.py:283
  65.3 9.4 %collective-permute-done.10.refs_1_ = bf16[512,512]{1,0:T(8,128)(2,1)S(1)} collective-permute-done((bf16[512,512]{1,0:T(8,128)(2,1)S(1)}, bf16[512,512]{1,0:T(8,128)(2,1)S(1)}, u32[]{:S(2)}, u32[]{:S(2)}) %collective-permute-start.10) | collective-permute-done | bytes 524320 | tf_op jit(solution)/shard_map/ppermute | solution.py:283
  74.7 1.0 collective-permute-start.12
  75.7 0.0 collective-permute-done.13.refs_4_
  75.7 0.0 collective-permute-start.14
  75.7 0.0 collective-permute-done.7.refs_1_
  75.7 3.7 %transform.3 = (bf16[32,2,128,512]{3,2,1,0:T(8,128)(2,1)S(1)}, f32[32,8,128]{2,1,0:T(8,128)S(1)}) custom-call(s32[8,4]{1,0:T(8,128)S(1)} %bitcast.36, bf16[1024,512]{1,0:T(8,128)(2,1)S(1)} %fusion.2.refs_0_, bf16[1024,512]{1,0:T(8,128)(2,1)S(1)} %collective-permute-done.7.refs_1_, bf16[2,512,512]{2,1,0:T(8,128)(2,1)S(1)} %copy-done.1, ...), custom_call_target="tpu_custom_call" | custom-call | tf_op jit(solution)/shard_map/transform/pallas_call | solution.py:100
  79.4 6.5 %collective-permute-done.5.refs_0_ = bf16[512,512]{1,0:T(8,128)(2,1)S(1)} collective-permute-done((bf16[512,512]{1,0:T(8,128)(2,1)S(1)}, bf16[512,512]{1,0:T(8,128)(2,1)S(1)}, u32[]{:S(2)}, u32[]{:S(2)}) %collective-permute-start.5) | collective-permute-done | bytes 524320 | tf_op jit(solution)/shard_map/ppermute | solution.py:283
  85.9 0.0 collective-permute-done.6.refs_5_
  85.9 0.7 collective-permute-start.11
  86.6 0.0 collective-permute-start.15
  86.6 1.0 collective-permute-start.8
  87.6 0.0 collective-permute-done.12.refs_3_
  87.6 1.8 %collective-permute-start.9 = (bf16[512,512]{1,0:T(8,128)(2,1)S(1)}, bf16[512,512]{1,0:T(8,128)(2,1)S(1)}, u32[]{:S(2)}, u32[]{:S(2)}) collective-permute-start(bf16[512,512]{1,0:T(8,128)(2,1)S(1)} %collective-permute-done.6.refs_5_), channel_id=1, source_target_pairs={{0,96},{16,112},{32,0},{48,16},{64,32},{80,48},{96,64},{112,80},{1... | collective-permute-start | bytes 1572872 | tf_op jit(solution)/shard_map/ppermute | solution.py:283
  89.5 0.0 collective-permute-done.14.refs_6_
  89.5 0.0 collective-permute-done.11.refs_2_
  89.5 0.0 collective-permute-done.15.refs_7_
  89.5 6.8 %transform.4 = (bf16[32,2,128,512]{3,2,1,0:T(8,128)(2,1)S(1)}, f32[32,8,128]{2,1,0:T(8,128)S(1)}) custom-call(s32[8,4]{1,0:T(8,128)S(1)} %bitcast.37, bf16[512,512]{1,0:T(8,128)(2,1)S(1)} %collective-permute-done.5.refs_0_, bf16[512,512]{1,0:T(8,128)(2,1)S(1)} %collective-permute-done.10.refs_1_, ...), custom_call_target="tpu_custom_call", output_to_operand_aliasing={{0}: (11, {}), {1}: (12, {})} | custom-call | tf_op jit(solution)/shard_map/transform/pallas_call | solution.py:100
  96.3 4.7 %collective-permute-done.8.refs_0_ = bf16[512,512]{1,0:T(8,128)(2,1)S(1)} collective-permute-done((bf16[512,512]{1,0:T(8,128)(2,1)S(1)}, bf16[512,512]{1,0:T(8,128)(2,1)S(1)}, u32[]{:S(2)}, u32[]{:S(2)}) %collective-permute-start.8) | collective-permute-done | bytes 524320 | tf_op jit(solution)/shard_map/ppermute | solution.py:283
  101.0 0.0 collective-permute-done.9.refs_1_
  101.0 1.3 collective-permute-start.16
  102.3 0.1 collective-permute-start.17
  102.4 1.5 collective-permute-done.16.refs_2_
  103.8 0.7 collective-permute-done.17.refs_3_
  104.6 3.9 %transform.5 = (bf16[32,2,128,512]{3,2,1,0:T(8,128)(2,1)S(1)}, f32[32,8,128]{2,1,0:T(8,128)S(1)}) custom-call(s32[8,4]{1,0:T(8,128)S(1)} %bitcast.38, bf16[512,512]{1,0:T(8,128)(2,1)S(1)} %collective-permute-done.8.refs_0_, bf16[512,512]{1,0:T(8,128)(2,1)S(1)} %collective-permute-done.9.refs_1_, ...), custom_call_target="tpu_custom_call", output_to_operand_aliasing={{0}: (7, {}), {1}: (8, {})} | custom-call | tf_op jit(solution)/shard_map/transform/pallas_call | solution.py:100
  108.5 52.8 %attend.1 = bf16[8,128,512]{2,1,0:T(8,128)(2,1)} custom-call(s32[8,12]{1,0:T(8,128)S(1)} %copy-done.2, s32[8,12]{1,0:T(8,128)S(1)} %fusion.25.slot_ref, bf16[8,128,512]{2,1,0:T(8,128)(2,1)S(1)} %bitcast.35, bf16[8,12,128,128]{3,2,1,0:T(8,128)(2,1)S(1)} %copy-done, bf16[3,512,128]{2,1,0:T(8,128)(2,1)S(1)} %pad_maximum_fusion.tgt_ref, ...), custom_call_target="tpu_custom_call" | custom-call | tf_op jit(solution)/shard_map/attend/pallas_call | solution.py:224
  (22 shorter events, 0.2 us)
Async XLA Ops:
  4.0 7.8 %copy-start.6 = (s32[1,8,4]{1,2,0:T(4,128)S(1)}, s32[1,8,4]{1,2,0:T(4,128)}, u32[]{:S(2)}) copy-start(s32[1,8,4]{1,2,0:T(4,128)} %param.17) | copy-start | bytes 388
  4.0 13.6 %copy-start.3 = (f32[2,512]{1,0:T(2,128)S(1)}, f32[2,512]{1,0:T(2,128)}, u32[]{:S(2)}) copy-start(f32[2,512]{1,0:T(2,128)} %param.14) | copy-start | bytes 12292
  4.0 13.7 %copy-start.4 = (f32[2,512]{1,0:T(2,128)S(1)}, f32[2,512]{1,0:T(2,128)}, u32[]{:S(2)}) copy-start(f32[2,512]{1,0:T(2,128)} %param.13) | copy-start | bytes 12292
  4.0 13.7 %copy-start.1 = (bf16[2,512,512]{2,1,0:T(8,128)(2,1)S(1)}, bf16[2,512,512]{2,1,0:T(8,128)(2,1)}, u32[]{:S(2)}) copy-start(bf16[2,512,512]{2,1,0:T(8,128)(2,1)} %refs_4_.1) | copy-start | bytes 3145732
  4.0 14.8 %copy-start.7 = (s32[4,1]{0,1:T(1,128)S(1)}, s32[4,1]{0,1:T(1,128)}, u32[]{:S(2)}) copy-start(s32[4,1]{0,1:T(1,128)} %constant.134) | copy-start | bytes 52
  4.0 14.8 %copy-start.5 = (s32[8,12]{1,0:T(8,128)S(1)}, s32[8,12]{1,0:T(8,128)}, u32[]{:S(2)}) copy-start(s32[8,12]{1,0:T(8,128)} %param.18) | copy-start | bytes 1156
  4.0 46.7 %all-to-all-start = ((bf16[16,64,1280]{2,1,0:T(8,128)(2,1)}), bf16[16,64,1280]{2,1,0:T(8,128)(2,1)}, u32[]{:S(2)}, u32[]{:S(2)}) async-start(bf16[16,64,1280]{2,1,0:T(8,128)(2,1)} %arrange.1), calls=%async_computation | async-start | bytes 5242880 | tf_op jit(solution)/shard_map/all_to_all | solution.py:289
  11.8 7.4 %collective-permute-start = (s32[8,4]{0,1:T(4,128)S(1)}, s32[8,4]{0,1:T(4,128)S(1)}, u32[]{:S(2)}, u32[]{:S(2)}) collective-permute-start(s32[8,4]{0,1:T(4,128)S(1)} %bitcast.43), channel_id=1, source_target_pairs={{0,32},{16,48},{32,64},{48,80},{64,96},{80,112},{96,0},{112,16},{1... | collective-permute-start | bytes 392 | tf_op jit(solution)/shard_map/ppermute | solution.py:283
  13.5 5.7 %collective-permute-start.1 = (s32[8,4]{0,1:T(4,128)S(1)}, s32[8,4]{0,1:T(4,128)S(1)}, u32[]{:S(2)}, u32[]{:S(2)}) collective-permute-start(s32[8,4]{0,1:T(4,128)S(1)} %bitcast.44), channel_id=1, source_target_pairs={{0,64},{16,80},{32,96},{48,112},{64,0},{80,16},{96,32},{112,48},{1... | collective-permute-start | bytes 392 | tf_op jit(solution)/shard_map/ppermute | solution.py:283
  16.8 2.8 %collective-permute-start.2 = (s32[8,4]{0,1:T(4,128)S(1)}, s32[8,4]{0,1:T(4,128)S(1)}, u32[]{:S(2)}, u32[]{:S(2)}) collective-permute-start(s32[8,4]{0,1:T(4,128)S(1)} %bitcast.45), channel_id=1, source_target_pairs={{0,96},{16,112},{32,0},{48,16},{64,32},{80,48},{96,64},{112,80},{1... | collective-permute-start | bytes 392 | tf_op jit(solution)/shard_map/ppermute | solution.py:283
  19.7 9.4 %collective-permute-start.3 = (s32[4,8,4]{1,2,0:T(4,128)S(1)}, s32[4,8,4]{1,2,0:T(4,128)S(1)}, u32[]{:S(2)}, u32[]{:S(2)}) collective-permute-start(s32[4,8,4]{1,2,0:T(4,128)S(1)} %get-tuple-element.58), channel_id=1, source_target_pairs={{0,16},{16,0},{32,48},{48,32},{64,80},{80,64},{96,112},{112,96},{1... | collective-permute-start | bytes 1544 | tf_op jit(solution)/shard_map/ppermute | solution.py:283
  51.8 3.4 %collective-permute-start.4 = (bf16[1024,256]{1,0:T(8,128)(2,1)S(1)}, bf16[1024,256]{1,0:T(8,128)(2,1)S(1)}, u32[]{:S(2)}, u32[]{:S(2)}) collective-permute-start(bf16[1024,256]{1,0:T(8,128)(2,1)S(1)} %slice.13), channel_id=1, source_target_pairs={{0,16},{16,0},{32,48},{48,32},{64,80},{80,64},{96,112},{112,96},{1... | collective-permute-start | bytes 1572872 | tf_op jit(solution)/shard_map/ppermute | solution.py:283
  58.2 17.6 %collective-permute-start.7 = (bf16[1024,512]{1,0:T(8,128)(2,1)S(1)}, bf16[1024,512]{1,0:T(8,128)(2,1)S(1)}, u32[]{:S(2)}, u32[]{:S(2)}) collective-permute-start(bf16[1024,512]{1,0:T(8,128)(2,1)S(1)} %fusion.2.refs_0_), channel_id=1, source_target_pairs={{0,16},{16,0},{32,48},{48,32},{64,80},{80,64},{96,112},{112,96},{1... | collective-permute-start | bytes 3145736 | tf_op jit(solution)/shard_map/ppermute | solution.py:283
  58.7 16.0 %collective-permute-start.10 = (bf16[512,512]{1,0:T(8,128)(2,1)S(1)}, bf16[512,512]{1,0:T(8,128)(2,1)S(1)}, u32[]{:S(2)}, u32[]{:S(2)}) collective-permute-start(bf16[512,512]{1,0:T(8,128)(2,1)S(1)} %get-tuple-element.49), channel_id=1, source_target_pairs={{0,32},{16,48},{32,64},{48,80},{64,96},{80,112},{96,0},{112,16},{1... | collective-permute-start | bytes 1572872 | tf_op jit(solution)/shard_map/ppermute | solution.py:283
  60.4 15.3 %collective-permute-start.13 = (bf16[512,512]{1,0:T(8,128)(2,1)S(1)}, bf16[512,512]{1,0:T(8,128)(2,1)S(1)}, u32[]{:S(2)}, u32[]{:S(2)}) collective-permute-start(bf16[512,512]{1,0:T(8,128)(2,1)S(1)} %get-tuple-element.50), channel_id=1, source_target_pairs={{0,96},{16,112},{32,0},{48,16},{64,32},{80,48},{96,64},{112,80},{1... | collective-permute-start | bytes 1572872 | tf_op jit(solution)/shard_map/ppermute | solution.py:283
  62.6 23.3 %collective-permute-start.5 = (bf16[512,512]{1,0:T(8,128)(2,1)S(1)}, bf16[512,512]{1,0:T(8,128)(2,1)S(1)}, u32[]{:S(2)}, u32[]{:S(2)}) collective-permute-start(bf16[512,512]{1,0:T(8,128)(2,1)S(1)} %get-tuple-element.50), channel_id=1, source_target_pairs={{0,32},{16,48},{32,64},{48,80},{64,96},{80,112},{96,0},{112,16},{1... | collective-permute-start | bytes 1572872 | tf_op jit(solution)/shard_map/ppermute | solution.py:283
  62.6 23.3 %collective-permute-start.6 = (bf16[512,512]{1,0:T(8,128)(2,1)S(1)}, bf16[512,512]{1,0:T(8,128)(2,1)S(1)}, u32[]{:S(2)}, u32[]{:S(2)}) collective-permute-start(bf16[512,512]{1,0:T(8,128)(2,1)S(1)} %get-tuple-element.49), channel_id=1, source_target_pairs={{0,96},{16,112},{32,0},{48,16},{64,32},{80,48},{96,64},{112,80},{1... | collective-permute-start | bytes 1572872 | tf_op jit(solution)/shard_map/ppermute | solution.py:283
  74.7 13.0 %collective-permute-start.12 = (bf16[512,512]{1,0:T(8,128)(2,1)S(1)}, bf16[512,512]{1,0:T(8,128)(2,1)S(1)}, u32[]{:S(2)}, u32[]{:S(2)}) collective-permute-start(bf16[512,512]{1,0:T(8,128)(2,1)S(1)} %collective-permute-done.10.refs_1_), channel_id=1, source_target_pairs={{0,16},{16,0},{32,48},{48,32},{64,80},{80,64},{96,112},{112,96},{1... | collective-permute-start | bytes 1572872 | tf_op jit(solution)/shard_map/ppermute | solution.py:283
  75.7 13.7 %collective-permute-start.14 = (bf16[512,512]{1,0:T(8,128)(2,1)S(1)}, bf16[512,512]{1,0:T(8,128)(2,1)S(1)}, u32[]{:S(2)}, u32[]{:S(2)}) collective-permute-start(bf16[512,512]{1,0:T(8,128)(2,1)S(1)} %collective-permute-done.13.refs_4_), channel_id=1, source_target_pairs={{0,16},{16,0},{32,48},{48,32},{64,80},{80,64},{96,112},{112,96},{1... | collective-permute-start | bytes 1572872 | tf_op jit(solution)/shard_map/ppermute | solution.py:283
  85.9 3.6 %collective-permute-start.11 = (bf16[512,512]{1,0:T(8,128)(2,1)S(1)}, bf16[512,512]{1,0:T(8,128)(2,1)S(1)}, u32[]{:S(2)}, u32[]{:S(2)}) collective-permute-start(bf16[512,512]{1,0:T(8,128)(2,1)S(1)} %collective-permute-done.5.refs_0_), channel_id=1, source_target_pairs={{0,16},{16,0},{32,48},{48,32},{64,80},{80,64},{96,112},{112,96},{1... | collective-permute-start | bytes 1572872 | tf_op jit(solution)/shard_map/ppermute | solution.py:283
  86.6 2.8 %collective-permute-start.15 = (bf16[512,512]{1,0:T(8,128)(2,1)S(1)}, bf16[512,512]{1,0:T(8,128)(2,1)S(1)}, u32[]{:S(2)}, u32[]{:S(2)}) collective-permute-start(bf16[512,512]{1,0:T(8,128)(2,1)S(1)} %collective-permute-done.6.refs_5_), channel_id=1, source_target_pairs={{0,16},{16,0},{32,48},{48,32},{64,80},{80,64},{96,112},{112,96},{1... | collective-permute-start | bytes 1572872 | tf_op jit(solution)/shard_map/ppermute | solution.py:283
  86.6 14.4 %collective-permute-start.8 = (bf16[512,512]{1,0:T(8,128)(2,1)S(1)}, bf16[512,512]{1,0:T(8,128)(2,1)S(1)}, u32[]{:S(2)}, u32[]{:S(2)}) collective-permute-start(bf16[512,512]{1,0:T(8,128)(2,1)S(1)} %collective-permute-done.5.refs_0_), channel_id=1, source_target_pairs={{0,32},{16,48},{32,64},{48,80},{64,96},{80,112},{96,0},{112,16},{1... | collective-permute-start | bytes 1572872 | tf_op jit(solution)/shard_map/ppermute | solution.py:283
  87.6 13.4 %collective-permute-start.9 = (bf16[512,512]{1,0:T(8,128)(2,1)S(1)}, bf16[512,512]{1,0:T(8,128)(2,1)S(1)}, u32[]{:S(2)}, u32[]{:S(2)}) collective-permute-start(bf16[512,512]{1,0:T(8,128)(2,1)S(1)} %collective-permute-done.6.refs_5_), channel_id=1, source_target_pairs={{0,96},{16,112},{32,0},{48,16},{64,32},{80,48},{96,64},{112,80},{1... | collective-permute-start | bytes 1572872 | tf_op jit(solution)/shard_map/ppermute | solution.py:283
  101.0 7.5 %copy-start.2 = (s32[8,12]{1,0:T(8,128)S(1)}, s32[8,12]{1,0:T(8,128)}, u32[]{:S(2)}) copy-start(s32[8,12]{1,0:T(8,128)} %rel_ref.1) | copy-start | bytes 1156
  101.0 2.8 %collective-permute-start.16 = (bf16[512,512]{1,0:T(8,128)(2,1)S(1)}, bf16[512,512]{1,0:T(8,128)(2,1)S(1)}, u32[]{:S(2)}, u32[]{:S(2)}) collective-permute-start(bf16[512,512]{1,0:T(8,128)(2,1)S(1)} %collective-permute-done.8.refs_0_), channel_id=1, source_target_pairs={{0,16},{16,0},{32,48},{48,32},{64,80},{80,64},{96,112},{112,96},{1... | collective-permute-start | bytes 1572872 | tf_op jit(solution)/shard_map/ppermute | solution.py:283
  102.3 2.3 %collective-permute-start.17 = (bf16[512,512]{1,0:T(8,128)(2,1)S(1)}, bf16[512,512]{1,0:T(8,128)(2,1)S(1)}, u32[]{:S(2)}, u32[]{:S(2)}) collective-permute-start(bf16[512,512]{1,0:T(8,128)(2,1)S(1)} %collective-permute-done.9.refs_1_), channel_id=1, source_target_pairs={{0,16},{16,0},{32,48},{48,32},{64,80},{80,64},{96,112},{112,96},{1... | collective-permute-start | bytes 1572872 | tf_op jit(solution)/shard_map/ppermute | solution.py:283
  104.6 3.9 %copy-start = (bf16[8,12,128,128]{3,2,1,0:T(8,128)(2,1)S(1)}, bf16[8,12,128,128]{3,2,1,0:T(8,128)(2,1)}, u32[]{:S(2)}) copy-start(bf16[8,12,128,128]{3,2,1,0:T(8,128)(2,1)} %caps.1.cap_ref) | copy-start | bytes 9437188

commit v9 on v6

--- a/solution.py
+++ b/solution.py
@@ -289,8 +289,7 @@
         arrange(features, proj_weight, core, n_feat, 0, rows_a, half), "feat", 0, 0, tiled=True
     ).reshape(n_feat * depth, rows_a + half)
     outgoing = arrange(features, proj_weight, core, n_feat, rows_a, rows_local, 0)
-    got, outgoing, send_blocks, cap = lax.optimization_barrier((got, outgoing, send_blocks, caps(edge_mask)))
-    later = lax.all_to_all(outgoing, "feat", 0, 0, tiled=True).reshape(n_feat * depth, rows_local - rows_a)
+    outgoing, send_blocks = lax.optimization_barrier((outgoing, send_blocks))
 
     tables = jnp.stack([send_blocks[0]] + [send(send_blocks[0], d) for d in range(1, levels)])
     tables = jnp.stack([tables, send(tables, 0, 1)], axis=1)
@@ -301,7 +300,11 @@
     slots = (2 * (distance ^ (distance >> 1)) + (peer % 2 ^ core)) * CAP + source_slots % CAP
     src_vectors, tgt_vectors = score_vectors(relation_weight, att_source, att_target)
 
-    later, src_vectors, tgt_vectors, slots = lax.optimization_barrier((later, src_vectors, tgt_vectors, slots))
+    got, outgoing, cap, src_vectors, tgt_vectors, slots, index = lax.optimization_barrier(
+        (got, outgoing, caps(edge_mask), src_vectors, tgt_vectors, slots, index)
+    )
+    later = lax.all_to_all(outgoing, "feat", 0, 0, tiled=True).reshape(n_feat * depth, rows_local - rows_a)
+
     mine = got[:, rows_a:]
     other = send(mine, 0, 1)
     whole = jnp.where(core == 0, jnp.concatenate([mine, other], axis=1), jnp.concatenate([other, mine], axis=1))
@@ -324,8 +327,8 @@
 
     a = project(got[:, :rows_a])
     up_a, down_a = ring(a)
+    later, up_a, down_a = lax.optimization_barrier((later, up_a, down_a))
     far_a = forward(up_a, down_a)
-    later, far_a = lax.optimization_barrier((later, far_a))
     b = project(later)
     up_b, down_b = ring(b)
     done = spread(both([(a, 0, cut), (b, cut, local_blocks)]), 0, (None, None))

time: 185 us -> 172 us (0.930)
  waiting for transfers between devices: 50.2 us -> 43 us
  local copies, waits for them, and re-layouts: 8.69 us -> 2.03 us
  starting transfers between devices: 35.6 us -> 38.9 us
  other arithmetic: 3.68 us -> 0.52 us
    ppermute x23, waiting for transfers between devices: 38.9 us -> 20.3 us  [send(): return lax.ppermute(x, 'graph', pairs)]
    all_to_all x1, waiting for transfers between devices: 0.01 us -> 13.3 us  [shards(): lax.all_to_all(outgoing, 'feat', 0, 0, tiled=True)]
    ppermute x23, starting transfers between devices: 23.7 us -> 27.6 us  [send(): return lax.ppermute(x, 'graph', pairs)]
    slice x4, local copies, waits for them, and re-layouts: 2.67 us -> 0.07 us  [forward(): return (send(up[:middle], 1), send(down[middle:], -1))]
    all_to_all x1, waiting for transfers between devices: 11.3 us -> 9.4 us  [shards(): lax.all_to_all(arrange(features, proj_weight, core, n_feat, 0, rows_a, ha...]
    another operation x2, other arithmetic: 1.97 us -> 0.05 us  [shards(): tables = jnp.stack([tables, send(tables, 0, 1)], axis=1)]
    another operation x2, local copies, waits for them, and re-layouts: 2.08 us -> 0.2 us  [shards(): tables = jnp.stack([tables, send(tables, 0, 1)], axis=1)]
  transfers between devices with their start and end apart: 25 -> 25, of which waited for: 9 -> 8; matrix products, arithmetic and copies ran while one was open for 9% -> 4% of each run, Pallas kernels for 11% -> 12%
where the time goes in v9:
time: 172 us
  Pallas kernels  81 us (47%)
  waiting for transfers between devices  43 us (25%)
  starting transfers between devices  38.9 us (23%)
  matrix products  6.08 us (4%)
  local copies, waits for them, and re-layouts  2.03 us (1%)
    pallas_call x1, Pallas kernels, attend(): pl.pallas_call(attend_kernel, in_specs=[scalars] * 2 + [inside] * 5, out_...  52.8 us
    ppermute x23, starting transfers between devices, send(): return lax.ppermute(x, 'graph', pairs)  27.6 us
    ppermute x23, waiting for transfers between devices, send(): return lax.ppermute(x, 'graph', pairs)  20.3 us
    pallas_call x3, Pallas kernels, transform(): pl.pallas_call(functools.partial(transform_kernel, bounds, first), in_spe...  14 us
    all_to_all x1, waiting for transfers between devices, shards(): lax.all_to_all(outgoing, 'feat', 0, 0, tiled=True)  13.3 us
    all_to_all x1, waiting for transfers between devices, shards(): lax.all_to_all(arrange(features, proj_weight, core, n_feat, 0, rows_a, ha...  9.4 us
    pallas_call x2, Pallas kernels, arrange(): pl.pallas_call(functools.partial(arrange_kernel, low, high), grid_spec=pl...  7.24 us
    pallas_call x1, Pallas kernels, caps(): pl.pallas_call(cap_kernel, grid=shape[:1], in_specs=[spec], out_specs=spe...  6.91 us
  transfers between devices with their start and end apart: 25, of which 8 were waited for; matrix products, arithmetic and copies ran while one was open for 4% of the time, Pallas kernels for 12%

profile of v9, /device:TPU:1, one launch (start us, length us, event | category | flops | bytes accessed | tf_op | source)
XLA Modules:
  0.0 171.9 jit_solution(13144350089565812099)
XLA Ops:
  0.0 3.6 %arrange.3 = bf16[16,64,512]{2,1,0:T(8,128)(2,1)} custom-call(s32[1]{0:T(128)} %bitcast.core_ref, bf16[64,16384]{1,0:T(8,128)(2,1)} %bitcast.41, bf16[64,512]{1,0:T(8,128)(2,1)} %w_ref.3), custom_call_target="tpu_custom_call" | custom-call | tf_op jit(solution)/shard_map/arrange/pallas_call | solution.py:31
  3.6 2.5 %collective-permute-start = (s32[8,4]{0,1:T(4,128)S(1)}, s32[8,4]{0,1:T(4,128)S(1)}, u32[]{:S(2)}, u32[]{:S(2)}) collective-permute-start(s32[8,4]{0,1:T(4,128)S(1)} %bitcast.48), channel_id=1, source_target_pairs={{0,32},{16,48},{32,64},{48,80},{64,96},{80,112},{96,0},{112,16},{1... | collective-permute-start | bytes 392 | tf_op jit(solution)/shard_map/ppermute | solution.py:283
  6.0 3.3 %collective-permute-start.1 = (s32[8,4]{0,1:T(4,128)S(1)}, s32[8,4]{0,1:T(4,128)S(1)}, u32[]{:S(2)}, u32[]{:S(2)}) collective-permute-start(s32[8,4]{0,1:T(4,128)S(1)} %bitcast.49), channel_id=1, source_target_pairs={{0,64},{16,80},{32,96},{48,112},{64,0},{80,16},{96,32},{112,48},{1... | collective-permute-start | bytes 392 | tf_op jit(solution)/shard_map/ppermute | solution.py:283
  9.4 0.7 collective-permute-start.2
  10.1 3.7 %arrange.2 = bf16[16,64,768]{2,1,0:T(8,128)(2,1)} custom-call(s32[1]{0:T(128)} %bitcast.core_ref, bf16[64,16384]{1,0:T(8,128)(2,1)} %bitcast.42, bf16[64,512]{1,0:T(8,128)(2,1)} %w_ref.3), custom_call_target="tpu_custom_call" | custom-call | tf_op jit(solution)/shard_map/arrange/pallas_call | solution.py:31
  13.8 0.0 copy-start.8
  13.8 0.0 copy-start.6
  13.8 6.9 %all-to-all-start = ((bf16[16,64,768]{2,1,0:T(8,128)(2,1)}), bf16[16,64,768]{2,1,0:T(8,128)(2,1)S(1)}, u32[]{:S(2)}, u32[]{:S(2)}) async-start(bf16[16,64,768]{2,1,0:T(8,128)(2,1)} %arrange.2), calls=%async_computation | async-start | bytes 3145728 | tf_op jit(solution)/shard_map/all_to_all | solution.py:288
  20.7 0.1 copy.17
  20.9 0.9 fusion
  21.9 0.1 pad.24.clone
  22.0 0.1 maximum_maximum_fusion.refs_5_.refs_9_
  22.1 0.1 select_multiply_fusion
  22.3 0.1 fusion.6
  22.3 0.0 collective-permute-done
  22.4 0.0 collective-permute-done.2
  22.4 1.9 %collective-permute-start.3 = (s32[4,8,4]{1,2,0:T(4,128)S(1)}, s32[4,8,4]{1,2,0:T(4,128)S(1)}, u32[]{:S(2)}, u32[]{:S(2)}) collective-permute-start(s32[4,8,4]{1,2,0:T(4,128)S(1)} %get-tuple-element.64), channel_id=1, source_target_pairs={{0,16},{16,0},{32,48},{48,32},{64,80},{80,64},{96,112},{112,96},{1... | collective-permute-start | bytes 1544 | tf_op jit(solution)/shard_map/ppermute | solution.py:283
  24.3 6.9 %caps.1.cap_ref = bf16[8,12,128,128]{3,2,1,0:T(8,128)(2,1)} custom-call(s32[8,12,128,128]{3,2,1,0:T(8,128)} %mask_ref.1), custom_call_target="tpu_custom_call" | custom-call | tf_op jit(solution)/shard_map/caps/pallas_call | solution.py:125
  31.2 0.1 copy.18
  31.3 0.0 collective-permute-done.3
  31.3 0.1 copy.19
  31.5 0.6 gather_fusion
  32.0 9.4 %all-to-all-done = bf16[16,64,768]{2,1,0:T(8,128)(2,1)S(1)} async-done(((bf16[16,64,768]{2,1,0:T(8,128)(2,1)}), bf16[16,64,768]{2,1,0:T(8,128)(2,1)S(1)}, u32[]{:S(2)}, u32[]{:S(2)}) %all-to-all-start) | async-done | bytes 1572896 | tf_op jit(solution)/shard_map/all_to_all | solution.py:288
  41.4 0.9 slice.19
  42.3 3.8 %collective-permute-start.4 = (bf16[1024,256]{1,0:T(8,128)(2,1)}, bf16[1024,256]{1,0:T(8,128)(2,1)}, u32[]{:S(2)}, u32[]{:S(2)}) collective-permute-start(bf16[1024,256]{1,0:T(8,128)(2,1)} %slice.19), channel_id=1, source_target_pairs={{0,16},{16,0},{32,48},{48,32},{64,80},{80,64},{96,112},{112,96},{1... | collective-permute-start | bytes 1572872 | tf_op jit(solution)/shard_map/ppermute | solution.py:283
  46.2 4.3 %all-to-all-start.1 = ((bf16[16,64,512]{2,1,0:T(8,128)(2,1)}), bf16[16,64,512]{2,1,0:T(8,128)(2,1)}, u32[]{:S(2)}, u32[]{:S(2)}) async-start(bf16[16,64,512]{2,1,0:T(8,128)(2,1)} %arrange.3), calls=%async_computation.1 | async-start | bytes 2097152 | tf_op jit(solution)/shard_map/all_to_all | solution.py:306
  50.5 0.0 collective-permute-done.4
  50.5 2.6 %convolution_convert_fusion.1.refs_0_ = bf16[512,512]{1,0:T(8,128)(2,1)S(1)} fusion(bf16[1024,768]{1,0:T(8,128)(2,1)} %bitcast.44, bf16[1024,256]{1,0:T(8,128)(2,1)} %collective-permute-done.4, bf16[1024,256]{1,0:T(8,128)(2,1)} %slice.19, pred[]{:T(512)S(6)} %eq.25), kind=kOutput, calls=%fused_computation.2 | convolution fusion | flops 541851648 | bytes 2621441 | tf_op jit(solution)/shard_map/dot_general | solution.py:313
  53.1 0.8 collective-permute-start.5
  53.9 1.9 %collective-permute-start.6 = (bf16[512,512]{1,0:T(8,128)(2,1)S(1)}, bf16[512,512]{1,0:T(8,128)(2,1)S(1)}, u32[]{:S(2)}, u32[]{:S(2)}) collective-permute-start(bf16[512,512]{1,0:T(8,128)(2,1)S(1)} %convolution_convert_fusion.1.refs_0_), channel_id=1, source_target_pairs={{0,96},{16,112},{32,0},{48,16},{64,32},{80,48},{96,64},{112,80},{1... | collective-permute-start | bytes 1572872 | tf_op jit(solution)/shard_map/ppermute | solution.py:283
  55.9 0.6 collective-permute-start.11
  56.4 13.3 %all-to-all-done.1 = bf16[16,64,512]{2,1,0:T(8,128)(2,1)} async-done(((bf16[16,64,512]{2,1,0:T(8,128)(2,1)}), bf16[16,64,512]{2,1,0:T(8,128)(2,1)}, u32[]{:S(2)}, u32[]{:S(2)}) %all-to-all-start.1) | async-done | bytes 1048608 | tf_op jit(solution)/shard_map/all_to_all | solution.py:306
  69.8 0.0 collective-permute-done.5.refs_0_
  69.8 2.6 %convolution_convert_fusion.refs_1_ = bf16[512,512]{1,0:T(8,128)(2,1)S(1)} fusion(bf16[1024,512]{1,0:T(8,128)(2,1)} %bitcast.17, bf16[1024,256]{1,0:T(8,128)(2,1)} %collective-permute-done.4, bf16[1024,256]{1,0:T(8,128)(2,1)} %slice.19, pred[]{:T(512)S(6)} %eq.25), kind=kOutput, calls=%fused_computation.1 | convolution fusion | flops 541851648 | bytes 2621441 | tf_op jit(solution)/shard_map/dot_general | solution.py:313
  72.4 0.9 collective-permute-start.12
  73.2 0.9 collective-permute-start.10
  74.1 0.6 collective-permute-start.9
  74.7 0.8 collective-permute-start.7
  75.5 0.0 collective-permute-done.11.refs_2_
  75.5 0.9 collective-permute-start.15
  76.5 0.0 collective-permute-done.12.refs_3_
  76.5 0.1 collective-permute-start.17
  76.6 3.2 %transform.3 = (bf16[32,2,128,512]{3,2,1,0:T(8,128)(2,1)S(1)}, f32[32,8,128]{2,1,0:T(8,128)S(1)}) custom-call(s32[8,4]{1,0:T(8,128)S(1)} %bitcast.38, bf16[512,512]{1,0:T(8,128)(2,1)S(1)} %convolution_convert_fusion.1.refs_0_, bf16[512,512]{1,0:T(8,128)(2,1)S(1)} %convolution_convert_fusion.refs_1_, bf16[512,512]{1,0:T(8,128)(2,1)} %collective-permute-done.11.refs_2_, ...), custom_call_target="tpu_custom_call" | custom-call | tf_op jit(solution)/shard_map/transform/pallas_call | solution.py:100
  79.8 6.9 %collective-permute-done.10.refs_5_ = bf16[512,512]{1,0:T(8,128)(2,1)S(1)} collective-permute-done((bf16[512,512]{1,0:T(8,128)(2,1)S(1)}, bf16[512,512]{1,0:T(8,128)(2,1)S(1)}, u32[]{:S(2)}, u32[]{:S(2)}) %collective-permute-start.10) | collective-permute-done | bytes 524320 | tf_op jit(solution)/shard_map/ppermute | solution.py:283
  86.7 1.8 %collective-permute-done.9.refs_1_ = bf16[512,512]{1,0:T(8,128)(2,1)S(1)} collective-permute-done((bf16[512,512]{1,0:T(8,128)(2,1)S(1)}, bf16[512,512]{1,0:T(8,128)(2,1)S(1)}, u32[]{:S(2)}, u32[]{:S(2)}) %collective-permute-start.9) | collective-permute-done | bytes 524320 | tf_op jit(solution)/shard_map/ppermute | solution.py:283
  88.5 2.0 %collective-permute-start.16 = (bf16[512,512]{1,0:T(8,128)(2,1)S(1)}, bf16[512,512]{1,0:T(8,128)(2,1)S(1)}, u32[]{:S(2)}, u32[]{:S(2)}) collective-permute-start(bf16[512,512]{1,0:T(8,128)(2,1)S(1)} %collective-permute-done.9.refs_1_), channel_id=1, source_target_pairs={{0,16},{16,0},{32,48},{48,32},{64,80},{80,64},{96,112},{112,96},{1... | collective-permute-start | bytes 1572872 | tf_op jit(solution)/shard_map/ppermute | solution.py:283
  90.5 0.0 collective-permute-start.18
  90.5 3.7 %collective-permute-done.7.refs_0_ = bf16[256,512]{1,0:T(8,128)(2,1)S(1)} collective-permute-done((bf16[256,512]{1,0:T(8,128)(2,1)S(1)}, bf16[256,512]{1,0:T(8,128)(2,1)S(1)}, u32[]{:S(2)}, u32[]{:S(2)}) %collective-permute-start.7) | collective-permute-done | bytes 262176 | tf_op jit(solution)/shard_map/ppermute | solution.py:283
  94.1 0.0 collective-permute-start.8
  94.2 6.6 %collective-permute-done.8.refs_1_ = bf16[256,512]{1,0:T(8,128)(2,1)S(1)} collective-permute-done((bf16[256,512]{1,0:T(8,128)(2,1)S(1)}, bf16[256,512]{1,0:T(8,128)(2,1)S(1)}, u32[]{:S(2)}, u32[]{:S(2)}) %collective-permute-start.8) | collective-permute-done | bytes 262176 | tf_op jit(solution)/shard_map/ppermute | solution.py:283
  100.7 0.0 collective-permute-done.15.refs_2_
  100.7 2.7 %collective-permute-start.14 = (bf16[256,512]{1,0:T(8,128)(2,1)S(1)}, bf16[256,512]{1,0:T(8,128)(2,1)S(1)}, u32[]{:S(2)}, u32[]{:S(2)}) collective-permute-start(bf16[256,512]{1,0:T(8,128)(2,1)S(1)} %slice.23), channel_id=1, source_target_pairs={{0,96},{16,112},{32,0},{48,16},{64,32},{80,48},{96,64},{112,80},{1... | collective-permute-start | bytes 786440 | tf_op jit(solution)/shard_map/ppermute | solution.py:283
  103.4 0.0 collective-permute-done.17.refs_6_
  103.4 2.7 %collective-permute-start.19 = (bf16[256,512]{1,0:T(8,128)(2,1)S(1)}, bf16[256,512]{1,0:T(8,128)(2,1)S(1)}, u32[]{:S(2)}, u32[]{:S(2)}) collective-permute-start(bf16[256,512]{1,0:T(8,128)(2,1)S(1)} %collective-permute-done.7.refs_0_), channel_id=1, source_target_pairs={{0,16},{16,0},{32,48},{48,32},{64,80},{80,64},{96,112},{112,96},{1... | collective-permute-start | bytes 786440 | tf_op jit(solution)/shard_map/ppermute | solution.py:283
  106.1 0.1 collective-permute-start.20
  106.2 7.0 %transform.4 = (bf16[32,2,128,512]{3,2,1,0:T(8,128)(2,1)S(1)}, f32[32,8,128]{2,1,0:T(8,128)S(1)}) custom-call(s32[8,4]{1,0:T(8,128)S(1)} %bitcast.39, bf16[512,512]{1,0:T(8,128)(2,1)S(1)} %collective-permute-done.5.refs_0_, bf16[512,512]{1,0:T(8,128)(2,1)S(1)} %collective-permute-done.9.refs_1_, ...), custom_call_target="tpu_custom_call", output_to_operand_aliasing={{0}: (11, {}), {1}: (12, {})} | custom-call | tf_op jit(solution)/shard_map/transform/pallas_call | solution.py:100
  113.2 0.5 collective-permute-start.21
  113.7 0.1 collective-permute-start.22
  113.8 0.1 pad_maximum_fusion
  113.9 0.0 copy-start.2
  113.9 1.0 collective-permute-done.21.refs_6_
  114.9 0.4 collective-permute-done.22.refs_7_
  115.2 3.8 %transform.5 = (bf16[32,2,128,512]{3,2,1,0:T(8,128)(2,1)S(1)}, f32[32,8,128]{2,1,0:T(8,128)S(1)}) custom-call(s32[8,4]{1,0:T(8,128)S(1)} %bitcast.40, bf16[256,512]{1,0:T(8,128)(2,1)S(1)} %collective-permute-done.7.refs_0_, bf16[256,512]{1,0:T(8,128)(2,1)S(1)} %collective-permute-done.8.refs_1_, ...), custom_call_target="tpu_custom_call", output_to_operand_aliasing={{0}: (11, {}), {1}: (12, {})} | custom-call | tf_op jit(solution)/shard_map/transform/pallas_call | solution.py:100
  119.1 52.8 %attend.1 = bf16[8,128,512]{2,1,0:T(8,128)(2,1)} custom-call(s32[8,12]{1,0:T(8,128)S(1)} %copy-done.2, s32[8,12]{1,0:T(8,128)S(1)} %fusion.15.slot_ref, bf16[8,128,512]{2,1,0:T(8,128)(2,1)S(1)} %bitcast.37, bf16[8,12,128,128]{3,2,1,0:T(8,128)(2,1)S(1)} %copy-done, bf16[3,512,128]{2,1,0:T(8,128)(2,1)S(1)} %pad_maximum_fusion.1.tgt_ref, ...), custom_call_target="tpu_custom_call" | custom-call | tf_op jit(solution)/shard_map/attend/pallas_call | solution.py:224
  (42 shorter events, 0.3 us)
Async XLA Ops:
  0.0 3.6 %copy-start.7 = (s32[1,8,4]{1,2,0:T(4,128)S(1)}, s32[1,8,4]{1,2,0:T(4,128)}, u32[]{:S(2)}) copy-start(s32[1,8,4]{1,2,0:T(4,128)} %param.17) | copy-start | bytes 388
  3.6 18.8 %collective-permute-start = (s32[8,4]{0,1:T(4,128)S(1)}, s32[8,4]{0,1:T(4,128)S(1)}, u32[]{:S(2)}, u32[]{:S(2)}) collective-permute-start(s32[8,4]{0,1:T(4,128)S(1)} %bitcast.48), channel_id=1, source_target_pairs={{0,32},{16,48},{32,64},{48,80},{64,96},{80,112},{96,0},{112,16},{1... | collective-permute-start | bytes 392 | tf_op jit(solution)/shard_map/ppermute | solution.py:283
  6.0 16.3 %collective-permute-start.1 = (s32[8,4]{0,1:T(4,128)S(1)}, s32[8,4]{0,1:T(4,128)S(1)}, u32[]{:S(2)}, u32[]{:S(2)}) collective-permute-start(s32[8,4]{0,1:T(4,128)S(1)} %bitcast.49), channel_id=1, source_target_pairs={{0,64},{16,80},{32,96},{48,112},{64,0},{80,16},{96,32},{112,48},{1... | collective-permute-start | bytes 392 | tf_op jit(solution)/shard_map/ppermute | solution.py:283
  9.4 13.0 %collective-permute-start.2 = (s32[8,4]{0,1:T(4,128)S(1)}, s32[8,4]{0,1:T(4,128)S(1)}, u32[]{:S(2)}, u32[]{:S(2)}) collective-permute-start(s32[8,4]{0,1:T(4,128)S(1)} %bitcast.50), channel_id=1, source_target_pairs={{0,96},{16,112},{32,0},{48,16},{64,32},{80,48},{96,64},{112,80},{1... | collective-permute-start | bytes 392 | tf_op jit(solution)/shard_map/ppermute | solution.py:283
  13.7 7.0 %copy-start.4 = (f32[2,512]{1,0:T(2,128)S(1)}, f32[2,512]{1,0:T(2,128)}, u32[]{:S(2)}) copy-start(f32[2,512]{1,0:T(2,128)} %param.14) | copy-start | bytes 12292
  13.8 7.1 %copy-start.5 = (f32[2,512]{1,0:T(2,128)S(1)}, f32[2,512]{1,0:T(2,128)}, u32[]{:S(2)}) copy-start(f32[2,512]{1,0:T(2,128)} %param.13) | copy-start | bytes 12292
  13.8 7.2 %copy-start.1 = (bf16[2,512,512]{2,1,0:T(8,128)(2,1)S(1)}, bf16[2,512,512]{2,1,0:T(8,128)(2,1)}, u32[]{:S(2)}) copy-start(bf16[2,512,512]{2,1,0:T(8,128)(2,1)} %refs_8_.3) | copy-start | bytes 3145732
  13.8 8.1 %copy-start.8 = (s32[4,1]{0,1:T(1,128)S(1)}, s32[4,1]{0,1:T(1,128)}, u32[]{:S(2)}) copy-start(s32[4,1]{0,1:T(1,128)} %constant.134) | copy-start | bytes 52
  13.8 8.2 %copy-start.6 = (s32[8,12]{1,0:T(8,128)S(1)}, s32[8,12]{1,0:T(8,128)}, u32[]{:S(2)}) copy-start(s32[8,12]{1,0:T(8,128)} %param.18) | copy-start | bytes 1156
  13.8 27.7 %all-to-all-start = ((bf16[16,64,768]{2,1,0:T(8,128)(2,1)}), bf16[16,64,768]{2,1,0:T(8,128)(2,1)S(1)}, u32[]{:S(2)}, u32[]{:S(2)}) async-start(bf16[16,64,768]{2,1,0:T(8,128)(2,1)} %arrange.2), calls=%async_computation | async-start | bytes 3145728 | tf_op jit(solution)/shard_map/all_to_all | solution.py:288
  22.4 8.9 %collective-permute-start.3 = (s32[4,8,4]{1,2,0:T(4,128)S(1)}, s32[4,8,4]{1,2,0:T(4,128)S(1)}, u32[]{:S(2)}, u32[]{:S(2)}) collective-permute-start(s32[4,8,4]{1,2,0:T(4,128)S(1)} %get-tuple-element.64), channel_id=1, source_target_pairs={{0,16},{16,0},{32,48},{48,32},{64,80},{80,64},{96,112},{112,96},{1... | collective-permute-start | bytes 1544 | tf_op jit(solution)/shard_map/ppermute | solution.py:283
  41.4 9.1 %copy-start.3 = (bf16[16,64,768]{2,1,0:T(8,128)(2,1)}, bf16[16,64,768]{2,1,0:T(8,128)(2,1)S(1)}, u32[]{:S(2)}) copy-start(bf16[16,64,768]{2,1,0:T(8,128)(2,1)S(1)} %all-to-all-done) | copy-start | bytes 4718596
  42.3 8.2 %collective-permute-start.4 = (bf16[1024,256]{1,0:T(8,128)(2,1)}, bf16[1024,256]{1,0:T(8,128)(2,1)}, u32[]{:S(2)}, u32[]{:S(2)}) collective-permute-start(bf16[1024,256]{1,0:T(8,128)(2,1)} %slice.19), channel_id=1, source_target_pairs={{0,16},{16,0},{32,48},{48,32},{64,80},{80,64},{96,112},{112,96},{1... | collective-permute-start | bytes 1572872 | tf_op jit(solution)/shard_map/ppermute | solution.py:283
  46.2 23.6 %all-to-all-start.1 = ((bf16[16,64,512]{2,1,0:T(8,128)(2,1)}), bf16[16,64,512]{2,1,0:T(8,128)(2,1)}, u32[]{:S(2)}, u32[]{:S(2)}) async-start(bf16[16,64,512]{2,1,0:T(8,128)(2,1)} %arrange.3), calls=%async_computation.1 | async-start | bytes 2097152 | tf_op jit(solution)/shard_map/all_to_all | solution.py:306
  53.1 16.6 %collective-permute-start.5 = (bf16[512,512]{1,0:T(8,128)(2,1)S(1)}, bf16[512,512]{1,0:T(8,128)(2,1)S(1)}, u32[]{:S(2)}, u32[]{:S(2)}) collective-permute-start(bf16[512,512]{1,0:T(8,128)(2,1)S(1)} %convolution_convert_fusion.1.refs_0_), channel_id=1, source_target_pairs={{0,32},{16,48},{32,64},{48,80},{64,96},{80,112},{96,0},{112,16},{1... | collective-permute-start | bytes 1572872 | tf_op jit(solution)/shard_map/ppermute | solution.py:283
  53.9 15.8 %collective-permute-start.6 = (bf16[512,512]{1,0:T(8,128)(2,1)S(1)}, bf16[512,512]{1,0:T(8,128)(2,1)S(1)}, u32[]{:S(2)}, u32[]{:S(2)}) collective-permute-start(bf16[512,512]{1,0:T(8,128)(2,1)S(1)} %convolution_convert_fusion.1.refs_0_), channel_id=1, source_target_pairs={{0,96},{16,112},{32,0},{48,16},{64,32},{80,48},{96,64},{112,80},{1... | collective-permute-start | bytes 1572872 | tf_op jit(solution)/shard_map/ppermute | solution.py:283
  55.9 19.7 %collective-permute-start.11 = (bf16[512,512]{1,0:T(8,128)(2,1)S(1)}, bf16[512,512]{1,0:T(8,128)(2,1)}, u32[]{:S(2)}, u32[]{:S(2)}) collective-permute-start(bf16[512,512]{1,0:T(8,128)(2,1)S(1)} %convolution_convert_fusion.1.refs_0_), channel_id=1, source_target_pairs={{0,16},{16,0},{32,48},{48,32},{64,80},{80,64},{96,112},{112,96},{1... | collective-permute-start | bytes 1572872 | tf_op jit(solution)/shard_map/ppermute | solution.py:283
  72.4 4.1 %collective-permute-start.12 = (bf16[512,512]{1,0:T(8,128)(2,1)S(1)}, bf16[512,512]{1,0:T(8,128)(2,1)S(1)}, u32[]{:S(2)}, u32[]{:S(2)}) collective-permute-start(bf16[512,512]{1,0:T(8,128)(2,1)S(1)} %convolution_convert_fusion.refs_1_), channel_id=1, source_target_pairs={{0,16},{16,0},{32,48},{48,32},{64,80},{80,64},{96,112},{112,96},{1... | collective-permute-start | bytes 1572872 | tf_op jit(solution)/shard_map/ppermute | solution.py:283
  73.2 13.5 %collective-permute-start.10 = (bf16[512,512]{1,0:T(8,128)(2,1)S(1)}, bf16[512,512]{1,0:T(8,128)(2,1)S(1)}, u32[]{:S(2)}, u32[]{:S(2)}) collective-permute-start(bf16[512,512]{1,0:T(8,128)(2,1)S(1)} %convolution_convert_fusion.refs_1_), channel_id=1, source_target_pairs={{0,96},{16,112},{32,0},{48,16},{64,32},{80,48},{96,64},{112,80},{1... | collective-permute-start | bytes 1572872 | tf_op jit(solution)/shard_map/ppermute | solution.py:283
  74.1 14.4 %collective-permute-start.9 = (bf16[512,512]{1,0:T(8,128)(2,1)S(1)}, bf16[512,512]{1,0:T(8,128)(2,1)S(1)}, u32[]{:S(2)}, u32[]{:S(2)}) collective-permute-start(bf16[512,512]{1,0:T(8,128)(2,1)S(1)} %convolution_convert_fusion.refs_1_), channel_id=1, source_target_pairs={{0,32},{16,48},{32,64},{48,80},{64,96},{80,112},{96,0},{112,16},{1... | collective-permute-start | bytes 1572872 | tf_op jit(solution)/shard_map/ppermute | solution.py:283
  74.7 19.4 %collective-permute-start.7 = (bf16[256,512]{1,0:T(8,128)(2,1)S(1)}, bf16[256,512]{1,0:T(8,128)(2,1)S(1)}, u32[]{:S(2)}, u32[]{:S(2)}) collective-permute-start(bf16[256,512]{1,0:T(8,128)(2,1)S(1)} %slice.20), channel_id=1, source_target_pairs={{0,32},{16,48},{32,64},{48,80},{64,96},{80,112},{96,0},{112,16},{1... | collective-permute-start | bytes 786440 | tf_op jit(solution)/shard_map/ppermute | solution.py:283
  75.5 25.2 %collective-permute-start.15 = (bf16[512,512]{1,0:T(8,128)(2,1)S(1)}, bf16[512,512]{1,0:T(8,128)(2,1)S(1)}, u32[]{:S(2)}, u32[]{:S(2)}) collective-permute-start(bf16[512,512]{1,0:T(8,128)(2,1)S(1)} %collective-permute-done.5.refs_0_), channel_id=1, source_target_pairs={{0,16},{16,0},{32,48},{48,32},{64,80},{80,64},{96,112},{112,96},{1... | collective-permute-start | bytes 1572872 | tf_op jit(solution)/shard_map/ppermute | solution.py:283
  76.5 26.9 %collective-permute-start.17 = (bf16[512,512]{1,0:T(8,128)(2,1)S(1)}, bf16[512,512]{1,0:T(8,128)(2,1)S(1)}, u32[]{:S(2)}, u32[]{:S(2)}) collective-permute-start(bf16[512,512]{1,0:T(8,128)(2,1)S(1)} %collective-permute-done.6.refs_4_), channel_id=1, source_target_pairs={{0,16},{16,0},{32,48},{48,32},{64,80},{80,64},{96,112},{112,96},{1... | collective-permute-start | bytes 1572872 | tf_op jit(solution)/shard_map/ppermute | solution.py:283
  88.5 17.6 %collective-permute-start.16 = (bf16[512,512]{1,0:T(8,128)(2,1)S(1)}, bf16[512,512]{1,0:T(8,128)(2,1)S(1)}, u32[]{:S(2)}, u32[]{:S(2)}) collective-permute-start(bf16[512,512]{1,0:T(8,128)(2,1)S(1)} %collective-permute-done.9.refs_1_), channel_id=1, source_target_pairs={{0,16},{16,0},{32,48},{48,32},{64,80},{80,64},{96,112},{112,96},{1... | collective-permute-start | bytes 1572872 | tf_op jit(solution)/shard_map/ppermute | solution.py:283
  90.5 15.7 %collective-permute-start.18 = (bf16[512,512]{1,0:T(8,128)(2,1)S(1)}, bf16[512,512]{1,0:T(8,128)(2,1)S(1)}, u32[]{:S(2)}, u32[]{:S(2)}) collective-permute-start(bf16[512,512]{1,0:T(8,128)(2,1)S(1)} %collective-permute-done.10.refs_5_), channel_id=1, source_target_pairs={{0,16},{16,0},{32,48},{48,32},{64,80},{80,64},{96,112},{112,96},{1... | collective-permute-start | bytes 1572872 | tf_op jit(solution)/shard_map/ppermute | solution.py:283
  94.1 6.6 %collective-permute-start.8 = (bf16[256,512]{1,0:T(8,128)(2,1)S(1)}, bf16[256,512]{1,0:T(8,128)(2,1)S(1)}, u32[]{:S(2)}, u32[]{:S(2)}) collective-permute-start(bf16[256,512]{1,0:T(8,128)(2,1)S(1)} %slice.21), channel_id=1, source_target_pairs={{0,96},{16,112},{32,0},{48,16},{64,32},{80,48},{96,64},{112,80},{1... | collective-permute-start | bytes 786440 | tf_op jit(solution)/shard_map/ppermute | solution.py:283
  100.7 12.5 %collective-permute-start.13 = (bf16[256,512]{1,0:T(8,128)(2,1)S(1)}, bf16[256,512]{1,0:T(8,128)(2,1)S(1)}, u32[]{:S(2)}, u32[]{:S(2)}) collective-permute-start(bf16[256,512]{1,0:T(8,128)(2,1)S(1)} %slice.22), channel_id=1, source_target_pairs={{0,32},{16,48},{32,64},{48,80},{64,96},{80,112},{96,0},{112,16},{1... | collective-permute-start | bytes 786440 | tf_op jit(solution)/shard_map/ppermute | solution.py:283
  100.7 12.5 %collective-permute-start.14 = (bf16[256,512]{1,0:T(8,128)(2,1)S(1)}, bf16[256,512]{1,0:T(8,128)(2,1)S(1)}, u32[]{:S(2)}, u32[]{:S(2)}) collective-permute-start(bf16[256,512]{1,0:T(8,128)(2,1)S(1)} %slice.23), channel_id=1, source_target_pairs={{0,96},{16,112},{32,0},{48,16},{64,32},{80,48},{96,64},{112,80},{1... | collective-permute-start | bytes 786440 | tf_op jit(solution)/shard_map/ppermute | solution.py:283
  103.4 10.5 %collective-permute-start.19 = (bf16[256,512]{1,0:T(8,128)(2,1)S(1)}, bf16[256,512]{1,0:T(8,128)(2,1)S(1)}, u32[]{:S(2)}, u32[]{:S(2)}) collective-permute-start(bf16[256,512]{1,0:T(8,128)(2,1)S(1)} %collective-permute-done.7.refs_0_), channel_id=1, source_target_pairs={{0,16},{16,0},{32,48},{48,32},{64,80},{80,64},{96,112},{112,96},{1... | collective-permute-start | bytes 786440 | tf_op jit(solution)/shard_map/ppermute | solution.py:283
  106.1 7.8 %collective-permute-start.20 = (bf16[256,512]{1,0:T(8,128)(2,1)S(1)}, bf16[256,512]{1,0:T(8,128)(2,1)S(1)}, u32[]{:S(2)}, u32[]{:S(2)}) collective-permute-start(bf16[256,512]{1,0:T(8,128)(2,1)S(1)} %collective-permute-done.8.refs_1_), channel_id=1, source_target_pairs={{0,16},{16,0},{32,48},{48,32},{64,80},{80,64},{96,112},{112,96},{1... | collective-permute-start | bytes 786440 | tf_op jit(solution)/shard_map/ppermute | solution.py:283
  113.2 1.7 collective-permute-start.21
  113.7 1.5 collective-permute-start.22
  113.9 5.2 %copy-start.2 = (s32[8,12]{1,0:T(8,128)S(1)}, s32[8,12]{1,0:T(8,128)}, u32[]{:S(2)}) copy-start(s32[8,12]{1,0:T(8,128)} %rel_ref.1) | copy-start | bytes 1156
  115.2 3.8 %copy-start = (bf16[8,12,128,128]{3,2,1,0:T(8,128)(2,1)S(1)}, bf16[8,12,128,128]{3,2,1,0:T(8,128)(2,1)}, u32[]{:S(2)}) copy-start(bf16[8,12,128,128]{3,2,1,0:T(8,128)(2,1)} %caps.1.cap_ref) | copy-start | bytes 9437188

commit v10 on v9

--- a/solution.py
+++ b/solution.py
@@ -285,9 +285,9 @@
     cut = local_blocks // 2
     rows_a, half = cut * block_rows, width // 2
     features = node_features.T
-    got = lax.all_to_all(
-        arrange(features, proj_weight, core, n_feat, 0, rows_a, half), "feat", 0, 0, tiled=True
-    ).reshape(n_feat * depth, rows_a + half)
+    first = arrange(features, proj_weight, core, n_feat, 0, rows_a, half)
+    first, features = lax.optimization_barrier((first, features))
+    got = lax.all_to_all(first, "feat", 0, 0, tiled=True).reshape(n_feat * depth, rows_a + half)
     outgoing = arrange(features, proj_weight, core, n_feat, rows_a, rows_local, 0)
     outgoing, send_blocks = lax.optimization_barrier((outgoing, send_blocks))
 
@@ -332,7 +332,7 @@
     b = project(later)
     up_b, down_b = ring(b)
     done = spread(both([(a, 0, cut), (b, cut, local_blocks)]), 0, (None, None))
-    up_b, down_b, done = lax.optimization_barrier((up_b, down_b, done))
+    up_b, down_b, far_a, done = lax.optimization_barrier((up_b, down_b, far_a, done))
     far_b = forward(up_b, down_b)
     done = spread(
         both([(up_a, 0, cut), (up_b, cut, local_blocks)]) + both([(down_a, 0, cut), (down_b, cut, local_blocks)]), 2, done

time: 172 us -> 165 us (0.959)
  waiting for transfers between devices: 43 us -> 34.8 us
    ppermute x23, waiting for transfers between devices: 20.3 us -> 11.8 us  [send(): return lax.ppermute(x, 'graph', pairs)]
  transfers between devices with their start and end apart: 25 -> 25, of which waited for: 8 -> 5; matrix products, arithmetic and copies ran while one was open for 4% -> 4% of each run, Pallas kernels for 12% -> 11%
where the time goes in v10:
time: 165 us; the launch traced here: 164 us
  Pallas kernels  81.3 us (49%)
  starting transfers between devices  39.4 us (24%)
  waiting for transfers between devices  34.8 us (21%)
  matrix products  5.64 us (3%)
  local copies, waits for them, and re-layouts  2.21 us (1%)
    pallas_call x1, Pallas kernels, attend(): pl.pallas_call(attend_kernel, in_specs=[scalars] * 2 + [inside] * 5, out_...  52.8 us
    ppermute x23, starting transfers between devices, send(): return lax.ppermute(x, 'graph', pairs)  28.2 us
    pallas_call x3, Pallas kernels, transform(): pl.pallas_call(functools.partial(transform_kernel, bounds, first), in_spe...  14.3 us
    all_to_all x1, waiting for transfers between devices, shards(): lax.all_to_all(outgoing, 'feat', 0, 0, tiled=True)  13.6 us
    ppermute x23, waiting for transfers between devices, send(): return lax.ppermute(x, 'graph', pairs)  11.8 us
    all_to_all x1, waiting for transfers between devices, shards(): lax.all_to_all(first, 'feat', 0, 0, tiled=True)  9.44 us
    pallas_call x2, Pallas kernels, arrange(): pl.pallas_call(functools.partial(arrange_kernel, low, high), grid_spec=pl...  7.3 us
    pallas_call x1, Pallas kernels, caps(): pl.pallas_call(cap_kernel, grid=shape[:1], in_specs=[spec], out_specs=spe...  6.93 us
  transfers between devices with their start and end apart: 25, of which 5 were waited for; matrix products, arithmetic and copies ran while one was open for 4% of the time, Pallas kernels for 11%

profile of v10, /device:TPU:1, one launch (start us, length us, event | category | flops | bytes accessed | tf_op | source)
XLA Modules:
  0.0 164.4 jit_solution(14507065970464842988)
XLA Ops:
  0.0 3.7 %arrange.2 = bf16[16,64,768]{2,1,0:T(8,128)(2,1)} custom-call(s32[1]{0:T(128)} %bitcast.core_ref, bf16[64,16384]{1,0:T(8,128)(2,1)} %bitcast.41, bf16[64,512]{1,0:T(8,128)(2,1)} %w_ref.3), custom_call_target="tpu_custom_call" | custom-call | tf_op jit(solution)/shard_map/arrange/pallas_call | solution.py:31
  3.7 3.6 %arrange.3 = bf16[16,64,512]{2,1,0:T(8,128)(2,1)} custom-call(s32[1]{0:T(128)} %bitcast.core_ref, bf16[64,16384]{1,0:T(8,128)(2,1)} %bitcast.42, bf16[64,512]{1,0:T(8,128)(2,1)} %w_ref.3), custom_call_target="tpu_custom_call" | custom-call | tf_op jit(solution)/shard_map/arrange/pallas_call | solution.py:31
  7.3 0.0 copy-start.9
  7.3 0.0 copy-start.6
  7.3 2.5 %collective-permute-start = (s32[8,4]{0,1:T(4,128)S(1)}, s32[8,4]{0,1:T(4,128)S(1)}, u32[]{:S(2)}, u32[]{:S(2)}) collective-permute-start(s32[8,4]{0,1:T(4,128)S(1)} %bitcast.46), channel_id=1, source_target_pairs={{0,32},{16,48},{32,64},{48,80},{64,96},{80,112},{96,0},{112,16},{1... | collective-permute-start | bytes 392 | tf_op jit(solution)/shard_map/ppermute | solution.py:283
  9.9 3.3 %collective-permute-start.1 = (s32[8,4]{0,1:T(4,128)S(1)}, s32[8,4]{0,1:T(4,128)S(1)}, u32[]{:S(2)}, u32[]{:S(2)}) collective-permute-start(s32[8,4]{0,1:T(4,128)S(1)} %bitcast.47), channel_id=1, source_target_pairs={{0,64},{16,80},{32,96},{48,112},{64,0},{80,16},{96,32},{112,48},{1... | collective-permute-start | bytes 392 | tf_op jit(solution)/shard_map/ppermute | solution.py:283
  13.2 0.7 collective-permute-start.2
  13.9 6.8 %all-to-all-start = ((bf16[16,64,768]{2,1,0:T(8,128)(2,1)}), bf16[16,64,768]{2,1,0:T(8,128)(2,1)}, u32[]{:S(2)}, u32[]{:S(2)}) async-start(bf16[16,64,768]{2,1,0:T(8,128)(2,1)} %arrange.2), calls=%async_computation | async-start | bytes 3145728 | tf_op jit(solution)/shard_map/all_to_all | solution.py:290
  20.8 0.1 copy.17
  20.9 0.9 fusion
  22.0 0.1 pad.24.clone
  22.1 0.1 maximum_maximum_fusion.refs_5_.refs_9_
  22.2 0.1 select_multiply_fusion
  22.3 0.1 fusion.6
  22.4 0.0 collective-permute-done
  22.4 0.0 collective-permute-done.2
  22.4 1.9 %collective-permute-start.3 = (s32[4,8,4]{1,2,0:T(4,128)S(1)}, s32[4,8,4]{1,2,0:T(4,128)S(1)}, u32[]{:S(2)}, u32[]{:S(2)}) collective-permute-start(s32[4,8,4]{1,2,0:T(4,128)S(1)} %get-tuple-element.72), channel_id=1, source_target_pairs={{0,16},{16,0},{32,48},{48,32},{64,80},{80,64},{96,112},{112,96},{1... | collective-permute-start | bytes 1544 | tf_op jit(solution)/shard_map/ppermute | solution.py:283
  24.4 6.9 %caps.1.cap_ref = bf16[8,12,128,128]{3,2,1,0:T(8,128)(2,1)} custom-call(s32[8,12,128,128]{3,2,1,0:T(8,128)} %mask_ref.1), custom_call_target="tpu_custom_call" | custom-call | tf_op jit(solution)/shard_map/caps/pallas_call | solution.py:125
  31.3 0.1 copy.18
  31.4 0.1 copy.19
  31.5 0.6 gather_fusion
  32.1 9.4 %all-to-all-done = bf16[16,64,768]{2,1,0:T(8,128)(2,1)} async-done(((bf16[16,64,768]{2,1,0:T(8,128)(2,1)}), bf16[16,64,768]{2,1,0:T(8,128)(2,1)}, u32[]{:S(2)}, u32[]{:S(2)}) %all-to-all-start) | async-done | bytes 1572896 | tf_op jit(solution)/shard_map/all_to_all | solution.py:290
  41.5 1.1 slice.19
  42.6 3.9 %collective-permute-start.4 = (bf16[1024,256]{1,0:T(8,128)(2,1)S(1)}, bf16[1024,256]{1,0:T(8,128)(2,1)S(1)}, u32[]{:S(2)}, u32[]{:S(2)}) collective-permute-start(bf16[1024,256]{1,0:T(8,128)(2,1)S(1)} %slice.19), channel_id=1, source_target_pairs={{0,16},{16,0},{32,48},{48,32},{64,80},{80,64},{96,112},{112,96},{1... | collective-permute-start | bytes 1572872 | tf_op jit(solution)/shard_map/ppermute | solution.py:283
  46.5 4.3 %all-to-all-start.1 = ((bf16[16,64,512]{2,1,0:T(8,128)(2,1)}), bf16[16,64,512]{2,1,0:T(8,128)(2,1)}, u32[]{:S(2)}, u32[]{:S(2)}) async-start(bf16[16,64,512]{2,1,0:T(8,128)(2,1)} %arrange.3), calls=%async_computation.1 | async-start | bytes 2097152 | tf_op jit(solution)/shard_map/all_to_all | solution.py:306
  50.9 0.0 collective-permute-done.4
  50.9 2.2 %convolution_convert_fusion.1.refs_0_ = bf16[512,512]{1,0:T(8,128)(2,1)S(1)} fusion(bf16[1024,768]{1,0:T(8,128)(2,1)} %bitcast.2, bf16[1024,256]{1,0:T(8,128)(2,1)S(1)} %collective-permute-done.4, bf16[1024,256]{1,0:T(8,128)(2,1)S(1)} %slice.19, pred[]{:T(512)S(6)} %eq.25), kind=kOutput, calls=%fused_computation.2 | convolution fusion | flops 541851648 | bytes 2621441 | tf_op jit(solution)/shard_map/dot_general | solution.py:313
  53.1 0.8 collective-permute-start.5
  53.9 1.9 %collective-permute-start.6 = (bf16[512,512]{1,0:T(8,128)(2,1)S(1)}, bf16[512,512]{1,0:T(8,128)(2,1)S(1)}, u32[]{:S(2)}, u32[]{:S(2)}) collective-permute-start(bf16[512,512]{1,0:T(8,128)(2,1)S(1)} %convolution_convert_fusion.1.refs_0_), channel_id=1, source_target_pairs={{0,96},{16,112},{32,0},{48,16},{64,32},{80,48},{96,64},{112,80},{1... | collective-permute-start | bytes 1572872 | tf_op jit(solution)/shard_map/ppermute | solution.py:283
  55.9 0.6 collective-permute-start.11
  56.4 13.6 %all-to-all-done.1 = bf16[16,64,512]{2,1,0:T(8,128)(2,1)} async-done(((bf16[16,64,512]{2,1,0:T(8,128)(2,1)}), bf16[16,64,512]{2,1,0:T(8,128)(2,1)}, u32[]{:S(2)}, u32[]{:S(2)}) %all-to-all-start.1) | async-done | bytes 1048608 | tf_op jit(solution)/shard_map/all_to_all | solution.py:306
  70.0 0.0 collective-permute-done.6.refs_4_
  70.0 2.6 %convolution_convert_fusion.refs_1_ = bf16[512,512]{1,0:T(8,128)(2,1)S(1)} fusion(bf16[1024,512]{1,0:T(8,128)(2,1)} %bitcast.17, bf16[1024,256]{1,0:T(8,128)(2,1)} %copy-done.8, bf16[1024,256]{1,0:T(8,128)(2,1)} %copy-done.3, pred[]{:T(512)S(6)} %eq.25), kind=kOutput, calls=%fused_computation.1 | convolution fusion | flops 541851648 | bytes 2621441 | tf_op jit(solution)/shard_map/dot_general | solution.py:313
  72.6 0.9 collective-permute-start.12
  73.5 0.7 collective-permute-start.7
  74.2 1.9 %collective-permute-start.8 = (bf16[512,512]{1,0:T(8,128)(2,1)S(1)}, bf16[512,512]{1,0:T(8,128)(2,1)S(1)}, u32[]{:S(2)}, u32[]{:S(2)}) collective-permute-start(bf16[512,512]{1,0:T(8,128)(2,1)S(1)} %convolution_convert_fusion.refs_1_), channel_id=1, source_target_pairs={{0,96},{16,112},{32,0},{48,16},{64,32},{80,48},{96,64},{112,80},{1... | collective-permute-start | bytes 1572872 | tf_op jit(solution)/shard_map/ppermute | solution.py:283
  76.2 0.1 collective-permute-start.10
  76.3 1.5 collective-permute-start.9
  77.8 1.2 collective-permute-start.15
  79.0 3.5 %transform.3 = (bf16[32,2,128,512]{3,2,1,0:T(8,128)(2,1)S(1)}, f32[32,8,128]{2,1,0:T(8,128)S(1)}) custom-call(s32[8,4]{1,0:T(8,128)S(1)} %bitcast.38, bf16[512,512]{1,0:T(8,128)(2,1)S(1)} %convolution_convert_fusion.1.refs_0_, bf16[512,512]{1,0:T(8,128)(2,1)S(1)} %convolution_convert_fusion.refs_1_, bf16[512,512]{1,0:T(8,128)(2,1)} %collective-permute-done.11.refs_2_, ...), custom_call_target="tpu_custom_call" | custom-call | tf_op jit(solution)/shard_map/transform/pallas_call | solution.py:100
  82.6 10.5 %collective-permute-done.10.refs_1_ = bf16[256,512]{1,0:T(8,128)(2,1)S(1)} collective-permute-done((bf16[256,512]{1,0:T(8,128)(2,1)S(1)}, bf16[256,512]{1,0:T(8,128)(2,1)S(1)}, u32[]{:S(2)}, u32[]{:S(2)}) %collective-permute-start.10) | collective-permute-done | bytes 262176 | tf_op jit(solution)/shard_map/ppermute | solution.py:283
  93.0 1.2 collective-permute-start.17
  94.2 0.0 collective-permute-done.9.refs_0_
  94.2 0.0 collective-permute-done.7.refs_1_
  94.2 0.0 collective-permute-done.8.refs_5_
  94.2 0.5 collective-permute-start.16
  94.7 0.1 collective-permute-start.18
  94.9 0.1 collective-permute-start.13
  94.9 3.2 %collective-permute-start.14 = (bf16[256,512]{1,0:T(8,128)(2,1)S(1)}, bf16[256,512]{1,0:T(8,128)(2,1)S(1)}, u32[]{:S(2)}, u32[]{:S(2)}) collective-permute-start(bf16[256,512]{1,0:T(8,128)(2,1)S(1)} %slice.23), channel_id=1, source_target_pairs={{0,96},{16,112},{32,0},{48,16},{64,32},{80,48},{96,64},{112,80},{1... | collective-permute-start | bytes 786440 | tf_op jit(solution)/shard_map/ppermute | solution.py:283
  98.2 0.0 collective-permute-done.17.refs_6_
  98.2 0.4 collective-permute-start.19
  98.6 0.0 collective-permute-done.16.refs_3_
  98.6 0.1 collective-permute-start.20
  98.7 0.0 collective-permute-done.18.refs_7_
  98.7 7.0 %transform.4 = (bf16[32,2,128,512]{3,2,1,0:T(8,128)(2,1)S(1)}, f32[32,8,128]{2,1,0:T(8,128)S(1)}) custom-call(s32[8,4]{1,0:T(8,128)S(1)} %bitcast.39, bf16[512,512]{1,0:T(8,128)(2,1)S(1)} %collective-permute-done.5.refs_0_, bf16[512,512]{1,0:T(8,128)(2,1)S(1)} %collective-permute-done.7.refs_1_, ...), custom_call_target="tpu_custom_call", output_to_operand_aliasing={{0}: (11, {}), {1}: (12, {})} | custom-call | tf_op jit(solution)/shard_map/transform/pallas_call | solution.py:100
  105.8 0.4 collective-permute-start.21
  106.2 0.1 collective-permute-start.22
  106.3 0.1 pad_maximum_fusion
  106.4 0.0 copy-start.2
  106.4 0.0 collective-permute-done.20.refs_5_
  106.4 0.9 collective-permute-done.21.refs_6_
  107.4 0.4 collective-permute-done.22.refs_7_
  107.7 3.8 %transform.5 = (bf16[32,2,128,512]{3,2,1,0:T(8,128)(2,1)S(1)}, f32[32,8,128]{2,1,0:T(8,128)S(1)}) custom-call(s32[8,4]{1,0:T(8,128)S(1)} %bitcast.40, bf16[256,512]{1,0:T(8,128)(2,1)S(1)} %collective-permute-done.9.refs_0_, bf16[256,512]{1,0:T(8,128)(2,1)S(1)} %collective-permute-done.10.refs_1_, ...), custom_call_target="tpu_custom_call", output_to_operand_aliasing={{0}: (11, {}), {1}: (12, {})} | custom-call | tf_op jit(solution)/shard_map/transform/pallas_call | solution.py:100
  111.6 52.8 %attend.1 = bf16[8,128,512]{2,1,0:T(8,128)(2,1)} custom-call(s32[8,12]{1,0:T(8,128)S(1)} %copy-done.2, s32[8,12]{1,0:T(8,128)S(1)} %fusion.15.slot_ref, bf16[8,128,512]{2,1,0:T(8,128)(2,1)S(1)} %bitcast.37, bf16[8,12,128,128]{3,2,1,0:T(8,128)(2,1)S(1)} %copy-done, bf16[3,512,128]{2,1,0:T(8,128)(2,1)S(1)} %pad_maximum_fusion.1.tgt_ref, ...), custom_call_target="tpu_custom_call" | custom-call | tf_op jit(solution)/shard_map/attend/pallas_call | solution.py:224
  (44 shorter events, 0.3 us)
Async XLA Ops:
  3.7 3.6 %copy-start.7 = (s32[1,8,4]{1,2,0:T(4,128)S(1)}, s32[1,8,4]{1,2,0:T(4,128)}, u32[]{:S(2)}) copy-start(s32[1,8,4]{1,2,0:T(4,128)} %param.17) | copy-start | bytes 388
  7.3 13.4 %copy-start.4 = (f32[2,512]{1,0:T(2,128)S(1)}, f32[2,512]{1,0:T(2,128)}, u32[]{:S(2)}) copy-start(f32[2,512]{1,0:T(2,128)} %param.14) | copy-start | bytes 12292
  7.3 13.6 %copy-start.5 = (f32[2,512]{1,0:T(2,128)S(1)}, f32[2,512]{1,0:T(2,128)}, u32[]{:S(2)}) copy-start(f32[2,512]{1,0:T(2,128)} %param.13) | copy-start | bytes 12292
  7.3 13.6 %copy-start.1 = (bf16[2,512,512]{2,1,0:T(8,128)(2,1)S(1)}, bf16[2,512,512]{2,1,0:T(8,128)(2,1)}, u32[]{:S(2)}) copy-start(bf16[2,512,512]{2,1,0:T(8,128)(2,1)} %refs_8_.3) | copy-start | bytes 3145732
  7.3 14.6 %copy-start.9 = (s32[4,1]{0,1:T(1,128)S(1)}, s32[4,1]{0,1:T(1,128)}, u32[]{:S(2)}) copy-start(s32[4,1]{0,1:T(1,128)} %constant.134) | copy-start | bytes 52
  7.3 14.7 %copy-start.6 = (s32[8,12]{1,0:T(8,128)S(1)}, s32[8,12]{1,0:T(8,128)}, u32[]{:S(2)}) copy-start(s32[8,12]{1,0:T(8,128)} %param.18) | copy-start | bytes 1156
  7.3 15.0 %collective-permute-start = (s32[8,4]{0,1:T(4,128)S(1)}, s32[8,4]{0,1:T(4,128)S(1)}, u32[]{:S(2)}, u32[]{:S(2)}) collective-permute-start(s32[8,4]{0,1:T(4,128)S(1)} %bitcast.46), channel_id=1, source_target_pairs={{0,32},{16,48},{32,64},{48,80},{64,96},{80,112},{96,0},{112,16},{1... | collective-permute-start | bytes 392 | tf_op jit(solution)/shard_map/ppermute | solution.py:283
  9.9 12.5 %collective-permute-start.1 = (s32[8,4]{0,1:T(4,128)S(1)}, s32[8,4]{0,1:T(4,128)S(1)}, u32[]{:S(2)}, u32[]{:S(2)}) collective-permute-start(s32[8,4]{0,1:T(4,128)S(1)} %bitcast.47), channel_id=1, source_target_pairs={{0,64},{16,80},{32,96},{48,112},{64,0},{80,16},{96,32},{112,48},{1... | collective-permute-start | bytes 392 | tf_op jit(solution)/shard_map/ppermute | solution.py:283
  13.2 9.2 %collective-permute-start.2 = (s32[8,4]{0,1:T(4,128)S(1)}, s32[8,4]{0,1:T(4,128)S(1)}, u32[]{:S(2)}, u32[]{:S(2)}) collective-permute-start(s32[8,4]{0,1:T(4,128)S(1)} %bitcast.48), channel_id=1, source_target_pairs={{0,96},{16,112},{32,0},{48,16},{64,32},{80,48},{96,64},{112,80},{1... | collective-permute-start | bytes 392 | tf_op jit(solution)/shard_map/ppermute | solution.py:283
  13.9 27.6 %all-to-all-start = ((bf16[16,64,768]{2,1,0:T(8,128)(2,1)}), bf16[16,64,768]{2,1,0:T(8,128)(2,1)}, u32[]{:S(2)}, u32[]{:S(2)}) async-start(bf16[16,64,768]{2,1,0:T(8,128)(2,1)} %arrange.2), calls=%async_computation | async-start | bytes 3145728 | tf_op jit(solution)/shard_map/all_to_all | solution.py:290
  22.4 9.0 %collective-permute-start.3 = (s32[4,8,4]{1,2,0:T(4,128)S(1)}, s32[4,8,4]{1,2,0:T(4,128)S(1)}, u32[]{:S(2)}, u32[]{:S(2)}) collective-permute-start(s32[4,8,4]{1,2,0:T(4,128)S(1)} %get-tuple-element.72), channel_id=1, source_target_pairs={{0,16},{16,0},{32,48},{48,32},{64,80},{80,64},{96,112},{112,96},{1... | collective-permute-start | bytes 1544 | tf_op jit(solution)/shard_map/ppermute | solution.py:283
  42.6 8.3 %copy-start.3 = (bf16[1024,256]{1,0:T(8,128)(2,1)}, bf16[1024,256]{1,0:T(8,128)(2,1)S(1)}, u32[]{:S(2)}) copy-start(bf16[1024,256]{1,0:T(8,128)(2,1)S(1)} %slice.19) | copy-start | bytes 1572868
  42.6 8.3 %collective-permute-start.4 = (bf16[1024,256]{1,0:T(8,128)(2,1)S(1)}, bf16[1024,256]{1,0:T(8,128)(2,1)S(1)}, u32[]{:S(2)}, u32[]{:S(2)}) collective-permute-start(bf16[1024,256]{1,0:T(8,128)(2,1)S(1)} %slice.19), channel_id=1, source_target_pairs={{0,16},{16,0},{32,48},{48,32},{64,80},{80,64},{96,112},{112,96},{1... | collective-permute-start | bytes 1572872 | tf_op jit(solution)/shard_map/ppermute | solution.py:283
  46.5 23.5 %all-to-all-start.1 = ((bf16[16,64,512]{2,1,0:T(8,128)(2,1)}), bf16[16,64,512]{2,1,0:T(8,128)(2,1)}, u32[]{:S(2)}, u32[]{:S(2)}) async-start(bf16[16,64,512]{2,1,0:T(8,128)(2,1)} %arrange.3), calls=%async_computation.1 | async-start | bytes 2097152 | tf_op jit(solution)/shard_map/all_to_all | solution.py:306
  50.9 2.2 %copy-start.8 = (bf16[1024,256]{1,0:T(8,128)(2,1)}, bf16[1024,256]{1,0:T(8,128)(2,1)S(1)}, u32[]{:S(2)}) copy-start(bf16[1024,256]{1,0:T(8,128)(2,1)S(1)} %collective-permute-done.4) | copy-start | bytes 1572868
  53.1 16.9 %collective-permute-start.5 = (bf16[512,512]{1,0:T(8,128)(2,1)S(1)}, bf16[512,512]{1,0:T(8,128)(2,1)S(1)}, u32[]{:S(2)}, u32[]{:S(2)}) collective-permute-start(bf16[512,512]{1,0:T(8,128)(2,1)S(1)} %convolution_convert_fusion.1.refs_0_), channel_id=1, source_target_pairs={{0,32},{16,48},{32,64},{48,80},{64,96},{80,112},{96,0},{112,16},{1... | collective-permute-start | bytes 1572872 | tf_op jit(solution)/shard_map/ppermute | solution.py:283
  53.9 16.1 %collective-permute-start.6 = (bf16[512,512]{1,0:T(8,128)(2,1)S(1)}, bf16[512,512]{1,0:T(8,128)(2,1)S(1)}, u32[]{:S(2)}, u32[]{:S(2)}) collective-permute-start(bf16[512,512]{1,0:T(8,128)(2,1)S(1)} %convolution_convert_fusion.1.refs_0_), channel_id=1, source_target_pairs={{0,96},{16,112},{32,0},{48,16},{64,32},{80,48},{96,64},{112,80},{1... | collective-permute-start | bytes 1572872 | tf_op jit(solution)/shard_map/ppermute | solution.py:283
  55.9 20.5 %collective-permute-start.11 = (bf16[512,512]{1,0:T(8,128)(2,1)S(1)}, bf16[512,512]{1,0:T(8,128)(2,1)}, u32[]{:S(2)}, u32[]{:S(2)}) collective-permute-start(bf16[512,512]{1,0:T(8,128)(2,1)S(1)} %convolution_convert_fusion.1.refs_0_), channel_id=1, source_target_pairs={{0,16},{16,0},{32,48},{48,32},{64,80},{80,64},{96,112},{112,96},{1... | collective-permute-start | bytes 1572872 | tf_op jit(solution)/shard_map/ppermute | solution.py:283
  72.6 5.2 %collective-permute-start.12 = (bf16[512,512]{1,0:T(8,128)(2,1)S(1)}, bf16[512,512]{1,0:T(8,128)(2,1)S(1)}, u32[]{:S(2)}, u32[]{:S(2)}) collective-permute-start(bf16[512,512]{1,0:T(8,128)(2,1)S(1)} %convolution_convert_fusion.refs_1_), channel_id=1, source_target_pairs={{0,16},{16,0},{32,48},{48,32},{64,80},{80,64},{96,112},{112,96},{1... | collective-permute-start | bytes 1572872 | tf_op jit(solution)/shard_map/ppermute | solution.py:283
  73.5 20.7 %collective-permute-start.7 = (bf16[512,512]{1,0:T(8,128)(2,1)S(1)}, bf16[512,512]{1,0:T(8,128)(2,1)S(1)}, u32[]{:S(2)}, u32[]{:S(2)}) collective-permute-start(bf16[512,512]{1,0:T(8,128)(2,1)S(1)} %convolution_convert_fusion.refs_1_), channel_id=1, source_target_pairs={{0,32},{16,48},{32,64},{48,80},{64,96},{80,112},{96,0},{112,16},{1... | collective-permute-start | bytes 1572872 | tf_op jit(solution)/shard_map/ppermute | solution.py:283
  74.2 20.0 %collective-permute-start.8 = (bf16[512,512]{1,0:T(8,128)(2,1)S(1)}, bf16[512,512]{1,0:T(8,128)(2,1)S(1)}, u32[]{:S(2)}, u32[]{:S(2)}) collective-permute-start(bf16[512,512]{1,0:T(8,128)(2,1)S(1)} %convolution_convert_fusion.refs_1_), channel_id=1, source_target_pairs={{0,96},{16,112},{32,0},{48,16},{64,32},{80,48},{96,64},{112,80},{1... | collective-permute-start | bytes 1572872 | tf_op jit(solution)/shard_map/ppermute | solution.py:283
  76.2 16.8 %collective-permute-start.10 = (bf16[256,512]{1,0:T(8,128)(2,1)S(1)}, bf16[256,512]{1,0:T(8,128)(2,1)S(1)}, u32[]{:S(2)}, u32[]{:S(2)}) collective-permute-start(bf16[256,512]{1,0:T(8,128)(2,1)S(1)} %slice.21), channel_id=1, source_target_pairs={{0,96},{16,112},{32,0},{48,16},{64,32},{80,48},{96,64},{112,80},{1... | collective-permute-start | bytes 786440 | tf_op jit(solution)/shard_map/ppermute | solution.py:283
  76.3 17.9 %collective-permute-start.9 = (bf16[256,512]{1,0:T(8,128)(2,1)S(1)}, bf16[256,512]{1,0:T(8,128)(2,1)S(1)}, u32[]{:S(2)}, u32[]{:S(2)}) collective-permute-start(bf16[256,512]{1,0:T(8,128)(2,1)S(1)} %slice.20), channel_id=1, source_target_pairs={{0,32},{16,48},{32,64},{48,80},{64,96},{80,112},{96,0},{112,16},{1... | collective-permute-start | bytes 786440 | tf_op jit(solution)/shard_map/ppermute | solution.py:283
  77.8 17.1 %collective-permute-start.15 = (bf16[512,512]{1,0:T(8,128)(2,1)S(1)}, bf16[512,512]{1,0:T(8,128)(2,1)S(1)}, u32[]{:S(2)}, u32[]{:S(2)}) collective-permute-start(bf16[512,512]{1,0:T(8,128)(2,1)S(1)} %collective-permute-done.5.refs_0_), channel_id=1, source_target_pairs={{0,16},{16,0},{32,48},{48,32},{64,80},{80,64},{96,112},{112,96},{1... | collective-permute-start | bytes 1572872 | tf_op jit(solution)/shard_map/ppermute | solution.py:283
  93.0 5.2 %collective-permute-start.17 = (bf16[512,512]{1,0:T(8,128)(2,1)S(1)}, bf16[512,512]{1,0:T(8,128)(2,1)S(1)}, u32[]{:S(2)}, u32[]{:S(2)}) collective-permute-start(bf16[512,512]{1,0:T(8,128)(2,1)S(1)} %collective-permute-done.6.refs_4_), channel_id=1, source_target_pairs={{0,16},{16,0},{32,48},{48,32},{64,80},{80,64},{96,112},{112,96},{1... | collective-permute-start | bytes 1572872 | tf_op jit(solution)/shard_map/ppermute | solution.py:283
  94.2 4.3 %collective-permute-start.16 = (bf16[512,512]{1,0:T(8,128)(2,1)S(1)}, bf16[512,512]{1,0:T(8,128)(2,1)S(1)}, u32[]{:S(2)}, u32[]{:S(2)}) collective-permute-start(bf16[512,512]{1,0:T(8,128)(2,1)S(1)} %collective-permute-done.7.refs_1_), channel_id=1, source_target_pairs={{0,16},{16,0},{32,48},{48,32},{64,80},{80,64},{96,112},{112,96},{1... | collective-permute-start | bytes 1572872 | tf_op jit(solution)/shard_map/ppermute | solution.py:283
  94.7 4.0 %collective-permute-start.18 = (bf16[512,512]{1,0:T(8,128)(2,1)S(1)}, bf16[512,512]{1,0:T(8,128)(2,1)S(1)}, u32[]{:S(2)}, u32[]{:S(2)}) collective-permute-start(bf16[512,512]{1,0:T(8,128)(2,1)S(1)} %collective-permute-done.8.refs_5_), channel_id=1, source_target_pairs={{0,16},{16,0},{32,48},{48,32},{64,80},{80,64},{96,112},{112,96},{1... | collective-permute-start | bytes 1572872 | tf_op jit(solution)/shard_map/ppermute | solution.py:283
  94.9 10.9 %collective-permute-start.13 = (bf16[256,512]{1,0:T(8,128)(2,1)S(1)}, bf16[256,512]{1,0:T(8,128)(2,1)S(1)}, u32[]{:S(2)}, u32[]{:S(2)}) collective-permute-start(bf16[256,512]{1,0:T(8,128)(2,1)S(1)} %slice.22), channel_id=1, source_target_pairs={{0,32},{16,48},{32,64},{48,80},{64,96},{80,112},{96,0},{112,16},{1... | collective-permute-start | bytes 786440 | tf_op jit(solution)/shard_map/ppermute | solution.py:283
  94.9 10.8 %collective-permute-start.14 = (bf16[256,512]{1,0:T(8,128)(2,1)S(1)}, bf16[256,512]{1,0:T(8,128)(2,1)S(1)}, u32[]{:S(2)}, u32[]{:S(2)}) collective-permute-start(bf16[256,512]{1,0:T(8,128)(2,1)S(1)} %slice.23), channel_id=1, source_target_pairs={{0,96},{16,112},{32,0},{48,16},{64,32},{80,48},{96,64},{112,80},{1... | collective-permute-start | bytes 786440 | tf_op jit(solution)/shard_map/ppermute | solution.py:283
  98.2 8.2 %collective-permute-start.19 = (bf16[256,512]{1,0:T(8,128)(2,1)S(1)}, bf16[256,512]{1,0:T(8,128)(2,1)S(1)}, u32[]{:S(2)}, u32[]{:S(2)}) collective-permute-start(bf16[256,512]{1,0:T(8,128)(2,1)S(1)} %collective-permute-done.9.refs_0_), channel_id=1, source_target_pairs={{0,16},{16,0},{32,48},{48,32},{64,80},{80,64},{96,112},{112,96},{1... | collective-permute-start | bytes 786440 | tf_op jit(solution)/shard_map/ppermute | solution.py:283
  98.6 7.9 %collective-permute-start.20 = (bf16[256,512]{1,0:T(8,128)(2,1)S(1)}, bf16[256,512]{1,0:T(8,128)(2,1)S(1)}, u32[]{:S(2)}, u32[]{:S(2)}) collective-permute-start(bf16[256,512]{1,0:T(8,128)(2,1)S(1)} %collective-permute-done.10.refs_1_), channel_id=1, source_target_pairs={{0,16},{16,0},{32,48},{48,32},{64,80},{80,64},{96,112},{112,96},{1... | collective-permute-start | bytes 786440 | tf_op jit(solution)/shard_map/ppermute | solution.py:283
  105.8 1.6 collective-permute-start.21
  106.2 1.5 collective-permute-start.22
  106.4 5.1 %copy-start.2 = (s32[8,12]{1,0:T(8,128)S(1)}, s32[8,12]{1,0:T(8,128)}, u32[]{:S(2)}) copy-start(s32[8,12]{1,0:T(8,128)} %rel_ref.1) | copy-start | bytes 1156
  107.7 3.8 %copy-start = (bf16[8,12,128,128]{3,2,1,0:T(8,128)(2,1)S(1)}, bf16[8,12,128,128]{3,2,1,0:T(8,128)(2,1)}, u32[]{:S(2)}) copy-start(bf16[8,12,128,128]{3,2,1,0:T(8,128)(2,1)} %caps.1.cap_ref) | copy-start | bytes 9437188

commit v11 on v10

--- a/solution.py
+++ b/solution.py
@@ -300,8 +300,8 @@
     slots = (2 * (distance ^ (distance >> 1)) + (peer % 2 ^ core)) * CAP + source_slots % CAP
     src_vectors, tgt_vectors = score_vectors(relation_weight, att_source, att_target)
 
-    got, outgoing, cap, src_vectors, tgt_vectors, slots, index = lax.optimization_barrier(
-        (got, outgoing, caps(edge_mask), src_vectors, tgt_vectors, slots, index)
+    got, outgoing, src_vectors, tgt_vectors, slots, index = lax.optimization_barrier(
+        (got, outgoing, src_vectors, tgt_vectors, slots, index)
     )
     later = lax.all_to_all(outgoing, "feat", 0, 0, tiled=True).reshape(n_feat * depth, rows_local - rows_a)
 
@@ -332,7 +332,9 @@
     b = project(later)
     up_b, down_b = ring(b)
     done = spread(both([(a, 0, cut), (b, cut, local_blocks)]), 0, (None, None))
-    up_b, down_b, far_a, done = lax.optimization_barrier((up_b, down_b, far_a, done))
+    edge_mask, done = lax.optimization_barrier((edge_mask, done))
+    cap = caps(edge_mask)
+    up_b, down_b, far_a, cap, done = lax.optimization_barrier((up_b, down_b, far_a, cap, done))
     far_b = forward(up_b, down_b)
     done = spread(
         both([(up_a, 0, cut), (up_b, cut, local_blocks)]) + both([(down_a, 0, cut), (down_b, cut, local_blocks)]), 2, done

time: 165 us -> 176 us (1.067)
  local copies, waits for them, and re-layouts: 2.21 us -> 18.9 us
  waiting for transfers between devices: 34.8 us -> 30.5 us
    unnamed x20 -> x34, local copies, waits for them, and re-layouts: 0.05 us -> 14.4 us
    ppermute x23, waiting for transfers between devices: 11.8 us -> 2.03 us  [send(): return lax.ppermute(x, 'graph', pairs)]
    all_to_all x1, waiting for transfers between devices: 9.44 us -> 15 us  [shards(): lax.all_to_all(first, 'feat', 0, 0, tiled=True)]
    slice x4, local copies, waits for them, and re-layouts: 0.07 us -> 3.39 us  [forward(): return (send(up[:middle], 1), send(down[middle:], -1))]
  transfers between devices with their start and end apart: 25 -> 25, of which waited for: 5 -> 5; matrix products, arithmetic and copies ran while one was open for 4% -> 7% of each run, Pallas kernels for 11% -> 9%
where the time goes in v11:
time: 176 us; the launch traced here: 175 us
  Pallas kernels  80.2 us (46%)
  starting transfers between devices  38.4 us (22%)
  waiting for transfers between devices  30.5 us (17%)
  local copies, waits for them, and re-layouts  18.9 us (11%)
  matrix products  5.96 us (3%)
    pallas_call x1, Pallas kernels, attend(): pl.pallas_call(attend_kernel, in_specs=[scalars] * 2 + [inside] * 5, out_...  52.8 us
    ppermute x23, starting transfers between devices, send(): return lax.ppermute(x, 'graph', pairs)  27.3 us
    all_to_all x1, waiting for transfers between devices, shards(): lax.all_to_all(first, 'feat', 0, 0, tiled=True)  15 us
    unnamed x34, local copies, waits for them, and re-layouts  14.4 us
    all_to_all x1, waiting for transfers between devices, shards(): lax.all_to_all(outgoing, 'feat', 0, 0, tiled=True)  13.5 us
    pallas_call x3, Pallas kernels, transform(): pl.pallas_call(functools.partial(transform_kernel, bounds, first), in_spe...  13.2 us
    pallas_call x2, Pallas kernels, arrange(): pl.pallas_call(functools.partial(arrange_kernel, low, high), grid_spec=pl...  7.27 us
    pallas_call x1, Pallas kernels, caps(): pl.pallas_call(cap_kernel, grid=shape[:1], in_specs=[spec], out_specs=spe...  6.89 us
  transfers between devices with their start and end apart: 25, of which 5 were waited for; matrix products, arithmetic and copies ran while one was open for 7% of the time, Pallas kernels for 9%

profile of v11, /device:TPU:1, one launch (start us, length us, event | category | flops | bytes accessed | tf_op | source)
XLA Modules:
  0.0 175.5 jit_solution(14123905031685042301)
XLA Ops:
  0.0 3.7 %arrange.2 = bf16[16,64,768]{2,1,0:T(8,128)(2,1)} custom-call(s32[1]{0:T(128)} %bitcast.core_ref, bf16[64,16384]{1,0:T(8,128)(2,1)} %bitcast.41, bf16[64,512]{1,0:T(8,128)(2,1)} %w_ref.3), custom_call_target="tpu_custom_call" | custom-call | tf_op jit(solution)/shard_map/arrange/pallas_call | solution.py:31
  3.7 3.6 %arrange.3 = bf16[16,64,512]{2,1,0:T(8,128)(2,1)} custom-call(s32[1]{0:T(128)} %bitcast.core_ref, bf16[64,16384]{1,0:T(8,128)(2,1)} %bitcast.42, bf16[64,512]{1,0:T(8,128)(2,1)} %w_ref.3), custom_call_target="tpu_custom_call" | custom-call | tf_op jit(solution)/shard_map/arrange/pallas_call | solution.py:31
  7.3 0.0 copy-start.16
  7.3 0.0 copy-start.14
  7.3 2.5 %collective-permute-start = (s32[8,4]{0,1:T(4,128)S(1)}, s32[8,4]{0,1:T(4,128)S(1)}, u32[]{:S(2)}, u32[]{:S(2)}) collective-permute-start(s32[8,4]{0,1:T(4,128)S(1)} %bitcast.48), channel_id=1, source_target_pairs={{0,32},{16,48},{32,64},{48,80},{64,96},{80,112},{96,0},{112,16},{1... | collective-permute-start | bytes 392 | tf_op jit(solution)/shard_map/ppermute | solution.py:283
  9.8 3.3 %collective-permute-start.1 = (s32[8,4]{0,1:T(4,128)S(1)}, s32[8,4]{0,1:T(4,128)S(1)}, u32[]{:S(2)}, u32[]{:S(2)}) collective-permute-start(s32[8,4]{0,1:T(4,128)S(1)} %bitcast.49), channel_id=1, source_target_pairs={{0,64},{16,80},{32,96},{48,112},{64,0},{80,16},{96,32},{112,48},{1... | collective-permute-start | bytes 392 | tf_op jit(solution)/shard_map/ppermute | solution.py:283
  13.2 0.7 collective-permute-start.2
  13.9 6.8 %all-to-all-start = ((bf16[16,64,768]{2,1,0:T(8,128)(2,1)}), bf16[16,64,768]{2,1,0:T(8,128)(2,1)S(1)}, u32[]{:S(2)}, u32[]{:S(2)}) async-start(bf16[16,64,768]{2,1,0:T(8,128)(2,1)} %arrange.2), calls=%async_computation | async-start | bytes 3145728 | tf_op jit(solution)/shard_map/all_to_all | solution.py:290
  20.7 0.1 copy.17
  20.9 0.9 fusion
  21.9 0.1 pad.24.clone
  22.0 0.7 maximum_maximum_fusion.refs_5_.refs_9_
  22.7 0.1 select_multiply_fusion
  22.8 0.1 fusion.6
  22.9 0.0 collective-permute-done.1
  22.9 0.0 collective-permute-done.2
  23.0 1.9 %collective-permute-start.3 = (s32[4,8,4]{1,2,0:T(4,128)S(1)}, s32[4,8,4]{1,2,0:T(4,128)S(1)}, u32[]{:S(2)}, u32[]{:S(2)}) collective-permute-start(s32[4,8,4]{1,2,0:T(4,128)S(1)} %get-tuple-element.78), channel_id=1, source_target_pairs={{0,16},{16,0},{32,48},{48,32},{64,80},{80,64},{96,112},{112,96},{1... | collective-permute-start | bytes 1544 | tf_op jit(solution)/shard_map/ppermute | solution.py:283
  24.9 0.1 copy.18
  25.0 0.7 collective-permute-done.3
  25.7 0.1 copy.19
  25.8 0.6 gather_fusion
  26.4 15.0 %all-to-all-done = bf16[16,64,768]{2,1,0:T(8,128)(2,1)S(1)} async-done(((bf16[16,64,768]{2,1,0:T(8,128)(2,1)}), bf16[16,64,768]{2,1,0:T(8,128)(2,1)S(1)}, u32[]{:S(2)}, u32[]{:S(2)}) %all-to-all-start) | async-done | bytes 1572896 | tf_op jit(solution)/shard_map/all_to_all | solution.py:290
  41.4 3.9 %collective-permute-start.4 = (bf16[1024,256]{1,0:T(8,128)(2,1)S(1)}, bf16[1024,256]{1,0:T(8,128)(2,1)}, u32[]{:S(2)}, u32[]{:S(2)}) collective-permute-start(bf16[1024,256]{1,0:T(8,128)(2,1)S(1)} %slice.19), channel_id=1, source_target_pairs={{0,16},{16,0},{32,48},{48,32},{64,80},{80,64},{96,112},{112,96},{1... | collective-permute-start | bytes 1572872 | tf_op jit(solution)/shard_map/ppermute | solution.py:283
  45.4 4.3 %all-to-all-start.1 = ((bf16[16,64,512]{2,1,0:T(8,128)(2,1)}), bf16[16,64,512]{2,1,0:T(8,128)(2,1)}, u32[]{:S(2)}, u32[]{:S(2)}) async-start(bf16[16,64,512]{2,1,0:T(8,128)(2,1)} %arrange.3), calls=%async_computation.1 | async-start | bytes 2097152 | tf_op jit(solution)/shard_map/all_to_all | solution.py:306
  49.7 2.3 %convolution_convert_fusion.1.refs_0_ = bf16[512,512]{1,0:T(8,128)(2,1)S(1)} fusion(bf16[1024,768]{1,0:T(8,128)(2,1)S(1)} %bitcast.44, bf16[1024,256]{1,0:T(8,128)(2,1)} %collective-permute-done.4, bf16[1024,256]{1,0:T(8,128)(2,1)} %copy-done.11, pred[]{:T(512)S(6)} %eq.25), kind=kOutput, calls=%fused_computation.2 | convolution fusion | flops 541851648 | bytes 2621441 | tf_op jit(solution)/shard_map/dot_general | solution.py:313
  52.0 0.8 collective-permute-start.5
  52.8 1.9 %collective-permute-start.6 = (bf16[512,512]{1,0:T(8,128)(2,1)S(1)}, bf16[512,512]{1,0:T(8,128)(2,1)S(1)}, u32[]{:S(2)}, u32[]{:S(2)}) collective-permute-start(bf16[512,512]{1,0:T(8,128)(2,1)S(1)} %convolution_convert_fusion.1.refs_0_), channel_id=1, source_target_pairs={{0,96},{16,112},{32,0},{48,16},{64,32},{80,48},{96,64},{112,80},{1... | collective-permute-start | bytes 1572872 | tf_op jit(solution)/shard_map/ppermute | solution.py:283
  54.8 0.6 collective-permute-start.11
  55.4 13.5 %all-to-all-done.1 = bf16[16,64,512]{2,1,0:T(8,128)(2,1)} async-done(((bf16[16,64,512]{2,1,0:T(8,128)(2,1)}), bf16[16,64,512]{2,1,0:T(8,128)(2,1)}, u32[]{:S(2)}, u32[]{:S(2)}) %all-to-all-start.1) | async-done | bytes 1048608 | tf_op jit(solution)/shard_map/all_to_all | solution.py:306
  68.8 0.0 collective-permute-done.5.refs_0_
  68.8 2.8 %convolution_convert_fusion.refs_1_ = bf16[512,512]{1,0:T(8,128)(2,1)S(1)} fusion(bf16[1024,512]{1,0:T(8,128)(2,1)} %bitcast.17, bf16[1024,256]{1,0:T(8,128)(2,1)} %collective-permute-done.4, bf16[1024,256]{1,0:T(8,128)(2,1)} %copy-done.11, pred[]{:T(512)S(6)} %eq.25), kind=kOutput, calls=%fused_computation.1 | convolution fusion | flops 541851648 | bytes 2621441 | tf_op jit(solution)/shard_map/dot_general | solution.py:313
  71.6 0.9 collective-permute-start.12
  72.5 0.7 collective-permute-start.7
  73.3 1.9 %collective-permute-start.8 = (bf16[512,512]{1,0:T(8,128)(2,1)S(1)}, bf16[512,512]{1,0:T(8,128)(2,1)}, u32[]{:S(2)}, u32[]{:S(2)}) collective-permute-start(bf16[512,512]{1,0:T(8,128)(2,1)S(1)} %convolution_convert_fusion.refs_1_), channel_id=1, source_target_pairs={{0,96},{16,112},{32,0},{48,16},{64,32},{80,48},{96,64},{112,80},{1... | collective-permute-start | bytes 1572872 | tf_op jit(solution)/shard_map/ppermute | solution.py:283
  75.2 0.7 slice.21
  75.9 0.0 collective-permute-start.10
  75.9 0.7 slice.20
  76.7 1.5 collective-permute-start.9
  78.1 1.2 collective-permute-start.15
  79.3 3.4 %transform.3 = (bf16[32,2,128,512]{3,2,1,0:T(8,128)(2,1)S(1)}, f32[32,8,128]{2,1,0:T(8,128)S(1)}) custom-call(s32[8,4]{1,0:T(8,128)S(1)} %bitcast.38, bf16[512,512]{1,0:T(8,128)(2,1)S(1)} %convolution_convert_fusion.1.refs_0_, bf16[512,512]{1,0:T(8,128)(2,1)S(1)} %convolution_convert_fusion.refs_1_, bf16[512,512]{1,0:T(8,128)(2,1)} %collective-permute-done.11.refs_2_, ...), custom_call_target="tpu_custom_call" | custom-call | tf_op jit(solution)/shard_map/transform/pallas_call | solution.py:100
  82.7 3.3 %copy-done = bf16[32,2,128,512]{3,2,1,0:T(8,128)(2,1)} copy-done((bf16[32,2,128,512]{3,2,1,0:T(8,128)(2,1)}, bf16[32,2,128,512]{3,2,1,0:T(8,128)(2,1)S(1)}, u32[]{:S(2)}) %copy-start) | copy-done | bytes 8388632
  86.0 6.9 %caps.1.cap_ref = bf16[8,12,128,128]{3,2,1,0:T(8,128)(2,1)} custom-call(s32[8,12,128,128]{3,2,1,0:T(8,128)} %mask_ref), custom_call_target="tpu_custom_call" | custom-call | tf_op jit(solution)/shard_map/caps/pallas_call | solution.py:125
  92.9 0.4 collective-permute-start.17
  93.3 0.5 collective-permute-start.16
  93.8 0.1 collective-permute-start.18
  93.9 1.0 slice.22
  94.9 1.0 slice.23
  95.9 0.1 collective-permute-start.13
  96.0 3.2 %collective-permute-start.14 = (bf16[256,512]{1,0:T(8,128)(2,1)S(1)}, bf16[256,512]{1,0:T(8,128)(2,1)S(1)}, u32[]{:S(2)}, u32[]{:S(2)}) collective-permute-start(bf16[256,512]{1,0:T(8,128)(2,1)S(1)} %slice.23), channel_id=1, source_target_pairs={{0,96},{16,112},{32,0},{48,16},{64,32},{80,48},{96,64},{112,80},{1... | collective-permute-start | bytes 786440 | tf_op jit(solution)/shard_map/ppermute | solution.py:283
  99.2 0.4 collective-permute-start.19
  99.6 0.1 collective-permute-start.20
  99.7 3.4 %copy-done.1 = bf16[32,2,128,512]{3,2,1,0:T(8,128)(2,1)S(1)} copy-done((bf16[32,2,128,512]{3,2,1,0:T(8,128)(2,1)S(1)}, bf16[32,2,128,512]{3,2,1,0:T(8,128)(2,1)}, u32[]{:S(2)}) %copy-start.1) | copy-done | bytes 8388632
  103.1 1.0 copy-done.7
  104.2 6.1 %transform.4 = (bf16[32,2,128,512]{3,2,1,0:T(8,128)(2,1)S(1)}, f32[32,8,128]{2,1,0:T(8,128)S(1)}) custom-call(s32[8,4]{1,0:T(8,128)S(1)} %bitcast.39, bf16[512,512]{1,0:T(8,128)(2,1)S(1)} %collective-permute-done.5.refs_0_, bf16[512,512]{1,0:T(8,128)(2,1)} %collective-permute-done.7.refs_1_, ...), custom_call_target="tpu_custom_call", output_to_operand_aliasing={{0}: (11, {}), {1}: (12, {})} | custom-call | tf_op jit(solution)/shard_map/transform/pallas_call | solution.py:100
  110.3 0.3 collective-permute-start.21
  110.6 0.3 collective-permute-start.22
  110.9 0.1 pad_maximum_fusion
  111.0 0.0 copy-start.10
  111.0 0.9 collective-permute-done.21.refs_6_
  111.9 0.4 collective-permute-done.22.refs_7_
  112.3 3.7 %transform.5 = (bf16[32,2,128,512]{3,2,1,0:T(8,128)(2,1)S(1)}, f32[32,8,128]{2,1,0:T(8,128)S(1)}) custom-call(s32[8,4]{1,0:T(8,128)S(1)} %bitcast.40, bf16[256,512]{1,0:T(8,128)(2,1)} %collective-permute-done.9.refs_0_, bf16[256,512]{1,0:T(8,128)(2,1)} %collective-permute-done.10.refs_1_, ...), custom_call_target="tpu_custom_call", output_to_operand_aliasing={{0}: (11, {}), {1}: (12, {})} | custom-call | tf_op jit(solution)/shard_map/transform/pallas_call | solution.py:100
  116.0 3.3 %copy-done.2 = bf16[32,2,128,512]{3,2,1,0:T(8,128)(2,1)} copy-done((bf16[32,2,128,512]{3,2,1,0:T(8,128)(2,1)}, bf16[32,2,128,512]{3,2,1,0:T(8,128)(2,1)S(1)}, u32[]{:S(2)}) %copy-start.2) | copy-done | bytes 8388632
  119.3 3.4 %copy-done.3 = bf16[32,2,128,512]{3,2,1,0:T(8,128)(2,1)S(1)} copy-done((bf16[32,2,128,512]{3,2,1,0:T(8,128)(2,1)S(1)}, bf16[32,2,128,512]{3,2,1,0:T(8,128)(2,1)}, u32[]{:S(2)}) %copy-start.3) | copy-done | bytes 8388632
  122.7 52.8 %attend.1 = bf16[8,128,512]{2,1,0:T(8,128)(2,1)} custom-call(s32[8,12]{1,0:T(8,128)S(1)} %copy-done.10, s32[8,12]{1,0:T(8,128)S(1)} %fusion.15.slot_ref, bf16[8,128,512]{2,1,0:T(8,128)(2,1)S(1)} %bitcast.37, bf16[8,12,128,128]{3,2,1,0:T(8,128)(2,1)S(1)} %copy-done.4, bf16[3,512,128]{2,1,0:T(8,128)(2,1)S(1)} %pad_maximum_fusion.1.tgt_ref, ...), custom_call_target="tpu_custom_call" | custom-call | tf_op jit(solution)/shard_map/attend/pallas_call | solution.py:224
  (58 shorter events, 0.3 us)
Async XLA Ops:
  3.7 3.6 %copy-start.15 = (s32[1,8,4]{1,2,0:T(4,128)S(1)}, s32[1,8,4]{1,2,0:T(4,128)}, u32[]{:S(2)}) copy-start(s32[1,8,4]{1,2,0:T(4,128)} %param.17) | copy-start | bytes 388
  7.3 13.4 %copy-start.12 = (f32[2,512]{1,0:T(2,128)S(1)}, f32[2,512]{1,0:T(2,128)}, u32[]{:S(2)}) copy-start(f32[2,512]{1,0:T(2,128)} %param.14) | copy-start | bytes 12292
  7.3 13.6 %copy-start.13 = (f32[2,512]{1,0:T(2,128)S(1)}, f32[2,512]{1,0:T(2,128)}, u32[]{:S(2)}) copy-start(f32[2,512]{1,0:T(2,128)} %param.13) | copy-start | bytes 12292
  7.3 13.6 %copy-start.5 = (bf16[2,512,512]{2,1,0:T(8,128)(2,1)S(1)}, bf16[2,512,512]{2,1,0:T(8,128)(2,1)}, u32[]{:S(2)}) copy-start(bf16[2,512,512]{2,1,0:T(8,128)(2,1)} %refs_8_.3) | copy-start | bytes 3145732
  7.3 14.5 %copy-start.16 = (s32[4,1]{0,1:T(1,128)S(1)}, s32[4,1]{0,1:T(1,128)}, u32[]{:S(2)}) copy-start(s32[4,1]{0,1:T(1,128)} %constant.134) | copy-start | bytes 52
  7.3 14.7 %copy-start.14 = (s32[8,12]{1,0:T(8,128)S(1)}, s32[8,12]{1,0:T(8,128)}, u32[]{:S(2)}) copy-start(s32[8,12]{1,0:T(8,128)} %param.18) | copy-start | bytes 1156
  7.3 15.6 %collective-permute-start = (s32[8,4]{0,1:T(4,128)S(1)}, s32[8,4]{0,1:T(4,128)S(1)}, u32[]{:S(2)}, u32[]{:S(2)}) collective-permute-start(s32[8,4]{0,1:T(4,128)S(1)} %bitcast.48), channel_id=1, source_target_pairs={{0,32},{16,48},{32,64},{48,80},{64,96},{80,112},{96,0},{112,16},{1... | collective-permute-start | bytes 392 | tf_op jit(solution)/shard_map/ppermute | solution.py:283
  9.8 13.1 %collective-permute-start.1 = (s32[8,4]{0,1:T(4,128)S(1)}, s32[8,4]{0,1:T(4,128)S(1)}, u32[]{:S(2)}, u32[]{:S(2)}) collective-permute-start(s32[8,4]{0,1:T(4,128)S(1)} %bitcast.49), channel_id=1, source_target_pairs={{0,64},{16,80},{32,96},{48,112},{64,0},{80,16},{96,32},{112,48},{1... | collective-permute-start | bytes 392 | tf_op jit(solution)/shard_map/ppermute | solution.py:283
  13.2 9.8 %collective-permute-start.2 = (s32[8,4]{0,1:T(4,128)S(1)}, s32[8,4]{0,1:T(4,128)S(1)}, u32[]{:S(2)}, u32[]{:S(2)}) collective-permute-start(s32[8,4]{0,1:T(4,128)S(1)} %bitcast.50), channel_id=1, source_target_pairs={{0,96},{16,112},{32,0},{48,16},{64,32},{80,48},{96,64},{112,80},{1... | collective-permute-start | bytes 392 | tf_op jit(solution)/shard_map/ppermute | solution.py:283
  13.9 27.5 %all-to-all-start = ((bf16[16,64,768]{2,1,0:T(8,128)(2,1)}), bf16[16,64,768]{2,1,0:T(8,128)(2,1)S(1)}, u32[]{:S(2)}, u32[]{:S(2)}) async-start(bf16[16,64,768]{2,1,0:T(8,128)(2,1)} %arrange.2), calls=%async_computation | async-start | bytes 3145728 | tf_op jit(solution)/shard_map/all_to_all | solution.py:290
  23.0 2.7 %collective-permute-start.3 = (s32[4,8,4]{1,2,0:T(4,128)S(1)}, s32[4,8,4]{1,2,0:T(4,128)S(1)}, u32[]{:S(2)}, u32[]{:S(2)}) collective-permute-start(s32[4,8,4]{1,2,0:T(4,128)S(1)} %get-tuple-element.78), channel_id=1, source_target_pairs={{0,16},{16,0},{32,48},{48,32},{64,80},{80,64},{96,112},{112,96},{1... | collective-permute-start | bytes 1544 | tf_op jit(solution)/shard_map/ppermute | solution.py:283
  41.4 8.3 %copy-start.11 = (bf16[1024,256]{1,0:T(8,128)(2,1)}, bf16[1024,256]{1,0:T(8,128)(2,1)S(1)}, u32[]{:S(2)}) copy-start(bf16[1024,256]{1,0:T(8,128)(2,1)S(1)} %slice.19) | copy-start | bytes 1572868
  41.4 8.3 %collective-permute-start.4 = (bf16[1024,256]{1,0:T(8,128)(2,1)S(1)}, bf16[1024,256]{1,0:T(8,128)(2,1)}, u32[]{:S(2)}, u32[]{:S(2)}) collective-permute-start(bf16[1024,256]{1,0:T(8,128)(2,1)S(1)} %slice.19), channel_id=1, source_target_pairs={{0,16},{16,0},{32,48},{48,32},{64,80},{80,64},{96,112},{112,96},{1... | collective-permute-start | bytes 1572872 | tf_op jit(solution)/shard_map/ppermute | solution.py:283
  45.4 23.5 %all-to-all-start.1 = ((bf16[16,64,512]{2,1,0:T(8,128)(2,1)}), bf16[16,64,512]{2,1,0:T(8,128)(2,1)}, u32[]{:S(2)}, u32[]{:S(2)}) async-start(bf16[16,64,512]{2,1,0:T(8,128)(2,1)} %arrange.3), calls=%async_computation.1 | async-start | bytes 2097152 | tf_op jit(solution)/shard_map/all_to_all | solution.py:306
  52.0 16.8 %collective-permute-start.5 = (bf16[512,512]{1,0:T(8,128)(2,1)S(1)}, bf16[512,512]{1,0:T(8,128)(2,1)S(1)}, u32[]{:S(2)}, u32[]{:S(2)}) collective-permute-start(bf16[512,512]{1,0:T(8,128)(2,1)S(1)} %convolution_convert_fusion.1.refs_0_), channel_id=1, source_target_pairs={{0,32},{16,48},{32,64},{48,80},{64,96},{80,112},{96,0},{112,16},{1... | collective-permute-start | bytes 1572872 | tf_op jit(solution)/shard_map/ppermute | solution.py:283
  52.8 16.0 %collective-permute-start.6 = (bf16[512,512]{1,0:T(8,128)(2,1)S(1)}, bf16[512,512]{1,0:T(8,128)(2,1)S(1)}, u32[]{:S(2)}, u32[]{:S(2)}) collective-permute-start(bf16[512,512]{1,0:T(8,128)(2,1)S(1)} %convolution_convert_fusion.1.refs_0_), channel_id=1, source_target_pairs={{0,96},{16,112},{32,0},{48,16},{64,32},{80,48},{96,64},{112,80},{1... | collective-permute-start | bytes 1572872 | tf_op jit(solution)/shard_map/ppermute | solution.py:283
  54.8 21.9 %collective-permute-start.11 = (bf16[512,512]{1,0:T(8,128)(2,1)S(1)}, bf16[512,512]{1,0:T(8,128)(2,1)}, u32[]{:S(2)}, u32[]{:S(2)}) collective-permute-start(bf16[512,512]{1,0:T(8,128)(2,1)S(1)} %convolution_convert_fusion.1.refs_0_), channel_id=1, source_target_pairs={{0,16},{16,0},{32,48},{48,32},{64,80},{80,64},{96,112},{112,96},{1... | collective-permute-start | bytes 1572872 | tf_op jit(solution)/shard_map/ppermute | solution.py:283
  68.8 9.3 %copy-start.6 = (bf16[512,512]{1,0:T(8,128)(2,1)}, bf16[512,512]{1,0:T(8,128)(2,1)S(1)}, u32[]{:S(2)}) copy-start(bf16[512,512]{1,0:T(8,128)(2,1)S(1)} %collective-permute-done.6.refs_4_) | copy-start | bytes 1572868
  68.8 10.5 %copy-start.8 = (bf16[32,512]{1,0:T(8,128)(2,1)S(1)}, bf16[32,512]{1,0:T(8,128)(2,1)}, u32[]{:S(2)}) copy-start(bf16[32,512]{1,0:T(8,128)(2,1)} %maximum_maximum_fusion.refs_5_.refs_9_) | copy-start | bytes 98308
  71.6 6.5 %collective-permute-start.12 = (bf16[512,512]{1,0:T(8,128)(2,1)S(1)}, bf16[512,512]{1,0:T(8,128)(2,1)S(1)}, u32[]{:S(2)}, u32[]{:S(2)}) collective-permute-start(bf16[512,512]{1,0:T(8,128)(2,1)S(1)} %convolution_convert_fusion.refs_1_), channel_id=1, source_target_pairs={{0,16},{16,0},{32,48},{48,32},{64,80},{80,64},{96,112},{112,96},{1... | collective-permute-start | bytes 1572872 | tf_op jit(solution)/shard_map/ppermute | solution.py:283
  72.5 20.8 %collective-permute-start.7 = (bf16[512,512]{1,0:T(8,128)(2,1)S(1)}, bf16[512,512]{1,0:T(8,128)(2,1)}, u32[]{:S(2)}, u32[]{:S(2)}) collective-permute-start(bf16[512,512]{1,0:T(8,128)(2,1)S(1)} %convolution_convert_fusion.refs_1_), channel_id=1, source_target_pairs={{0,32},{16,48},{32,64},{48,80},{64,96},{80,112},{96,0},{112,16},{1... | collective-permute-start | bytes 1572872 | tf_op jit(solution)/shard_map/ppermute | solution.py:283
  73.3 20.1 %collective-permute-start.8 = (bf16[512,512]{1,0:T(8,128)(2,1)S(1)}, bf16[512,512]{1,0:T(8,128)(2,1)}, u32[]{:S(2)}, u32[]{:S(2)}) collective-permute-start(bf16[512,512]{1,0:T(8,128)(2,1)S(1)} %convolution_convert_fusion.refs_1_), channel_id=1, source_target_pairs={{0,96},{16,112},{32,0},{48,16},{64,32},{80,48},{96,64},{112,80},{1... | collective-permute-start | bytes 1572872 | tf_op jit(solution)/shard_map/ppermute | solution.py:283
  75.9 17.0 %collective-permute-start.10 = (bf16[256,512]{1,0:T(8,128)(2,1)}, bf16[256,512]{1,0:T(8,128)(2,1)}, u32[]{:S(2)}, u32[]{:S(2)}) collective-permute-start(bf16[256,512]{1,0:T(8,128)(2,1)} %slice.21), channel_id=1, source_target_pairs={{0,96},{16,112},{32,0},{48,16},{64,32},{80,48},{96,64},{112,80},{1... | collective-permute-start | bytes 786440 | tf_op jit(solution)/shard_map/ppermute | solution.py:283
  76.7 16.7 %collective-permute-start.9 = (bf16[256,512]{1,0:T(8,128)(2,1)}, bf16[256,512]{1,0:T(8,128)(2,1)}, u32[]{:S(2)}, u32[]{:S(2)}) collective-permute-start(bf16[256,512]{1,0:T(8,128)(2,1)} %slice.20), channel_id=1, source_target_pairs={{0,32},{16,48},{32,64},{48,80},{64,96},{80,112},{96,0},{112,16},{1... | collective-permute-start | bytes 786440 | tf_op jit(solution)/shard_map/ppermute | solution.py:283
  78.1 17.8 %collective-permute-start.15 = (bf16[512,512]{1,0:T(8,128)(2,1)S(1)}, bf16[512,512]{1,0:T(8,128)(2,1)}, u32[]{:S(2)}, u32[]{:S(2)}) collective-permute-start(bf16[512,512]{1,0:T(8,128)(2,1)S(1)} %collective-permute-done.5.refs_0_), channel_id=1, source_target_pairs={{0,16},{16,0},{32,48},{48,32},{64,80},{80,64},{96,112},{112,96},{1... | collective-permute-start | bytes 1572872 | tf_op jit(solution)/shard_map/ppermute | solution.py:283
  82.7 3.3 %copy-start = (bf16[32,2,128,512]{3,2,1,0:T(8,128)(2,1)}, bf16[32,2,128,512]{3,2,1,0:T(8,128)(2,1)S(1)}, u32[]{:S(2)}) copy-start(bf16[32,2,128,512]{3,2,1,0:T(8,128)(2,1)S(1)} %get-tuple-element.61.refs_10_) | copy-start | bytes 25165828
  86.0 13.7 %copy-start.9 = (bf16[32,512]{1,0:T(8,128)(2,1)S(1)}, bf16[32,512]{1,0:T(8,128)(2,1)}, u32[]{:S(2)}) copy-start(bf16[32,512]{1,0:T(8,128)(2,1)} %maximum_maximum_fusion.refs_5_.refs_9_) | copy-start | bytes 98308
  92.9 6.3 %collective-permute-start.17 = (bf16[512,512]{1,0:T(8,128)(2,1)}, bf16[512,512]{1,0:T(8,128)(2,1)S(1)}, u32[]{:S(2)}, u32[]{:S(2)}) collective-permute-start(bf16[512,512]{1,0:T(8,128)(2,1)} %copy-done.6), channel_id=1, source_target_pairs={{0,16},{16,0},{32,48},{48,32},{64,80},{80,64},{96,112},{112,96},{1... | collective-permute-start | bytes 1572872 | tf_op jit(solution)/shard_map/ppermute | solution.py:283
  93.3 6.2 %collective-permute-start.16 = (bf16[512,512]{1,0:T(8,128)(2,1)}, bf16[512,512]{1,0:T(8,128)(2,1)S(1)}, u32[]{:S(2)}, u32[]{:S(2)}) collective-permute-start(bf16[512,512]{1,0:T(8,128)(2,1)} %collective-permute-done.7.refs_1_), channel_id=1, source_target_pairs={{0,16},{16,0},{32,48},{48,32},{64,80},{80,64},{96,112},{112,96},{1... | collective-permute-start | bytes 1572872 | tf_op jit(solution)/shard_map/ppermute | solution.py:283
  93.8 5.9 %collective-permute-start.18 = (bf16[512,512]{1,0:T(8,128)(2,1)}, bf16[512,512]{1,0:T(8,128)(2,1)S(1)}, u32[]{:S(2)}, u32[]{:S(2)}) collective-permute-start(bf16[512,512]{1,0:T(8,128)(2,1)} %collective-permute-done.8.refs_5_), channel_id=1, source_target_pairs={{0,16},{16,0},{32,48},{48,32},{64,80},{80,64},{96,112},{112,96},{1... | collective-permute-start | bytes 1572872 | tf_op jit(solution)/shard_map/ppermute | solution.py:283
  95.9 14.4 %collective-permute-start.13 = (bf16[256,512]{1,0:T(8,128)(2,1)S(1)}, bf16[256,512]{1,0:T(8,128)(2,1)S(1)}, u32[]{:S(2)}, u32[]{:S(2)}) collective-permute-start(bf16[256,512]{1,0:T(8,128)(2,1)S(1)} %slice.22), channel_id=1, source_target_pairs={{0,32},{16,48},{32,64},{48,80},{64,96},{80,112},{96,0},{112,16},{1... | collective-permute-start | bytes 786440 | tf_op jit(solution)/shard_map/ppermute | solution.py:283
  96.0 14.3 %collective-permute-start.14 = (bf16[256,512]{1,0:T(8,128)(2,1)S(1)}, bf16[256,512]{1,0:T(8,128)(2,1)S(1)}, u32[]{:S(2)}, u32[]{:S(2)}) collective-permute-start(bf16[256,512]{1,0:T(8,128)(2,1)S(1)} %slice.23), channel_id=1, source_target_pairs={{0,96},{16,112},{32,0},{48,16},{64,32},{80,48},{96,64},{112,80},{1... | collective-permute-start | bytes 786440 | tf_op jit(solution)/shard_map/ppermute | solution.py:283
  99.2 11.8 %collective-permute-start.19 = (bf16[256,512]{1,0:T(8,128)(2,1)}, bf16[256,512]{1,0:T(8,128)(2,1)S(1)}, u32[]{:S(2)}, u32[]{:S(2)}) collective-permute-start(bf16[256,512]{1,0:T(8,128)(2,1)} %collective-permute-done.9.refs_0_), channel_id=1, source_target_pairs={{0,16},{16,0},{32,48},{48,32},{64,80},{80,64},{96,112},{112,96},{1... | collective-permute-start | bytes 786440 | tf_op jit(solution)/shard_map/ppermute | solution.py:283
  99.6 11.4 %collective-permute-start.20 = (bf16[256,512]{1,0:T(8,128)(2,1)}, bf16[256,512]{1,0:T(8,128)(2,1)S(1)}, u32[]{:S(2)}, u32[]{:S(2)}) collective-permute-start(bf16[256,512]{1,0:T(8,128)(2,1)} %collective-permute-done.10.refs_1_), channel_id=1, source_target_pairs={{0,16},{16,0},{32,48},{48,32},{64,80},{80,64},{96,112},{112,96},{1... | collective-permute-start | bytes 786440 | tf_op jit(solution)/shard_map/ppermute | solution.py:283
  99.7 3.4 %copy-start.1 = (bf16[32,2,128,512]{3,2,1,0:T(8,128)(2,1)S(1)}, bf16[32,2,128,512]{3,2,1,0:T(8,128)(2,1)}, u32[]{:S(2)}) copy-start(bf16[32,2,128,512]{3,2,1,0:T(8,128)(2,1)} %copy-done) | copy-start | bytes 25165828
  103.1 1.0 copy-start.7
  110.3 1.6 collective-permute-start.21
  110.6 1.7 collective-permute-start.22
  111.0 8.3 %copy-start.10 = (s32[8,12]{1,0:T(8,128)S(1)}, s32[8,12]{1,0:T(8,128)}, u32[]{:S(2)}) copy-start(s32[8,12]{1,0:T(8,128)} %rel_ref.1) | copy-start | bytes 1156
  112.3 7.0 %copy-start.4 = (bf16[8,12,128,128]{3,2,1,0:T(8,128)(2,1)S(1)}, bf16[8,12,128,128]{3,2,1,0:T(8,128)(2,1)}, u32[]{:S(2)}) copy-start(bf16[8,12,128,128]{3,2,1,0:T(8,128)(2,1)} %caps.1.cap_ref) | copy-start | bytes 9437188
  116.0 3.3 %copy-start.2 = (bf16[32,2,128,512]{3,2,1,0:T(8,128)(2,1)}, bf16[32,2,128,512]{3,2,1,0:T(8,128)(2,1)S(1)}, u32[]{:S(2)}) copy-start(bf16[32,2,128,512]{3,2,1,0:T(8,128)(2,1)S(1)} %get-tuple-element.69.val_ref) | copy-start | bytes 25165828
  119.3 3.4 %copy-start.3 = (bf16[32,2,128,512]{3,2,1,0:T(8,128)(2,1)S(1)}, bf16[32,2,128,512]{3,2,1,0:T(8,128)(2,1)}, u32[]{:S(2)}) copy-start(bf16[32,2,128,512]{3,2,1,0:T(8,128)(2,1)} %copy-done.2) | copy-start | bytes 25165828

commit v12 on v10

--- a/solution.py
+++ b/solution.py
@@ -286,10 +286,9 @@
     rows_a, half = cut * block_rows, width // 2
     features = node_features.T
     first = arrange(features, proj_weight, core, n_feat, 0, rows_a, half)
-    first, features = lax.optimization_barrier((first, features))
+    first, features, send_blocks = lax.optimization_barrier((first, features, send_blocks))
     got = lax.all_to_all(first, "feat", 0, 0, tiled=True).reshape(n_feat * depth, rows_a + half)
     outgoing = arrange(features, proj_weight, core, n_feat, rows_a, rows_local, 0)
-    outgoing, send_blocks = lax.optimization_barrier((outgoing, send_blocks))
 
     tables = jnp.stack([send_blocks[0]] + [send(send_blocks[0], d) for d in range(1, levels)])
     tables = jnp.stack([tables, send(tables, 0, 1)], axis=1)

time: 165 us -> 161 us (0.976)
  waiting for transfers between devices: 34.8 us -> 31 us
    all_to_all x1, waiting for transfers between devices: 9.44 us -> 5.83 us  [shards(): lax.all_to_all(first, 'feat', 0, 0, tiled=True)]
  transfers between devices with their start and end apart: 25 -> 25, of which waited for: 5 -> 5; matrix products, arithmetic and copies ran while one was open for 4% -> 5% of each run, Pallas kernels for 11% -> 13%
where the time goes in v12:
time: 161 us; the launch traced here: 160 us
  Pallas kernels  80.7 us (50%)
  starting transfers between devices  39.2 us (24%)
  waiting for transfers between devices  31 us (19%)
  matrix products  6.08 us (4%)
  local copies, waits for them, and re-layouts  2.03 us (1%)
    pallas_call x1, Pallas kernels, attend(): pl.pallas_call(attend_kernel, in_specs=[scalars] * 2 + [inside] * 5, out_...  52.3 us
    ppermute x23, starting transfers between devices, send(): return lax.ppermute(x, 'graph', pairs)  28.1 us
    pallas_call x3, Pallas kernels, transform(): pl.pallas_call(functools.partial(transform_kernel, bounds, first), in_spe...  14.3 us
    all_to_all x1, waiting for transfers between devices, shards(): lax.all_to_all(outgoing, 'feat', 0, 0, tiled=True)  13.3 us
    ppermute x23, waiting for transfers between devices, send(): return lax.ppermute(x, 'graph', pairs)  11.9 us
    pallas_call x2, Pallas kernels, arrange(): pl.pallas_call(functools.partial(arrange_kernel, low, high), grid_spec=pl...  7.26 us
    pallas_call x1, Pallas kernels, caps(): pl.pallas_call(cap_kernel, grid=shape[:1], in_specs=[spec], out_specs=spe...  6.9 us
    all_to_all x1, starting transfers between devices, shards(): lax.all_to_all(first, 'feat', 0, 0, tiled=True)  6.75 us
  transfers between devices with their start and end apart: 25, of which 5 were waited for; matrix products, arithmetic and copies ran while one was open for 5% of the time, Pallas kernels for 13%

profile of v12, /device:TPU:1, one launch (start us, length us, event | category | flops | bytes accessed | tf_op | source)
XLA Modules:
  0.0 160.0 jit_solution(12586307213063148590)
XLA Ops:
  0.0 3.7 %arrange.2 = bf16[16,64,768]{2,1,0:T(8,128)(2,1)} custom-call(s32[1]{0:T(128)} %bitcast.core_ref, bf16[64,16384]{1,0:T(8,128)(2,1)} %bitcast.41, bf16[64,512]{1,0:T(8,128)(2,1)} %w_ref.3), custom_call_target="tpu_custom_call" | custom-call | tf_op jit(solution)/shard_map/arrange/pallas_call | solution.py:31
  3.7 0.0 copy-start.8
  3.7 0.0 copy-start.6
  3.7 2.5 %collective-permute-start = (s32[8,4]{0,1:T(4,128)S(1)}, s32[8,4]{0,1:T(4,128)S(1)}, u32[]{:S(2)}, u32[]{:S(2)}) collective-permute-start(s32[8,4]{0,1:T(4,128)S(1)} %bitcast.48), channel_id=1, source_target_pairs={{0,32},{16,48},{32,64},{48,80},{64,96},{80,112},{96,0},{112,16},{1... | collective-permute-start | bytes 392 | tf_op jit(solution)/shard_map/ppermute | solution.py:283
  6.3 3.3 %collective-permute-start.1 = (s32[8,4]{0,1:T(4,128)S(1)}, s32[8,4]{0,1:T(4,128)S(1)}, u32[]{:S(2)}, u32[]{:S(2)}) collective-permute-start(s32[8,4]{0,1:T(4,128)S(1)} %bitcast.49), channel_id=1, source_target_pairs={{0,64},{16,80},{32,96},{48,112},{64,0},{80,16},{96,32},{112,48},{1... | collective-permute-start | bytes 392 | tf_op jit(solution)/shard_map/ppermute | solution.py:283
  9.6 0.7 collective-permute-start.2
  10.3 6.8 %all-to-all-start = ((bf16[16,64,768]{2,1,0:T(8,128)(2,1)}), bf16[16,64,768]{2,1,0:T(8,128)(2,1)S(1)}, u32[]{:S(2)}, u32[]{:S(2)}) async-start(bf16[16,64,768]{2,1,0:T(8,128)(2,1)} %arrange.2), calls=%async_computation | async-start | bytes 3145728 | tf_op jit(solution)/shard_map/all_to_all | solution.py:290
  17.1 0.1 copy.17
  17.3 0.9 fusion
  18.3 0.1 pad.24.clone
  18.4 0.1 maximum_maximum_fusion.refs_5_.refs_9_
  18.5 0.1 select_multiply_fusion
  18.6 0.1 fusion.6
  18.7 0.0 collective-permute-done
  18.7 0.0 collective-permute-done.1
  18.8 1.9 %collective-permute-start.3 = (s32[4,8,4]{1,2,0:T(4,128)S(1)}, s32[4,8,4]{1,2,0:T(4,128)S(1)}, u32[]{:S(2)}, u32[]{:S(2)}) collective-permute-start(s32[4,8,4]{1,2,0:T(4,128)S(1)} %get-tuple-element.70), channel_id=1, source_target_pairs={{0,16},{16,0},{32,48},{48,32},{64,80},{80,64},{96,112},{112,96},{1... | collective-permute-start | bytes 1544 | tf_op jit(solution)/shard_map/ppermute | solution.py:283
  20.7 3.6 %arrange.3 = bf16[16,64,512]{2,1,0:T(8,128)(2,1)} custom-call(s32[1]{0:T(128)} %bitcast.core_ref, bf16[64,16384]{1,0:T(8,128)(2,1)} %bitcast.42, bf16[64,512]{1,0:T(8,128)(2,1)} %w_ref.3), custom_call_target="tpu_custom_call" | custom-call | tf_op jit(solution)/shard_map/arrange/pallas_call | solution.py:31
  24.3 6.9 %caps.1.cap_ref = bf16[8,12,128,128]{3,2,1,0:T(8,128)(2,1)} custom-call(s32[8,12,128,128]{3,2,1,0:T(8,128)} %mask_ref.1), custom_call_target="tpu_custom_call" | custom-call | tf_op jit(solution)/shard_map/caps/pallas_call | solution.py:125
  31.2 0.1 copy.18
  31.3 0.0 collective-permute-done.3
  31.3 0.1 copy.19
  31.4 0.6 gather_fusion
  32.0 5.8 %all-to-all-done = bf16[16,64,768]{2,1,0:T(8,128)(2,1)S(1)} async-done(((bf16[16,64,768]{2,1,0:T(8,128)(2,1)}), bf16[16,64,768]{2,1,0:T(8,128)(2,1)S(1)}, u32[]{:S(2)}, u32[]{:S(2)}) %all-to-all-start) | async-done | bytes 1572896 | tf_op jit(solution)/shard_map/all_to_all | solution.py:290
  37.8 0.9 slice.19
  38.7 3.8 %collective-permute-start.4 = (bf16[1024,256]{1,0:T(8,128)(2,1)}, bf16[1024,256]{1,0:T(8,128)(2,1)}, u32[]{:S(2)}, u32[]{:S(2)}) collective-permute-start(bf16[1024,256]{1,0:T(8,128)(2,1)} %slice.19), channel_id=1, source_target_pairs={{0,16},{16,0},{32,48},{48,32},{64,80},{80,64},{96,112},{112,96},{1... | collective-permute-start | bytes 1572872 | tf_op jit(solution)/shard_map/ppermute | solution.py:283
  42.5 4.3 %all-to-all-start.1 = ((bf16[16,64,512]{2,1,0:T(8,128)(2,1)}), bf16[16,64,512]{2,1,0:T(8,128)(2,1)}, u32[]{:S(2)}, u32[]{:S(2)}) async-start(bf16[16,64,512]{2,1,0:T(8,128)(2,1)} %arrange.3), calls=%async_computation.1 | async-start | bytes 2097152 | tf_op jit(solution)/shard_map/all_to_all | solution.py:305
  46.9 0.0 collective-permute-done.4
  46.9 2.6 %convolution_convert_fusion.1.refs_0_ = bf16[512,512]{1,0:T(8,128)(2,1)S(1)} fusion(bf16[1024,768]{1,0:T(8,128)(2,1)} %bitcast.44, bf16[1024,256]{1,0:T(8,128)(2,1)} %collective-permute-done.4, bf16[1024,256]{1,0:T(8,128)(2,1)} %slice.19, pred[]{:T(512)S(6)} %eq.25), kind=kOutput, calls=%fused_computation.2 | convolution fusion | flops 541851648 | bytes 2621441 | tf_op jit(solution)/shard_map/dot_general | solution.py:312
  49.5 0.8 collective-permute-start.5
  50.3 1.9 %collective-permute-start.6 = (bf16[512,512]{1,0:T(8,128)(2,1)S(1)}, bf16[512,512]{1,0:T(8,128)(2,1)S(1)}, u32[]{:S(2)}, u32[]{:S(2)}) collective-permute-start(bf16[512,512]{1,0:T(8,128)(2,1)S(1)} %convolution_convert_fusion.1.refs_0_), channel_id=1, source_target_pairs={{0,96},{16,112},{32,0},{48,16},{64,32},{80,48},{96,64},{112,80},{1... | collective-permute-start | bytes 1572872 | tf_op jit(solution)/shard_map/ppermute | solution.py:283
  52.3 0.6 collective-permute-start.11
  52.8 13.3 %all-to-all-done.1 = bf16[16,64,512]{2,1,0:T(8,128)(2,1)} async-done(((bf16[16,64,512]{2,1,0:T(8,128)(2,1)}), bf16[16,64,512]{2,1,0:T(8,128)(2,1)}, u32[]{:S(2)}, u32[]{:S(2)}) %all-to-all-start.1) | async-done | bytes 1048608 | tf_op jit(solution)/shard_map/all_to_all | solution.py:305
  66.1 0.0 collective-permute-done.5.refs_0_
  66.1 0.0 collective-permute-done.6.refs_4_
  66.2 2.6 %convolution_convert_fusion.refs_1_ = bf16[512,512]{1,0:T(8,128)(2,1)S(1)} fusion(bf16[1024,512]{1,0:T(8,128)(2,1)} %bitcast.17, bf16[1024,256]{1,0:T(8,128)(2,1)} %collective-permute-done.4, bf16[1024,256]{1,0:T(8,128)(2,1)} %slice.19, pred[]{:T(512)S(6)} %eq.25), kind=kOutput, calls=%fused_computation.1 | convolution fusion | flops 541851648 | bytes 2621441 | tf_op jit(solution)/shard_map/dot_general | solution.py:312
  68.7 0.9 collective-permute-start.12
  69.6 0.8 collective-permute-start.7
  70.4 1.9 %collective-permute-start.8 = (bf16[512,512]{1,0:T(8,128)(2,1)S(1)}, bf16[512,512]{1,0:T(8,128)(2,1)S(1)}, u32[]{:S(2)}, u32[]{:S(2)}) collective-permute-start(bf16[512,512]{1,0:T(8,128)(2,1)S(1)} %convolution_convert_fusion.refs_1_), channel_id=1, source_target_pairs={{0,96},{16,112},{32,0},{48,16},{64,32},{80,48},{96,64},{112,80},{1... | collective-permute-start | bytes 1572872 | tf_op jit(solution)/shard_map/ppermute | solution.py:283
  72.3 0.1 collective-permute-start.10
  72.4 1.5 collective-permute-start.9
  73.9 0.0 collective-permute-done.12.refs_3_
  74.0 1.2 collective-permute-start.15
  75.1 3.5 %transform.3 = (bf16[32,2,128,512]{3,2,1,0:T(8,128)(2,1)S(1)}, f32[32,8,128]{2,1,0:T(8,128)S(1)}) custom-call(s32[8,4]{1,0:T(8,128)S(1)} %bitcast.38, bf16[512,512]{1,0:T(8,128)(2,1)S(1)} %convolution_convert_fusion.1.refs_0_, bf16[512,512]{1,0:T(8,128)(2,1)S(1)} %convolution_convert_fusion.refs_1_, bf16[512,512]{1,0:T(8,128)(2,1)} %collective-permute-done.11.refs_2_, ...), custom_call_target="tpu_custom_call" | custom-call | tf_op jit(solution)/shard_map/transform/pallas_call | solution.py:100
  78.6 10.5 %collective-permute-done.10.refs_1_ = bf16[256,512]{1,0:T(8,128)(2,1)S(1)} collective-permute-done((bf16[256,512]{1,0:T(8,128)(2,1)S(1)}, bf16[256,512]{1,0:T(8,128)(2,1)S(1)}, u32[]{:S(2)}, u32[]{:S(2)}) %collective-permute-start.10) | collective-permute-done | bytes 262176 | tf_op jit(solution)/shard_map/ppermute | solution.py:283
  89.1 1.2 collective-permute-start.17
  90.3 0.5 collective-permute-start.16
  90.8 0.1 collective-permute-start.18
  91.0 0.1 collective-permute-start.13
  91.0 0.0 collective-permute-done.15.refs_2_
  91.1 3.2 %collective-permute-start.14 = (bf16[256,512]{1,0:T(8,128)(2,1)S(1)}, bf16[256,512]{1,0:T(8,128)(2,1)S(1)}, u32[]{:S(2)}, u32[]{:S(2)}) collective-permute-start(bf16[256,512]{1,0:T(8,128)(2,1)S(1)} %slice.23), channel_id=1, source_target_pairs={{0,96},{16,112},{32,0},{48,16},{64,32},{80,48},{96,64},{112,80},{1... | collective-permute-start | bytes 786440 | tf_op jit(solution)/shard_map/ppermute | solution.py:283
  94.3 0.0 collective-permute-done.17.refs_6_
  94.3 0.4 collective-permute-start.19
  94.7 0.0 collective-permute-done.16.refs_3_
  94.7 0.1 collective-permute-start.20
  94.8 0.0 collective-permute-done.18.refs_7_
  94.8 7.0 %transform.4 = (bf16[32,2,128,512]{3,2,1,0:T(8,128)(2,1)S(1)}, f32[32,8,128]{2,1,0:T(8,128)S(1)}) custom-call(s32[8,4]{1,0:T(8,128)S(1)} %bitcast.39, bf16[512,512]{1,0:T(8,128)(2,1)S(1)} %collective-permute-done.5.refs_0_, bf16[512,512]{1,0:T(8,128)(2,1)S(1)} %collective-permute-done.7.refs_1_, ...), custom_call_target="tpu_custom_call", output_to_operand_aliasing={{0}: (11, {}), {1}: (12, {})} | custom-call | tf_op jit(solution)/shard_map/transform/pallas_call | solution.py:100
  101.9 0.4 collective-permute-start.21
  102.3 0.1 collective-permute-start.22
  102.4 0.1 pad_maximum_fusion
  102.5 0.0 copy-start.2
  102.5 0.9 collective-permute-done.21.refs_6_
  103.5 0.4 collective-permute-done.22.refs_7_
  103.8 3.8 %transform.5 = (bf16[32,2,128,512]{3,2,1,0:T(8,128)(2,1)S(1)}, f32[32,8,128]{2,1,0:T(8,128)S(1)}) custom-call(s32[8,4]{1,0:T(8,128)S(1)} %bitcast.40, bf16[256,512]{1,0:T(8,128)(2,1)S(1)} %collective-permute-done.9.refs_0_, bf16[256,512]{1,0:T(8,128)(2,1)S(1)} %collective-permute-done.10.refs_1_, ...), custom_call_target="tpu_custom_call", output_to_operand_aliasing={{0}: (11, {}), {1}: (12, {})} | custom-call | tf_op jit(solution)/shard_map/transform/pallas_call | solution.py:100
  107.7 52.3 %attend.1 = bf16[8,128,512]{2,1,0:T(8,128)(2,1)} custom-call(s32[8,12]{1,0:T(8,128)S(1)} %copy-done.2, s32[8,12]{1,0:T(8,128)S(1)} %fusion.15.slot_ref, bf16[8,128,512]{2,1,0:T(8,128)(2,1)S(1)} %bitcast.37, bf16[8,12,128,128]{3,2,1,0:T(8,128)(2,1)S(1)} %copy-done, bf16[3,512,128]{2,1,0:T(8,128)(2,1)S(1)} %pad_maximum_fusion.1.tgt_ref, ...), custom_call_target="tpu_custom_call" | custom-call | tf_op jit(solution)/shard_map/attend/pallas_call | solution.py:224
  (42 shorter events, 0.3 us)
Async XLA Ops:
  0.0 3.7 %copy-start.7 = (s32[1,8,4]{1,2,0:T(4,128)S(1)}, s32[1,8,4]{1,2,0:T(4,128)}, u32[]{:S(2)}) copy-start(s32[1,8,4]{1,2,0:T(4,128)} %param.17) | copy-start | bytes 388
  3.7 13.4 %copy-start.4 = (f32[2,512]{1,0:T(2,128)S(1)}, f32[2,512]{1,0:T(2,128)}, u32[]{:S(2)}) copy-start(f32[2,512]{1,0:T(2,128)} %param.14) | copy-start | bytes 12292
  3.7 13.6 %copy-start.5 = (f32[2,512]{1,0:T(2,128)S(1)}, f32[2,512]{1,0:T(2,128)}, u32[]{:S(2)}) copy-start(f32[2,512]{1,0:T(2,128)} %param.13) | copy-start | bytes 12292
  3.7 13.6 %copy-start.1 = (bf16[2,512,512]{2,1,0:T(8,128)(2,1)S(1)}, bf16[2,512,512]{2,1,0:T(8,128)(2,1)}, u32[]{:S(2)}) copy-start(bf16[2,512,512]{2,1,0:T(8,128)(2,1)} %refs_8_.3) | copy-start | bytes 3145732
  3.7 14.5 %copy-start.8 = (s32[4,1]{0,1:T(1,128)S(1)}, s32[4,1]{0,1:T(1,128)}, u32[]{:S(2)}) copy-start(s32[4,1]{0,1:T(1,128)} %constant.134) | copy-start | bytes 52
  3.7 14.7 %copy-start.6 = (s32[8,12]{1,0:T(8,128)S(1)}, s32[8,12]{1,0:T(8,128)}, u32[]{:S(2)}) copy-start(s32[8,12]{1,0:T(8,128)} %param.18) | copy-start | bytes 1156
  3.7 15.0 %collective-permute-start = (s32[8,4]{0,1:T(4,128)S(1)}, s32[8,4]{0,1:T(4,128)S(1)}, u32[]{:S(2)}, u32[]{:S(2)}) collective-permute-start(s32[8,4]{0,1:T(4,128)S(1)} %bitcast.48), channel_id=1, source_target_pairs={{0,32},{16,48},{32,64},{48,80},{64,96},{80,112},{96,0},{112,16},{1... | collective-permute-start | bytes 392 | tf_op jit(solution)/shard_map/ppermute | solution.py:283
  6.3 12.5 %collective-permute-start.1 = (s32[8,4]{0,1:T(4,128)S(1)}, s32[8,4]{0,1:T(4,128)S(1)}, u32[]{:S(2)}, u32[]{:S(2)}) collective-permute-start(s32[8,4]{0,1:T(4,128)S(1)} %bitcast.49), channel_id=1, source_target_pairs={{0,64},{16,80},{32,96},{48,112},{64,0},{80,16},{96,32},{112,48},{1... | collective-permute-start | bytes 392 | tf_op jit(solution)/shard_map/ppermute | solution.py:283
  9.6 9.2 %collective-permute-start.2 = (s32[8,4]{0,1:T(4,128)S(1)}, s32[8,4]{0,1:T(4,128)S(1)}, u32[]{:S(2)}, u32[]{:S(2)}) collective-permute-start(s32[8,4]{0,1:T(4,128)S(1)} %bitcast.50), channel_id=1, source_target_pairs={{0,96},{16,112},{32,0},{48,16},{64,32},{80,48},{96,64},{112,80},{1... | collective-permute-start | bytes 392 | tf_op jit(solution)/shard_map/ppermute | solution.py:283
  10.3 27.5 %all-to-all-start = ((bf16[16,64,768]{2,1,0:T(8,128)(2,1)}), bf16[16,64,768]{2,1,0:T(8,128)(2,1)S(1)}, u32[]{:S(2)}, u32[]{:S(2)}) async-start(bf16[16,64,768]{2,1,0:T(8,128)(2,1)} %arrange.2), calls=%async_computation | async-start | bytes 3145728 | tf_op jit(solution)/shard_map/all_to_all | solution.py:290
  18.8 12.5 %collective-permute-start.3 = (s32[4,8,4]{1,2,0:T(4,128)S(1)}, s32[4,8,4]{1,2,0:T(4,128)S(1)}, u32[]{:S(2)}, u32[]{:S(2)}) collective-permute-start(s32[4,8,4]{1,2,0:T(4,128)S(1)} %get-tuple-element.70), channel_id=1, source_target_pairs={{0,16},{16,0},{32,48},{48,32},{64,80},{80,64},{96,112},{112,96},{1... | collective-permute-start | bytes 1544 | tf_op jit(solution)/shard_map/ppermute | solution.py:283
  37.8 9.1 %copy-start.3 = (bf16[16,64,768]{2,1,0:T(8,128)(2,1)}, bf16[16,64,768]{2,1,0:T(8,128)(2,1)S(1)}, u32[]{:S(2)}) copy-start(bf16[16,64,768]{2,1,0:T(8,128)(2,1)S(1)} %all-to-all-done) | copy-start | bytes 4718596
  38.7 8.2 %collective-permute-start.4 = (bf16[1024,256]{1,0:T(8,128)(2,1)}, bf16[1024,256]{1,0:T(8,128)(2,1)}, u32[]{:S(2)}, u32[]{:S(2)}) collective-permute-start(bf16[1024,256]{1,0:T(8,128)(2,1)} %slice.19), channel_id=1, source_target_pairs={{0,16},{16,0},{32,48},{48,32},{64,80},{80,64},{96,112},{112,96},{1... | collective-permute-start | bytes 1572872 | tf_op jit(solution)/shard_map/ppermute | solution.py:283
  42.5 23.6 %all-to-all-start.1 = ((bf16[16,64,512]{2,1,0:T(8,128)(2,1)}), bf16[16,64,512]{2,1,0:T(8,128)(2,1)}, u32[]{:S(2)}, u32[]{:S(2)}) async-start(bf16[16,64,512]{2,1,0:T(8,128)(2,1)} %arrange.3), calls=%async_computation.1 | async-start | bytes 2097152 | tf_op jit(solution)/shard_map/all_to_all | solution.py:305
  49.5 16.6 %collective-permute-start.5 = (bf16[512,512]{1,0:T(8,128)(2,1)S(1)}, bf16[512,512]{1,0:T(8,128)(2,1)S(1)}, u32[]{:S(2)}, u32[]{:S(2)}) collective-permute-start(bf16[512,512]{1,0:T(8,128)(2,1)S(1)} %convolution_convert_fusion.1.refs_0_), channel_id=1, source_target_pairs={{0,32},{16,48},{32,64},{48,80},{64,96},{80,112},{96,0},{112,16},{1... | collective-permute-start | bytes 1572872 | tf_op jit(solution)/shard_map/ppermute | solution.py:283
  50.3 15.8 %collective-permute-start.6 = (bf16[512,512]{1,0:T(8,128)(2,1)S(1)}, bf16[512,512]{1,0:T(8,128)(2,1)S(1)}, u32[]{:S(2)}, u32[]{:S(2)}) collective-permute-start(bf16[512,512]{1,0:T(8,128)(2,1)S(1)} %convolution_convert_fusion.1.refs_0_), channel_id=1, source_target_pairs={{0,96},{16,112},{32,0},{48,16},{64,32},{80,48},{96,64},{112,80},{1... | collective-permute-start | bytes 1572872 | tf_op jit(solution)/shard_map/ppermute | solution.py:283
  52.3 20.2 %collective-permute-start.11 = (bf16[512,512]{1,0:T(8,128)(2,1)S(1)}, bf16[512,512]{1,0:T(8,128)(2,1)}, u32[]{:S(2)}, u32[]{:S(2)}) collective-permute-start(bf16[512,512]{1,0:T(8,128)(2,1)S(1)} %convolution_convert_fusion.1.refs_0_), channel_id=1, source_target_pairs={{0,16},{16,0},{32,48},{48,32},{64,80},{80,64},{96,112},{112,96},{1... | collective-permute-start | bytes 1572872 | tf_op jit(solution)/shard_map/ppermute | solution.py:283
  68.7 5.2 %collective-permute-start.12 = (bf16[512,512]{1,0:T(8,128)(2,1)S(1)}, bf16[512,512]{1,0:T(8,128)(2,1)S(1)}, u32[]{:S(2)}, u32[]{:S(2)}) collective-permute-start(bf16[512,512]{1,0:T(8,128)(2,1)S(1)} %convolution_convert_fusion.refs_1_), channel_id=1, source_target_pairs={{0,16},{16,0},{32,48},{48,32},{64,80},{80,64},{96,112},{112,96},{1... | collective-permute-start | bytes 1572872 | tf_op jit(solution)/shard_map/ppermute | solution.py:283
  69.6 20.7 %collective-permute-start.7 = (bf16[512,512]{1,0:T(8,128)(2,1)S(1)}, bf16[512,512]{1,0:T(8,128)(2,1)S(1)}, u32[]{:S(2)}, u32[]{:S(2)}) collective-permute-start(bf16[512,512]{1,0:T(8,128)(2,1)S(1)} %convolution_convert_fusion.refs_1_), channel_id=1, source_target_pairs={{0,32},{16,48},{32,64},{48,80},{64,96},{80,112},{96,0},{112,16},{1... | collective-permute-start | bytes 1572872 | tf_op jit(solution)/shard_map/ppermute | solution.py:283
  70.4 20.0 %collective-permute-start.8 = (bf16[512,512]{1,0:T(8,128)(2,1)S(1)}, bf16[512,512]{1,0:T(8,128)(2,1)S(1)}, u32[]{:S(2)}, u32[]{:S(2)}) collective-permute-start(bf16[512,512]{1,0:T(8,128)(2,1)S(1)} %convolution_convert_fusion.refs_1_), channel_id=1, source_target_pairs={{0,96},{16,112},{32,0},{48,16},{64,32},{80,48},{96,64},{112,80},{1... | collective-permute-start | bytes 1572872 | tf_op jit(solution)/shard_map/ppermute | solution.py:283
  72.3 16.8 %collective-permute-start.10 = (bf16[256,512]{1,0:T(8,128)(2,1)S(1)}, bf16[256,512]{1,0:T(8,128)(2,1)S(1)}, u32[]{:S(2)}, u32[]{:S(2)}) collective-permute-start(bf16[256,512]{1,0:T(8,128)(2,1)S(1)} %slice.21), channel_id=1, source_target_pairs={{0,96},{16,112},{32,0},{48,16},{64,32},{80,48},{96,64},{112,80},{1... | collective-permute-start | bytes 786440 | tf_op jit(solution)/shard_map/ppermute | solution.py:283
  72.4 17.9 %collective-permute-start.9 = (bf16[256,512]{1,0:T(8,128)(2,1)S(1)}, bf16[256,512]{1,0:T(8,128)(2,1)S(1)}, u32[]{:S(2)}, u32[]{:S(2)}) collective-permute-start(bf16[256,512]{1,0:T(8,128)(2,1)S(1)} %slice.20), channel_id=1, source_target_pairs={{0,32},{16,48},{32,64},{48,80},{64,96},{80,112},{96,0},{112,16},{1... | collective-permute-start | bytes 786440 | tf_op jit(solution)/shard_map/ppermute | solution.py:283
  74.0 17.1 %collective-permute-start.15 = (bf16[512,512]{1,0:T(8,128)(2,1)S(1)}, bf16[512,512]{1,0:T(8,128)(2,1)S(1)}, u32[]{:S(2)}, u32[]{:S(2)}) collective-permute-start(bf16[512,512]{1,0:T(8,128)(2,1)S(1)} %collective-permute-done.5.refs_0_), channel_id=1, source_target_pairs={{0,16},{16,0},{32,48},{48,32},{64,80},{80,64},{96,112},{112,96},{1... | collective-permute-start | bytes 1572872 | tf_op jit(solution)/shard_map/ppermute | solution.py:283
  89.1 5.2 %collective-permute-start.17 = (bf16[512,512]{1,0:T(8,128)(2,1)S(1)}, bf16[512,512]{1,0:T(8,128)(2,1)S(1)}, u32[]{:S(2)}, u32[]{:S(2)}) collective-permute-start(bf16[512,512]{1,0:T(8,128)(2,1)S(1)} %collective-permute-done.6.refs_4_), channel_id=1, source_target_pairs={{0,16},{16,0},{32,48},{48,32},{64,80},{80,64},{96,112},{112,96},{1... | collective-permute-start | bytes 1572872 | tf_op jit(solution)/shard_map/ppermute | solution.py:283
  90.3 4.3 %collective-permute-start.16 = (bf16[512,512]{1,0:T(8,128)(2,1)S(1)}, bf16[512,512]{1,0:T(8,128)(2,1)S(1)}, u32[]{:S(2)}, u32[]{:S(2)}) collective-permute-start(bf16[512,512]{1,0:T(8,128)(2,1)S(1)} %collective-permute-done.7.refs_1_), channel_id=1, source_target_pairs={{0,16},{16,0},{32,48},{48,32},{64,80},{80,64},{96,112},{112,96},{1... | collective-permute-start | bytes 1572872 | tf_op jit(solution)/shard_map/ppermute | solution.py:283
  90.8 4.0 %collective-permute-start.18 = (bf16[512,512]{1,0:T(8,128)(2,1)S(1)}, bf16[512,512]{1,0:T(8,128)(2,1)S(1)}, u32[]{:S(2)}, u32[]{:S(2)}) collective-permute-start(bf16[512,512]{1,0:T(8,128)(2,1)S(1)} %collective-permute-done.8.refs_5_), channel_id=1, source_target_pairs={{0,16},{16,0},{32,48},{48,32},{64,80},{80,64},{96,112},{112,96},{1... | collective-permute-start | bytes 1572872 | tf_op jit(solution)/shard_map/ppermute | solution.py:283
  91.0 10.9 %collective-permute-start.13 = (bf16[256,512]{1,0:T(8,128)(2,1)S(1)}, bf16[256,512]{1,0:T(8,128)(2,1)S(1)}, u32[]{:S(2)}, u32[]{:S(2)}) collective-permute-start(bf16[256,512]{1,0:T(8,128)(2,1)S(1)} %slice.22), channel_id=1, source_target_pairs={{0,32},{16,48},{32,64},{48,80},{64,96},{80,112},{96,0},{112,16},{1... | collective-permute-start | bytes 786440 | tf_op jit(solution)/shard_map/ppermute | solution.py:283
  91.1 10.8 %collective-permute-start.14 = (bf16[256,512]{1,0:T(8,128)(2,1)S(1)}, bf16[256,512]{1,0:T(8,128)(2,1)S(1)}, u32[]{:S(2)}, u32[]{:S(2)}) collective-permute-start(bf16[256,512]{1,0:T(8,128)(2,1)S(1)} %slice.23), channel_id=1, source_target_pairs={{0,96},{16,112},{32,0},{48,16},{64,32},{80,48},{96,64},{112,80},{1... | collective-permute-start | bytes 786440 | tf_op jit(solution)/shard_map/ppermute | solution.py:283
  94.3 8.2 %collective-permute-start.19 = (bf16[256,512]{1,0:T(8,128)(2,1)S(1)}, bf16[256,512]{1,0:T(8,128)(2,1)S(1)}, u32[]{:S(2)}, u32[]{:S(2)}) collective-permute-start(bf16[256,512]{1,0:T(8,128)(2,1)S(1)} %collective-permute-done.9.refs_0_), channel_id=1, source_target_pairs={{0,16},{16,0},{32,48},{48,32},{64,80},{80,64},{96,112},{112,96},{1... | collective-permute-start | bytes 786440 | tf_op jit(solution)/shard_map/ppermute | solution.py:283
  94.7 7.9 %collective-permute-start.20 = (bf16[256,512]{1,0:T(8,128)(2,1)S(1)}, bf16[256,512]{1,0:T(8,128)(2,1)S(1)}, u32[]{:S(2)}, u32[]{:S(2)}) collective-permute-start(bf16[256,512]{1,0:T(8,128)(2,1)S(1)} %collective-permute-done.10.refs_1_), channel_id=1, source_target_pairs={{0,16},{16,0},{32,48},{48,32},{64,80},{80,64},{96,112},{112,96},{1... | collective-permute-start | bytes 786440 | tf_op jit(solution)/shard_map/ppermute | solution.py:283
  101.9 1.6 %collective-permute-start.21 = (bf16[256,512]{1,0:T(8,128)(2,1)S(1)}, bf16[256,512]{1,0:T(8,128)(2,1)S(1)}, u32[]{:S(2)}, u32[]{:S(2)}) collective-permute-start(bf16[256,512]{1,0:T(8,128)(2,1)S(1)} %collective-permute-done.13.refs_2_), channel_id=1, source_target_pairs={{0,16},{16,0},{32,48},{48,32},{64,80},{80,64},{96,112},{112,96},{1... | collective-permute-start | bytes 786440 | tf_op jit(solution)/shard_map/ppermute | solution.py:283
  102.3 1.5 collective-permute-start.22
  102.5 5.1 %copy-start.2 = (s32[8,12]{1,0:T(8,128)S(1)}, s32[8,12]{1,0:T(8,128)}, u32[]{:S(2)}) copy-start(s32[8,12]{1,0:T(8,128)} %rel_ref.1) | copy-start | bytes 1156
  103.8 3.8 %copy-start = (bf16[8,12,128,128]{3,2,1,0:T(8,128)(2,1)S(1)}, bf16[8,12,128,128]{3,2,1,0:T(8,128)(2,1)}, u32[]{:S(2)}) copy-start(bf16[8,12,128,128]{3,2,1,0:T(8,128)(2,1)} %caps.1.cap_ref) | copy-start | bytes 9437188

commit v13 on v12

--- a/solution.py
+++ b/solution.py
@@ -282,7 +282,7 @@
         pairs = [(p, (p + 2 * up) % n_graph ^ cores) for p in range(n_graph)]
         return lax.ppermute(x, "graph", pairs)
 
-    cut = local_blocks // 2
+    cut = local_blocks // 2 + 1
     rows_a, half = cut * block_rows, width // 2
     features = node_features.T
     first = arrange(features, proj_weight, core, n_feat, 0, rows_a, half)
@@ -302,8 +302,6 @@
     got, outgoing, cap, src_vectors, tgt_vectors, slots, index = lax.optimization_barrier(
         (got, outgoing, caps(edge_mask), src_vectors, tgt_vectors, slots, index)
     )
-    later = lax.all_to_all(outgoing, "feat", 0, 0, tiled=True).reshape(n_feat * depth, rows_local - rows_a)
-
     mine = got[:, rows_a:]
     other = send(mine, 0, 1)
     whole = jnp.where(core == 0, jnp.concatenate([mine, other], axis=1), jnp.concatenate([other, mine], axis=1))
@@ -320,25 +318,30 @@
     def ring(part):
         return send(part, 1), send(part, -1)
 
-    def forward(up, down):
-        middle = up.shape[0] // 2
-        return send(up[:middle], 1), send(down[middle:], -1)
+    def forward(up, down, middle):
+        return send(up[: middle * block_rows], 1), send(down[middle * block_rows :], -1)
 
     a = project(got[:, :rows_a])
     up_a, down_a = ring(a)
+    swap_a = send(a, 0, 1)
+    outgoing, swap_a = lax.optimization_barrier((outgoing, swap_a))
+    later = lax.all_to_all(outgoing, "feat", 0, 0, tiled=True).reshape(n_feat * depth, rows_local - rows_a)
+    middle_a = (cut + 1) // 2
+    middle_b = local_blocks // 2 - middle_a
     later, up_a, down_a = lax.optimization_barrier((later, up_a, down_a))
-    far_a = forward(up_a, down_a)
+    far_a = forward(up_a, down_a, middle_a)
     b = project(later)
     up_b, down_b = ring(b)
-    done = spread(both([(a, 0, cut), (b, cut, local_blocks)]), 0, (None, None))
+    own = [[(a, 0, cut), (b, cut, local_blocks)], [(swap_a, 0, cut), (send(b, 0, 1), cut, local_blocks)]]
+    done = spread(own, 0, (None, None))
     up_b, down_b, far_a, done = lax.optimization_barrier((up_b, down_b, far_a, done))
-    far_b = forward(up_b, down_b)
+    far_b = forward(up_b, down_b, middle_b)
     done = spread(
         both([(up_a, 0, cut), (up_b, cut, local_blocks)]) + both([(down_a, 0, cut), (down_b, cut, local_blocks)]), 2, done
     )
     far_b, done = lax.optimization_barrier((far_b, done))
-    quarter = cut // 2
-    far = [(x, n * quarter, (n + 1) * quarter) for n, x in enumerate(far_a + far_b)]
+    ends = (0, middle_a, cut, cut + middle_b, local_blocks)
+    far = list(zip(far_a + far_b, ends[:-1], ends[1:]))
     values, scores = spread(both(far), 6, done)
     return attend(jnp.concatenate([a, b]), cap, relation_ids, slots, values, scores, tgt_vectors)
 

time: 161 us -> 172 us (1.068)
  waiting for transfers between devices: 31 us -> 40.4 us
  local copies, waits for them, and re-layouts: 2.03 us -> 3.88 us
    ppermute x23, waiting for transfers between devices: 11.9 us -> 31.3 us  [send(): return lax.ppermute(x, 'graph', pairs)]
    all_to_all x1, waiting for transfers between devices: 13.3 us -> 0.01 us  [shards(): lax.all_to_all(outgoing, 'feat', 0, 0, tiled=True)]
    all_to_all x1, waiting for transfers between devices: 5.83 us -> 9.1 us  [shards(): lax.all_to_all(first, 'feat', 0, 0, tiled=True)]
  transfers between devices with their start and end apart: 25 -> 25, of which waited for: 5 -> 8; matrix products, arithmetic and copies ran while one was open for 5% -> 1% of each run, Pallas kernels for 13% -> 12%
where the time goes in v13:
time: 172 us
  Pallas kernels  81.2 us (47%)
  waiting for transfers between devices  40.4 us (23%)
  starting transfers between devices  39.7 us (23%)
  matrix products  5.53 us (3%)
  local copies, waits for them, and re-layouts  3.88 us (2%)
    pallas_call x1, Pallas kernels, attend(): pl.pallas_call(attend_kernel, in_specs=[scalars] * 2 + [inside] * 5, out_...  52.5 us
    ppermute x23, waiting for transfers between devices, send(): return lax.ppermute(x, 'graph', pairs)  31.3 us
    ppermute x23, starting transfers between devices, send(): return lax.ppermute(x, 'graph', pairs)  28.6 us
    pallas_call x3, Pallas kernels, transform(): pl.pallas_call(functools.partial(transform_kernel, bounds, first), in_spe...  14.5 us
    all_to_all x1, waiting for transfers between devices, shards(): lax.all_to_all(first, 'feat', 0, 0, tiled=True)  9.1 us
    pallas_call x2, Pallas kernels, arrange(): pl.pallas_call(functools.partial(arrange_kernel, low, high), grid_spec=pl...  7.29 us
    pallas_call x1, Pallas kernels, caps(): pl.pallas_call(cap_kernel, grid=shape[:1], in_specs=[spec], out_specs=spe...  6.91 us
    all_to_all x1, starting transfers between devices, shards(): lax.all_to_all(first, 'feat', 0, 0, tiled=True)  6.8 us
  transfers between devices with their start and end apart: 25, of which 8 were waited for; matrix products, arithmetic and copies ran while one was open for 1% of the time, Pallas kernels for 12%

profile of v13, /device:TPU:1, one launch (start us, length us, event | category | flops | bytes accessed | tf_op | source)
XLA Modules:
  0.0 171.7 jit_solution(16217970588987582033)
XLA Ops:
  0.0 3.8 %arrange.2 = bf16[16,64,896]{2,1,0:T(8,128)(2,1)} custom-call(s32[1]{0:T(128)} %bitcast.core_ref, bf16[64,16384]{1,0:T(8,128)(2,1)} %bitcast.41, bf16[64,512]{1,0:T(8,128)(2,1)} %w_ref.3), custom_call_target="tpu_custom_call" | custom-call | tf_op jit(solution)/shard_map/arrange/pallas_call | solution.py:31
  3.8 0.0 copy-start.6
  3.8 0.0 copy-start.11
  3.8 0.0 copy-start.8
  3.8 2.5 %collective-permute-start = (s32[8,4]{0,1:T(4,128)S(1)}, s32[8,4]{0,1:T(4,128)S(1)}, u32[]{:S(2)}, u32[]{:S(2)}) collective-permute-start(s32[8,4]{0,1:T(4,128)S(1)} %bitcast.46), channel_id=1, source_target_pairs={{0,32},{16,48},{32,64},{48,80},{64,96},{80,112},{96,0},{112,16},{1... | collective-permute-start | bytes 392 | tf_op jit(solution)/shard_map/ppermute | solution.py:283
  6.3 3.3 %collective-permute-start.1 = (s32[8,4]{0,1:T(4,128)S(1)}, s32[8,4]{0,1:T(4,128)S(1)}, u32[]{:S(2)}, u32[]{:S(2)}) collective-permute-start(s32[8,4]{0,1:T(4,128)S(1)} %bitcast.47), channel_id=1, source_target_pairs={{0,64},{16,80},{32,96},{48,112},{64,0},{80,16},{96,32},{112,48},{1... | collective-permute-start | bytes 392 | tf_op jit(solution)/shard_map/ppermute | solution.py:283
  9.6 0.7 collective-permute-start.2
  10.4 6.8 %all-to-all-start = ((bf16[16,64,896]{2,1,0:T(8,128)(2,1)}), bf16[16,64,896]{2,1,0:T(8,128)(2,1)}, u32[]{:S(2)}, u32[]{:S(2)}) async-start(bf16[16,64,896]{2,1,0:T(8,128)(2,1)} %arrange.2), calls=%async_computation | async-start | bytes 3670016 | tf_op jit(solution)/shard_map/all_to_all | solution.py:290
  17.2 0.9 fusion.1
  18.2 0.1 copy.17
  18.4 0.1 pad.24.clone
  18.5 0.1 maximum_maximum_fusion.refs_5_.refs_9_
  18.6 0.1 select_multiply_fusion
  18.7 0.1 fusion.6
  18.8 0.0 collective-permute-done
  18.8 0.0 collective-permute-done.1
  18.9 1.9 %collective-permute-start.3 = (s32[4,8,4]{1,2,0:T(4,128)S(1)}, s32[4,8,4]{1,2,0:T(4,128)S(1)}, u32[]{:S(2)}, u32[]{:S(2)}) collective-permute-start(s32[4,8,4]{1,2,0:T(4,128)S(1)} %get-tuple-element.74), channel_id=1, source_target_pairs={{0,16},{16,0},{32,48},{48,32},{64,80},{80,64},{96,112},{112,96},{1... | collective-permute-start | bytes 1544 | tf_op jit(solution)/shard_map/ppermute | solution.py:283
  20.8 3.5 %arrange.3 = bf16[16,64,384]{2,1,0:T(8,128)(2,1)} custom-call(s32[1]{0:T(128)} %bitcast.core_ref, bf16[64,16384]{1,0:T(8,128)(2,1)} %bitcast.42, bf16[64,512]{1,0:T(8,128)(2,1)} %w_ref.3), custom_call_target="tpu_custom_call" | custom-call | tf_op jit(solution)/shard_map/arrange/pallas_call | solution.py:31
  24.3 6.9 %caps.1.cap_ref = bf16[8,12,128,128]{3,2,1,0:T(8,128)(2,1)} custom-call(s32[8,12,128,128]{3,2,1,0:T(8,128)} %mask_ref.1), custom_call_target="tpu_custom_call" | custom-call | tf_op jit(solution)/shard_map/caps/pallas_call | solution.py:125
  31.2 0.1 copy.18
  31.3 0.0 collective-permute-done.3
  31.3 0.1 copy.19
  31.5 0.6 gather_fusion
  32.0 9.1 %all-to-all-done = bf16[16,64,896]{2,1,0:T(8,128)(2,1)} async-done(((bf16[16,64,896]{2,1,0:T(8,128)(2,1)}), bf16[16,64,896]{2,1,0:T(8,128)(2,1)}, u32[]{:S(2)}, u32[]{:S(2)}) %all-to-all-start) | async-done | bytes 1835040 | tf_op jit(solution)/shard_map/all_to_all | solution.py:290
  41.1 1.1 slice.19
  42.2 4.5 %collective-permute-start.4 = (bf16[1024,256]{1,0:T(8,128)(2,1)S(1)}, bf16[1024,256]{1,0:T(8,128)(2,1)S(1)}, u32[]{:S(2)}, u32[]{:S(2)}) collective-permute-start(bf16[1024,256]{1,0:T(8,128)(2,1)S(1)} %slice.19), channel_id=1, source_target_pairs={{0,16},{16,0},{32,48},{48,32},{64,80},{80,64},{96,112},{112,96},{1... | collective-permute-start | bytes 1572872 | tf_op jit(solution)/shard_map/ppermute | solution.py:283
  46.7 1.5 collective-permute-done.4
  48.3 0.8 copy-done.10
  49.1 2.2 %convolution_convert_fusion.refs_0_ = bf16[640,512]{1,0:T(8,128)(2,1)S(1)} fusion(bf16[1024,896]{1,0:T(8,128)(2,1)} %bitcast.2, bf16[1024,256]{1,0:T(8,128)(2,1)S(1)} %collective-permute-done.4, bf16[1024,256]{1,0:T(8,128)(2,1)S(1)} %slice.19, pred[]{:T(512)S(6)} %eq.25), kind=kOutput, calls=%fused_computation.1 | convolution fusion | flops 676134912 | bytes 3014657 | tf_op jit(solution)/shard_map/dot_general | solution.py:310
  51.3 0.5 collective-permute-start.5
  51.8 1.7 %collective-permute-done.5.refs_2_ = bf16[640,512]{1,0:T(8,128)(2,1)S(1)} collective-permute-done((bf16[640,512]{1,0:T(8,128)(2,1)S(1)}, bf16[640,512]{1,0:T(8,128)(2,1)S(1)}, u32[]{:S(2)}, u32[]{:S(2)}) %collective-permute-start.5) | collective-permute-done | bytes 655392 | tf_op jit(solution)/shard_map/ppermute | solution.py:283
  53.5 0.9 copy-done.2
  54.3 4.3 %all-to-all-start.1 = ((bf16[16,64,384]{2,1,0:T(8,128)(2,1)}), bf16[16,64,384]{2,1,0:T(8,128)(2,1)}, u32[]{:S(2)}, u32[]{:S(2)}) async-start(bf16[16,64,384]{2,1,0:T(8,128)(2,1)} %arrange.3), calls=%async_computation.1 | async-start | bytes 1572864 | tf_op jit(solution)/shard_map/all_to_all | solution.py:328
  58.6 0.8 collective-permute-start.6
  59.4 1.9 %collective-permute-start.7 = (bf16[640,512]{1,0:T(8,128)(2,1)S(1)}, bf16[640,512]{1,0:T(8,128)(2,1)S(1)}, u32[]{:S(2)}, u32[]{:S(2)}) collective-permute-start(bf16[640,512]{1,0:T(8,128)(2,1)S(1)} %convolution_convert_fusion.refs_0_), channel_id=1, source_target_pairs={{0,96},{16,112},{32,0},{48,16},{64,32},{80,48},{96,64},{112,80},{1... | collective-permute-start | bytes 1966088 | tf_op jit(solution)/shard_map/ppermute | solution.py:283
  61.4 14.5 %collective-permute-done.6.refs_0_ = bf16[640,512]{1,0:T(8,128)(2,1)S(1)} collective-permute-done((bf16[640,512]{1,0:T(8,128)(2,1)S(1)}, bf16[640,512]{1,0:T(8,128)(2,1)S(1)}, u32[]{:S(2)}, u32[]{:S(2)}) %collective-permute-start.6) | collective-permute-done | bytes 655392 | tf_op jit(solution)/shard_map/ppermute | solution.py:283
  75.9 2.4 %convolution_convert_fusion.1.refs_1_ = bf16[384,512]{1,0:T(8,128)(2,1)S(1)} fusion(bf16[1024,384]{1,0:T(8,128)(2,1)} %bitcast.17, bf16[1024,256]{1,0:T(8,128)(2,1)} %copy-done.10, bf16[1024,256]{1,0:T(8,128)(2,1)} %copy-done.5, pred[]{:T(512)S(6)} %eq.25), kind=kOutput, calls=%fused_computation.3 | convolution fusion | flops 407568384 | bytes 2228225 | tf_op jit(solution)/shard_map/dot_general | solution.py:310
  78.3 1.3 collective-permute-start.12
  79.6 2.7 %collective-permute-start.11 = (bf16[256,512]{1,0:T(8,128)(2,1)S(1)}, bf16[256,512]{1,0:T(8,128)(2,1)S(1)}, u32[]{:S(2)}, u32[]{:S(2)}) collective-permute-start(bf16[256,512]{1,0:T(8,128)(2,1)S(1)} %slice.21), channel_id=1, source_target_pairs={{0,96},{16,112},{32,0},{48,16},{64,32},{80,48},{96,64},{112,80},{1... | collective-permute-start | bytes 786440 | tf_op jit(solution)/shard_map/ppermute | solution.py:283
  82.4 0.1 collective-permute-start.10
  82.5 0.1 collective-permute-start.8
  82.5 2.7 %collective-permute-start.9 = (bf16[384,512]{1,0:T(8,128)(2,1)S(1)}, bf16[384,512]{1,0:T(8,128)(2,1)S(1)}, u32[]{:S(2)}, u32[]{:S(2)}) collective-permute-start(bf16[384,512]{1,0:T(8,128)(2,1)S(1)} %convolution_convert_fusion.1.refs_1_), channel_id=1, source_target_pairs={{0,96},{16,112},{32,0},{48,16},{64,32},{80,48},{96,64},{112,80},{1... | collective-permute-start | bytes 1179656 | tf_op jit(solution)/shard_map/ppermute | solution.py:283
  85.2 2.9 %collective-permute-done.11.refs_1_ = bf16[256,512]{1,0:T(8,128)(2,1)S(1)} collective-permute-done((bf16[256,512]{1,0:T(8,128)(2,1)S(1)}, bf16[256,512]{1,0:T(8,128)(2,1)S(1)}, u32[]{:S(2)}, u32[]{:S(2)}) %collective-permute-start.11) | collective-permute-done | bytes 262176 | tf_op jit(solution)/shard_map/ppermute | solution.py:283
  88.1 1.2 collective-permute-start.15
  89.3 0.0 collective-permute-start.17
  89.3 3.7 %transform.3 = (bf16[32,2,128,512]{3,2,1,0:T(8,128)(2,1)S(1)}, f32[32,8,128]{2,1,0:T(8,128)S(1)}) custom-call(s32[8,4]{1,0:T(8,128)S(1)} %bitcast.38, bf16[640,512]{1,0:T(8,128)(2,1)S(1)} %convolution_convert_fusion.refs_0_, bf16[384,512]{1,0:T(8,128)(2,1)S(1)} %convolution_convert_fusion.1.refs_1_, bf16[640,512]{1,0:T(8,128)(2,1)S(1)} %copy-done.3, ...), custom_call_target="tpu_custom_call" | custom-call | tf_op jit(solution)/shard_map/transform/pallas_call | solution.py:100
  93.0 1.1 collective-permute-done.10.refs_0_
  94.1 8.4 %collective-permute-done.8.refs_1_ = bf16[384,512]{1,0:T(8,128)(2,1)S(1)} collective-permute-done((bf16[384,512]{1,0:T(8,128)(2,1)S(1)}, bf16[384,512]{1,0:T(8,128)(2,1)S(1)}, u32[]{:S(2)}, u32[]{:S(2)}) %collective-permute-start.8) | collective-permute-done | bytes 393248 | tf_op jit(solution)/shard_map/ppermute | solution.py:283
  102.5 0.0 collective-permute-done.9.refs_5_
  102.5 1.1 collective-permute-start.16
  103.6 0.0 collective-permute-start.18
  103.6 0.1 collective-permute-start.14
  103.7 0.0 collective-permute-done.15.refs_2_
  103.7 1.5 collective-permute-start.13
  105.3 1.1 collective-permute-start.19
  106.3 0.1 collective-permute-start.20
  106.4 7.0 %transform.4 = (bf16[32,2,128,512]{3,2,1,0:T(8,128)(2,1)S(1)}, f32[32,8,128]{2,1,0:T(8,128)S(1)}) custom-call(s32[8,4]{1,0:T(8,128)S(1)} %bitcast.39, bf16[640,512]{1,0:T(8,128)(2,1)S(1)} %collective-permute-done.6.refs_0_, bf16[384,512]{1,0:T(8,128)(2,1)S(1)} %collective-permute-done.8.refs_1_, ...), custom_call_target="tpu_custom_call", output_to_operand_aliasing={{0}: (11, {}), {1}: (12, {})} | custom-call | tf_op jit(solution)/shard_map/transform/pallas_call | solution.py:100
  113.5 0.5 collective-permute-start.22
  114.0 0.1 collective-permute-start.21
  114.1 0.1 pad_maximum_fusion
  114.1 0.0 copy-start.4
  114.2 1.2 collective-permute-done.21.refs_6_
  115.3 3.8 %transform.5 = (bf16[32,2,128,512]{3,2,1,0:T(8,128)(2,1)S(1)}, f32[32,8,128]{2,1,0:T(8,128)S(1)}) custom-call(s32[8,4]{1,0:T(8,128)S(1)} %bitcast.40, bf16[384,512]{1,0:T(8,128)(2,1)S(1)} %collective-permute-done.10.refs_0_, bf16[256,512]{1,0:T(8,128)(2,1)S(1)} %collective-permute-done.11.refs_1_, ...), custom_call_target="tpu_custom_call", output_to_operand_aliasing={{0}: (11, {}), {1}: (12, {})} | custom-call | tf_op jit(solution)/shard_map/transform/pallas_call | solution.py:100
  119.2 52.5 %attend.1 = bf16[8,128,512]{2,1,0:T(8,128)(2,1)} custom-call(s32[8,12]{1,0:T(8,128)S(1)} %copy-done.4, s32[8,12]{1,0:T(8,128)S(1)} %fusion.15.slot_ref, bf16[8,128,512]{2,1,0:T(8,128)(2,1)S(1)} %bitcast.37, bf16[8,12,128,128]{3,2,1,0:T(8,128)(2,1)S(1)} %copy-done, bf16[3,512,128]{2,1,0:T(8,128)(2,1)S(1)} %pad_maximum_fusion.1.tgt_ref, ...), custom_call_target="tpu_custom_call" | custom-call | tf_op jit(solution)/shard_map/attend/pallas_call | solution.py:224
  (48 shorter events, 0.3 us)
Async XLA Ops:
  0.0 3.8 %copy-start.9 = (s32[1,8,4]{1,2,0:T(4,128)S(1)}, s32[1,8,4]{1,2,0:T(4,128)}, u32[]{:S(2)}) copy-start(s32[1,8,4]{1,2,0:T(4,128)} %param.17) | copy-start | bytes 388
  3.8 13.4 %copy-start.7 = (f32[2,512]{1,0:T(2,128)S(1)}, f32[2,512]{1,0:T(2,128)}, u32[]{:S(2)}) copy-start(f32[2,512]{1,0:T(2,128)} %param.13) | copy-start | bytes 12292
  3.8 13.4 %copy-start.1 = (bf16[2,512,512]{2,1,0:T(8,128)(2,1)S(1)}, bf16[2,512,512]{2,1,0:T(8,128)(2,1)}, u32[]{:S(2)}) copy-start(bf16[2,512,512]{2,1,0:T(8,128)(2,1)} %refs_8_.3) | copy-start | bytes 3145732
  3.8 14.4 %copy-start.6 = (f32[2,512]{1,0:T(2,128)S(1)}, f32[2,512]{1,0:T(2,128)}, u32[]{:S(2)}) copy-start(f32[2,512]{1,0:T(2,128)} %param.14) | copy-start | bytes 12292
  3.8 14.7 %copy-start.11 = (s32[4,1]{0,1:T(1,128)S(1)}, s32[4,1]{0,1:T(1,128)}, u32[]{:S(2)}) copy-start(s32[4,1]{0,1:T(1,128)} %constant.134) | copy-start | bytes 52
  3.8 14.7 %copy-start.8 = (s32[8,12]{1,0:T(8,128)S(1)}, s32[8,12]{1,0:T(8,128)}, u32[]{:S(2)}) copy-start(s32[8,12]{1,0:T(8,128)} %param.18) | copy-start | bytes 1156
  3.8 15.0 %collective-permute-start = (s32[8,4]{0,1:T(4,128)S(1)}, s32[8,4]{0,1:T(4,128)S(1)}, u32[]{:S(2)}, u32[]{:S(2)}) collective-permute-start(s32[8,4]{0,1:T(4,128)S(1)} %bitcast.46), channel_id=1, source_target_pairs={{0,32},{16,48},{32,64},{48,80},{64,96},{80,112},{96,0},{112,16},{1... | collective-permute-start | bytes 392 | tf_op jit(solution)/shard_map/ppermute | solution.py:283
  6.3 12.5 %collective-permute-start.1 = (s32[8,4]{0,1:T(4,128)S(1)}, s32[8,4]{0,1:T(4,128)S(1)}, u32[]{:S(2)}, u32[]{:S(2)}) collective-permute-start(s32[8,4]{0,1:T(4,128)S(1)} %bitcast.47), channel_id=1, source_target_pairs={{0,64},{16,80},{32,96},{48,112},{64,0},{80,16},{96,32},{112,48},{1... | collective-permute-start | bytes 392 | tf_op jit(solution)/shard_map/ppermute | solution.py:283
  9.6 9.2 %collective-permute-start.2 = (s32[8,4]{0,1:T(4,128)S(1)}, s32[8,4]{0,1:T(4,128)S(1)}, u32[]{:S(2)}, u32[]{:S(2)}) collective-permute-start(s32[8,4]{0,1:T(4,128)S(1)} %bitcast.48), channel_id=1, source_target_pairs={{0,96},{16,112},{32,0},{48,16},{64,32},{80,48},{96,64},{112,80},{1... | collective-permute-start | bytes 392 | tf_op jit(solution)/shard_map/ppermute | solution.py:283
  10.4 30.8 %all-to-all-start = ((bf16[16,64,896]{2,1,0:T(8,128)(2,1)}), bf16[16,64,896]{2,1,0:T(8,128)(2,1)}, u32[]{:S(2)}, u32[]{:S(2)}) async-start(bf16[16,64,896]{2,1,0:T(8,128)(2,1)} %arrange.2), calls=%async_computation | async-start | bytes 3670016 | tf_op jit(solution)/shard_map/all_to_all | solution.py:290
  18.9 12.5 %collective-permute-start.3 = (s32[4,8,4]{1,2,0:T(4,128)S(1)}, s32[4,8,4]{1,2,0:T(4,128)S(1)}, u32[]{:S(2)}, u32[]{:S(2)}) collective-permute-start(s32[4,8,4]{1,2,0:T(4,128)S(1)} %get-tuple-element.74), channel_id=1, source_target_pairs={{0,16},{16,0},{32,48},{48,32},{64,80},{80,64},{96,112},{112,96},{1... | collective-permute-start | bytes 1544 | tf_op jit(solution)/shard_map/ppermute | solution.py:283
  42.2 6.1 %copy-start.5 = (bf16[1024,256]{1,0:T(8,128)(2,1)}, bf16[1024,256]{1,0:T(8,128)(2,1)S(1)}, u32[]{:S(2)}) copy-start(bf16[1024,256]{1,0:T(8,128)(2,1)S(1)} %slice.19) | copy-start | bytes 1572868
  42.2 6.0 %collective-permute-start.4 = (bf16[1024,256]{1,0:T(8,128)(2,1)S(1)}, bf16[1024,256]{1,0:T(8,128)(2,1)S(1)}, u32[]{:S(2)}, u32[]{:S(2)}) collective-permute-start(bf16[1024,256]{1,0:T(8,128)(2,1)S(1)} %slice.19), channel_id=1, source_target_pairs={{0,16},{16,0},{32,48},{48,32},{64,80},{80,64},{96,112},{112,96},{1... | collective-permute-start | bytes 1572872 | tf_op jit(solution)/shard_map/ppermute | solution.py:283
  48.3 0.8 copy-start.10
  51.3 2.2 %collective-permute-start.5 = (bf16[640,512]{1,0:T(8,128)(2,1)S(1)}, bf16[640,512]{1,0:T(8,128)(2,1)S(1)}, u32[]{:S(2)}, u32[]{:S(2)}) collective-permute-start(bf16[640,512]{1,0:T(8,128)(2,1)S(1)} %convolution_convert_fusion.refs_0_), channel_id=1, source_target_pairs={{0,16},{16,0},{32,48},{48,32},{64,80},{80,64},{96,112},{112,96},{1... | collective-permute-start | bytes 1966088 | tf_op jit(solution)/shard_map/ppermute | solution.py:283
  53.5 0.9 copy-start.2
  54.3 21.5 %all-to-all-start.1 = ((bf16[16,64,384]{2,1,0:T(8,128)(2,1)}), bf16[16,64,384]{2,1,0:T(8,128)(2,1)}, u32[]{:S(2)}, u32[]{:S(2)}) async-start(bf16[16,64,384]{2,1,0:T(8,128)(2,1)} %arrange.3), calls=%async_computation.1 | async-start | bytes 1572864 | tf_op jit(solution)/shard_map/all_to_all | solution.py:328
  58.6 17.2 %collective-permute-start.6 = (bf16[640,512]{1,0:T(8,128)(2,1)S(1)}, bf16[640,512]{1,0:T(8,128)(2,1)S(1)}, u32[]{:S(2)}, u32[]{:S(2)}) collective-permute-start(bf16[640,512]{1,0:T(8,128)(2,1)S(1)} %convolution_convert_fusion.refs_0_), channel_id=1, source_target_pairs={{0,32},{16,48},{32,64},{48,80},{64,96},{80,112},{96,0},{112,16},{1... | collective-permute-start | bytes 1966088 | tf_op jit(solution)/shard_map/ppermute | solution.py:283
  59.4 16.4 %collective-permute-start.7 = (bf16[640,512]{1,0:T(8,128)(2,1)S(1)}, bf16[640,512]{1,0:T(8,128)(2,1)S(1)}, u32[]{:S(2)}, u32[]{:S(2)}) collective-permute-start(bf16[640,512]{1,0:T(8,128)(2,1)S(1)} %convolution_convert_fusion.refs_0_), channel_id=1, source_target_pairs={{0,96},{16,112},{32,0},{48,16},{64,32},{80,48},{96,64},{112,80},{1... | collective-permute-start | bytes 1966088 | tf_op jit(solution)/shard_map/ppermute | solution.py:283
  75.9 13.4 %copy-start.3 = (bf16[640,512]{1,0:T(8,128)(2,1)S(1)}, bf16[640,512]{1,0:T(8,128)(2,1)}, u32[]{:S(2)}) copy-start(bf16[640,512]{1,0:T(8,128)(2,1)} %copy-done.2) | copy-start | bytes 1966084
  78.3 11.0 %collective-permute-start.12 = (bf16[384,512]{1,0:T(8,128)(2,1)S(1)}, bf16[384,512]{1,0:T(8,128)(2,1)S(1)}, u32[]{:S(2)}, u32[]{:S(2)}) collective-permute-start(bf16[384,512]{1,0:T(8,128)(2,1)S(1)} %convolution_convert_fusion.1.refs_1_), channel_id=1, source_target_pairs={{0,16},{16,0},{32,48},{48,32},{64,80},{80,64},{96,112},{112,96},{1... | collective-permute-start | bytes 1179656 | tf_op jit(solution)/shard_map/ppermute | solution.py:283
  79.6 8.5 %collective-permute-start.11 = (bf16[256,512]{1,0:T(8,128)(2,1)S(1)}, bf16[256,512]{1,0:T(8,128)(2,1)S(1)}, u32[]{:S(2)}, u32[]{:S(2)}) collective-permute-start(bf16[256,512]{1,0:T(8,128)(2,1)S(1)} %slice.21), channel_id=1, source_target_pairs={{0,96},{16,112},{32,0},{48,16},{64,32},{80,48},{96,64},{112,80},{1... | collective-permute-start | bytes 786440 | tf_op jit(solution)/shard_map/ppermute | solution.py:283
  82.4 11.7 %collective-permute-start.10 = (bf16[384,512]{1,0:T(8,128)(2,1)S(1)}, bf16[384,512]{1,0:T(8,128)(2,1)S(1)}, u32[]{:S(2)}, u32[]{:S(2)}) collective-permute-start(bf16[384,512]{1,0:T(8,128)(2,1)S(1)} %slice.20), channel_id=1, source_target_pairs={{0,32},{16,48},{32,64},{48,80},{64,96},{80,112},{96,0},{112,16},{1... | collective-permute-start | bytes 1179656 | tf_op jit(solution)/shard_map/ppermute | solution.py:283
  82.5 20.0 %collective-permute-start.8 = (bf16[384,512]{1,0:T(8,128)(2,1)S(1)}, bf16[384,512]{1,0:T(8,128)(2,1)S(1)}, u32[]{:S(2)}, u32[]{:S(2)}) collective-permute-start(bf16[384,512]{1,0:T(8,128)(2,1)S(1)} %convolution_convert_fusion.1.refs_1_), channel_id=1, source_target_pairs={{0,32},{16,48},{32,64},{48,80},{64,96},{80,112},{96,0},{112,16},{1... | collective-permute-start | bytes 1179656 | tf_op jit(solution)/shard_map/ppermute | solution.py:283
  82.5 20.0 %collective-permute-start.9 = (bf16[384,512]{1,0:T(8,128)(2,1)S(1)}, bf16[384,512]{1,0:T(8,128)(2,1)S(1)}, u32[]{:S(2)}, u32[]{:S(2)}) collective-permute-start(bf16[384,512]{1,0:T(8,128)(2,1)S(1)} %convolution_convert_fusion.1.refs_1_), channel_id=1, source_target_pairs={{0,96},{16,112},{32,0},{48,16},{64,32},{80,48},{96,64},{112,80},{1... | collective-permute-start | bytes 1179656 | tf_op jit(solution)/shard_map/ppermute | solution.py:283
  88.1 15.7 %collective-permute-start.15 = (bf16[640,512]{1,0:T(8,128)(2,1)S(1)}, bf16[640,512]{1,0:T(8,128)(2,1)S(1)}, u32[]{:S(2)}, u32[]{:S(2)}) collective-permute-start(bf16[640,512]{1,0:T(8,128)(2,1)S(1)} %collective-permute-done.6.refs_0_), channel_id=1, source_target_pairs={{0,16},{16,0},{32,48},{48,32},{64,80},{80,64},{96,112},{112,96},{1... | collective-permute-start | bytes 1966088 | tf_op jit(solution)/shard_map/ppermute | solution.py:283
  89.3 16.0 %collective-permute-start.17 = (bf16[640,512]{1,0:T(8,128)(2,1)S(1)}, bf16[640,512]{1,0:T(8,128)(2,1)S(1)}, u32[]{:S(2)}, u32[]{:S(2)}) collective-permute-start(bf16[640,512]{1,0:T(8,128)(2,1)S(1)} %collective-permute-done.7.refs_4_), channel_id=1, source_target_pairs={{0,16},{16,0},{32,48},{48,32},{64,80},{80,64},{96,112},{112,96},{1... | collective-permute-start | bytes 1966088 | tf_op jit(solution)/shard_map/ppermute | solution.py:283
  102.5 3.8 %collective-permute-start.16 = (bf16[384,512]{1,0:T(8,128)(2,1)S(1)}, bf16[384,512]{1,0:T(8,128)(2,1)S(1)}, u32[]{:S(2)}, u32[]{:S(2)}) collective-permute-start(bf16[384,512]{1,0:T(8,128)(2,1)S(1)} %collective-permute-done.8.refs_1_), channel_id=1, source_target_pairs={{0,16},{16,0},{32,48},{48,32},{64,80},{80,64},{96,112},{112,96},{1... | collective-permute-start | bytes 1179656 | tf_op jit(solution)/shard_map/ppermute | solution.py:283
  103.6 2.8 %collective-permute-start.18 = (bf16[384,512]{1,0:T(8,128)(2,1)S(1)}, bf16[384,512]{1,0:T(8,128)(2,1)S(1)}, u32[]{:S(2)}, u32[]{:S(2)}) collective-permute-start(bf16[384,512]{1,0:T(8,128)(2,1)S(1)} %collective-permute-done.9.refs_5_), channel_id=1, source_target_pairs={{0,16},{16,0},{32,48},{48,32},{64,80},{80,64},{96,112},{112,96},{1... | collective-permute-start | bytes 1179656 | tf_op jit(solution)/shard_map/ppermute | solution.py:283
  103.6 9.8 %collective-permute-start.14 = (bf16[256,512]{1,0:T(8,128)(2,1)S(1)}, bf16[256,512]{1,0:T(8,128)(2,1)S(1)}, u32[]{:S(2)}, u32[]{:S(2)}) collective-permute-start(bf16[256,512]{1,0:T(8,128)(2,1)S(1)} %slice.23), channel_id=1, source_target_pairs={{0,96},{16,112},{32,0},{48,16},{64,32},{80,48},{96,64},{112,80},{1... | collective-permute-start | bytes 786440 | tf_op jit(solution)/shard_map/ppermute | solution.py:283
  103.7 9.7 %collective-permute-start.13 = (bf16[128,512]{1,0:T(8,128)(2,1)S(1)}, bf16[128,512]{1,0:T(8,128)(2,1)S(1)}, u32[]{:S(2)}, u32[]{:S(2)}) collective-permute-start(bf16[128,512]{1,0:T(8,128)(2,1)S(1)} %slice.22), channel_id=1, source_target_pairs={{0,32},{16,48},{32,64},{48,80},{64,96},{80,112},{96,0},{112,16},{1... | collective-permute-start | bytes 393224 | tf_op jit(solution)/shard_map/ppermute | solution.py:283
  105.3 8.9 %collective-permute-start.19 = (bf16[384,512]{1,0:T(8,128)(2,1)S(1)}, bf16[384,512]{1,0:T(8,128)(2,1)S(1)}, u32[]{:S(2)}, u32[]{:S(2)}) collective-permute-start(bf16[384,512]{1,0:T(8,128)(2,1)S(1)} %collective-permute-done.10.refs_0_), channel_id=1, source_target_pairs={{0,16},{16,0},{32,48},{48,32},{64,80},{80,64},{96,112},{112,96},{1... | collective-permute-start | bytes 1179656 | tf_op jit(solution)/shard_map/ppermute | solution.py:283
  106.3 7.8 %collective-permute-start.20 = (bf16[256,512]{1,0:T(8,128)(2,1)S(1)}, bf16[256,512]{1,0:T(8,128)(2,1)S(1)}, u32[]{:S(2)}, u32[]{:S(2)}) collective-permute-start(bf16[256,512]{1,0:T(8,128)(2,1)S(1)} %collective-permute-done.11.refs_1_), channel_id=1, source_target_pairs={{0,16},{16,0},{32,48},{48,32},{64,80},{80,64},{96,112},{112,96},{1... | collective-permute-start | bytes 786440 | tf_op jit(solution)/shard_map/ppermute | solution.py:283
  113.5 1.9 %collective-permute-start.22 = (bf16[256,512]{1,0:T(8,128)(2,1)S(1)}, bf16[256,512]{1,0:T(8,128)(2,1)S(1)}, u32[]{:S(2)}, u32[]{:S(2)}) collective-permute-start(bf16[256,512]{1,0:T(8,128)(2,1)S(1)} %collective-permute-done.14.refs_3_), channel_id=1, source_target_pairs={{0,16},{16,0},{32,48},{48,32},{64,80},{80,64},{96,112},{112,96},{1... | collective-permute-start | bytes 786440 | tf_op jit(solution)/shard_map/ppermute | solution.py:283
  114.0 1.3 collective-permute-start.21
  114.1 5.0 %copy-start.4 = (s32[8,12]{1,0:T(8,128)S(1)}, s32[8,12]{1,0:T(8,128)}, u32[]{:S(2)}) copy-start(s32[8,12]{1,0:T(8,128)} %rel_ref.1) | copy-start | bytes 1156
  115.3 3.8 %copy-start = (bf16[8,12,128,128]{3,2,1,0:T(8,128)(2,1)S(1)}, bf16[8,12,128,128]{3,2,1,0:T(8,128)(2,1)}, u32[]{:S(2)}) copy-start(bf16[8,12,128,128]{3,2,1,0:T(8,128)(2,1)} %caps.1.cap_ref) | copy-start | bytes 9437188

commit v14 on v10

--- a/solution.py
+++ b/solution.py
@@ -289,19 +289,20 @@
     first, features = lax.optimization_barrier((first, features))
     got = lax.all_to_all(first, "feat", 0, 0, tiled=True).reshape(n_feat * depth, rows_a + half)
     outgoing = arrange(features, proj_weight, core, n_feat, rows_a, rows_local, 0)
-    outgoing, send_blocks = lax.optimization_barrier((outgoing, send_blocks))
-
-    tables = jnp.stack([send_blocks[0]] + [send(send_blocks[0], d) for d in range(1, levels)])
-    tables = jnp.stack([tables, send(tables, 0, 1)], axis=1)
-    order = jnp.array([0, 1, 3, 2])
-    index = tables[order, :, place].reshape(n_graph, CAP)
+
+    table = jnp.broadcast_to(send_blocks.astype(BF16).reshape(1, n_graph * CAP, 1), (depth, n_graph * CAP, 16))
+    tables = lax.all_gather(table.reshape(depth, n_graph * CAP * 16), "graph")
+    tables = tables[:, 0].reshape(n_graph, n_graph, CAP, 16)[:, :, :, 0]
+    steps = jnp.arange(n_graph) // 2
+    sender = 2 * ((level - (steps ^ (steps >> 1)) + levels) % levels) + (jnp.arange(n_graph) % 2 ^ core)
+    index = tables[sender, place].astype(jnp.int32)
     peer = source_slots // CAP
     distance = (level - peer // 2 + levels) % levels
     slots = (2 * (distance ^ (distance >> 1)) + (peer % 2 ^ core)) * CAP + source_slots % CAP
     src_vectors, tgt_vectors = score_vectors(relation_weight, att_source, att_target)
 
-    got, outgoing, cap, src_vectors, tgt_vectors, slots, index = lax.optimization_barrier(
-        (got, outgoing, caps(edge_mask), src_vectors, tgt_vectors, slots, index)
+    got, outgoing, cap, src_vectors, tgt_vectors, slots = lax.optimization_barrier(
+        (got, outgoing, caps(edge_mask), src_vectors, tgt_vectors, slots)
     )
     later = lax.all_to_all(outgoing, "feat", 0, 0, tiled=True).reshape(n_feat * depth, rows_local - rows_a)
 

time: 165 us -> 177 us (1.073)
  blocking collectives: 0 us -> 20.7 us
  waiting for transfers between devices: 34.8 us -> 24.5 us
  local copies, waits for them, and re-layouts: 2.21 us -> 10.6 us
  starting transfers between devices: 39.4 us -> 32 us
    all_gather x0 -> x1, blocking collectives: none -> 20.7 us  [shards(): tables = lax.all_gather(table.reshape(depth, n_graph * CAP * 16), 'graph')]
    ppermute x23 -> x19, waiting for transfers between devices: 11.8 us -> 1.87 us  [send(): return lax.ppermute(x, 'graph', pairs)]
    ppermute x23 -> x19, starting transfers between devices: 28.2 us -> 19.9 us  [send(): return lax.ppermute(x, 'graph', pairs)]
    unnamed x20 -> x26, local copies, waits for them, and re-layouts: 0.05 us -> 4.64 us
    slice x4, local copies, waits for them, and re-layouts: 0.07 us -> 3.37 us  [forward(): return (send(up[:middle], 1), send(down[middle:], -1))]
  transfers between devices with their start and end apart: 25 -> 21, of which waited for: 5 -> 5; matrix products, arithmetic and copies ran while one was open for 4% -> 9% of each run, Pallas kernels for 11% -> 11%
where the time goes in v14:
time: 177 us; the launch traced here: 176 us
  Pallas kernels  80.4 us (45%)
  starting transfers between devices  32 us (18%)
  waiting for transfers between devices  24.5 us (14%)
  blocking collectives  20.7 us (12%)
  local copies, waits for them, and re-layouts  10.6 us (6%)
  matrix products  5.82 us (3%)
  other arithmetic  1.89 us (1%)
    pallas_call x1, Pallas kernels, attend(): pl.pallas_call(attend_kernel, in_specs=[scalars] * 2 + [inside] * 5, out_...  52.9 us
    all_gather x1, blocking collectives, shards(): tables = lax.all_gather(table.reshape(depth, n_graph * CAP * 16), 'graph')  20.7 us
    ppermute x19, starting transfers between devices, send(): return lax.ppermute(x, 'graph', pairs)  19.9 us
    pallas_call x3, Pallas kernels, transform(): pl.pallas_call(functools.partial(transform_kernel, bounds, first), in_spe...  13.2 us
    all_to_all x1, waiting for transfers between devices, shards(): lax.all_to_all(outgoing, 'feat', 0, 0, tiled=True)  12.5 us
    all_to_all x1, waiting for transfers between devices, shards(): lax.all_to_all(first, 'feat', 0, 0, tiled=True)  10.1 us
    all_to_all x1, starting transfers between devices, shards(): lax.all_to_all(first, 'feat', 0, 0, tiled=True)  7.72 us
    pallas_call x2, Pallas kernels, arrange(): pl.pallas_call(functools.partial(arrange_kernel, low, high), grid_spec=pl...  7.28 us
  transfers between devices with their start and end apart: 21, of which 5 were waited for; matrix products, arithmetic and copies ran while one was open for 9% of the time, Pallas kernels for 11%

profile of v14, /device:TPU:1, one launch (start us, length us, event | category | flops | bytes accessed | tf_op | source)
XLA Modules:
  0.0 176.1 jit_solution(15988339819106376899)
XLA Ops:
  0.0 3.7 %arrange.2 = bf16[16,64,768]{2,1,0:T(8,128)(2,1)} custom-call(s32[1]{0:T(128)} %bitcast.core_ref, bf16[64,16384]{1,0:T(8,128)(2,1)} %bitcast.32, bf16[64,512]{1,0:T(8,128)(2,1)} %w_ref.3), custom_call_target="tpu_custom_call" | custom-call | tf_op jit(solution)/shard_map/arrange/pallas_call | solution.py:31
  3.7 7.7 %all-to-all-start = ((bf16[16,64,768]{2,1,0:T(8,128)(2,1)}), bf16[16,64,768]{2,1,0:T(8,128)(2,1)S(1)}, u32[]{:S(2)}, u32[]{:S(2)}) async-start(bf16[16,64,768]{2,1,0:T(8,128)(2,1)} %arrange.2), calls=%async_computation | async-start | bytes 3145728 | tf_op jit(solution)/shard_map/all_to_all | solution.py:290
  11.5 0.0 copy-start.8
  11.5 0.9 fusion
  12.4 3.6 %arrange.3 = bf16[16,64,512]{2,1,0:T(8,128)(2,1)} custom-call(s32[1]{0:T(128)} %bitcast.core_ref, bf16[64,16384]{1,0:T(8,128)(2,1)} %bitcast.33, bf16[64,512]{1,0:T(8,128)(2,1)} %w_ref.3), custom_call_target="tpu_custom_call" | custom-call | tf_op jit(solution)/shard_map/arrange/pallas_call | solution.py:31
  16.0 0.1 copy.19
  16.2 0.0 copy-start.10
  16.2 6.9 %caps.1.cap_ref = bf16[8,12,128,128]{3,2,1,0:T(8,128)(2,1)} custom-call(s32[8,12,128,128]{3,2,1,0:T(8,128)} %mask_ref.1), custom_call_target="tpu_custom_call" | custom-call | tf_op jit(solution)/shard_map/caps/pallas_call | solution.py:125
  23.1 0.1 pad.18.clone
  23.2 0.1 select_multiply_fusion
  23.3 0.1 fusion.6
  23.5 0.7 maximum_maximum_fusion.refs_5_.refs_9_
  24.2 10.1 %all-to-all-done = bf16[16,64,768]{2,1,0:T(8,128)(2,1)S(1)} async-done(((bf16[16,64,768]{2,1,0:T(8,128)(2,1)}), bf16[16,64,768]{2,1,0:T(8,128)(2,1)S(1)}, u32[]{:S(2)}, u32[]{:S(2)}) %all-to-all-start) | async-done | bytes 1572896 | tf_op jit(solution)/shard_map/all_to_all | solution.py:290
  34.4 2.6 %collective-permute-start = (bf16[1024,256]{1,0:T(8,128)(2,1)S(1)}, bf16[1024,256]{1,0:T(8,128)(2,1)}, u32[]{:S(2)}, u32[]{:S(2)}) collective-permute-start(bf16[1024,256]{1,0:T(8,128)(2,1)S(1)} %slice.25), channel_id=1, source_target_pairs={{0,16},{16,0},{32,48},{48,32},{64,80},{80,64},{96,112},{112,96},{1... | collective-permute-start | bytes 1572872 | tf_op jit(solution)/shard_map/ppermute | solution.py:283
  37.0 4.3 %all-to-all-start.1 = ((bf16[16,64,512]{2,1,0:T(8,128)(2,1)}), bf16[16,64,512]{2,1,0:T(8,128)(2,1)}, u32[]{:S(2)}, u32[]{:S(2)}) async-start(bf16[16,64,512]{2,1,0:T(8,128)(2,1)} %arrange.3), calls=%async_computation.1 | async-start | bytes 2097152 | tf_op jit(solution)/shard_map/all_to_all | solution.py:307
  41.3 0.0 collective-permute-done
  41.3 2.3 %convolution_convert_fusion.1.refs_0_ = bf16[512,512]{1,0:T(8,128)(2,1)S(1)} fusion(bf16[1024,768]{1,0:T(8,128)(2,1)S(1)} %bitcast.35, bf16[1024,256]{1,0:T(8,128)(2,1)} %collective-permute-done, bf16[1024,256]{1,0:T(8,128)(2,1)} %copy-done.7, pred[]{:T(512)S(6)} %eq.28), kind=kOutput, calls=%fused_computation.2 | convolution fusion | flops 541851648 | bytes 2621441 | tf_op jit(solution)/shard_map/dot_general | solution.py:314
  43.7 1.7 collective-permute-start.1
  45.4 2.2 %collective-permute-start.2 = (bf16[512,512]{1,0:T(8,128)(2,1)S(1)}, bf16[512,512]{1,0:T(8,128)(2,1)S(1)}, u32[]{:S(2)}, u32[]{:S(2)}) collective-permute-start(bf16[512,512]{1,0:T(8,128)(2,1)S(1)} %convolution_convert_fusion.1.refs_0_), channel_id=1, source_target_pairs={{0,96},{16,112},{32,0},{48,16},{64,32},{80,48},{96,64},{112,80},{1... | collective-permute-start | bytes 1572872 | tf_op jit(solution)/shard_map/ppermute | solution.py:283
  47.6 0.3 collective-permute-start.7
  47.9 12.5 %all-to-all-done.1 = bf16[16,64,512]{2,1,0:T(8,128)(2,1)} async-done(((bf16[16,64,512]{2,1,0:T(8,128)(2,1)}), bf16[16,64,512]{2,1,0:T(8,128)(2,1)}, u32[]{:S(2)}, u32[]{:S(2)}) %all-to-all-start.1) | async-done | bytes 1048608 | tf_op jit(solution)/shard_map/all_to_all | solution.py:307
  60.4 2.6 %convolution_convert_fusion.refs_1_ = bf16[512,512]{1,0:T(8,128)(2,1)S(1)} fusion(bf16[1024,512]{1,0:T(8,128)(2,1)} %bitcast.9, bf16[1024,256]{1,0:T(8,128)(2,1)} %collective-permute-done, bf16[1024,256]{1,0:T(8,128)(2,1)} %copy-done.7, pred[]{:T(512)S(6)} %eq.28), kind=kOutput, calls=%fused_computation.1 | convolution fusion | flops 541851648 | bytes 2621441 | tf_op jit(solution)/shard_map/dot_general | solution.py:314
  63.0 0.9 collective-permute-start.8
  63.9 1.6 collective-permute-start.3
  65.6 2.1 %collective-permute-start.4 = (bf16[512,512]{1,0:T(8,128)(2,1)S(1)}, bf16[512,512]{1,0:T(8,128)(2,1)}, u32[]{:S(2)}, u32[]{:S(2)}) collective-permute-start(bf16[512,512]{1,0:T(8,128)(2,1)S(1)} %convolution_convert_fusion.refs_1_), channel_id=1, source_target_pairs={{0,96},{16,112},{32,0},{48,16},{64,32},{80,48},{96,64},{112,80},{1... | collective-permute-start | bytes 1572872 | tf_op jit(solution)/shard_map/ppermute | solution.py:283
  67.7 0.7 slice.28
  68.4 0.0 collective-permute-start.5
  68.4 0.7 slice.29
  69.1 0.0 collective-permute-done.7.refs_2_
  69.1 2.7 %collective-permute-start.6 = (bf16[256,512]{1,0:T(8,128)(2,1)}, bf16[256,512]{1,0:T(8,128)(2,1)}, u32[]{:S(2)}, u32[]{:S(2)}) collective-permute-start(bf16[256,512]{1,0:T(8,128)(2,1)} %slice.29), channel_id=1, source_target_pairs={{0,96},{16,112},{32,0},{48,16},{64,32},{80,48},{96,64},{112,80},{1... | collective-permute-start | bytes 786440 | tf_op jit(solution)/shard_map/ppermute | solution.py:283
  71.8 0.8 copy-done.4
  72.6 1.0 collective-permute-start.11
  73.6 0.1 copy.20
  73.7 0.1 broadcast_in_dim.28
  73.8 0.1 broadcast_in_dim.29
  73.9 0.1 reshape.216
  74.0 20.7 %all-gather.1 = bf16[8,1,512]{2,1,0:T(2,128)(2,1)} all-gather(bf16[1,1,512]{2,1,0:T(2,128)(2,1)S(1)} %reshape.216), channel_id=3, replica_groups=mesh['graph'=8,'feat'=16] {'graph'}, dimensions={0}, use_global_device_ids=true | all-gather | bytes 9216 | tf_op jit(solution)/shard_map/all_gather | solution.py:294
  94.6 0.8 reduce
  95.4 0.7 reshape_squeeze.3
  96.1 1.9 %copy.25 = bf16[8,8,4,1]{2,1,0,3:T(8,128)(2,1)} copy(bf16[8,8,4,1]{3,2,1,0:T(4,128)(2,1)} %bitcast.36) | data formatting | bytes 1024
  98.1 1.3 gather_fusion
  99.4 0.8 copy-done.2
  100.2 1.0 copy-done.5
  101.2 3.4 %transform.3 = (bf16[32,2,128,512]{3,2,1,0:T(8,128)(2,1)S(1)}, f32[32,8,128]{2,1,0:T(8,128)S(1)}) custom-call(s32[8,4]{1,0:T(8,128)S(1)} %convert_element_type.42.idx_ref, bf16[512,512]{1,0:T(8,128)(2,1)S(1)} %convolution_convert_fusion.1.refs_0_, bf16[512,512]{1,0:T(8,128)(2,1)S(1)} %convolution_convert_fusion.refs_1_, ...), custom_call_target="tpu_custom_call" | custom-call | tf_op jit(solution)/shard_map/transform/pallas_call | solution.py:100
  104.6 0.3 collective-permute-start.13
  104.9 0.4 collective-permute-start.12
  105.3 0.2 collective-permute-start.14
  105.5 1.0 slice.31
  106.4 1.0 slice.30
  107.4 0.7 collective-permute-start.10
  108.1 0.9 collective-permute-start.9
  109.0 0.0 collective-permute-done.13.refs_6_
  109.0 0.9 collective-permute-start.15
  109.8 0.1 collective-permute-start.16
  109.9 6.3 %transform.4 = (bf16[32,2,128,512]{3,2,1,0:T(8,128)(2,1)S(1)}, f32[32,8,128]{2,1,0:T(8,128)S(1)}) custom-call(s32[8,4]{1,0:T(8,128)S(1)} %convert_element_type.42.idx_ref, bf16[512,512]{1,0:T(8,128)(2,1)S(1)} %collective-permute-done.1.refs_0_, bf16[512,512]{1,0:T(8,128)(2,1)} %collective-permute-done.3.refs_1_, ...), custom_call_target="tpu_custom_call", output_to_operand_aliasing={{0}: (11, {}), {1}: (12, {})} | custom-call | tf_op jit(solution)/shard_map/transform/pallas_call | solution.py:100
  116.2 0.4 collective-permute-done.9.refs_2_
  116.6 1.4 collective-permute-start.17
  118.0 0.0 collective-permute-start.18
  118.0 0.1 pad_maximum_fusion
  118.1 0.0 copy-start.6
  118.1 1.1 collective-permute-done.17.refs_6_
  119.2 0.4 collective-permute-done.18.refs_7_
  119.6 3.6 %transform.5 = (bf16[32,2,128,512]{3,2,1,0:T(8,128)(2,1)S(1)}, f32[32,8,128]{2,1,0:T(8,128)S(1)}) custom-call(s32[8,4]{1,0:T(8,128)S(1)} %convert_element_type.42.idx_ref, bf16[256,512]{1,0:T(8,128)(2,1)} %collective-permute-done.5.refs_0_, bf16[256,512]{1,0:T(8,128)(2,1)} %collective-permute-done.6.refs_1_, ...), custom_call_target="tpu_custom_call", output_to_operand_aliasing={{0}: (11, {}), {1}: (12, {})} | custom-call | tf_op jit(solution)/shard_map/transform/pallas_call | solution.py:100
  123.2 52.9 %attend.1 = bf16[8,128,512]{2,1,0:T(8,128)(2,1)} custom-call(s32[8,12]{1,0:T(8,128)S(1)} %copy-done.6, s32[8,12]{1,0:T(8,128)S(1)} %fusion.15.slot_ref, bf16[8,128,512]{2,1,0:T(8,128)(2,1)S(1)} %bitcast.31, bf16[8,12,128,128]{3,2,1,0:T(8,128)(2,1)S(1)} %copy-done, bf16[3,512,128]{2,1,0:T(8,128)(2,1)S(1)} %pad_maximum_fusion.1.tgt_ref, ...), custom_call_target="tpu_custom_call" | custom-call | tf_op jit(solution)/shard_map/attend/pallas_call | solution.py:224
  (46 shorter events, 0.3 us)
Async XLA Ops:
  3.7 7.7 %copy-start.9 = (f32[2,512]{1,0:T(2,128)S(1)}, f32[2,512]{1,0:T(2,128)}, u32[]{:S(2)}) copy-start(f32[2,512]{1,0:T(2,128)} %param.12) | copy-start | bytes 12292
  3.7 7.8 %copy-start.1 = (bf16[2,512,512]{2,1,0:T(8,128)(2,1)S(1)}, bf16[2,512,512]{2,1,0:T(8,128)(2,1)}, u32[]{:S(2)}) copy-start(bf16[2,512,512]{2,1,0:T(8,128)(2,1)} %refs_8_.3) | copy-start | bytes 3145732
  3.7 30.6 %all-to-all-start = ((bf16[16,64,768]{2,1,0:T(8,128)(2,1)}), bf16[16,64,768]{2,1,0:T(8,128)(2,1)S(1)}, u32[]{:S(2)}, u32[]{:S(2)}) async-start(bf16[16,64,768]{2,1,0:T(8,128)(2,1)} %arrange.2), calls=%async_computation | async-start | bytes 3145728 | tf_op jit(solution)/shard_map/all_to_all | solution.py:290
  11.5 4.5 %copy-start.8 = (f32[2,512]{1,0:T(2,128)S(1)}, f32[2,512]{1,0:T(2,128)}, u32[]{:S(2)}) copy-start(f32[2,512]{1,0:T(2,128)} %param.13) | copy-start | bytes 12292
  16.2 7.3 %copy-start.10 = (s32[8,12]{1,0:T(8,128)S(1)}, s32[8,12]{1,0:T(8,128)}, u32[]{:S(2)}) copy-start(s32[8,12]{1,0:T(8,128)} %param.17) | copy-start | bytes 1156
  34.3 7.0 %copy-start.7 = (bf16[1024,256]{1,0:T(8,128)(2,1)}, bf16[1024,256]{1,0:T(8,128)(2,1)S(1)}, u32[]{:S(2)}) copy-start(bf16[1024,256]{1,0:T(8,128)(2,1)S(1)} %slice.25) | copy-start | bytes 1572868
  34.4 7.0 %collective-permute-start = (bf16[1024,256]{1,0:T(8,128)(2,1)S(1)}, bf16[1024,256]{1,0:T(8,128)(2,1)}, u32[]{:S(2)}, u32[]{:S(2)}) collective-permute-start(bf16[1024,256]{1,0:T(8,128)(2,1)S(1)} %slice.25), channel_id=1, source_target_pairs={{0,16},{16,0},{32,48},{48,32},{64,80},{80,64},{96,112},{112,96},{1... | collective-permute-start | bytes 1572872 | tf_op jit(solution)/shard_map/ppermute | solution.py:283
  37.0 23.5 %all-to-all-start.1 = ((bf16[16,64,512]{2,1,0:T(8,128)(2,1)}), bf16[16,64,512]{2,1,0:T(8,128)(2,1)}, u32[]{:S(2)}, u32[]{:S(2)}) async-start(bf16[16,64,512]{2,1,0:T(8,128)(2,1)} %arrange.3), calls=%async_computation.1 | async-start | bytes 2097152 | tf_op jit(solution)/shard_map/all_to_all | solution.py:307
  43.7 16.8 %collective-permute-start.1 = (bf16[512,512]{1,0:T(8,128)(2,1)S(1)}, bf16[512,512]{1,0:T(8,128)(2,1)S(1)}, u32[]{:S(2)}, u32[]{:S(2)}) collective-permute-start(bf16[512,512]{1,0:T(8,128)(2,1)S(1)} %convolution_convert_fusion.1.refs_0_), channel_id=1, source_target_pairs={{0,32},{16,48},{32,64},{48,80},{64,96},{80,112},{96,0},{112,16},{1... | collective-permute-start | bytes 1572872 | tf_op jit(solution)/shard_map/ppermute | solution.py:283
  45.4 15.1 %collective-permute-start.2 = (bf16[512,512]{1,0:T(8,128)(2,1)S(1)}, bf16[512,512]{1,0:T(8,128)(2,1)S(1)}, u32[]{:S(2)}, u32[]{:S(2)}) collective-permute-start(bf16[512,512]{1,0:T(8,128)(2,1)S(1)} %convolution_convert_fusion.1.refs_0_), channel_id=1, source_target_pairs={{0,96},{16,112},{32,0},{48,16},{64,32},{80,48},{96,64},{112,80},{1... | collective-permute-start | bytes 1572872 | tf_op jit(solution)/shard_map/ppermute | solution.py:283
  47.6 21.5 %collective-permute-start.7 = (bf16[512,512]{1,0:T(8,128)(2,1)S(1)}, bf16[512,512]{1,0:T(8,128)(2,1)}, u32[]{:S(2)}, u32[]{:S(2)}) collective-permute-start(bf16[512,512]{1,0:T(8,128)(2,1)S(1)} %convolution_convert_fusion.1.refs_0_), channel_id=1, source_target_pairs={{0,16},{16,0},{32,48},{48,32},{64,80},{80,64},{96,112},{112,96},{1... | collective-permute-start | bytes 1572872 | tf_op jit(solution)/shard_map/ppermute | solution.py:283
  60.4 13.2 %copy-start.11 = (s32[1,8,4]{1,2,0:T(4,128)S(1)}, s32[1,8,4]{1,2,0:T(4,128)}, u32[]{:S(2)}) copy-start(s32[1,8,4]{1,2,0:T(4,128)} %param.16) | copy-start | bytes 388
  63.0 8.8 %collective-permute-start.8 = (bf16[512,512]{1,0:T(8,128)(2,1)S(1)}, bf16[512,512]{1,0:T(8,128)(2,1)S(1)}, u32[]{:S(2)}, u32[]{:S(2)}) collective-permute-start(bf16[512,512]{1,0:T(8,128)(2,1)S(1)} %convolution_convert_fusion.refs_1_), channel_id=1, source_target_pairs={{0,16},{16,0},{32,48},{48,32},{64,80},{80,64},{96,112},{112,96},{1... | collective-permute-start | bytes 1572872 | tf_op jit(solution)/shard_map/ppermute | solution.py:283
  63.9 41.0 %collective-permute-start.3 = (bf16[512,512]{1,0:T(8,128)(2,1)S(1)}, bf16[512,512]{1,0:T(8,128)(2,1)}, u32[]{:S(2)}, u32[]{:S(2)}) collective-permute-start(bf16[512,512]{1,0:T(8,128)(2,1)S(1)} %convolution_convert_fusion.refs_1_), channel_id=1, source_target_pairs={{0,32},{16,48},{32,64},{48,80},{64,96},{80,112},{96,0},{112,16},{1... | collective-permute-start | bytes 1572872 | tf_op jit(solution)/shard_map/ppermute | solution.py:283
  65.6 39.3 %collective-permute-start.4 = (bf16[512,512]{1,0:T(8,128)(2,1)S(1)}, bf16[512,512]{1,0:T(8,128)(2,1)}, u32[]{:S(2)}, u32[]{:S(2)}) collective-permute-start(bf16[512,512]{1,0:T(8,128)(2,1)S(1)} %convolution_convert_fusion.refs_1_), channel_id=1, source_target_pairs={{0,96},{16,112},{32,0},{48,16},{64,32},{80,48},{96,64},{112,80},{1... | collective-permute-start | bytes 1572872 | tf_op jit(solution)/shard_map/ppermute | solution.py:283
  68.4 36.2 %collective-permute-start.5 = (bf16[256,512]{1,0:T(8,128)(2,1)}, bf16[256,512]{1,0:T(8,128)(2,1)}, u32[]{:S(2)}, u32[]{:S(2)}) collective-permute-start(bf16[256,512]{1,0:T(8,128)(2,1)} %slice.28), channel_id=1, source_target_pairs={{0,32},{16,48},{32,64},{48,80},{64,96},{80,112},{96,0},{112,16},{1... | collective-permute-start | bytes 786440 | tf_op jit(solution)/shard_map/ppermute | solution.py:283
  69.1 35.8 %collective-permute-start.6 = (bf16[256,512]{1,0:T(8,128)(2,1)}, bf16[256,512]{1,0:T(8,128)(2,1)}, u32[]{:S(2)}, u32[]{:S(2)}) collective-permute-start(bf16[256,512]{1,0:T(8,128)(2,1)} %slice.29), channel_id=1, source_target_pairs={{0,96},{16,112},{32,0},{48,16},{64,32},{80,48},{96,64},{112,80},{1... | collective-permute-start | bytes 786440 | tf_op jit(solution)/shard_map/ppermute | solution.py:283
  71.8 0.8 copy-start.4
  72.6 35.5 %collective-permute-start.11 = (bf16[512,512]{1,0:T(8,128)(2,1)S(1)}, bf16[512,512]{1,0:T(8,128)(2,1)}, u32[]{:S(2)}, u32[]{:S(2)}) collective-permute-start(bf16[512,512]{1,0:T(8,128)(2,1)S(1)} %collective-permute-done.1.refs_0_), channel_id=1, source_target_pairs={{0,16},{16,0},{32,48},{48,32},{64,80},{80,64},{96,112},{112,96},{1... | collective-permute-start | bytes 1572872 | tf_op jit(solution)/shard_map/ppermute | solution.py:283
  99.4 0.8 copy-start.2
  100.2 1.0 copy-start.5
  104.6 4.4 %collective-permute-start.13 = (bf16[512,512]{1,0:T(8,128)(2,1)S(1)}, bf16[512,512]{1,0:T(8,128)(2,1)S(1)}, u32[]{:S(2)}, u32[]{:S(2)}) collective-permute-start(bf16[512,512]{1,0:T(8,128)(2,1)S(1)} %collective-permute-done.2.refs_4_), channel_id=1, source_target_pairs={{0,16},{16,0},{32,48},{48,32},{64,80},{80,64},{96,112},{112,96},{1... | collective-permute-start | bytes 1572872 | tf_op jit(solution)/shard_map/ppermute | solution.py:283
  104.9 4.9 %collective-permute-start.12 = (bf16[512,512]{1,0:T(8,128)(2,1)}, bf16[512,512]{1,0:T(8,128)(2,1)S(1)}, u32[]{:S(2)}, u32[]{:S(2)}) collective-permute-start(bf16[512,512]{1,0:T(8,128)(2,1)} %collective-permute-done.3.refs_1_), channel_id=1, source_target_pairs={{0,16},{16,0},{32,48},{48,32},{64,80},{80,64},{96,112},{112,96},{1... | collective-permute-start | bytes 1572872 | tf_op jit(solution)/shard_map/ppermute | solution.py:283
  105.3 4.6 %collective-permute-start.14 = (bf16[512,512]{1,0:T(8,128)(2,1)}, bf16[512,512]{1,0:T(8,128)(2,1)S(1)}, u32[]{:S(2)}, u32[]{:S(2)}) collective-permute-start(bf16[512,512]{1,0:T(8,128)(2,1)} %collective-permute-done.4.refs_5_), channel_id=1, source_target_pairs={{0,16},{16,0},{32,48},{48,32},{64,80},{80,64},{96,112},{112,96},{1... | collective-permute-start | bytes 1572872 | tf_op jit(solution)/shard_map/ppermute | solution.py:283
  107.4 8.8 %collective-permute-start.10 = (bf16[256,512]{1,0:T(8,128)(2,1)S(1)}, bf16[256,512]{1,0:T(8,128)(2,1)S(1)}, u32[]{:S(2)}, u32[]{:S(2)}) collective-permute-start(bf16[256,512]{1,0:T(8,128)(2,1)S(1)} %slice.31), channel_id=1, source_target_pairs={{0,96},{16,112},{32,0},{48,16},{64,32},{80,48},{96,64},{112,80},{1... | collective-permute-start | bytes 786440 | tf_op jit(solution)/shard_map/ppermute | solution.py:283
  108.1 8.5 %collective-permute-start.9 = (bf16[256,512]{1,0:T(8,128)(2,1)S(1)}, bf16[256,512]{1,0:T(8,128)(2,1)S(1)}, u32[]{:S(2)}, u32[]{:S(2)}) collective-permute-start(bf16[256,512]{1,0:T(8,128)(2,1)S(1)} %slice.30), channel_id=1, source_target_pairs={{0,32},{16,48},{32,64},{48,80},{64,96},{80,112},{96,0},{112,16},{1... | collective-permute-start | bytes 786440 | tf_op jit(solution)/shard_map/ppermute | solution.py:283
  109.0 9.2 %collective-permute-start.15 = (bf16[256,512]{1,0:T(8,128)(2,1)}, bf16[256,512]{1,0:T(8,128)(2,1)S(1)}, u32[]{:S(2)}, u32[]{:S(2)}) collective-permute-start(bf16[256,512]{1,0:T(8,128)(2,1)} %collective-permute-done.5.refs_0_), channel_id=1, source_target_pairs={{0,16},{16,0},{32,48},{48,32},{64,80},{80,64},{96,112},{112,96},{1... | collective-permute-start | bytes 786440 | tf_op jit(solution)/shard_map/ppermute | solution.py:283
  109.8 8.3 %collective-permute-start.16 = (bf16[256,512]{1,0:T(8,128)(2,1)}, bf16[256,512]{1,0:T(8,128)(2,1)S(1)}, u32[]{:S(2)}, u32[]{:S(2)}) collective-permute-start(bf16[256,512]{1,0:T(8,128)(2,1)} %collective-permute-done.6.refs_1_), channel_id=1, source_target_pairs={{0,16},{16,0},{32,48},{48,32},{64,80},{80,64},{96,112},{112,96},{1... | collective-permute-start | bytes 786440 | tf_op jit(solution)/shard_map/ppermute | solution.py:283
  116.2 3.3 %copy-start.3 = (bf16[32,512]{1,0:T(8,128)(2,1)S(1)}, bf16[32,512]{1,0:T(8,128)(2,1)}, u32[]{:S(2)}) copy-start(bf16[32,512]{1,0:T(8,128)(2,1)} %maximum_maximum_fusion.refs_5_.refs_9_) | copy-start | bytes 98308
  116.6 2.6 %collective-permute-start.17 = (bf16[256,512]{1,0:T(8,128)(2,1)S(1)}, bf16[256,512]{1,0:T(8,128)(2,1)S(1)}, u32[]{:S(2)}, u32[]{:S(2)}) collective-permute-start(bf16[256,512]{1,0:T(8,128)(2,1)S(1)} %collective-permute-done.9.refs_2_), channel_id=1, source_target_pairs={{0,16},{16,0},{32,48},{48,32},{64,80},{80,64},{96,112},{112,96},{1... | collective-permute-start | bytes 786440 | tf_op jit(solution)/shard_map/ppermute | solution.py:283
  118.0 1.5 collective-permute-start.18
  118.1 5.0 %copy-start.6 = (s32[8,12]{1,0:T(8,128)S(1)}, s32[8,12]{1,0:T(8,128)}, u32[]{:S(2)}) copy-start(s32[8,12]{1,0:T(8,128)} %rel_ref.1) | copy-start | bytes 1156
  119.6 3.6 %copy-start = (bf16[8,12,128,128]{3,2,1,0:T(8,128)(2,1)S(1)}, bf16[8,12,128,128]{3,2,1,0:T(8,128)(2,1)}, u32[]{:S(2)}) copy-start(bf16[8,12,128,128]{3,2,1,0:T(8,128)(2,1)} %caps.1.cap_ref) | copy-start | bytes 9437188

commit v15 on v12

--- a/solution.py
+++ b/solution.py
@@ -51,7 +51,8 @@
     return hi.astype(BF16), mid.astype(BF16), (rest - mid).astype(BF16)
 
 
-def transform_kernel(bounds, first, idx_ref, *refs):
+def transform_kernel(bounds, first, *refs):
+    index, refs = refs[: len(bounds) // 2], refs[len(bounds) // 2 :]
     n_pieces = sum(len(p) for p in bounds)
     pieces = refs[:n_pieces]
     rw_ref, src_ref = refs[n_pieces : n_pieces + 2]
@@ -67,7 +68,7 @@
     begin = 0
     for source in range(len(bounds)):
         for c in range(cap):
-            wanted = idx_ref[first + source, c]
+            wanted = index[source // 2][source % 2, c]
             for n, (low, high) in enumerate(bounds[source]):
 
                 @pl.when((wanted >= low) & (wanted < high))
@@ -89,17 +90,17 @@
         for c in range(cap):
             score_ref[at + c] = score[:, c * block : (c + 1) * block]
 
-def transform(sources, first, index, relation_weight, src_vectors, block, values, scores):
+def transform(sources, peers, first, index, relation_weight, src_vectors, block, values, scores):
     bounds = tuple(tuple((low, high) for _, low, high in pieces) for pieces in sources)
     arrays = [array for pieces in sources for array, _, _ in pieces]
-    peers, cap = index.shape
+    cap = index[0].shape[1]
     relations, width = relation_weight.shape[:2]
     anywhere, inside = pl.BlockSpec(memory_space=pl.ANY), pl.BlockSpec(memory_space=pltpu.VMEM)
     kept = () if values is None else (values, scores)
-    at = 1 + len(arrays) + 2
+    at = len(index) + len(arrays) + 2
     return pl.pallas_call(
         functools.partial(transform_kernel, bounds, first),
-        in_specs=[pl.BlockSpec(memory_space=pltpu.SMEM)] + [anywhere] * len(arrays) + [inside] * (2 + len(kept)),
+        in_specs=[pl.BlockSpec(memory_space=pltpu.SMEM)] * len(index) + [anywhere] * len(arrays) + [inside] * (2 + len(kept)),
         out_specs=[inside, inside],
         scratch_shapes=[
             pltpu.VMEM((len(bounds), cap * block, width), BF16),
@@ -112,7 +113,7 @@
         input_output_aliases={at + n: n for n in range(len(kept))},
         compiler_params=pltpu.CompilerParams(vmem_limit_bytes=24 * 1024 * 1024),
         name="transform",
-    )(index, *arrays, relation_weight, src_vectors, *kept)
+    )(*index, *arrays, relation_weight, src_vectors, *kept)
 
 
 def cap_kernel(mask_ref, cap_ref):
@@ -290,17 +291,15 @@
     got = lax.all_to_all(first, "feat", 0, 0, tiled=True).reshape(n_feat * depth, rows_a + half)
     outgoing = arrange(features, proj_weight, core, n_feat, rows_a, rows_local, 0)
 
-    tables = jnp.stack([send_blocks[0]] + [send(send_blocks[0], d) for d in range(1, levels)])
-    tables = jnp.stack([tables, send(tables, 0, 1)], axis=1)
-    order = jnp.array([0, 1, 3, 2])
-    index = tables[order, :, place].reshape(n_graph, CAP)
+    pair = jnp.stack([send_blocks[0], send(send_blocks[0], 0, 1)])
+    lists = [pair[:, 2 * ((level + d) % levels) + core] for d in range(levels)]
     peer = source_slots // CAP
     distance = (level - peer // 2 + levels) % levels
     slots = (2 * (distance ^ (distance >> 1)) + (peer % 2 ^ core)) * CAP + source_slots % CAP
     src_vectors, tgt_vectors = score_vectors(relation_weight, att_source, att_target)
 
-    got, outgoing, cap, src_vectors, tgt_vectors, slots, index = lax.optimization_barrier(
-        (got, outgoing, caps(edge_mask), src_vectors, tgt_vectors, slots, index)
+    got, outgoing, cap, src_vectors, tgt_vectors, slots, lists = lax.optimization_barrier(
+        (got, outgoing, caps(edge_mask), src_vectors, tgt_vectors, slots, lists)
     )
     later = lax.all_to_all(outgoing, "feat", 0, 0, tiled=True).reshape(n_feat * depth, rows_local - rows_a)
 
@@ -314,8 +313,8 @@
     def both(pieces):
         return [pieces, [(send(x, 0, 1), low, high) for x, low, high in pieces]]
 
-    def spread(group, first, kept):
-        return transform(group, first, index, relation_weight, src_vectors, block_rows, *kept)
+    def spread(group, first, index, kept):
+        return transform(group, n_graph, first, index, relation_weight, src_vectors, block_rows, *kept)
 
     def ring(part):
         return send(part, 1), send(part, -1)
@@ -330,16 +329,21 @@
     far_a = forward(up_a, down_a)
     b = project(later)
     up_b, down_b = ring(b)
-    done = spread(both([(a, 0, cut), (b, cut, local_blocks)]), 0, (None, None))
-    up_b, down_b, far_a, done = lax.optimization_barrier((up_b, down_b, far_a, done))
+    done = spread(both([(a, 0, cut), (b, cut, local_blocks)]), 0, lists[:1], (None, None))
+    lists, done = lax.optimization_barrier((lists, done))
+    lists = [send(lists[d], d) for d in range(1, levels)]
+    up_b, down_b, far_a, lists, done = lax.optimization_barrier((up_b, down_b, far_a, lists, done))
     far_b = forward(up_b, down_b)
     done = spread(
-        both([(up_a, 0, cut), (up_b, cut, local_blocks)]) + both([(down_a, 0, cut), (down_b, cut, local_blocks)]), 2, done
+        both([(up_a, 0, cut), (up_b, cut, local_blocks)]) + both([(down_a, 0, cut), (down_b, cut, local_blocks)]),
+        2,
+        (lists[0], lists[2]),
+        done,
     )
     far_b, done = lax.optimization_barrier((far_b, done))
     quarter = cut // 2
     far = [(x, n * quarter, (n + 1) * quarter) for n, x in enumerate(far_a + far_b)]
-    values, scores = spread(both(far), 6, done)
+    values, scores = spread(both(far), 6, lists[1:2], done)
     return attend(jnp.concatenate([a, b]), cap, relation_ids, slots, values, scores, tgt_vectors)
 
 

time: 161 us -> 166 us (1.031)
  waiting for transfers between devices: 31 us -> 38.6 us
    all_to_all x1, waiting for transfers between devices: 5.83 us -> 12.3 us  [shards(): lax.all_to_all(first, 'feat', 0, 0, tiled=True)]
    ppermute x23, waiting for transfers between devices: 11.9 us -> 14 us  [send(): return lax.ppermute(x, 'graph', pairs)]
  transfers between devices with their start and end apart: 25 -> 25, of which waited for: 5 -> 8; matrix products, arithmetic and copies ran while one was open for 5% -> 4% of each run, Pallas kernels for 13% -> 13%
where the time goes in v15:
time: 166 us
  Pallas kernels  80.8 us (49%)
  waiting for transfers between devices  38.6 us (23%)
  starting transfers between devices  37.6 us (23%)
  matrix products  6.17 us (4%)
    pallas_call x1, Pallas kernels, attend(): pl.pallas_call(attend_kernel, in_specs=[scalars] * 2 + [inside] * 5, out_...  52.4 us
    ppermute x23, starting transfers between devices, send(): return lax.ppermute(x, 'graph', pairs)  26.5 us
    pallas_call x3, Pallas kernels, transform(): pl.pallas_call(functools.partial(transform_kernel, bounds, first), in_spe...  14.1 us
    ppermute x23, waiting for transfers between devices, send(): return lax.ppermute(x, 'graph', pairs)  14 us
    all_to_all x1, waiting for transfers between devices, shards(): lax.all_to_all(outgoing, 'feat', 0, 0, tiled=True)  12.3 us
    all_to_all x1, waiting for transfers between devices, shards(): lax.all_to_all(first, 'feat', 0, 0, tiled=True)  12.3 us
    pallas_call x2, Pallas kernels, arrange(): pl.pallas_call(functools.partial(arrange_kernel, low, high), grid_spec=pl...  7.27 us
    pallas_call x1, Pallas kernels, caps(): pl.pallas_call(cap_kernel, grid=shape[:1], in_specs=[spec], out_specs=spe...  6.92 us
  transfers between devices with their start and end apart: 25, of which 8 were waited for; matrix products, arithmetic and copies ran while one was open for 4% of the time, Pallas kernels for 13%

profile of v15, /device:TPU:1, one launch (start us, length us, event | category | flops | bytes accessed | tf_op | source)
XLA Modules:
  0.0 165.6 jit_solution(8056534612910449044)
XLA Ops:
  0.0 3.7 %arrange.2 = bf16[16,64,768]{2,1,0:T(8,128)(2,1)} custom-call(s32[1]{0:T(128)} %bitcast.core_ref, bf16[64,16384]{1,0:T(8,128)(2,1)} %bitcast.30, bf16[64,512]{1,0:T(8,128)(2,1)} %w_ref.3), custom_call_target="tpu_custom_call" | custom-call | tf_op jit(solution)/shard_map/arrange/pallas_call | solution.py:31
  3.7 1.5 collective-permute-start
  5.2 6.8 %all-to-all-start = ((bf16[16,64,768]{2,1,0:T(8,128)(2,1)}), bf16[16,64,768]{2,1,0:T(8,128)(2,1)S(1)}, u32[]{:S(2)}, u32[]{:S(2)}) async-start(bf16[16,64,768]{2,1,0:T(8,128)(2,1)} %arrange.2), calls=%async_computation | async-start | bytes 3145728 | tf_op jit(solution)/shard_map/all_to_all | solution.py:291
  12.1 0.0 copy-start.4
  12.1 0.9 fusion
  13.1 3.6 %arrange.3 = bf16[16,64,512]{2,1,0:T(8,128)(2,1)} custom-call(s32[1]{0:T(128)} %bitcast.core_ref, bf16[64,16384]{1,0:T(8,128)(2,1)} %bitcast.31, bf16[64,512]{1,0:T(8,128)(2,1)} %w_ref.3), custom_call_target="tpu_custom_call" | custom-call | tf_op jit(solution)/shard_map/arrange/pallas_call | solution.py:31
  16.7 0.1 copy.15
  16.9 0.0 copy-start.6
  16.9 6.9 %caps.1.cap_ref = bf16[8,12,128,128]{3,2,1,0:T(8,128)(2,1)} custom-call(s32[8,12,128,128]{3,2,1,0:T(8,128)} %mask_ref.1), custom_call_target="tpu_custom_call" | custom-call | tf_op jit(solution)/shard_map/caps/pallas_call | solution.py:126
  23.8 0.1 pad.19.clone
  23.9 0.1 select_multiply_fusion
  24.1 0.1 fusion.6
  24.3 0.1 maximum_maximum_fusion.refs_6_.refs_11_.refs_10_
  24.3 0.0 collective-permute-done
  24.3 0.3 fusion.10
  24.6 12.3 %all-to-all-done = bf16[16,64,768]{2,1,0:T(8,128)(2,1)S(1)} async-done(((bf16[16,64,768]{2,1,0:T(8,128)(2,1)}), bf16[16,64,768]{2,1,0:T(8,128)(2,1)S(1)}, u32[]{:S(2)}, u32[]{:S(2)}) %all-to-all-start) | async-done | bytes 1572896 | tf_op jit(solution)/shard_map/all_to_all | solution.py:291
  36.9 0.9 slice.19
  37.8 1.3 collective-permute-start.1
  39.1 4.3 %all-to-all-start.1 = ((bf16[16,64,512]{2,1,0:T(8,128)(2,1)}), bf16[16,64,512]{2,1,0:T(8,128)(2,1)}, u32[]{:S(2)}, u32[]{:S(2)}) async-start(bf16[16,64,512]{2,1,0:T(8,128)(2,1)} %arrange.3), calls=%async_computation.1 | async-start | bytes 2097152 | tf_op jit(solution)/shard_map/all_to_all | solution.py:304
  43.5 0.0 collective-permute-done.1
  43.5 2.7 %convolution_convert_fusion.1.refs_1_ = bf16[512,512]{1,0:T(8,128)(2,1)S(1)} fusion(bf16[1024,768]{1,0:T(8,128)(2,1)} %bitcast.33, bf16[1024,256]{1,0:T(8,128)(2,1)} %collective-permute-done.1, bf16[1024,256]{1,0:T(8,128)(2,1)} %slice.19, pred[]{:T(512)S(6)} %eq.30), kind=kOutput, calls=%fused_computation.1 | convolution fusion | flops 541851648 | bytes 2621441 | tf_op jit(solution)/shard_map/dot_general | solution.py:311
  46.1 1.7 %collective-permute-start.2 = (bf16[512,512]{1,0:T(8,128)(2,1)S(1)}, bf16[512,512]{1,0:T(8,128)(2,1)S(1)}, u32[]{:S(2)}, u32[]{:S(2)}) collective-permute-start(bf16[512,512]{1,0:T(8,128)(2,1)S(1)} %convolution_convert_fusion.1.refs_1_), channel_id=1, source_target_pairs={{0,32},{16,48},{32,64},{48,80},{64,96},{80,112},{96,0},{112,16},{1... | collective-permute-start | bytes 1572872 | tf_op jit(solution)/shard_map/ppermute | solution.py:284
  47.9 2.2 %collective-permute-start.3 = (bf16[512,512]{1,0:T(8,128)(2,1)S(1)}, bf16[512,512]{1,0:T(8,128)(2,1)S(1)}, u32[]{:S(2)}, u32[]{:S(2)}) collective-permute-start(bf16[512,512]{1,0:T(8,128)(2,1)S(1)} %convolution_convert_fusion.1.refs_1_), channel_id=1, source_target_pairs={{0,96},{16,112},{32,0},{48,16},{64,32},{80,48},{96,64},{112,80},{1... | collective-permute-start | bytes 1572872 | tf_op jit(solution)/shard_map/ppermute | solution.py:284
  50.1 0.3 collective-permute-start.8
  50.3 12.3 %all-to-all-done.1 = bf16[16,64,512]{2,1,0:T(8,128)(2,1)} async-done(((bf16[16,64,512]{2,1,0:T(8,128)(2,1)}), bf16[16,64,512]{2,1,0:T(8,128)(2,1)}, u32[]{:S(2)}, u32[]{:S(2)}) %all-to-all-start.1) | async-done | bytes 1048608 | tf_op jit(solution)/shard_map/all_to_all | solution.py:304
  62.7 0.0 collective-permute-done.2.refs_2_
  62.7 0.0 collective-permute-done.3.refs_6_
  62.7 2.6 %convolution_convert_fusion.refs_2_ = bf16[512,512]{1,0:T(8,128)(2,1)S(1)} fusion(bf16[1024,512]{1,0:T(8,128)(2,1)} %bitcast.11, bf16[1024,256]{1,0:T(8,128)(2,1)} %collective-permute-done.1, bf16[1024,256]{1,0:T(8,128)(2,1)} %slice.19, pred[]{:T(512)S(6)} %eq.30), kind=kOutput, calls=%fused_computation | convolution fusion | flops 541851648 | bytes 2621441 | tf_op jit(solution)/shard_map/dot_general | solution.py:311
  65.3 0.9 collective-permute-start.9
  66.2 1.6 collective-permute-start.4
  67.8 2.1 %collective-permute-start.5 = (bf16[512,512]{1,0:T(8,128)(2,1)S(1)}, bf16[512,512]{1,0:T(8,128)(2,1)S(1)}, u32[]{:S(2)}, u32[]{:S(2)}) collective-permute-start(bf16[512,512]{1,0:T(8,128)(2,1)S(1)} %convolution_convert_fusion.refs_2_), channel_id=1, source_target_pairs={{0,96},{16,112},{32,0},{48,16},{64,32},{80,48},{96,64},{112,80},{1... | collective-permute-start | bytes 1572872 | tf_op jit(solution)/shard_map/ppermute | solution.py:284
  69.9 0.1 collective-permute-start.6
  70.0 0.0 collective-permute-done.8.refs_3_
  70.1 2.7 %collective-permute-start.7 = (bf16[256,512]{1,0:T(8,128)(2,1)S(1)}, bf16[256,512]{1,0:T(8,128)(2,1)S(1)}, u32[]{:S(2)}, u32[]{:S(2)}) collective-permute-start(bf16[256,512]{1,0:T(8,128)(2,1)S(1)} %slice.21), channel_id=1, source_target_pairs={{0,96},{16,112},{32,0},{48,16},{64,32},{80,48},{96,64},{112,80},{1... | collective-permute-start | bytes 786440 | tf_op jit(solution)/shard_map/ppermute | solution.py:284
  72.8 0.0 collective-permute-done.9.refs_4_
  72.8 1.0 collective-permute-start.15
  73.8 3.4 %transform.3 = (bf16[32,2,128,512]{3,2,1,0:T(8,128)(2,1)S(1)}, f32[32,8,128]{2,1,0:T(8,128)S(1)}) custom-call(s32[2,4]{1,0:T(2,128)S(1)} %get-tuple-element.56.refs_0_, bf16[512,512]{1,0:T(8,128)(2,1)S(1)} %convolution_convert_fusion.1.refs_1_, bf16[512,512]{1,0:T(8,128)(2,1)S(1)} %convolution_convert_fusion.refs_2_, ...), custom_call_target="tpu_custom_call" | custom-call | tf_op jit(solution)/shard_map/transform/pallas_call | solution.py:101
  77.2 10.5 %collective-permute-done.6.refs_1_ = bf16[256,512]{1,0:T(8,128)(2,1)S(1)} collective-permute-done((bf16[256,512]{1,0:T(8,128)(2,1)S(1)}, bf16[256,512]{1,0:T(8,128)(2,1)S(1)}, u32[]{:S(2)}, u32[]{:S(2)}) %collective-permute-start.6) | collective-permute-done | bytes 262176 | tf_op jit(solution)/shard_map/ppermute | solution.py:284
  87.7 0.7 collective-permute-start.17
  88.4 2.9 %collective-permute-start.11 = (s32[2,4]{1,0:T(2,128)S(1)}, s32[2,4]{1,0:T(2,128)S(1)}, u32[]{:S(2)}, u32[]{:S(2)}) collective-permute-start(s32[2,4]{1,0:T(2,128)S(1)} %get-tuple-element.64), channel_id=1, source_target_pairs={{0,64},{16,80},{32,96},{48,112},{64,0},{80,16},{96,32},{112,48},{1... | collective-permute-start | bytes 104 | tf_op jit(solution)/shard_map/ppermute | solution.py:284
  91.3 0.7 collective-permute-start.12
  92.0 0.1 collective-permute-done.10.refs_0_
  92.0 0.4 collective-permute-done.11.refs_0_
  92.4 1.6 collective-permute-done.12.refs_1_
  94.0 2.4 %collective-permute-start.16 = (bf16[512,512]{1,0:T(8,128)(2,1)S(1)}, bf16[512,512]{1,0:T(8,128)(2,1)S(1)}, u32[]{:S(2)}, u32[]{:S(2)}) collective-permute-start(bf16[512,512]{1,0:T(8,128)(2,1)S(1)} %collective-permute-done.4.refs_3_), channel_id=1, source_target_pairs={{0,16},{16,0},{32,48},{48,32},{64,80},{80,64},{96,112},{112,96},{1... | collective-permute-start | bytes 1572872 | tf_op jit(solution)/shard_map/ppermute | solution.py:284
  96.4 0.0 collective-permute-start.18
  96.5 0.1 collective-permute-start.13
  96.5 0.0 collective-permute-done.15.refs_4_
  96.5 2.7 %collective-permute-start.14 = (bf16[256,512]{1,0:T(8,128)(2,1)S(1)}, bf16[256,512]{1,0:T(8,128)(2,1)S(1)}, u32[]{:S(2)}, u32[]{:S(2)}) collective-permute-start(bf16[256,512]{1,0:T(8,128)(2,1)S(1)} %slice.23), channel_id=1, source_target_pairs={{0,96},{16,112},{32,0},{48,16},{64,32},{80,48},{96,64},{112,80},{1... | collective-permute-start | bytes 786440 | tf_op jit(solution)/shard_map/ppermute | solution.py:284
  99.2 1.1 collective-permute-start.19
  100.3 0.0 collective-permute-done.16.refs_5_
  100.3 0.1 collective-permute-start.20
  100.4 7.0 %transform.4 = (bf16[32,2,128,512]{3,2,1,0:T(8,128)(2,1)S(1)}, f32[32,8,128]{2,1,0:T(8,128)S(1)}) custom-call(s32[2,4]{1,0:T(2,128)S(1)} %collective-permute-done.10.refs_0_, s32[2,4]{1,0:T(2,128)S(1)} %collective-permute-done.12.refs_1_, bf16[512,512]{1,0:T(8,128)(2,1)S(1)} %collective-permute-done.2.refs_2_, ...), custom_call_target="tpu_custom_call", output_to_operand_aliasing={{0}: (12, {}), {1}: (13, {})} | custom-call | tf_op jit(solution)/shard_map/transform/pallas_call | solution.py:101
  107.3 0.0 collective-permute-done.13.refs_3_
  107.3 0.0 collective-permute-done.14.refs_4_
  107.4 0.5 collective-permute-start.21
  107.9 0.1 collective-permute-start.22
  108.0 0.1 pad_maximum_fusion
  108.0 0.0 copy-start.2
  108.0 0.0 collective-permute-done.19.refs_5_
  108.1 1.0 collective-permute-done.21.refs_7_
  109.0 0.4 collective-permute-done.22.refs_8_
  109.4 3.8 %transform.5 = (bf16[32,2,128,512]{3,2,1,0:T(8,128)(2,1)S(1)}, f32[32,8,128]{2,1,0:T(8,128)S(1)}) custom-call(s32[2,4]{1,0:T(2,128)S(1)} %collective-permute-done.11.refs_0_, bf16[256,512]{1,0:T(8,128)(2,1)S(1)} %collective-permute-done.6.refs_1_, ...), custom_call_target="tpu_custom_call", output_to_operand_aliasing={{0}: (11, {}), {1}: (12, {})} | custom-call | tf_op jit(solution)/shard_map/transform/pallas_call | solution.py:101
  113.2 52.4 %attend.1 = bf16[8,128,512]{2,1,0:T(8,128)(2,1)} custom-call(s32[8,12]{1,0:T(8,128)S(1)} %copy-done.2, s32[8,12]{1,0:T(8,128)S(1)} %fusion.23.slot_ref, bf16[8,128,512]{2,1,0:T(8,128)(2,1)S(1)} %bitcast.29, bf16[8,12,128,128]{3,2,1,0:T(8,128)(2,1)S(1)} %copy-done, bf16[3,512,128]{2,1,0:T(8,128)(2,1)S(1)} %pad_maximum_fusion.1.tgt_ref, ...), custom_call_target="tpu_custom_call" | custom-call | tf_op jit(solution)/shard_map/attend/pallas_call | solution.py:225
  (35 shorter events, 0.3 us)
Async XLA Ops:
  0.0 3.7 %copy-start.7 = (s32[1,8,4]{1,2,0:T(4,128)S(1)}, s32[1,8,4]{1,2,0:T(4,128)}, u32[]{:S(2)}) copy-start(s32[1,8,4]{1,2,0:T(4,128)} %param.16) | copy-start | bytes 388
  3.7 8.4 %copy-start.5 = (f32[2,512]{1,0:T(2,128)S(1)}, f32[2,512]{1,0:T(2,128)}, u32[]{:S(2)}) copy-start(f32[2,512]{1,0:T(2,128)} %param.12) | copy-start | bytes 12292
  3.7 8.4 %copy-start.1 = (bf16[2,512,512]{2,1,0:T(8,128)(2,1)S(1)}, bf16[2,512,512]{2,1,0:T(8,128)(2,1)}, u32[]{:S(2)}) copy-start(bf16[2,512,512]{2,1,0:T(8,128)(2,1)} %refs_9_.1) | copy-start | bytes 3145732
  3.7 20.6 %collective-permute-start = (s32[8,4]{0,1:T(4,128)S(1)}, s32[8,4]{0,1:T(4,128)S(1)}, u32[]{:S(2)}, u32[]{:S(2)}) collective-permute-start(s32[8,4]{0,1:T(4,128)S(1)} %bitcast.36), channel_id=1, source_target_pairs={{0,16},{16,0},{32,48},{48,32},{64,80},{80,64},{96,112},{112,96},{1... | collective-permute-start | bytes 392 | tf_op jit(solution)/shard_map/ppermute | solution.py:284
  5.2 31.7 %all-to-all-start = ((bf16[16,64,768]{2,1,0:T(8,128)(2,1)}), bf16[16,64,768]{2,1,0:T(8,128)(2,1)S(1)}, u32[]{:S(2)}, u32[]{:S(2)}) async-start(bf16[16,64,768]{2,1,0:T(8,128)(2,1)} %arrange.2), calls=%async_computation | async-start | bytes 3145728 | tf_op jit(solution)/shard_map/all_to_all | solution.py:291
  12.1 4.6 %copy-start.4 = (f32[2,512]{1,0:T(2,128)S(1)}, f32[2,512]{1,0:T(2,128)}, u32[]{:S(2)}) copy-start(f32[2,512]{1,0:T(2,128)} %param.13) | copy-start | bytes 12292
  16.9 7.3 %copy-start.6 = (s32[8,12]{1,0:T(8,128)S(1)}, s32[8,12]{1,0:T(8,128)}, u32[]{:S(2)}) copy-start(s32[8,12]{1,0:T(8,128)} %param.17) | copy-start | bytes 1156
  36.9 6.5 %copy-start.3 = (bf16[16,64,768]{2,1,0:T(8,128)(2,1)}, bf16[16,64,768]{2,1,0:T(8,128)(2,1)S(1)}, u32[]{:S(2)}) copy-start(bf16[16,64,768]{2,1,0:T(8,128)(2,1)S(1)} %all-to-all-done) | copy-start | bytes 4718596
  37.8 5.6 %collective-permute-start.1 = (bf16[1024,256]{1,0:T(8,128)(2,1)}, bf16[1024,256]{1,0:T(8,128)(2,1)}, u32[]{:S(2)}, u32[]{:S(2)}) collective-permute-start(bf16[1024,256]{1,0:T(8,128)(2,1)} %slice.19), channel_id=1, source_target_pairs={{0,16},{16,0},{32,48},{48,32},{64,80},{80,64},{96,112},{112,96},{1... | collective-permute-start | bytes 1572872 | tf_op jit(solution)/shard_map/ppermute | solution.py:284
  39.1 23.6 %all-to-all-start.1 = ((bf16[16,64,512]{2,1,0:T(8,128)(2,1)}), bf16[16,64,512]{2,1,0:T(8,128)(2,1)}, u32[]{:S(2)}, u32[]{:S(2)}) async-start(bf16[16,64,512]{2,1,0:T(8,128)(2,1)} %arrange.3), calls=%async_computation.1 | async-start | bytes 2097152 | tf_op jit(solution)/shard_map/all_to_all | solution.py:304
  46.1 16.6 %collective-permute-start.2 = (bf16[512,512]{1,0:T(8,128)(2,1)S(1)}, bf16[512,512]{1,0:T(8,128)(2,1)S(1)}, u32[]{:S(2)}, u32[]{:S(2)}) collective-permute-start(bf16[512,512]{1,0:T(8,128)(2,1)S(1)} %convolution_convert_fusion.1.refs_1_), channel_id=1, source_target_pairs={{0,32},{16,48},{32,64},{48,80},{64,96},{80,112},{96,0},{112,16},{1... | collective-permute-start | bytes 1572872 | tf_op jit(solution)/shard_map/ppermute | solution.py:284
  47.9 14.8 %collective-permute-start.3 = (bf16[512,512]{1,0:T(8,128)(2,1)S(1)}, bf16[512,512]{1,0:T(8,128)(2,1)S(1)}, u32[]{:S(2)}, u32[]{:S(2)}) collective-permute-start(bf16[512,512]{1,0:T(8,128)(2,1)S(1)} %convolution_convert_fusion.1.refs_1_), channel_id=1, source_target_pairs={{0,96},{16,112},{32,0},{48,16},{64,32},{80,48},{96,64},{112,80},{1... | collective-permute-start | bytes 1572872 | tf_op jit(solution)/shard_map/ppermute | solution.py:284
  50.1 20.0 %collective-permute-start.8 = (bf16[512,512]{1,0:T(8,128)(2,1)S(1)}, bf16[512,512]{1,0:T(8,128)(2,1)}, u32[]{:S(2)}, u32[]{:S(2)}) collective-permute-start(bf16[512,512]{1,0:T(8,128)(2,1)S(1)} %convolution_convert_fusion.1.refs_1_), channel_id=1, source_target_pairs={{0,16},{16,0},{32,48},{48,32},{64,80},{80,64},{96,112},{112,96},{1... | collective-permute-start | bytes 1572872 | tf_op jit(solution)/shard_map/ppermute | solution.py:284
  65.3 7.5 %collective-permute-start.9 = (bf16[512,512]{1,0:T(8,128)(2,1)S(1)}, bf16[512,512]{1,0:T(8,128)(2,1)S(1)}, u32[]{:S(2)}, u32[]{:S(2)}) collective-permute-start(bf16[512,512]{1,0:T(8,128)(2,1)S(1)} %convolution_convert_fusion.refs_2_), channel_id=1, source_target_pairs={{0,16},{16,0},{32,48},{48,32},{64,80},{80,64},{96,112},{112,96},{1... | collective-permute-start | bytes 1572872 | tf_op jit(solution)/shard_map/ppermute | solution.py:284
  66.2 22.3 %collective-permute-start.4 = (bf16[512,512]{1,0:T(8,128)(2,1)S(1)}, bf16[512,512]{1,0:T(8,128)(2,1)S(1)}, u32[]{:S(2)}, u32[]{:S(2)}) collective-permute-start(bf16[512,512]{1,0:T(8,128)(2,1)S(1)} %convolution_convert_fusion.refs_2_), channel_id=1, source_target_pairs={{0,32},{16,48},{32,64},{48,80},{64,96},{80,112},{96,0},{112,16},{1... | collective-permute-start | bytes 1572872 | tf_op jit(solution)/shard_map/ppermute | solution.py:284
  67.8 23.5 %collective-permute-start.5 = (bf16[512,512]{1,0:T(8,128)(2,1)S(1)}, bf16[512,512]{1,0:T(8,128)(2,1)S(1)}, u32[]{:S(2)}, u32[]{:S(2)}) collective-permute-start(bf16[512,512]{1,0:T(8,128)(2,1)S(1)} %convolution_convert_fusion.refs_2_), channel_id=1, source_target_pairs={{0,96},{16,112},{32,0},{48,16},{64,32},{80,48},{96,64},{112,80},{1... | collective-permute-start | bytes 1572872 | tf_op jit(solution)/shard_map/ppermute | solution.py:284
  69.9 17.8 %collective-permute-start.6 = (bf16[256,512]{1,0:T(8,128)(2,1)S(1)}, bf16[256,512]{1,0:T(8,128)(2,1)S(1)}, u32[]{:S(2)}, u32[]{:S(2)}) collective-permute-start(bf16[256,512]{1,0:T(8,128)(2,1)S(1)} %slice.20), channel_id=1, source_target_pairs={{0,32},{16,48},{32,64},{48,80},{64,96},{80,112},{96,0},{112,16},{1... | collective-permute-start | bytes 786440 | tf_op jit(solution)/shard_map/ppermute | solution.py:284
  70.1 18.4 %collective-permute-start.7 = (bf16[256,512]{1,0:T(8,128)(2,1)S(1)}, bf16[256,512]{1,0:T(8,128)(2,1)S(1)}, u32[]{:S(2)}, u32[]{:S(2)}) collective-permute-start(bf16[256,512]{1,0:T(8,128)(2,1)S(1)} %slice.21), channel_id=1, source_target_pairs={{0,96},{16,112},{32,0},{48,16},{64,32},{80,48},{96,64},{112,80},{1... | collective-permute-start | bytes 786440 | tf_op jit(solution)/shard_map/ppermute | solution.py:284
  72.8 23.8 %collective-permute-start.15 = (bf16[512,512]{1,0:T(8,128)(2,1)S(1)}, bf16[512,512]{1,0:T(8,128)(2,1)S(1)}, u32[]{:S(2)}, u32[]{:S(2)}) collective-permute-start(bf16[512,512]{1,0:T(8,128)(2,1)S(1)} %collective-permute-done.2.refs_2_), channel_id=1, source_target_pairs={{0,16},{16,0},{32,48},{48,32},{64,80},{80,64},{96,112},{112,96},{1... | collective-permute-start | bytes 1572872 | tf_op jit(solution)/shard_map/ppermute | solution.py:284
  87.7 11.5 %collective-permute-start.17 = (bf16[512,512]{1,0:T(8,128)(2,1)S(1)}, bf16[512,512]{1,0:T(8,128)(2,1)S(1)}, u32[]{:S(2)}, u32[]{:S(2)}) collective-permute-start(bf16[512,512]{1,0:T(8,128)(2,1)S(1)} %collective-permute-done.3.refs_6_), channel_id=1, source_target_pairs={{0,16},{16,0},{32,48},{48,32},{64,80},{80,64},{96,112},{112,96},{1... | collective-permute-start | bytes 1572872 | tf_op jit(solution)/shard_map/ppermute | solution.py:284
  88.4 3.6 %collective-permute-start.10 = (s32[2,4]{1,0:T(2,128)S(1)}, s32[2,4]{1,0:T(2,128)S(1)}, u32[]{:S(2)}, u32[]{:S(2)}) collective-permute-start(s32[2,4]{1,0:T(2,128)S(1)} %get-tuple-element.63), channel_id=1, source_target_pairs={{0,32},{16,48},{32,64},{48,80},{64,96},{80,112},{96,0},{112,16},{1... | collective-permute-start | bytes 104 | tf_op jit(solution)/shard_map/ppermute | solution.py:284
  88.4 4.0 %collective-permute-start.11 = (s32[2,4]{1,0:T(2,128)S(1)}, s32[2,4]{1,0:T(2,128)S(1)}, u32[]{:S(2)}, u32[]{:S(2)}) collective-permute-start(s32[2,4]{1,0:T(2,128)S(1)} %get-tuple-element.64), channel_id=1, source_target_pairs={{0,64},{16,80},{32,96},{48,112},{64,0},{80,16},{96,32},{112,48},{1... | collective-permute-start | bytes 104 | tf_op jit(solution)/shard_map/ppermute | solution.py:284
  91.3 2.7 %collective-permute-start.12 = (s32[2,4]{1,0:T(2,128)S(1)}, s32[2,4]{1,0:T(2,128)S(1)}, u32[]{:S(2)}, u32[]{:S(2)}) collective-permute-start(s32[2,4]{1,0:T(2,128)S(1)} %get-tuple-element.65), channel_id=1, source_target_pairs={{0,96},{16,112},{32,0},{48,16},{64,32},{80,48},{96,64},{112,80},{1... | collective-permute-start | bytes 104 | tf_op jit(solution)/shard_map/ppermute | solution.py:284
  94.0 6.3 %collective-permute-start.16 = (bf16[512,512]{1,0:T(8,128)(2,1)S(1)}, bf16[512,512]{1,0:T(8,128)(2,1)S(1)}, u32[]{:S(2)}, u32[]{:S(2)}) collective-permute-start(bf16[512,512]{1,0:T(8,128)(2,1)S(1)} %collective-permute-done.4.refs_3_), channel_id=1, source_target_pairs={{0,16},{16,0},{32,48},{48,32},{64,80},{80,64},{96,112},{112,96},{1... | collective-permute-start | bytes 1572872 | tf_op jit(solution)/shard_map/ppermute | solution.py:284
  96.4 4.0 %collective-permute-start.18 = (bf16[512,512]{1,0:T(8,128)(2,1)S(1)}, bf16[512,512]{1,0:T(8,128)(2,1)S(1)}, u32[]{:S(2)}, u32[]{:S(2)}) collective-permute-start(bf16[512,512]{1,0:T(8,128)(2,1)S(1)} %collective-permute-done.5.refs_7_), channel_id=1, source_target_pairs={{0,16},{16,0},{32,48},{48,32},{64,80},{80,64},{96,112},{112,96},{1... | collective-permute-start | bytes 1572872 | tf_op jit(solution)/shard_map/ppermute | solution.py:284
  96.5 10.9 %collective-permute-start.13 = (bf16[256,512]{1,0:T(8,128)(2,1)S(1)}, bf16[256,512]{1,0:T(8,128)(2,1)S(1)}, u32[]{:S(2)}, u32[]{:S(2)}) collective-permute-start(bf16[256,512]{1,0:T(8,128)(2,1)S(1)} %slice.22), channel_id=1, source_target_pairs={{0,32},{16,48},{32,64},{48,80},{64,96},{80,112},{96,0},{112,16},{1... | collective-permute-start | bytes 786440 | tf_op jit(solution)/shard_map/ppermute | solution.py:284
  96.5 10.8 %collective-permute-start.14 = (bf16[256,512]{1,0:T(8,128)(2,1)S(1)}, bf16[256,512]{1,0:T(8,128)(2,1)S(1)}, u32[]{:S(2)}, u32[]{:S(2)}) collective-permute-start(bf16[256,512]{1,0:T(8,128)(2,1)S(1)} %slice.23), channel_id=1, source_target_pairs={{0,96},{16,112},{32,0},{48,16},{64,32},{80,48},{96,64},{112,80},{1... | collective-permute-start | bytes 786440 | tf_op jit(solution)/shard_map/ppermute | solution.py:284
  99.2 8.8 %collective-permute-start.19 = (bf16[256,512]{1,0:T(8,128)(2,1)S(1)}, bf16[256,512]{1,0:T(8,128)(2,1)S(1)}, u32[]{:S(2)}, u32[]{:S(2)}) collective-permute-start(bf16[256,512]{1,0:T(8,128)(2,1)S(1)} %collective-permute-done.6.refs_1_), channel_id=1, source_target_pairs={{0,16},{16,0},{32,48},{48,32},{64,80},{80,64},{96,112},{112,96},{1... | collective-permute-start | bytes 786440 | tf_op jit(solution)/shard_map/ppermute | solution.py:284
  100.3 7.8 %collective-permute-start.20 = (bf16[256,512]{1,0:T(8,128)(2,1)S(1)}, bf16[256,512]{1,0:T(8,128)(2,1)S(1)}, u32[]{:S(2)}, u32[]{:S(2)}) collective-permute-start(bf16[256,512]{1,0:T(8,128)(2,1)S(1)} %collective-permute-done.7.refs_2_), channel_id=1, source_target_pairs={{0,16},{16,0},{32,48},{48,32},{64,80},{80,64},{96,112},{112,96},{1... | collective-permute-start | bytes 786440 | tf_op jit(solution)/shard_map/ppermute | solution.py:284
  107.4 1.7 %collective-permute-start.21 = (bf16[256,512]{1,0:T(8,128)(2,1)S(1)}, bf16[256,512]{1,0:T(8,128)(2,1)S(1)}, u32[]{:S(2)}, u32[]{:S(2)}) collective-permute-start(bf16[256,512]{1,0:T(8,128)(2,1)S(1)} %collective-permute-done.13.refs_3_), channel_id=1, source_target_pairs={{0,16},{16,0},{32,48},{48,32},{64,80},{80,64},{96,112},{112,96},{1... | collective-permute-start | bytes 786440 | tf_op jit(solution)/shard_map/ppermute | solution.py:284
  107.9 1.5 collective-permute-start.22
  108.0 5.1 %copy-start.2 = (s32[8,12]{1,0:T(8,128)S(1)}, s32[8,12]{1,0:T(8,128)}, u32[]{:S(2)}) copy-start(s32[8,12]{1,0:T(8,128)} %rel_ref.1) | copy-start | bytes 1156
  109.4 3.8 %copy-start = (bf16[8,12,128,128]{3,2,1,0:T(8,128)(2,1)S(1)}, bf16[8,12,128,128]{3,2,1,0:T(8,128)(2,1)}, u32[]{:S(2)}) copy-start(bf16[8,12,128,128]{3,2,1,0:T(8,128)(2,1)} %caps.1.cap_ref) | copy-start | bytes 9437188

commit v16 on v15

--- a/solution.py
+++ b/solution.py
@@ -325,14 +325,13 @@
 
     a = project(got[:, :rows_a])
     up_a, down_a = ring(a)
-    later, up_a, down_a = lax.optimization_barrier((later, up_a, down_a))
+    near, lists = lists[:1], [send(lists[d], d) for d in range(1, levels)]
+    later, up_a, down_a, lists = lax.optimization_barrier((later, up_a, down_a, lists))
     far_a = forward(up_a, down_a)
     b = project(later)
     up_b, down_b = ring(b)
-    done = spread(both([(a, 0, cut), (b, cut, local_blocks)]), 0, lists[:1], (None, None))
-    lists, done = lax.optimization_barrier((lists, done))
-    lists = [send(lists[d], d) for d in range(1, levels)]
-    up_b, down_b, far_a, lists, done = lax.optimization_barrier((up_b, down_b, far_a, lists, done))
+    done = spread(both([(a, 0, cut), (b, cut, local_blocks)]), 0, near, (None, None))
+    up_b, down_b, far_a, done = lax.optimization_barrier((up_b, down_b, far_a, done))
     far_b = forward(up_b, down_b)
     done = spread(
         both([(up_a, 0, cut), (up_b, cut, local_blocks)]) + both([(down_a, 0, cut), (down_b, cut, local_blocks)]),

time: 166 us -> 158 us (0.952)
  waiting for transfers between devices: 38.6 us -> 33.9 us
  starting transfers between devices: 37.6 us -> 34.5 us
    all_to_all x1, waiting for transfers between devices: 12.3 us -> 0.01 us  [shards(): lax.all_to_all(outgoing, 'feat', 0, 0, tiled=True)]
    ppermute x23, waiting for transfers between devices: 14 us -> 21.6 us  [send(): return lax.ppermute(x, 'graph', pairs)]
    ppermute x23, starting transfers between devices: 26.5 us -> 23.3 us  [send(): return lax.ppermute(x, 'graph', pairs)]
  transfers between devices with their start and end apart: 25 -> 25, of which waited for: 8 -> 6; matrix products, arithmetic and copies ran while one was open for 4% -> 5% of each run, Pallas kernels for 13% -> 13%
where the time goes in v16:
time: 158 us; the launch traced here: 157 us
  Pallas kernels  80.5 us (51%)
  starting transfers between devices  34.5 us (22%)
  waiting for transfers between devices  33.9 us (21%)
  matrix products  6.17 us (4%)
    pallas_call x1, Pallas kernels, attend(): pl.pallas_call(attend_kernel, in_specs=[scalars] * 2 + [inside] * 5, out_...  52.3 us
    ppermute x23, starting transfers between devices, send(): return lax.ppermute(x, 'graph', pairs)  23.3 us
    ppermute x23, waiting for transfers between devices, send(): return lax.ppermute(x, 'graph', pairs)  21.6 us
    pallas_call x3, Pallas kernels, transform(): pl.pallas_call(functools.partial(transform_kernel, bounds, first), in_spe...  14 us
    all_to_all x1, waiting for transfers between devices, shards(): lax.all_to_all(first, 'feat', 0, 0, tiled=True)  12.3 us
    pallas_call x2, Pallas kernels, arrange(): pl.pallas_call(functools.partial(arrange_kernel, low, high), grid_spec=pl...  7.27 us
    pallas_call x1, Pallas kernels, caps(): pl.pallas_call(cap_kernel, grid=shape[:1], in_specs=[spec], out_specs=spe...  6.92 us
    all_to_all x1, starting transfers between devices, shards(): lax.all_to_all(first, 'feat', 0, 0, tiled=True)  6.84 us
  transfers between devices with their start and end apart: 25, of which 6 were waited for; matrix products, arithmetic and copies ran while one was open for 5% of the time, Pallas kernels for 13%

profile of v16, /device:TPU:1, one launch (start us, length us, event | category | flops | bytes accessed | tf_op | source)
XLA Modules:
  0.0 157.5 jit_solution(17888396196848095724)
XLA Ops:
  0.0 3.7 %arrange.2 = bf16[16,64,768]{2,1,0:T(8,128)(2,1)} custom-call(s32[1]{0:T(128)} %bitcast.core_ref, bf16[64,16384]{1,0:T(8,128)(2,1)} %bitcast.30, bf16[64,512]{1,0:T(8,128)(2,1)} %w_ref.3), custom_call_target="tpu_custom_call" | custom-call | tf_op jit(solution)/shard_map/arrange/pallas_call | solution.py:31
  3.7 1.5 collective-permute-start
  5.2 6.8 %all-to-all-start = ((bf16[16,64,768]{2,1,0:T(8,128)(2,1)}), bf16[16,64,768]{2,1,0:T(8,128)(2,1)S(1)}, u32[]{:S(2)}, u32[]{:S(2)}) async-start(bf16[16,64,768]{2,1,0:T(8,128)(2,1)} %arrange.2), calls=%async_computation | async-start | bytes 3145728 | tf_op jit(solution)/shard_map/all_to_all | solution.py:291
  12.1 0.0 copy-start.4
  12.1 0.9 fusion
  13.1 3.6 %arrange.3 = bf16[16,64,512]{2,1,0:T(8,128)(2,1)} custom-call(s32[1]{0:T(128)} %bitcast.core_ref, bf16[64,16384]{1,0:T(8,128)(2,1)} %bitcast.31, bf16[64,512]{1,0:T(8,128)(2,1)} %w_ref.3), custom_call_target="tpu_custom_call" | custom-call | tf_op jit(solution)/shard_map/arrange/pallas_call | solution.py:31
  16.7 0.1 copy.15
  16.9 0.0 copy-start.6
  16.9 6.9 %caps.1.cap_ref = bf16[8,12,128,128]{3,2,1,0:T(8,128)(2,1)} custom-call(s32[8,12,128,128]{3,2,1,0:T(8,128)} %mask_ref.1), custom_call_target="tpu_custom_call" | custom-call | tf_op jit(solution)/shard_map/caps/pallas_call | solution.py:126
  23.8 0.1 pad.19.clone
  23.9 0.1 select_multiply_fusion
  24.1 0.1 fusion.6
  24.3 0.1 maximum_maximum_fusion.refs_6_.refs_11_.refs_10_
  24.3 0.3 fusion.10
  24.6 12.3 %all-to-all-done = bf16[16,64,768]{2,1,0:T(8,128)(2,1)S(1)} async-done(((bf16[16,64,768]{2,1,0:T(8,128)(2,1)}), bf16[16,64,768]{2,1,0:T(8,128)(2,1)S(1)}, u32[]{:S(2)}, u32[]{:S(2)}) %all-to-all-start) | async-done | bytes 1572896 | tf_op jit(solution)/shard_map/all_to_all | solution.py:291
  36.9 0.9 slice.19
  37.8 1.3 collective-permute-start.1
  39.1 4.3 %all-to-all-start.1 = ((bf16[16,64,512]{2,1,0:T(8,128)(2,1)}), bf16[16,64,512]{2,1,0:T(8,128)(2,1)}, u32[]{:S(2)}, u32[]{:S(2)}) async-start(bf16[16,64,512]{2,1,0:T(8,128)(2,1)} %arrange.3), calls=%async_computation.1 | async-start | bytes 2097152 | tf_op jit(solution)/shard_map/all_to_all | solution.py:304
  43.5 0.0 collective-permute-done.1
  43.5 2.7 %convolution_convert_fusion.1.refs_1_ = bf16[512,512]{1,0:T(8,128)(2,1)S(1)} fusion(bf16[1024,768]{1,0:T(8,128)(2,1)} %bitcast.33, bf16[1024,256]{1,0:T(8,128)(2,1)} %collective-permute-done.1, bf16[1024,256]{1,0:T(8,128)(2,1)} %slice.19, pred[]{:T(512)S(6)} %eq.30), kind=kOutput, calls=%fused_computation.1 | convolution fusion | flops 541851648 | bytes 2621441 | tf_op jit(solution)/shard_map/dot_general | solution.py:311
  46.1 1.7 %collective-permute-start.2 = (bf16[512,512]{1,0:T(8,128)(2,1)S(1)}, bf16[512,512]{1,0:T(8,128)(2,1)S(1)}, u32[]{:S(2)}, u32[]{:S(2)}) collective-permute-start(bf16[512,512]{1,0:T(8,128)(2,1)S(1)} %convolution_convert_fusion.1.refs_1_), channel_id=1, source_target_pairs={{0,32},{16,48},{32,64},{48,80},{64,96},{80,112},{96,0},{112,16},{1... | collective-permute-start | bytes 1572872 | tf_op jit(solution)/shard_map/ppermute | solution.py:284
  47.9 2.2 %collective-permute-start.3 = (bf16[512,512]{1,0:T(8,128)(2,1)S(1)}, bf16[512,512]{1,0:T(8,128)(2,1)S(1)}, u32[]{:S(2)}, u32[]{:S(2)}) collective-permute-start(bf16[512,512]{1,0:T(8,128)(2,1)S(1)} %convolution_convert_fusion.1.refs_1_), channel_id=1, source_target_pairs={{0,96},{16,112},{32,0},{48,16},{64,32},{80,48},{96,64},{112,80},{1... | collective-permute-start | bytes 1572872 | tf_op jit(solution)/shard_map/ppermute | solution.py:284
  50.1 2.6 %collective-permute-start.5 = (s32[2,4]{1,0:T(2,128)S(1)}, s32[2,4]{1,0:T(2,128)S(1)}, u32[]{:S(2)}, u32[]{:S(2)}) collective-permute-start(s32[2,4]{1,0:T(2,128)S(1)} %get-tuple-element.47), channel_id=1, source_target_pairs={{0,64},{16,80},{32,96},{48,112},{64,0},{80,16},{96,32},{112,48},{1... | collective-permute-start | bytes 104 | tf_op jit(solution)/shard_map/ppermute | solution.py:284
  52.6 0.7 collective-permute-start.6
  53.3 9.0 %collective-permute-done.4.refs_0_ = s32[2,4]{1,0:T(2,128)S(1)} collective-permute-done((s32[2,4]{1,0:T(2,128)S(1)}, s32[2,4]{1,0:T(2,128)S(1)}, u32[]{:S(2)}, u32[]{:S(2)}) %collective-permute-start.4) | collective-permute-done | bytes 64 | tf_op jit(solution)/shard_map/ppermute | solution.py:284
  62.4 0.5 collective-permute-start.11
  62.9 0.2 collective-permute-done.5.refs_0_
  63.1 0.0 collective-permute-done.6.refs_1_
  63.1 0.0 all-to-all-done.1
  63.1 0.0 collective-permute-done.2.refs_2_
  63.1 0.0 collective-permute-done.3.refs_6_
  63.1 2.6 %convolution_convert_fusion.refs_2_ = bf16[512,512]{1,0:T(8,128)(2,1)S(1)} fusion(bf16[1024,512]{1,0:T(8,128)(2,1)} %bitcast.11, bf16[1024,256]{1,0:T(8,128)(2,1)} %collective-permute-done.1, bf16[1024,256]{1,0:T(8,128)(2,1)} %slice.19, pred[]{:T(512)S(6)} %eq.30), kind=kOutput, calls=%fused_computation | convolution fusion | flops 541851648 | bytes 2621441 | tf_op jit(solution)/shard_map/dot_general | solution.py:311
  65.7 1.1 collective-permute-start.12
  66.8 1.0 collective-permute-start.7
  67.8 2.1 %collective-permute-start.8 = (bf16[512,512]{1,0:T(8,128)(2,1)S(1)}, bf16[512,512]{1,0:T(8,128)(2,1)S(1)}, u32[]{:S(2)}, u32[]{:S(2)}) collective-permute-start(bf16[512,512]{1,0:T(8,128)(2,1)S(1)} %convolution_convert_fusion.refs_2_), channel_id=1, source_target_pairs={{0,96},{16,112},{32,0},{48,16},{64,32},{80,48},{96,64},{112,80},{1... | collective-permute-start | bytes 1572872 | tf_op jit(solution)/shard_map/ppermute | solution.py:284
  69.9 1.5 collective-permute-start.10
  71.5 0.0 collective-permute-done.11.refs_3_
  71.5 0.1 collective-permute-start.9
  71.6 0.0 collective-permute-done.12.refs_4_
  71.6 1.0 collective-permute-start.15
  72.6 3.3 %transform.3 = (bf16[32,2,128,512]{3,2,1,0:T(8,128)(2,1)S(1)}, f32[32,8,128]{2,1,0:T(8,128)S(1)}) custom-call(s32[2,4]{1,0:T(2,128)S(1)} %get-tuple-element.55.refs_0_, bf16[512,512]{1,0:T(8,128)(2,1)S(1)} %convolution_convert_fusion.1.refs_1_, bf16[512,512]{1,0:T(8,128)(2,1)S(1)} %convolution_convert_fusion.refs_2_, ...), custom_call_target="tpu_custom_call" | custom-call | tf_op jit(solution)/shard_map/transform/pallas_call | solution.py:101
  75.9 11.0 %collective-permute-done.10.refs_2_ = bf16[256,512]{1,0:T(8,128)(2,1)S(1)} collective-permute-done((bf16[256,512]{1,0:T(8,128)(2,1)S(1)}, bf16[256,512]{1,0:T(8,128)(2,1)S(1)}, u32[]{:S(2)}, u32[]{:S(2)}) %collective-permute-start.10) | collective-permute-done | bytes 262176 | tf_op jit(solution)/shard_map/ppermute | solution.py:284
  87.0 1.0 collective-permute-start.17
  87.9 0.0 collective-permute-done.9.refs_1_
  87.9 0.0 collective-permute-done.7.refs_3_
  87.9 0.0 collective-permute-done.8.refs_7_
  88.0 0.5 collective-permute-start.16
  88.4 0.1 collective-permute-start.18
  88.6 1.5 collective-permute-start.13
  90.1 0.0 collective-permute-done.15.refs_4_
  90.1 1.8 %collective-permute-start.14 = (bf16[256,512]{1,0:T(8,128)(2,1)S(1)}, bf16[256,512]{1,0:T(8,128)(2,1)S(1)}, u32[]{:S(2)}, u32[]{:S(2)}) collective-permute-start(bf16[256,512]{1,0:T(8,128)(2,1)S(1)} %slice.23), channel_id=1, source_target_pairs={{0,96},{16,112},{32,0},{48,16},{64,32},{80,48},{96,64},{112,80},{1... | collective-permute-start | bytes 786440 | tf_op jit(solution)/shard_map/ppermute | solution.py:284
  91.9 0.0 collective-permute-done.17.refs_8_
  91.9 0.4 collective-permute-start.19
  92.3 0.0 collective-permute-done.16.refs_5_
  92.3 0.1 collective-permute-start.20
  92.4 7.0 %transform.4 = (bf16[32,2,128,512]{3,2,1,0:T(8,128)(2,1)S(1)}, f32[32,8,128]{2,1,0:T(8,128)S(1)}) custom-call(s32[2,4]{1,0:T(2,128)S(1)} %collective-permute-done.4.refs_0_, s32[2,4]{1,0:T(2,128)S(1)} %collective-permute-done.6.refs_1_, bf16[512,512]{1,0:T(8,128)(2,1)S(1)} %collective-permute-done.2.refs_2_, ...), custom_call_target="tpu_custom_call", output_to_operand_aliasing={{0}: (12, {}), {1}: (13, {})} | custom-call | tf_op jit(solution)/shard_map/transform/pallas_call | solution.py:101
  99.4 0.4 collective-permute-start.21
  99.9 0.1 collective-permute-start.22
  100.0 0.1 pad_maximum_fusion
  100.1 0.0 copy-start.2
  100.1 0.9 collective-permute-done.21.refs_7_
  101.0 0.4 collective-permute-done.22.refs_8_
  101.4 3.8 %transform.5 = (bf16[32,2,128,512]{3,2,1,0:T(8,128)(2,1)S(1)}, f32[32,8,128]{2,1,0:T(8,128)S(1)}) custom-call(s32[2,4]{1,0:T(2,128)S(1)} %collective-permute-done.5.refs_0_, bf16[256,512]{1,0:T(8,128)(2,1)S(1)} %collective-permute-done.9.refs_1_, ...), custom_call_target="tpu_custom_call", output_to_operand_aliasing={{0}: (11, {}), {1}: (12, {})} | custom-call | tf_op jit(solution)/shard_map/transform/pallas_call | solution.py:101
  105.2 52.3 %attend.1 = bf16[8,128,512]{2,1,0:T(8,128)(2,1)} custom-call(s32[8,12]{1,0:T(8,128)S(1)} %copy-done.2, s32[8,12]{1,0:T(8,128)S(1)} %fusion.23.slot_ref, bf16[8,128,512]{2,1,0:T(8,128)(2,1)S(1)} %bitcast.29, bf16[8,12,128,128]{3,2,1,0:T(8,128)(2,1)S(1)} %copy-done, bf16[3,512,128]{2,1,0:T(8,128)(2,1)S(1)} %pad_maximum_fusion.1.tgt_ref, ...), custom_call_target="tpu_custom_call" | custom-call | tf_op jit(solution)/shard_map/attend/pallas_call | solution.py:225
  (35 shorter events, 0.3 us)
Async XLA Ops:
  0.0 3.7 %copy-start.7 = (s32[1,8,4]{1,2,0:T(4,128)S(1)}, s32[1,8,4]{1,2,0:T(4,128)}, u32[]{:S(2)}) copy-start(s32[1,8,4]{1,2,0:T(4,128)} %param.16) | copy-start | bytes 388
  3.7 8.4 %copy-start.5 = (f32[2,512]{1,0:T(2,128)S(1)}, f32[2,512]{1,0:T(2,128)}, u32[]{:S(2)}) copy-start(f32[2,512]{1,0:T(2,128)} %param.12) | copy-start | bytes 12292
  3.7 8.4 %copy-start.1 = (bf16[2,512,512]{2,1,0:T(8,128)(2,1)S(1)}, bf16[2,512,512]{2,1,0:T(8,128)(2,1)}, u32[]{:S(2)}) copy-start(bf16[2,512,512]{2,1,0:T(8,128)(2,1)} %refs_9_.1) | copy-start | bytes 3145732
  3.7 20.6 %collective-permute-start = (s32[8,4]{0,1:T(4,128)S(1)}, s32[8,4]{0,1:T(4,128)S(1)}, u32[]{:S(2)}, u32[]{:S(2)}) collective-permute-start(s32[8,4]{0,1:T(4,128)S(1)} %bitcast.36), channel_id=1, source_target_pairs={{0,16},{16,0},{32,48},{48,32},{64,80},{80,64},{96,112},{112,96},{1... | collective-permute-start | bytes 392 | tf_op jit(solution)/shard_map/ppermute | solution.py:284
  5.2 31.7 %all-to-all-start = ((bf16[16,64,768]{2,1,0:T(8,128)(2,1)}), bf16[16,64,768]{2,1,0:T(8,128)(2,1)S(1)}, u32[]{:S(2)}, u32[]{:S(2)}) async-start(bf16[16,64,768]{2,1,0:T(8,128)(2,1)} %arrange.2), calls=%async_computation | async-start | bytes 3145728 | tf_op jit(solution)/shard_map/all_to_all | solution.py:291
  12.1 4.6 %copy-start.4 = (f32[2,512]{1,0:T(2,128)S(1)}, f32[2,512]{1,0:T(2,128)}, u32[]{:S(2)}) copy-start(f32[2,512]{1,0:T(2,128)} %param.13) | copy-start | bytes 12292
  16.9 7.3 %copy-start.6 = (s32[8,12]{1,0:T(8,128)S(1)}, s32[8,12]{1,0:T(8,128)}, u32[]{:S(2)}) copy-start(s32[8,12]{1,0:T(8,128)} %param.17) | copy-start | bytes 1156
  36.9 6.5 %copy-start.3 = (bf16[16,64,768]{2,1,0:T(8,128)(2,1)}, bf16[16,64,768]{2,1,0:T(8,128)(2,1)S(1)}, u32[]{:S(2)}) copy-start(bf16[16,64,768]{2,1,0:T(8,128)(2,1)S(1)} %all-to-all-done) | copy-start | bytes 4718596
  37.8 5.6 %collective-permute-start.1 = (bf16[1024,256]{1,0:T(8,128)(2,1)}, bf16[1024,256]{1,0:T(8,128)(2,1)}, u32[]{:S(2)}, u32[]{:S(2)}) collective-permute-start(bf16[1024,256]{1,0:T(8,128)(2,1)} %slice.19), channel_id=1, source_target_pairs={{0,16},{16,0},{32,48},{48,32},{64,80},{80,64},{96,112},{112,96},{1... | collective-permute-start | bytes 1572872 | tf_op jit(solution)/shard_map/ppermute | solution.py:284
  39.1 24.0 %all-to-all-start.1 = ((bf16[16,64,512]{2,1,0:T(8,128)(2,1)}), bf16[16,64,512]{2,1,0:T(8,128)(2,1)}, u32[]{:S(2)}, u32[]{:S(2)}) async-start(bf16[16,64,512]{2,1,0:T(8,128)(2,1)} %arrange.3), calls=%async_computation.1 | async-start | bytes 2097152 | tf_op jit(solution)/shard_map/all_to_all | solution.py:304
  46.1 16.9 %collective-permute-start.2 = (bf16[512,512]{1,0:T(8,128)(2,1)S(1)}, bf16[512,512]{1,0:T(8,128)(2,1)S(1)}, u32[]{:S(2)}, u32[]{:S(2)}) collective-permute-start(bf16[512,512]{1,0:T(8,128)(2,1)S(1)} %convolution_convert_fusion.1.refs_1_), channel_id=1, source_target_pairs={{0,32},{16,48},{32,64},{48,80},{64,96},{80,112},{96,0},{112,16},{1... | collective-permute-start | bytes 1572872 | tf_op jit(solution)/shard_map/ppermute | solution.py:284
  47.9 15.2 %collective-permute-start.3 = (bf16[512,512]{1,0:T(8,128)(2,1)S(1)}, bf16[512,512]{1,0:T(8,128)(2,1)S(1)}, u32[]{:S(2)}, u32[]{:S(2)}) collective-permute-start(bf16[512,512]{1,0:T(8,128)(2,1)S(1)} %convolution_convert_fusion.1.refs_1_), channel_id=1, source_target_pairs={{0,96},{16,112},{32,0},{48,16},{64,32},{80,48},{96,64},{112,80},{1... | collective-permute-start | bytes 1572872 | tf_op jit(solution)/shard_map/ppermute | solution.py:284
  50.1 12.3 %collective-permute-start.4 = (s32[2,4]{1,0:T(2,128)S(1)}, s32[2,4]{1,0:T(2,128)S(1)}, u32[]{:S(2)}, u32[]{:S(2)}) collective-permute-start(s32[2,4]{1,0:T(2,128)S(1)} %get-tuple-element.46), channel_id=1, source_target_pairs={{0,32},{16,48},{32,64},{48,80},{64,96},{80,112},{96,0},{112,16},{1... | collective-permute-start | bytes 104 | tf_op jit(solution)/shard_map/ppermute | solution.py:284
  50.1 13.0 %collective-permute-start.5 = (s32[2,4]{1,0:T(2,128)S(1)}, s32[2,4]{1,0:T(2,128)S(1)}, u32[]{:S(2)}, u32[]{:S(2)}) collective-permute-start(s32[2,4]{1,0:T(2,128)S(1)} %get-tuple-element.47), channel_id=1, source_target_pairs={{0,64},{16,80},{32,96},{48,112},{64,0},{80,16},{96,32},{112,48},{1... | collective-permute-start | bytes 104 | tf_op jit(solution)/shard_map/ppermute | solution.py:284
  52.6 10.5 %collective-permute-start.6 = (s32[2,4]{1,0:T(2,128)S(1)}, s32[2,4]{1,0:T(2,128)S(1)}, u32[]{:S(2)}, u32[]{:S(2)}) collective-permute-start(s32[2,4]{1,0:T(2,128)S(1)} %get-tuple-element.48), channel_id=1, source_target_pairs={{0,96},{16,112},{32,0},{48,16},{64,32},{80,48},{96,64},{112,80},{1... | collective-permute-start | bytes 104 | tf_op jit(solution)/shard_map/ppermute | solution.py:284
  62.4 9.1 %collective-permute-start.11 = (bf16[512,512]{1,0:T(8,128)(2,1)S(1)}, bf16[512,512]{1,0:T(8,128)(2,1)}, u32[]{:S(2)}, u32[]{:S(2)}) collective-permute-start(bf16[512,512]{1,0:T(8,128)(2,1)S(1)} %convolution_convert_fusion.1.refs_1_), channel_id=1, source_target_pairs={{0,16},{16,0},{32,48},{48,32},{64,80},{80,64},{96,112},{112,96},{1... | collective-permute-start | bytes 1572872 | tf_op jit(solution)/shard_map/ppermute | solution.py:284
  65.7 5.9 %collective-permute-start.12 = (bf16[512,512]{1,0:T(8,128)(2,1)S(1)}, bf16[512,512]{1,0:T(8,128)(2,1)S(1)}, u32[]{:S(2)}, u32[]{:S(2)}) collective-permute-start(bf16[512,512]{1,0:T(8,128)(2,1)S(1)} %convolution_convert_fusion.refs_2_), channel_id=1, source_target_pairs={{0,16},{16,0},{32,48},{48,32},{64,80},{80,64},{96,112},{112,96},{1... | collective-permute-start | bytes 1572872 | tf_op jit(solution)/shard_map/ppermute | solution.py:284
  66.8 21.2 %collective-permute-start.7 = (bf16[512,512]{1,0:T(8,128)(2,1)S(1)}, bf16[512,512]{1,0:T(8,128)(2,1)S(1)}, u32[]{:S(2)}, u32[]{:S(2)}) collective-permute-start(bf16[512,512]{1,0:T(8,128)(2,1)S(1)} %convolution_convert_fusion.refs_2_), channel_id=1, source_target_pairs={{0,32},{16,48},{32,64},{48,80},{64,96},{80,112},{96,0},{112,16},{1... | collective-permute-start | bytes 1572872 | tf_op jit(solution)/shard_map/ppermute | solution.py:284
  67.8 20.2 %collective-permute-start.8 = (bf16[512,512]{1,0:T(8,128)(2,1)S(1)}, bf16[512,512]{1,0:T(8,128)(2,1)S(1)}, u32[]{:S(2)}, u32[]{:S(2)}) collective-permute-start(bf16[512,512]{1,0:T(8,128)(2,1)S(1)} %convolution_convert_fusion.refs_2_), channel_id=1, source_target_pairs={{0,96},{16,112},{32,0},{48,16},{64,32},{80,48},{96,64},{112,80},{1... | collective-permute-start | bytes 1572872 | tf_op jit(solution)/shard_map/ppermute | solution.py:284
  69.9 17.0 %collective-permute-start.10 = (bf16[256,512]{1,0:T(8,128)(2,1)S(1)}, bf16[256,512]{1,0:T(8,128)(2,1)S(1)}, u32[]{:S(2)}, u32[]{:S(2)}) collective-permute-start(bf16[256,512]{1,0:T(8,128)(2,1)S(1)} %slice.21), channel_id=1, source_target_pairs={{0,96},{16,112},{32,0},{48,16},{64,32},{80,48},{96,64},{112,80},{1... | collective-permute-start | bytes 786440 | tf_op jit(solution)/shard_map/ppermute | solution.py:284
  71.5 16.4 %collective-permute-start.9 = (bf16[256,512]{1,0:T(8,128)(2,1)S(1)}, bf16[256,512]{1,0:T(8,128)(2,1)S(1)}, u32[]{:S(2)}, u32[]{:S(2)}) collective-permute-start(bf16[256,512]{1,0:T(8,128)(2,1)S(1)} %slice.20), channel_id=1, source_target_pairs={{0,32},{16,48},{32,64},{48,80},{64,96},{80,112},{96,0},{112,16},{1... | collective-permute-start | bytes 786440 | tf_op jit(solution)/shard_map/ppermute | solution.py:284
  71.6 18.5 %collective-permute-start.15 = (bf16[512,512]{1,0:T(8,128)(2,1)S(1)}, bf16[512,512]{1,0:T(8,128)(2,1)S(1)}, u32[]{:S(2)}, u32[]{:S(2)}) collective-permute-start(bf16[512,512]{1,0:T(8,128)(2,1)S(1)} %collective-permute-done.2.refs_2_), channel_id=1, source_target_pairs={{0,16},{16,0},{32,48},{48,32},{64,80},{80,64},{96,112},{112,96},{1... | collective-permute-start | bytes 1572872 | tf_op jit(solution)/shard_map/ppermute | solution.py:284
  87.0 4.9 %collective-permute-start.17 = (bf16[512,512]{1,0:T(8,128)(2,1)S(1)}, bf16[512,512]{1,0:T(8,128)(2,1)S(1)}, u32[]{:S(2)}, u32[]{:S(2)}) collective-permute-start(bf16[512,512]{1,0:T(8,128)(2,1)S(1)} %collective-permute-done.3.refs_6_), channel_id=1, source_target_pairs={{0,16},{16,0},{32,48},{48,32},{64,80},{80,64},{96,112},{112,96},{1... | collective-permute-start | bytes 1572872 | tf_op jit(solution)/shard_map/ppermute | solution.py:284
  88.0 4.3 %collective-permute-start.16 = (bf16[512,512]{1,0:T(8,128)(2,1)S(1)}, bf16[512,512]{1,0:T(8,128)(2,1)S(1)}, u32[]{:S(2)}, u32[]{:S(2)}) collective-permute-start(bf16[512,512]{1,0:T(8,128)(2,1)S(1)} %collective-permute-done.7.refs_3_), channel_id=1, source_target_pairs={{0,16},{16,0},{32,48},{48,32},{64,80},{80,64},{96,112},{112,96},{1... | collective-permute-start | bytes 1572872 | tf_op jit(solution)/shard_map/ppermute | solution.py:284
  88.4 4.0 %collective-permute-start.18 = (bf16[512,512]{1,0:T(8,128)(2,1)S(1)}, bf16[512,512]{1,0:T(8,128)(2,1)S(1)}, u32[]{:S(2)}, u32[]{:S(2)}) collective-permute-start(bf16[512,512]{1,0:T(8,128)(2,1)S(1)} %collective-permute-done.8.refs_7_), channel_id=1, source_target_pairs={{0,16},{16,0},{32,48},{48,32},{64,80},{80,64},{96,112},{112,96},{1... | collective-permute-start | bytes 1572872 | tf_op jit(solution)/shard_map/ppermute | solution.py:284
  88.6 10.8 %collective-permute-start.13 = (bf16[256,512]{1,0:T(8,128)(2,1)S(1)}, bf16[256,512]{1,0:T(8,128)(2,1)S(1)}, u32[]{:S(2)}, u32[]{:S(2)}) collective-permute-start(bf16[256,512]{1,0:T(8,128)(2,1)S(1)} %slice.22), channel_id=1, source_target_pairs={{0,32},{16,48},{32,64},{48,80},{64,96},{80,112},{96,0},{112,16},{1... | collective-permute-start | bytes 786440 | tf_op jit(solution)/shard_map/ppermute | solution.py:284
  90.1 9.3 %collective-permute-start.14 = (bf16[256,512]{1,0:T(8,128)(2,1)S(1)}, bf16[256,512]{1,0:T(8,128)(2,1)S(1)}, u32[]{:S(2)}, u32[]{:S(2)}) collective-permute-start(bf16[256,512]{1,0:T(8,128)(2,1)S(1)} %slice.23), channel_id=1, source_target_pairs={{0,96},{16,112},{32,0},{48,16},{64,32},{80,48},{96,64},{112,80},{1... | collective-permute-start | bytes 786440 | tf_op jit(solution)/shard_map/ppermute | solution.py:284
  91.9 8.2 %collective-permute-start.19 = (bf16[256,512]{1,0:T(8,128)(2,1)S(1)}, bf16[256,512]{1,0:T(8,128)(2,1)S(1)}, u32[]{:S(2)}, u32[]{:S(2)}) collective-permute-start(bf16[256,512]{1,0:T(8,128)(2,1)S(1)} %collective-permute-done.9.refs_1_), channel_id=1, source_target_pairs={{0,16},{16,0},{32,48},{48,32},{64,80},{80,64},{96,112},{112,96},{1... | collective-permute-start | bytes 786440 | tf_op jit(solution)/shard_map/ppermute | solution.py:284
  92.3 7.8 %collective-permute-start.20 = (bf16[256,512]{1,0:T(8,128)(2,1)S(1)}, bf16[256,512]{1,0:T(8,128)(2,1)S(1)}, u32[]{:S(2)}, u32[]{:S(2)}) collective-permute-start(bf16[256,512]{1,0:T(8,128)(2,1)S(1)} %collective-permute-done.10.refs_2_), channel_id=1, source_target_pairs={{0,16},{16,0},{32,48},{48,32},{64,80},{80,64},{96,112},{112,96},{1... | collective-permute-start | bytes 786440 | tf_op jit(solution)/shard_map/ppermute | solution.py:284
  99.4 1.6 %collective-permute-start.21 = (bf16[256,512]{1,0:T(8,128)(2,1)S(1)}, bf16[256,512]{1,0:T(8,128)(2,1)S(1)}, u32[]{:S(2)}, u32[]{:S(2)}) collective-permute-start(bf16[256,512]{1,0:T(8,128)(2,1)S(1)} %collective-permute-done.13.refs_3_), channel_id=1, source_target_pairs={{0,16},{16,0},{32,48},{48,32},{64,80},{80,64},{96,112},{112,96},{1... | collective-permute-start | bytes 786440 | tf_op jit(solution)/shard_map/ppermute | solution.py:284
  99.9 1.5 collective-permute-start.22
  100.1 5.1 %copy-start.2 = (s32[8,12]{1,0:T(8,128)S(1)}, s32[8,12]{1,0:T(8,128)}, u32[]{:S(2)}) copy-start(s32[8,12]{1,0:T(8,128)} %rel_ref.1) | copy-start | bytes 1156
  101.4 3.8 %copy-start = (bf16[8,12,128,128]{3,2,1,0:T(8,128)(2,1)S(1)}, bf16[8,12,128,128]{3,2,1,0:T(8,128)(2,1)}, u32[]{:S(2)}) copy-start(bf16[8,12,128,128]{3,2,1,0:T(8,128)(2,1)} %caps.1.cap_ref) | copy-start | bytes 9437188

commit v17 on v16

--- a/solution.py
+++ b/solution.py
@@ -56,15 +56,9 @@
     n_pieces = sum(len(p) for p in bounds)
     pieces = refs[:n_pieces]
     rw_ref, src_ref = refs[n_pieces : n_pieces + 2]
-    val_ref, score_ref, hid_ref, sem = refs[-4:]
+    val_ref, score_ref, hid_ref = refs[-3:]
     relations, block = val_ref.shape[1:3]
-    cap = sem.shape[1]
-
-    def copy(piece, row, source, c):
-        return pltpu.make_async_copy(
-            piece.at[pl.ds(row, block)], hid_ref.at[source, pl.ds(c * block, block)], sem.at[source, c]
-        )
-
+    cap = index[0].shape[1]
     begin = 0
     for source in range(len(bounds)):
         for c in range(cap):
@@ -73,12 +67,11 @@
 
                 @pl.when((wanted >= low) & (wanted < high))
                 def _():
-                    copy(pieces[begin + n], pl.multiple_of((wanted - low) * block, block), source, c).start()
+                    row = pl.multiple_of((wanted - low) * block, block)
+                    hid_ref[source, c * block : (c + 1) * block] = pieces[begin + n][pl.ds(row, block), :]
 
         begin += len(bounds[source])
     for source in range(len(bounds)):
-        for c in range(cap):
-            copy(pieces[0], 0, source, c).wait()
         hid = hid_ref[source]
         at = (first + source) * cap
         for r in range(relations):
@@ -90,22 +83,20 @@
         for c in range(cap):
             score_ref[at + c] = score[:, c * block : (c + 1) * block]
 
+
 def transform(sources, peers, first, index, relation_weight, src_vectors, block, values, scores):
     bounds = tuple(tuple((low, high) for _, low, high in pieces) for pieces in sources)
     arrays = [array for pieces in sources for array, _, _ in pieces]
     cap = index[0].shape[1]
     relations, width = relation_weight.shape[:2]
-    anywhere, inside = pl.BlockSpec(memory_space=pl.ANY), pl.BlockSpec(memory_space=pltpu.VMEM)
+    inside = pl.BlockSpec(memory_space=pltpu.VMEM)
     kept = () if values is None else (values, scores)
     at = len(index) + len(arrays) + 2
     return pl.pallas_call(
         functools.partial(transform_kernel, bounds, first),
-        in_specs=[pl.BlockSpec(memory_space=pltpu.SMEM)] * len(index) + [anywhere] * len(arrays) + [inside] * (2 + len(kept)),
+        in_specs=[pl.BlockSpec(memory_space=pltpu.SMEM)] * len(index) + [inside] * (len(arrays) + 2 + len(kept)),
         out_specs=[inside, inside],
-        scratch_shapes=[
-            pltpu.VMEM((len(bounds), cap * block, width), BF16),
-            pltpu.SemaphoreType.DMA((len(bounds), cap)),
-        ],
+        scratch_shapes=[pltpu.VMEM((len(bounds), cap * block, width), BF16)],
         out_shape=[
             jax.ShapeDtypeStruct((peers * cap, relations, block, width), BF16),
             jax.ShapeDtypeStruct((peers * cap, 8, block), F32),
@@ -134,13 +125,13 @@
 
 
 def attend_kernel(
-    rel_ref, slot_ref, own_ref, cap_ref, tgt_ref, val_ref, score_ref, out_ref, u_ref, w_ref, prob_ref
+    rel_ref, slot_ref, own_ref, cap_ref, tgt_ref, val_ref, score_ref, out_ref, u_ref, w_ref, prob_ref, least_ref
 ):
     blocks, lists, rows, cols = cap_ref.shape
     relations = u_ref.shape[1]
     ones = jnp.ones((lists * cols, cols), BF16)
 
-    def body(b, carry):
+    def parts(b):
         own = own_ref[b]
         target = jnp.dot(own, tgt_ref[0], preferred_element_type=F32)
         target += jnp.dot(own, tgt_ref[1], preferred_element_type=F32)
@@ -151,15 +142,19 @@
         def spread(r, h):
             return jnp.broadcast_to(target[:, r * HEADS + h : r * HEADS + h + 1], (rows, cols))
 
-        def finish(h):
+        def finish(h, weights):
             lanes = slice(h * cols, (h + 1) * cols)
             value = jnp.concatenate([val_ref[slots[k], rels[k], :, lanes] for k in range(lists)], axis=0)
-            summed = jnp.dot(prob_ref[h], jnp.concatenate([value, ones], axis=1), preferred_element_type=F32)
+            summed = jnp.dot(weights, jnp.concatenate([value, ones], axis=1), preferred_element_type=F32)
             total = summed[:, cols:]
             mixed = summed[:, :cols] / total + own[:, lanes].astype(F32)
             out_ref[b, :, lanes] = jnp.where(mixed > 0, mixed, jnp.exp(jnp.minimum(mixed, 0.0)) - 1.0).astype(BF16)
             return total
 
+        return rels, slots, spread, finish
+
+    def body(b, carry):
+        rels, slots, spread, finish = parts(b)
         reach = [jnp.full((8, cols), -jnp.inf, F32) for _ in range(relations)]
         for k in range(lists):
             source = score_ref[slots[k]]
@@ -176,45 +171,52 @@
                 w_ref[h, r] = 0.2 * spread(r, h) - bound
         least = jnp.full((rows, cols), jnp.inf, F32)
         for h in range(HEADS):
+            probs = []
             for k in range(lists):
                 source = score_ref[slots[k], pl.ds(rels[k] * HEADS + h, 1), :]
                 logit = jnp.maximum(u_ref[h, rels[k]] + source, w_ref[h, rels[k]] + 0.2 * source)
                 prob = jnp.exp2(logit).astype(BF16)
-                prob_ref[h, :, k * cols : (k + 1) * cols] = jnp.minimum(prob, cap_ref[b, k])
+                probs.append(jnp.minimum(prob, cap_ref[b, k]))
+            least = jnp.minimum(least, finish(h, jnp.concatenate(probs, axis=1)))
+
+        least_ref[...] = jnp.minimum(least_ref[...], least)
+        return carry
+
+    least_ref[...] = jnp.full(least_ref.shape, jnp.inf, F32)
+    lax.fori_loop(0, blocks, body, 0)
+
+    def redo(b, carry):
+        _, _, spread, finish = parts(b)
         for h in range(HEADS):
-            least = jnp.minimum(least, finish(h))
-
-        @pl.when(jnp.logical_not(jnp.min(least) > 2.0**-90))
-        def _():
-            for h in range(HEADS):
-                for r in range(relations):
-                    u_ref[h, r] = spread(r, h)
-
-                def raw(k):
-                    r, slot = rel_ref[b, k], slot_ref[b, k]
-                    x = u_ref[h, r] + score_ref[slot, pl.ds(r * HEADS + h, 1), :]
-                    return jnp.where(cap_ref[b, k].astype(F32) > 0, jnp.maximum(x, 0.2 * x), -jnp.inf)
-
-                w_ref[h, 0] = jnp.full((rows, cols), -jnp.inf, F32)
-
-                def climb(k, carry):
-                    w_ref[h, 0] = jnp.maximum(w_ref[h, 0], raw(k))
-                    return carry
-
-                lax.fori_loop(0, lists, climb, 0)
-                w_ref[h, 0] = jnp.broadcast_to(jnp.max(w_ref[h, 0], axis=1, keepdims=True), (rows, cols))
-
-                def weigh(k, carry):
-                    at = pl.ds(pl.multiple_of(k * cols, cols), cols)
-                    prob_ref[h, :, at] = jnp.exp2(raw(k) - w_ref[h, 0]).astype(BF16)
-                    return carry
-
-                lax.fori_loop(0, lists, weigh, 0)
-                finish(h)
-
+            for r in range(relations):
+                u_ref[h, r] = spread(r, h)
+
+            def raw(k):
+                r, slot = rel_ref[b, k], slot_ref[b, k]
+                x = u_ref[h, r] + score_ref[slot, pl.ds(r * HEADS + h, 1), :]
+                return jnp.where(cap_ref[b, k].astype(F32) > 0, jnp.maximum(x, 0.2 * x), -jnp.inf)
+
+            w_ref[h, 0] = jnp.full((rows, cols), -jnp.inf, F32)
+
+            def climb(k, carry):
+                w_ref[h, 0] = jnp.maximum(w_ref[h, 0], raw(k))
+                return carry
+
+            lax.fori_loop(0, lists, climb, 0)
+            w_ref[h, 0] = jnp.broadcast_to(jnp.max(w_ref[h, 0], axis=1, keepdims=True), (rows, cols))
+
+            def weigh(k, carry):
+                at = pl.ds(pl.multiple_of(k * cols, cols), cols)
+                prob_ref[h, :, at] = jnp.exp2(raw(k) - w_ref[h, 0]).astype(BF16)
+                return carry
+
+            lax.fori_loop(0, lists, weigh, 0)
+            finish(h, prob_ref[h])
         return carry
 
-    lax.fori_loop(0, blocks, body, 0)
+    @pl.when(jnp.logical_not(jnp.min(least_ref[...]) > 2.0**-90))
+    def _():
+        lax.fori_loop(0, blocks, redo, 0)
 
 
 def attend(hidden, cap, relation_ids, source_slots, values, scores, tgt_vectors):
@@ -230,6 +232,7 @@
             pltpu.VMEM((HEADS, relations, rows, cols), F32),
             pltpu.VMEM((HEADS, relations, rows, cols), F32),
             pltpu.VMEM((HEADS, rows, lists * cols), BF16),
+            pltpu.VMEM((rows, cols), F32),
         ],
         out_shape=jax.ShapeDtypeStruct((blocks, rows, width), BF16),
         compiler_params=pltpu.CompilerParams(vmem_limit_bytes=24 * 1024 * 1024),

time: 158 us -> 155 us (0.981)
  Pallas kernels: 80.5 us -> 74.3 us
  waiting for transfers between devices: 33.9 us -> 36.7 us
    pallas_call x3, Pallas kernels: 14 us -> 8.86 us  [transform(): pl.pallas_call(functools.partial(transform_kernel, bounds, first), in_spe...]
    ppermute x23, waiting for transfers between devices: 21.6 us -> 24.4 us  [send(): return lax.ppermute(x, 'graph', pairs)]
  transfers between devices with their start and end apart: 25 -> 25, of which waited for: 6 -> 7; matrix products, arithmetic and copies ran while one was open for 5% -> 5% of each run, Pallas kernels for 13% -> 11%
where the time goes in v17:
time: 155 us; the launch traced here: 154 us
  Pallas kernels  74.3 us (48%)
  waiting for transfers between devices  36.7 us (24%)
  starting transfers between devices  34.6 us (22%)
  matrix products  6.17 us (4%)
    pallas_call x1, Pallas kernels, attend(): pl.pallas_call(attend_kernel, in_specs=[scalars] * 2 + [inside] * 5, out_...  51.3 us
    ppermute x23, waiting for transfers between devices, send(): return lax.ppermute(x, 'graph', pairs)  24.4 us
    ppermute x23, starting transfers between devices, send(): return lax.ppermute(x, 'graph', pairs)  23.4 us
    all_to_all x1, waiting for transfers between devices, shards(): lax.all_to_all(first, 'feat', 0, 0, tiled=True)  12.3 us
    pallas_call x3, Pallas kernels, transform(): pl.pallas_call(functools.partial(transform_kernel, bounds, first), in_spe...  8.86 us
    pallas_call x2, Pallas kernels, arrange(): pl.pallas_call(functools.partial(arrange_kernel, low, high), grid_spec=pl...  7.27 us
    pallas_call x1, Pallas kernels, caps(): pl.pallas_call(cap_kernel, grid=shape[:1], in_specs=[spec], out_specs=spe...  6.92 us
    all_to_all x1, starting transfers between devices, shards(): lax.all_to_all(first, 'feat', 0, 0, tiled=True)  6.84 us
  transfers between devices with their start and end apart: 25, of which 7 were waited for; matrix products, arithmetic and copies ran while one was open for 5% of the time, Pallas kernels for 11%

profile of v17, /device:TPU:1, one launch (start us, length us, event | category | flops | bytes accessed | tf_op | source)
XLA Modules:
  0.0 154.2 jit_solution(6555973184864355388)
XLA Ops:
  0.0 3.7 %arrange.2 = bf16[16,64,768]{2,1,0:T(8,128)(2,1)} custom-call(s32[1]{0:T(128)} %bitcast.core_ref, bf16[64,16384]{1,0:T(8,128)(2,1)} %bitcast.30, bf16[64,512]{1,0:T(8,128)(2,1)} %w_ref.3), custom_call_target="tpu_custom_call" | custom-call | tf_op jit(solution)/shard_map/arrange/pallas_call | solution.py:31
  3.7 1.5 collective-permute-start
  5.2 6.8 %all-to-all-start = ((bf16[16,64,768]{2,1,0:T(8,128)(2,1)}), bf16[16,64,768]{2,1,0:T(8,128)(2,1)S(1)}, u32[]{:S(2)}, u32[]{:S(2)}) async-start(bf16[16,64,768]{2,1,0:T(8,128)(2,1)} %arrange.2), calls=%async_computation | async-start | bytes 3145728 | tf_op jit(solution)/shard_map/all_to_all | solution.py:294
  12.1 0.0 copy-start.4
  12.1 0.9 fusion
  13.1 3.6 %arrange.3 = bf16[16,64,512]{2,1,0:T(8,128)(2,1)} custom-call(s32[1]{0:T(128)} %bitcast.core_ref, bf16[64,16384]{1,0:T(8,128)(2,1)} %bitcast.31, bf16[64,512]{1,0:T(8,128)(2,1)} %w_ref.3), custom_call_target="tpu_custom_call" | custom-call | tf_op jit(solution)/shard_map/arrange/pallas_call | solution.py:31
  16.7 0.1 copy.15
  16.9 0.0 copy-start.6
  16.9 6.9 %caps.1.cap_ref = bf16[8,12,128,128]{3,2,1,0:T(8,128)(2,1)} custom-call(s32[8,12,128,128]{3,2,1,0:T(8,128)} %mask_ref.1), custom_call_target="tpu_custom_call" | custom-call | tf_op jit(solution)/shard_map/caps/pallas_call | solution.py:117
  23.8 0.1 pad.19.clone
  23.9 0.1 select_multiply_fusion
  24.1 0.1 fusion.6
  24.3 0.1 maximum_maximum_fusion.refs_6_.refs_11_.refs_10_
  24.3 0.0 collective-permute-done
  24.3 0.3 fusion.10
  24.6 12.3 %all-to-all-done = bf16[16,64,768]{2,1,0:T(8,128)(2,1)S(1)} async-done(((bf16[16,64,768]{2,1,0:T(8,128)(2,1)}), bf16[16,64,768]{2,1,0:T(8,128)(2,1)S(1)}, u32[]{:S(2)}, u32[]{:S(2)}) %all-to-all-start) | async-done | bytes 1572896 | tf_op jit(solution)/shard_map/all_to_all | solution.py:294
  36.9 0.9 slice.19
  37.8 1.3 collective-permute-start.1
  39.1 4.3 %all-to-all-start.1 = ((bf16[16,64,512]{2,1,0:T(8,128)(2,1)}), bf16[16,64,512]{2,1,0:T(8,128)(2,1)}, u32[]{:S(2)}, u32[]{:S(2)}) async-start(bf16[16,64,512]{2,1,0:T(8,128)(2,1)} %arrange.3), calls=%async_computation.1 | async-start | bytes 2097152 | tf_op jit(solution)/shard_map/all_to_all | solution.py:307
  43.5 0.0 collective-permute-done.1
  43.5 2.7 %convolution_convert_fusion.1.refs_1_ = bf16[512,512]{1,0:T(8,128)(2,1)S(1)} fusion(bf16[1024,768]{1,0:T(8,128)(2,1)} %bitcast.33, bf16[1024,256]{1,0:T(8,128)(2,1)} %collective-permute-done.1, bf16[1024,256]{1,0:T(8,128)(2,1)} %slice.19, pred[]{:T(512)S(6)} %eq.30), kind=kOutput, calls=%fused_computation.1 | convolution fusion | flops 541851648 | bytes 2621441 | tf_op jit(solution)/shard_map/dot_general | solution.py:314
  46.1 1.7 %collective-permute-start.2 = (bf16[512,512]{1,0:T(8,128)(2,1)S(1)}, bf16[512,512]{1,0:T(8,128)(2,1)S(1)}, u32[]{:S(2)}, u32[]{:S(2)}) collective-permute-start(bf16[512,512]{1,0:T(8,128)(2,1)S(1)} %convolution_convert_fusion.1.refs_1_), channel_id=1, source_target_pairs={{0,32},{16,48},{32,64},{48,80},{64,96},{80,112},{96,0},{112,16},{1... | collective-permute-start | bytes 1572872 | tf_op jit(solution)/shard_map/ppermute | solution.py:287
  47.9 2.2 %collective-permute-start.3 = (bf16[512,512]{1,0:T(8,128)(2,1)S(1)}, bf16[512,512]{1,0:T(8,128)(2,1)S(1)}, u32[]{:S(2)}, u32[]{:S(2)}) collective-permute-start(bf16[512,512]{1,0:T(8,128)(2,1)S(1)} %convolution_convert_fusion.1.refs_1_), channel_id=1, source_target_pairs={{0,96},{16,112},{32,0},{48,16},{64,32},{80,48},{96,64},{112,80},{1... | collective-permute-start | bytes 1572872 | tf_op jit(solution)/shard_map/ppermute | solution.py:287
  50.1 0.0 collective-permute-start.4
  50.1 2.6 %collective-permute-start.5 = (s32[2,4]{1,0:T(2,128)S(1)}, s32[2,4]{1,0:T(2,128)S(1)}, u32[]{:S(2)}, u32[]{:S(2)}) collective-permute-start(s32[2,4]{1,0:T(2,128)S(1)} %get-tuple-element.47), channel_id=1, source_target_pairs={{0,64},{16,80},{32,96},{48,112},{64,0},{80,16},{96,32},{112,48},{1... | collective-permute-start | bytes 104 | tf_op jit(solution)/shard_map/ppermute | solution.py:287
  52.6 0.7 collective-permute-start.6
  53.3 9.0 %collective-permute-done.4.refs_0_ = s32[2,4]{1,0:T(2,128)S(1)} collective-permute-done((s32[2,4]{1,0:T(2,128)S(1)}, s32[2,4]{1,0:T(2,128)S(1)}, u32[]{:S(2)}, u32[]{:S(2)}) %collective-permute-start.4) | collective-permute-done | bytes 64 | tf_op jit(solution)/shard_map/ppermute | solution.py:287
  62.4 0.5 collective-permute-start.11
  62.9 0.2 collective-permute-done.5.refs_0_
  63.1 0.0 collective-permute-done.6.refs_1_
  63.1 0.0 collective-permute-done.3.refs_6_
  63.1 2.6 %convolution_convert_fusion.refs_2_ = bf16[512,512]{1,0:T(8,128)(2,1)S(1)} fusion(bf16[1024,512]{1,0:T(8,128)(2,1)} %bitcast.11, bf16[1024,256]{1,0:T(8,128)(2,1)} %collective-permute-done.1, bf16[1024,256]{1,0:T(8,128)(2,1)} %slice.19, pred[]{:T(512)S(6)} %eq.30), kind=kOutput, calls=%fused_computation | convolution fusion | flops 541851648 | bytes 2621441 | tf_op jit(solution)/shard_map/dot_general | solution.py:314
  65.7 1.1 collective-permute-start.12
  66.8 1.0 collective-permute-start.7
  67.8 2.1 %collective-permute-start.8 = (bf16[512,512]{1,0:T(8,128)(2,1)S(1)}, bf16[512,512]{1,0:T(8,128)(2,1)S(1)}, u32[]{:S(2)}, u32[]{:S(2)}) collective-permute-start(bf16[512,512]{1,0:T(8,128)(2,1)S(1)} %convolution_convert_fusion.refs_2_), channel_id=1, source_target_pairs={{0,96},{16,112},{32,0},{48,16},{64,32},{80,48},{96,64},{112,80},{1... | collective-permute-start | bytes 1572872 | tf_op jit(solution)/shard_map/ppermute | solution.py:287
  69.9 1.5 %collective-permute-start.10 = (bf16[256,512]{1,0:T(8,128)(2,1)S(1)}, bf16[256,512]{1,0:T(8,128)(2,1)S(1)}, u32[]{:S(2)}, u32[]{:S(2)}) collective-permute-start(bf16[256,512]{1,0:T(8,128)(2,1)S(1)} %slice.21), channel_id=1, source_target_pairs={{0,96},{16,112},{32,0},{48,16},{64,32},{80,48},{96,64},{112,80},{1... | collective-permute-start | bytes 786440 | tf_op jit(solution)/shard_map/ppermute | solution.py:287
  71.5 0.0 collective-permute-done.11.refs_3_
  71.5 0.1 collective-permute-start.9
  71.6 1.0 collective-permute-start.15
  72.6 2.7 %transform.3 = (bf16[32,2,128,512]{3,2,1,0:T(8,128)(2,1)S(1)}, f32[32,8,128]{2,1,0:T(8,128)S(1)}) custom-call(s32[2,4]{1,0:T(2,128)S(1)} %get-tuple-element.55.refs_0_, bf16[512,512]{1,0:T(8,128)(2,1)S(1)} %convolution_convert_fusion.1.refs_1_, bf16[512,512]{1,0:T(8,128)(2,1)S(1)} %convolution_convert_fusion.refs_2_, ...), custom_call_target="tpu_custom_call" | custom-call | tf_op jit(solution)/shard_map/transform/pallas_call | solution.py:95
  75.3 11.7 %collective-permute-done.10.refs_2_ = bf16[256,512]{1,0:T(8,128)(2,1)S(1)} collective-permute-done((bf16[256,512]{1,0:T(8,128)(2,1)S(1)}, bf16[256,512]{1,0:T(8,128)(2,1)S(1)}, u32[]{:S(2)}, u32[]{:S(2)}) %collective-permute-start.10) | collective-permute-done | bytes 262176 | tf_op jit(solution)/shard_map/ppermute | solution.py:287
  87.0 1.0 collective-permute-start.17
  87.9 0.0 collective-permute-done.8.refs_7_
  88.0 0.5 collective-permute-start.16
  88.4 0.1 collective-permute-start.18
  88.6 1.5 %collective-permute-start.13 = (bf16[256,512]{1,0:T(8,128)(2,1)S(1)}, bf16[256,512]{1,0:T(8,128)(2,1)S(1)}, u32[]{:S(2)}, u32[]{:S(2)}) collective-permute-start(bf16[256,512]{1,0:T(8,128)(2,1)S(1)} %slice.22), channel_id=1, source_target_pairs={{0,32},{16,48},{32,64},{48,80},{64,96},{80,112},{96,0},{112,16},{1... | collective-permute-start | bytes 786440 | tf_op jit(solution)/shard_map/ppermute | solution.py:287
  90.1 1.8 %collective-permute-start.14 = (bf16[256,512]{1,0:T(8,128)(2,1)S(1)}, bf16[256,512]{1,0:T(8,128)(2,1)S(1)}, u32[]{:S(2)}, u32[]{:S(2)}) collective-permute-start(bf16[256,512]{1,0:T(8,128)(2,1)S(1)} %slice.23), channel_id=1, source_target_pairs={{0,96},{16,112},{32,0},{48,16},{64,32},{80,48},{96,64},{112,80},{1... | collective-permute-start | bytes 786440 | tf_op jit(solution)/shard_map/ppermute | solution.py:287
  91.9 0.0 collective-permute-done.17.refs_8_
  91.9 0.4 collective-permute-start.19
  92.3 0.1 collective-permute-start.20
  92.4 0.0 collective-permute-done.18.refs_9_
  92.4 3.9 %transform.4 = (bf16[32,2,128,512]{3,2,1,0:T(8,128)(2,1)S(1)}, f32[32,8,128]{2,1,0:T(8,128)S(1)}) custom-call(s32[2,4]{1,0:T(2,128)S(1)} %collective-permute-done.4.refs_0_, s32[2,4]{1,0:T(2,128)S(1)} %collective-permute-done.6.refs_1_, bf16[512,512]{1,0:T(8,128)(2,1)S(1)} %collective-permute-done.2.refs_2_, ...), custom_call_target="tpu_custom_call", output_to_operand_aliasing={{0}: (12, {}), {1}: (13, {})} | custom-call | tf_op jit(solution)/shard_map/transform/pallas_call | solution.py:95
  96.3 2.0 %collective-permute-done.13.refs_3_ = bf16[256,512]{1,0:T(8,128)(2,1)S(1)} collective-permute-done((bf16[256,512]{1,0:T(8,128)(2,1)S(1)}, bf16[256,512]{1,0:T(8,128)(2,1)S(1)}, u32[]{:S(2)}, u32[]{:S(2)}) %collective-permute-start.13) | collective-permute-done | bytes 262176 | tf_op jit(solution)/shard_map/ppermute | solution.py:287
  98.4 0.0 collective-permute-done.14.refs_4_
  98.4 0.7 collective-permute-start.21
  99.1 0.0 collective-permute-start.22
  99.1 0.1 pad_maximum_fusion
  99.1 0.0 copy-start.2
  99.2 0.0 collective-permute-done.19.refs_5_
  99.2 1.1 collective-permute-done.21.refs_7_
  100.2 0.4 collective-permute-done.22.refs_8_
  100.6 2.3 %transform.5 = (bf16[32,2,128,512]{3,2,1,0:T(8,128)(2,1)S(1)}, f32[32,8,128]{2,1,0:T(8,128)S(1)}) custom-call(s32[2,4]{1,0:T(2,128)S(1)} %collective-permute-done.5.refs_0_, bf16[256,512]{1,0:T(8,128)(2,1)S(1)} %collective-permute-done.9.refs_1_, ...), custom_call_target="tpu_custom_call", output_to_operand_aliasing={{0}: (11, {}), {1}: (12, {})} | custom-call | tf_op jit(solution)/shard_map/transform/pallas_call | solution.py:95
  102.9 0.0 copy-done
  102.9 51.3 %attend.1 = bf16[8,128,512]{2,1,0:T(8,128)(2,1)} custom-call(s32[8,12]{1,0:T(8,128)S(1)} %copy-done.2, s32[8,12]{1,0:T(8,128)S(1)} %fusion.23.slot_ref, bf16[8,128,512]{2,1,0:T(8,128)(2,1)S(1)} %bitcast.29, bf16[8,12,128,128]{3,2,1,0:T(8,128)(2,1)S(1)} %copy-done, bf16[3,512,128]{2,1,0:T(8,128)(2,1)S(1)} %pad_maximum_fusion.1.tgt_ref, ...), custom_call_target="tpu_custom_call" | custom-call | tf_op jit(solution)/shard_map/attend/pallas_call | solution.py:227
  (35 shorter events, 0.3 us)
Async XLA Ops:
  0.0 3.7 %copy-start.7 = (s32[1,8,4]{1,2,0:T(4,128)S(1)}, s32[1,8,4]{1,2,0:T(4,128)}, u32[]{:S(2)}) copy-start(s32[1,8,4]{1,2,0:T(4,128)} %param.16) | copy-start | bytes 388
  3.7 8.4 %copy-start.5 = (f32[2,512]{1,0:T(2,128)S(1)}, f32[2,512]{1,0:T(2,128)}, u32[]{:S(2)}) copy-start(f32[2,512]{1,0:T(2,128)} %param.12) | copy-start | bytes 12292
  3.7 8.4 %copy-start.1 = (bf16[2,512,512]{2,1,0:T(8,128)(2,1)S(1)}, bf16[2,512,512]{2,1,0:T(8,128)(2,1)}, u32[]{:S(2)}) copy-start(bf16[2,512,512]{2,1,0:T(8,128)(2,1)} %refs_9_.1) | copy-start | bytes 3145732
  3.7 20.6 %collective-permute-start = (s32[8,4]{0,1:T(4,128)S(1)}, s32[8,4]{0,1:T(4,128)S(1)}, u32[]{:S(2)}, u32[]{:S(2)}) collective-permute-start(s32[8,4]{0,1:T(4,128)S(1)} %bitcast.36), channel_id=1, source_target_pairs={{0,16},{16,0},{32,48},{48,32},{64,80},{80,64},{96,112},{112,96},{1... | collective-permute-start | bytes 392 | tf_op jit(solution)/shard_map/ppermute | solution.py:287
  5.2 31.7 %all-to-all-start = ((bf16[16,64,768]{2,1,0:T(8,128)(2,1)}), bf16[16,64,768]{2,1,0:T(8,128)(2,1)S(1)}, u32[]{:S(2)}, u32[]{:S(2)}) async-start(bf16[16,64,768]{2,1,0:T(8,128)(2,1)} %arrange.2), calls=%async_computation | async-start | bytes 3145728 | tf_op jit(solution)/shard_map/all_to_all | solution.py:294
  12.1 4.6 %copy-start.4 = (f32[2,512]{1,0:T(2,128)S(1)}, f32[2,512]{1,0:T(2,128)}, u32[]{:S(2)}) copy-start(f32[2,512]{1,0:T(2,128)} %param.13) | copy-start | bytes 12292
  16.9 7.3 %copy-start.6 = (s32[8,12]{1,0:T(8,128)S(1)}, s32[8,12]{1,0:T(8,128)}, u32[]{:S(2)}) copy-start(s32[8,12]{1,0:T(8,128)} %param.17) | copy-start | bytes 1156
  36.9 6.5 %copy-start.3 = (bf16[16,64,768]{2,1,0:T(8,128)(2,1)}, bf16[16,64,768]{2,1,0:T(8,128)(2,1)S(1)}, u32[]{:S(2)}) copy-start(bf16[16,64,768]{2,1,0:T(8,128)(2,1)S(1)} %all-to-all-done) | copy-start | bytes 4718596
  37.8 5.6 %collective-permute-start.1 = (bf16[1024,256]{1,0:T(8,128)(2,1)}, bf16[1024,256]{1,0:T(8,128)(2,1)}, u32[]{:S(2)}, u32[]{:S(2)}) collective-permute-start(bf16[1024,256]{1,0:T(8,128)(2,1)} %slice.19), channel_id=1, source_target_pairs={{0,16},{16,0},{32,48},{48,32},{64,80},{80,64},{96,112},{112,96},{1... | collective-permute-start | bytes 1572872 | tf_op jit(solution)/shard_map/ppermute | solution.py:287
  39.1 24.0 %all-to-all-start.1 = ((bf16[16,64,512]{2,1,0:T(8,128)(2,1)}), bf16[16,64,512]{2,1,0:T(8,128)(2,1)}, u32[]{:S(2)}, u32[]{:S(2)}) async-start(bf16[16,64,512]{2,1,0:T(8,128)(2,1)} %arrange.3), calls=%async_computation.1 | async-start | bytes 2097152 | tf_op jit(solution)/shard_map/all_to_all | solution.py:307
  46.1 16.9 %collective-permute-start.2 = (bf16[512,512]{1,0:T(8,128)(2,1)S(1)}, bf16[512,512]{1,0:T(8,128)(2,1)S(1)}, u32[]{:S(2)}, u32[]{:S(2)}) collective-permute-start(bf16[512,512]{1,0:T(8,128)(2,1)S(1)} %convolution_convert_fusion.1.refs_1_), channel_id=1, source_target_pairs={{0,32},{16,48},{32,64},{48,80},{64,96},{80,112},{96,0},{112,16},{1... | collective-permute-start | bytes 1572872 | tf_op jit(solution)/shard_map/ppermute | solution.py:287
  47.9 15.2 %collective-permute-start.3 = (bf16[512,512]{1,0:T(8,128)(2,1)S(1)}, bf16[512,512]{1,0:T(8,128)(2,1)S(1)}, u32[]{:S(2)}, u32[]{:S(2)}) collective-permute-start(bf16[512,512]{1,0:T(8,128)(2,1)S(1)} %convolution_convert_fusion.1.refs_1_), channel_id=1, source_target_pairs={{0,96},{16,112},{32,0},{48,16},{64,32},{80,48},{96,64},{112,80},{1... | collective-permute-start | bytes 1572872 | tf_op jit(solution)/shard_map/ppermute | solution.py:287
  50.1 12.3 %collective-permute-start.4 = (s32[2,4]{1,0:T(2,128)S(1)}, s32[2,4]{1,0:T(2,128)S(1)}, u32[]{:S(2)}, u32[]{:S(2)}) collective-permute-start(s32[2,4]{1,0:T(2,128)S(1)} %get-tuple-element.46), channel_id=1, source_target_pairs={{0,32},{16,48},{32,64},{48,80},{64,96},{80,112},{96,0},{112,16},{1... | collective-permute-start | bytes 104 | tf_op jit(solution)/shard_map/ppermute | solution.py:287
  50.1 13.0 %collective-permute-start.5 = (s32[2,4]{1,0:T(2,128)S(1)}, s32[2,4]{1,0:T(2,128)S(1)}, u32[]{:S(2)}, u32[]{:S(2)}) collective-permute-start(s32[2,4]{1,0:T(2,128)S(1)} %get-tuple-element.47), channel_id=1, source_target_pairs={{0,64},{16,80},{32,96},{48,112},{64,0},{80,16},{96,32},{112,48},{1... | collective-permute-start | bytes 104 | tf_op jit(solution)/shard_map/ppermute | solution.py:287
  52.6 10.5 %collective-permute-start.6 = (s32[2,4]{1,0:T(2,128)S(1)}, s32[2,4]{1,0:T(2,128)S(1)}, u32[]{:S(2)}, u32[]{:S(2)}) collective-permute-start(s32[2,4]{1,0:T(2,128)S(1)} %get-tuple-element.48), channel_id=1, source_target_pairs={{0,96},{16,112},{32,0},{48,16},{64,32},{80,48},{96,64},{112,80},{1... | collective-permute-start | bytes 104 | tf_op jit(solution)/shard_map/ppermute | solution.py:287
  62.4 9.1 %collective-permute-start.11 = (bf16[512,512]{1,0:T(8,128)(2,1)S(1)}, bf16[512,512]{1,0:T(8,128)(2,1)}, u32[]{:S(2)}, u32[]{:S(2)}) collective-permute-start(bf16[512,512]{1,0:T(8,128)(2,1)S(1)} %convolution_convert_fusion.1.refs_1_), channel_id=1, source_target_pairs={{0,16},{16,0},{32,48},{48,32},{64,80},{80,64},{96,112},{112,96},{1... | collective-permute-start | bytes 1572872 | tf_op jit(solution)/shard_map/ppermute | solution.py:287
  65.7 5.9 %collective-permute-start.12 = (bf16[512,512]{1,0:T(8,128)(2,1)S(1)}, bf16[512,512]{1,0:T(8,128)(2,1)S(1)}, u32[]{:S(2)}, u32[]{:S(2)}) collective-permute-start(bf16[512,512]{1,0:T(8,128)(2,1)S(1)} %convolution_convert_fusion.refs_2_), channel_id=1, source_target_pairs={{0,16},{16,0},{32,48},{48,32},{64,80},{80,64},{96,112},{112,96},{1... | collective-permute-start | bytes 1572872 | tf_op jit(solution)/shard_map/ppermute | solution.py:287
  66.8 21.2 %collective-permute-start.7 = (bf16[512,512]{1,0:T(8,128)(2,1)S(1)}, bf16[512,512]{1,0:T(8,128)(2,1)S(1)}, u32[]{:S(2)}, u32[]{:S(2)}) collective-permute-start(bf16[512,512]{1,0:T(8,128)(2,1)S(1)} %convolution_convert_fusion.refs_2_), channel_id=1, source_target_pairs={{0,32},{16,48},{32,64},{48,80},{64,96},{80,112},{96,0},{112,16},{1... | collective-permute-start | bytes 1572872 | tf_op jit(solution)/shard_map/ppermute | solution.py:287
  67.8 20.2 %collective-permute-start.8 = (bf16[512,512]{1,0:T(8,128)(2,1)S(1)}, bf16[512,512]{1,0:T(8,128)(2,1)S(1)}, u32[]{:S(2)}, u32[]{:S(2)}) collective-permute-start(bf16[512,512]{1,0:T(8,128)(2,1)S(1)} %convolution_convert_fusion.refs_2_), channel_id=1, source_target_pairs={{0,96},{16,112},{32,0},{48,16},{64,32},{80,48},{96,64},{112,80},{1... | collective-permute-start | bytes 1572872 | tf_op jit(solution)/shard_map/ppermute | solution.py:287
  69.9 17.0 %collective-permute-start.10 = (bf16[256,512]{1,0:T(8,128)(2,1)S(1)}, bf16[256,512]{1,0:T(8,128)(2,1)S(1)}, u32[]{:S(2)}, u32[]{:S(2)}) collective-permute-start(bf16[256,512]{1,0:T(8,128)(2,1)S(1)} %slice.21), channel_id=1, source_target_pairs={{0,96},{16,112},{32,0},{48,16},{64,32},{80,48},{96,64},{112,80},{1... | collective-permute-start | bytes 786440 | tf_op jit(solution)/shard_map/ppermute | solution.py:287
  71.5 16.4 %collective-permute-start.9 = (bf16[256,512]{1,0:T(8,128)(2,1)S(1)}, bf16[256,512]{1,0:T(8,128)(2,1)S(1)}, u32[]{:S(2)}, u32[]{:S(2)}) collective-permute-start(bf16[256,512]{1,0:T(8,128)(2,1)S(1)} %slice.20), channel_id=1, source_target_pairs={{0,32},{16,48},{32,64},{48,80},{64,96},{80,112},{96,0},{112,16},{1... | collective-permute-start | bytes 786440 | tf_op jit(solution)/shard_map/ppermute | solution.py:287
  71.6 18.5 %collective-permute-start.15 = (bf16[512,512]{1,0:T(8,128)(2,1)S(1)}, bf16[512,512]{1,0:T(8,128)(2,1)S(1)}, u32[]{:S(2)}, u32[]{:S(2)}) collective-permute-start(bf16[512,512]{1,0:T(8,128)(2,1)S(1)} %collective-permute-done.2.refs_2_), channel_id=1, source_target_pairs={{0,16},{16,0},{32,48},{48,32},{64,80},{80,64},{96,112},{112,96},{1... | collective-permute-start | bytes 1572872 | tf_op jit(solution)/shard_map/ppermute | solution.py:287
  87.0 4.9 %collective-permute-start.17 = (bf16[512,512]{1,0:T(8,128)(2,1)S(1)}, bf16[512,512]{1,0:T(8,128)(2,1)S(1)}, u32[]{:S(2)}, u32[]{:S(2)}) collective-permute-start(bf16[512,512]{1,0:T(8,128)(2,1)S(1)} %collective-permute-done.3.refs_6_), channel_id=1, source_target_pairs={{0,16},{16,0},{32,48},{48,32},{64,80},{80,64},{96,112},{112,96},{1... | collective-permute-start | bytes 1572872 | tf_op jit(solution)/shard_map/ppermute | solution.py:287
  88.0 4.3 %collective-permute-start.16 = (bf16[512,512]{1,0:T(8,128)(2,1)S(1)}, bf16[512,512]{1,0:T(8,128)(2,1)S(1)}, u32[]{:S(2)}, u32[]{:S(2)}) collective-permute-start(bf16[512,512]{1,0:T(8,128)(2,1)S(1)} %collective-permute-done.7.refs_3_), channel_id=1, source_target_pairs={{0,16},{16,0},{32,48},{48,32},{64,80},{80,64},{96,112},{112,96},{1... | collective-permute-start | bytes 1572872 | tf_op jit(solution)/shard_map/ppermute | solution.py:287
  88.4 4.0 %collective-permute-start.18 = (bf16[512,512]{1,0:T(8,128)(2,1)S(1)}, bf16[512,512]{1,0:T(8,128)(2,1)S(1)}, u32[]{:S(2)}, u32[]{:S(2)}) collective-permute-start(bf16[512,512]{1,0:T(8,128)(2,1)S(1)} %collective-permute-done.8.refs_7_), channel_id=1, source_target_pairs={{0,16},{16,0},{32,48},{48,32},{64,80},{80,64},{96,112},{112,96},{1... | collective-permute-start | bytes 1572872 | tf_op jit(solution)/shard_map/ppermute | solution.py:287
  88.6 9.8 %collective-permute-start.13 = (bf16[256,512]{1,0:T(8,128)(2,1)S(1)}, bf16[256,512]{1,0:T(8,128)(2,1)S(1)}, u32[]{:S(2)}, u32[]{:S(2)}) collective-permute-start(bf16[256,512]{1,0:T(8,128)(2,1)S(1)} %slice.22), channel_id=1, source_target_pairs={{0,32},{16,48},{32,64},{48,80},{64,96},{80,112},{96,0},{112,16},{1... | collective-permute-start | bytes 786440 | tf_op jit(solution)/shard_map/ppermute | solution.py:287
  90.1 8.2 %collective-permute-start.14 = (bf16[256,512]{1,0:T(8,128)(2,1)S(1)}, bf16[256,512]{1,0:T(8,128)(2,1)S(1)}, u32[]{:S(2)}, u32[]{:S(2)}) collective-permute-start(bf16[256,512]{1,0:T(8,128)(2,1)S(1)} %slice.23), channel_id=1, source_target_pairs={{0,96},{16,112},{32,0},{48,16},{64,32},{80,48},{96,64},{112,80},{1... | collective-permute-start | bytes 786440 | tf_op jit(solution)/shard_map/ppermute | solution.py:287
  91.9 7.2 %collective-permute-start.19 = (bf16[256,512]{1,0:T(8,128)(2,1)S(1)}, bf16[256,512]{1,0:T(8,128)(2,1)S(1)}, u32[]{:S(2)}, u32[]{:S(2)}) collective-permute-start(bf16[256,512]{1,0:T(8,128)(2,1)S(1)} %collective-permute-done.9.refs_1_), channel_id=1, source_target_pairs={{0,16},{16,0},{32,48},{48,32},{64,80},{80,64},{96,112},{112,96},{1... | collective-permute-start | bytes 786440 | tf_op jit(solution)/shard_map/ppermute | solution.py:287
  92.3 6.9 %collective-permute-start.20 = (bf16[256,512]{1,0:T(8,128)(2,1)S(1)}, bf16[256,512]{1,0:T(8,128)(2,1)S(1)}, u32[]{:S(2)}, u32[]{:S(2)}) collective-permute-start(bf16[256,512]{1,0:T(8,128)(2,1)S(1)} %collective-permute-done.10.refs_2_), channel_id=1, source_target_pairs={{0,16},{16,0},{32,48},{48,32},{64,80},{80,64},{96,112},{112,96},{1... | collective-permute-start | bytes 786440 | tf_op jit(solution)/shard_map/ppermute | solution.py:287
  98.4 1.8 %collective-permute-start.21 = (bf16[256,512]{1,0:T(8,128)(2,1)S(1)}, bf16[256,512]{1,0:T(8,128)(2,1)S(1)}, u32[]{:S(2)}, u32[]{:S(2)}) collective-permute-start(bf16[256,512]{1,0:T(8,128)(2,1)S(1)} %collective-permute-done.13.refs_3_), channel_id=1, source_target_pairs={{0,16},{16,0},{32,48},{48,32},{64,80},{80,64},{96,112},{112,96},{1... | collective-permute-start | bytes 786440 | tf_op jit(solution)/shard_map/ppermute | solution.py:287
  99.1 1.5 collective-permute-start.22
  99.1 3.7 %copy-start.2 = (s32[8,12]{1,0:T(8,128)S(1)}, s32[8,12]{1,0:T(8,128)}, u32[]{:S(2)}) copy-start(s32[8,12]{1,0:T(8,128)} %rel_ref.1) | copy-start | bytes 1156
  100.6 2.3 %copy-start = (bf16[8,12,128,128]{3,2,1,0:T(8,128)(2,1)S(1)}, bf16[8,12,128,128]{3,2,1,0:T(8,128)(2,1)}, u32[]{:S(2)}) copy-start(bf16[8,12,128,128]{3,2,1,0:T(8,128)(2,1)} %caps.1.cap_ref) | copy-start | bytes 9437188

commit v18 on v17

--- a/solution.py
+++ b/solution.py
@@ -124,8 +124,38 @@
     )(edge_mask)
 
 
+def target_kernel(own_ref, tgt_ref, tile_ref):
+    blocks, relations, _, rows, cols = tile_ref.shape
+
+    def body(b, carry):
+        own = own_ref[b]
+        target = jnp.dot(own, tgt_ref[0], preferred_element_type=F32)
+        target += jnp.dot(own, tgt_ref[1], preferred_element_type=F32)
+        target += jnp.dot(own, tgt_ref[2], preferred_element_type=F32)
+        for r in range(relations):
+            for h in range(HEADS):
+                c = r * HEADS + h
+                tile_ref[b, r, h] = jnp.broadcast_to(target[:, c : c + 1], (rows, cols))
+        return carry
+
+    lax.fori_loop(0, blocks, body, 0)
+
+
+def target_tiles(hidden, tgt_vectors, blocks, relations):
+    rows, width = hidden.shape[0] // blocks, hidden.shape[1]
+    inside = pl.BlockSpec(memory_space=pltpu.VMEM)
+    return pl.pallas_call(
+        target_kernel,
+        in_specs=[inside, inside],
+        out_specs=inside,
+        out_shape=jax.ShapeDtypeStruct((blocks, relations, HEADS, rows, rows), F32),
+        compiler_params=pltpu.CompilerParams(vmem_limit_bytes=8 * 1024 * 1024),
+        name="targets",
+    )(hidden.reshape(blocks, rows, width), tgt_vectors)
+
+
 def attend_kernel(
-    rel_ref, slot_ref, own_ref, cap_ref, tgt_ref, val_ref, score_ref, out_ref, u_ref, w_ref, prob_ref, least_ref
+    rel_ref, slot_ref, own_ref, cap_ref, tile_ref, val_ref, score_ref, out_ref, u_ref, w_ref, prob_ref, least_ref
 ):
     blocks, lists, rows, cols = cap_ref.shape
     relations = u_ref.shape[1]
@@ -133,14 +163,11 @@
 
     def parts(b):
         own = own_ref[b]
-        target = jnp.dot(own, tgt_ref[0], preferred_element_type=F32)
-        target += jnp.dot(own, tgt_ref[1], preferred_element_type=F32)
-        target += jnp.dot(own, tgt_ref[2], preferred_element_type=F32)
         rels = [rel_ref[b, k] for k in range(lists)]
         slots = [slot_ref[b, k] for k in range(lists)]
 
         def spread(r, h):
-            return jnp.broadcast_to(target[:, r * HEADS + h : r * HEADS + h + 1], (rows, cols))
+            return tile_ref[b, r, h]
 
         def finish(h, weights):
             lanes = slice(h * cols, (h + 1) * cols)
@@ -219,7 +246,7 @@
         lax.fori_loop(0, blocks, redo, 0)
 
 
-def attend(hidden, cap, relation_ids, source_slots, values, scores, tgt_vectors):
+def attend(hidden, cap, relation_ids, source_slots, values, scores, tiles):
     blocks, lists, rows, cols = cap.shape
     width = hidden.shape[1]
     relations = values.shape[1]
@@ -237,7 +264,7 @@
         out_shape=jax.ShapeDtypeStruct((blocks, rows, width), BF16),
         compiler_params=pltpu.CompilerParams(vmem_limit_bytes=24 * 1024 * 1024),
         name="attend",
-    )(relation_ids, source_slots, hidden.reshape(blocks, rows, width), cap, tgt_vectors, values, scores).reshape(
+    )(relation_ids, source_slots, hidden.reshape(blocks, rows, width), cap, tiles, values, scores).reshape(
         blocks * rows, width
     )
 
@@ -286,7 +313,9 @@
         pairs = [(p, (p + 2 * up) % n_graph ^ cores) for p in range(n_graph)]
         return lax.ppermute(x, "graph", pairs)
 
-    cut = local_blocks // 2
+    cut = local_blocks // 2 + 1
+    middle_a = (cut + 1) // 2
+    middle_b = local_blocks // 2 - middle_a
     rows_a, half = cut * block_rows, width // 2
     features = node_features.T
     first = arrange(features, proj_weight, core, n_feat, 0, rows_a, half)
@@ -322,20 +351,21 @@
     def ring(part):
         return send(part, 1), send(part, -1)
 
-    def forward(up, down):
-        middle = up.shape[0] // 2
-        return send(up[:middle], 1), send(down[middle:], -1)
+    def forward(up, down, middle):
+        return send(up[: middle * block_rows], 1), send(down[middle * block_rows :], -1)
 
     a = project(got[:, :rows_a])
     up_a, down_a = ring(a)
     near, lists = lists[:1], [send(lists[d], d) for d in range(1, levels)]
     later, up_a, down_a, lists = lax.optimization_barrier((later, up_a, down_a, lists))
-    far_a = forward(up_a, down_a)
+    far_a = forward(up_a, down_a, middle_a)
     b = project(later)
     up_b, down_b = ring(b)
     done = spread(both([(a, 0, cut), (b, cut, local_blocks)]), 0, near, (None, None))
-    up_b, down_b, far_a, done = lax.optimization_barrier((up_b, down_b, far_a, done))
-    far_b = forward(up_b, down_b)
+    hidden = jnp.concatenate([a, b])
+    tiles = target_tiles(hidden, tgt_vectors, local_blocks, relation_weight.shape[0])
+    up_b, down_b, far_a, tiles, done = lax.optimization_barrier((up_b, down_b, far_a, tiles, done))
+    far_b = forward(up_b, down_b, middle_b)
     done = spread(
         both([(up_a, 0, cut), (up_b, cut, local_blocks)]) + both([(down_a, 0, cut), (down_b, cut, local_blocks)]),
         2,
@@ -343,10 +373,10 @@
         done,
     )
     far_b, done = lax.optimization_barrier((far_b, done))
-    quarter = cut // 2
-    far = [(x, n * quarter, (n + 1) * quarter) for n, x in enumerate(far_a + far_b)]
+    ends = (0, middle_a, cut, cut + middle_b, local_blocks)
+    far = list(zip(far_a + far_b, ends[:-1], ends[1:]))
     values, scores = spread(both(far), 6, lists[1:2], done)
-    return attend(jnp.concatenate([a, b]), cap, relation_ids, slots, values, scores, tgt_vectors)
+    return attend(hidden, cap, relation_ids, slots, values, scores, tiles)
 
 
 def solution(mesh):

time: 155 us -> 157 us (1.013)
  waiting for transfers between devices: 36.7 us -> 39.9 us
    all_to_all x1, waiting for transfers between devices: 12.3 us -> 16.6 us  [shards(): lax.all_to_all(first, 'feat', 0, 0, tiled=True)]
    pallas_call x1, Pallas kernels: 51.3 us -> 47.1 us  [attend(): pl.pallas_call(attend_kernel, in_specs=[scalars] * 2 + [inside] * 5, out_...]
    pallas_call x0 -> x1, Pallas kernels: none -> 3.72 us  [target_tiles(): pl.pallas_call(target_kernel, in_specs=[inside, inside], out_specs=inside...]
  transfers between devices with their start and end apart: 25 -> 25, of which waited for: 7 -> 7; matrix products, arithmetic and copies ran while one was open for 5% -> 4% of each run, Pallas kernels for 11% -> 13%
where the time goes in v18:
time: 157 us
  Pallas kernels  74 us (47%)
  waiting for transfers between devices  39.9 us (25%)
  starting transfers between devices  34 us (22%)
  matrix products  5.51 us (4%)
  local copies, waits for them, and re-layouts  2.23 us (1%)
    pallas_call x1, Pallas kernels, attend(): pl.pallas_call(attend_kernel, in_specs=[scalars] * 2 + [inside] * 5, out_...  47.1 us
    ppermute x23, waiting for transfers between devices, send(): return lax.ppermute(x, 'graph', pairs)  23.4 us
    ppermute x23, starting transfers between devices, send(): return lax.ppermute(x, 'graph', pairs)  22.8 us
    all_to_all x1, waiting for transfers between devices, shards(): lax.all_to_all(first, 'feat', 0, 0, tiled=True)  16.6 us
    pallas_call x3, Pallas kernels, transform(): pl.pallas_call(functools.partial(transform_kernel, bounds, first), in_spe...  8.91 us
    pallas_call x2, Pallas kernels, arrange(): pl.pallas_call(functools.partial(arrange_kernel, low, high), grid_spec=pl...  7.34 us
    pallas_call x1, Pallas kernels, caps(): pl.pallas_call(cap_kernel, grid=shape[:1], in_specs=[spec], out_specs=spe...  6.92 us
    all_to_all x1, starting transfers between devices, shards(): lax.all_to_all(first, 'feat', 0, 0, tiled=True)  6.88 us
  transfers between devices with their start and end apart: 25, of which 7 were waited for; matrix products, arithmetic and copies ran while one was open for 4% of the time, Pallas kernels for 13%

profile of v18, /device:TPU:1, one launch (start us, length us, event | category | flops | bytes accessed | tf_op | source)
XLA Modules:
  0.0 156.7 jit_solution(5766255718079977758)
XLA Ops:
  0.0 3.8 %arrange.2 = bf16[16,64,896]{2,1,0:T(8,128)(2,1)} custom-call(s32[1]{0:T(128)} %bitcast.core_ref, bf16[64,16384]{1,0:T(8,128)(2,1)} %bitcast.31, bf16[64,512]{1,0:T(8,128)(2,1)} %w_ref.3), custom_call_target="tpu_custom_call" | custom-call | tf_op jit(solution)/shard_map/arrange/pallas_call | solution.py:31
  3.8 1.5 collective-permute-start
  5.3 6.9 %all-to-all-start = ((bf16[16,64,896]{2,1,0:T(8,128)(2,1)}), bf16[16,64,896]{2,1,0:T(8,128)(2,1)}, u32[]{:S(2)}, u32[]{:S(2)}) async-start(bf16[16,64,896]{2,1,0:T(8,128)(2,1)} %arrange.2), calls=%async_computation | async-start | bytes 3670016 | tf_op jit(solution)/shard_map/all_to_all | solution.py:323
  12.3 0.0 copy-start.4
  12.3 0.9 fusion.1
  13.2 3.5 %arrange.3 = bf16[16,64,384]{2,1,0:T(8,128)(2,1)} custom-call(s32[1]{0:T(128)} %bitcast.core_ref, bf16[64,16384]{1,0:T(8,128)(2,1)} %bitcast.32, bf16[64,512]{1,0:T(8,128)(2,1)} %w_ref.3), custom_call_target="tpu_custom_call" | custom-call | tf_op jit(solution)/shard_map/arrange/pallas_call | solution.py:31
  16.8 0.1 copy.15
  16.9 0.0 copy-start.6
  17.0 6.9 %caps.1.cap_ref = bf16[8,12,128,128]{3,2,1,0:T(8,128)(2,1)} custom-call(s32[8,12,128,128]{3,2,1,0:T(8,128)} %mask_ref.1), custom_call_target="tpu_custom_call" | custom-call | tf_op jit(solution)/shard_map/caps/pallas_call | solution.py:117
  23.9 0.1 pad.19.clone
  24.0 0.1 select_multiply_fusion
  24.1 0.1 fusion.6
  24.3 0.1 maximum_maximum_fusion.refs_6_.refs_11_.refs_10_
  24.4 0.0 collective-permute-done
  24.4 0.3 fusion.10
  24.7 16.6 %all-to-all-done = bf16[16,64,896]{2,1,0:T(8,128)(2,1)} async-done(((bf16[16,64,896]{2,1,0:T(8,128)(2,1)}), bf16[16,64,896]{2,1,0:T(8,128)(2,1)}, u32[]{:S(2)}, u32[]{:S(2)}) %all-to-all-start) | async-done | bytes 1835040 | tf_op jit(solution)/shard_map/all_to_all | solution.py:323
  41.3 1.1 slice.19
  42.3 1.4 collective-permute-start.1
  43.7 4.3 %all-to-all-start.1 = ((bf16[16,64,384]{2,1,0:T(8,128)(2,1)}), bf16[16,64,384]{2,1,0:T(8,128)(2,1)}, u32[]{:S(2)}, u32[]{:S(2)}) async-start(bf16[16,64,384]{2,1,0:T(8,128)(2,1)} %arrange.3), calls=%async_computation.1 | async-start | bytes 1572864 | tf_op jit(solution)/shard_map/all_to_all | solution.py:336
  48.0 0.0 collective-permute-done.1
  48.0 0.8 copy-done.8
  48.8 2.2 %convolution_convert_fusion.refs_1_ = bf16[640,512]{1,0:T(8,128)(2,1)S(1)} fusion(bf16[1024,896]{1,0:T(8,128)(2,1)} %bitcast.2, bf16[1024,256]{1,0:T(8,128)(2,1)S(1)} %collective-permute-done.1, bf16[1024,256]{1,0:T(8,128)(2,1)S(1)} %slice.19, pred[]{:T(512)S(6)} %eq.30), kind=kOutput, calls=%fused_computation | convolution fusion | flops 676134912 | bytes 3014657 | tf_op jit(solution)/shard_map/dot_general | solution.py:343
  51.0 1.7 %collective-permute-start.2 = (bf16[640,512]{1,0:T(8,128)(2,1)S(1)}, bf16[640,512]{1,0:T(8,128)(2,1)S(1)}, u32[]{:S(2)}, u32[]{:S(2)}) collective-permute-start(bf16[640,512]{1,0:T(8,128)(2,1)S(1)} %convolution_convert_fusion.refs_1_), channel_id=1, source_target_pairs={{0,32},{16,48},{32,64},{48,80},{64,96},{80,112},{96,0},{112,16},{1... | collective-permute-start | bytes 1966088 | tf_op jit(solution)/shard_map/ppermute | solution.py:314
  52.7 2.2 %collective-permute-start.3 = (bf16[640,512]{1,0:T(8,128)(2,1)S(1)}, bf16[640,512]{1,0:T(8,128)(2,1)S(1)}, u32[]{:S(2)}, u32[]{:S(2)}) collective-permute-start(bf16[640,512]{1,0:T(8,128)(2,1)S(1)} %convolution_convert_fusion.refs_1_), channel_id=1, source_target_pairs={{0,96},{16,112},{32,0},{48,16},{64,32},{80,48},{96,64},{112,80},{1... | collective-permute-start | bytes 1966088 | tf_op jit(solution)/shard_map/ppermute | solution.py:314
  55.0 0.0 collective-permute-start.4
  55.0 2.6 %collective-permute-start.5 = (s32[2,4]{1,0:T(2,128)S(1)}, s32[2,4]{1,0:T(2,128)S(1)}, u32[]{:S(2)}, u32[]{:S(2)}) collective-permute-start(s32[2,4]{1,0:T(2,128)S(1)} %get-tuple-element.48), channel_id=1, source_target_pairs={{0,64},{16,80},{32,96},{48,112},{64,0},{80,16},{96,32},{112,48},{1... | collective-permute-start | bytes 104 | tf_op jit(solution)/shard_map/ppermute | solution.py:314
  57.5 0.7 collective-permute-start.6
  58.3 11.7 %collective-permute-done.4.refs_0_ = s32[2,4]{1,0:T(2,128)S(1)} collective-permute-done((s32[2,4]{1,0:T(2,128)S(1)}, s32[2,4]{1,0:T(2,128)S(1)}, u32[]{:S(2)}, u32[]{:S(2)}) %collective-permute-start.4) | collective-permute-done | bytes 64 | tf_op jit(solution)/shard_map/ppermute | solution.py:314
  70.0 0.7 collective-permute-start.11
  70.6 0.0 collective-permute-done.5.refs_0_
  70.7 0.0 collective-permute-done.6.refs_1_
  70.7 2.4 %convolution_convert_fusion.1.refs_2_ = bf16[384,512]{1,0:T(8,128)(2,1)S(1)} fusion(bf16[1024,384]{1,0:T(8,128)(2,1)} %bitcast.11, bf16[1024,256]{1,0:T(8,128)(2,1)} %copy-done.8, bf16[1024,256]{1,0:T(8,128)(2,1)} %copy-done.3, pred[]{:T(512)S(6)} %eq.30), kind=kOutput, calls=%fused_computation.2 | convolution fusion | flops 407568384 | bytes 2228225 | tf_op jit(solution)/shard_map/dot_general | solution.py:343
  73.1 1.2 collective-permute-start.12
  74.3 1.7 %collective-permute-start.10 = (bf16[256,512]{1,0:T(8,128)(2,1)S(1)}, bf16[256,512]{1,0:T(8,128)(2,1)S(1)}, u32[]{:S(2)}, u32[]{:S(2)}) collective-permute-start(bf16[256,512]{1,0:T(8,128)(2,1)S(1)} %slice.21), channel_id=1, source_target_pairs={{0,96},{16,112},{32,0},{48,16},{64,32},{80,48},{96,64},{112,80},{1... | collective-permute-start | bytes 786440 | tf_op jit(solution)/shard_map/ppermute | solution.py:314
  76.0 2.7 %collective-permute-start.8 = (bf16[384,512]{1,0:T(8,128)(2,1)S(1)}, bf16[384,512]{1,0:T(8,128)(2,1)S(1)}, u32[]{:S(2)}, u32[]{:S(2)}) collective-permute-start(bf16[384,512]{1,0:T(8,128)(2,1)S(1)} %convolution_convert_fusion.1.refs_2_), channel_id=1, source_target_pairs={{0,96},{16,112},{32,0},{48,16},{64,32},{80,48},{96,64},{112,80},{1... | collective-permute-start | bytes 1179656 | tf_op jit(solution)/shard_map/ppermute | solution.py:314
  78.7 0.1 collective-permute-start.9
  78.8 3.5 %collective-permute-done.10.refs_2_ = bf16[256,512]{1,0:T(8,128)(2,1)S(1)} collective-permute-done((bf16[256,512]{1,0:T(8,128)(2,1)S(1)}, bf16[256,512]{1,0:T(8,128)(2,1)S(1)}, u32[]{:S(2)}, u32[]{:S(2)}) %collective-permute-start.10) | collective-permute-done | bytes 262176 | tf_op jit(solution)/shard_map/ppermute | solution.py:314
  82.3 1.2 collective-permute-start.15
  83.5 0.0 collective-permute-start.17
  83.5 0.1 pad_maximum_fusion
  83.6 3.7 %targets.1.tile_ref = f32[8,2,4,128,128]{4,3,2,1,0:T(8,128)S(1)} custom-call(bf16[8,128,512]{2,1,0:T(8,128)(2,1)S(1)} %bitcast.29, bf16[3,512,128]{2,1,0:T(8,128)(2,1)S(1)} %pad_maximum_fusion.1.tgt_ref), custom_call_target="tpu_custom_call" | custom-call | tf_op jit(solution)/shard_map/targets/pallas_call | solution.py:147
  87.3 2.7 %transform.3 = (bf16[32,2,128,512]{3,2,1,0:T(8,128)(2,1)S(1)}, f32[32,8,128]{2,1,0:T(8,128)S(1)}) custom-call(s32[2,4]{1,0:T(2,128)S(1)} %get-tuple-element.55.refs_0_, bf16[640,512]{1,0:T(8,128)(2,1)S(1)} %convolution_convert_fusion.refs_1_, bf16[384,512]{1,0:T(8,128)(2,1)S(1)} %convolution_convert_fusion.1.refs_2_, ...), custom_call_target="tpu_custom_call" | custom-call | tf_op jit(solution)/shard_map/transform/pallas_call | solution.py:95
  90.0 0.0 collective-permute-done.7.refs_3_
  90.0 0.7 collective-permute-done.8.refs_7_
  90.7 5.3 %collective-permute-done.9.refs_1_ = bf16[384,512]{1,0:T(8,128)(2,1)S(1)} collective-permute-done((bf16[384,512]{1,0:T(8,128)(2,1)S(1)}, bf16[384,512]{1,0:T(8,128)(2,1)S(1)}, u32[]{:S(2)}, u32[]{:S(2)}) %collective-permute-start.9) | collective-permute-done | bytes 393248 | tf_op jit(solution)/shard_map/ppermute | solution.py:314
  96.0 1.1 collective-permute-start.16
  97.2 0.0 collective-permute-start.18
  97.2 0.1 collective-permute-start.14
  97.3 0.0 collective-permute-done.15.refs_4_
  97.3 1.5 collective-permute-start.13
  98.8 0.0 collective-permute-done.17.refs_8_
  98.8 1.1 collective-permute-start.19
  99.9 0.1 collective-permute-start.20
  100.0 0.0 collective-permute-done.18.refs_9_
  100.0 3.9 %transform.4 = (bf16[32,2,128,512]{3,2,1,0:T(8,128)(2,1)S(1)}, f32[32,8,128]{2,1,0:T(8,128)S(1)}) custom-call(s32[2,4]{1,0:T(2,128)S(1)} %collective-permute-done.4.refs_0_, s32[2,4]{1,0:T(2,128)S(1)} %collective-permute-done.6.refs_1_, bf16[640,512]{1,0:T(8,128)(2,1)S(1)} %collective-permute-done.2.refs_2_, ...), custom_call_target="tpu_custom_call", output_to_operand_aliasing={{0}: (12, {}), {1}: (13, {})} | custom-call | tf_op jit(solution)/shard_map/transform/pallas_call | solution.py:95
  103.9 0.0 collective-permute-done.13.refs_3_
  103.9 0.7 collective-permute-done.14.refs_4_
  104.6 1.4 collective-permute-start.22
  106.0 0.0 collective-permute-start.21
  106.0 1.3 collective-permute-done.21.refs_7_
  107.3 0.0 collective-permute-done.22.refs_8_
  107.3 2.3 %transform.5 = (bf16[32,2,128,512]{3,2,1,0:T(8,128)(2,1)S(1)}, f32[32,8,128]{2,1,0:T(8,128)S(1)}) custom-call(s32[2,4]{1,0:T(2,128)S(1)} %collective-permute-done.5.refs_0_, bf16[384,512]{1,0:T(8,128)(2,1)S(1)} %collective-permute-done.9.refs_1_, ...), custom_call_target="tpu_custom_call", output_to_operand_aliasing={{0}: (11, {}), {1}: (12, {})} | custom-call | tf_op jit(solution)/shard_map/transform/pallas_call | solution.py:95
  109.6 0.0 copy-done
  109.6 47.1 %attend.1 = bf16[8,128,512]{2,1,0:T(8,128)(2,1)} custom-call(s32[8,12]{1,0:T(8,128)S(1)} %copy-done.2, s32[8,12]{1,0:T(8,128)S(1)} %fusion.23.slot_ref, bf16[8,128,512]{2,1,0:T(8,128)(2,1)S(1)} %bitcast.30, bf16[8,12,128,128]{3,2,1,0:T(8,128)(2,1)S(1)} %copy-done, f32[8,2,4,128,128]{4,3,2,1,0:T(8,128)S(1)} %targets.1.tile_ref, ...), custom_call_target="tpu_custom_call" | custom-call | tf_op jit(solution)/shard_map/attend/pallas_call | solution.py:254
  (38 shorter events, 0.3 us)
Async XLA Ops:
  0.0 3.8 %copy-start.7 = (s32[1,8,4]{1,2,0:T(4,128)S(1)}, s32[1,8,4]{1,2,0:T(4,128)}, u32[]{:S(2)}) copy-start(s32[1,8,4]{1,2,0:T(4,128)} %param.16) | copy-start | bytes 388
  3.8 8.4 %copy-start.5 = (f32[2,512]{1,0:T(2,128)S(1)}, f32[2,512]{1,0:T(2,128)}, u32[]{:S(2)}) copy-start(f32[2,512]{1,0:T(2,128)} %param.12) | copy-start | bytes 12292
  3.8 8.4 %copy-start.1 = (bf16[2,512,512]{2,1,0:T(8,128)(2,1)S(1)}, bf16[2,512,512]{2,1,0:T(8,128)(2,1)}, u32[]{:S(2)}) copy-start(bf16[2,512,512]{2,1,0:T(8,128)(2,1)} %refs_9_.1) | copy-start | bytes 3145732
  3.8 20.6 %collective-permute-start = (s32[8,4]{0,1:T(4,128)S(1)}, s32[8,4]{0,1:T(4,128)S(1)}, u32[]{:S(2)}, u32[]{:S(2)}) collective-permute-start(s32[8,4]{0,1:T(4,128)S(1)} %bitcast.35), channel_id=1, source_target_pairs={{0,16},{16,0},{32,48},{48,32},{64,80},{80,64},{96,112},{112,96},{1... | collective-permute-start | bytes 392 | tf_op jit(solution)/shard_map/ppermute | solution.py:314
  5.3 35.9 %all-to-all-start = ((bf16[16,64,896]{2,1,0:T(8,128)(2,1)}), bf16[16,64,896]{2,1,0:T(8,128)(2,1)}, u32[]{:S(2)}, u32[]{:S(2)}) async-start(bf16[16,64,896]{2,1,0:T(8,128)(2,1)} %arrange.2), calls=%async_computation | async-start | bytes 3670016 | tf_op jit(solution)/shard_map/all_to_all | solution.py:323
  12.3 4.5 %copy-start.4 = (f32[2,512]{1,0:T(2,128)S(1)}, f32[2,512]{1,0:T(2,128)}, u32[]{:S(2)}) copy-start(f32[2,512]{1,0:T(2,128)} %param.13) | copy-start | bytes 12292
  16.9 7.3 %copy-start.6 = (s32[8,12]{1,0:T(8,128)S(1)}, s32[8,12]{1,0:T(8,128)}, u32[]{:S(2)}) copy-start(s32[8,12]{1,0:T(8,128)} %param.17) | copy-start | bytes 1156
  42.3 5.7 %copy-start.3 = (bf16[1024,256]{1,0:T(8,128)(2,1)}, bf16[1024,256]{1,0:T(8,128)(2,1)S(1)}, u32[]{:S(2)}) copy-start(bf16[1024,256]{1,0:T(8,128)(2,1)S(1)} %slice.19) | copy-start | bytes 1572868
  42.3 5.7 %collective-permute-start.1 = (bf16[1024,256]{1,0:T(8,128)(2,1)S(1)}, bf16[1024,256]{1,0:T(8,128)(2,1)S(1)}, u32[]{:S(2)}, u32[]{:S(2)}) collective-permute-start(bf16[1024,256]{1,0:T(8,128)(2,1)S(1)} %slice.19), channel_id=1, source_target_pairs={{0,16},{16,0},{32,48},{48,32},{64,80},{80,64},{96,112},{112,96},{1... | collective-permute-start | bytes 1572872 | tf_op jit(solution)/shard_map/ppermute | solution.py:314
  43.7 27.0 %all-to-all-start.1 = ((bf16[16,64,384]{2,1,0:T(8,128)(2,1)}), bf16[16,64,384]{2,1,0:T(8,128)(2,1)}, u32[]{:S(2)}, u32[]{:S(2)}) async-start(bf16[16,64,384]{2,1,0:T(8,128)(2,1)} %arrange.3), calls=%async_computation.1 | async-start | bytes 1572864 | tf_op jit(solution)/shard_map/all_to_all | solution.py:336
  48.0 0.8 copy-start.8
  51.0 19.6 %collective-permute-start.2 = (bf16[640,512]{1,0:T(8,128)(2,1)S(1)}, bf16[640,512]{1,0:T(8,128)(2,1)S(1)}, u32[]{:S(2)}, u32[]{:S(2)}) collective-permute-start(bf16[640,512]{1,0:T(8,128)(2,1)S(1)} %convolution_convert_fusion.refs_1_), channel_id=1, source_target_pairs={{0,32},{16,48},{32,64},{48,80},{64,96},{80,112},{96,0},{112,16},{1... | collective-permute-start | bytes 1966088 | tf_op jit(solution)/shard_map/ppermute | solution.py:314
  52.7 17.9 %collective-permute-start.3 = (bf16[640,512]{1,0:T(8,128)(2,1)S(1)}, bf16[640,512]{1,0:T(8,128)(2,1)S(1)}, u32[]{:S(2)}, u32[]{:S(2)}) collective-permute-start(bf16[640,512]{1,0:T(8,128)(2,1)S(1)} %convolution_convert_fusion.refs_1_), channel_id=1, source_target_pairs={{0,96},{16,112},{32,0},{48,16},{64,32},{80,48},{96,64},{112,80},{1... | collective-permute-start | bytes 1966088 | tf_op jit(solution)/shard_map/ppermute | solution.py:314
  55.0 15.0 %collective-permute-start.4 = (s32[2,4]{1,0:T(2,128)S(1)}, s32[2,4]{1,0:T(2,128)S(1)}, u32[]{:S(2)}, u32[]{:S(2)}) collective-permute-start(s32[2,4]{1,0:T(2,128)S(1)} %get-tuple-element.47), channel_id=1, source_target_pairs={{0,32},{16,48},{32,64},{48,80},{64,96},{80,112},{96,0},{112,16},{1... | collective-permute-start | bytes 104 | tf_op jit(solution)/shard_map/ppermute | solution.py:314
  55.0 15.7 %collective-permute-start.5 = (s32[2,4]{1,0:T(2,128)S(1)}, s32[2,4]{1,0:T(2,128)S(1)}, u32[]{:S(2)}, u32[]{:S(2)}) collective-permute-start(s32[2,4]{1,0:T(2,128)S(1)} %get-tuple-element.48), channel_id=1, source_target_pairs={{0,64},{16,80},{32,96},{48,112},{64,0},{80,16},{96,32},{112,48},{1... | collective-permute-start | bytes 104 | tf_op jit(solution)/shard_map/ppermute | solution.py:314
  57.5 13.1 %collective-permute-start.6 = (s32[2,4]{1,0:T(2,128)S(1)}, s32[2,4]{1,0:T(2,128)S(1)}, u32[]{:S(2)}, u32[]{:S(2)}) collective-permute-start(s32[2,4]{1,0:T(2,128)S(1)} %get-tuple-element.49), channel_id=1, source_target_pairs={{0,96},{16,112},{32,0},{48,16},{64,32},{80,48},{96,64},{112,80},{1... | collective-permute-start | bytes 104 | tf_op jit(solution)/shard_map/ppermute | solution.py:314
  70.0 8.7 %collective-permute-start.11 = (bf16[640,512]{1,0:T(8,128)(2,1)S(1)}, bf16[640,512]{1,0:T(8,128)(2,1)}, u32[]{:S(2)}, u32[]{:S(2)}) collective-permute-start(bf16[640,512]{1,0:T(8,128)(2,1)S(1)} %convolution_convert_fusion.refs_1_), channel_id=1, source_target_pairs={{0,16},{16,0},{32,48},{48,32},{64,80},{80,64},{96,112},{112,96},{1... | collective-permute-start | bytes 1966088 | tf_op jit(solution)/shard_map/ppermute | solution.py:314
  73.1 10.4 %collective-permute-start.12 = (bf16[384,512]{1,0:T(8,128)(2,1)S(1)}, bf16[384,512]{1,0:T(8,128)(2,1)S(1)}, u32[]{:S(2)}, u32[]{:S(2)}) collective-permute-start(bf16[384,512]{1,0:T(8,128)(2,1)S(1)} %convolution_convert_fusion.1.refs_2_), channel_id=1, source_target_pairs={{0,16},{16,0},{32,48},{48,32},{64,80},{80,64},{96,112},{112,96},{1... | collective-permute-start | bytes 1179656 | tf_op jit(solution)/shard_map/ppermute | solution.py:314
  74.3 8.0 %collective-permute-start.10 = (bf16[256,512]{1,0:T(8,128)(2,1)S(1)}, bf16[256,512]{1,0:T(8,128)(2,1)S(1)}, u32[]{:S(2)}, u32[]{:S(2)}) collective-permute-start(bf16[256,512]{1,0:T(8,128)(2,1)S(1)} %slice.21), channel_id=1, source_target_pairs={{0,96},{16,112},{32,0},{48,16},{64,32},{80,48},{96,64},{112,80},{1... | collective-permute-start | bytes 786440 | tf_op jit(solution)/shard_map/ppermute | solution.py:314
  76.0 14.0 %collective-permute-start.7 = (bf16[384,512]{1,0:T(8,128)(2,1)S(1)}, bf16[384,512]{1,0:T(8,128)(2,1)S(1)}, u32[]{:S(2)}, u32[]{:S(2)}) collective-permute-start(bf16[384,512]{1,0:T(8,128)(2,1)S(1)} %convolution_convert_fusion.1.refs_2_), channel_id=1, source_target_pairs={{0,32},{16,48},{32,64},{48,80},{64,96},{80,112},{96,0},{112,16},{1... | collective-permute-start | bytes 1179656 | tf_op jit(solution)/shard_map/ppermute | solution.py:314
  76.0 14.7 %collective-permute-start.8 = (bf16[384,512]{1,0:T(8,128)(2,1)S(1)}, bf16[384,512]{1,0:T(8,128)(2,1)S(1)}, u32[]{:S(2)}, u32[]{:S(2)}) collective-permute-start(bf16[384,512]{1,0:T(8,128)(2,1)S(1)} %convolution_convert_fusion.1.refs_2_), channel_id=1, source_target_pairs={{0,96},{16,112},{32,0},{48,16},{64,32},{80,48},{96,64},{112,80},{1... | collective-permute-start | bytes 1179656 | tf_op jit(solution)/shard_map/ppermute | solution.py:314
  78.7 17.3 %collective-permute-start.9 = (bf16[384,512]{1,0:T(8,128)(2,1)S(1)}, bf16[384,512]{1,0:T(8,128)(2,1)S(1)}, u32[]{:S(2)}, u32[]{:S(2)}) collective-permute-start(bf16[384,512]{1,0:T(8,128)(2,1)S(1)} %slice.20), channel_id=1, source_target_pairs={{0,32},{16,48},{32,64},{48,80},{64,96},{80,112},{96,0},{112,16},{1... | collective-permute-start | bytes 1179656 | tf_op jit(solution)/shard_map/ppermute | solution.py:314
  82.3 15.0 %collective-permute-start.15 = (bf16[640,512]{1,0:T(8,128)(2,1)S(1)}, bf16[640,512]{1,0:T(8,128)(2,1)S(1)}, u32[]{:S(2)}, u32[]{:S(2)}) collective-permute-start(bf16[640,512]{1,0:T(8,128)(2,1)S(1)} %collective-permute-done.2.refs_2_), channel_id=1, source_target_pairs={{0,16},{16,0},{32,48},{48,32},{64,80},{80,64},{96,112},{112,96},{1... | collective-permute-start | bytes 1966088 | tf_op jit(solution)/shard_map/ppermute | solution.py:314
  83.5 15.3 %collective-permute-start.17 = (bf16[640,512]{1,0:T(8,128)(2,1)S(1)}, bf16[640,512]{1,0:T(8,128)(2,1)S(1)}, u32[]{:S(2)}, u32[]{:S(2)}) collective-permute-start(bf16[640,512]{1,0:T(8,128)(2,1)S(1)} %collective-permute-done.3.refs_6_), channel_id=1, source_target_pairs={{0,16},{16,0},{32,48},{48,32},{64,80},{80,64},{96,112},{112,96},{1... | collective-permute-start | bytes 1966088 | tf_op jit(solution)/shard_map/ppermute | solution.py:314
  96.0 3.8 %collective-permute-start.16 = (bf16[384,512]{1,0:T(8,128)(2,1)S(1)}, bf16[384,512]{1,0:T(8,128)(2,1)S(1)}, u32[]{:S(2)}, u32[]{:S(2)}) collective-permute-start(bf16[384,512]{1,0:T(8,128)(2,1)S(1)} %collective-permute-done.7.refs_3_), channel_id=1, source_target_pairs={{0,16},{16,0},{32,48},{48,32},{64,80},{80,64},{96,112},{112,96},{1... | collective-permute-start | bytes 1179656 | tf_op jit(solution)/shard_map/ppermute | solution.py:314
  97.2 2.8 %collective-permute-start.18 = (bf16[384,512]{1,0:T(8,128)(2,1)S(1)}, bf16[384,512]{1,0:T(8,128)(2,1)S(1)}, u32[]{:S(2)}, u32[]{:S(2)}) collective-permute-start(bf16[384,512]{1,0:T(8,128)(2,1)S(1)} %collective-permute-done.8.refs_7_), channel_id=1, source_target_pairs={{0,16},{16,0},{32,48},{48,32},{64,80},{80,64},{96,112},{112,96},{1... | collective-permute-start | bytes 1179656 | tf_op jit(solution)/shard_map/ppermute | solution.py:314
  97.2 7.4 %collective-permute-start.14 = (bf16[256,512]{1,0:T(8,128)(2,1)S(1)}, bf16[256,512]{1,0:T(8,128)(2,1)S(1)}, u32[]{:S(2)}, u32[]{:S(2)}) collective-permute-start(bf16[256,512]{1,0:T(8,128)(2,1)S(1)} %slice.23), channel_id=1, source_target_pairs={{0,96},{16,112},{32,0},{48,16},{64,32},{80,48},{96,64},{112,80},{1... | collective-permute-start | bytes 786440 | tf_op jit(solution)/shard_map/ppermute | solution.py:314
  97.3 6.6 %collective-permute-start.13 = (bf16[128,512]{1,0:T(8,128)(2,1)S(1)}, bf16[128,512]{1,0:T(8,128)(2,1)S(1)}, u32[]{:S(2)}, u32[]{:S(2)}) collective-permute-start(bf16[128,512]{1,0:T(8,128)(2,1)S(1)} %slice.22), channel_id=1, source_target_pairs={{0,32},{16,48},{32,64},{48,80},{64,96},{80,112},{96,0},{112,16},{1... | collective-permute-start | bytes 393224 | tf_op jit(solution)/shard_map/ppermute | solution.py:314
  98.8 7.2 %collective-permute-start.19 = (bf16[384,512]{1,0:T(8,128)(2,1)S(1)}, bf16[384,512]{1,0:T(8,128)(2,1)S(1)}, u32[]{:S(2)}, u32[]{:S(2)}) collective-permute-start(bf16[384,512]{1,0:T(8,128)(2,1)S(1)} %collective-permute-done.9.refs_1_), channel_id=1, source_target_pairs={{0,16},{16,0},{32,48},{48,32},{64,80},{80,64},{96,112},{112,96},{1... | collective-permute-start | bytes 1179656 | tf_op jit(solution)/shard_map/ppermute | solution.py:314
  99.9 6.1 %collective-permute-start.20 = (bf16[256,512]{1,0:T(8,128)(2,1)S(1)}, bf16[256,512]{1,0:T(8,128)(2,1)S(1)}, u32[]{:S(2)}, u32[]{:S(2)}) collective-permute-start(bf16[256,512]{1,0:T(8,128)(2,1)S(1)} %collective-permute-done.10.refs_2_), channel_id=1, source_target_pairs={{0,16},{16,0},{32,48},{48,32},{64,80},{80,64},{96,112},{112,96},{1... | collective-permute-start | bytes 786440 | tf_op jit(solution)/shard_map/ppermute | solution.py:314
  104.6 5.0 %copy-start.2 = (s32[8,12]{1,0:T(8,128)S(1)}, s32[8,12]{1,0:T(8,128)}, u32[]{:S(2)}) copy-start(s32[8,12]{1,0:T(8,128)} %rel_ref.1) | copy-start | bytes 1156
  104.6 2.7 %collective-permute-start.22 = (bf16[256,512]{1,0:T(8,128)(2,1)S(1)}, bf16[256,512]{1,0:T(8,128)(2,1)S(1)}, u32[]{:S(2)}, u32[]{:S(2)}) collective-permute-start(bf16[256,512]{1,0:T(8,128)(2,1)S(1)} %collective-permute-done.14.refs_4_), channel_id=1, source_target_pairs={{0,16},{16,0},{32,48},{48,32},{64,80},{80,64},{96,112},{112,96},{1... | collective-permute-start | bytes 786440 | tf_op jit(solution)/shard_map/ppermute | solution.py:314
  106.0 1.3 collective-permute-start.21
  107.3 2.3 %copy-start = (bf16[8,12,128,128]{3,2,1,0:T(8,128)(2,1)S(1)}, bf16[8,12,128,128]{3,2,1,0:T(8,128)(2,1)}, u32[]{:S(2)}) copy-start(bf16[8,12,128,128]{3,2,1,0:T(8,128)(2,1)} %caps.1.cap_ref) | copy-start | bytes 9437188

commit v19 on v18

--- a/solution.py
+++ b/solution.py
@@ -313,9 +313,7 @@
         pairs = [(p, (p + 2 * up) % n_graph ^ cores) for p in range(n_graph)]
         return lax.ppermute(x, "graph", pairs)
 
-    cut = local_blocks // 2 + 1
-    middle_a = (cut + 1) // 2
-    middle_b = local_blocks // 2 - middle_a
+    cut = local_blocks // 2
     rows_a, half = cut * block_rows, width // 2
     features = node_features.T
     first = arrange(features, proj_weight, core, n_feat, 0, rows_a, half)
@@ -351,21 +349,22 @@
     def ring(part):
         return send(part, 1), send(part, -1)
 
-    def forward(up, down, middle):
-        return send(up[: middle * block_rows], 1), send(down[middle * block_rows :], -1)
+    def forward(up, down):
+        middle = up.shape[0] // 2
+        return send(up[:middle], 1), send(down[middle:], -1)
 
     a = project(got[:, :rows_a])
     up_a, down_a = ring(a)
     near, lists = lists[:1], [send(lists[d], d) for d in range(1, levels)]
     later, up_a, down_a, lists = lax.optimization_barrier((later, up_a, down_a, lists))
-    far_a = forward(up_a, down_a, middle_a)
+    far_a = forward(up_a, down_a)
     b = project(later)
     up_b, down_b = ring(b)
     done = spread(both([(a, 0, cut), (b, cut, local_blocks)]), 0, near, (None, None))
     hidden = jnp.concatenate([a, b])
     tiles = target_tiles(hidden, tgt_vectors, local_blocks, relation_weight.shape[0])
     up_b, down_b, far_a, tiles, done = lax.optimization_barrier((up_b, down_b, far_a, tiles, done))
-    far_b = forward(up_b, down_b, middle_b)
+    far_b = forward(up_b, down_b)
     done = spread(
         both([(up_a, 0, cut), (up_b, cut, local_blocks)]) + both([(down_a, 0, cut), (down_b, cut, local_blocks)]),
         2,
@@ -373,8 +372,8 @@
         done,
     )
     far_b, done = lax.optimization_barrier((far_b, done))
-    ends = (0, middle_a, cut, cut + middle_b, local_blocks)
-    far = list(zip(far_a + far_b, ends[:-1], ends[1:]))
+    quarter = cut // 2
+    far = [(x, n * quarter, (n + 1) * quarter) for n, x in enumerate(far_a + far_b)]
     values, scores = spread(both(far), 6, lists[1:2], done)
     return attend(hidden, cap, relation_ids, slots, values, scores, tiles)
 

time: 157 us -> 151 us (0.962)
  waiting for transfers between devices: 39.9 us -> 33.2 us
    all_to_all x1, waiting for transfers between devices: 16.6 us -> 12.3 us  [shards(): lax.all_to_all(first, 'feat', 0, 0, tiled=True)]
    ppermute x23, waiting for transfers between devices: 23.4 us -> 20.9 us  [send(): return lax.ppermute(x, 'graph', pairs)]
  transfers between devices with their start and end apart: 25 -> 25, of which waited for: 7 -> 7; matrix products, arithmetic and copies ran while one was open for 4% -> 4% of each run, Pallas kernels for 13% -> 14%
where the time goes in v19:
time: 151 us; the launch traced here: 150 us
  Pallas kernels  73.9 us (49%)
  starting transfers between devices  34.9 us (23%)
  waiting for transfers between devices  33.2 us (22%)
  matrix products  5.67 us (4%)
    pallas_call x1, Pallas kernels, attend(): pl.pallas_call(attend_kernel, in_specs=[scalars] * 2 + [inside] * 5, out_...  47.1 us
    ppermute x23, starting transfers between devices, send(): return lax.ppermute(x, 'graph', pairs)  23.7 us
    ppermute x23, waiting for transfers between devices, send(): return lax.ppermute(x, 'graph', pairs)  20.9 us
    all_to_all x1, waiting for transfers between devices, shards(): lax.all_to_all(first, 'feat', 0, 0, tiled=True)  12.3 us
    pallas_call x3, Pallas kernels, transform(): pl.pallas_call(functools.partial(transform_kernel, bounds, first), in_spe...  8.87 us
    pallas_call x2, Pallas kernels, arrange(): pl.pallas_call(functools.partial(arrange_kernel, low, high), grid_spec=pl...  7.26 us
    pallas_call x1, Pallas kernels, caps(): pl.pallas_call(cap_kernel, grid=shape[:1], in_specs=[spec], out_specs=spe...  6.92 us
    all_to_all x1, starting transfers between devices, shards(): lax.all_to_all(first, 'feat', 0, 0, tiled=True)  6.88 us
  transfers between devices with their start and end apart: 25, of which 7 were waited for; matrix products, arithmetic and copies ran while one was open for 4% of the time, Pallas kernels for 14%

profile of v19, /device:TPU:1, one launch (start us, length us, event | category | flops | bytes accessed | tf_op | source)
XLA Modules:
  0.0 150.2 jit_solution(6473152615099632829)
XLA Ops:
  0.0 3.7 %arrange.2 = bf16[16,64,768]{2,1,0:T(8,128)(2,1)} custom-call(s32[1]{0:T(128)} %bitcast.core_ref, bf16[64,16384]{1,0:T(8,128)(2,1)} %bitcast.31, bf16[64,512]{1,0:T(8,128)(2,1)} %w_ref.3), custom_call_target="tpu_custom_call" | custom-call | tf_op jit(solution)/shard_map/arrange/pallas_call | solution.py:31
  3.7 1.5 collective-permute-start
  5.2 6.9 %all-to-all-start = ((bf16[16,64,768]{2,1,0:T(8,128)(2,1)}), bf16[16,64,768]{2,1,0:T(8,128)(2,1)}, u32[]{:S(2)}, u32[]{:S(2)}) async-start(bf16[16,64,768]{2,1,0:T(8,128)(2,1)} %arrange.2), calls=%async_computation | async-start | bytes 3145728 | tf_op jit(solution)/shard_map/all_to_all | solution.py:321
  12.1 0.0 copy-start.4
  12.1 0.9 fusion
  13.2 3.6 %arrange.3 = bf16[16,64,512]{2,1,0:T(8,128)(2,1)} custom-call(s32[1]{0:T(128)} %bitcast.core_ref, bf16[64,16384]{1,0:T(8,128)(2,1)} %bitcast.32, bf16[64,512]{1,0:T(8,128)(2,1)} %w_ref.3), custom_call_target="tpu_custom_call" | custom-call | tf_op jit(solution)/shard_map/arrange/pallas_call | solution.py:31
  16.8 0.1 copy.15
  16.9 0.0 copy-start.6
  16.9 6.9 %caps.1.cap_ref = bf16[8,12,128,128]{3,2,1,0:T(8,128)(2,1)} custom-call(s32[8,12,128,128]{3,2,1,0:T(8,128)} %mask_ref.1), custom_call_target="tpu_custom_call" | custom-call | tf_op jit(solution)/shard_map/caps/pallas_call | solution.py:117
  23.9 0.1 pad.19.clone
  23.9 0.1 select_multiply_fusion
  24.1 0.1 fusion.6
  24.3 0.1 maximum_maximum_fusion.refs_6_.refs_11_.refs_10_
  24.4 0.0 collective-permute-done
  24.4 0.3 fusion.10
  24.7 12.3 %all-to-all-done = bf16[16,64,768]{2,1,0:T(8,128)(2,1)} async-done(((bf16[16,64,768]{2,1,0:T(8,128)(2,1)}), bf16[16,64,768]{2,1,0:T(8,128)(2,1)}, u32[]{:S(2)}, u32[]{:S(2)}) %all-to-all-start) | async-done | bytes 1572896 | tf_op jit(solution)/shard_map/all_to_all | solution.py:321
  37.0 1.1 slice.19
  38.1 1.4 collective-permute-start.1
  39.5 4.3 %all-to-all-start.1 = ((bf16[16,64,512]{2,1,0:T(8,128)(2,1)}), bf16[16,64,512]{2,1,0:T(8,128)(2,1)}, u32[]{:S(2)}, u32[]{:S(2)}) async-start(bf16[16,64,512]{2,1,0:T(8,128)(2,1)} %arrange.3), calls=%async_computation.1 | async-start | bytes 2097152 | tf_op jit(solution)/shard_map/all_to_all | solution.py:334
  43.8 2.2 %convolution_convert_fusion.1.refs_1_ = bf16[512,512]{1,0:T(8,128)(2,1)S(1)} fusion(bf16[1024,768]{1,0:T(8,128)(2,1)} %bitcast.2, bf16[1024,256]{1,0:T(8,128)(2,1)S(1)} %collective-permute-done.1, bf16[1024,256]{1,0:T(8,128)(2,1)S(1)} %slice.19, pred[]{:T(512)S(6)} %eq.30), kind=kOutput, calls=%fused_computation.1 | convolution fusion | flops 541851648 | bytes 2621441 | tf_op jit(solution)/shard_map/dot_general | solution.py:341
  46.0 1.7 %collective-permute-start.2 = (bf16[512,512]{1,0:T(8,128)(2,1)S(1)}, bf16[512,512]{1,0:T(8,128)(2,1)S(1)}, u32[]{:S(2)}, u32[]{:S(2)}) collective-permute-start(bf16[512,512]{1,0:T(8,128)(2,1)S(1)} %convolution_convert_fusion.1.refs_1_), channel_id=1, source_target_pairs={{0,32},{16,48},{32,64},{48,80},{64,96},{80,112},{96,0},{112,16},{1... | collective-permute-start | bytes 1572872 | tf_op jit(solution)/shard_map/ppermute | solution.py:314
  47.7 2.2 %collective-permute-start.3 = (bf16[512,512]{1,0:T(8,128)(2,1)S(1)}, bf16[512,512]{1,0:T(8,128)(2,1)S(1)}, u32[]{:S(2)}, u32[]{:S(2)}) collective-permute-start(bf16[512,512]{1,0:T(8,128)(2,1)S(1)} %convolution_convert_fusion.1.refs_1_), channel_id=1, source_target_pairs={{0,96},{16,112},{32,0},{48,16},{64,32},{80,48},{96,64},{112,80},{1... | collective-permute-start | bytes 1572872 | tf_op jit(solution)/shard_map/ppermute | solution.py:314
  49.9 0.0 collective-permute-start.4
  49.9 2.6 %collective-permute-start.5 = (s32[2,4]{1,0:T(2,128)S(1)}, s32[2,4]{1,0:T(2,128)S(1)}, u32[]{:S(2)}, u32[]{:S(2)}) collective-permute-start(s32[2,4]{1,0:T(2,128)S(1)} %get-tuple-element.48), channel_id=1, source_target_pairs={{0,64},{16,80},{32,96},{48,112},{64,0},{80,16},{96,32},{112,48},{1... | collective-permute-start | bytes 104 | tf_op jit(solution)/shard_map/ppermute | solution.py:314
  52.5 0.7 collective-permute-start.6
  53.2 9.0 %collective-permute-done.4.refs_0_ = s32[2,4]{1,0:T(2,128)S(1)} collective-permute-done((s32[2,4]{1,0:T(2,128)S(1)}, s32[2,4]{1,0:T(2,128)S(1)}, u32[]{:S(2)}, u32[]{:S(2)}) %collective-permute-start.4) | collective-permute-done | bytes 64 | tf_op jit(solution)/shard_map/ppermute | solution.py:314
  62.3 0.5 collective-permute-start.11
  62.8 0.5 collective-permute-done.5.refs_0_
  63.3 0.0 collective-permute-done.3.refs_6_
  63.3 2.6 %convolution_convert_fusion.refs_2_ = bf16[512,512]{1,0:T(8,128)(2,1)S(1)} fusion(bf16[1024,512]{1,0:T(8,128)(2,1)} %bitcast.11, bf16[1024,256]{1,0:T(8,128)(2,1)} %copy-done.8, bf16[1024,256]{1,0:T(8,128)(2,1)} %copy-done.3, pred[]{:T(512)S(6)} %eq.30), kind=kOutput, calls=%fused_computation | convolution fusion | flops 541851648 | bytes 2621441 | tf_op jit(solution)/shard_map/dot_general | solution.py:341
  65.9 0.8 collective-permute-start.12
  66.6 1.4 collective-permute-start.7
  68.0 2.1 %collective-permute-start.8 = (bf16[512,512]{1,0:T(8,128)(2,1)S(1)}, bf16[512,512]{1,0:T(8,128)(2,1)S(1)}, u32[]{:S(2)}, u32[]{:S(2)}) collective-permute-start(bf16[512,512]{1,0:T(8,128)(2,1)S(1)} %convolution_convert_fusion.refs_2_), channel_id=1, source_target_pairs={{0,96},{16,112},{32,0},{48,16},{64,32},{80,48},{96,64},{112,80},{1... | collective-permute-start | bytes 1572872 | tf_op jit(solution)/shard_map/ppermute | solution.py:314
  70.2 1.5 %collective-permute-start.10 = (bf16[256,512]{1,0:T(8,128)(2,1)S(1)}, bf16[256,512]{1,0:T(8,128)(2,1)S(1)}, u32[]{:S(2)}, u32[]{:S(2)}) collective-permute-start(bf16[256,512]{1,0:T(8,128)(2,1)S(1)} %slice.21), channel_id=1, source_target_pairs={{0,96},{16,112},{32,0},{48,16},{64,32},{80,48},{96,64},{112,80},{1... | collective-permute-start | bytes 786440 | tf_op jit(solution)/shard_map/ppermute | solution.py:314
  71.7 0.1 collective-permute-start.9
  71.8 0.0 collective-permute-done.12.refs_4_
  71.8 1.0 collective-permute-start.15
  72.8 0.1 pad_maximum_fusion
  72.9 3.7 %targets.1.tile_ref = f32[8,2,4,128,128]{4,3,2,1,0:T(8,128)S(1)} custom-call(bf16[8,128,512]{2,1,0:T(8,128)(2,1)S(1)} %bitcast.29, bf16[3,512,128]{2,1,0:T(8,128)(2,1)S(1)} %pad_maximum_fusion.1.tgt_ref), custom_call_target="tpu_custom_call" | custom-call | tf_op jit(solution)/shard_map/targets/pallas_call | solution.py:147
  76.6 2.7 %transform.3 = (bf16[32,2,128,512]{3,2,1,0:T(8,128)(2,1)S(1)}, f32[32,8,128]{2,1,0:T(8,128)S(1)}) custom-call(s32[2,4]{1,0:T(2,128)S(1)} %get-tuple-element.55.refs_0_, bf16[512,512]{1,0:T(8,128)(2,1)S(1)} %convolution_convert_fusion.1.refs_1_, bf16[512,512]{1,0:T(8,128)(2,1)S(1)} %convolution_convert_fusion.refs_2_, ...), custom_call_target="tpu_custom_call" | custom-call | tf_op jit(solution)/shard_map/transform/pallas_call | solution.py:95
  79.3 7.9 %collective-permute-done.10.refs_2_ = bf16[256,512]{1,0:T(8,128)(2,1)S(1)} collective-permute-done((bf16[256,512]{1,0:T(8,128)(2,1)S(1)}, bf16[256,512]{1,0:T(8,128)(2,1)S(1)}, u32[]{:S(2)}, u32[]{:S(2)}) %collective-permute-start.10) | collective-permute-done | bytes 262176 | tf_op jit(solution)/shard_map/ppermute | solution.py:314
  87.2 1.0 collective-permute-start.17
  88.2 0.0 collective-permute-done.9.refs_1_
  88.2 0.0 collective-permute-done.7.refs_3_
  88.2 0.5 collective-permute-start.16
  88.6 0.1 collective-permute-start.18
  88.8 1.5 %collective-permute-start.13 = (bf16[256,512]{1,0:T(8,128)(2,1)S(1)}, bf16[256,512]{1,0:T(8,128)(2,1)S(1)}, u32[]{:S(2)}, u32[]{:S(2)}) collective-permute-start(bf16[256,512]{1,0:T(8,128)(2,1)S(1)} %slice.22), channel_id=1, source_target_pairs={{0,32},{16,48},{32,64},{48,80},{64,96},{80,112},{96,0},{112,16},{1... | collective-permute-start | bytes 786440 | tf_op jit(solution)/shard_map/ppermute | solution.py:314
  90.4 0.0 collective-permute-done.15.refs_4_
  90.4 1.8 %collective-permute-start.14 = (bf16[256,512]{1,0:T(8,128)(2,1)S(1)}, bf16[256,512]{1,0:T(8,128)(2,1)S(1)}, u32[]{:S(2)}, u32[]{:S(2)}) collective-permute-start(bf16[256,512]{1,0:T(8,128)(2,1)S(1)} %slice.23), channel_id=1, source_target_pairs={{0,96},{16,112},{32,0},{48,16},{64,32},{80,48},{96,64},{112,80},{1... | collective-permute-start | bytes 786440 | tf_op jit(solution)/shard_map/ppermute | solution.py:314
  92.2 0.4 collective-permute-start.19
  92.5 0.0 collective-permute-done.16.refs_5_
  92.5 0.1 collective-permute-start.20
  92.7 3.9 %transform.4 = (bf16[32,2,128,512]{3,2,1,0:T(8,128)(2,1)S(1)}, f32[32,8,128]{2,1,0:T(8,128)S(1)}) custom-call(s32[2,4]{1,0:T(2,128)S(1)} %collective-permute-done.4.refs_0_, s32[2,4]{1,0:T(2,128)S(1)} %collective-permute-done.6.refs_1_, bf16[512,512]{1,0:T(8,128)(2,1)S(1)} %collective-permute-done.2.refs_2_, ...), custom_call_target="tpu_custom_call", output_to_operand_aliasing={{0}: (12, {}), {1}: (13, {})} | custom-call | tf_op jit(solution)/shard_map/transform/pallas_call | solution.py:95
  96.6 2.0 %collective-permute-done.13.refs_3_ = bf16[256,512]{1,0:T(8,128)(2,1)S(1)} collective-permute-done((bf16[256,512]{1,0:T(8,128)(2,1)S(1)}, bf16[256,512]{1,0:T(8,128)(2,1)S(1)}, u32[]{:S(2)}, u32[]{:S(2)}) %collective-permute-start.13) | collective-permute-done | bytes 262176 | tf_op jit(solution)/shard_map/ppermute | solution.py:314
  98.6 0.0 collective-permute-done.14.refs_4_
  98.6 0.7 collective-permute-start.21
  99.3 0.1 collective-permute-start.22
  99.4 0.0 collective-permute-done.19.refs_5_
  99.4 0.0 collective-permute-done.20.refs_6_
  99.4 1.1 collective-permute-done.21.refs_7_
  100.5 0.4 collective-permute-done.22.refs_8_
  100.8 2.3 %transform.5 = (bf16[32,2,128,512]{3,2,1,0:T(8,128)(2,1)S(1)}, f32[32,8,128]{2,1,0:T(8,128)S(1)}) custom-call(s32[2,4]{1,0:T(2,128)S(1)} %collective-permute-done.5.refs_0_, bf16[256,512]{1,0:T(8,128)(2,1)S(1)} %collective-permute-done.9.refs_1_, ...), custom_call_target="tpu_custom_call", output_to_operand_aliasing={{0}: (11, {}), {1}: (12, {})} | custom-call | tf_op jit(solution)/shard_map/transform/pallas_call | solution.py:95
  103.1 0.0 copy-done
  103.1 47.1 %attend.1 = bf16[8,128,512]{2,1,0:T(8,128)(2,1)} custom-call(s32[8,12]{1,0:T(8,128)S(1)} %copy-done.2, s32[8,12]{1,0:T(8,128)S(1)} %fusion.23.slot_ref, bf16[8,128,512]{2,1,0:T(8,128)(2,1)S(1)} %bitcast.30, bf16[8,12,128,128]{3,2,1,0:T(8,128)(2,1)S(1)} %copy-done, f32[8,2,4,128,128]{4,3,2,1,0:T(8,128)S(1)} %targets.1.tile_ref, ...), custom_call_target="tpu_custom_call" | custom-call | tf_op jit(solution)/shard_map/attend/pallas_call | solution.py:254
  (38 shorter events, 0.3 us)
Async XLA Ops:
  0.0 3.7 %copy-start.7 = (s32[1,8,4]{1,2,0:T(4,128)S(1)}, s32[1,8,4]{1,2,0:T(4,128)}, u32[]{:S(2)}) copy-start(s32[1,8,4]{1,2,0:T(4,128)} %param.16) | copy-start | bytes 388
  3.7 8.4 %copy-start.5 = (f32[2,512]{1,0:T(2,128)S(1)}, f32[2,512]{1,0:T(2,128)}, u32[]{:S(2)}) copy-start(f32[2,512]{1,0:T(2,128)} %param.12) | copy-start | bytes 12292
  3.7 8.4 %copy-start.1 = (bf16[2,512,512]{2,1,0:T(8,128)(2,1)S(1)}, bf16[2,512,512]{2,1,0:T(8,128)(2,1)}, u32[]{:S(2)}) copy-start(bf16[2,512,512]{2,1,0:T(8,128)(2,1)} %refs_9_.1) | copy-start | bytes 3145732
  3.7 20.7 %collective-permute-start = (s32[8,4]{0,1:T(4,128)S(1)}, s32[8,4]{0,1:T(4,128)S(1)}, u32[]{:S(2)}, u32[]{:S(2)}) collective-permute-start(s32[8,4]{0,1:T(4,128)S(1)} %bitcast.35), channel_id=1, source_target_pairs={{0,16},{16,0},{32,48},{48,32},{64,80},{80,64},{96,112},{112,96},{1... | collective-permute-start | bytes 392 | tf_op jit(solution)/shard_map/ppermute | solution.py:314
  5.2 31.8 %all-to-all-start = ((bf16[16,64,768]{2,1,0:T(8,128)(2,1)}), bf16[16,64,768]{2,1,0:T(8,128)(2,1)}, u32[]{:S(2)}, u32[]{:S(2)}) async-start(bf16[16,64,768]{2,1,0:T(8,128)(2,1)} %arrange.2), calls=%async_computation | async-start | bytes 3145728 | tf_op jit(solution)/shard_map/all_to_all | solution.py:321
  12.1 4.6 %copy-start.4 = (f32[2,512]{1,0:T(2,128)S(1)}, f32[2,512]{1,0:T(2,128)}, u32[]{:S(2)}) copy-start(f32[2,512]{1,0:T(2,128)} %param.13) | copy-start | bytes 12292
  16.9 7.3 %copy-start.6 = (s32[8,12]{1,0:T(8,128)S(1)}, s32[8,12]{1,0:T(8,128)}, u32[]{:S(2)}) copy-start(s32[8,12]{1,0:T(8,128)} %param.17) | copy-start | bytes 1156
  38.1 5.7 %copy-start.3 = (bf16[1024,256]{1,0:T(8,128)(2,1)}, bf16[1024,256]{1,0:T(8,128)(2,1)S(1)}, u32[]{:S(2)}) copy-start(bf16[1024,256]{1,0:T(8,128)(2,1)S(1)} %slice.19) | copy-start | bytes 1572868
  38.1 5.7 %collective-permute-start.1 = (bf16[1024,256]{1,0:T(8,128)(2,1)S(1)}, bf16[1024,256]{1,0:T(8,128)(2,1)S(1)}, u32[]{:S(2)}, u32[]{:S(2)}) collective-permute-start(bf16[1024,256]{1,0:T(8,128)(2,1)S(1)} %slice.19), channel_id=1, source_target_pairs={{0,16},{16,0},{32,48},{48,32},{64,80},{80,64},{96,112},{112,96},{1... | collective-permute-start | bytes 1572872 | tf_op jit(solution)/shard_map/ppermute | solution.py:314
  39.5 23.8 %all-to-all-start.1 = ((bf16[16,64,512]{2,1,0:T(8,128)(2,1)}), bf16[16,64,512]{2,1,0:T(8,128)(2,1)}, u32[]{:S(2)}, u32[]{:S(2)}) async-start(bf16[16,64,512]{2,1,0:T(8,128)(2,1)} %arrange.3), calls=%async_computation.1 | async-start | bytes 2097152 | tf_op jit(solution)/shard_map/all_to_all | solution.py:334
  43.8 2.2 %copy-start.8 = (bf16[1024,256]{1,0:T(8,128)(2,1)}, bf16[1024,256]{1,0:T(8,128)(2,1)S(1)}, u32[]{:S(2)}) copy-start(bf16[1024,256]{1,0:T(8,128)(2,1)S(1)} %collective-permute-done.1) | copy-start | bytes 1572868
  46.0 17.2 %collective-permute-start.2 = (bf16[512,512]{1,0:T(8,128)(2,1)S(1)}, bf16[512,512]{1,0:T(8,128)(2,1)S(1)}, u32[]{:S(2)}, u32[]{:S(2)}) collective-permute-start(bf16[512,512]{1,0:T(8,128)(2,1)S(1)} %convolution_convert_fusion.1.refs_1_), channel_id=1, source_target_pairs={{0,32},{16,48},{32,64},{48,80},{64,96},{80,112},{96,0},{112,16},{1... | collective-permute-start | bytes 1572872 | tf_op jit(solution)/shard_map/ppermute | solution.py:314
  47.7 15.5 %collective-permute-start.3 = (bf16[512,512]{1,0:T(8,128)(2,1)S(1)}, bf16[512,512]{1,0:T(8,128)(2,1)S(1)}, u32[]{:S(2)}, u32[]{:S(2)}) collective-permute-start(bf16[512,512]{1,0:T(8,128)(2,1)S(1)} %convolution_convert_fusion.1.refs_1_), channel_id=1, source_target_pairs={{0,96},{16,112},{32,0},{48,16},{64,32},{80,48},{96,64},{112,80},{1... | collective-permute-start | bytes 1572872 | tf_op jit(solution)/shard_map/ppermute | solution.py:314
  49.9 12.3 %collective-permute-start.4 = (s32[2,4]{1,0:T(2,128)S(1)}, s32[2,4]{1,0:T(2,128)S(1)}, u32[]{:S(2)}, u32[]{:S(2)}) collective-permute-start(s32[2,4]{1,0:T(2,128)S(1)} %get-tuple-element.47), channel_id=1, source_target_pairs={{0,32},{16,48},{32,64},{48,80},{64,96},{80,112},{96,0},{112,16},{1... | collective-permute-start | bytes 104 | tf_op jit(solution)/shard_map/ppermute | solution.py:314
  49.9 13.3 %collective-permute-start.5 = (s32[2,4]{1,0:T(2,128)S(1)}, s32[2,4]{1,0:T(2,128)S(1)}, u32[]{:S(2)}, u32[]{:S(2)}) collective-permute-start(s32[2,4]{1,0:T(2,128)S(1)} %get-tuple-element.48), channel_id=1, source_target_pairs={{0,64},{16,80},{32,96},{48,112},{64,0},{80,16},{96,32},{112,48},{1... | collective-permute-start | bytes 104 | tf_op jit(solution)/shard_map/ppermute | solution.py:314
  52.5 10.7 %collective-permute-start.6 = (s32[2,4]{1,0:T(2,128)S(1)}, s32[2,4]{1,0:T(2,128)S(1)}, u32[]{:S(2)}, u32[]{:S(2)}) collective-permute-start(s32[2,4]{1,0:T(2,128)S(1)} %get-tuple-element.49), channel_id=1, source_target_pairs={{0,96},{16,112},{32,0},{48,16},{64,32},{80,48},{96,64},{112,80},{1... | collective-permute-start | bytes 104 | tf_op jit(solution)/shard_map/ppermute | solution.py:314
  62.3 9.5 %collective-permute-start.11 = (bf16[512,512]{1,0:T(8,128)(2,1)S(1)}, bf16[512,512]{1,0:T(8,128)(2,1)}, u32[]{:S(2)}, u32[]{:S(2)}) collective-permute-start(bf16[512,512]{1,0:T(8,128)(2,1)S(1)} %convolution_convert_fusion.1.refs_1_), channel_id=1, source_target_pairs={{0,16},{16,0},{32,48},{48,32},{64,80},{80,64},{96,112},{112,96},{1... | collective-permute-start | bytes 1572872 | tf_op jit(solution)/shard_map/ppermute | solution.py:314
  65.9 6.0 %collective-permute-start.12 = (bf16[512,512]{1,0:T(8,128)(2,1)S(1)}, bf16[512,512]{1,0:T(8,128)(2,1)S(1)}, u32[]{:S(2)}, u32[]{:S(2)}) collective-permute-start(bf16[512,512]{1,0:T(8,128)(2,1)S(1)} %convolution_convert_fusion.refs_2_), channel_id=1, source_target_pairs={{0,16},{16,0},{32,48},{48,32},{64,80},{80,64},{96,112},{112,96},{1... | collective-permute-start | bytes 1572872 | tf_op jit(solution)/shard_map/ppermute | solution.py:314
  66.6 21.5 %collective-permute-start.7 = (bf16[512,512]{1,0:T(8,128)(2,1)S(1)}, bf16[512,512]{1,0:T(8,128)(2,1)S(1)}, u32[]{:S(2)}, u32[]{:S(2)}) collective-permute-start(bf16[512,512]{1,0:T(8,128)(2,1)S(1)} %convolution_convert_fusion.refs_2_), channel_id=1, source_target_pairs={{0,32},{16,48},{32,64},{48,80},{64,96},{80,112},{96,0},{112,16},{1... | collective-permute-start | bytes 1572872 | tf_op jit(solution)/shard_map/ppermute | solution.py:314
  68.0 20.1 %collective-permute-start.8 = (bf16[512,512]{1,0:T(8,128)(2,1)S(1)}, bf16[512,512]{1,0:T(8,128)(2,1)S(1)}, u32[]{:S(2)}, u32[]{:S(2)}) collective-permute-start(bf16[512,512]{1,0:T(8,128)(2,1)S(1)} %convolution_convert_fusion.refs_2_), channel_id=1, source_target_pairs={{0,96},{16,112},{32,0},{48,16},{64,32},{80,48},{96,64},{112,80},{1... | collective-permute-start | bytes 1572872 | tf_op jit(solution)/shard_map/ppermute | solution.py:314
  70.2 17.0 %collective-permute-start.10 = (bf16[256,512]{1,0:T(8,128)(2,1)S(1)}, bf16[256,512]{1,0:T(8,128)(2,1)S(1)}, u32[]{:S(2)}, u32[]{:S(2)}) collective-permute-start(bf16[256,512]{1,0:T(8,128)(2,1)S(1)} %slice.21), channel_id=1, source_target_pairs={{0,96},{16,112},{32,0},{48,16},{64,32},{80,48},{96,64},{112,80},{1... | collective-permute-start | bytes 786440 | tf_op jit(solution)/shard_map/ppermute | solution.py:314
  71.7 16.4 %collective-permute-start.9 = (bf16[256,512]{1,0:T(8,128)(2,1)S(1)}, bf16[256,512]{1,0:T(8,128)(2,1)S(1)}, u32[]{:S(2)}, u32[]{:S(2)}) collective-permute-start(bf16[256,512]{1,0:T(8,128)(2,1)S(1)} %slice.20), channel_id=1, source_target_pairs={{0,32},{16,48},{32,64},{48,80},{64,96},{80,112},{96,0},{112,16},{1... | collective-permute-start | bytes 786440 | tf_op jit(solution)/shard_map/ppermute | solution.py:314
  71.8 18.5 %collective-permute-start.15 = (bf16[512,512]{1,0:T(8,128)(2,1)S(1)}, bf16[512,512]{1,0:T(8,128)(2,1)S(1)}, u32[]{:S(2)}, u32[]{:S(2)}) collective-permute-start(bf16[512,512]{1,0:T(8,128)(2,1)S(1)} %collective-permute-done.2.refs_2_), channel_id=1, source_target_pairs={{0,16},{16,0},{32,48},{48,32},{64,80},{80,64},{96,112},{112,96},{1... | collective-permute-start | bytes 1572872 | tf_op jit(solution)/shard_map/ppermute | solution.py:314
  87.2 5.0 %collective-permute-start.17 = (bf16[512,512]{1,0:T(8,128)(2,1)S(1)}, bf16[512,512]{1,0:T(8,128)(2,1)S(1)}, u32[]{:S(2)}, u32[]{:S(2)}) collective-permute-start(bf16[512,512]{1,0:T(8,128)(2,1)S(1)} %collective-permute-done.3.refs_6_), channel_id=1, source_target_pairs={{0,16},{16,0},{32,48},{48,32},{64,80},{80,64},{96,112},{112,96},{1... | collective-permute-start | bytes 1572872 | tf_op jit(solution)/shard_map/ppermute | solution.py:314
  88.2 4.3 %collective-permute-start.16 = (bf16[512,512]{1,0:T(8,128)(2,1)S(1)}, bf16[512,512]{1,0:T(8,128)(2,1)S(1)}, u32[]{:S(2)}, u32[]{:S(2)}) collective-permute-start(bf16[512,512]{1,0:T(8,128)(2,1)S(1)} %collective-permute-done.7.refs_3_), channel_id=1, source_target_pairs={{0,16},{16,0},{32,48},{48,32},{64,80},{80,64},{96,112},{112,96},{1... | collective-permute-start | bytes 1572872 | tf_op jit(solution)/shard_map/ppermute | solution.py:314
  88.6 4.0 %collective-permute-start.18 = (bf16[512,512]{1,0:T(8,128)(2,1)S(1)}, bf16[512,512]{1,0:T(8,128)(2,1)S(1)}, u32[]{:S(2)}, u32[]{:S(2)}) collective-permute-start(bf16[512,512]{1,0:T(8,128)(2,1)S(1)} %collective-permute-done.8.refs_7_), channel_id=1, source_target_pairs={{0,16},{16,0},{32,48},{48,32},{64,80},{80,64},{96,112},{112,96},{1... | collective-permute-start | bytes 1572872 | tf_op jit(solution)/shard_map/ppermute | solution.py:314
  88.8 9.8 %collective-permute-start.13 = (bf16[256,512]{1,0:T(8,128)(2,1)S(1)}, bf16[256,512]{1,0:T(8,128)(2,1)S(1)}, u32[]{:S(2)}, u32[]{:S(2)}) collective-permute-start(bf16[256,512]{1,0:T(8,128)(2,1)S(1)} %slice.22), channel_id=1, source_target_pairs={{0,32},{16,48},{32,64},{48,80},{64,96},{80,112},{96,0},{112,16},{1... | collective-permute-start | bytes 786440 | tf_op jit(solution)/shard_map/ppermute | solution.py:314
  90.4 8.2 %collective-permute-start.14 = (bf16[256,512]{1,0:T(8,128)(2,1)S(1)}, bf16[256,512]{1,0:T(8,128)(2,1)S(1)}, u32[]{:S(2)}, u32[]{:S(2)}) collective-permute-start(bf16[256,512]{1,0:T(8,128)(2,1)S(1)} %slice.23), channel_id=1, source_target_pairs={{0,96},{16,112},{32,0},{48,16},{64,32},{80,48},{96,64},{112,80},{1... | collective-permute-start | bytes 786440 | tf_op jit(solution)/shard_map/ppermute | solution.py:314
  92.2 7.2 %collective-permute-start.19 = (bf16[256,512]{1,0:T(8,128)(2,1)S(1)}, bf16[256,512]{1,0:T(8,128)(2,1)S(1)}, u32[]{:S(2)}, u32[]{:S(2)}) collective-permute-start(bf16[256,512]{1,0:T(8,128)(2,1)S(1)} %collective-permute-done.9.refs_1_), channel_id=1, source_target_pairs={{0,16},{16,0},{32,48},{48,32},{64,80},{80,64},{96,112},{112,96},{1... | collective-permute-start | bytes 786440 | tf_op jit(solution)/shard_map/ppermute | solution.py:314
  92.5 6.9 %collective-permute-start.20 = (bf16[256,512]{1,0:T(8,128)(2,1)S(1)}, bf16[256,512]{1,0:T(8,128)(2,1)S(1)}, u32[]{:S(2)}, u32[]{:S(2)}) collective-permute-start(bf16[256,512]{1,0:T(8,128)(2,1)S(1)} %collective-permute-done.10.refs_2_), channel_id=1, source_target_pairs={{0,16},{16,0},{32,48},{48,32},{64,80},{80,64},{96,112},{112,96},{1... | collective-permute-start | bytes 786440 | tf_op jit(solution)/shard_map/ppermute | solution.py:314
  98.6 4.5 %copy-start.2 = (s32[8,12]{1,0:T(8,128)S(1)}, s32[8,12]{1,0:T(8,128)}, u32[]{:S(2)}) copy-start(s32[8,12]{1,0:T(8,128)} %rel_ref.1) | copy-start | bytes 1156
  98.6 1.8 %collective-permute-start.21 = (bf16[256,512]{1,0:T(8,128)(2,1)S(1)}, bf16[256,512]{1,0:T(8,128)(2,1)S(1)}, u32[]{:S(2)}, u32[]{:S(2)}) collective-permute-start(bf16[256,512]{1,0:T(8,128)(2,1)S(1)} %collective-permute-done.13.refs_3_), channel_id=1, source_target_pairs={{0,16},{16,0},{32,48},{48,32},{64,80},{80,64},{96,112},{112,96},{1... | collective-permute-start | bytes 786440 | tf_op jit(solution)/shard_map/ppermute | solution.py:314
  99.3 1.5 %collective-permute-start.22 = (bf16[256,512]{1,0:T(8,128)(2,1)S(1)}, bf16[256,512]{1,0:T(8,128)(2,1)S(1)}, u32[]{:S(2)}, u32[]{:S(2)}) collective-permute-start(bf16[256,512]{1,0:T(8,128)(2,1)S(1)} %collective-permute-done.14.refs_4_), channel_id=1, source_target_pairs={{0,16},{16,0},{32,48},{48,32},{64,80},{80,64},{96,112},{112,96},{1... | collective-permute-start | bytes 786440 | tf_op jit(solution)/shard_map/ppermute | solution.py:314
  100.8 2.3 %copy-start = (bf16[8,12,128,128]{3,2,1,0:T(8,128)(2,1)S(1)}, bf16[8,12,128,128]{3,2,1,0:T(8,128)(2,1)}, u32[]{:S(2)}) copy-start(bf16[8,12,128,128]{3,2,1,0:T(8,128)(2,1)} %caps.1.cap_ref) | copy-start | bytes 9437188

commit v20 on v19

--- a/solution.py
+++ b/solution.py
@@ -360,17 +360,20 @@
     far_a = forward(up_a, down_a)
     b = project(later)
     up_b, down_b = ring(b)
-    done = spread(both([(a, 0, cut), (b, cut, local_blocks)]), 0, near, (None, None))
     hidden = jnp.concatenate([a, b])
     tiles = target_tiles(hidden, tgt_vectors, local_blocks, relation_weight.shape[0])
-    up_b, down_b, far_a, tiles, done = lax.optimization_barrier((up_b, down_b, far_a, tiles, done))
+    later_a, later_b, tiles = lax.optimization_barrier((a, b, tiles))
+    front, back = (0, cut), (cut, local_blocks)
+    own = [[(a, *front), (b, *back)], [(send(later_a, 0, 1), *front), (send(later_b, 0, 1), *back)]]
+    done = spread(own, 0, near, (None, None))
+    swap_up, swap_down = send(up_a, 0, 1), send(down_a, 0, 1)
+    up_b, down_b, far_a, tiles, done, swap_up, swap_down = lax.optimization_barrier(
+        (up_b, down_b, far_a, tiles, done, swap_up, swap_down)
+    )
     far_b = forward(up_b, down_b)
-    done = spread(
-        both([(up_a, 0, cut), (up_b, cut, local_blocks)]) + both([(down_a, 0, cut), (down_b, cut, local_blocks)]),
-        2,
-        (lists[0], lists[2]),
-        done,
-    )
+    rows = [[(up_a, *front), (up_b, *back)], [(swap_up, *front), (send(up_b, 0, 1), *back)]]
+    rows += [[(down_a, *front), (down_b, *back)], [(swap_down, *front), (send(down_b, 0, 1), *back)]]
+    done = spread(rows, 2, (lists[0], lists[2]), done)
     far_b, done = lax.optimization_barrier((far_b, done))
     quarter = cut // 2
     far = [(x, n * quarter, (n + 1) * quarter) for n, x in enumerate(far_a + far_b)]

time: 151 us -> 157 us (1.040)
  waiting for transfers between devices: 33.2 us -> 37.4 us
  starting transfers between devices: 34.9 us -> 37.4 us
    ppermute x23, waiting for transfers between devices: 20.9 us -> 25.1 us  [send(): return lax.ppermute(x, 'graph', pairs)]
    ppermute x23, starting transfers between devices: 23.7 us -> 26.2 us  [send(): return lax.ppermute(x, 'graph', pairs)]
  transfers between devices with their start and end apart: 25 -> 25, of which waited for: 7 -> 8; matrix products, arithmetic and copies ran while one was open for 4% -> 3% of each run, Pallas kernels for 14% -> 11%
where the time goes in v20:
time: 157 us; the launch traced here: 156 us
  Pallas kernels  73.4 us (47%)
  starting transfers between devices  37.4 us (24%)
  waiting for transfers between devices  37.4 us (24%)
  matrix products  5.67 us (4%)
    pallas_call x1, Pallas kernels, attend(): pl.pallas_call(attend_kernel, in_specs=[scalars] * 2 + [inside] * 5, out_...  47.1 us
    ppermute x23, starting transfers between devices, send(): return lax.ppermute(x, 'graph', pairs)  26.2 us
    ppermute x23, waiting for transfers between devices, send(): return lax.ppermute(x, 'graph', pairs)  25.1 us
    all_to_all x1, waiting for transfers between devices, shards(): lax.all_to_all(first, 'feat', 0, 0, tiled=True)  12.3 us
    pallas_call x3, Pallas kernels, transform(): pl.pallas_call(functools.partial(transform_kernel, bounds, first), in_spe...  8.36 us
    pallas_call x2, Pallas kernels, arrange(): pl.pallas_call(functools.partial(arrange_kernel, low, high), grid_spec=pl...  7.26 us
    pallas_call x1, Pallas kernels, caps(): pl.pallas_call(cap_kernel, grid=shape[:1], in_specs=[spec], out_specs=spe...  6.92 us
    all_to_all x1, starting transfers between devices, shards(): lax.all_to_all(first, 'feat', 0, 0, tiled=True)  6.88 us
  transfers between devices with their start and end apart: 25, of which 8 were waited for; matrix products, arithmetic and copies ran while one was open for 3% of the time, Pallas kernels for 11%

profile of v20, /device:TPU:1, one launch (start us, length us, event | category | flops | bytes accessed | tf_op | source)
XLA Modules:
  0.0 156.5 jit_solution(11590252187982075310)
XLA Ops:
  0.0 3.7 %arrange.2 = bf16[16,64,768]{2,1,0:T(8,128)(2,1)} custom-call(s32[1]{0:T(128)} %bitcast.core_ref, bf16[64,16384]{1,0:T(8,128)(2,1)} %bitcast.31, bf16[64,512]{1,0:T(8,128)(2,1)} %w_ref.3), custom_call_target="tpu_custom_call" | custom-call | tf_op jit(solution)/shard_map/arrange/pallas_call | solution.py:31
  3.7 1.5 collective-permute-start
  5.2 6.9 %all-to-all-start = ((bf16[16,64,768]{2,1,0:T(8,128)(2,1)}), bf16[16,64,768]{2,1,0:T(8,128)(2,1)}, u32[]{:S(2)}, u32[]{:S(2)}) async-start(bf16[16,64,768]{2,1,0:T(8,128)(2,1)} %arrange.2), calls=%async_computation | async-start | bytes 3145728 | tf_op jit(solution)/shard_map/all_to_all | solution.py:321
  12.1 0.0 copy-start.4
  12.1 0.9 fusion
  13.2 3.6 %arrange.3 = bf16[16,64,512]{2,1,0:T(8,128)(2,1)} custom-call(s32[1]{0:T(128)} %bitcast.core_ref, bf16[64,16384]{1,0:T(8,128)(2,1)} %bitcast.32, bf16[64,512]{1,0:T(8,128)(2,1)} %w_ref.3), custom_call_target="tpu_custom_call" | custom-call | tf_op jit(solution)/shard_map/arrange/pallas_call | solution.py:31
  16.8 0.1 copy.15
  16.9 0.0 copy-start.6
  16.9 6.9 %caps.1.cap_ref = bf16[8,12,128,128]{3,2,1,0:T(8,128)(2,1)} custom-call(s32[8,12,128,128]{3,2,1,0:T(8,128)} %mask_ref.1), custom_call_target="tpu_custom_call" | custom-call | tf_op jit(solution)/shard_map/caps/pallas_call | solution.py:117
  23.9 0.1 pad.19.clone
  23.9 0.1 select_multiply_fusion
  24.1 0.1 fusion.6
  24.3 0.1 maximum_maximum_fusion.refs_6_.refs_11_.refs_10_
  24.4 0.0 collective-permute-done
  24.4 0.3 fusion.10
  24.7 12.3 %all-to-all-done = bf16[16,64,768]{2,1,0:T(8,128)(2,1)} async-done(((bf16[16,64,768]{2,1,0:T(8,128)(2,1)}), bf16[16,64,768]{2,1,0:T(8,128)(2,1)}, u32[]{:S(2)}, u32[]{:S(2)}) %all-to-all-start) | async-done | bytes 1572896 | tf_op jit(solution)/shard_map/all_to_all | solution.py:321
  37.0 1.1 slice.19
  38.1 1.4 collective-permute-start.1
  39.5 4.3 %all-to-all-start.1 = ((bf16[16,64,512]{2,1,0:T(8,128)(2,1)}), bf16[16,64,512]{2,1,0:T(8,128)(2,1)}, u32[]{:S(2)}, u32[]{:S(2)}) async-start(bf16[16,64,512]{2,1,0:T(8,128)(2,1)} %arrange.3), calls=%async_computation.1 | async-start | bytes 2097152 | tf_op jit(solution)/shard_map/all_to_all | solution.py:334
  43.8 0.0 collective-permute-done.1
  43.8 2.2 %convolution_convert_fusion.1.refs_1_ = bf16[512,512]{1,0:T(8,128)(2,1)S(1)} fusion(bf16[1024,768]{1,0:T(8,128)(2,1)} %bitcast.2, bf16[1024,256]{1,0:T(8,128)(2,1)S(1)} %collective-permute-done.1, bf16[1024,256]{1,0:T(8,128)(2,1)S(1)} %slice.19, pred[]{:T(512)S(6)} %eq.30), kind=kOutput, calls=%fused_computation.1 | convolution fusion | flops 541851648 | bytes 2621441 | tf_op jit(solution)/shard_map/dot_general | solution.py:341
  46.0 1.7 %collective-permute-start.2 = (bf16[512,512]{1,0:T(8,128)(2,1)S(1)}, bf16[512,512]{1,0:T(8,128)(2,1)S(1)}, u32[]{:S(2)}, u32[]{:S(2)}) collective-permute-start(bf16[512,512]{1,0:T(8,128)(2,1)S(1)} %convolution_convert_fusion.1.refs_1_), channel_id=1, source_target_pairs={{0,32},{16,48},{32,64},{48,80},{64,96},{80,112},{96,0},{112,16},{1... | collective-permute-start | bytes 1572872 | tf_op jit(solution)/shard_map/ppermute | solution.py:314
  47.7 2.2 %collective-permute-start.3 = (bf16[512,512]{1,0:T(8,128)(2,1)S(1)}, bf16[512,512]{1,0:T(8,128)(2,1)S(1)}, u32[]{:S(2)}, u32[]{:S(2)}) collective-permute-start(bf16[512,512]{1,0:T(8,128)(2,1)S(1)} %convolution_convert_fusion.1.refs_1_), channel_id=1, source_target_pairs={{0,96},{16,112},{32,0},{48,16},{64,32},{80,48},{96,64},{112,80},{1... | collective-permute-start | bytes 1572872 | tf_op jit(solution)/shard_map/ppermute | solution.py:314
  49.9 0.0 collective-permute-start.4
  49.9 2.6 %collective-permute-start.5 = (s32[2,4]{1,0:T(2,128)S(1)}, s32[2,4]{1,0:T(2,128)S(1)}, u32[]{:S(2)}, u32[]{:S(2)}) collective-permute-start(s32[2,4]{1,0:T(2,128)S(1)} %get-tuple-element.53), channel_id=1, source_target_pairs={{0,64},{16,80},{32,96},{48,112},{64,0},{80,16},{96,32},{112,48},{1... | collective-permute-start | bytes 104 | tf_op jit(solution)/shard_map/ppermute | solution.py:314
  52.5 0.7 collective-permute-start.6
  53.2 9.0 %collective-permute-done.4.refs_0_ = s32[2,4]{1,0:T(2,128)S(1)} collective-permute-done((s32[2,4]{1,0:T(2,128)S(1)}, s32[2,4]{1,0:T(2,128)S(1)}, u32[]{:S(2)}, u32[]{:S(2)}) %collective-permute-start.4) | collective-permute-done | bytes 64 | tf_op jit(solution)/shard_map/ppermute | solution.py:314
  62.3 1.0 collective-permute-done.5.refs_0_
  63.3 0.0 collective-permute-done.6.refs_1_
  63.3 2.6 %convolution_convert_fusion.refs_2_ = bf16[512,512]{1,0:T(8,128)(2,1)S(1)} fusion(bf16[1024,512]{1,0:T(8,128)(2,1)} %bitcast.11, bf16[1024,256]{1,0:T(8,128)(2,1)} %copy-done.8, bf16[1024,256]{1,0:T(8,128)(2,1)} %copy-done.3, pred[]{:T(512)S(6)} %eq.30), kind=kOutput, calls=%fused_computation | convolution fusion | flops 541851648 | bytes 2621441 | tf_op jit(solution)/shard_map/dot_general | solution.py:341
  65.9 0.1 pad_maximum_fusion
  65.9 3.7 %targets.1.tile_ref = f32[8,2,4,128,128]{4,3,2,1,0:T(8,128)S(1)} custom-call(bf16[8,128,512]{2,1,0:T(8,128)(2,1)S(1)} %bitcast.29, bf16[3,512,128]{2,1,0:T(8,128)(2,1)S(1)} %pad_maximum_fusion.1.tgt_ref), custom_call_target="tpu_custom_call" | custom-call | tf_op jit(solution)/shard_map/targets/pallas_call | solution.py:147
  69.7 0.8 collective-permute-start.11
  70.4 0.1 collective-permute-start.12
  70.6 3.6 %collective-permute-start.10 = (bf16[256,512]{1,0:T(8,128)(2,1)S(1)}, bf16[256,512]{1,0:T(8,128)(2,1)S(1)}, u32[]{:S(2)}, u32[]{:S(2)}) collective-permute-start(bf16[256,512]{1,0:T(8,128)(2,1)S(1)} %slice.21), channel_id=1, source_target_pairs={{0,96},{16,112},{32,0},{48,16},{64,32},{80,48},{96,64},{112,80},{1... | collective-permute-start | bytes 786440 | tf_op jit(solution)/shard_map/ppermute | solution.py:314
  74.1 0.0 collective-permute-start.7
  74.1 2.7 %collective-permute-start.8 = (bf16[512,512]{1,0:T(8,128)(2,1)S(1)}, bf16[512,512]{1,0:T(8,128)(2,1)S(1)}, u32[]{:S(2)}, u32[]{:S(2)}) collective-permute-start(bf16[512,512]{1,0:T(8,128)(2,1)S(1)} %convolution_convert_fusion.refs_2_), channel_id=1, source_target_pairs={{0,96},{16,112},{32,0},{48,16},{64,32},{80,48},{96,64},{112,80},{1... | collective-permute-start | bytes 1572872 | tf_op jit(solution)/shard_map/ppermute | solution.py:314
  76.8 2.6 %collective-permute-done.10.refs_2_ = bf16[256,512]{1,0:T(8,128)(2,1)S(1)} collective-permute-done((bf16[256,512]{1,0:T(8,128)(2,1)S(1)}, bf16[256,512]{1,0:T(8,128)(2,1)S(1)}, u32[]{:S(2)}, u32[]{:S(2)}) %collective-permute-start.10) | collective-permute-done | bytes 262176 | tf_op jit(solution)/shard_map/ppermute | solution.py:314
  79.4 2.1 %collective-permute-start.13 = (bf16[512,512]{1,0:T(8,128)(2,1)S(1)}, bf16[512,512]{1,0:T(8,128)(2,1)S(1)}, u32[]{:S(2)}, u32[]{:S(2)}) collective-permute-start(bf16[512,512]{1,0:T(8,128)(2,1)S(1)} %collective-permute-done.2.refs_2_), channel_id=1, source_target_pairs={{0,16},{16,0},{32,48},{48,32},{64,80},{80,64},{96,112},{112,96},{1... | collective-permute-start | bytes 1572872 | tf_op jit(solution)/shard_map/ppermute | solution.py:314
  81.5 0.0 collective-permute-start.14
  81.5 0.0 collective-permute-done.12.refs_4_
  81.5 0.1 collective-permute-start.9
  81.7 2.2 %transform.3 = (bf16[32,2,128,512]{3,2,1,0:T(8,128)(2,1)S(1)}, f32[32,8,128]{2,1,0:T(8,128)S(1)}) custom-call(s32[2,4]{1,0:T(2,128)S(1)} %get-tuple-element.61.refs_0_, bf16[512,512]{1,0:T(8,128)(2,1)S(1)} %convolution_convert_fusion.1.refs_1_, bf16[512,512]{1,0:T(8,128)(2,1)S(1)} %convolution_convert_fusion.refs_2_, ...), custom_call_target="tpu_custom_call" | custom-call | tf_op jit(solution)/shard_map/transform/pallas_call | solution.py:95
  83.8 9.9 %collective-permute-done.9.refs_1_ = bf16[256,512]{1,0:T(8,128)(2,1)S(1)} collective-permute-done((bf16[256,512]{1,0:T(8,128)(2,1)S(1)}, bf16[256,512]{1,0:T(8,128)(2,1)S(1)}, u32[]{:S(2)}, u32[]{:S(2)}) %collective-permute-start.9) | collective-permute-done | bytes 262176 | tf_op jit(solution)/shard_map/ppermute | solution.py:314
  93.7 0.0 collective-permute-done.7.refs_3_
  93.7 0.0 collective-permute-done.8.refs_7_
  93.7 0.0 collective-permute-done.13.refs_4_
  93.7 1.7 %collective-permute-start.17 = (bf16[512,512]{1,0:T(8,128)(2,1)S(1)}, bf16[512,512]{1,0:T(8,128)(2,1)S(1)}, u32[]{:S(2)}, u32[]{:S(2)}) collective-permute-start(bf16[512,512]{1,0:T(8,128)(2,1)S(1)} %collective-permute-done.7.refs_3_), channel_id=1, source_target_pairs={{0,16},{16,0},{32,48},{48,32},{64,80},{80,64},{96,112},{112,96},{1... | collective-permute-start | bytes 1572872 | tf_op jit(solution)/shard_map/ppermute | solution.py:314
  95.4 0.1 collective-permute-start.18
  95.5 0.1 collective-permute-start.15
  95.6 2.7 %collective-permute-start.16 = (bf16[256,512]{1,0:T(8,128)(2,1)S(1)}, bf16[256,512]{1,0:T(8,128)(2,1)S(1)}, u32[]{:S(2)}, u32[]{:S(2)}) collective-permute-start(bf16[256,512]{1,0:T(8,128)(2,1)S(1)} %slice.23), channel_id=1, source_target_pairs={{0,96},{16,112},{32,0},{48,16},{64,32},{80,48},{96,64},{112,80},{1... | collective-permute-start | bytes 786440 | tf_op jit(solution)/shard_map/ppermute | solution.py:314
  98.3 1.0 collective-permute-start.19
  99.3 0.0 collective-permute-done.17.refs_5_
  99.3 0.0 collective-permute-start.20
  99.3 0.0 collective-permute-done.18.refs_9_
  99.3 3.9 %transform.4 = (bf16[32,2,128,512]{3,2,1,0:T(8,128)(2,1)S(1)}, f32[32,8,128]{2,1,0:T(8,128)S(1)}) custom-call(s32[2,4]{1,0:T(2,128)S(1)} %collective-permute-done.4.refs_0_, s32[2,4]{1,0:T(2,128)S(1)} %collective-permute-done.6.refs_1_, bf16[512,512]{1,0:T(8,128)(2,1)S(1)} %collective-permute-done.2.refs_2_, ...), custom_call_target="tpu_custom_call", output_to_operand_aliasing={{0}: (12, {}), {1}: (13, {})} | custom-call | tf_op jit(solution)/shard_map/transform/pallas_call | solution.py:95
  103.2 1.1 collective-permute-done.15.refs_3_
  104.3 1.3 collective-permute-start.21
  105.5 0.1 collective-permute-start.22
  105.6 1.1 collective-permute-done.21.refs_7_
  106.7 0.4 collective-permute-done.22.refs_8_
  107.1 2.3 %transform.5 = (bf16[32,2,128,512]{3,2,1,0:T(8,128)(2,1)S(1)}, f32[32,8,128]{2,1,0:T(8,128)S(1)}) custom-call(s32[2,4]{1,0:T(2,128)S(1)} %collective-permute-done.5.refs_0_, bf16[256,512]{1,0:T(8,128)(2,1)S(1)} %collective-permute-done.9.refs_1_, ...), custom_call_target="tpu_custom_call", output_to_operand_aliasing={{0}: (11, {}), {1}: (12, {})} | custom-call | tf_op jit(solution)/shard_map/transform/pallas_call | solution.py:95
  109.4 0.0 copy-done
  109.4 47.1 %attend.1 = bf16[8,128,512]{2,1,0:T(8,128)(2,1)} custom-call(s32[8,12]{1,0:T(8,128)S(1)} %copy-done.2, s32[8,12]{1,0:T(8,128)S(1)} %fusion.23.slot_ref, bf16[8,128,512]{2,1,0:T(8,128)(2,1)S(1)} %bitcast.30, bf16[8,12,128,128]{3,2,1,0:T(8,128)(2,1)S(1)} %copy-done, f32[8,2,4,128,128]{4,3,2,1,0:T(8,128)S(1)} %targets.1.tile_ref, ...), custom_call_target="tpu_custom_call" | custom-call | tf_op jit(solution)/shard_map/attend/pallas_call | solution.py:254
  (38 shorter events, 0.3 us)
Async XLA Ops:
  0.0 3.7 %copy-start.7 = (s32[1,8,4]{1,2,0:T(4,128)S(1)}, s32[1,8,4]{1,2,0:T(4,128)}, u32[]{:S(2)}) copy-start(s32[1,8,4]{1,2,0:T(4,128)} %param.16) | copy-start | bytes 388
  3.7 8.4 %copy-start.5 = (f32[2,512]{1,0:T(2,128)S(1)}, f32[2,512]{1,0:T(2,128)}, u32[]{:S(2)}) copy-start(f32[2,512]{1,0:T(2,128)} %param.12) | copy-start | bytes 12292
  3.7 8.4 %copy-start.1 = (bf16[2,512,512]{2,1,0:T(8,128)(2,1)S(1)}, bf16[2,512,512]{2,1,0:T(8,128)(2,1)}, u32[]{:S(2)}) copy-start(bf16[2,512,512]{2,1,0:T(8,128)(2,1)} %refs_9_.1) | copy-start | bytes 3145732
  3.7 20.7 %collective-permute-start = (s32[8,4]{0,1:T(4,128)S(1)}, s32[8,4]{0,1:T(4,128)S(1)}, u32[]{:S(2)}, u32[]{:S(2)}) collective-permute-start(s32[8,4]{0,1:T(4,128)S(1)} %bitcast.35), channel_id=1, source_target_pairs={{0,16},{16,0},{32,48},{48,32},{64,80},{80,64},{96,112},{112,96},{1... | collective-permute-start | bytes 392 | tf_op jit(solution)/shard_map/ppermute | solution.py:314
  5.2 31.8 %all-to-all-start = ((bf16[16,64,768]{2,1,0:T(8,128)(2,1)}), bf16[16,64,768]{2,1,0:T(8,128)(2,1)}, u32[]{:S(2)}, u32[]{:S(2)}) async-start(bf16[16,64,768]{2,1,0:T(8,128)(2,1)} %arrange.2), calls=%async_computation | async-start | bytes 3145728 | tf_op jit(solution)/shard_map/all_to_all | solution.py:321
  12.1 4.6 %copy-start.4 = (f32[2,512]{1,0:T(2,128)S(1)}, f32[2,512]{1,0:T(2,128)}, u32[]{:S(2)}) copy-start(f32[2,512]{1,0:T(2,128)} %param.13) | copy-start | bytes 12292
  16.9 7.3 %copy-start.6 = (s32[8,12]{1,0:T(8,128)S(1)}, s32[8,12]{1,0:T(8,128)}, u32[]{:S(2)}) copy-start(s32[8,12]{1,0:T(8,128)} %param.17) | copy-start | bytes 1156
  38.1 5.7 %copy-start.3 = (bf16[1024,256]{1,0:T(8,128)(2,1)}, bf16[1024,256]{1,0:T(8,128)(2,1)S(1)}, u32[]{:S(2)}) copy-start(bf16[1024,256]{1,0:T(8,128)(2,1)S(1)} %slice.19) | copy-start | bytes 1572868
  38.1 5.7 %collective-permute-start.1 = (bf16[1024,256]{1,0:T(8,128)(2,1)S(1)}, bf16[1024,256]{1,0:T(8,128)(2,1)S(1)}, u32[]{:S(2)}, u32[]{:S(2)}) collective-permute-start(bf16[1024,256]{1,0:T(8,128)(2,1)S(1)} %slice.19), channel_id=1, source_target_pairs={{0,16},{16,0},{32,48},{48,32},{64,80},{80,64},{96,112},{112,96},{1... | collective-permute-start | bytes 1572872 | tf_op jit(solution)/shard_map/ppermute | solution.py:314
  39.5 23.8 %all-to-all-start.1 = ((bf16[16,64,512]{2,1,0:T(8,128)(2,1)}), bf16[16,64,512]{2,1,0:T(8,128)(2,1)}, u32[]{:S(2)}, u32[]{:S(2)}) async-start(bf16[16,64,512]{2,1,0:T(8,128)(2,1)} %arrange.3), calls=%async_computation.1 | async-start | bytes 2097152 | tf_op jit(solution)/shard_map/all_to_all | solution.py:334
  43.8 2.2 %copy-start.8 = (bf16[1024,256]{1,0:T(8,128)(2,1)}, bf16[1024,256]{1,0:T(8,128)(2,1)S(1)}, u32[]{:S(2)}) copy-start(bf16[1024,256]{1,0:T(8,128)(2,1)S(1)} %collective-permute-done.1) | copy-start | bytes 1572868
  46.0 17.2 %collective-permute-start.2 = (bf16[512,512]{1,0:T(8,128)(2,1)S(1)}, bf16[512,512]{1,0:T(8,128)(2,1)S(1)}, u32[]{:S(2)}, u32[]{:S(2)}) collective-permute-start(bf16[512,512]{1,0:T(8,128)(2,1)S(1)} %convolution_convert_fusion.1.refs_1_), channel_id=1, source_target_pairs={{0,32},{16,48},{32,64},{48,80},{64,96},{80,112},{96,0},{112,16},{1... | collective-permute-start | bytes 1572872 | tf_op jit(solution)/shard_map/ppermute | solution.py:314
  47.7 15.5 %collective-permute-start.3 = (bf16[512,512]{1,0:T(8,128)(2,1)S(1)}, bf16[512,512]{1,0:T(8,128)(2,1)S(1)}, u32[]{:S(2)}, u32[]{:S(2)}) collective-permute-start(bf16[512,512]{1,0:T(8,128)(2,1)S(1)} %convolution_convert_fusion.1.refs_1_), channel_id=1, source_target_pairs={{0,96},{16,112},{32,0},{48,16},{64,32},{80,48},{96,64},{112,80},{1... | collective-permute-start | bytes 1572872 | tf_op jit(solution)/shard_map/ppermute | solution.py:314
  49.9 12.3 %collective-permute-start.4 = (s32[2,4]{1,0:T(2,128)S(1)}, s32[2,4]{1,0:T(2,128)S(1)}, u32[]{:S(2)}, u32[]{:S(2)}) collective-permute-start(s32[2,4]{1,0:T(2,128)S(1)} %get-tuple-element.52), channel_id=1, source_target_pairs={{0,32},{16,48},{32,64},{48,80},{64,96},{80,112},{96,0},{112,16},{1... | collective-permute-start | bytes 104 | tf_op jit(solution)/shard_map/ppermute | solution.py:314
  49.9 13.3 %collective-permute-start.5 = (s32[2,4]{1,0:T(2,128)S(1)}, s32[2,4]{1,0:T(2,128)S(1)}, u32[]{:S(2)}, u32[]{:S(2)}) collective-permute-start(s32[2,4]{1,0:T(2,128)S(1)} %get-tuple-element.53), channel_id=1, source_target_pairs={{0,64},{16,80},{32,96},{48,112},{64,0},{80,16},{96,32},{112,48},{1... | collective-permute-start | bytes 104 | tf_op jit(solution)/shard_map/ppermute | solution.py:314
  52.5 10.7 %collective-permute-start.6 = (s32[2,4]{1,0:T(2,128)S(1)}, s32[2,4]{1,0:T(2,128)S(1)}, u32[]{:S(2)}, u32[]{:S(2)}) collective-permute-start(s32[2,4]{1,0:T(2,128)S(1)} %get-tuple-element.54), channel_id=1, source_target_pairs={{0,96},{16,112},{32,0},{48,16},{64,32},{80,48},{96,64},{112,80},{1... | collective-permute-start | bytes 104 | tf_op jit(solution)/shard_map/ppermute | solution.py:314
  69.7 11.8 %collective-permute-start.11 = (bf16[512,512]{1,0:T(8,128)(2,1)S(1)}, bf16[512,512]{1,0:T(8,128)(2,1)S(1)}, u32[]{:S(2)}, u32[]{:S(2)}) collective-permute-start(bf16[512,512]{1,0:T(8,128)(2,1)S(1)} %convolution_convert_fusion.1.refs_1_), channel_id=1, source_target_pairs={{0,16},{16,0},{32,48},{48,32},{64,80},{80,64},{96,112},{112,96},{1... | collective-permute-start | bytes 1572872 | tf_op jit(solution)/shard_map/ppermute | solution.py:314
  70.4 11.1 %collective-permute-start.12 = (bf16[512,512]{1,0:T(8,128)(2,1)S(1)}, bf16[512,512]{1,0:T(8,128)(2,1)S(1)}, u32[]{:S(2)}, u32[]{:S(2)}) collective-permute-start(bf16[512,512]{1,0:T(8,128)(2,1)S(1)} %convolution_convert_fusion.refs_2_), channel_id=1, source_target_pairs={{0,16},{16,0},{32,48},{48,32},{64,80},{80,64},{96,112},{112,96},{1... | collective-permute-start | bytes 1572872 | tf_op jit(solution)/shard_map/ppermute | solution.py:314
  70.6 8.8 %collective-permute-start.10 = (bf16[256,512]{1,0:T(8,128)(2,1)S(1)}, bf16[256,512]{1,0:T(8,128)(2,1)S(1)}, u32[]{:S(2)}, u32[]{:S(2)}) collective-permute-start(bf16[256,512]{1,0:T(8,128)(2,1)S(1)} %slice.21), channel_id=1, source_target_pairs={{0,96},{16,112},{32,0},{48,16},{64,32},{80,48},{96,64},{112,80},{1... | collective-permute-start | bytes 786440 | tf_op jit(solution)/shard_map/ppermute | solution.py:314
  74.1 19.6 %collective-permute-start.7 = (bf16[512,512]{1,0:T(8,128)(2,1)S(1)}, bf16[512,512]{1,0:T(8,128)(2,1)S(1)}, u32[]{:S(2)}, u32[]{:S(2)}) collective-permute-start(bf16[512,512]{1,0:T(8,128)(2,1)S(1)} %convolution_convert_fusion.refs_2_), channel_id=1, source_target_pairs={{0,32},{16,48},{32,64},{48,80},{64,96},{80,112},{96,0},{112,16},{1... | collective-permute-start | bytes 1572872 | tf_op jit(solution)/shard_map/ppermute | solution.py:314
  74.1 19.6 %collective-permute-start.8 = (bf16[512,512]{1,0:T(8,128)(2,1)S(1)}, bf16[512,512]{1,0:T(8,128)(2,1)S(1)}, u32[]{:S(2)}, u32[]{:S(2)}) collective-permute-start(bf16[512,512]{1,0:T(8,128)(2,1)S(1)} %convolution_convert_fusion.refs_2_), channel_id=1, source_target_pairs={{0,96},{16,112},{32,0},{48,16},{64,32},{80,48},{96,64},{112,80},{1... | collective-permute-start | bytes 1572872 | tf_op jit(solution)/shard_map/ppermute | solution.py:314
  79.4 14.3 %collective-permute-start.13 = (bf16[512,512]{1,0:T(8,128)(2,1)S(1)}, bf16[512,512]{1,0:T(8,128)(2,1)S(1)}, u32[]{:S(2)}, u32[]{:S(2)}) collective-permute-start(bf16[512,512]{1,0:T(8,128)(2,1)S(1)} %collective-permute-done.2.refs_2_), channel_id=1, source_target_pairs={{0,16},{16,0},{32,48},{48,32},{64,80},{80,64},{96,112},{112,96},{1... | collective-permute-start | bytes 1572872 | tf_op jit(solution)/shard_map/ppermute | solution.py:314
  81.5 12.2 %collective-permute-start.14 = (bf16[512,512]{1,0:T(8,128)(2,1)S(1)}, bf16[512,512]{1,0:T(8,128)(2,1)S(1)}, u32[]{:S(2)}, u32[]{:S(2)}) collective-permute-start(bf16[512,512]{1,0:T(8,128)(2,1)S(1)} %collective-permute-done.3.refs_6_), channel_id=1, source_target_pairs={{0,16},{16,0},{32,48},{48,32},{64,80},{80,64},{96,112},{112,96},{1... | collective-permute-start | bytes 1572872 | tf_op jit(solution)/shard_map/ppermute | solution.py:314
  81.5 12.2 %collective-permute-start.9 = (bf16[256,512]{1,0:T(8,128)(2,1)S(1)}, bf16[256,512]{1,0:T(8,128)(2,1)S(1)}, u32[]{:S(2)}, u32[]{:S(2)}) collective-permute-start(bf16[256,512]{1,0:T(8,128)(2,1)S(1)} %slice.20), channel_id=1, source_target_pairs={{0,32},{16,48},{32,64},{48,80},{64,96},{80,112},{96,0},{112,16},{1... | collective-permute-start | bytes 786440 | tf_op jit(solution)/shard_map/ppermute | solution.py:314
  93.7 5.5 %collective-permute-start.17 = (bf16[512,512]{1,0:T(8,128)(2,1)S(1)}, bf16[512,512]{1,0:T(8,128)(2,1)S(1)}, u32[]{:S(2)}, u32[]{:S(2)}) collective-permute-start(bf16[512,512]{1,0:T(8,128)(2,1)S(1)} %collective-permute-done.7.refs_3_), channel_id=1, source_target_pairs={{0,16},{16,0},{32,48},{48,32},{64,80},{80,64},{96,112},{112,96},{1... | collective-permute-start | bytes 1572872 | tf_op jit(solution)/shard_map/ppermute | solution.py:314
  95.4 3.9 %collective-permute-start.18 = (bf16[512,512]{1,0:T(8,128)(2,1)S(1)}, bf16[512,512]{1,0:T(8,128)(2,1)S(1)}, u32[]{:S(2)}, u32[]{:S(2)}) collective-permute-start(bf16[512,512]{1,0:T(8,128)(2,1)S(1)} %collective-permute-done.8.refs_7_), channel_id=1, source_target_pairs={{0,16},{16,0},{32,48},{48,32},{64,80},{80,64},{96,112},{112,96},{1... | collective-permute-start | bytes 1572872 | tf_op jit(solution)/shard_map/ppermute | solution.py:314
  95.5 8.8 %collective-permute-start.15 = (bf16[256,512]{1,0:T(8,128)(2,1)S(1)}, bf16[256,512]{1,0:T(8,128)(2,1)S(1)}, u32[]{:S(2)}, u32[]{:S(2)}) collective-permute-start(bf16[256,512]{1,0:T(8,128)(2,1)S(1)} %slice.22), channel_id=1, source_target_pairs={{0,32},{16,48},{32,64},{48,80},{64,96},{80,112},{96,0},{112,16},{1... | collective-permute-start | bytes 786440 | tf_op jit(solution)/shard_map/ppermute | solution.py:314
  95.6 8.7 %collective-permute-start.16 = (bf16[256,512]{1,0:T(8,128)(2,1)S(1)}, bf16[256,512]{1,0:T(8,128)(2,1)S(1)}, u32[]{:S(2)}, u32[]{:S(2)}) collective-permute-start(bf16[256,512]{1,0:T(8,128)(2,1)S(1)} %slice.23), channel_id=1, source_target_pairs={{0,96},{16,112},{32,0},{48,16},{64,32},{80,48},{96,64},{112,80},{1... | collective-permute-start | bytes 786440 | tf_op jit(solution)/shard_map/ppermute | solution.py:314
  98.3 7.3 %collective-permute-start.19 = (bf16[256,512]{1,0:T(8,128)(2,1)S(1)}, bf16[256,512]{1,0:T(8,128)(2,1)S(1)}, u32[]{:S(2)}, u32[]{:S(2)}) collective-permute-start(bf16[256,512]{1,0:T(8,128)(2,1)S(1)} %collective-permute-done.9.refs_1_), channel_id=1, source_target_pairs={{0,16},{16,0},{32,48},{48,32},{64,80},{80,64},{96,112},{112,96},{1... | collective-permute-start | bytes 786440 | tf_op jit(solution)/shard_map/ppermute | solution.py:314
  99.3 6.4 %collective-permute-start.20 = (bf16[256,512]{1,0:T(8,128)(2,1)S(1)}, bf16[256,512]{1,0:T(8,128)(2,1)S(1)}, u32[]{:S(2)}, u32[]{:S(2)}) collective-permute-start(bf16[256,512]{1,0:T(8,128)(2,1)S(1)} %collective-permute-done.10.refs_2_), channel_id=1, source_target_pairs={{0,16},{16,0},{32,48},{48,32},{64,80},{80,64},{96,112},{112,96},{1... | collective-permute-start | bytes 786440 | tf_op jit(solution)/shard_map/ppermute | solution.py:314
  104.3 5.1 %copy-start.2 = (s32[8,12]{1,0:T(8,128)S(1)}, s32[8,12]{1,0:T(8,128)}, u32[]{:S(2)}) copy-start(s32[8,12]{1,0:T(8,128)} %rel_ref.1) | copy-start | bytes 1156
  104.3 2.4 %collective-permute-start.21 = (bf16[256,512]{1,0:T(8,128)(2,1)S(1)}, bf16[256,512]{1,0:T(8,128)(2,1)S(1)}, u32[]{:S(2)}, u32[]{:S(2)}) collective-permute-start(bf16[256,512]{1,0:T(8,128)(2,1)S(1)} %collective-permute-done.15.refs_3_), channel_id=1, source_target_pairs={{0,16},{16,0},{32,48},{48,32},{64,80},{80,64},{96,112},{112,96},{1... | collective-permute-start | bytes 786440 | tf_op jit(solution)/shard_map/ppermute | solution.py:314
  105.5 1.5 collective-permute-start.22
  107.1 2.3 %copy-start = (bf16[8,12,128,128]{3,2,1,0:T(8,128)(2,1)S(1)}, bf16[8,12,128,128]{3,2,1,0:T(8,128)(2,1)}, u32[]{:S(2)}) copy-start(bf16[8,12,128,128]{3,2,1,0:T(8,128)(2,1)} %caps.1.cap_ref) | copy-start | bytes 9437188

commit v21 on v20

--- a/solution.py
+++ b/solution.py
@@ -360,17 +360,15 @@
     far_a = forward(up_a, down_a)
     b = project(later)
     up_b, down_b = ring(b)
+    done = spread(both([(a, 0, cut), (b, cut, local_blocks)]), 0, near, (None, None))
     hidden = jnp.concatenate([a, b])
     tiles = target_tiles(hidden, tgt_vectors, local_blocks, relation_weight.shape[0])
-    later_a, later_b, tiles = lax.optimization_barrier((a, b, tiles))
-    front, back = (0, cut), (cut, local_blocks)
-    own = [[(a, *front), (b, *back)], [(send(later_a, 0, 1), *front), (send(later_b, 0, 1), *back)]]
-    done = spread(own, 0, near, (None, None))
     swap_up, swap_down = send(up_a, 0, 1), send(down_a, 0, 1)
     up_b, down_b, far_a, tiles, done, swap_up, swap_down = lax.optimization_barrier(
         (up_b, down_b, far_a, tiles, done, swap_up, swap_down)
     )
     far_b = forward(up_b, down_b)
+    front, back = (0, cut), (cut, local_blocks)
     rows = [[(up_a, *front), (up_b, *back)], [(swap_up, *front), (send(up_b, 0, 1), *back)]]
     rows += [[(down_a, *front), (down_b, *back)], [(swap_down, *front), (send(down_b, 0, 1), *back)]]
     done = spread(rows, 2, (lists[0], lists[2]), done)

time: 157 us -> 153 us (0.975)
  waiting for transfers between devices: 37.4 us -> 33 us
    ppermute x23, waiting for transfers between devices: 25.1 us -> 20.6 us  [send(): return lax.ppermute(x, 'graph', pairs)]
  transfers between devices with their start and end apart: 25 -> 25, of which waited for: 8 -> 8; matrix products, arithmetic and copies ran while one was open for 3% -> 4% of each run, Pallas kernels for 11% -> 14%
where the time goes in v21:
time: 153 us
  Pallas kernels  73.9 us (48%)
  starting transfers between devices  37.5 us (25%)
  waiting for transfers between devices  33 us (22%)
  matrix products  5.67 us (4%)
    pallas_call x1, Pallas kernels, attend(): pl.pallas_call(attend_kernel, in_specs=[scalars] * 2 + [inside] * 5, out_...  47.1 us
    ppermute x23, starting transfers between devices, send(): return lax.ppermute(x, 'graph', pairs)  26.3 us
    ppermute x23, waiting for transfers between devices, send(): return lax.ppermute(x, 'graph', pairs)  20.6 us
    all_to_all x1, waiting for transfers between devices, shards(): lax.all_to_all(first, 'feat', 0, 0, tiled=True)  12.3 us
    pallas_call x3, Pallas kernels, transform(): pl.pallas_call(functools.partial(transform_kernel, bounds, first), in_spe...  8.87 us
    pallas_call x2, Pallas kernels, arrange(): pl.pallas_call(functools.partial(arrange_kernel, low, high), grid_spec=pl...  7.26 us
    pallas_call x1, Pallas kernels, caps(): pl.pallas_call(cap_kernel, grid=shape[:1], in_specs=[spec], out_specs=spe...  6.92 us
    all_to_all x1, starting transfers between devices, shards(): lax.all_to_all(first, 'feat', 0, 0, tiled=True)  6.88 us
  transfers between devices with their start and end apart: 25, of which 8 were waited for; matrix products, arithmetic and copies ran while one was open for 4% of the time, Pallas kernels for 14%

profile of v21, /device:TPU:1, one launch (start us, length us, event | category | flops | bytes accessed | tf_op | source)
XLA Modules:
  0.0 152.6 jit_solution(14468145862558634988)
XLA Ops:
  0.0 3.7 %arrange.2 = bf16[16,64,768]{2,1,0:T(8,128)(2,1)} custom-call(s32[1]{0:T(128)} %bitcast.core_ref, bf16[64,16384]{1,0:T(8,128)(2,1)} %bitcast.31, bf16[64,512]{1,0:T(8,128)(2,1)} %w_ref.3), custom_call_target="tpu_custom_call" | custom-call | tf_op jit(solution)/shard_map/arrange/pallas_call | solution.py:31
  3.7 1.5 collective-permute-start
  5.2 6.9 %all-to-all-start = ((bf16[16,64,768]{2,1,0:T(8,128)(2,1)}), bf16[16,64,768]{2,1,0:T(8,128)(2,1)}, u32[]{:S(2)}, u32[]{:S(2)}) async-start(bf16[16,64,768]{2,1,0:T(8,128)(2,1)} %arrange.2), calls=%async_computation | async-start | bytes 3145728 | tf_op jit(solution)/shard_map/all_to_all | solution.py:321
  12.1 0.0 copy-start.4
  12.1 0.9 fusion
  13.2 3.6 %arrange.3 = bf16[16,64,512]{2,1,0:T(8,128)(2,1)} custom-call(s32[1]{0:T(128)} %bitcast.core_ref, bf16[64,16384]{1,0:T(8,128)(2,1)} %bitcast.32, bf16[64,512]{1,0:T(8,128)(2,1)} %w_ref.3), custom_call_target="tpu_custom_call" | custom-call | tf_op jit(solution)/shard_map/arrange/pallas_call | solution.py:31
  16.8 0.1 copy.15
  16.9 0.0 copy-start.6
  16.9 6.9 %caps.1.cap_ref = bf16[8,12,128,128]{3,2,1,0:T(8,128)(2,1)} custom-call(s32[8,12,128,128]{3,2,1,0:T(8,128)} %mask_ref.1), custom_call_target="tpu_custom_call" | custom-call | tf_op jit(solution)/shard_map/caps/pallas_call | solution.py:117
  23.9 0.1 pad.19.clone
  23.9 0.1 select_multiply_fusion
  24.1 0.1 fusion.6
  24.3 0.1 maximum_maximum_fusion.refs_6_.refs_11_.refs_10_
  24.4 0.0 collective-permute-done
  24.4 0.3 fusion.10
  24.7 12.3 %all-to-all-done = bf16[16,64,768]{2,1,0:T(8,128)(2,1)} async-done(((bf16[16,64,768]{2,1,0:T(8,128)(2,1)}), bf16[16,64,768]{2,1,0:T(8,128)(2,1)}, u32[]{:S(2)}, u32[]{:S(2)}) %all-to-all-start) | async-done | bytes 1572896 | tf_op jit(solution)/shard_map/all_to_all | solution.py:321
  37.0 1.1 slice.19
  38.1 1.4 collective-permute-start.1
  39.5 4.3 %all-to-all-start.1 = ((bf16[16,64,512]{2,1,0:T(8,128)(2,1)}), bf16[16,64,512]{2,1,0:T(8,128)(2,1)}, u32[]{:S(2)}, u32[]{:S(2)}) async-start(bf16[16,64,512]{2,1,0:T(8,128)(2,1)} %arrange.3), calls=%async_computation.1 | async-start | bytes 2097152 | tf_op jit(solution)/shard_map/all_to_all | solution.py:334
  43.8 2.2 %convolution_convert_fusion.1.refs_1_ = bf16[512,512]{1,0:T(8,128)(2,1)S(1)} fusion(bf16[1024,768]{1,0:T(8,128)(2,1)} %bitcast.2, bf16[1024,256]{1,0:T(8,128)(2,1)S(1)} %collective-permute-done.1, bf16[1024,256]{1,0:T(8,128)(2,1)S(1)} %slice.19, pred[]{:T(512)S(6)} %eq.30), kind=kOutput, calls=%fused_computation.1 | convolution fusion | flops 541851648 | bytes 2621441 | tf_op jit(solution)/shard_map/dot_general | solution.py:341
  46.0 1.7 %collective-permute-start.2 = (bf16[512,512]{1,0:T(8,128)(2,1)S(1)}, bf16[512,512]{1,0:T(8,128)(2,1)S(1)}, u32[]{:S(2)}, u32[]{:S(2)}) collective-permute-start(bf16[512,512]{1,0:T(8,128)(2,1)S(1)} %convolution_convert_fusion.1.refs_1_), channel_id=1, source_target_pairs={{0,32},{16,48},{32,64},{48,80},{64,96},{80,112},{96,0},{112,16},{1... | collective-permute-start | bytes 1572872 | tf_op jit(solution)/shard_map/ppermute | solution.py:314
  47.7 2.2 %collective-permute-start.3 = (bf16[512,512]{1,0:T(8,128)(2,1)S(1)}, bf16[512,512]{1,0:T(8,128)(2,1)S(1)}, u32[]{:S(2)}, u32[]{:S(2)}) collective-permute-start(bf16[512,512]{1,0:T(8,128)(2,1)S(1)} %convolution_convert_fusion.1.refs_1_), channel_id=1, source_target_pairs={{0,96},{16,112},{32,0},{48,16},{64,32},{80,48},{96,64},{112,80},{1... | collective-permute-start | bytes 1572872 | tf_op jit(solution)/shard_map/ppermute | solution.py:314
  49.9 0.0 collective-permute-start.4
  49.9 2.6 %collective-permute-start.5 = (s32[2,4]{1,0:T(2,128)S(1)}, s32[2,4]{1,0:T(2,128)S(1)}, u32[]{:S(2)}, u32[]{:S(2)}) collective-permute-start(s32[2,4]{1,0:T(2,128)S(1)} %get-tuple-element.50), channel_id=1, source_target_pairs={{0,64},{16,80},{32,96},{48,112},{64,0},{80,16},{96,32},{112,48},{1... | collective-permute-start | bytes 104 | tf_op jit(solution)/shard_map/ppermute | solution.py:314
  52.5 0.7 collective-permute-start.6
  53.2 9.0 %collective-permute-done.4.refs_0_ = s32[2,4]{1,0:T(2,128)S(1)} collective-permute-done((s32[2,4]{1,0:T(2,128)S(1)}, s32[2,4]{1,0:T(2,128)S(1)}, u32[]{:S(2)}, u32[]{:S(2)}) %collective-permute-start.4) | collective-permute-done | bytes 64 | tf_op jit(solution)/shard_map/ppermute | solution.py:314
  62.3 0.5 collective-permute-start.11
  62.8 0.5 collective-permute-done.5.refs_0_
  63.3 0.0 collective-permute-done.3.refs_6_
  63.3 2.6 %convolution_convert_fusion.refs_2_ = bf16[512,512]{1,0:T(8,128)(2,1)S(1)} fusion(bf16[1024,512]{1,0:T(8,128)(2,1)} %bitcast.11, bf16[1024,256]{1,0:T(8,128)(2,1)} %copy-done.8, bf16[1024,256]{1,0:T(8,128)(2,1)} %copy-done.3, pred[]{:T(512)S(6)} %eq.30), kind=kOutput, calls=%fused_computation | convolution fusion | flops 541851648 | bytes 2621441 | tf_op jit(solution)/shard_map/dot_general | solution.py:341
  65.9 0.8 collective-permute-start.12
  66.7 3.6 %collective-permute-start.10 = (bf16[256,512]{1,0:T(8,128)(2,1)S(1)}, bf16[256,512]{1,0:T(8,128)(2,1)S(1)}, u32[]{:S(2)}, u32[]{:S(2)}) collective-permute-start(bf16[256,512]{1,0:T(8,128)(2,1)S(1)} %slice.21), channel_id=1, source_target_pairs={{0,96},{16,112},{32,0},{48,16},{64,32},{80,48},{96,64},{112,80},{1... | collective-permute-start | bytes 786440 | tf_op jit(solution)/shard_map/ppermute | solution.py:314
  70.2 2.7 %collective-permute-start.8 = (bf16[512,512]{1,0:T(8,128)(2,1)S(1)}, bf16[512,512]{1,0:T(8,128)(2,1)S(1)}, u32[]{:S(2)}, u32[]{:S(2)}) collective-permute-start(bf16[512,512]{1,0:T(8,128)(2,1)S(1)} %convolution_convert_fusion.refs_2_), channel_id=1, source_target_pairs={{0,96},{16,112},{32,0},{48,16},{64,32},{80,48},{96,64},{112,80},{1... | collective-permute-start | bytes 1572872 | tf_op jit(solution)/shard_map/ppermute | solution.py:314
  72.9 0.0 collective-permute-done.11.refs_3_
  72.9 0.9 collective-permute-start.13
  73.8 2.2 %collective-permute-done.10.refs_2_ = bf16[256,512]{1,0:T(8,128)(2,1)S(1)} collective-permute-done((bf16[256,512]{1,0:T(8,128)(2,1)S(1)}, bf16[256,512]{1,0:T(8,128)(2,1)S(1)}, u32[]{:S(2)}, u32[]{:S(2)}) %collective-permute-start.10) | collective-permute-done | bytes 262176 | tf_op jit(solution)/shard_map/ppermute | solution.py:314
  76.0 1.2 collective-permute-start.14
  77.2 0.2 collective-permute-start.9
  77.4 0.1 pad_maximum_fusion
  77.5 3.7 %targets.1.tile_ref = f32[8,2,4,128,128]{4,3,2,1,0:T(8,128)S(1)} custom-call(bf16[8,128,512]{2,1,0:T(8,128)(2,1)S(1)} %bitcast.29, bf16[3,512,128]{2,1,0:T(8,128)(2,1)S(1)} %pad_maximum_fusion.1.tgt_ref), custom_call_target="tpu_custom_call" | custom-call | tf_op jit(solution)/shard_map/targets/pallas_call | solution.py:147
  81.2 2.7 %transform.3 = (bf16[32,2,128,512]{3,2,1,0:T(8,128)(2,1)S(1)}, f32[32,8,128]{2,1,0:T(8,128)S(1)}) custom-call(s32[2,4]{1,0:T(2,128)S(1)} %get-tuple-element.57.refs_0_, bf16[512,512]{1,0:T(8,128)(2,1)S(1)} %convolution_convert_fusion.1.refs_1_, bf16[512,512]{1,0:T(8,128)(2,1)S(1)} %convolution_convert_fusion.refs_2_, ...), custom_call_target="tpu_custom_call" | custom-call | tf_op jit(solution)/shard_map/transform/pallas_call | solution.py:95
  83.9 6.4 %collective-permute-done.9.refs_1_ = bf16[256,512]{1,0:T(8,128)(2,1)S(1)} collective-permute-done((bf16[256,512]{1,0:T(8,128)(2,1)S(1)}, bf16[256,512]{1,0:T(8,128)(2,1)S(1)}, u32[]{:S(2)}, u32[]{:S(2)}) %collective-permute-start.9) | collective-permute-done | bytes 262176 | tf_op jit(solution)/shard_map/ppermute | solution.py:314
  90.3 0.0 collective-permute-done.8.refs_7_
  90.3 0.0 collective-permute-done.13.refs_4_
  90.3 0.0 collective-permute-done.14.refs_8_
  90.3 1.2 collective-permute-start.17
  91.5 0.1 collective-permute-start.18
  91.6 0.1 collective-permute-start.15
  91.7 2.7 %collective-permute-start.16 = (bf16[256,512]{1,0:T(8,128)(2,1)S(1)}, bf16[256,512]{1,0:T(8,128)(2,1)S(1)}, u32[]{:S(2)}, u32[]{:S(2)}) collective-permute-start(bf16[256,512]{1,0:T(8,128)(2,1)S(1)} %slice.23), channel_id=1, source_target_pairs={{0,96},{16,112},{32,0},{48,16},{64,32},{80,48},{96,64},{112,80},{1... | collective-permute-start | bytes 786440 | tf_op jit(solution)/shard_map/ppermute | solution.py:314
  94.4 1.0 collective-permute-start.19
  95.4 0.0 collective-permute-done.17.refs_5_
  95.4 0.0 collective-permute-start.20
  95.4 3.9 %transform.4 = (bf16[32,2,128,512]{3,2,1,0:T(8,128)(2,1)S(1)}, f32[32,8,128]{2,1,0:T(8,128)S(1)}) custom-call(s32[2,4]{1,0:T(2,128)S(1)} %collective-permute-done.4.refs_0_, s32[2,4]{1,0:T(2,128)S(1)} %collective-permute-done.6.refs_1_, bf16[512,512]{1,0:T(8,128)(2,1)S(1)} %collective-permute-done.2.refs_2_, ...), custom_call_target="tpu_custom_call", output_to_operand_aliasing={{0}: (12, {}), {1}: (13, {})} | custom-call | tf_op jit(solution)/shard_map/transform/pallas_call | solution.py:95
  99.3 1.1 collective-permute-done.15.refs_3_
  100.4 0.0 collective-permute-done.16.refs_4_
  100.4 1.3 collective-permute-start.21
  101.7 0.1 collective-permute-start.22
  101.7 0.0 collective-permute-done.19.refs_5_
  101.7 0.0 collective-permute-done.20.refs_6_
  101.7 1.1 collective-permute-done.21.refs_7_
  102.8 0.4 collective-permute-done.22.refs_8_
  103.2 2.3 %transform.5 = (bf16[32,2,128,512]{3,2,1,0:T(8,128)(2,1)S(1)}, f32[32,8,128]{2,1,0:T(8,128)S(1)}) custom-call(s32[2,4]{1,0:T(2,128)S(1)} %collective-permute-done.5.refs_0_, bf16[256,512]{1,0:T(8,128)(2,1)S(1)} %collective-permute-done.9.refs_1_, ...), custom_call_target="tpu_custom_call", output_to_operand_aliasing={{0}: (11, {}), {1}: (12, {})} | custom-call | tf_op jit(solution)/shard_map/transform/pallas_call | solution.py:95
  105.5 0.0 copy-done
  105.5 47.1 %attend.1 = bf16[8,128,512]{2,1,0:T(8,128)(2,1)} custom-call(s32[8,12]{1,0:T(8,128)S(1)} %copy-done.2, s32[8,12]{1,0:T(8,128)S(1)} %fusion.23.slot_ref, bf16[8,128,512]{2,1,0:T(8,128)(2,1)S(1)} %bitcast.30, bf16[8,12,128,128]{3,2,1,0:T(8,128)(2,1)S(1)} %copy-done, f32[8,2,4,128,128]{4,3,2,1,0:T(8,128)S(1)} %targets.1.tile_ref, ...), custom_call_target="tpu_custom_call" | custom-call | tf_op jit(solution)/shard_map/attend/pallas_call | solution.py:254
  (38 shorter events, 0.3 us)
Async XLA Ops:
  0.0 3.7 %copy-start.7 = (s32[1,8,4]{1,2,0:T(4,128)S(1)}, s32[1,8,4]{1,2,0:T(4,128)}, u32[]{:S(2)}) copy-start(s32[1,8,4]{1,2,0:T(4,128)} %param.16) | copy-start | bytes 388
  3.7 8.4 %copy-start.5 = (f32[2,512]{1,0:T(2,128)S(1)}, f32[2,512]{1,0:T(2,128)}, u32[]{:S(2)}) copy-start(f32[2,512]{1,0:T(2,128)} %param.12) | copy-start | bytes 12292
  3.7 8.4 %copy-start.1 = (bf16[2,512,512]{2,1,0:T(8,128)(2,1)S(1)}, bf16[2,512,512]{2,1,0:T(8,128)(2,1)}, u32[]{:S(2)}) copy-start(bf16[2,512,512]{2,1,0:T(8,128)(2,1)} %refs_9_.1) | copy-start | bytes 3145732
  3.7 20.7 %collective-permute-start = (s32[8,4]{0,1:T(4,128)S(1)}, s32[8,4]{0,1:T(4,128)S(1)}, u32[]{:S(2)}, u32[]{:S(2)}) collective-permute-start(s32[8,4]{0,1:T(4,128)S(1)} %bitcast.35), channel_id=1, source_target_pairs={{0,16},{16,0},{32,48},{48,32},{64,80},{80,64},{96,112},{112,96},{1... | collective-permute-start | bytes 392 | tf_op jit(solution)/shard_map/ppermute | solution.py:314
  5.2 31.8 %all-to-all-start = ((bf16[16,64,768]{2,1,0:T(8,128)(2,1)}), bf16[16,64,768]{2,1,0:T(8,128)(2,1)}, u32[]{:S(2)}, u32[]{:S(2)}) async-start(bf16[16,64,768]{2,1,0:T(8,128)(2,1)} %arrange.2), calls=%async_computation | async-start | bytes 3145728 | tf_op jit(solution)/shard_map/all_to_all | solution.py:321
  12.1 4.6 %copy-start.4 = (f32[2,512]{1,0:T(2,128)S(1)}, f32[2,512]{1,0:T(2,128)}, u32[]{:S(2)}) copy-start(f32[2,512]{1,0:T(2,128)} %param.13) | copy-start | bytes 12292
  16.9 7.3 %copy-start.6 = (s32[8,12]{1,0:T(8,128)S(1)}, s32[8,12]{1,0:T(8,128)}, u32[]{:S(2)}) copy-start(s32[8,12]{1,0:T(8,128)} %param.17) | copy-start | bytes 1156
  38.1 5.7 %copy-start.3 = (bf16[1024,256]{1,0:T(8,128)(2,1)}, bf16[1024,256]{1,0:T(8,128)(2,1)S(1)}, u32[]{:S(2)}) copy-start(bf16[1024,256]{1,0:T(8,128)(2,1)S(1)} %slice.19) | copy-start | bytes 1572868
  38.1 5.7 %collective-permute-start.1 = (bf16[1024,256]{1,0:T(8,128)(2,1)S(1)}, bf16[1024,256]{1,0:T(8,128)(2,1)S(1)}, u32[]{:S(2)}, u32[]{:S(2)}) collective-permute-start(bf16[1024,256]{1,0:T(8,128)(2,1)S(1)} %slice.19), channel_id=1, source_target_pairs={{0,16},{16,0},{32,48},{48,32},{64,80},{80,64},{96,112},{112,96},{1... | collective-permute-start | bytes 1572872 | tf_op jit(solution)/shard_map/ppermute | solution.py:314
  39.5 23.8 %all-to-all-start.1 = ((bf16[16,64,512]{2,1,0:T(8,128)(2,1)}), bf16[16,64,512]{2,1,0:T(8,128)(2,1)}, u32[]{:S(2)}, u32[]{:S(2)}) async-start(bf16[16,64,512]{2,1,0:T(8,128)(2,1)} %arrange.3), calls=%async_computation.1 | async-start | bytes 2097152 | tf_op jit(solution)/shard_map/all_to_all | solution.py:334
  43.8 2.2 %copy-start.8 = (bf16[1024,256]{1,0:T(8,128)(2,1)}, bf16[1024,256]{1,0:T(8,128)(2,1)S(1)}, u32[]{:S(2)}) copy-start(bf16[1024,256]{1,0:T(8,128)(2,1)S(1)} %collective-permute-done.1) | copy-start | bytes 1572868
  46.0 17.2 %collective-permute-start.2 = (bf16[512,512]{1,0:T(8,128)(2,1)S(1)}, bf16[512,512]{1,0:T(8,128)(2,1)S(1)}, u32[]{:S(2)}, u32[]{:S(2)}) collective-permute-start(bf16[512,512]{1,0:T(8,128)(2,1)S(1)} %convolution_convert_fusion.1.refs_1_), channel_id=1, source_target_pairs={{0,32},{16,48},{32,64},{48,80},{64,96},{80,112},{96,0},{112,16},{1... | collective-permute-start | bytes 1572872 | tf_op jit(solution)/shard_map/ppermute | solution.py:314
  47.7 15.5 %collective-permute-start.3 = (bf16[512,512]{1,0:T(8,128)(2,1)S(1)}, bf16[512,512]{1,0:T(8,128)(2,1)S(1)}, u32[]{:S(2)}, u32[]{:S(2)}) collective-permute-start(bf16[512,512]{1,0:T(8,128)(2,1)S(1)} %convolution_convert_fusion.1.refs_1_), channel_id=1, source_target_pairs={{0,96},{16,112},{32,0},{48,16},{64,32},{80,48},{96,64},{112,80},{1... | collective-permute-start | bytes 1572872 | tf_op jit(solution)/shard_map/ppermute | solution.py:314
  49.9 12.3 %collective-permute-start.4 = (s32[2,4]{1,0:T(2,128)S(1)}, s32[2,4]{1,0:T(2,128)S(1)}, u32[]{:S(2)}, u32[]{:S(2)}) collective-permute-start(s32[2,4]{1,0:T(2,128)S(1)} %get-tuple-element.49), channel_id=1, source_target_pairs={{0,32},{16,48},{32,64},{48,80},{64,96},{80,112},{96,0},{112,16},{1... | collective-permute-start | bytes 104 | tf_op jit(solution)/shard_map/ppermute | solution.py:314
  49.9 13.3 %collective-permute-start.5 = (s32[2,4]{1,0:T(2,128)S(1)}, s32[2,4]{1,0:T(2,128)S(1)}, u32[]{:S(2)}, u32[]{:S(2)}) collective-permute-start(s32[2,4]{1,0:T(2,128)S(1)} %get-tuple-element.50), channel_id=1, source_target_pairs={{0,64},{16,80},{32,96},{48,112},{64,0},{80,16},{96,32},{112,48},{1... | collective-permute-start | bytes 104 | tf_op jit(solution)/shard_map/ppermute | solution.py:314
  52.5 10.7 %collective-permute-start.6 = (s32[2,4]{1,0:T(2,128)S(1)}, s32[2,4]{1,0:T(2,128)S(1)}, u32[]{:S(2)}, u32[]{:S(2)}) collective-permute-start(s32[2,4]{1,0:T(2,128)S(1)} %get-tuple-element.51), channel_id=1, source_target_pairs={{0,96},{16,112},{32,0},{48,16},{64,32},{80,48},{96,64},{112,80},{1... | collective-permute-start | bytes 104 | tf_op jit(solution)/shard_map/ppermute | solution.py:314
  62.3 10.7 %collective-permute-start.11 = (bf16[512,512]{1,0:T(8,128)(2,1)S(1)}, bf16[512,512]{1,0:T(8,128)(2,1)}, u32[]{:S(2)}, u32[]{:S(2)}) collective-permute-start(bf16[512,512]{1,0:T(8,128)(2,1)S(1)} %convolution_convert_fusion.1.refs_1_), channel_id=1, source_target_pairs={{0,16},{16,0},{32,48},{48,32},{64,80},{80,64},{96,112},{112,96},{1... | collective-permute-start | bytes 1572872 | tf_op jit(solution)/shard_map/ppermute | solution.py:314
  65.9 11.3 %collective-permute-start.12 = (bf16[512,512]{1,0:T(8,128)(2,1)S(1)}, bf16[512,512]{1,0:T(8,128)(2,1)S(1)}, u32[]{:S(2)}, u32[]{:S(2)}) collective-permute-start(bf16[512,512]{1,0:T(8,128)(2,1)S(1)} %convolution_convert_fusion.refs_2_), channel_id=1, source_target_pairs={{0,16},{16,0},{32,48},{48,32},{64,80},{80,64},{96,112},{112,96},{1... | collective-permute-start | bytes 1572872 | tf_op jit(solution)/shard_map/ppermute | solution.py:314
  66.7 9.3 %collective-permute-start.10 = (bf16[256,512]{1,0:T(8,128)(2,1)S(1)}, bf16[256,512]{1,0:T(8,128)(2,1)S(1)}, u32[]{:S(2)}, u32[]{:S(2)}) collective-permute-start(bf16[256,512]{1,0:T(8,128)(2,1)S(1)} %slice.21), channel_id=1, source_target_pairs={{0,96},{16,112},{32,0},{48,16},{64,32},{80,48},{96,64},{112,80},{1... | collective-permute-start | bytes 786440 | tf_op jit(solution)/shard_map/ppermute | solution.py:314
  70.2 20.1 %collective-permute-start.7 = (bf16[512,512]{1,0:T(8,128)(2,1)S(1)}, bf16[512,512]{1,0:T(8,128)(2,1)S(1)}, u32[]{:S(2)}, u32[]{:S(2)}) collective-permute-start(bf16[512,512]{1,0:T(8,128)(2,1)S(1)} %convolution_convert_fusion.refs_2_), channel_id=1, source_target_pairs={{0,32},{16,48},{32,64},{48,80},{64,96},{80,112},{96,0},{112,16},{1... | collective-permute-start | bytes 1572872 | tf_op jit(solution)/shard_map/ppermute | solution.py:314
  70.2 20.1 %collective-permute-start.8 = (bf16[512,512]{1,0:T(8,128)(2,1)S(1)}, bf16[512,512]{1,0:T(8,128)(2,1)S(1)}, u32[]{:S(2)}, u32[]{:S(2)}) collective-permute-start(bf16[512,512]{1,0:T(8,128)(2,1)S(1)} %convolution_convert_fusion.refs_2_), channel_id=1, source_target_pairs={{0,96},{16,112},{32,0},{48,16},{64,32},{80,48},{96,64},{112,80},{1... | collective-permute-start | bytes 1572872 | tf_op jit(solution)/shard_map/ppermute | solution.py:314
  72.9 17.4 %collective-permute-start.13 = (bf16[512,512]{1,0:T(8,128)(2,1)S(1)}, bf16[512,512]{1,0:T(8,128)(2,1)S(1)}, u32[]{:S(2)}, u32[]{:S(2)}) collective-permute-start(bf16[512,512]{1,0:T(8,128)(2,1)S(1)} %collective-permute-done.2.refs_2_), channel_id=1, source_target_pairs={{0,16},{16,0},{32,48},{48,32},{64,80},{80,64},{96,112},{112,96},{1... | collective-permute-start | bytes 1572872 | tf_op jit(solution)/shard_map/ppermute | solution.py:314
  76.0 14.3 %collective-permute-start.14 = (bf16[512,512]{1,0:T(8,128)(2,1)S(1)}, bf16[512,512]{1,0:T(8,128)(2,1)S(1)}, u32[]{:S(2)}, u32[]{:S(2)}) collective-permute-start(bf16[512,512]{1,0:T(8,128)(2,1)S(1)} %collective-permute-done.3.refs_6_), channel_id=1, source_target_pairs={{0,16},{16,0},{32,48},{48,32},{64,80},{80,64},{96,112},{112,96},{1... | collective-permute-start | bytes 1572872 | tf_op jit(solution)/shard_map/ppermute | solution.py:314
  77.2 13.1 %collective-permute-start.9 = (bf16[256,512]{1,0:T(8,128)(2,1)S(1)}, bf16[256,512]{1,0:T(8,128)(2,1)S(1)}, u32[]{:S(2)}, u32[]{:S(2)}) collective-permute-start(bf16[256,512]{1,0:T(8,128)(2,1)S(1)} %slice.20), channel_id=1, source_target_pairs={{0,32},{16,48},{32,64},{48,80},{64,96},{80,112},{96,0},{112,16},{1... | collective-permute-start | bytes 786440 | tf_op jit(solution)/shard_map/ppermute | solution.py:314
  90.3 5.1 %collective-permute-start.17 = (bf16[512,512]{1,0:T(8,128)(2,1)S(1)}, bf16[512,512]{1,0:T(8,128)(2,1)S(1)}, u32[]{:S(2)}, u32[]{:S(2)}) collective-permute-start(bf16[512,512]{1,0:T(8,128)(2,1)S(1)} %collective-permute-done.7.refs_3_), channel_id=1, source_target_pairs={{0,16},{16,0},{32,48},{48,32},{64,80},{80,64},{96,112},{112,96},{1... | collective-permute-start | bytes 1572872 | tf_op jit(solution)/shard_map/ppermute | solution.py:314
  91.5 3.9 %collective-permute-start.18 = (bf16[512,512]{1,0:T(8,128)(2,1)S(1)}, bf16[512,512]{1,0:T(8,128)(2,1)S(1)}, u32[]{:S(2)}, u32[]{:S(2)}) collective-permute-start(bf16[512,512]{1,0:T(8,128)(2,1)S(1)} %collective-permute-done.8.refs_7_), channel_id=1, source_target_pairs={{0,16},{16,0},{32,48},{48,32},{64,80},{80,64},{96,112},{112,96},{1... | collective-permute-start | bytes 1572872 | tf_op jit(solution)/shard_map/ppermute | solution.py:314
  91.6 8.8 %collective-permute-start.15 = (bf16[256,512]{1,0:T(8,128)(2,1)S(1)}, bf16[256,512]{1,0:T(8,128)(2,1)S(1)}, u32[]{:S(2)}, u32[]{:S(2)}) collective-permute-start(bf16[256,512]{1,0:T(8,128)(2,1)S(1)} %slice.22), channel_id=1, source_target_pairs={{0,32},{16,48},{32,64},{48,80},{64,96},{80,112},{96,0},{112,16},{1... | collective-permute-start | bytes 786440 | tf_op jit(solution)/shard_map/ppermute | solution.py:314
  91.7 8.7 %collective-permute-start.16 = (bf16[256,512]{1,0:T(8,128)(2,1)S(1)}, bf16[256,512]{1,0:T(8,128)(2,1)S(1)}, u32[]{:S(2)}, u32[]{:S(2)}) collective-permute-start(bf16[256,512]{1,0:T(8,128)(2,1)S(1)} %slice.23), channel_id=1, source_target_pairs={{0,96},{16,112},{32,0},{48,16},{64,32},{80,48},{96,64},{112,80},{1... | collective-permute-start | bytes 786440 | tf_op jit(solution)/shard_map/ppermute | solution.py:314
  94.4 7.3 %collective-permute-start.19 = (bf16[256,512]{1,0:T(8,128)(2,1)S(1)}, bf16[256,512]{1,0:T(8,128)(2,1)S(1)}, u32[]{:S(2)}, u32[]{:S(2)}) collective-permute-start(bf16[256,512]{1,0:T(8,128)(2,1)S(1)} %collective-permute-done.9.refs_1_), channel_id=1, source_target_pairs={{0,16},{16,0},{32,48},{48,32},{64,80},{80,64},{96,112},{112,96},{1... | collective-permute-start | bytes 786440 | tf_op jit(solution)/shard_map/ppermute | solution.py:314
  95.4 6.4 %collective-permute-start.20 = (bf16[256,512]{1,0:T(8,128)(2,1)S(1)}, bf16[256,512]{1,0:T(8,128)(2,1)S(1)}, u32[]{:S(2)}, u32[]{:S(2)}) collective-permute-start(bf16[256,512]{1,0:T(8,128)(2,1)S(1)} %collective-permute-done.10.refs_2_), channel_id=1, source_target_pairs={{0,16},{16,0},{32,48},{48,32},{64,80},{80,64},{96,112},{112,96},{1... | collective-permute-start | bytes 786440 | tf_op jit(solution)/shard_map/ppermute | solution.py:314
  100.4 5.1 %copy-start.2 = (s32[8,12]{1,0:T(8,128)S(1)}, s32[8,12]{1,0:T(8,128)}, u32[]{:S(2)}) copy-start(s32[8,12]{1,0:T(8,128)} %rel_ref.1) | copy-start | bytes 1156
  100.4 2.4 %collective-permute-start.21 = (bf16[256,512]{1,0:T(8,128)(2,1)S(1)}, bf16[256,512]{1,0:T(8,128)(2,1)S(1)}, u32[]{:S(2)}, u32[]{:S(2)}) collective-permute-start(bf16[256,512]{1,0:T(8,128)(2,1)S(1)} %collective-permute-done.15.refs_3_), channel_id=1, source_target_pairs={{0,16},{16,0},{32,48},{48,32},{64,80},{80,64},{96,112},{112,96},{1... | collective-permute-start | bytes 786440 | tf_op jit(solution)/shard_map/ppermute | solution.py:314
  101.7 1.5 %collective-permute-start.22 = (bf16[256,512]{1,0:T(8,128)(2,1)S(1)}, bf16[256,512]{1,0:T(8,128)(2,1)S(1)}, u32[]{:S(2)}, u32[]{:S(2)}) collective-permute-start(bf16[256,512]{1,0:T(8,128)(2,1)S(1)} %collective-permute-done.16.refs_4_), channel_id=1, source_target_pairs={{0,16},{16,0},{32,48},{48,32},{64,80},{80,64},{96,112},{112,96},{1... | collective-permute-start | bytes 786440 | tf_op jit(solution)/shard_map/ppermute | solution.py:314
  103.2 2.3 %copy-start = (bf16[8,12,128,128]{3,2,1,0:T(8,128)(2,1)S(1)}, bf16[8,12,128,128]{3,2,1,0:T(8,128)(2,1)}, u32[]{:S(2)}) copy-start(bf16[8,12,128,128]{3,2,1,0:T(8,128)(2,1)} %caps.1.cap_ref) | copy-start | bytes 9437188

commit v22 on v19

--- a/solution.py
+++ b/solution.py
@@ -210,7 +210,7 @@
         return carry
 
     least_ref[...] = jnp.full(least_ref.shape, jnp.inf, F32)
-    lax.fori_loop(0, blocks, body, 0)
+    lax.fori_loop(0, blocks, body, 0, unroll=2)
 
     def redo(b, carry):
         _, _, spread, finish = parts(b)
@@ -246,27 +246,45 @@
         lax.fori_loop(0, blocks, redo, 0)
 
 
-def attend(hidden, cap, relation_ids, source_slots, values, scores, tiles):
+def finale_kernel(bounds, first, rel_ref, slot_ref, *refs):
+    moved = 1 + sum(len(p) for p in bounds) + 2
+    own_ref, cap_ref, tile_ref = refs[moved : moved + 3]
+    out_ref, val_ref, score_ref, hid_ref, *scratch = refs[moved + 5 :]
+    transform_kernel(bounds, first, *refs[:moved], val_ref, score_ref, hid_ref)
+    attend_kernel(rel_ref, slot_ref, own_ref, cap_ref, tile_ref, val_ref, score_ref, out_ref, *scratch)
+
+
+def finale(sources, first, index, relation_weight, src_vectors, hidden, cap, relation_ids, source_slots, values, scores, tiles):
+    bounds = tuple(tuple((low, high) for _, low, high in pieces) for pieces in sources)
+    arrays = [array for pieces in sources for array, _, _ in pieces]
     blocks, lists, rows, cols = cap.shape
     width = hidden.shape[1]
     relations = values.shape[1]
     scalars, inside = pl.BlockSpec(memory_space=pltpu.SMEM), pl.BlockSpec(memory_space=pltpu.VMEM)
+    at = 3 + len(arrays) + 2 + 3
     return pl.pallas_call(
-        attend_kernel,
-        in_specs=[scalars] * 2 + [inside] * 5,
-        out_specs=inside,
+        functools.partial(finale_kernel, bounds, first),
+        in_specs=[scalars] * 3 + [inside] * (len(arrays) + 7),
+        out_specs=[inside] * 3,
         scratch_shapes=[
+            pltpu.VMEM((len(bounds), index.shape[1] * rows, width), BF16),
             pltpu.VMEM((HEADS, relations, rows, cols), F32),
             pltpu.VMEM((HEADS, relations, rows, cols), F32),
             pltpu.VMEM((HEADS, rows, lists * cols), BF16),
             pltpu.VMEM((rows, cols), F32),
         ],
-        out_shape=jax.ShapeDtypeStruct((blocks, rows, width), BF16),
+        out_shape=[
+            jax.ShapeDtypeStruct((blocks, rows, width), BF16),
+            jax.ShapeDtypeStruct(values.shape, BF16),
+            jax.ShapeDtypeStruct(scores.shape, F32),
+        ],
+        input_output_aliases={at: 1, at + 1: 2},
         compiler_params=pltpu.CompilerParams(vmem_limit_bytes=24 * 1024 * 1024),
-        name="attend",
-    )(relation_ids, source_slots, hidden.reshape(blocks, rows, width), cap, tiles, values, scores).reshape(
-        blocks * rows, width
-    )
+        name="finale",
+    )(
+        relation_ids, source_slots, index, *arrays, relation_weight, src_vectors,
+        hidden.reshape(blocks, rows, width), cap, tiles, values, scores,
+    )[0].reshape(blocks * rows, width)
 
 
 def score_vectors(relation_weight, att_source, att_target):
@@ -374,8 +392,9 @@
     far_b, done = lax.optimization_barrier((far_b, done))
     quarter = cut // 2
     far = [(x, n * quarter, (n + 1) * quarter) for n, x in enumerate(far_a + far_b)]
-    values, scores = spread(both(far), 6, lists[1:2], done)
-    return attend(hidden, cap, relation_ids, slots, values, scores, tiles)
+    return finale(
+        both(far), 6, lists[1], relation_weight, src_vectors, hidden, cap, relation_ids, slots, *done, tiles
+    )
 
 
 def solution(mesh):

time: 151 us -> 150 us (level)
    pallas_call x3 -> x2, Pallas kernels: 8.87 us -> 6.59 us  [transform(): pl.pallas_call(functools.partial(transform_kernel, bounds, first), in_spe...]
  transfers between devices with their start and end apart: 25 -> 25, of which waited for: 7 -> 7; matrix products, arithmetic and copies ran while one was open for 4% -> 5% of each run, Pallas kernels for 14% -> 14%
where the time goes in v22:
time: 150 us; the launch traced here: 149 us
  Pallas kernels  73 us (49%)
  starting transfers between devices  34.8 us (23%)
  waiting for transfers between devices  33.2 us (22%)
  matrix products  5.64 us (4%)
    pallas_call x1, Pallas kernels, finale(): pl.pallas_call(functools.partial(finale_kernel, bounds, first), in_specs=...  48.5 us
    ppermute x23, starting transfers between devices, send(): return lax.ppermute(x, 'graph', pairs)  23.6 us
    ppermute x23, waiting for transfers between devices, send(): return lax.ppermute(x, 'graph', pairs)  20.9 us
    all_to_all x1, waiting for transfers between devices, shards(): lax.all_to_all(first, 'feat', 0, 0, tiled=True)  12.3 us
    pallas_call x2, Pallas kernels, arrange(): pl.pallas_call(functools.partial(arrange_kernel, low, high), grid_spec=pl...  7.26 us
    pallas_call x1, Pallas kernels, caps(): pl.pallas_call(cap_kernel, grid=shape[:1], in_specs=[spec], out_specs=spe...  6.92 us
    all_to_all x1, starting transfers between devices, shards(): lax.all_to_all(first, 'feat', 0, 0, tiled=True)  6.88 us
    pallas_call x2, Pallas kernels, transform(): pl.pallas_call(functools.partial(transform_kernel, bounds, first), in_spe...  6.59 us
  transfers between devices with their start and end apart: 25, of which 7 were waited for; matrix products, arithmetic and copies ran while one was open for 5% of the time, Pallas kernels for 14%

profile of v22, /device:TPU:1, one launch (start us, length us, event | category | flops | bytes accessed | tf_op | source)
XLA Modules:
  0.0 149.3 jit_solution(18254167063474965724)
XLA Ops:
  0.0 3.7 %arrange.2 = bf16[16,64,768]{2,1,0:T(8,128)(2,1)} custom-call(s32[1]{0:T(128)} %bitcast.core_ref, bf16[64,16384]{1,0:T(8,128)(2,1)} %bitcast.31, bf16[64,512]{1,0:T(8,128)(2,1)} %w_ref.3), custom_call_target="tpu_custom_call" | custom-call | tf_op jit(solution)/shard_map/arrange/pallas_call | solution.py:31
  3.7 1.5 %collective-permute-start = (s32[8,4]{0,1:T(4,128)S(1)}, s32[8,4]{0,1:T(4,128)S(1)}, u32[]{:S(2)}, u32[]{:S(2)}) collective-permute-start(s32[8,4]{0,1:T(4,128)S(1)} %bitcast.35), channel_id=1, source_target_pairs={{0,16},{16,0},{32,48},{48,32},{64,80},{80,64},{96,112},{112,96},{1... | collective-permute-start | bytes 392 | tf_op jit(solution)/shard_map/ppermute | solution.py:332
  5.2 6.9 %all-to-all-start = ((bf16[16,64,768]{2,1,0:T(8,128)(2,1)}), bf16[16,64,768]{2,1,0:T(8,128)(2,1)}, u32[]{:S(2)}, u32[]{:S(2)}) async-start(bf16[16,64,768]{2,1,0:T(8,128)(2,1)} %arrange.2), calls=%async_computation | async-start | bytes 3145728 | tf_op jit(solution)/shard_map/all_to_all | solution.py:339
  12.1 0.0 copy-start.4
  12.1 0.9 fusion
  13.2 3.6 %arrange.3 = bf16[16,64,512]{2,1,0:T(8,128)(2,1)} custom-call(s32[1]{0:T(128)} %bitcast.core_ref, bf16[64,16384]{1,0:T(8,128)(2,1)} %bitcast.32, bf16[64,512]{1,0:T(8,128)(2,1)} %w_ref.3), custom_call_target="tpu_custom_call" | custom-call | tf_op jit(solution)/shard_map/arrange/pallas_call | solution.py:31
  16.8 0.1 copy.15
  16.9 0.0 copy-start.6
  16.9 6.9 %caps.1.refs_12_ = bf16[8,12,128,128]{3,2,1,0:T(8,128)(2,1)} custom-call(s32[8,12,128,128]{3,2,1,0:T(8,128)} %mask_ref.1), custom_call_target="tpu_custom_call" | custom-call | tf_op jit(solution)/shard_map/caps/pallas_call | solution.py:117
  23.9 0.1 pad.19.clone
  23.9 0.1 select_multiply_fusion
  24.1 0.1 fusion.6
  24.3 0.1 maximum_maximum_fusion.refs_6_.refs_11_.refs_10_
  24.4 0.0 collective-permute-done
  24.4 0.3 fusion.10
  24.7 12.3 %all-to-all-done = bf16[16,64,768]{2,1,0:T(8,128)(2,1)} async-done(((bf16[16,64,768]{2,1,0:T(8,128)(2,1)}), bf16[16,64,768]{2,1,0:T(8,128)(2,1)}, u32[]{:S(2)}, u32[]{:S(2)}) %all-to-all-start) | async-done | bytes 1572896 | tf_op jit(solution)/shard_map/all_to_all | solution.py:339
  37.0 1.1 slice.19
  38.1 1.4 collective-permute-start.1
  39.5 4.3 %all-to-all-start.1 = ((bf16[16,64,512]{2,1,0:T(8,128)(2,1)}), bf16[16,64,512]{2,1,0:T(8,128)(2,1)}, u32[]{:S(2)}, u32[]{:S(2)}) async-start(bf16[16,64,512]{2,1,0:T(8,128)(2,1)} %arrange.3), calls=%async_computation.1 | async-start | bytes 2097152 | tf_op jit(solution)/shard_map/all_to_all | solution.py:352
  43.8 0.0 collective-permute-done.1
  43.8 2.2 %convolution_convert_fusion.1.refs_1_ = bf16[512,512]{1,0:T(8,128)(2,1)S(1)} fusion(bf16[1024,768]{1,0:T(8,128)(2,1)} %bitcast.2, bf16[1024,256]{1,0:T(8,128)(2,1)S(1)} %collective-permute-done.1, bf16[1024,256]{1,0:T(8,128)(2,1)S(1)} %slice.19, pred[]{:T(512)S(6)} %eq.30), kind=kOutput, calls=%fused_computation.1 | convolution fusion | flops 541851648 | bytes 2621441 | tf_op jit(solution)/shard_map/dot_general | solution.py:359
  46.0 1.7 %collective-permute-start.2 = (bf16[512,512]{1,0:T(8,128)(2,1)S(1)}, bf16[512,512]{1,0:T(8,128)(2,1)S(1)}, u32[]{:S(2)}, u32[]{:S(2)}) collective-permute-start(bf16[512,512]{1,0:T(8,128)(2,1)S(1)} %convolution_convert_fusion.1.refs_1_), channel_id=1, source_target_pairs={{0,32},{16,48},{32,64},{48,80},{64,96},{80,112},{96,0},{112,16},{1... | collective-permute-start | bytes 1572872 | tf_op jit(solution)/shard_map/ppermute | solution.py:332
  47.7 2.2 %collective-permute-start.3 = (bf16[512,512]{1,0:T(8,128)(2,1)S(1)}, bf16[512,512]{1,0:T(8,128)(2,1)S(1)}, u32[]{:S(2)}, u32[]{:S(2)}) collective-permute-start(bf16[512,512]{1,0:T(8,128)(2,1)S(1)} %convolution_convert_fusion.1.refs_1_), channel_id=1, source_target_pairs={{0,96},{16,112},{32,0},{48,16},{64,32},{80,48},{96,64},{112,80},{1... | collective-permute-start | bytes 1572872 | tf_op jit(solution)/shard_map/ppermute | solution.py:332
  49.9 0.0 collective-permute-start.4
  49.9 2.6 %collective-permute-start.5 = (s32[2,4]{1,0:T(2,128)S(1)}, s32[2,4]{1,0:T(2,128)S(1)}, u32[]{:S(2)}, u32[]{:S(2)}) collective-permute-start(s32[2,4]{1,0:T(2,128)S(1)} %get-tuple-element.47), channel_id=1, source_target_pairs={{0,64},{16,80},{32,96},{48,112},{64,0},{80,16},{96,32},{112,48},{1... | collective-permute-start | bytes 104 | tf_op jit(solution)/shard_map/ppermute | solution.py:332
  52.5 0.7 collective-permute-start.6
  53.2 9.0 %collective-permute-done.4.refs_0_ = s32[2,4]{1,0:T(2,128)S(1)} collective-permute-done((s32[2,4]{1,0:T(2,128)S(1)}, s32[2,4]{1,0:T(2,128)S(1)}, u32[]{:S(2)}, u32[]{:S(2)}) %collective-permute-start.4) | collective-permute-done | bytes 64 | tf_op jit(solution)/shard_map/ppermute | solution.py:332
  62.2 0.5 collective-permute-start.11
  62.8 0.5 collective-permute-done.5.refs_0_
  63.2 0.0 collective-permute-done.6.refs_1_
  63.2 0.0 all-to-all-done.1
  63.2 0.0 collective-permute-done.2.refs_2_
  63.2 0.0 collective-permute-done.3.refs_6_
  63.3 2.6 %convolution_convert_fusion.refs_2_ = bf16[512,512]{1,0:T(8,128)(2,1)S(1)} fusion(bf16[1024,512]{1,0:T(8,128)(2,1)} %bitcast.11, bf16[1024,256]{1,0:T(8,128)(2,1)} %copy-done.8, bf16[1024,256]{1,0:T(8,128)(2,1)} %copy-done.3, pred[]{:T(512)S(6)} %eq.30), kind=kOutput, calls=%fused_computation | convolution fusion | flops 541851648 | bytes 2621441 | tf_op jit(solution)/shard_map/dot_general | solution.py:359
  65.8 0.8 collective-permute-start.12
  66.6 1.4 collective-permute-start.7
  68.0 2.1 %collective-permute-start.8 = (bf16[512,512]{1,0:T(8,128)(2,1)S(1)}, bf16[512,512]{1,0:T(8,128)(2,1)S(1)}, u32[]{:S(2)}, u32[]{:S(2)}) collective-permute-start(bf16[512,512]{1,0:T(8,128)(2,1)S(1)} %convolution_convert_fusion.refs_2_), channel_id=1, source_target_pairs={{0,96},{16,112},{32,0},{48,16},{64,32},{80,48},{96,64},{112,80},{1... | collective-permute-start | bytes 1572872 | tf_op jit(solution)/shard_map/ppermute | solution.py:332
  70.2 1.5 %collective-permute-start.10 = (bf16[256,512]{1,0:T(8,128)(2,1)S(1)}, bf16[256,512]{1,0:T(8,128)(2,1)S(1)}, u32[]{:S(2)}, u32[]{:S(2)}) collective-permute-start(bf16[256,512]{1,0:T(8,128)(2,1)S(1)} %slice.21), channel_id=1, source_target_pairs={{0,96},{16,112},{32,0},{48,16},{64,32},{80,48},{96,64},{112,80},{1... | collective-permute-start | bytes 786440 | tf_op jit(solution)/shard_map/ppermute | solution.py:332
  71.7 0.0 collective-permute-done.11.refs_3_
  71.7 0.1 collective-permute-start.9
  71.8 1.0 collective-permute-start.15
  72.8 0.1 pad_maximum_fusion
  72.9 3.8 %targets.1.refs_13_ = f32[8,2,4,128,128]{4,3,2,1,0:T(8,128)S(1)} custom-call(bf16[8,128,512]{2,1,0:T(8,128)(2,1)S(1)} %bitcast.29, bf16[3,512,128]{2,1,0:T(8,128)(2,1)S(1)} %pad_maximum_fusion.1.tgt_ref), custom_call_target="tpu_custom_call" | custom-call | tf_op jit(solution)/shard_map/targets/pallas_call | solution.py:147
  76.7 2.7 %transform.2 = (bf16[32,2,128,512]{3,2,1,0:T(8,128)(2,1)S(1)}, f32[32,8,128]{2,1,0:T(8,128)S(1)}) custom-call(s32[2,4]{1,0:T(2,128)S(1)} %get-tuple-element.54.refs_0_, bf16[512,512]{1,0:T(8,128)(2,1)S(1)} %convolution_convert_fusion.1.refs_1_, bf16[512,512]{1,0:T(8,128)(2,1)S(1)} %convolution_convert_fusion.refs_2_, ...), custom_call_target="tpu_custom_call" | custom-call | tf_op jit(solution)/shard_map/transform/pallas_call | solution.py:95
  79.4 7.8 %collective-permute-done.10.refs_2_ = bf16[256,512]{1,0:T(8,128)(2,1)S(1)} collective-permute-done((bf16[256,512]{1,0:T(8,128)(2,1)S(1)}, bf16[256,512]{1,0:T(8,128)(2,1)S(1)}, u32[]{:S(2)}, u32[]{:S(2)}) %collective-permute-start.10) | collective-permute-done | bytes 262176 | tf_op jit(solution)/shard_map/ppermute | solution.py:332
  87.2 1.0 collective-permute-start.17
  88.2 0.5 collective-permute-start.16
  88.6 0.1 collective-permute-start.18
  88.8 0.0 copy-start.2
  88.8 1.5 %collective-permute-start.13 = (bf16[256,512]{1,0:T(8,128)(2,1)S(1)}, bf16[256,512]{1,0:T(8,128)(2,1)S(1)}, u32[]{:S(2)}, u32[]{:S(2)}) collective-permute-start(bf16[256,512]{1,0:T(8,128)(2,1)S(1)} %slice.22), channel_id=1, source_target_pairs={{0,32},{16,48},{32,64},{48,80},{64,96},{80,112},{96,0},{112,16},{1... | collective-permute-start | bytes 786440 | tf_op jit(solution)/shard_map/ppermute | solution.py:332
  90.4 0.0 collective-permute-done.15.refs_4_
  90.4 1.8 %collective-permute-start.14 = (bf16[256,512]{1,0:T(8,128)(2,1)S(1)}, bf16[256,512]{1,0:T(8,128)(2,1)S(1)}, u32[]{:S(2)}, u32[]{:S(2)}) collective-permute-start(bf16[256,512]{1,0:T(8,128)(2,1)S(1)} %slice.23), channel_id=1, source_target_pairs={{0,96},{16,112},{32,0},{48,16},{64,32},{80,48},{96,64},{112,80},{1... | collective-permute-start | bytes 786440 | tf_op jit(solution)/shard_map/ppermute | solution.py:332
  92.2 0.4 collective-permute-start.19
  92.5 0.0 collective-permute-done.16.refs_5_
  92.5 0.1 collective-permute-start.20
  92.7 3.9 %transform.3 = (bf16[32,2,128,512]{3,2,1,0:T(8,128)(2,1)S(1)}, f32[32,8,128]{2,1,0:T(8,128)S(1)}) custom-call(s32[2,4]{1,0:T(2,128)S(1)} %collective-permute-done.4.refs_0_, s32[2,4]{1,0:T(2,128)S(1)} %collective-permute-done.6.refs_1_, bf16[512,512]{1,0:T(8,128)(2,1)S(1)} %collective-permute-done.2.refs_2_, ...), custom_call_target="tpu_custom_call", output_to_operand_aliasing={{0}: (12, {}), {1}: (13, {})} | custom-call | tf_op jit(solution)/shard_map/transform/pallas_call | solution.py:95
  96.6 2.0 %collective-permute-done.13.refs_3_ = bf16[256,512]{1,0:T(8,128)(2,1)S(1)} collective-permute-done((bf16[256,512]{1,0:T(8,128)(2,1)S(1)}, bf16[256,512]{1,0:T(8,128)(2,1)S(1)}, u32[]{:S(2)}, u32[]{:S(2)}) %collective-permute-start.13) | collective-permute-done | bytes 262176 | tf_op jit(solution)/shard_map/ppermute | solution.py:332
  98.6 0.0 collective-permute-done.14.refs_4_
  98.6 0.7 collective-permute-start.21
  99.3 0.0 collective-permute-start.22
  99.3 0.0 collective-permute-done.20.refs_6_
  99.3 1.1 collective-permute-done.21.refs_7_
  100.5 0.4 collective-permute-done.22.refs_8_
  100.9 48.5 %finale.1 = (bf16[8,128,512]{2,1,0:T(8,128)(2,1)}, bf16[32,2,128,512]{3,2,1,0:T(8,128)(2,1)S(1)}, f32[32,8,128]{2,1,0:T(8,128)S(1)}) custom-call(s32[8,12]{1,0:T(8,128)S(1)} %copy-done.2, s32[8,12]{1,0:T(8,128)S(1)} %fusion.23.slot_ref, s32[2,4]{1,0:T(2,128)S(1)} %collective-permute-done.5.refs_0_, ...), custom_call_target="tpu_custom_call", output_to_operand_aliasing={{1}: (16, {}), {2}: (17, {})} | custom-call | tf_op jit(solution)/shard_map/finale/pallas_call | solution.py:265
  (37 shorter events, 0.3 us)
Async XLA Ops:
  0.0 3.7 %copy-start.7 = (s32[1,8,4]{1,2,0:T(4,128)S(1)}, s32[1,8,4]{1,2,0:T(4,128)}, u32[]{:S(2)}) copy-start(s32[1,8,4]{1,2,0:T(4,128)} %param.16) | copy-start | bytes 388
  3.7 8.4 %copy-start.5 = (f32[2,512]{1,0:T(2,128)S(1)}, f32[2,512]{1,0:T(2,128)}, u32[]{:S(2)}) copy-start(f32[2,512]{1,0:T(2,128)} %param.12) | copy-start | bytes 12292
  3.7 8.4 %copy-start.1 = (bf16[2,512,512]{2,1,0:T(8,128)(2,1)S(1)}, bf16[2,512,512]{2,1,0:T(8,128)(2,1)}, u32[]{:S(2)}) copy-start(bf16[2,512,512]{2,1,0:T(8,128)(2,1)} %refs_9_.1) | copy-start | bytes 3145732
  3.7 20.7 %collective-permute-start = (s32[8,4]{0,1:T(4,128)S(1)}, s32[8,4]{0,1:T(4,128)S(1)}, u32[]{:S(2)}, u32[]{:S(2)}) collective-permute-start(s32[8,4]{0,1:T(4,128)S(1)} %bitcast.35), channel_id=1, source_target_pairs={{0,16},{16,0},{32,48},{48,32},{64,80},{80,64},{96,112},{112,96},{1... | collective-permute-start | bytes 392 | tf_op jit(solution)/shard_map/ppermute | solution.py:332
  5.2 31.8 %all-to-all-start = ((bf16[16,64,768]{2,1,0:T(8,128)(2,1)}), bf16[16,64,768]{2,1,0:T(8,128)(2,1)}, u32[]{:S(2)}, u32[]{:S(2)}) async-start(bf16[16,64,768]{2,1,0:T(8,128)(2,1)} %arrange.2), calls=%async_computation | async-start | bytes 3145728 | tf_op jit(solution)/shard_map/all_to_all | solution.py:339
  12.1 4.6 %copy-start.4 = (f32[2,512]{1,0:T(2,128)S(1)}, f32[2,512]{1,0:T(2,128)}, u32[]{:S(2)}) copy-start(f32[2,512]{1,0:T(2,128)} %param.13) | copy-start | bytes 12292
  16.9 7.3 %copy-start.6 = (s32[8,12]{1,0:T(8,128)S(1)}, s32[8,12]{1,0:T(8,128)}, u32[]{:S(2)}) copy-start(s32[8,12]{1,0:T(8,128)} %param.17) | copy-start | bytes 1156
  38.1 5.7 %copy-start.3 = (bf16[1024,256]{1,0:T(8,128)(2,1)}, bf16[1024,256]{1,0:T(8,128)(2,1)S(1)}, u32[]{:S(2)}) copy-start(bf16[1024,256]{1,0:T(8,128)(2,1)S(1)} %slice.19) | copy-start | bytes 1572868
  38.1 5.7 %collective-permute-start.1 = (bf16[1024,256]{1,0:T(8,128)(2,1)S(1)}, bf16[1024,256]{1,0:T(8,128)(2,1)S(1)}, u32[]{:S(2)}, u32[]{:S(2)}) collective-permute-start(bf16[1024,256]{1,0:T(8,128)(2,1)S(1)} %slice.19), channel_id=1, source_target_pairs={{0,16},{16,0},{32,48},{48,32},{64,80},{80,64},{96,112},{112,96},{1... | collective-permute-start | bytes 1572872 | tf_op jit(solution)/shard_map/ppermute | solution.py:332
  39.5 23.8 %all-to-all-start.1 = ((bf16[16,64,512]{2,1,0:T(8,128)(2,1)}), bf16[16,64,512]{2,1,0:T(8,128)(2,1)}, u32[]{:S(2)}, u32[]{:S(2)}) async-start(bf16[16,64,512]{2,1,0:T(8,128)(2,1)} %arrange.3), calls=%async_computation.1 | async-start | bytes 2097152 | tf_op jit(solution)/shard_map/all_to_all | solution.py:352
  43.8 2.2 %copy-start.8 = (bf16[1024,256]{1,0:T(8,128)(2,1)}, bf16[1024,256]{1,0:T(8,128)(2,1)S(1)}, u32[]{:S(2)}) copy-start(bf16[1024,256]{1,0:T(8,128)(2,1)S(1)} %collective-permute-done.1) | copy-start | bytes 1572868
  46.0 17.2 %collective-permute-start.2 = (bf16[512,512]{1,0:T(8,128)(2,1)S(1)}, bf16[512,512]{1,0:T(8,128)(2,1)S(1)}, u32[]{:S(2)}, u32[]{:S(2)}) collective-permute-start(bf16[512,512]{1,0:T(8,128)(2,1)S(1)} %convolution_convert_fusion.1.refs_1_), channel_id=1, source_target_pairs={{0,32},{16,48},{32,64},{48,80},{64,96},{80,112},{96,0},{112,16},{1... | collective-permute-start | bytes 1572872 | tf_op jit(solution)/shard_map/ppermute | solution.py:332
  47.7 15.5 %collective-permute-start.3 = (bf16[512,512]{1,0:T(8,128)(2,1)S(1)}, bf16[512,512]{1,0:T(8,128)(2,1)S(1)}, u32[]{:S(2)}, u32[]{:S(2)}) collective-permute-start(bf16[512,512]{1,0:T(8,128)(2,1)S(1)} %convolution_convert_fusion.1.refs_1_), channel_id=1, source_target_pairs={{0,96},{16,112},{32,0},{48,16},{64,32},{80,48},{96,64},{112,80},{1... | collective-permute-start | bytes 1572872 | tf_op jit(solution)/shard_map/ppermute | solution.py:332
  49.9 12.3 %collective-permute-start.4 = (s32[2,4]{1,0:T(2,128)S(1)}, s32[2,4]{1,0:T(2,128)S(1)}, u32[]{:S(2)}, u32[]{:S(2)}) collective-permute-start(s32[2,4]{1,0:T(2,128)S(1)} %get-tuple-element.46), channel_id=1, source_target_pairs={{0,32},{16,48},{32,64},{48,80},{64,96},{80,112},{96,0},{112,16},{1... | collective-permute-start | bytes 104 | tf_op jit(solution)/shard_map/ppermute | solution.py:332
  49.9 13.3 %collective-permute-start.5 = (s32[2,4]{1,0:T(2,128)S(1)}, s32[2,4]{1,0:T(2,128)S(1)}, u32[]{:S(2)}, u32[]{:S(2)}) collective-permute-start(s32[2,4]{1,0:T(2,128)S(1)} %get-tuple-element.47), channel_id=1, source_target_pairs={{0,64},{16,80},{32,96},{48,112},{64,0},{80,16},{96,32},{112,48},{1... | collective-permute-start | bytes 104 | tf_op jit(solution)/shard_map/ppermute | solution.py:332
  52.5 10.7 %collective-permute-start.6 = (s32[2,4]{1,0:T(2,128)S(1)}, s32[2,4]{1,0:T(2,128)S(1)}, u32[]{:S(2)}, u32[]{:S(2)}) collective-permute-start(s32[2,4]{1,0:T(2,128)S(1)} %get-tuple-element.48), channel_id=1, source_target_pairs={{0,96},{16,112},{32,0},{48,16},{64,32},{80,48},{96,64},{112,80},{1... | collective-permute-start | bytes 104 | tf_op jit(solution)/shard_map/ppermute | solution.py:332
  62.2 9.5 %collective-permute-start.11 = (bf16[512,512]{1,0:T(8,128)(2,1)S(1)}, bf16[512,512]{1,0:T(8,128)(2,1)}, u32[]{:S(2)}, u32[]{:S(2)}) collective-permute-start(bf16[512,512]{1,0:T(8,128)(2,1)S(1)} %convolution_convert_fusion.1.refs_1_), channel_id=1, source_target_pairs={{0,16},{16,0},{32,48},{48,32},{64,80},{80,64},{96,112},{112,96},{1... | collective-permute-start | bytes 1572872 | tf_op jit(solution)/shard_map/ppermute | solution.py:332
  65.8 6.0 %collective-permute-start.12 = (bf16[512,512]{1,0:T(8,128)(2,1)S(1)}, bf16[512,512]{1,0:T(8,128)(2,1)S(1)}, u32[]{:S(2)}, u32[]{:S(2)}) collective-permute-start(bf16[512,512]{1,0:T(8,128)(2,1)S(1)} %convolution_convert_fusion.refs_2_), channel_id=1, source_target_pairs={{0,16},{16,0},{32,48},{48,32},{64,80},{80,64},{96,112},{112,96},{1... | collective-permute-start | bytes 1572872 | tf_op jit(solution)/shard_map/ppermute | solution.py:332
  66.6 21.6 %collective-permute-start.7 = (bf16[512,512]{1,0:T(8,128)(2,1)S(1)}, bf16[512,512]{1,0:T(8,128)(2,1)S(1)}, u32[]{:S(2)}, u32[]{:S(2)}) collective-permute-start(bf16[512,512]{1,0:T(8,128)(2,1)S(1)} %convolution_convert_fusion.refs_2_), channel_id=1, source_target_pairs={{0,32},{16,48},{32,64},{48,80},{64,96},{80,112},{96,0},{112,16},{1... | collective-permute-start | bytes 1572872 | tf_op jit(solution)/shard_map/ppermute | solution.py:332
  68.0 20.1 %collective-permute-start.8 = (bf16[512,512]{1,0:T(8,128)(2,1)S(1)}, bf16[512,512]{1,0:T(8,128)(2,1)S(1)}, u32[]{:S(2)}, u32[]{:S(2)}) collective-permute-start(bf16[512,512]{1,0:T(8,128)(2,1)S(1)} %convolution_convert_fusion.refs_2_), channel_id=1, source_target_pairs={{0,96},{16,112},{32,0},{48,16},{64,32},{80,48},{96,64},{112,80},{1... | collective-permute-start | bytes 1572872 | tf_op jit(solution)/shard_map/ppermute | solution.py:332
  70.2 17.0 %collective-permute-start.10 = (bf16[256,512]{1,0:T(8,128)(2,1)S(1)}, bf16[256,512]{1,0:T(8,128)(2,1)S(1)}, u32[]{:S(2)}, u32[]{:S(2)}) collective-permute-start(bf16[256,512]{1,0:T(8,128)(2,1)S(1)} %slice.21), channel_id=1, source_target_pairs={{0,96},{16,112},{32,0},{48,16},{64,32},{80,48},{96,64},{112,80},{1... | collective-permute-start | bytes 786440 | tf_op jit(solution)/shard_map/ppermute | solution.py:332
  71.7 16.4 %collective-permute-start.9 = (bf16[256,512]{1,0:T(8,128)(2,1)S(1)}, bf16[256,512]{1,0:T(8,128)(2,1)S(1)}, u32[]{:S(2)}, u32[]{:S(2)}) collective-permute-start(bf16[256,512]{1,0:T(8,128)(2,1)S(1)} %slice.20), channel_id=1, source_target_pairs={{0,32},{16,48},{32,64},{48,80},{64,96},{80,112},{96,0},{112,16},{1... | collective-permute-start | bytes 786440 | tf_op jit(solution)/shard_map/ppermute | solution.py:332
  71.8 18.5 %collective-permute-start.15 = (bf16[512,512]{1,0:T(8,128)(2,1)S(1)}, bf16[512,512]{1,0:T(8,128)(2,1)S(1)}, u32[]{:S(2)}, u32[]{:S(2)}) collective-permute-start(bf16[512,512]{1,0:T(8,128)(2,1)S(1)} %collective-permute-done.2.refs_2_), channel_id=1, source_target_pairs={{0,16},{16,0},{32,48},{48,32},{64,80},{80,64},{96,112},{112,96},{1... | collective-permute-start | bytes 1572872 | tf_op jit(solution)/shard_map/ppermute | solution.py:332
  87.2 5.0 %collective-permute-start.17 = (bf16[512,512]{1,0:T(8,128)(2,1)S(1)}, bf16[512,512]{1,0:T(8,128)(2,1)S(1)}, u32[]{:S(2)}, u32[]{:S(2)}) collective-permute-start(bf16[512,512]{1,0:T(8,128)(2,1)S(1)} %collective-permute-done.3.refs_6_), channel_id=1, source_target_pairs={{0,16},{16,0},{32,48},{48,32},{64,80},{80,64},{96,112},{112,96},{1... | collective-permute-start | bytes 1572872 | tf_op jit(solution)/shard_map/ppermute | solution.py:332
  88.2 4.3 %collective-permute-start.16 = (bf16[512,512]{1,0:T(8,128)(2,1)S(1)}, bf16[512,512]{1,0:T(8,128)(2,1)S(1)}, u32[]{:S(2)}, u32[]{:S(2)}) collective-permute-start(bf16[512,512]{1,0:T(8,128)(2,1)S(1)} %collective-permute-done.7.refs_3_), channel_id=1, source_target_pairs={{0,16},{16,0},{32,48},{48,32},{64,80},{80,64},{96,112},{112,96},{1... | collective-permute-start | bytes 1572872 | tf_op jit(solution)/shard_map/ppermute | solution.py:332
  88.6 4.0 %collective-permute-start.18 = (bf16[512,512]{1,0:T(8,128)(2,1)S(1)}, bf16[512,512]{1,0:T(8,128)(2,1)S(1)}, u32[]{:S(2)}, u32[]{:S(2)}) collective-permute-start(bf16[512,512]{1,0:T(8,128)(2,1)S(1)} %collective-permute-done.8.refs_7_), channel_id=1, source_target_pairs={{0,16},{16,0},{32,48},{48,32},{64,80},{80,64},{96,112},{112,96},{1... | collective-permute-start | bytes 1572872 | tf_op jit(solution)/shard_map/ppermute | solution.py:332
  88.8 12.0 %copy-start.2 = (s32[8,12]{1,0:T(8,128)S(1)}, s32[8,12]{1,0:T(8,128)}, u32[]{:S(2)}) copy-start(s32[8,12]{1,0:T(8,128)} %rel_ref.1) | copy-start | bytes 1156
  88.8 9.8 %collective-permute-start.13 = (bf16[256,512]{1,0:T(8,128)(2,1)S(1)}, bf16[256,512]{1,0:T(8,128)(2,1)S(1)}, u32[]{:S(2)}, u32[]{:S(2)}) collective-permute-start(bf16[256,512]{1,0:T(8,128)(2,1)S(1)} %slice.22), channel_id=1, source_target_pairs={{0,32},{16,48},{32,64},{48,80},{64,96},{80,112},{96,0},{112,16},{1... | collective-permute-start | bytes 786440 | tf_op jit(solution)/shard_map/ppermute | solution.py:332
  90.4 8.2 %collective-permute-start.14 = (bf16[256,512]{1,0:T(8,128)(2,1)S(1)}, bf16[256,512]{1,0:T(8,128)(2,1)S(1)}, u32[]{:S(2)}, u32[]{:S(2)}) collective-permute-start(bf16[256,512]{1,0:T(8,128)(2,1)S(1)} %slice.23), channel_id=1, source_target_pairs={{0,96},{16,112},{32,0},{48,16},{64,32},{80,48},{96,64},{112,80},{1... | collective-permute-start | bytes 786440 | tf_op jit(solution)/shard_map/ppermute | solution.py:332
  92.2 7.1 %collective-permute-start.19 = (bf16[256,512]{1,0:T(8,128)(2,1)S(1)}, bf16[256,512]{1,0:T(8,128)(2,1)S(1)}, u32[]{:S(2)}, u32[]{:S(2)}) collective-permute-start(bf16[256,512]{1,0:T(8,128)(2,1)S(1)} %collective-permute-done.9.refs_1_), channel_id=1, source_target_pairs={{0,16},{16,0},{32,48},{48,32},{64,80},{80,64},{96,112},{112,96},{1... | collective-permute-start | bytes 786440 | tf_op jit(solution)/shard_map/ppermute | solution.py:332
  92.5 6.8 %collective-permute-start.20 = (bf16[256,512]{1,0:T(8,128)(2,1)S(1)}, bf16[256,512]{1,0:T(8,128)(2,1)S(1)}, u32[]{:S(2)}, u32[]{:S(2)}) collective-permute-start(bf16[256,512]{1,0:T(8,128)(2,1)S(1)} %collective-permute-done.10.refs_2_), channel_id=1, source_target_pairs={{0,16},{16,0},{32,48},{48,32},{64,80},{80,64},{96,112},{112,96},{1... | collective-permute-start | bytes 786440 | tf_op jit(solution)/shard_map/ppermute | solution.py:332
  92.7 8.2 %copy-start = (bf16[8,12,128,128]{3,2,1,0:T(8,128)(2,1)S(1)}, bf16[8,12,128,128]{3,2,1,0:T(8,128)(2,1)}, u32[]{:S(2)}) copy-start(bf16[8,12,128,128]{3,2,1,0:T(8,128)(2,1)} %caps.1.refs_12_) | copy-start | bytes 9437188
  98.6 1.8 %collective-permute-start.21 = (bf16[256,512]{1,0:T(8,128)(2,1)S(1)}, bf16[256,512]{1,0:T(8,128)(2,1)S(1)}, u32[]{:S(2)}, u32[]{:S(2)}) collective-permute-start(bf16[256,512]{1,0:T(8,128)(2,1)S(1)} %collective-permute-done.13.refs_3_), channel_id=1, source_target_pairs={{0,16},{16,0},{32,48},{48,32},{64,80},{80,64},{96,112},{112,96},{1... | collective-permute-start | bytes 786440 | tf_op jit(solution)/shard_map/ppermute | solution.py:332
  99.3 1.5 %collective-permute-start.22 = (bf16[256,512]{1,0:T(8,128)(2,1)S(1)}, bf16[256,512]{1,0:T(8,128)(2,1)S(1)}, u32[]{:S(2)}, u32[]{:S(2)}) collective-permute-start(bf16[256,512]{1,0:T(8,128)(2,1)S(1)} %collective-permute-done.14.refs_4_), channel_id=1, source_target_pairs={{0,16},{16,0},{32,48},{48,32},{64,80},{80,64},{96,112},{112,96},{1... | collective-permute-start | bytes 786440 | tf_op jit(solution)/shard_map/ppermute | solution.py:332

commit v23 on v22

--- a/solution.py
+++ b/solution.py
@@ -14,32 +14,36 @@
 BF16 = jnp.bfloat16
 
 
-def arrange_kernel(low, high, core_ref, x_ref, w_ref, out_ref):
+def arrange_kernel(low, high, core_ref, x_ref, w_ref, out_ref, sem):
     peers, _, columns = out_ref.shape
     total = x_ref.shape[1] // peers
     rows = high - low
-    for q in range(peers):
-        out_ref[q, :, :rows] = x_ref[:, q * total + low : q * total + high]
-        if columns > rows:
-            out_ref[q, :, rows:] = w_ref[...]
+    copies = [
+        pltpu.make_async_copy(
+            x_ref.at[:, pl.ds(q * total + low, rows)], out_ref.at[q, :, pl.ds(0, rows)], sem.at[q]
+        )
+        for q in range(peers)
+    ]
+    for c in copies:
+        c.start()
+    if columns > rows:
+        half = columns - rows
+        share = w_ref[:, pl.ds(pl.multiple_of(core_ref[0] * half, half), half)]
+        for q in range(peers):
+            out_ref[q, :, rows:] = share
+    for c in copies:
+        c.wait()
 
 
 def arrange(features, weight, core, peers, low, high, half):
-    depth, columns = features.shape
-    rows = columns // peers
-    step = 4
+    depth = features.shape[0]
+    inside = pl.BlockSpec(memory_space=pltpu.VMEM)
     return pl.pallas_call(
         functools.partial(arrange_kernel, low, high),
-        grid_spec=pltpu.PrefetchScalarGridSpec(
-            num_scalar_prefetch=1,
-            grid=(peers // step,),
-            in_specs=[
-                pl.BlockSpec((depth, step * rows), lambda i, core_ref: (0, i)),
-                pl.BlockSpec((depth, weight.shape[1] // 2), lambda i, core_ref: (0, core_ref[0])),
-            ],
-            out_specs=pl.BlockSpec((step, depth, high - low + half), lambda i, core_ref: (i, 0, 0)),
-        ),
+        in_specs=[pl.BlockSpec(memory_space=pltpu.SMEM), pl.BlockSpec(memory_space=pl.ANY), inside],
+        out_specs=inside,
         out_shape=jax.ShapeDtypeStruct((peers, depth, high - low + half), BF16),
+        scratch_shapes=[pltpu.SemaphoreType.DMA((peers,))],
         name="arrange",
     )(core.reshape(1), features, weight)
 

time: 150 us -> 150 us (level)
  no operation moved by 1% of the time
where the time goes in v23:
time: 150 us; the launch traced here: 149 us
  Pallas kernels  72.3 us (48%)
  starting transfers between devices  34.8 us (23%)
  waiting for transfers between devices  33.6 us (22%)
  matrix products  5.65 us (4%)
    pallas_call x1, Pallas kernels, finale(): pl.pallas_call(functools.partial(finale_kernel, bounds, first), in_specs=...  48.5 us
    ppermute x23, starting transfers between devices, send(): return lax.ppermute(x, 'graph', pairs)  23.6 us
    ppermute x23, waiting for transfers between devices, send(): return lax.ppermute(x, 'graph', pairs)  20.9 us
    all_to_all x1, waiting for transfers between devices, shards(): lax.all_to_all(first, 'feat', 0, 0, tiled=True)  12.7 us
    pallas_call x1, Pallas kernels, caps(): pl.pallas_call(cap_kernel, grid=shape[:1], in_specs=[spec], out_specs=spe...  6.92 us
    all_to_all x1, starting transfers between devices, shards(): lax.all_to_all(first, 'feat', 0, 0, tiled=True)  6.88 us
    pallas_call x2, Pallas kernels, arrange(): pl.pallas_call(functools.partial(arrange_kernel, low, high), in_specs=[pl...  6.62 us
    pallas_call x2, Pallas kernels, transform(): pl.pallas_call(functools.partial(transform_kernel, bounds, first), in_spe...  6.59 us
  transfers between devices with their start and end apart: 25, of which 7 were waited for; matrix products, arithmetic and copies ran while one was open for 5% of the time, Pallas kernels for 14%

profile of v23, /device:TPU:1, one launch (start us, length us, event | category | flops | bytes accessed | tf_op | source)
XLA Modules:
  0.0 149.1 jit_solution(8415287501426412564)
XLA Ops:
  0.0 3.4 %arrange.2 = bf16[16,64,768]{2,1,0:T(8,128)(2,1)} custom-call(s32[1]{0:T(128)} %bitcast.core_ref, bf16[64,16384]{1,0:T(8,128)(2,1)} %bitcast.31, bf16[64,512]{1,0:T(8,128)(2,1)} %w_ref.3), custom_call_target="tpu_custom_call" | custom-call | tf_op jit(solution)/shard_map/arrange/pallas_call | solution.py:41
  3.4 0.0 copy-start.5
  3.5 0.0 copy-start.1
  3.5 1.5 %collective-permute-start = (s32[8,4]{0,1:T(4,128)S(1)}, s32[8,4]{0,1:T(4,128)S(1)}, u32[]{:S(2)}, u32[]{:S(2)}) collective-permute-start(s32[8,4]{0,1:T(4,128)S(1)} %bitcast.35), channel_id=1, source_target_pairs={{0,16},{16,0},{32,48},{48,32},{64,80},{80,64},{96,112},{112,96},{1... | collective-permute-start | bytes 392 | tf_op jit(solution)/shard_map/ppermute | solution.py:336
  5.0 6.9 %all-to-all-start = ((bf16[16,64,768]{2,1,0:T(8,128)(2,1)}), bf16[16,64,768]{2,1,0:T(8,128)(2,1)}, u32[]{:S(2)}, u32[]{:S(2)}) async-start(bf16[16,64,768]{2,1,0:T(8,128)(2,1)} %arrange.2), calls=%async_computation | async-start | bytes 3145728 | tf_op jit(solution)/shard_map/all_to_all | solution.py:343
  11.9 0.0 copy-start.4
  11.9 0.9 fusion
  13.0 3.2 %arrange.3 = bf16[16,64,512]{2,1,0:T(8,128)(2,1)} custom-call(s32[1]{0:T(128)} %bitcast.core_ref, bf16[64,16384]{1,0:T(8,128)(2,1)} %bitcast.32, bf16[64,512]{1,0:T(8,128)(2,1)} %w_ref.3), custom_call_target="tpu_custom_call" | custom-call | tf_op jit(solution)/shard_map/arrange/pallas_call | solution.py:41
  16.2 0.1 copy.15
  16.3 0.0 copy-start.6
  16.4 6.9 %caps.1.refs_12_ = bf16[8,12,128,128]{3,2,1,0:T(8,128)(2,1)} custom-call(s32[8,12,128,128]{3,2,1,0:T(8,128)} %mask_ref.1), custom_call_target="tpu_custom_call" | custom-call | tf_op jit(solution)/shard_map/caps/pallas_call | solution.py:121
  23.3 0.1 pad.19.clone
  23.4 0.1 select_multiply_fusion
  23.5 0.1 fusion.6
  23.7 0.1 maximum_maximum_fusion.refs_6_.refs_11_.refs_10_
  23.8 0.0 collective-permute-done
  23.8 0.3 fusion.10
  24.1 12.7 %all-to-all-done = bf16[16,64,768]{2,1,0:T(8,128)(2,1)} async-done(((bf16[16,64,768]{2,1,0:T(8,128)(2,1)}), bf16[16,64,768]{2,1,0:T(8,128)(2,1)}, u32[]{:S(2)}, u32[]{:S(2)}) %all-to-all-start) | async-done | bytes 1572896 | tf_op jit(solution)/shard_map/all_to_all | solution.py:343
  36.8 1.1 slice.19
  37.9 1.4 collective-permute-start.1
  39.2 4.3 %all-to-all-start.1 = ((bf16[16,64,512]{2,1,0:T(8,128)(2,1)}), bf16[16,64,512]{2,1,0:T(8,128)(2,1)}, u32[]{:S(2)}, u32[]{:S(2)}) async-start(bf16[16,64,512]{2,1,0:T(8,128)(2,1)} %arrange.3), calls=%async_computation.1 | async-start | bytes 2097152 | tf_op jit(solution)/shard_map/all_to_all | solution.py:356
  43.6 0.0 collective-permute-done.1
  43.6 2.2 %convolution_convert_fusion.1.refs_1_ = bf16[512,512]{1,0:T(8,128)(2,1)S(1)} fusion(bf16[1024,768]{1,0:T(8,128)(2,1)} %bitcast.2, bf16[1024,256]{1,0:T(8,128)(2,1)S(1)} %collective-permute-done.1, bf16[1024,256]{1,0:T(8,128)(2,1)S(1)} %slice.19, pred[]{:T(512)S(6)} %eq.30), kind=kOutput, calls=%fused_computation.1 | convolution fusion | flops 541851648 | bytes 2621441 | tf_op jit(solution)/shard_map/dot_general | solution.py:363
  45.8 1.7 %collective-permute-start.2 = (bf16[512,512]{1,0:T(8,128)(2,1)S(1)}, bf16[512,512]{1,0:T(8,128)(2,1)S(1)}, u32[]{:S(2)}, u32[]{:S(2)}) collective-permute-start(bf16[512,512]{1,0:T(8,128)(2,1)S(1)} %convolution_convert_fusion.1.refs_1_), channel_id=1, source_target_pairs={{0,32},{16,48},{32,64},{48,80},{64,96},{80,112},{96,0},{112,16},{1... | collective-permute-start | bytes 1572872 | tf_op jit(solution)/shard_map/ppermute | solution.py:336
  47.5 2.2 %collective-permute-start.3 = (bf16[512,512]{1,0:T(8,128)(2,1)S(1)}, bf16[512,512]{1,0:T(8,128)(2,1)S(1)}, u32[]{:S(2)}, u32[]{:S(2)}) collective-permute-start(bf16[512,512]{1,0:T(8,128)(2,1)S(1)} %convolution_convert_fusion.1.refs_1_), channel_id=1, source_target_pairs={{0,96},{16,112},{32,0},{48,16},{64,32},{80,48},{96,64},{112,80},{1... | collective-permute-start | bytes 1572872 | tf_op jit(solution)/shard_map/ppermute | solution.py:336
  49.7 0.0 collective-permute-start.4
  49.7 2.6 %collective-permute-start.5 = (s32[2,4]{1,0:T(2,128)S(1)}, s32[2,4]{1,0:T(2,128)S(1)}, u32[]{:S(2)}, u32[]{:S(2)}) collective-permute-start(s32[2,4]{1,0:T(2,128)S(1)} %get-tuple-element.47), channel_id=1, source_target_pairs={{0,64},{16,80},{32,96},{48,112},{64,0},{80,16},{96,32},{112,48},{1... | collective-permute-start | bytes 104 | tf_op jit(solution)/shard_map/ppermute | solution.py:336
  52.3 0.7 collective-permute-start.6
  53.0 9.0 %collective-permute-done.4.refs_0_ = s32[2,4]{1,0:T(2,128)S(1)} collective-permute-done((s32[2,4]{1,0:T(2,128)S(1)}, s32[2,4]{1,0:T(2,128)S(1)}, u32[]{:S(2)}, u32[]{:S(2)}) %collective-permute-start.4) | collective-permute-done | bytes 64 | tf_op jit(solution)/shard_map/ppermute | solution.py:336
  62.0 0.5 collective-permute-start.11
  62.6 0.5 collective-permute-done.5.refs_0_
  63.0 0.0 collective-permute-done.3.refs_6_
  63.0 2.6 %convolution_convert_fusion.refs_2_ = bf16[512,512]{1,0:T(8,128)(2,1)S(1)} fusion(bf16[1024,512]{1,0:T(8,128)(2,1)} %bitcast.11, bf16[1024,256]{1,0:T(8,128)(2,1)} %copy-done.8, bf16[1024,256]{1,0:T(8,128)(2,1)} %copy-done.3, pred[]{:T(512)S(6)} %eq.30), kind=kOutput, calls=%fused_computation | convolution fusion | flops 541851648 | bytes 2621441 | tf_op jit(solution)/shard_map/dot_general | solution.py:363
  65.6 0.8 collective-permute-start.12
  66.4 1.4 collective-permute-start.7
  67.8 2.1 %collective-permute-start.8 = (bf16[512,512]{1,0:T(8,128)(2,1)S(1)}, bf16[512,512]{1,0:T(8,128)(2,1)S(1)}, u32[]{:S(2)}, u32[]{:S(2)}) collective-permute-start(bf16[512,512]{1,0:T(8,128)(2,1)S(1)} %convolution_convert_fusion.refs_2_), channel_id=1, source_target_pairs={{0,96},{16,112},{32,0},{48,16},{64,32},{80,48},{96,64},{112,80},{1... | collective-permute-start | bytes 1572872 | tf_op jit(solution)/shard_map/ppermute | solution.py:336
  69.9 1.5 %collective-permute-start.10 = (bf16[256,512]{1,0:T(8,128)(2,1)S(1)}, bf16[256,512]{1,0:T(8,128)(2,1)S(1)}, u32[]{:S(2)}, u32[]{:S(2)}) collective-permute-start(bf16[256,512]{1,0:T(8,128)(2,1)S(1)} %slice.21), channel_id=1, source_target_pairs={{0,96},{16,112},{32,0},{48,16},{64,32},{80,48},{96,64},{112,80},{1... | collective-permute-start | bytes 786440 | tf_op jit(solution)/shard_map/ppermute | solution.py:336
  71.5 0.1 collective-permute-start.9
  71.6 1.0 collective-permute-start.15
  72.6 0.1 pad_maximum_fusion
  72.7 3.8 %targets.1.refs_13_ = f32[8,2,4,128,128]{4,3,2,1,0:T(8,128)S(1)} custom-call(bf16[8,128,512]{2,1,0:T(8,128)(2,1)S(1)} %bitcast.29, bf16[3,512,128]{2,1,0:T(8,128)(2,1)S(1)} %pad_maximum_fusion.1.tgt_ref), custom_call_target="tpu_custom_call" | custom-call | tf_op jit(solution)/shard_map/targets/pallas_call | solution.py:151
  76.5 2.7 %transform.2 = (bf16[32,2,128,512]{3,2,1,0:T(8,128)(2,1)S(1)}, f32[32,8,128]{2,1,0:T(8,128)S(1)}) custom-call(s32[2,4]{1,0:T(2,128)S(1)} %get-tuple-element.54.refs_0_, bf16[512,512]{1,0:T(8,128)(2,1)S(1)} %convolution_convert_fusion.1.refs_1_, bf16[512,512]{1,0:T(8,128)(2,1)S(1)} %convolution_convert_fusion.refs_2_, ...), custom_call_target="tpu_custom_call" | custom-call | tf_op jit(solution)/shard_map/transform/pallas_call | solution.py:99
  79.2 7.8 %collective-permute-done.10.refs_2_ = bf16[256,512]{1,0:T(8,128)(2,1)S(1)} collective-permute-done((bf16[256,512]{1,0:T(8,128)(2,1)S(1)}, bf16[256,512]{1,0:T(8,128)(2,1)S(1)}, u32[]{:S(2)}, u32[]{:S(2)}) %collective-permute-start.10) | collective-permute-done | bytes 262176 | tf_op jit(solution)/shard_map/ppermute | solution.py:336
  87.0 1.0 collective-permute-start.17
  88.0 0.0 collective-permute-done.9.refs_1_
  88.0 0.0 collective-permute-done.7.refs_3_
  88.0 0.0 collective-permute-done.8.refs_7_
  88.0 0.5 collective-permute-start.16
  88.4 0.1 collective-permute-start.18
  88.6 0.0 copy-start.2
  88.6 1.5 %collective-permute-start.13 = (bf16[256,512]{1,0:T(8,128)(2,1)S(1)}, bf16[256,512]{1,0:T(8,128)(2,1)S(1)}, u32[]{:S(2)}, u32[]{:S(2)}) collective-permute-start(bf16[256,512]{1,0:T(8,128)(2,1)S(1)} %slice.22), channel_id=1, source_target_pairs={{0,32},{16,48},{32,64},{48,80},{64,96},{80,112},{96,0},{112,16},{1... | collective-permute-start | bytes 786440 | tf_op jit(solution)/shard_map/ppermute | solution.py:336
  90.2 1.8 %collective-permute-start.14 = (bf16[256,512]{1,0:T(8,128)(2,1)S(1)}, bf16[256,512]{1,0:T(8,128)(2,1)S(1)}, u32[]{:S(2)}, u32[]{:S(2)}) collective-permute-start(bf16[256,512]{1,0:T(8,128)(2,1)S(1)} %slice.23), channel_id=1, source_target_pairs={{0,96},{16,112},{32,0},{48,16},{64,32},{80,48},{96,64},{112,80},{1... | collective-permute-start | bytes 786440 | tf_op jit(solution)/shard_map/ppermute | solution.py:336
  91.9 0.0 collective-permute-done.17.refs_8_
  92.0 0.4 collective-permute-start.19
  92.3 0.0 collective-permute-done.16.refs_5_
  92.3 0.1 collective-permute-start.20
  92.5 0.0 collective-permute-done.18.refs_9_
  92.5 3.9 %transform.3 = (bf16[32,2,128,512]{3,2,1,0:T(8,128)(2,1)S(1)}, f32[32,8,128]{2,1,0:T(8,128)S(1)}) custom-call(s32[2,4]{1,0:T(2,128)S(1)} %collective-permute-done.4.refs_0_, s32[2,4]{1,0:T(2,128)S(1)} %collective-permute-done.6.refs_1_, bf16[512,512]{1,0:T(8,128)(2,1)S(1)} %collective-permute-done.2.refs_2_, ...), custom_call_target="tpu_custom_call", output_to_operand_aliasing={{0}: (12, {}), {1}: (13, {})} | custom-call | tf_op jit(solution)/shard_map/transform/pallas_call | solution.py:99
  96.4 2.0 %collective-permute-done.13.refs_3_ = bf16[256,512]{1,0:T(8,128)(2,1)S(1)} collective-permute-done((bf16[256,512]{1,0:T(8,128)(2,1)S(1)}, bf16[256,512]{1,0:T(8,128)(2,1)S(1)}, u32[]{:S(2)}, u32[]{:S(2)}) %collective-permute-start.13) | collective-permute-done | bytes 262176 | tf_op jit(solution)/shard_map/ppermute | solution.py:336
  98.4 0.7 collective-permute-start.21
  99.1 0.0 collective-permute-start.22
  99.1 1.1 collective-permute-done.21.refs_7_
  100.3 0.4 collective-permute-done.22.refs_8_
  100.6 48.5 %finale.1 = (bf16[8,128,512]{2,1,0:T(8,128)(2,1)}, bf16[32,2,128,512]{3,2,1,0:T(8,128)(2,1)S(1)}, f32[32,8,128]{2,1,0:T(8,128)S(1)}) custom-call(s32[8,12]{1,0:T(8,128)S(1)} %copy-done.2, s32[8,12]{1,0:T(8,128)S(1)} %fusion.23.slot_ref, s32[2,4]{1,0:T(2,128)S(1)} %collective-permute-done.5.refs_0_, ...), custom_call_target="tpu_custom_call", output_to_operand_aliasing={{1}: (16, {}), {2}: (17, {})} | custom-call | tf_op jit(solution)/shard_map/finale/pallas_call | solution.py:269
  (37 shorter events, 0.3 us)
Async XLA Ops:
  0.0 3.5 %copy-start.7 = (s32[1,8,4]{1,2,0:T(4,128)S(1)}, s32[1,8,4]{1,2,0:T(4,128)}, u32[]{:S(2)}) copy-start(s32[1,8,4]{1,2,0:T(4,128)} %param.16) | copy-start | bytes 388
  3.4 8.4 %copy-start.5 = (f32[2,512]{1,0:T(2,128)S(1)}, f32[2,512]{1,0:T(2,128)}, u32[]{:S(2)}) copy-start(f32[2,512]{1,0:T(2,128)} %param.12) | copy-start | bytes 12292
  3.5 8.4 %copy-start.1 = (bf16[2,512,512]{2,1,0:T(8,128)(2,1)S(1)}, bf16[2,512,512]{2,1,0:T(8,128)(2,1)}, u32[]{:S(2)}) copy-start(bf16[2,512,512]{2,1,0:T(8,128)(2,1)} %refs_9_.1) | copy-start | bytes 3145732
  3.5 20.3 %collective-permute-start = (s32[8,4]{0,1:T(4,128)S(1)}, s32[8,4]{0,1:T(4,128)S(1)}, u32[]{:S(2)}, u32[]{:S(2)}) collective-permute-start(s32[8,4]{0,1:T(4,128)S(1)} %bitcast.35), channel_id=1, source_target_pairs={{0,16},{16,0},{32,48},{48,32},{64,80},{80,64},{96,112},{112,96},{1... | collective-permute-start | bytes 392 | tf_op jit(solution)/shard_map/ppermute | solution.py:336
  5.0 31.8 %all-to-all-start = ((bf16[16,64,768]{2,1,0:T(8,128)(2,1)}), bf16[16,64,768]{2,1,0:T(8,128)(2,1)}, u32[]{:S(2)}, u32[]{:S(2)}) async-start(bf16[16,64,768]{2,1,0:T(8,128)(2,1)} %arrange.2), calls=%async_computation | async-start | bytes 3145728 | tf_op jit(solution)/shard_map/all_to_all | solution.py:343
  11.9 4.3 %copy-start.4 = (f32[2,512]{1,0:T(2,128)S(1)}, f32[2,512]{1,0:T(2,128)}, u32[]{:S(2)}) copy-start(f32[2,512]{1,0:T(2,128)} %param.13) | copy-start | bytes 12292
  16.3 7.3 %copy-start.6 = (s32[8,12]{1,0:T(8,128)S(1)}, s32[8,12]{1,0:T(8,128)}, u32[]{:S(2)}) copy-start(s32[8,12]{1,0:T(8,128)} %param.17) | copy-start | bytes 1156
  37.9 5.7 %copy-start.3 = (bf16[1024,256]{1,0:T(8,128)(2,1)}, bf16[1024,256]{1,0:T(8,128)(2,1)S(1)}, u32[]{:S(2)}) copy-start(bf16[1024,256]{1,0:T(8,128)(2,1)S(1)} %slice.19) | copy-start | bytes 1572868
  37.9 5.7 %collective-permute-start.1 = (bf16[1024,256]{1,0:T(8,128)(2,1)S(1)}, bf16[1024,256]{1,0:T(8,128)(2,1)S(1)}, u32[]{:S(2)}, u32[]{:S(2)}) collective-permute-start(bf16[1024,256]{1,0:T(8,128)(2,1)S(1)} %slice.19), channel_id=1, source_target_pairs={{0,16},{16,0},{32,48},{48,32},{64,80},{80,64},{96,112},{112,96},{1... | collective-permute-start | bytes 1572872 | tf_op jit(solution)/shard_map/ppermute | solution.py:336
  39.2 23.8 %all-to-all-start.1 = ((bf16[16,64,512]{2,1,0:T(8,128)(2,1)}), bf16[16,64,512]{2,1,0:T(8,128)(2,1)}, u32[]{:S(2)}, u32[]{:S(2)}) async-start(bf16[16,64,512]{2,1,0:T(8,128)(2,1)} %arrange.3), calls=%async_computation.1 | async-start | bytes 2097152 | tf_op jit(solution)/shard_map/all_to_all | solution.py:356
  43.6 2.2 %copy-start.8 = (bf16[1024,256]{1,0:T(8,128)(2,1)}, bf16[1024,256]{1,0:T(8,128)(2,1)S(1)}, u32[]{:S(2)}) copy-start(bf16[1024,256]{1,0:T(8,128)(2,1)S(1)} %collective-permute-done.1) | copy-start | bytes 1572868
  45.8 17.2 %collective-permute-start.2 = (bf16[512,512]{1,0:T(8,128)(2,1)S(1)}, bf16[512,512]{1,0:T(8,128)(2,1)S(1)}, u32[]{:S(2)}, u32[]{:S(2)}) collective-permute-start(bf16[512,512]{1,0:T(8,128)(2,1)S(1)} %convolution_convert_fusion.1.refs_1_), channel_id=1, source_target_pairs={{0,32},{16,48},{32,64},{48,80},{64,96},{80,112},{96,0},{112,16},{1... | collective-permute-start | bytes 1572872 | tf_op jit(solution)/shard_map/ppermute | solution.py:336
  47.5 15.5 %collective-permute-start.3 = (bf16[512,512]{1,0:T(8,128)(2,1)S(1)}, bf16[512,512]{1,0:T(8,128)(2,1)S(1)}, u32[]{:S(2)}, u32[]{:S(2)}) collective-permute-start(bf16[512,512]{1,0:T(8,128)(2,1)S(1)} %convolution_convert_fusion.1.refs_1_), channel_id=1, source_target_pairs={{0,96},{16,112},{32,0},{48,16},{64,32},{80,48},{96,64},{112,80},{1... | collective-permute-start | bytes 1572872 | tf_op jit(solution)/shard_map/ppermute | solution.py:336
  49.7 12.3 %collective-permute-start.4 = (s32[2,4]{1,0:T(2,128)S(1)}, s32[2,4]{1,0:T(2,128)S(1)}, u32[]{:S(2)}, u32[]{:S(2)}) collective-permute-start(s32[2,4]{1,0:T(2,128)S(1)} %get-tuple-element.46), channel_id=1, source_target_pairs={{0,32},{16,48},{32,64},{48,80},{64,96},{80,112},{96,0},{112,16},{1... | collective-permute-start | bytes 104 | tf_op jit(solution)/shard_map/ppermute | solution.py:336
  49.7 13.3 %collective-permute-start.5 = (s32[2,4]{1,0:T(2,128)S(1)}, s32[2,4]{1,0:T(2,128)S(1)}, u32[]{:S(2)}, u32[]{:S(2)}) collective-permute-start(s32[2,4]{1,0:T(2,128)S(1)} %get-tuple-element.47), channel_id=1, source_target_pairs={{0,64},{16,80},{32,96},{48,112},{64,0},{80,16},{96,32},{112,48},{1... | collective-permute-start | bytes 104 | tf_op jit(solution)/shard_map/ppermute | solution.py:336
  52.3 10.7 %collective-permute-start.6 = (s32[2,4]{1,0:T(2,128)S(1)}, s32[2,4]{1,0:T(2,128)S(1)}, u32[]{:S(2)}, u32[]{:S(2)}) collective-permute-start(s32[2,4]{1,0:T(2,128)S(1)} %get-tuple-element.48), channel_id=1, source_target_pairs={{0,96},{16,112},{32,0},{48,16},{64,32},{80,48},{96,64},{112,80},{1... | collective-permute-start | bytes 104 | tf_op jit(solution)/shard_map/ppermute | solution.py:336
  62.0 9.5 %collective-permute-start.11 = (bf16[512,512]{1,0:T(8,128)(2,1)S(1)}, bf16[512,512]{1,0:T(8,128)(2,1)}, u32[]{:S(2)}, u32[]{:S(2)}) collective-permute-start(bf16[512,512]{1,0:T(8,128)(2,1)S(1)} %convolution_convert_fusion.1.refs_1_), channel_id=1, source_target_pairs={{0,16},{16,0},{32,48},{48,32},{64,80},{80,64},{96,112},{112,96},{1... | collective-permute-start | bytes 1572872 | tf_op jit(solution)/shard_map/ppermute | solution.py:336
  65.6 6.0 %collective-permute-start.12 = (bf16[512,512]{1,0:T(8,128)(2,1)S(1)}, bf16[512,512]{1,0:T(8,128)(2,1)S(1)}, u32[]{:S(2)}, u32[]{:S(2)}) collective-permute-start(bf16[512,512]{1,0:T(8,128)(2,1)S(1)} %convolution_convert_fusion.refs_2_), channel_id=1, source_target_pairs={{0,16},{16,0},{32,48},{48,32},{64,80},{80,64},{96,112},{112,96},{1... | collective-permute-start | bytes 1572872 | tf_op jit(solution)/shard_map/ppermute | solution.py:336
  66.4 21.6 %collective-permute-start.7 = (bf16[512,512]{1,0:T(8,128)(2,1)S(1)}, bf16[512,512]{1,0:T(8,128)(2,1)S(1)}, u32[]{:S(2)}, u32[]{:S(2)}) collective-permute-start(bf16[512,512]{1,0:T(8,128)(2,1)S(1)} %convolution_convert_fusion.refs_2_), channel_id=1, source_target_pairs={{0,32},{16,48},{32,64},{48,80},{64,96},{80,112},{96,0},{112,16},{1... | collective-permute-start | bytes 1572872 | tf_op jit(solution)/shard_map/ppermute | solution.py:336
  67.8 20.1 %collective-permute-start.8 = (bf16[512,512]{1,0:T(8,128)(2,1)S(1)}, bf16[512,512]{1,0:T(8,128)(2,1)S(1)}, u32[]{:S(2)}, u32[]{:S(2)}) collective-permute-start(bf16[512,512]{1,0:T(8,128)(2,1)S(1)} %convolution_convert_fusion.refs_2_), channel_id=1, source_target_pairs={{0,96},{16,112},{32,0},{48,16},{64,32},{80,48},{96,64},{112,80},{1... | collective-permute-start | bytes 1572872 | tf_op jit(solution)/shard_map/ppermute | solution.py:336
  69.9 17.0 %collective-permute-start.10 = (bf16[256,512]{1,0:T(8,128)(2,1)S(1)}, bf16[256,512]{1,0:T(8,128)(2,1)S(1)}, u32[]{:S(2)}, u32[]{:S(2)}) collective-permute-start(bf16[256,512]{1,0:T(8,128)(2,1)S(1)} %slice.21), channel_id=1, source_target_pairs={{0,96},{16,112},{32,0},{48,16},{64,32},{80,48},{96,64},{112,80},{1... | collective-permute-start | bytes 786440 | tf_op jit(solution)/shard_map/ppermute | solution.py:336
  71.5 16.4 %collective-permute-start.9 = (bf16[256,512]{1,0:T(8,128)(2,1)S(1)}, bf16[256,512]{1,0:T(8,128)(2,1)S(1)}, u32[]{:S(2)}, u32[]{:S(2)}) collective-permute-start(bf16[256,512]{1,0:T(8,128)(2,1)S(1)} %slice.20), channel_id=1, source_target_pairs={{0,32},{16,48},{32,64},{48,80},{64,96},{80,112},{96,0},{112,16},{1... | collective-permute-start | bytes 786440 | tf_op jit(solution)/shard_map/ppermute | solution.py:336
  71.6 18.5 %collective-permute-start.15 = (bf16[512,512]{1,0:T(8,128)(2,1)S(1)}, bf16[512,512]{1,0:T(8,128)(2,1)S(1)}, u32[]{:S(2)}, u32[]{:S(2)}) collective-permute-start(bf16[512,512]{1,0:T(8,128)(2,1)S(1)} %collective-permute-done.2.refs_2_), channel_id=1, source_target_pairs={{0,16},{16,0},{32,48},{48,32},{64,80},{80,64},{96,112},{112,96},{1... | collective-permute-start | bytes 1572872 | tf_op jit(solution)/shard_map/ppermute | solution.py:336
  87.0 5.0 %collective-permute-start.17 = (bf16[512,512]{1,0:T(8,128)(2,1)S(1)}, bf16[512,512]{1,0:T(8,128)(2,1)S(1)}, u32[]{:S(2)}, u32[]{:S(2)}) collective-permute-start(bf16[512,512]{1,0:T(8,128)(2,1)S(1)} %collective-permute-done.3.refs_6_), channel_id=1, source_target_pairs={{0,16},{16,0},{32,48},{48,32},{64,80},{80,64},{96,112},{112,96},{1... | collective-permute-start | bytes 1572872 | tf_op jit(solution)/shard_map/ppermute | solution.py:336
  88.0 4.3 %collective-permute-start.16 = (bf16[512,512]{1,0:T(8,128)(2,1)S(1)}, bf16[512,512]{1,0:T(8,128)(2,1)S(1)}, u32[]{:S(2)}, u32[]{:S(2)}) collective-permute-start(bf16[512,512]{1,0:T(8,128)(2,1)S(1)} %collective-permute-done.7.refs_3_), channel_id=1, source_target_pairs={{0,16},{16,0},{32,48},{48,32},{64,80},{80,64},{96,112},{112,96},{1... | collective-permute-start | bytes 1572872 | tf_op jit(solution)/shard_map/ppermute | solution.py:336
  88.4 4.0 %collective-permute-start.18 = (bf16[512,512]{1,0:T(8,128)(2,1)S(1)}, bf16[512,512]{1,0:T(8,128)(2,1)S(1)}, u32[]{:S(2)}, u32[]{:S(2)}) collective-permute-start(bf16[512,512]{1,0:T(8,128)(2,1)S(1)} %collective-permute-done.8.refs_7_), channel_id=1, source_target_pairs={{0,16},{16,0},{32,48},{48,32},{64,80},{80,64},{96,112},{112,96},{1... | collective-permute-start | bytes 1572872 | tf_op jit(solution)/shard_map/ppermute | solution.py:336
  88.6 12.0 %copy-start.2 = (s32[8,12]{1,0:T(8,128)S(1)}, s32[8,12]{1,0:T(8,128)}, u32[]{:S(2)}) copy-start(s32[8,12]{1,0:T(8,128)} %rel_ref.1) | copy-start | bytes 1156
  88.6 9.8 %collective-permute-start.13 = (bf16[256,512]{1,0:T(8,128)(2,1)S(1)}, bf16[256,512]{1,0:T(8,128)(2,1)S(1)}, u32[]{:S(2)}, u32[]{:S(2)}) collective-permute-start(bf16[256,512]{1,0:T(8,128)(2,1)S(1)} %slice.22), channel_id=1, source_target_pairs={{0,32},{16,48},{32,64},{48,80},{64,96},{80,112},{96,0},{112,16},{1... | collective-permute-start | bytes 786440 | tf_op jit(solution)/shard_map/ppermute | solution.py:336
  90.2 8.2 %collective-permute-start.14 = (bf16[256,512]{1,0:T(8,128)(2,1)S(1)}, bf16[256,512]{1,0:T(8,128)(2,1)S(1)}, u32[]{:S(2)}, u32[]{:S(2)}) collective-permute-start(bf16[256,512]{1,0:T(8,128)(2,1)S(1)} %slice.23), channel_id=1, source_target_pairs={{0,96},{16,112},{32,0},{48,16},{64,32},{80,48},{96,64},{112,80},{1... | collective-permute-start | bytes 786440 | tf_op jit(solution)/shard_map/ppermute | solution.py:336
  92.0 7.1 %collective-permute-start.19 = (bf16[256,512]{1,0:T(8,128)(2,1)S(1)}, bf16[256,512]{1,0:T(8,128)(2,1)S(1)}, u32[]{:S(2)}, u32[]{:S(2)}) collective-permute-start(bf16[256,512]{1,0:T(8,128)(2,1)S(1)} %collective-permute-done.9.refs_1_), channel_id=1, source_target_pairs={{0,16},{16,0},{32,48},{48,32},{64,80},{80,64},{96,112},{112,96},{1... | collective-permute-start | bytes 786440 | tf_op jit(solution)/shard_map/ppermute | solution.py:336
  92.3 6.8 %collective-permute-start.20 = (bf16[256,512]{1,0:T(8,128)(2,1)S(1)}, bf16[256,512]{1,0:T(8,128)(2,1)S(1)}, u32[]{:S(2)}, u32[]{:S(2)}) collective-permute-start(bf16[256,512]{1,0:T(8,128)(2,1)S(1)} %collective-permute-done.10.refs_2_), channel_id=1, source_target_pairs={{0,16},{16,0},{32,48},{48,32},{64,80},{80,64},{96,112},{112,96},{1... | collective-permute-start | bytes 786440 | tf_op jit(solution)/shard_map/ppermute | solution.py:336
  92.5 8.2 %copy-start = (bf16[8,12,128,128]{3,2,1,0:T(8,128)(2,1)S(1)}, bf16[8,12,128,128]{3,2,1,0:T(8,128)(2,1)}, u32[]{:S(2)}) copy-start(bf16[8,12,128,128]{3,2,1,0:T(8,128)(2,1)} %caps.1.refs_12_) | copy-start | bytes 9437188
  98.4 1.8 %collective-permute-start.21 = (bf16[256,512]{1,0:T(8,128)(2,1)S(1)}, bf16[256,512]{1,0:T(8,128)(2,1)S(1)}, u32[]{:S(2)}, u32[]{:S(2)}) collective-permute-start(bf16[256,512]{1,0:T(8,128)(2,1)S(1)} %collective-permute-done.13.refs_3_), channel_id=1, source_target_pairs={{0,16},{16,0},{32,48},{48,32},{64,80},{80,64},{96,112},{112,96},{1... | collective-permute-start | bytes 786440 | tf_op jit(solution)/shard_map/ppermute | solution.py:336
  99.1 1.5 %collective-permute-start.22 = (bf16[256,512]{1,0:T(8,128)(2,1)S(1)}, bf16[256,512]{1,0:T(8,128)(2,1)S(1)}, u32[]{:S(2)}, u32[]{:S(2)}) collective-permute-start(bf16[256,512]{1,0:T(8,128)(2,1)S(1)} %collective-permute-done.14.refs_4_), channel_id=1, source_target_pairs={{0,16},{16,0},{32,48},{48,32},{64,80},{80,64},{96,112},{112,96},{1... | collective-permute-start | bytes 786440 | tf_op jit(solution)/shard_map/ppermute | solution.py:336
